TPU v7x, 32 devices: a whole 2x2x4 slice. The times are simulated.
32 devices in a mesh: dp: 4 (over y, x), expert: 8 (over z, core).
Axes of the slice: x: 2, y: 2, z: 4, core: 2. Of those that a mesh axis runs over, the one named last changes fastest.
Arguments:
- tokens: bfloat16 [384, 4096], P(('dp', 'expert')), may hold values from -6 to 6
- expert_ids: int32 [384, 8], P(('dp', 'expert')), may hold values from 0 to 15, all different within a row; in each aligned block of 12 rows (0 to 11, 12 to 23, ...) at most 12 rows name the same one
- gate_probs: float32 [384, 8], P(('dp', 'expert')), may hold values from 0.02 to 5
- in_weight: bfloat16 [16, 4096, 3072], P('expert', None, 'dp'), may hold values from -0.09375 to 0.09375
- out_weight: bfloat16 [16, 1536, 4096], P('expert', 'dp'), may hold values from -0.15625 to 0.15625
- swap_slot: int32 [8], replicated, may hold values from 0 to 1
Outputs:
- mixed_out: bfloat16 [384, 4096], P(('dp', 'expert'))
- owner_load: float32 [8], replicated
Inputs may be any that keep to these rules, and one draw needn't show every extreme that they name: `expert_ids`: among the rows of one device no expert is named more than 12 times, and in every draw some device's rows name some expert exactly 12 times; a row names 8 different experts.
All inputs are finite; a program needn't handle non-finite values.
Results may differ from a plain program's by a relative error of at most 0.018.
Values may be sent and summed in bfloat16 or wider, within the bound.
No kernel may reach another device: no remote copies, remote signals or barrier semaphores. Data moves between devices by JAX's collectives and lax.ppermute only.
A program may use at most 128 MiB of HBM per device.

v0:
```python
import jax
import jax.numpy as jnp
from jax import lax
from jax.sharding import PartitionSpec as P


def lookup_small(values_table, index_array):
    columns = jnp.arange(values_table.shape[0], dtype=jnp.int32)
    return jnp.sum(jnp.where(index_array[..., None] == columns, values_table, 0), -1)


def planned_holder(expert_index, swap_slot, per_device, owners):
    home = expert_index // per_device
    within = expert_index % per_device
    partner = (home + owners // 2) % owners
    moved = within == lookup_small(swap_slot, home)
    return jnp.where(moved, partner, home)


def slot_ranks(expert_index, experts_all):
    columns = jnp.arange(experts_all, dtype=jnp.int32)
    onehot = (expert_index[..., None] == columns).astype(jnp.int32)
    before = jnp.cumsum(onehot, axis=-2) - onehot
    return jnp.sum(before * onehot, -1)


def on_device(tokens, expert_ids, gate_probs, in_weight, out_weight, swap_slot):
    owners = lax.axis_size("expert")
    groups = lax.axis_size("dp")
    per_device = in_weight.shape[0]
    model_width = tokens.shape[1]
    local_rows, top_count = expert_ids.shape
    experts_all = per_device * owners
    capacity = max(2, (2 * local_rows * top_count + experts_all - 1) // experts_all)
    slots_dev = owners * capacity
    all_experts = jnp.arange(experts_all, dtype=jnp.int32)
    hits = jnp.where(
        expert_ids.reshape(-1)[:, None] == all_experts,
        gate_probs.reshape(-1)[:, None],
        jnp.float32(0.0),
    )
    totals = lax.psum(jnp.sum(hits, 0), ("dp", "expert"))
    holder = planned_holder(all_experts, swap_slot, per_device, owners)
    holder_hot = (holder[:, None] == jnp.arange(owners, dtype=jnp.int32)).astype(jnp.float32)
    owner_load = jnp.dot(totals, holder_hot, precision=lax.Precision.HIGHEST) * (
        owners / (groups * owners * local_rows)
    )
    own_ids = expert_ids.reshape(1, -1)
    own_rank = slot_ranks(own_ids, experts_all)
    own_pos = (
        (own_ids // per_device * capacity + own_rank) * per_device + own_ids % per_device
    ).reshape(-1)
    group_tokens, group_ids = (
        lax.all_gather(tokens, "dp", axis=0, tiled=True),
        lax.all_gather(expert_ids, "dp", axis=0, tiled=True),
    )
    group_ids = group_ids.reshape(groups, -1)
    group_rank = slot_ranks(group_ids, experts_all)
    group_index = jnp.arange(groups, dtype=jnp.int32)[:, None]
    group_pos = (
        ((group_index * owners + group_ids // per_device) * capacity + group_rank) * per_device
        + group_ids % per_device
    ).reshape(-1)
    sources = jnp.repeat(group_tokens, top_count, axis=0)
    outgoing = (
        jnp.zeros((groups * slots_dev * per_device, model_width), jnp.bfloat16)
        .at[group_pos]
        .set(sources)
    )
    arrived = lax.all_to_all(
        outgoing.reshape(groups, slots_dev, per_device, model_width),
        "expert",
        split_axis=1,
        concat_axis=1,
        tiled=True,
    )
    gathered = arrived.reshape(groups * slots_dev, per_device, model_width)
    half_width = out_weight.shape[1]
    both_halves = jnp.einsum(
        "rsd,sdf->rsf", gathered, in_weight, preferred_element_type=jnp.float32
    )
    hidden = (jax.nn.silu(both_halves[..., :half_width]) * both_halves[..., half_width:]).astype(
        jnp.bfloat16
    )
    summed = lax.psum_scatter(
        jnp.einsum("rsf,sfd->rsd", hidden, out_weight, preferred_element_type=jnp.float32).astype(
            jnp.bfloat16
        ),
        "dp",
        scatter_dimension=0,
        tiled=True,
    )
    returned = lax.all_to_all(summed, "expert", split_axis=0, concat_axis=0, tiled=True)
    picked = jnp.take(returned.reshape(-1, model_width), own_pos, axis=0).reshape(
        local_rows, top_count, model_width
    )
    mixed_out = jnp.sum(gate_probs[..., None] * picked.astype(jnp.float32), 1).astype(jnp.bfloat16)
    return (mixed_out, owner_load)


def solution(mesh):
    return jax.shard_map(
        on_device,
        mesh=mesh,
        in_specs=(
            P(("dp", "expert"), None),
            P(("dp", "expert"), None),
            P(("dp", "expert"), None),
            P("expert", None, "dp"),
            P("expert", "dp", None),
            P(),
        ),
        out_specs=(P(("dp", "expert"), None), P()),
        check_vma=False,
    )
```

profile of v0, /device:TPU:0, one launch (start us, length us, event | category | flops | bytes accessed | tf_op | source)
XLA Modules:
  0.0 362.4 jit_solution(3783331306621220483)
XLA Ops:
  7.2 0.0 reduce-scatter.2.cloned.1.call-start
  7.2 9.7 %all-gather = s32[4,12,8]{1,2,0:T(8,128)S(1)} all-gather(s32[1,12,8]{1,2,0:T(8,128)} %bitcast.36), channel_id=1, replica_groups=mesh['dp'=4,'expert'=8] {'dp'}, dimensions={0}, use_global_device_ids=true | all-gather | bytes 1920 | tf_op jit(solution)/shard_map/all_gather | solution.py:55
  17.0 0.1 copy.47
  17.1 0.1 eq.99
  17.1 0.1 reshape.512
  17.2 0.1 fusion.9
  17.4 0.2 reduce_window_sum.23
  17.6 0.2 select_reduce_fusion
  17.8 0.1 reduce_sum.54
  17.9 0.1 add.215
  18.0 0.1 add.216
  18.0 10.5 %all-gather.1 = bf16[4,12,4096]{2,1,0:T(8,128)(2,1)S(1)} all-gather(bf16[1,12,4096]{2,1,0:T(8,128)(2,1)} %bitcast.35), channel_id=1, replica_groups=mesh['dp'=4,'expert'=8] {'dp'}, dimensions={0}, use_global_device_ids=true | all-gather | bytes 491520 | tf_op jit(solution)/shard_map/all_gather | solution.py:54
  28.6 0.1 reshape.537
  28.7 8.5 %scatter_custom_fusion = bf16[768,4096]{1,0:T(8,128)(2,1)} fusion(s32[384]{0:T(512)S(1)} %fusion.21, bf16[]{:T(256)} %constant.113.clone.1, bf16[48,4096]{1,0:T(8,128)(2,1)S(1)} %reshape.537), kind=kCustom, calls=%fused_computation.4 | custom fusion | bytes 6684674 | tf_op jit(solution)/shard_map/scatter | solution.py:68
  37.2 10.9 %reshape.514 = bf16[4,96,2,4096]{3,2,1,0:T(2,128)(2,1)} reshape(bf16[768,4096]{1,0:T(8,128)(2,1)} %scatter_custom_fusion) | data formatting | bytes 12582912 | tf_op jit(solution)/shard_map/reshape | solution.py:71
  48.1 6.9 %copy.49 = bf16[4,96,2,4096]{3,2,0,1:T(2,128)(2,1)S(1)} copy(bf16[4,96,2,4096]{3,2,1,0:T(2,128)(2,1)} %reshape.514) | data formatting | bytes 12582912 | tf_op jit(solution)/shard_map/reshape | solution.py:71
  54.9 143.8 %all_to_all.10 = bf16[4,96,2,4096]{3,2,0,1:T(2,128)(2,1)S(1)} all-to-all(bf16[4,96,2,4096]{3,2,0,1:T(2,128)(2,1)S(1)} %copy.49), channel_id=1, replica_groups=mesh['dp'=4,'expert'=8] {'expert'}, dimensions={1} | all-to-all | bytes 12582912 | tf_op jit(solution)/shard_map/all_to_all | solution.py:70
  198.7 4.5 %copy.50 = bf16[4,96,2,4096]{3,1,0,2:T(8,128)(2,1)S(1)} copy(bf16[4,96,2,4096]{3,2,0,1:T(2,128)(2,1)S(1)} %all_to_all.10) | data formatting | bytes 12582912 | tf_op jit(solution)/shard_map/all_to_all | solution.py:70
  203.3 0.0 slice-start.1
  203.3 8.3 %convolution_bitcast_fusion = f32[384,2,768]{2,0,1:T(8,128)S(1)} fusion(bf16[384,2,4096]{2,0,1:T(8,128)(2,1)S(1)} %bitcast.34, bf16[2,4096,768]{2,1,0:T(8,128)(2,1)} %param.9), kind=kOutput, calls=%fused_computation.7 | convolution fusion | flops 4831838208 | bytes 21233664 | tf_op jit(solution)/shard_map/rsd,sdf->rsf/dot_general | solution.py:79
  211.6 0.0 slice-done
  211.6 0.0 slice-done.1
  211.6 5.4 %fusion = bf16[384,2,4096]{2,0,1:T(8,128)(2,1)} fusion(bf16[2,384,4096]{2,1,0:T(8,128)(2,1)S(1)} %bitcast.38, f32[384,2,768]{2,0,1:T(8,128)S(1)} %convolution_bitcast_fusion), kind=kOutput, calls=%fused_computation.3 | convolution fusion | flops 2420834304 | bytes 14942208 | tf_op jit(solution)/shard_map/rsf,sfd->rsd/dot_general | solution.py:86
  217.0 0.0 reduce-scatter.2.cloned.1.call-update
  217.0 0.0 copy-start
  217.0 0.0 copy-start.1
  217.1 0.0 copy-start.2
  217.1 68.1 %reduce-scatter.2.cloned.1.call-done = bf16[96,2,4096]{2,0,1:T(8,128)(2,1)} async-done(((bf16[384,2,4096]{2,0,1:T(8,128)(2,1)}), bf16[96,2,4096]{2,0,1:T(8,128)(2,1)}) %reduce-scatter.2.cloned.1.call-update) | async-done | bytes 1572880 | tf_op jit(solution)/shard_map/reduce_scatter | solution.py:85
  285.2 4.2 %copy.51 = bf16[96,2,4096]{2,1,0:T(2,128)(2,1)} copy(bf16[96,2,4096]{2,0,1:T(8,128)(2,1)} %reduce-scatter.2.cloned.1.call-done) | data formatting | bytes 3145728 | tf_op jit(solution)/shard_map/reduce_scatter | solution.py:85
  289.4 4.6 %all-to-all-start.1 = ((bf16[96,2,4096]{2,1,0:T(2,128)(2,1)}), bf16[96,2,4096]{2,1,0:T(2,128)(2,1)S(1)}, u32[]{:S(2)}, u32[]{:S(2)}) async-start(bf16[96,2,4096]{2,1,0:T(2,128)(2,1)} %copy.51), calls=%async_computation.2 | async-start | bytes 3145728 | tf_op jit(solution)/shard_map/all_to_all | solution.py:93
  294.0 0.0 copy-done
  294.0 0.1 copy.42
  294.1 0.1 eq.95
  294.2 0.1 copy.41
  294.3 0.1 broadcast_in_dim.52
  294.3 0.1 select_reduce_fusion.2
  294.5 56.7 %psum.7 = f32[16]{0:T(128)S(1)} all-reduce(f32[16]{0:T(128)S(1)} %select_reduce_fusion.2), channel_id=1, replica_groups=mesh['dp'=4,'expert'=8] {'dp','expert'}, use_global_device_ids=true, to_apply=%region_8.9 | all-reduce | flops 16 | bytes 128 | tf_op jit(solution)/shard_map/psum | solution.py:42
  351.2 0.1 reshape.517
  351.3 0.1 fusion.10
  351.3 0.1 reduce_window_sum.22
  351.5 0.2 select_reduce_fusion.1
  351.7 0.1 reduce_sum.52
  351.8 0.1 select_reduce_fusion.3
  351.9 0.7 fusion.6
  352.6 0.0 all-to-all-done.1
  352.6 0.6 reshape.516
  353.3 1.0 gather_fusion
  354.3 1.3 multiply_reduce_fusion
  (11 shorter events, 0.1 us)
Async XLA Ops:
  7.2 278.0 %reduce-scatter.2.cloned.1.call-start = ((), (), s32[]{:S(2)}) async-start(), calls=%async_computation.3 | async-start | bytes 7864320 | tf_op jit(solution)/shard_map/reduce_scatter | solution.py:85
  198.7 12.8 %slice-start = ((s8[6291456]{0:T(1024)(128)(4,1)}), s8[2097152]{0:T(1024)(128)(4,1)S(1)}, s32[]{:S(2)}) async-start(s8[6291456]{0:T(1024)(128)(4,1)} %bitcast.37), calls=%async_computation.4 | async-start | bytes 4194304
  203.3 8.3 %slice-start.1 = ((s8[6291456]{0:T(1024)(128)(4,1)}), s8[4194304]{0:T(1024)(128)(4,1)S(1)}, s32[]{:S(2)}) async-start(s8[6291456]{0:T(1024)(128)(4,1)} %bitcast.37), calls=%async_computation.5 | async-start | bytes 8388608
  217.0 77.0 %copy-start = (s32[12,8]{0,1:T(8,128)S(1)}, s32[12,8]{0,1:T(8,128)}, u32[]{:S(2)}) copy-start(s32[12,8]{0,1:T(8,128)} %param.7) | copy-start | bytes 1156
  217.0 77.1 %copy-start.1 = (f32[12,8]{0,1:T(8,128)S(1)}, f32[12,8]{0,1:T(8,128)}, u32[]{:S(2)}) copy-start(f32[12,8]{0,1:T(8,128)} %param.8) | copy-start | bytes 1156
  217.1 134.7 %copy-start.2 = (s32[8]{0:T(128)S(1)}, s32[8]{0:T(128)}, u32[]{:S(2)}) copy-start(s32[8]{0:T(128)} %param.11) | copy-start | bytes 100
  289.4 63.2 %all-to-all-start.1 = ((bf16[96,2,4096]{2,1,0:T(2,128)(2,1)}), bf16[96,2,4096]{2,1,0:T(2,128)(2,1)S(1)}, u32[]{:S(2)}, u32[]{:S(2)}) async-start(bf16[96,2,4096]{2,1,0:T(2,128)(2,1)} %copy.51), calls=%async_computation.2 | async-start | bytes 3145728 | tf_op jit(solution)/shard_map/all_to_all | solution.py:93
Sparse Core Ops, SparseCore 0:
  217.2 67.9 reduce-scatter.1
where the time goes:
time: 363 us; the launch traced here: 362 us
  blocking collectives  221 us (61%)
  waiting for transfers between devices  68.1 us (19%)
  local copies, waits for them, and re-layouts  37.8 us (10%)
  matrix products  14.4 us (4%)
  between operations  14.2 us (4%)
  starting transfers between devices  4.63 us (1%)
    all_to_all x1, blocking collectives, on_device(): lax.all_to_all(outgoing.reshape(groups, slots_dev, per_device, model_widt...  144 us
    reduce_scatter x1, waiting for transfers between devices, on_device(): lax.psum_scatter(jnp.einsum('rsf,sfd->rsd', hidden, out_weight, preferred...  68.1 us
    psum x1, blocking collectives, on_device(): totals = lax.psum(jnp.sum(hits, 0), ('dp', 'expert'))  56.7 us
    reshape x2, local copies, waits for them, and re-layouts, on_device(): outgoing.reshape(groups, slots_dev, per_device, model_width)  17.7 us
    all_gather x1, blocking collectives, on_device(): lax.all_gather(tokens, 'dp', axis=0, tiled=True)  10.5 us
    all_gather x1, blocking collectives, on_device(): lax.all_gather(expert_ids, 'dp', axis=0, tiled=True)  9.74 us
    scatter x1, local copies, waits for them, and re-layouts, on_device(): outgoing = jnp.zeros((groups * slots_dev * per_device, model_width), jnp....  8.48 us
    dot_general x1, matrix products, on_device(): jnp.einsum('rsd,sdf->rsf', gathered, in_weight, preferred_element_type=jn...  8.28 us
  transfers between devices with their start and end apart: 2, of which 1 were waited for; matrix products, arithmetic and copies ran while one was open for 1% of the time, Pallas kernels for 0%

commit v1 on v0

v1 whole, which is shorter than its diff:
```python
import jax
import jax.numpy as jnp
from jax import lax
from jax.sharding import PartitionSpec as P


def lookup_small(values_table, index_array):
    columns = jnp.arange(values_table.shape[0], dtype=jnp.int32)
    return jnp.sum(jnp.where(index_array[..., None] == columns, values_table, 0), -1)


def planned_holder(expert_index, swap_slot, per_device, owners):
    home = expert_index // per_device
    within = expert_index % per_device
    partner = (home + owners // 2) % owners
    moved = within == lookup_small(swap_slot, home)
    return jnp.where(moved, partner, home)


def on_device(tokens, expert_ids, gate_probs, in_weight, out_weight, swap_slot):
    owners = lax.axis_size("expert")
    per_device = in_weight.shape[0]
    top_count = expert_ids.shape[1]
    experts_all = per_device * owners
    half_width = out_weight.shape[1]
    axes = ("dp", "expert")
    routing = lax.all_gather(
        jnp.concatenate([expert_ids.astype(jnp.float32), gate_probs], 1), axes, axis=0, tiled=True
    )
    all_tokens = lax.all_gather(tokens, axes, axis=0, tiled=True)
    all_ids = routing[:, :top_count].astype(jnp.int32)
    all_gates = routing[:, top_count:]
    all_experts = jnp.arange(experts_all, dtype=jnp.int32)
    dense_gates = jnp.sum(
        jnp.where(all_ids[..., None] == all_experts, all_gates[..., None], jnp.float32(0.0)), 1
    )
    totals = jnp.sum(dense_gates, 0)
    holder = planned_holder(all_experts, swap_slot, per_device, owners)
    owner_load = jnp.sum(
        jnp.where(
            holder == jnp.arange(owners, dtype=jnp.int32)[:, None], totals[None, :], jnp.float32(0.0)
        ),
        1,
    ) * (owners / all_ids.shape[0])
    own = lax.axis_index("expert") * per_device + jnp.arange(per_device, dtype=jnp.int32)
    own_gates = jnp.sum(
        jnp.where(all_ids[..., None] == own, all_gates[..., None], jnp.float32(0.0)), 1
    )
    both = jnp.einsum("td,sdf->tsf", all_tokens, in_weight, preferred_element_type=jnp.float32)
    hidden = jax.nn.silu(both[..., :half_width]) * both[..., half_width:]
    hidden = (hidden * own_gates[..., None]).astype(jnp.bfloat16)
    partial = jnp.einsum("tsf,sfd->td", hidden, out_weight, preferred_element_type=jnp.float32)
    partial = partial.astype(jnp.bfloat16).reshape(-1, *tokens.shape)
    mixed_out = lax.psum_scatter(partial, axes, scatter_dimension=0, tiled=False)
    return (mixed_out, owner_load)


def solution(mesh):
    return jax.shard_map(
        on_device,
        mesh=mesh,
        in_specs=(
            P(("dp", "expert"), None),
            P(("dp", "expert"), None),
            P(("dp", "expert"), None),
            P("expert", None, "dp"),
            P("expert", "dp", None),
            P(),
        ),
        out_specs=(P(("dp", "expert"), None), P()),
        check_vma=False,
    )
```

time: 363 us -> 245 us (0.67)
  blocking collectives: 221 us -> 44.6 us
  waiting for transfers between devices: 68.1 us -> 162 us
  local copies, waits for them, and re-layouts: 37.8 us -> 7.72 us
  starting transfers between devices: 4.63 us -> 0.08 us
    all_to_all x1 -> x0, blocking collectives: 144 us -> none  [on_device(): lax.all_to_all(outgoing.reshape(groups, slots_dev, per_device, model_widt...]
    reduce_scatter x1, waiting for transfers between devices: 68.1 us -> 140 us  [on_device(): lax.psum_scatter(partial, axes, scatter_dimension=0, tiled=False)]
    psum x1 -> x0, blocking collectives: 56.7 us -> none  [on_device(): totals = lax.psum(jnp.sum(hits, 0), ('dp', 'expert'))]
    all_gather x2 -> x1, blocking collectives: 20.3 us -> 44.6 us  [on_device(): lax.all_gather(jnp.concatenate([expert_ids.astype(jnp.float32), gate_prob...]
    all_gather x0 -> x1, waiting for transfers between devices: none -> 21.6 us  [on_device(): all_tokens = lax.all_gather(tokens, axes, axis=0, tiled=True)]
    reshape x5 -> x1, local copies, waits for them, and re-layouts: 18.5 us -> 2.71 us  [on_device(): partial = partial.astype(jnp.bfloat16).reshape(-1, *tokens.shape)]
    scatter x1 -> x0, local copies, waits for them, and re-layouts: 8.48 us -> none  [on_device(): outgoing = jnp.zeros((groups * slots_dev * per_device, model_width), jnp....]
    unnamed x13 -> x7, local copies, waits for them, and re-layouts: 0.29 us -> 4.9 us
  transfers between devices with their start and end apart: 2 -> 2, of which waited for: 1 -> 2; matrix products, arithmetic and copies ran while one was open for 1% -> 1% of each run, Pallas kernels for 0% -> 0%
where the time goes in v1:
time: 245 us
  waiting for transfers between devices  162 us (66%)
  blocking collectives  44.6 us (18%)
  matrix products  14.1 us (6%)
  between operations  14.1 us (6%)
  local copies, waits for them, and re-layouts  7.72 us (3%)
    reduce_scatter x1, waiting for transfers between devices, on_device(): lax.psum_scatter(partial, axes, scatter_dimension=0, tiled=False)  140 us
    all_gather x1, blocking collectives, on_device(): lax.all_gather(jnp.concatenate([expert_ids.astype(jnp.float32), gate_prob...  44.6 us
    all_gather x1, waiting for transfers between devices, on_device(): all_tokens = lax.all_gather(tokens, axes, axis=0, tiled=True)  21.6 us
    dot_general x1, matrix products, on_device(): jnp.einsum('td,sdf->tsf', all_tokens, in_weight, preferred_element_type=j...  8.18 us
    dot_general x1, matrix products, on_device(): jnp.einsum('tsf,sfd->td', hidden, out_weight, preferred_element_type=jnp....  5.9 us
  transfers between devices with their start and end apart: 2, of which 2 were waited for; matrix products, arithmetic and copies ran while one was open for 1% of the time, Pallas kernels for 0%

profile of v1, /device:TPU:0, one launch (start us, length us, event | category | flops | bytes accessed | tf_op | source)
XLA Modules:
  0.0 244.9 jit_solution(1570282857436647588)
XLA Ops:
  7.2 0.0 all-gather.4.cloned.1.call-start
  7.2 0.7 all-gather.4.cloned.1.call-update
  7.9 0.0 reduce-scatter.2.cloned.1.call-start
  7.9 0.7 convert_element_type.12
  8.6 0.7 maximum_bitcast_fusion
  9.3 0.1 copy.23
  9.4 44.6 %all-gather.1 = f32[32,12,16]{2,1,0:T(8,128)S(1)} all-gather(f32[1,12,16]{2,1,0:T(8,128)S(1)} %copy.23), channel_id=1, replica_groups=mesh['dp'=4,'expert'=8] {'dp','expert'}, dimensions={0}, use_global_device_ids=true | all-gather | bytes 25344 | tf_op jit(solution)/shard_map/all_gather | solution.py:27
  54.0 0.1 fusion.7
  54.2 0.1 copy.26
  54.3 0.1 copy.27
  54.4 0.1 select_reduce_fusion.1
  54.5 21.6 %all-gather.4.cloned.1.call-done = bf16[32,12,4096]{2,1,0:T(8,128)(2,1)} async-done(((bf16[1,12,4096]{2,1,0:T(8,128)(2,1)}), bf16[32,12,4096]{2,1,0:T(8,128)(2,1)}) %all-gather.4.cloned.1.call-update) | async-done | bytes 3145744 | tf_op jit(solution)/shard_map/all_gather | solution.py:30
  76.0 4.0 %reshape.69 = bf16[384,4096,1]{1,0,2:T(8,128)(2,1)S(1)} reshape(bf16[32,12,4096]{2,1,0:T(8,128)(2,1)} %all-gather.4.cloned.1.call-done) | data formatting | bytes 6291456
  80.0 8.2 %fusion.8 = f32[384,2,768]{2,0,1:T(8,128)S(1)} fusion(bf16[384,4096,1]{1,0,2:T(8,128)(2,1)S(1)} %reshape.69, bf16[2,4096,768]{2,1,0:T(8,128)(2,1)} %param.9), kind=kOutput, calls=%fused_computation.28 | convolution fusion | flops 4831838208 | bytes 18087936 | tf_op jit(solution)/shard_map/td,sdf->tsf/dot_general | solution.py:49
  88.2 5.9 %bitcast_convert_fusion = bf16[384,4096]{1,0:T(8,128)(2,1)S(1)} fusion(bf16[2,384,4096]{2,1,0:T(8,128)(2,1)} %param.10, f32[384,2,768]{2,0,1:T(8,128)S(1)} %fusion.8, f32[384,2]{0,1:T(2,128)S(1)} %select_reduce_fusion.1), kind=kOutput, calls=%fused_computation | convolution fusion | flops 2419556352 | bytes 11799552 | tf_op jit(solution)/shard_map/tsf,sfd->td/dot_general | solution.py:52
  94.1 2.7 %reshape.64 = bf16[32,12,4096]{2,1,0:T(8,128)(2,1)} reshape(bf16[384,4096]{1,0:T(8,128)(2,1)S(1)} %bitcast_convert_fusion) | data formatting | bytes 6291456 | tf_op jit(solution)/shard_map/reshape | solution.py:53
  96.8 0.0 copy-start
  96.8 0.0 reduce-scatter.2.cloned.1.call-update
  96.9 0.6 copy-done
  97.5 0.1 select_reduce_fusion.3
  97.6 0.1 select_reduce_fusion
  97.7 0.1 select_reduce_fusion.2
  97.8 0.5 broadcast_multiply_fusion
  98.4 139.7 %reduce-scatter.2.cloned.1.call-done = bf16[1,12,4096]{2,1,0:T(8,128)(2,1)} async-done(((bf16[32,12,4096]{2,1,0:T(8,128)(2,1)}), bf16[1,12,4096]{2,1,0:T(8,128)(2,1)}) %reduce-scatter.2.cloned.1.call-update) | async-done | bytes 98320 | tf_op jit(solution)/shard_map/reduce_scatter | solution.py:54
  (5 shorter events, 0.0 us)
Async XLA Ops:
  7.2 68.9 %all-gather.4.cloned.1.call-start = ((), (), s32[]{:S(2)}) async-start(), calls=%async_computation.2 | async-start | bytes 4325376 | tf_op jit(solution)/shard_map/all_gather | solution.py:30
  7.9 230.2 %reduce-scatter.2.cloned.1.call-start = ((), (), s32[]{:S(2)}) async-start(), calls=%async_computation.1 | async-start | bytes 4325376 | tf_op jit(solution)/shard_map/reduce_scatter | solution.py:54
  96.8 0.7 copy-start
Sparse Core Ops, SparseCore 0:
  11.0 64.9 all-gather.3
  97.0 141.0 reduce-scatter.1

commit v2 on v1

v2 whole, which is shorter than its diff:
```python
import jax
import jax.numpy as jnp
from jax import lax
from jax.sharding import Mesh, PartitionSpec as P

LANES = 128


def lookup_small(values_table, index_array):
    columns = jnp.arange(values_table.shape[0], dtype=jnp.int32)
    return jnp.sum(jnp.where(index_array[..., None] == columns, values_table, 0), -1)


def planned_holder(expert_index, swap_slot, per_device, owners):
    home = expert_index // per_device
    within = expert_index % per_device
    partner = (home + owners // 2) % owners
    moved = within == lookup_small(swap_slot, home)
    return jnp.where(moved, partner, home)


def swap(value, axis, distance):
    size = lax.axis_size(axis)
    return lax.ppermute(value, axis, [(i, i ^ distance) for i in range(size)])


def split_gates(gates):
    high = lax.reduce_precision(gates, 8, 7)
    middle = lax.reduce_precision(gates - high, 8, 7)
    return [part.astype(jnp.bfloat16) for part in (high, middle, gates - high - middle)]


def gathered(value, axis):
    pieces = [value] + [swap(value, axis, k) for k in range(1, lax.axis_size(axis))]
    return jnp.concatenate(pieces, 0)


def scattered(value, axis):
    size = lax.axis_size(axis)
    blocks = value.reshape(size, -1, value.shape[1])
    total = blocks[0].astype(jnp.float32)
    for k in range(1, size):
        total = total + swap(blocks[k], axis, k).astype(jnp.float32)
    return total.astype(jnp.bfloat16)


def in_order(blocks):
    for dim, axis in enumerate(("dp", "chip")):
        size = lax.axis_size(axis)
        here = jnp.arange(size, dtype=jnp.int32)
        match = (here[:, None] ^ here[None, :]) == lax.axis_index(axis)
        moved = jnp.moveaxis(blocks, dim, 0)
        picked = jnp.sum(jnp.where(match[..., None, None], moved[None], jnp.float32(0.0)), 1)
        blocks = jnp.moveaxis(picked, 0, dim)
    return blocks


def on_device(tokens, expert_ids, gate_probs, in_weight, out_weight, swap_slot):
    groups, chips = lax.axis_size("dp"), lax.axis_size("chip")
    owners = 2 * chips
    per_device = in_weight.shape[0]
    rows, width = tokens.shape
    part = width // 2
    top_count = expert_ids.shape[1]
    experts_all = per_device * owners
    half_width = out_weight.shape[1]
    core = lax.axis_index("core")
    first = core == 0

    routing = jnp.concatenate([expert_ids.astype(jnp.bfloat16), *split_gates(gate_probs)], 1)
    routing = jnp.pad(routing, ((0, 0), (0, LANES - routing.shape[1])))
    left, right = tokens[:, :part], tokens[:, part:]
    keep = jnp.concatenate([jnp.where(first, left, right), routing], 1)
    give = jnp.concatenate([jnp.where(first, right, left), routing], 1)
    taken = swap(give, "core", 1)
    both_cores = jnp.concatenate(
        [jnp.where(first, keep, taken), jnp.where(first, taken, keep)], 0
    )
    mine = gathered(gathered(both_cores, "chip"), "dp")
    own_half = mine[:, :part]
    other_half = swap(own_half, "core", 1)
    all_tokens = jnp.concatenate(
        [jnp.where(first, own_half, other_half), jnp.where(first, other_half, own_half)], 1
    )

    meta = mine[:, part:].astype(jnp.float32)
    all_ids = meta[:, :top_count].astype(jnp.int32)
    all_gates = (
        meta[:, top_count : 2 * top_count]
        + meta[:, 2 * top_count : 3 * top_count]
        + meta[:, 3 * top_count : 4 * top_count]
    )
    all_experts = jnp.arange(experts_all, dtype=jnp.int32)
    dense_gates = jnp.sum(
        jnp.where(all_ids[..., None] == all_experts, all_gates[..., None], jnp.float32(0.0)), 1
    )
    chip_totals = jnp.sum(dense_gates.reshape(groups, chips, 2 * rows, experts_all), 2)
    totals = jnp.sum(in_order(chip_totals), (0, 1))
    holder = planned_holder(all_experts, swap_slot, per_device, owners)
    owner_load = jnp.sum(
        jnp.where(
            holder == jnp.arange(owners, dtype=jnp.int32)[:, None], totals[None, :], jnp.float32(0.0)
        ),
        1,
    ) * (owners / all_ids.shape[0])

    home = lax.axis_index("chip") * 2 + core
    own = home * per_device + jnp.arange(per_device, dtype=jnp.int32)
    own_gates = jnp.sum(
        jnp.where(all_ids[..., None] == own, all_gates[..., None], jnp.float32(0.0)), 1
    )
    both = jnp.einsum("td,sdf->tsf", all_tokens, in_weight, preferred_element_type=jnp.float32)
    hidden = jax.nn.silu(both[..., :half_width]) * both[..., half_width:]
    hidden = (hidden * own_gates[..., None]).astype(jnp.bfloat16)
    partial = jnp.einsum(
        "tsf,sfd->td", hidden, out_weight, preferred_element_type=jnp.float32
    ).astype(jnp.bfloat16)

    left, right = partial[:, :part], partial[:, part:]
    arrived = swap(jnp.where(first, right, left), "core", 1)
    own_half = jnp.where(first, left, right).astype(jnp.float32) + arrived.astype(jnp.float32)
    summed = scattered(scattered(own_half.astype(jnp.bfloat16), "dp"), "chip")
    upper, lower = summed[:rows], summed[rows:]
    arrived = swap(jnp.where(first, lower, upper), "core", 1)
    kept = jnp.where(first, upper, lower)
    mixed_out = jnp.concatenate(
        [jnp.where(first, kept, arrived), jnp.where(first, arrived, kept)], 1
    )
    return (mixed_out, owner_load)


def solution(mesh):
    groups, owners = mesh.devices.shape
    fine = Mesh(mesh.devices.reshape(groups, owners // 2, 2), ("dp", "chip", "core"))
    rows = P(("dp", "chip", "core"), None)
    return jax.shard_map(
        on_device,
        mesh=fine,
        in_specs=(
            rows,
            rows,
            rows,
            P(("chip", "core"), None, "dp"),
            P(("chip", "core"), "dp", None),
            P(),
        ),
        out_specs=(rows, P()),
        check_vma=False,
    )
```

time: 245 us -> 159 us (0.65)
  waiting for transfers between devices: 162 us -> 97.1 us
  blocking collectives: 44.6 us -> 0 us
  starting transfers between devices: 0.08 us -> 17 us
  between operations: 14.1 us -> 0.86 us
  local copies, waits for them, and re-layouts: 7.72 us -> 20.3 us
  other arithmetic: 2.35 us -> 11 us
    reduce_scatter x1 -> x0, waiting for transfers between devices: 140 us -> none  [on_device(): lax.psum_scatter(partial, axes, scatter_dimension=0, tiled=False)]
    ppermute x0 -> x16, waiting for transfers between devices: none -> 97.1 us  [swap(): return lax.ppermute(value, axis, [(i, i ^ distance) for i in range(size)])]
    all_gather x1 -> x0, blocking collectives: 44.6 us -> none  [on_device(): lax.all_gather(jnp.concatenate([expert_ids.astype(jnp.float32), gate_prob...]
    all_gather x1 -> x0, waiting for transfers between devices: 21.6 us -> none  [on_device(): all_tokens = lax.all_gather(tokens, axes, axis=0, tiled=True)]
    ppermute x0 -> x16, starting transfers between devices: none -> 17 us  [swap(): return lax.ppermute(value, axis, [(i, i ^ distance) for i in range(size)])]
    ppermute x0 -> x7, local copies, waits for them, and re-layouts: none -> 8.01 us  [swap(): return lax.ppermute(value, axis, [(i, i ^ distance) for i in range(size)])]
    concatenate x0 -> x2, local copies, waits for them, and re-layouts: none -> 6.32 us  [gathered(): return jnp.concatenate(pieces, 0)]
    convert_element_type x2 -> x7, other arithmetic: 0.7 us -> 5.05 us  [the longest x1 2.01 us: on_device(): summed = scattered(scattered(own_half.astype(jnp.bfloat16), 'dp'), 'chip')]
  transfers between devices with their start and end apart: 2 -> 16, of which waited for: 2 -> 14; matrix products, arithmetic and copies ran while one was open for 1% -> 5% of each run, Pallas kernels for 0% -> 0%
where the time goes in v2:
time: 159 us
  waiting for transfers between devices  97.1 us (61%)
  local copies, waits for them, and re-layouts  20.3 us (13%)
  starting transfers between devices  17 us (11%)
  matrix products  12.7 us (8%)
  other arithmetic  11 us (7%)
    ppermute x16, waiting for transfers between devices, swap(): return lax.ppermute(value, axis, [(i, i ^ distance) for i in range(size)])  97.1 us
    ppermute x16, starting transfers between devices, swap(): return lax.ppermute(value, axis, [(i, i ^ distance) for i in range(size)])  17 us
    dot_general x1, matrix products, on_device(): jnp.einsum('td,sdf->tsf', all_tokens, in_weight, preferred_element_type=j...  8.64 us
    ppermute x7, local copies, waits for them, and re-layouts, swap(): return lax.ppermute(value, axis, [(i, i ^ distance) for i in range(size)])  8.01 us
    concatenate x2, local copies, waits for them, and re-layouts, gathered(): return jnp.concatenate(pieces, 0)  6.32 us
    dot_general x1, matrix products, on_device(): jnp.einsum('tsf,sfd->td', hidden, out_weight, preferred_element_type=jnp....  4.07 us
  transfers between devices with their start and end apart: 16, of which 14 were waited for; matrix products, arithmetic and copies ran while one was open for 5% of the time, Pallas kernels for 0%

profile of v2, /device:TPU:0, one launch (start us, length us, event | category | flops | bytes accessed | tf_op | source)
XLA Modules:
  0.0 158.9 jit_solution(13615729833421931337)
XLA Ops:
  0.6 0.7 convert_element_type.65
  1.3 0.7 reduce-precision_convert_fusion.1
  2.1 0.9 fusion.23
  3.9 0.5 collective-permute-start
  4.5 0.9 collective-permute-done
  5.4 0.3 copy.57
  6.5 5.0 %collective-permute-start.3 = (bf16[24,2176]{1,0:T(8,128)(2,1)S(1)}, bf16[24,2176]{1,0:T(8,128)(2,1)S(1)}, u32[]{:S(2)}, u32[]{:S(2)}) collective-permute-start(bf16[24,2176]{1,0:T(8,128)(2,1)S(1)} %pad_maximum_fusion.2), channel_id=1, source_target_pairs={{0,6},{2,4},{4,2},{6,0},{1,7},{3,5},{5,3},{7,1},{8,14},{10,12},{12... | collective-permute-start | bytes 313352 | tf_op jit(solution)/shard_map/ppermute | solution.py:24
  11.6 0.6 collective-permute-start.1
  12.2 3.2 %collective-permute-done.3 = bf16[24,2176]{1,0:T(8,128)(2,1)S(1)} collective-permute-done((bf16[24,2176]{1,0:T(8,128)(2,1)S(1)}, bf16[24,2176]{1,0:T(8,128)(2,1)S(1)}, u32[]{:S(2)}, u32[]{:S(2)}) %collective-permute-start.3) | collective-permute-done | bytes 104480 | tf_op jit(solution)/shard_map/ppermute | solution.py:24
  15.4 5.3 %collective-permute-done.2 = bf16[24,2176]{1,0:T(8,128)(2,1)S(1)} collective-permute-done((bf16[24,2176]{1,0:T(8,128)(2,1)S(1)}, bf16[24,2176]{1,0:T(8,128)(2,1)S(1)}, u32[]{:S(2)}, u32[]{:S(2)}) %collective-permute-start.2) | collective-permute-done | bytes 104480 | tf_op jit(solution)/shard_map/ppermute | solution.py:24
  21.0 2.5 %collective-permute-start.6 = (bf16[96,2176]{1,0:T(8,128)(2,1)S(1)}, bf16[96,2176]{1,0:T(8,128)(2,1)}, u32[]{:S(2)}, u32[]{:S(2)}) collective-permute-start(bf16[96,2176]{1,0:T(8,128)(2,1)S(1)} %concatenate.30), channel_id=1, source_target_pairs={{0,24},{8,16},{16,8},{24,0},{1,25},{9,17},{17,9},{25,1},{2,26},{10... | collective-permute-start | bytes 1253384 | tf_op jit(solution)/shard_map/ppermute | solution.py:24
  23.5 0.5 collective-permute-start.5
  24.0 0.5 collective-permute-start.4
  24.8 1.1 copy.64
  25.9 1.1 copy.63
  27.0 7.7 %collective-permute-done.6 = bf16[96,2176]{1,0:T(8,128)(2,1)} collective-permute-done((bf16[96,2176]{1,0:T(8,128)(2,1)S(1)}, bf16[96,2176]{1,0:T(8,128)(2,1)}, u32[]{:S(2)}, u32[]{:S(2)}) %collective-permute-start.6) | collective-permute-done | bytes 417824 | tf_op jit(solution)/shard_map/ppermute | solution.py:24
  34.6 2.1 %copy.68 = bf16[96,2176]{0,1:T(8,128)(2,1)} copy(bf16[96,2176]{1,0:T(8,128)(2,1)} %collective-permute-done.6) | data formatting | bytes 835584 | tf_op jit(solution)/shard_map/ppermute | solution.py:24
  36.7 5.1 %collective-permute-done.5 = bf16[96,2176]{1,0:T(8,128)(2,1)} collective-permute-done((bf16[96,2176]{1,0:T(8,128)(2,1)S(1)}, bf16[96,2176]{1,0:T(8,128)(2,1)}, u32[]{:S(2)}, u32[]{:S(2)}) %collective-permute-start.5) | collective-permute-done | bytes 417824 | tf_op jit(solution)/shard_map/ppermute | solution.py:24
  41.9 2.1 %copy.67 = bf16[96,2176]{0,1:T(8,128)(2,1)} copy(bf16[96,2176]{1,0:T(8,128)(2,1)} %collective-permute-done.5) | data formatting | bytes 835584 | tf_op jit(solution)/shard_map/ppermute | solution.py:24
  43.9 1.1 copy.66
  45.0 6.0 %concatenate.31 = bf16[384,2176]{0,1:T(8,128)(2,1)S(1)} concatenate(bf16[12,2176]{0,1:T(8,128)(2,1)S(1)} %get-tuple-element.10, bf16[12,2176]{0,1:T(8,128)(2,1)S(1)} %get-tuple-element.9, bf16[24,2176]{0,1:T(8,128)(2,1)} %copy.63, bf16[24,2176]{0,1:T(8,128)(2,1)} %copy.64, bf16[24,2176]{0,1:T(8,128)(2,1)S(1)} %copy.65, bf16[96,2176]{0,1:T(8,128)(2,1)} %copy.66, ...), dimensions={0} | concatenate | bytes 3342336 | tf_op jit(solution)/shard_map/concatenate | solution.py:35
  51.0 1.3 slice.96
  52.5 3.6 %collective-permute-done.7 = bf16[384,2048]{0,1:T(8,128)(2,1)} collective-permute-done((bf16[384,2048]{0,1:T(8,128)(2,1)}, bf16[384,2048]{0,1:T(8,128)(2,1)}, u32[]{:S(2)}, u32[]{:S(2)}) %collective-permute-start.7) | collective-permute-done | bytes 1572896 | tf_op jit(solution)/shard_map/ppermute | solution.py:24
  56.1 1.8 %broadcast_select_fusion.2 = (bf16[384,2048]{0,1:T(8,128)(2,1)S(1)}, bf16[384,2048]{0,1:T(8,128)(2,1)S(1)}) fusion(bf16[384,2048]{0,1:T(8,128)(2,1)} %collective-permute-done.7, pred[]{:T(512)S(6)} %eq.85, bf16[384,2176]{0,1:T(8,128)(2,1)S(1)} %concatenate.31), kind=kLoop, calls=%fused_computation.8 | loop fusion | flops 1572864 | bytes 6291457 | tf_op jit(solution)/shard_map/jit(_where)/select_n | solution.py:83
  58.0 8.6 %fusion = f32[384,2,768]{2,0,1:T(8,128)S(1)} fusion(bf16[2,4096,768]{2,1,0:T(8,128)(2,1)} %param.9, bf16[384,2048]{0,1:T(8,128)(2,1)S(1)} %get-tuple-element.5, bf16[384,2048]{0,1:T(8,128)(2,1)S(1)} %get-tuple-element.4), kind=kOutput, calls=%fused_computation.2 | convolution fusion | flops 4838129664 | bytes 18087936 | tf_op jit(solution)/shard_map/td,sdf->tsf/dot_general | solution.py:112
  66.6 4.1 %bitcast_convert_fusion = bf16[384,4096]{0,1:T(8,128)(2,1)S(1)} fusion(bf16[2,384,4096]{2,1,0:T(8,128)(2,1)S(1)} %bitcast.12, f32[384,2,768]{2,0,1:T(8,128)S(1)} %fusion, f32[384,2]{0,1:T(2,128)S(1)} %select_reduce_fusion.3), kind=kOutput, calls=%fused_computation | convolution fusion | flops 2419556352 | bytes 11799552 | tf_op jit(solution)/shard_map/tsf,sfd->td/dot_general | solution.py:115
  70.7 1.3 broadcast_select_fusion
  72.3 3.5 %collective-permute-done.8 = bf16[384,2048]{0,1:T(8,128)(2,1)} collective-permute-done((bf16[384,2048]{0,1:T(8,128)(2,1)}, bf16[384,2048]{0,1:T(8,128)(2,1)}, u32[]{:S(2)}, u32[]{:S(2)}) %collective-permute-start.8) | collective-permute-done | bytes 1572896 | tf_op jit(solution)/shard_map/ppermute | solution.py:24
  75.8 2.0 %add_convert_fusion = bf16[384,2048]{0,1:T(8,128)(2,1)S(1)} fusion(bf16[384,2048]{0,1:T(8,128)(2,1)} %collective-permute-done.8, pred[]{:T(512)S(6)} %eq.85, bf16[384,4096]{0,1:T(8,128)(2,1)S(1)} %bitcast_convert_fusion), kind=kLoop, calls=%fused_computation.5 | loop fusion | flops 3932160 | bytes 6291457 | tf_op jit(solution)/shard_map/convert_element_type | solution.py:122
  77.8 0.5 fusion.21
  78.4 0.6 copy-done
  79.0 1.5 collective-permute-start.9
  80.5 1.5 collective-permute-start.11
  82.0 0.5 collective-permute-start.10
  83.2 10.5 %collective-permute-done.9 = bf16[96,2048]{0,1:T(8,128)(2,1)S(1)} collective-permute-done((bf16[96,2048]{0,1:T(8,128)(2,1)S(1)}, bf16[96,2048]{0,1:T(8,128)(2,1)S(1)}, u32[]{:S(2)}, u32[]{:S(2)}) %collective-permute-start.9) | collective-permute-done | bytes 393248 | tf_op jit(solution)/shard_map/ppermute | solution.py:24
  93.7 11.5 %collective-permute-done.11 = bf16[96,2048]{0,1:T(8,128)(2,1)S(1)} collective-permute-done((bf16[96,2048]{0,1:T(8,128)(2,1)S(1)}, bf16[96,2048]{0,1:T(8,128)(2,1)S(1)}, u32[]{:S(2)}, u32[]{:S(2)}) %collective-permute-start.11) | collective-permute-done | bytes 393248 | tf_op jit(solution)/shard_map/ppermute | solution.py:24
  105.2 1.4 collective-permute-done.10
  106.6 1.3 add_convert_fusion.2
  107.9 0.5 fusion.22
  108.4 0.5 collective-permute-start.12
  108.9 2.2 %collective-permute-start.14 = (bf16[24,2048]{0,1:T(8,128)(2,1)S(1)}, bf16[24,2048]{0,1:T(8,128)(2,1)S(1)}, u32[]{:S(2)}, u32[]{:S(2)}) collective-permute-start(bf16[24,2048]{0,1:T(8,128)(2,1)S(1)} %get-tuple-element.16), channel_id=1, source_target_pairs={{0,6},{2,4},{4,2},{6,0},{1,7},{3,5},{5,3},{7,1},{8,14},{10,12},{12... | collective-permute-start | bytes 294920 | tf_op jit(solution)/shard_map/ppermute | solution.py:24
  111.0 0.9 collective-permute-start.13
  112.1 18.7 %collective-permute-done.12 = bf16[24,2048]{0,1:T(8,128)(2,1)S(1)} collective-permute-done((bf16[24,2048]{0,1:T(8,128)(2,1)S(1)}, bf16[24,2048]{0,1:T(8,128)(2,1)S(1)}, u32[]{:S(2)}, u32[]{:S(2)}) %collective-permute-start.12) | collective-permute-done | bytes 98336 | tf_op jit(solution)/shard_map/ppermute | solution.py:24
  130.8 4.3 %collective-permute-done.14 = bf16[24,2048]{0,1:T(8,128)(2,1)S(1)} collective-permute-done((bf16[24,2048]{0,1:T(8,128)(2,1)S(1)}, bf16[24,2048]{0,1:T(8,128)(2,1)S(1)}, u32[]{:S(2)}, u32[]{:S(2)}) %collective-permute-start.14) | collective-permute-done | bytes 98336 | tf_op jit(solution)/shard_map/ppermute | solution.py:24
  135.1 20.0 %collective-permute-done.13 = bf16[24,2048]{0,1:T(8,128)(2,1)S(1)} collective-permute-done((bf16[24,2048]{0,1:T(8,128)(2,1)S(1)}, bf16[24,2048]{0,1:T(8,128)(2,1)S(1)}, u32[]{:S(2)}, u32[]{:S(2)}) %collective-permute-start.13) | collective-permute-done | bytes 98336 | tf_op jit(solution)/shard_map/ppermute | solution.py:24
  155.7 0.5 broadcast_multiply_fusion
  156.2 1.4 collective-permute-done.15
  158.3 0.7 pad_maximum_fusion.1
  (49 shorter events, 4.9 us)
Async XLA Ops:
  3.9 1.4 collective-permute-start
  6.5 8.8 %collective-permute-start.3 = (bf16[24,2176]{1,0:T(8,128)(2,1)S(1)}, bf16[24,2176]{1,0:T(8,128)(2,1)S(1)}, u32[]{:S(2)}, u32[]{:S(2)}) collective-permute-start(bf16[24,2176]{1,0:T(8,128)(2,1)S(1)} %pad_maximum_fusion.2), channel_id=1, source_target_pairs={{0,6},{2,4},{4,2},{6,0},{1,7},{3,5},{5,3},{7,1},{8,14},{10,12},{12... | collective-permute-start | bytes 313352 | tf_op jit(solution)/shard_map/ppermute | solution.py:24
  11.6 9.1 %collective-permute-start.2 = (bf16[24,2176]{1,0:T(8,128)(2,1)S(1)}, bf16[24,2176]{1,0:T(8,128)(2,1)S(1)}, u32[]{:S(2)}, u32[]{:S(2)}) collective-permute-start(bf16[24,2176]{1,0:T(8,128)(2,1)S(1)} %pad_maximum_fusion.2), channel_id=1, source_target_pairs={{0,4},{2,6},{4,0},{6,2},{1,5},{3,7},{5,1},{7,3},{8,12},{10,14},{12... | collective-permute-start | bytes 313352 | tf_op jit(solution)/shard_map/ppermute | solution.py:24
  11.6 9.1 %collective-permute-start.1 = (bf16[24,2176]{1,0:T(8,128)(2,1)S(1)}, bf16[24,2176]{1,0:T(8,128)(2,1)S(1)}, u32[]{:S(2)}, u32[]{:S(2)}) collective-permute-start(bf16[24,2176]{1,0:T(8,128)(2,1)S(1)} %pad_maximum_fusion.2), channel_id=1, source_target_pairs={{0,2},{2,0},{4,6},{6,4},{1,3},{3,1},{5,7},{7,5},{8,10},{10,8},{12,... | collective-permute-start | bytes 313352 | tf_op jit(solution)/shard_map/ppermute | solution.py:24
  21.0 13.7 %collective-permute-start.6 = (bf16[96,2176]{1,0:T(8,128)(2,1)S(1)}, bf16[96,2176]{1,0:T(8,128)(2,1)}, u32[]{:S(2)}, u32[]{:S(2)}) collective-permute-start(bf16[96,2176]{1,0:T(8,128)(2,1)S(1)} %concatenate.30), channel_id=1, source_target_pairs={{0,24},{8,16},{16,8},{24,0},{1,25},{9,17},{17,9},{25,1},{2,26},{10... | collective-permute-start | bytes 1253384 | tf_op jit(solution)/shard_map/ppermute | solution.py:24
  23.5 18.4 %collective-permute-start.5 = (bf16[96,2176]{1,0:T(8,128)(2,1)S(1)}, bf16[96,2176]{1,0:T(8,128)(2,1)}, u32[]{:S(2)}, u32[]{:S(2)}) collective-permute-start(bf16[96,2176]{1,0:T(8,128)(2,1)S(1)} %concatenate.30), channel_id=1, source_target_pairs={{0,16},{8,24},{16,0},{24,8},{1,17},{9,25},{17,1},{25,9},{2,18},{10... | collective-permute-start | bytes 1253384 | tf_op jit(solution)/shard_map/ppermute | solution.py:24
  24.0 19.9 %collective-permute-start.4 = (bf16[96,2176]{1,0:T(8,128)(2,1)S(1)}, bf16[96,2176]{1,0:T(8,128)(2,1)S(1)}, u32[]{:S(2)}, u32[]{:S(2)}) collective-permute-start(bf16[96,2176]{1,0:T(8,128)(2,1)S(1)} %concatenate.30), channel_id=1, source_target_pairs={{0,8},{8,0},{16,24},{24,16},{1,9},{9,1},{17,25},{25,17},{2,10},{10... | collective-permute-start | bytes 1253384 | tf_op jit(solution)/shard_map/ppermute | solution.py:24
  52.3 3.8 %collective-permute-start.7 = (bf16[384,2048]{0,1:T(8,128)(2,1)}, bf16[384,2048]{0,1:T(8,128)(2,1)}, u32[]{:S(2)}, u32[]{:S(2)}) collective-permute-start(bf16[384,2048]{0,1:T(8,128)(2,1)} %slice.96), channel_id=1, source_target_pairs={{0,1},{1,0},{2,3},{3,2},{4,5},{5,4},{6,7},{7,6},{8,9},{9,8},{10,11... | collective-permute-start | bytes 4718600 | tf_op jit(solution)/shard_map/ppermute | solution.py:24
  56.1 10.5 %slice-start = ((s8[6291456]{0:T(1024)(128)(4,1)}), s8[4194304]{0:T(1024)(128)(4,1)S(1)}, s32[]{:S(2)}) async-start(s8[6291456]{0:T(1024)(128)(4,1)} %bitcast.11), calls=%async_computation | async-start | bytes 8388608
  57.9 8.7 %slice-start.1 = ((s8[6291456]{0:T(1024)(128)(4,1)}), s8[2097152]{0:T(1024)(128)(4,1)S(1)}, s32[]{:S(2)}) async-start(s8[6291456]{0:T(1024)(128)(4,1)} %bitcast.11), calls=%async_computation.1 | async-start | bytes 4194304
  70.7 1.5 copy-start.1
  72.1 3.8 %collective-permute-start.8 = (bf16[384,2048]{0,1:T(8,128)(2,1)}, bf16[384,2048]{0,1:T(8,128)(2,1)}, u32[]{:S(2)}, u32[]{:S(2)}) collective-permute-start(bf16[384,2048]{0,1:T(8,128)(2,1)} %broadcast_select_fusion), channel_id=1, source_target_pairs={{0,1},{1,0},{2,3},{3,2},{4,5},{5,4},{6,7},{7,6},{8,9},{9,8},{10,11... | collective-permute-start | bytes 4718600 | tf_op jit(solution)/shard_map/ppermute | solution.py:24
  77.8 1.2 copy-start
  79.0 14.8 %collective-permute-start.9 = (bf16[96,2048]{0,1:T(8,128)(2,1)S(1)}, bf16[96,2048]{0,1:T(8,128)(2,1)S(1)}, u32[]{:S(2)}, u32[]{:S(2)}) collective-permute-start(bf16[96,2048]{0,1:T(8,128)(2,1)S(1)} %get-tuple-element.6), channel_id=1, source_target_pairs={{0,8},{8,0},{16,24},{24,16},{1,9},{9,1},{17,25},{25,17},{2,10},{10... | collective-permute-start | bytes 1179656 | tf_op jit(solution)/shard_map/ppermute | solution.py:24
  80.5 24.8 %collective-permute-start.11 = (bf16[96,2048]{0,1:T(8,128)(2,1)S(1)}, bf16[96,2048]{0,1:T(8,128)(2,1)S(1)}, u32[]{:S(2)}, u32[]{:S(2)}) collective-permute-start(bf16[96,2048]{0,1:T(8,128)(2,1)S(1)} %get-tuple-element.7), channel_id=1, source_target_pairs={{0,24},{8,16},{16,8},{24,0},{1,25},{9,17},{17,9},{25,1},{2,26},{10... | collective-permute-start | bytes 1179656 | tf_op jit(solution)/shard_map/ppermute | solution.py:24
  82.0 24.6 %collective-permute-start.10 = (bf16[96,2048]{0,1:T(8,128)(2,1)S(1)}, bf16[96,2048]{0,1:T(8,128)(2,1)S(1)}, u32[]{:S(2)}, u32[]{:S(2)}) collective-permute-start(bf16[96,2048]{0,1:T(8,128)(2,1)S(1)} %get-tuple-element.8), channel_id=1, source_target_pairs={{0,16},{8,24},{16,0},{24,8},{1,17},{9,25},{17,1},{25,9},{2,18},{10... | collective-permute-start | bytes 1179656 | tf_op jit(solution)/shard_map/ppermute | solution.py:24
  108.4 22.4 %collective-permute-start.12 = (bf16[24,2048]{0,1:T(8,128)(2,1)S(1)}, bf16[24,2048]{0,1:T(8,128)(2,1)S(1)}, u32[]{:S(2)}, u32[]{:S(2)}) collective-permute-start(bf16[24,2048]{0,1:T(8,128)(2,1)S(1)} %get-tuple-element.15), channel_id=1, source_target_pairs={{0,2},{2,0},{4,6},{6,4},{1,3},{3,1},{5,7},{7,5},{8,10},{10,8},{12,... | collective-permute-start | bytes 294920 | tf_op jit(solution)/shard_map/ppermute | solution.py:24
  108.9 26.3 %collective-permute-start.14 = (bf16[24,2048]{0,1:T(8,128)(2,1)S(1)}, bf16[24,2048]{0,1:T(8,128)(2,1)S(1)}, u32[]{:S(2)}, u32[]{:S(2)}) collective-permute-start(bf16[24,2048]{0,1:T(8,128)(2,1)S(1)} %get-tuple-element.16), channel_id=1, source_target_pairs={{0,6},{2,4},{4,2},{6,0},{1,7},{3,5},{5,3},{7,1},{8,14},{10,12},{12... | collective-permute-start | bytes 294920 | tf_op jit(solution)/shard_map/ppermute | solution.py:24
  111.0 44.1 %collective-permute-start.13 = (bf16[24,2048]{0,1:T(8,128)(2,1)S(1)}, bf16[24,2048]{0,1:T(8,128)(2,1)S(1)}, u32[]{:S(2)}, u32[]{:S(2)}) collective-permute-start(bf16[24,2048]{0,1:T(8,128)(2,1)S(1)} %get-tuple-element.17), channel_id=1, source_target_pairs={{0,4},{2,6},{4,0},{6,2},{1,5},{3,7},{5,1},{7,3},{8,12},{10,14},{12... | collective-permute-start | bytes 294920 | tf_op jit(solution)/shard_map/ppermute | solution.py:24
  155.6 2.0 %collective-permute-start.15 = (bf16[12,2048]{0,1:T(8,128)(2,1)S(1)}, bf16[12,2048]{0,1:T(8,128)(2,1)S(1)}, u32[]{:S(2)}, u32[]{:S(2)}) collective-permute-start(bf16[12,2048]{0,1:T(8,128)(2,1)S(1)} %broadcast_select_fusion.7), channel_id=1, source_target_pairs={{0,1},{1,0},{2,3},{3,2},{4,5},{5,4},{6,7},{7,6},{8,9},{9,8},{10,11... | collective-permute-start | bytes 147464 | tf_op jit(solution)/shard_map/ppermute | solution.py:24

commit v3 on v2

v3 whole, which is shorter than its diff:
```python
import jax
import jax.numpy as jnp
from jax import lax
from jax.experimental.layout import Layout, with_layout_constraint
from jax.sharding import Mesh, PartitionSpec as P

LANES = 128


def lookup_small(values_table, index_array):
    columns = jnp.arange(values_table.shape[0], dtype=jnp.int32)
    return jnp.sum(jnp.where(index_array[..., None] == columns, values_table, 0), -1)


def planned_holder(expert_index, swap_slot, per_device, owners):
    home = expert_index // per_device
    within = expert_index % per_device
    partner = (home + owners // 2) % owners
    moved = within == lookup_small(swap_slot, home)
    return jnp.where(moved, partner, home)


def row_major(value):
    return with_layout_constraint(value, Layout(major_to_minor=tuple(range(value.ndim))))


def swap(value, axis, distance):
    size = lax.axis_size(axis)
    pairs = [(i, i ^ distance) for i in range(size)]
    return row_major(lax.ppermute(row_major(value), axis, pairs))


def split_gates(gates):
    high = lax.reduce_precision(gates, 8, 7)
    middle = lax.reduce_precision(gates - high, 8, 7)
    return [part.astype(jnp.bfloat16) for part in (high, middle, gates - high - middle)]


def spread(block):
    size = lax.axis_size("dp")
    if size != 4:
        return [block] + [swap(block, "dp", k) for k in range(1, size)]
    cut = block.shape[1] // (2 * LANES) * LANES
    near = [swap(block, "dp", 1), swap(block, "dp", 2)]
    far = [swap(near[0][:, :cut], "dp", 2), swap(near[1][:, cut:], "dp", 1)]
    return [block, *near, jnp.concatenate(far, 1)]


def wide(value):
    return value.astype(jnp.float32)


def collected(blocks):
    size = lax.axis_size("dp")
    if size != 4:
        total = wide(blocks[0])
        for k in range(1, size):
            total = total + wide(swap(blocks[k], "dp", k))
        return total.astype(jnp.bfloat16)
    own, one, two, both = blocks
    cut = own.shape[1] // (2 * LANES) * LANES
    upper = swap(both[:, :cut], "dp", 2)
    lower = swap(both[:, cut:], "dp", 1)
    one = jnp.concatenate(
        [(wide(one[:, :cut]) + wide(upper)).astype(jnp.bfloat16), one[:, cut:]], 1
    )
    two = jnp.concatenate(
        [two[:, :cut], (wide(two[:, cut:]) + wide(lower)).astype(jnp.bfloat16)], 1
    )
    total = wide(own) + wide(swap(one, "dp", 1)) + wide(swap(two, "dp", 2))
    return total.astype(jnp.bfloat16)


def in_order(blocks):
    for dim, axis in enumerate(("dp", "chip")):
        size = lax.axis_size(axis)
        here = jnp.arange(size, dtype=jnp.int32)
        match = (here[:, None] ^ here[None, :]) == lax.axis_index(axis)
        moved = jnp.moveaxis(blocks, dim, 0)
        picked = jnp.sum(jnp.where(match[..., None, None], moved[None], jnp.float32(0.0)), 1)
        blocks = jnp.moveaxis(picked, 0, dim)
    return blocks


def on_device(tokens, expert_ids, gate_probs, in_weight, out_weight, swap_slot):
    groups, chips = lax.axis_size("dp"), lax.axis_size("chip")
    owners = 2 * chips
    per_device = in_weight.shape[0]
    rows, width = tokens.shape
    part = width // 2
    top_count = expert_ids.shape[1]
    experts_all = per_device * owners
    half_width = out_weight.shape[1]
    core = lax.axis_index("core")
    first = core == 0
    all_experts = jnp.arange(experts_all, dtype=jnp.int32)
    home = lax.axis_index("chip") * 2 + core

    routing = jnp.concatenate(
        [row_major(expert_ids).astype(jnp.bfloat16), *split_gates(row_major(gate_probs))], 1
    )
    routing = row_major(jnp.pad(routing, ((0, 0), (0, LANES - routing.shape[1]))))
    left, right = tokens[:, :part], tokens[:, part:]
    keep = jnp.concatenate([jnp.where(first, left, right), routing], 1)
    give = jnp.concatenate([jnp.where(first, right, left), routing], 1)
    taken = swap(give, "core", 1)
    chip_rows = row_major(
        jnp.concatenate([jnp.where(first, keep, taken), jnp.where(first, taken, keep)], 0)
    )

    def routes(meta):
        ids = meta[:, :top_count].astype(jnp.int32)
        gates = sum(
            wide(meta[:, (i + 1) * top_count : (i + 2) * top_count]) for i in range(3)
        )
        return jnp.sum(
            jnp.where(ids[..., None] == all_experts, gates[..., None], jnp.float32(0.0)), 1
        )

    def expert_sum(held, own_gates):
        hidden = []
        for s in range(per_device):
            both = jnp.dot(held, in_weight[s], preferred_element_type=jnp.float32)
            unit = jax.nn.silu(both[:, :half_width]) * both[:, half_width:]
            hidden.append((unit * own_gates[:, s : s + 1]).astype(jnp.bfloat16))
        return jnp.dot(
            jnp.concatenate(hidden, 1),
            out_weight.reshape(per_device * half_width, width),
            preferred_element_type=jnp.float32,
        ).astype(jnp.bfloat16)

    chip_totals, returned = [], []
    for j in range(chips):
        block = chip_rows if j == 0 else swap(chip_rows, "chip", j)
        held = row_major(jnp.concatenate(spread(block), 0))
        own_half = held[:, :part]
        other_half = swap(own_half, "core", 1)
        held_tokens = row_major(
            jnp.concatenate(
                [
                    jnp.where(first, own_half, other_half),
                    jnp.where(first, other_half, own_half),
                ],
                1,
            )
        )
        dense_gates = routes(held[:, part:])
        chip_totals.append(jnp.sum(dense_gates.reshape(groups, 2 * rows, experts_all), 1))
        own = home * per_device + jnp.arange(per_device, dtype=jnp.int32)
        own_gates = jnp.sum(
            jnp.where(all_experts[:, None] == own, dense_gates[..., None], jnp.float32(0.0)), 1
        )
        summed = row_major(expert_sum(held_tokens, own_gates))
        left, right = summed[:, :part], summed[:, part:]
        arrived = swap(jnp.where(first, right, left), "core", 1)
        chip_sum = (wide(jnp.where(first, left, right)) + wide(arrived)).astype(jnp.bfloat16)
        chip_sum = row_major(chip_sum).reshape(groups, 2 * rows, part)
        block = collected([chip_sum[k] for k in range(groups)])
        returned.append(block if j == 0 else swap(block, "chip", j))

    total = sum(wide(block) for block in returned).astype(jnp.bfloat16)
    upper, lower = total[:rows], total[rows:]
    arrived = swap(jnp.where(first, lower, upper), "core", 1)
    kept = jnp.where(first, upper, lower)
    mixed_out = row_major(
        jnp.concatenate([jnp.where(first, kept, arrived), jnp.where(first, arrived, kept)], 1)
    )

    totals = jnp.sum(in_order(jnp.stack(chip_totals, 1)), (0, 1))
    holder = planned_holder(all_experts, swap_slot, per_device, owners)
    owner_load = jnp.sum(
        jnp.where(
            holder == jnp.arange(owners, dtype=jnp.int32)[:, None], totals[None, :], jnp.float32(0.0)
        ),
        1,
    ) * (owners / (groups * owners * rows))
    return (mixed_out, owner_load)


def solution(mesh):
    groups, owners = mesh.devices.shape
    fine = Mesh(mesh.devices.reshape(groups, owners // 2, 2), ("dp", "chip", "core"))
    rows = P(("dp", "chip", "core"), None)
    return jax.shard_map(
        on_device,
        mesh=fine,
        in_specs=(
            rows,
            rows,
            rows,
            P(("chip", "core"), None, "dp"),
            P(("chip", "core"), "dp", None),
            P(),
        ),
        out_specs=(rows, P()),
        check_vma=False,
    )
```

time: 159 us -> 109 us (0.69)
  waiting for transfers between devices: 97.1 us -> 21.3 us
  starting transfers between devices: 17 us -> 44.3 us
  local copies, waits for them, and re-layouts: 20.3 us -> 5.91 us
  matrix products: 12.7 us -> 19.8 us
  other arithmetic: 11 us -> 15.9 us
    ppermute x16 -> x48, waiting for transfers between devices: 97.1 us -> 21.3 us  [swap(): return row_major(lax.ppermute(row_major(value), axis, pairs))]
    ppermute x16 -> x48, starting transfers between devices: 17 us -> 44.3 us  [swap(): return row_major(lax.ppermute(row_major(value), axis, pairs))]
    ppermute x7 -> x0, local copies, waits for them, and re-layouts: 8.01 us -> none  [swap(): return lax.ppermute(value, axis, [(i, i ^ distance) for i in range(size)])]
    dot_general x2 -> x12, matrix products: 12.7 us -> 19.8 us  [the longest x8 15 us: expert_sum(): both = jnp.dot(held, in_weight[s], preferred_element_type=jnp.float32)]
    concatenate x2 -> x0, local copies, waits for them, and re-layouts: 6.32 us -> none  [gathered(): return jnp.concatenate(pieces, 0)]
    reduce_sum x4 -> x8, other arithmetic: 0.38 us -> 3.54 us  [the longest x4 2.64 us: on_device(): jnp.sum(dense_gates.reshape(groups, 2 * rows, experts_all), 1)]
    slice x4 -> x16, local copies, waits for them, and re-layouts: 3.21 us -> 0.24 us  [the longest x4 0.13 us: on_device(): own_half = held[:, :part]]
    convert_element_type x6 -> x25, other arithmetic: 4.35 us -> 1.64 us  [the longest x8 0.67 us: expert_sum(): hidden.append((unit * own_gates[:, s:s + 1]).astype(jnp.bfloat16))]
  transfers between devices with their start and end apart: 16 -> 48, of which waited for: 14 -> 23; matrix products, arithmetic and copies ran while one was open for 5% -> 35% of each run, Pallas kernels for 0% -> 0%
where the time goes in v3:
time: 109 us
  starting transfers between devices  44.3 us (41%)
  waiting for transfers between devices  21.3 us (20%)
  matrix products  19.8 us (18%)
  other arithmetic  15.9 us (15%)
  local copies, waits for them, and re-layouts  5.91 us (5%)
  between operations  1.38 us (1%)
    ppermute x48, starting transfers between devices, swap(): return row_major(lax.ppermute(row_major(value), axis, pairs))  44.3 us
    ppermute x48, waiting for transfers between devices, swap(): return row_major(lax.ppermute(row_major(value), axis, pairs))  21.3 us
    dot_general x8, matrix products, expert_sum(): both = jnp.dot(held, in_weight[s], preferred_element_type=jnp.float32)  15 us
    dot_general x4, matrix products, expert_sum(): jnp.dot(jnp.concatenate(hidden, 1), out_weight.reshape(per_device * half_...  4.79 us
    select_n x4, other arithmetic, on_device(): jnp.where(first, own_half, other_half)  4.27 us
    reduce_sum x4, other arithmetic, on_device(): jnp.sum(dense_gates.reshape(groups, 2 * rows, experts_all), 1)  2.64 us
  transfers between devices with their start and end apart: 48, of which 23 were waited for; matrix products, arithmetic and copies ran while one was open for 35% of the time, Pallas kernels for 0%

profile of v3, /device:TPU:0, one launch (start us, length us, event | category | flops | bytes accessed | tf_op | source)
XLA Modules:
  0.0 108.7 jit_solution(673992275266039914)
XLA Ops:
  2.2 0.9 broadcast_select_fusion.19
  5.2 2.6 %collective-permute-start.2 = (bf16[24,2176]{1,0:T(8,128)(2,1)S(1)}, bf16[24,2176]{1,0:T(8,128)(2,1)S(1)}, u32[]{:S(2)}, u32[]{:S(2)}) collective-permute-start(bf16[24,2176]{1,0:T(8,128)(2,1)S(1)} %pad_maximum_fusion.13), channel_id=1, source_target_pairs={{0,16},{8,24},{16,0},{24,8},{1,17},{9,25},{17,1},{25,9},{2,18},{10... | collective-permute-start | bytes 313352 | tf_op jit(solution)/shard_map/ppermute | solution.py:30
  7.8 1.5 %collective-permute-start.1 = (bf16[24,2176]{1,0:T(8,128)(2,1)S(1)}, bf16[24,2176]{1,0:T(8,128)(2,1)S(1)}, u32[]{:S(2)}, u32[]{:S(2)}) collective-permute-start(bf16[24,2176]{1,0:T(8,128)(2,1)S(1)} %pad_maximum_fusion.13), channel_id=1, source_target_pairs={{0,8},{8,0},{16,24},{24,16},{1,9},{9,1},{17,25},{25,17},{2,10},{10... | collective-permute-start | bytes 313352 | tf_op jit(solution)/shard_map/ppermute | solution.py:30
  9.9 3.6 %collective-permute-start.35 = (bf16[24,2176]{1,0:T(8,128)(2,1)S(1)}, bf16[24,2176]{1,0:T(8,128)(2,1)S(1)}, u32[]{:S(2)}, u32[]{:S(2)}) collective-permute-start(bf16[24,2176]{1,0:T(8,128)(2,1)S(1)} %pad_maximum_fusion.13), channel_id=1, source_target_pairs={{0,6},{2,4},{4,2},{6,0},{1,7},{3,5},{5,3},{7,1},{8,14},{10,12},{12... | collective-permute-start | bytes 313352 | tf_op jit(solution)/shard_map/ppermute | solution.py:30
  15.8 1.7 %collective-permute-done.35 = bf16[24,2176]{1,0:T(8,128)(2,1)S(1)} collective-permute-done((bf16[24,2176]{1,0:T(8,128)(2,1)S(1)}, bf16[24,2176]{1,0:T(8,128)(2,1)S(1)}, u32[]{:S(2)}, u32[]{:S(2)}) %collective-permute-start.35) | collective-permute-done | bytes 104480 | tf_op jit(solution)/shard_map/ppermute | solution.py:30
  18.0 1.7 %collective-permute-done.11 = bf16[24,2176]{1,0:T(8,128)(2,1)S(1)} collective-permute-done((bf16[24,2176]{1,0:T(8,128)(2,1)S(1)}, bf16[24,2176]{1,0:T(8,128)(2,1)S(1)}, u32[]{:S(2)}, u32[]{:S(2)}) %collective-permute-start.11) | collective-permute-done | bytes 104480 | tf_op jit(solution)/shard_map/ppermute | solution.py:30
  20.2 2.1 %collective-permute-done.23 = bf16[24,2176]{1,0:T(8,128)(2,1)S(1)} collective-permute-done((bf16[24,2176]{1,0:T(8,128)(2,1)S(1)}, bf16[24,2176]{1,0:T(8,128)(2,1)S(1)}, u32[]{:S(2)}, u32[]{:S(2)}) %collective-permute-start.23) | collective-permute-done | bytes 104480 | tf_op jit(solution)/shard_map/ppermute | solution.py:30
  23.4 1.5 %collective-permute-start.25 = (bf16[24,2176]{1,0:T(8,128)(2,1)S(1)}, bf16[24,2176]{1,0:T(8,128)(2,1)S(1)}, u32[]{:S(2)}, u32[]{:S(2)}) collective-permute-start(bf16[24,2176]{1,0:T(8,128)(2,1)S(1)} %collective-permute-done.23), channel_id=1, source_target_pairs={{0,16},{8,24},{16,0},{24,8},{1,17},{9,25},{17,1},{25,9},{2,18},{10... | collective-permute-start | bytes 313352 | tf_op jit(solution)/shard_map/ppermute | solution.py:30
  25.1 1.6 %collective-permute-start.24 = (bf16[24,2176]{1,0:T(8,128)(2,1)S(1)}, bf16[24,2176]{1,0:T(8,128)(2,1)S(1)}, u32[]{:S(2)}, u32[]{:S(2)}) collective-permute-start(bf16[24,2176]{1,0:T(8,128)(2,1)S(1)} %collective-permute-done.23), channel_id=1, source_target_pairs={{0,8},{8,0},{16,24},{24,16},{1,9},{9,1},{17,25},{25,17},{2,10},{10... | collective-permute-start | bytes 313352 | tf_op jit(solution)/shard_map/ppermute | solution.py:30
  27.6 1.1 collective-permute-start.38
  30.1 1.4 %collective-permute-start.14 = (bf16[24,1024]{1,0:T(8,128)(2,1)S(1)}, bf16[24,1024]{1,0:T(8,128)(2,1)S(1)}, u32[]{:S(2)}, u32[]{:S(2)}) collective-permute-start(bf16[24,1024]{1,0:T(8,128)(2,1)S(1)} %slice.470), channel_id=1, source_target_pairs={{0,16},{8,24},{16,0},{24,8},{1,17},{9,25},{17,1},{25,9},{2,18},{10... | collective-permute-start | bytes 147464 | tf_op jit(solution)/shard_map/ppermute | solution.py:30
  31.7 1.2 %collective-permute-start.27 = (bf16[24,1152]{1,0:T(8,128)(2,1)S(1)}, bf16[24,1152]{1,0:T(8,128)(2,1)S(1)}, u32[]{:S(2)}, u32[]{:S(2)}) collective-permute-start(bf16[24,1152]{1,0:T(8,128)(2,1)S(1)} %slice.487), channel_id=1, source_target_pairs={{0,8},{8,0},{16,24},{24,16},{1,9},{9,1},{17,25},{25,17},{2,10},{10... | collective-permute-start | bytes 165896 | tf_op jit(solution)/shard_map/ppermute | solution.py:30
  34.7 2.3 %collective-permute-done.26 = bf16[24,1024]{1,0:T(8,128)(2,1)S(1)} collective-permute-done((bf16[24,1024]{1,0:T(8,128)(2,1)S(1)}, bf16[24,1024]{1,0:T(8,128)(2,1)S(1)}, u32[]{:S(2)}, u32[]{:S(2)}) %collective-permute-start.26) | collective-permute-done | bytes 49184 | tf_op jit(solution)/shard_map/ppermute | solution.py:30
  42.5 0.8 reduce_sum.158
  46.0 1.1 broadcast_select_fusion.11
  47.1 4.1 %fusion.6 = f32[96,768]{1,0:T(8,128)S(1)} fusion(bf16[2,4096,768]{2,1,0:T(8,128)(2,1)} %param.9, bf16[96,2048]{1,0:T(8,128)(2,1)S(1)} %get-tuple-element.7, bf16[96,2048]{1,0:T(8,128)(2,1)S(1)} %get-tuple-element.6), kind=kOutput, calls=%fused_computation.6 | convolution fusion | flops 605552640 | bytes 7372800 | tf_op jit(solution)/shard_map/dot_general | solution.py:123
  51.2 4.1 %fusion.14 = f32[96,768]{1,0:T(8,128)S(1)} fusion(bf16[2,4096,768]{2,1,0:T(8,128)(2,1)} %param.9, bf16[96,2048]{1,0:T(8,128)(2,1)S(1)} %get-tuple-element.7, bf16[96,2048]{1,0:T(8,128)(2,1)S(1)} %get-tuple-element.6), kind=kOutput, calls=%fused_computation.14 | convolution fusion | flops 605552640 | bytes 7372800 | tf_op jit(solution)/shard_map/dot_general | solution.py:123
  55.5 1.2 %convolution_convert_fusion.3 = bf16[96,4096]{1,0:T(8,128)(2,1)S(1)} fusion(bf16[768,4096]{1,0:T(8,128)(2,1)S(1)} %bitcast.54, bf16[96,384]{1,0:T(8,128)(2,1)S(1)} %fusion.37, bf16[96,384]{1,0:T(8,128)(2,1)S(1)} %fusion.39), kind=kOutput, calls=%fused_computation.19 | convolution fusion | flops 604667904 | bytes 7225344 | tf_op jit(solution)/shard_map/dot_general | solution.py:126
  56.8 1.1 broadcast_select_fusion.2
  57.9 1.1 %fusion = f32[96,768]{1,0:T(8,128)S(1)} fusion(bf16[2,4096,768]{2,1,0:T(8,128)(2,1)S(1)} %bitcast.64, bf16[96,2048]{1,0:T(8,128)(2,1)S(1)} %get-tuple-element.13, bf16[96,2048]{1,0:T(8,128)(2,1)S(1)} %get-tuple-element.12), kind=kOutput, calls=%fused_computation | convolution fusion | flops 605552640 | bytes 7372800 | tf_op jit(solution)/shard_map/dot_general | solution.py:123
  59.1 1.1 %fusion.8 = f32[96,768]{1,0:T(8,128)S(1)} fusion(bf16[2,4096,768]{2,1,0:T(8,128)(2,1)S(1)} %bitcast.64, bf16[96,2048]{1,0:T(8,128)(2,1)S(1)} %get-tuple-element.13, bf16[96,2048]{1,0:T(8,128)(2,1)S(1)} %get-tuple-element.12), kind=kOutput, calls=%fused_computation.8 | convolution fusion | flops 605552640 | bytes 7372800 | tf_op jit(solution)/shard_map/dot_general | solution.py:123
  60.2 1.1 broadcast_select_fusion.5
  61.3 1.1 %fusion.2 = f32[96,768]{1,0:T(8,128)S(1)} fusion(bf16[2,4096,768]{2,1,0:T(8,128)(2,1)S(1)} %bitcast.64, bf16[96,2048]{1,0:T(8,128)(2,1)S(1)} %get-tuple-element.11, bf16[96,2048]{1,0:T(8,128)(2,1)S(1)} %get-tuple-element.10), kind=kOutput, calls=%fused_computation.2 | convolution fusion | flops 605552640 | bytes 7372800 | tf_op jit(solution)/shard_map/dot_general | solution.py:123
  62.5 1.1 %fusion.10 = f32[96,768]{1,0:T(8,128)S(1)} fusion(bf16[2,4096,768]{2,1,0:T(8,128)(2,1)S(1)} %bitcast.64, bf16[96,2048]{1,0:T(8,128)(2,1)S(1)} %get-tuple-element.11, bf16[96,2048]{1,0:T(8,128)(2,1)S(1)} %get-tuple-element.10), kind=kOutput, calls=%fused_computation.10 | convolution fusion | flops 605552640 | bytes 7372800 | tf_op jit(solution)/shard_map/dot_general | solution.py:123
  63.6 1.1 broadcast_select_fusion.8
  64.7 1.1 %fusion.4 = f32[96,768]{1,0:T(8,128)S(1)} fusion(bf16[2,4096,768]{2,1,0:T(8,128)(2,1)S(1)} %bitcast.64, bf16[96,2048]{1,0:T(8,128)(2,1)S(1)} %get-tuple-element.9, bf16[96,2048]{1,0:T(8,128)(2,1)S(1)} %get-tuple-element.8), kind=kOutput, calls=%fused_computation.4 | convolution fusion | flops 605552640 | bytes 7372800 | tf_op jit(solution)/shard_map/dot_general | solution.py:123
  65.8 1.1 %fusion.12 = f32[96,768]{1,0:T(8,128)S(1)} fusion(bf16[2,4096,768]{2,1,0:T(8,128)(2,1)S(1)} %bitcast.64, bf16[96,2048]{1,0:T(8,128)(2,1)S(1)} %get-tuple-element.9, bf16[96,2048]{1,0:T(8,128)(2,1)S(1)} %get-tuple-element.8), kind=kOutput, calls=%fused_computation.12 | convolution fusion | flops 605552640 | bytes 7372800 | tf_op jit(solution)/shard_map/dot_general | solution.py:123
  67.2 1.3 %convolution_convert_fusion = bf16[96,4096]{1,0:T(8,128)(2,1)S(1)} fusion(bf16[768,4096]{1,0:T(8,128)(2,1)S(1)} %bitcast.55, bf16[96,384]{1,0:T(8,128)(2,1)S(1)} %fusion.25, bf16[96,384]{1,0:T(8,128)(2,1)S(1)} %fusion.27), kind=kOutput, calls=%fused_computation.16 | convolution fusion | flops 604667904 | bytes 7225344 | tf_op jit(solution)/shard_map/dot_general | solution.py:126
  69.3 1.1 %convolution_convert_fusion.1 = bf16[96,4096]{1,0:T(8,128)(2,1)S(1)} fusion(bf16[768,4096]{1,0:T(8,128)(2,1)S(1)} %bitcast.56, bf16[96,384]{1,0:T(8,128)(2,1)S(1)} %fusion.29, bf16[96,384]{1,0:T(8,128)(2,1)S(1)} %fusion.31), kind=kOutput, calls=%fused_computation.17 | convolution fusion | flops 604667904 | bytes 7225344 | tf_op jit(solution)/shard_map/dot_general | solution.py:126
  70.7 1.1 %convolution_convert_fusion.2 = bf16[96,4096]{1,0:T(8,128)(2,1)S(1)} fusion(bf16[768,4096]{1,0:T(8,128)(2,1)S(1)} %bitcast.57, bf16[96,384]{1,0:T(8,128)(2,1)S(1)} %fusion.33, bf16[96,384]{1,0:T(8,128)(2,1)S(1)} %fusion.35), kind=kOutput, calls=%fused_computation.18 | convolution fusion | flops 604667904 | bytes 7225344 | tf_op jit(solution)/shard_map/dot_general | solution.py:126
  72.7 1.4 %collective-permute-start.9 = (bf16[24,1024]{1,0:T(8,128)(2,1)S(1)}, bf16[24,1024]{1,0:T(8,128)(2,1)S(1)}, u32[]{:S(2)}, u32[]{:S(2)}) collective-permute-start(bf16[24,1024]{1,0:T(8,128)(2,1)S(1)} %get-tuple-element.19), channel_id=1, source_target_pairs={{0,8},{8,0},{16,24},{24,16},{1,9},{9,1},{17,25},{25,17},{2,10},{10... | collective-permute-start | bytes 147464 | tf_op jit(solution)/shard_map/ppermute | solution.py:30
  74.1 2.1 %collective-permute-done.7 = bf16[24,1024]{1,0:T(8,128)(2,1)S(1)} collective-permute-done((bf16[24,1024]{1,0:T(8,128)(2,1)S(1)}, bf16[24,1024]{1,0:T(8,128)(2,1)S(1)}, u32[]{:S(2)}, u32[]{:S(2)}) %collective-permute-start.7) | collective-permute-done | bytes 49184 | tf_op jit(solution)/shard_map/ppermute | solution.py:30
  76.8 1.6 %collective-permute-start.10 = (bf16[24,2048]{1,0:T(8,128)(2,1)S(1)}, bf16[24,2048]{1,0:T(8,128)(2,1)S(1)}, u32[]{:S(2)}, u32[]{:S(2)}) collective-permute-start(bf16[24,2048]{1,0:T(8,128)(2,1)S(1)} %pad_maximum_fusion.15), channel_id=1, source_target_pairs={{0,16},{8,24},{16,0},{24,8},{1,17},{9,25},{17,1},{25,9},{2,18},{10... | collective-permute-start | bytes 294920 | tf_op jit(solution)/shard_map/ppermute | solution.py:30
  78.4 0.9 collective-permute-start.8
  79.4 1.1 %collective-permute-start.42 = (bf16[24,1024]{1,0:T(8,128)(2,1)S(1)}, bf16[24,1024]{1,0:T(8,128)(2,1)S(1)}, u32[]{:S(2)}, u32[]{:S(2)}) collective-permute-start(bf16[24,1024]{1,0:T(8,128)(2,1)S(1)} %get-tuple-element.34), channel_id=1, source_target_pairs={{0,16},{8,24},{16,0},{24,8},{1,17},{9,25},{17,1},{25,9},{2,18},{10... | collective-permute-start | bytes 147464 | tf_op jit(solution)/shard_map/ppermute | solution.py:30
  81.4 1.6 %collective-permute-start.30 = (bf16[24,1024]{1,0:T(8,128)(2,1)S(1)}, bf16[24,1024]{1,0:T(8,128)(2,1)S(1)}, u32[]{:S(2)}, u32[]{:S(2)}) collective-permute-start(bf16[24,1024]{1,0:T(8,128)(2,1)S(1)} %get-tuple-element.28), channel_id=1, source_target_pairs={{0,16},{8,24},{16,0},{24,8},{1,17},{9,25},{17,1},{25,9},{2,18},{10... | collective-permute-start | bytes 147464 | tf_op jit(solution)/shard_map/ppermute | solution.py:30
  83.6 1.2 %collective-permute-start.32 = (bf16[24,1024]{1,0:T(8,128)(2,1)S(1)}, bf16[24,1024]{1,0:T(8,128)(2,1)S(1)}, u32[]{:S(2)}, u32[]{:S(2)}) collective-permute-start(bf16[24,1024]{1,0:T(8,128)(2,1)S(1)} %get-tuple-element.31), channel_id=1, source_target_pairs={{0,8},{8,0},{16,24},{24,16},{1,9},{9,1},{17,25},{25,17},{2,10},{10... | collective-permute-start | bytes 147464 | tf_op jit(solution)/shard_map/ppermute | solution.py:30
  84.8 1.2 %collective-permute-start.18 = (bf16[24,1024]{1,0:T(8,128)(2,1)S(1)}, bf16[24,1024]{1,0:T(8,128)(2,1)S(1)}, u32[]{:S(2)}, u32[]{:S(2)}) collective-permute-start(bf16[24,1024]{1,0:T(8,128)(2,1)S(1)} %get-tuple-element.22), channel_id=1, source_target_pairs={{0,16},{8,24},{16,0},{24,8},{1,17},{9,25},{17,1},{25,9},{2,18},{10... | collective-permute-start | bytes 147464 | tf_op jit(solution)/shard_map/ppermute | solution.py:30
  86.1 1.4 %collective-permute-start.20 = (bf16[24,1024]{1,0:T(8,128)(2,1)S(1)}, bf16[24,1024]{1,0:T(8,128)(2,1)S(1)}, u32[]{:S(2)}, u32[]{:S(2)}) collective-permute-start(bf16[24,1024]{1,0:T(8,128)(2,1)S(1)} %get-tuple-element.25), channel_id=1, source_target_pairs={{0,8},{8,0},{16,24},{24,16},{1,9},{9,1},{17,25},{25,17},{2,10},{10... | collective-permute-start | bytes 147464 | tf_op jit(solution)/shard_map/ppermute | solution.py:30
  87.7 1.1 collective-permute-start.45
  90.2 1.3 %collective-permute-start.33 = (bf16[24,2048]{1,0:T(8,128)(2,1)S(1)}, bf16[24,2048]{1,0:T(8,128)(2,1)S(1)}, u32[]{:S(2)}, u32[]{:S(2)}) collective-permute-start(bf16[24,2048]{1,0:T(8,128)(2,1)S(1)} %pad_maximum_fusion.19), channel_id=1, source_target_pairs={{0,16},{8,24},{16,0},{24,8},{1,17},{9,25},{17,1},{25,9},{2,18},{10... | collective-permute-start | bytes 294920 | tf_op jit(solution)/shard_map/ppermute | solution.py:30
  92.3 1.2 %collective-permute-start.31 = (bf16[24,2048]{1,0:T(8,128)(2,1)S(1)}, bf16[24,2048]{1,0:T(8,128)(2,1)S(1)}, u32[]{:S(2)}, u32[]{:S(2)}) collective-permute-start(bf16[24,2048]{1,0:T(8,128)(2,1)S(1)} %pad_maximum_fusion.18), channel_id=1, source_target_pairs={{0,8},{8,0},{16,24},{24,16},{1,9},{9,1},{17,25},{25,17},{2,10},{10... | collective-permute-start | bytes 294920 | tf_op jit(solution)/shard_map/ppermute | solution.py:30
  93.5 1.5 %collective-permute-done.43 = bf16[24,2048]{1,0:T(8,128)(2,1)S(1)} collective-permute-done((bf16[24,2048]{1,0:T(8,128)(2,1)S(1)}, bf16[24,2048]{1,0:T(8,128)(2,1)S(1)}, u32[]{:S(2)}, u32[]{:S(2)}) %collective-permute-start.43) | collective-permute-done | bytes 98336 | tf_op jit(solution)/shard_map/ppermute | solution.py:30
  95.0 1.0 collective-permute-start.21
  96.9 3.1 %collective-permute-start.46 = (bf16[24,2048]{1,0:T(8,128)(2,1)S(1)}, bf16[24,2048]{1,0:T(8,128)(2,1)S(1)}, u32[]{:S(2)}, u32[]{:S(2)}) collective-permute-start(bf16[24,2048]{1,0:T(8,128)(2,1)S(1)} %add_convert_fusion.5), channel_id=1, source_target_pairs={{0,6},{2,4},{4,2},{6,0},{1,7},{3,5},{5,3},{7,1},{8,14},{10,12},{12... | collective-permute-start | bytes 294920 | tf_op jit(solution)/shard_map/ppermute | solution.py:30
  100.8 1.5 %collective-permute-start.22 = (bf16[24,2048]{1,0:T(8,128)(2,1)S(1)}, bf16[24,2048]{1,0:T(8,128)(2,1)S(1)}, u32[]{:S(2)}, u32[]{:S(2)}) collective-permute-start(bf16[24,2048]{1,0:T(8,128)(2,1)S(1)} %add_convert_fusion.7), channel_id=1, source_target_pairs={{0,2},{2,0},{4,6},{6,4},{1,3},{3,1},{5,7},{7,5},{8,10},{10,8},{12,... | collective-permute-start | bytes 294920 | tf_op jit(solution)/shard_map/ppermute | solution.py:30
  102.4 0.9 collective-permute-done.46
  103.3 2.4 %collective-permute-done.34 = bf16[24,2048]{1,0:T(8,128)(2,1)S(1)} collective-permute-done((bf16[24,2048]{1,0:T(8,128)(2,1)S(1)}, bf16[24,2048]{1,0:T(8,128)(2,1)S(1)}, u32[]{:S(2)}, u32[]{:S(2)}) %collective-permute-start.34) | collective-permute-done | bytes 98336 | tf_op jit(solution)/shard_map/ppermute | solution.py:30
  (195 shorter events, 32.9 us)
Async XLA Ops:
  3.2 1.9 %collective-permute-start = (bf16[12,2176]{1,0:T(8,128)(2,1)S(1)}, bf16[12,2176]{1,0:T(8,128)(2,1)S(1)}, u32[]{:S(2)}, u32[]{:S(2)}) collective-permute-start(bf16[12,2176]{1,0:T(8,128)(2,1)S(1)} %pad_maximum_fusion.22), channel_id=1, source_target_pairs={{0,1},{1,0},{2,3},{3,2},{4,5},{5,4},{6,7},{7,6},{8,9},{9,8},{10,11... | collective-permute-start | bytes 156680 | tf_op jit(solution)/shard_map/ppermute | solution.py:30
  5.2 9.1 %collective-permute-start.2 = (bf16[24,2176]{1,0:T(8,128)(2,1)S(1)}, bf16[24,2176]{1,0:T(8,128)(2,1)S(1)}, u32[]{:S(2)}, u32[]{:S(2)}) collective-permute-start(bf16[24,2176]{1,0:T(8,128)(2,1)S(1)} %pad_maximum_fusion.13), channel_id=1, source_target_pairs={{0,16},{8,24},{16,0},{24,8},{1,17},{9,25},{17,1},{25,9},{2,18},{10... | collective-permute-start | bytes 313352 | tf_op jit(solution)/shard_map/ppermute | solution.py:30
  7.8 7.1 %collective-permute-start.1 = (bf16[24,2176]{1,0:T(8,128)(2,1)S(1)}, bf16[24,2176]{1,0:T(8,128)(2,1)S(1)}, u32[]{:S(2)}, u32[]{:S(2)}) collective-permute-start(bf16[24,2176]{1,0:T(8,128)(2,1)S(1)} %pad_maximum_fusion.13), channel_id=1, source_target_pairs={{0,8},{8,0},{16,24},{24,16},{1,9},{9,1},{17,25},{25,17},{2,10},{10... | collective-permute-start | bytes 313352 | tf_op jit(solution)/shard_map/ppermute | solution.py:30
  9.9 7.6 %collective-permute-start.35 = (bf16[24,2176]{1,0:T(8,128)(2,1)S(1)}, bf16[24,2176]{1,0:T(8,128)(2,1)S(1)}, u32[]{:S(2)}, u32[]{:S(2)}) collective-permute-start(bf16[24,2176]{1,0:T(8,128)(2,1)S(1)} %pad_maximum_fusion.13), channel_id=1, source_target_pairs={{0,6},{2,4},{4,2},{6,0},{1,7},{3,5},{5,3},{7,1},{8,14},{10,12},{12... | collective-permute-start | bytes 313352 | tf_op jit(solution)/shard_map/ppermute | solution.py:30
  13.5 6.3 %collective-permute-start.11 = (bf16[24,2176]{1,0:T(8,128)(2,1)S(1)}, bf16[24,2176]{1,0:T(8,128)(2,1)S(1)}, u32[]{:S(2)}, u32[]{:S(2)}) collective-permute-start(bf16[24,2176]{1,0:T(8,128)(2,1)S(1)} %pad_maximum_fusion.13), channel_id=1, source_target_pairs={{0,2},{2,0},{4,6},{6,4},{1,3},{3,1},{5,7},{7,5},{8,10},{10,8},{12,... | collective-permute-start | bytes 313352 | tf_op jit(solution)/shard_map/ppermute | solution.py:30
  13.5 8.9 %collective-permute-start.23 = (bf16[24,2176]{1,0:T(8,128)(2,1)S(1)}, bf16[24,2176]{1,0:T(8,128)(2,1)S(1)}, u32[]{:S(2)}, u32[]{:S(2)}) collective-permute-start(bf16[24,2176]{1,0:T(8,128)(2,1)S(1)} %pad_maximum_fusion.13), channel_id=1, source_target_pairs={{0,4},{2,6},{4,0},{6,2},{1,5},{3,7},{5,1},{7,3},{8,12},{10,14},{12... | collective-permute-start | bytes 313352 | tf_op jit(solution)/shard_map/ppermute | solution.py:30
  14.3 9.1 %collective-permute-start.4 = (bf16[24,1152]{1,0:T(8,128)(2,1)S(1)}, bf16[24,1152]{1,0:T(8,128)(2,1)S(1)}, u32[]{:S(2)}, u32[]{:S(2)}) collective-permute-start(bf16[24,1152]{1,0:T(8,128)(2,1)S(1)} %slice.455), channel_id=1, source_target_pairs={{0,8},{8,0},{16,24},{24,16},{1,9},{9,1},{17,25},{25,17},{2,10},{10... | collective-permute-start | bytes 165896 | tf_op jit(solution)/shard_map/ppermute | solution.py:30
  14.9 8.0 %collective-permute-start.3 = (bf16[24,1024]{1,0:T(8,128)(2,1)S(1)}, bf16[24,1024]{1,0:T(8,128)(2,1)S(1)}, u32[]{:S(2)}, u32[]{:S(2)}) collective-permute-start(bf16[24,1024]{1,0:T(8,128)(2,1)S(1)} %slice.454), channel_id=1, source_target_pairs={{0,16},{8,24},{16,0},{24,8},{1,17},{9,25},{17,1},{25,9},{2,18},{10... | collective-permute-start | bytes 147464 | tf_op jit(solution)/shard_map/ppermute | solution.py:30
  17.5 7.6 %collective-permute-start.37 = (bf16[24,2176]{1,0:T(8,128)(2,1)S(1)}, bf16[24,2176]{1,0:T(8,128)(2,1)S(1)}, u32[]{:S(2)}, u32[]{:S(2)}) collective-permute-start(bf16[24,2176]{1,0:T(8,128)(2,1)S(1)} %collective-permute-done.35), channel_id=1, source_target_pairs={{0,16},{8,24},{16,0},{24,8},{1,17},{9,25},{17,1},{25,9},{2,18},{10... | collective-permute-start | bytes 313352 | tf_op jit(solution)/shard_map/ppermute | solution.py:30
  19.7 6.9 %collective-permute-start.36 = (bf16[24,2176]{1,0:T(8,128)(2,1)S(1)}, bf16[24,2176]{1,0:T(8,128)(2,1)S(1)}, u32[]{:S(2)}, u32[]{:S(2)}) collective-permute-start(bf16[24,2176]{1,0:T(8,128)(2,1)S(1)} %collective-permute-done.35), channel_id=1, source_target_pairs={{0,8},{8,0},{16,24},{24,16},{1,9},{9,1},{17,25},{25,17},{2,10},{10... | collective-permute-start | bytes 313352 | tf_op jit(solution)/shard_map/ppermute | solution.py:30
  22.3 5.2 %collective-permute-start.13 = (bf16[24,2176]{1,0:T(8,128)(2,1)S(1)}, bf16[24,2176]{1,0:T(8,128)(2,1)S(1)}, u32[]{:S(2)}, u32[]{:S(2)}) collective-permute-start(bf16[24,2176]{1,0:T(8,128)(2,1)S(1)} %collective-permute-done.11), channel_id=1, source_target_pairs={{0,16},{8,24},{16,0},{24,8},{1,17},{9,25},{17,1},{25,9},{2,18},{10... | collective-permute-start | bytes 313352 | tf_op jit(solution)/shard_map/ppermute | solution.py:30
  22.8 6.0 %collective-permute-start.12 = (bf16[24,2176]{1,0:T(8,128)(2,1)S(1)}, bf16[24,2176]{1,0:T(8,128)(2,1)S(1)}, u32[]{:S(2)}, u32[]{:S(2)}) collective-permute-start(bf16[24,2176]{1,0:T(8,128)(2,1)S(1)} %collective-permute-done.11), channel_id=1, source_target_pairs={{0,8},{8,0},{16,24},{24,16},{1,9},{9,1},{17,25},{25,17},{2,10},{10... | collective-permute-start | bytes 313352 | tf_op jit(solution)/shard_map/ppermute | solution.py:30
  23.4 5.8 %collective-permute-start.25 = (bf16[24,2176]{1,0:T(8,128)(2,1)S(1)}, bf16[24,2176]{1,0:T(8,128)(2,1)S(1)}, u32[]{:S(2)}, u32[]{:S(2)}) collective-permute-start(bf16[24,2176]{1,0:T(8,128)(2,1)S(1)} %collective-permute-done.23), channel_id=1, source_target_pairs={{0,16},{8,24},{16,0},{24,8},{1,17},{9,25},{17,1},{25,9},{2,18},{10... | collective-permute-start | bytes 313352 | tf_op jit(solution)/shard_map/ppermute | solution.py:30
  25.1 5.1 %collective-permute-start.24 = (bf16[24,2176]{1,0:T(8,128)(2,1)S(1)}, bf16[24,2176]{1,0:T(8,128)(2,1)S(1)}, u32[]{:S(2)}, u32[]{:S(2)}) collective-permute-start(bf16[24,2176]{1,0:T(8,128)(2,1)S(1)} %collective-permute-done.23), channel_id=1, source_target_pairs={{0,8},{8,0},{16,24},{24,16},{1,9},{9,1},{17,25},{25,17},{2,10},{10... | collective-permute-start | bytes 313352 | tf_op jit(solution)/shard_map/ppermute | solution.py:30
  26.6 6.3 %collective-permute-start.39 = (bf16[24,1152]{1,0:T(8,128)(2,1)S(1)}, bf16[24,1152]{1,0:T(8,128)(2,1)S(1)}, u32[]{:S(2)}, u32[]{:S(2)}) collective-permute-start(bf16[24,1152]{1,0:T(8,128)(2,1)S(1)} %slice.503), channel_id=1, source_target_pairs={{0,8},{8,0},{16,24},{24,16},{1,9},{9,1},{17,25},{25,17},{2,10},{10... | collective-permute-start | bytes 165896 | tf_op jit(solution)/shard_map/ppermute | solution.py:30
  27.6 4.1 %collective-permute-start.38 = (bf16[24,1024]{1,0:T(8,128)(2,1)S(1)}, bf16[24,1024]{1,0:T(8,128)(2,1)S(1)}, u32[]{:S(2)}, u32[]{:S(2)}) collective-permute-start(bf16[24,1024]{1,0:T(8,128)(2,1)S(1)} %slice.502), channel_id=1, source_target_pairs={{0,16},{8,24},{16,0},{24,8},{1,17},{9,25},{17,1},{25,9},{2,18},{10... | collective-permute-start | bytes 147464 | tf_op jit(solution)/shard_map/ppermute | solution.py:30
  28.8 17.1 %collective-permute-start.5 = (bf16[96,2048]{1,0:T(8,128)(2,1)S(1)}, bf16[96,2048]{1,0:T(8,128)(2,1)}, u32[]{:S(2)}, u32[]{:S(2)}) collective-permute-start(bf16[96,2048]{1,0:T(8,128)(2,1)S(1)} %slice.456), channel_id=1, source_target_pairs={{0,1},{1,0},{2,3},{3,2},{4,5},{5,4},{6,7},{7,6},{8,9},{9,8},{10,11... | collective-permute-start | bytes 1179656 | tf_op jit(solution)/shard_map/ppermute | solution.py:30
  29.2 5.0 %collective-permute-start.15 = (bf16[24,1152]{1,0:T(8,128)(2,1)S(1)}, bf16[24,1152]{1,0:T(8,128)(2,1)S(1)}, u32[]{:S(2)}, u32[]{:S(2)}) collective-permute-start(bf16[24,1152]{1,0:T(8,128)(2,1)S(1)} %slice.471), channel_id=1, source_target_pairs={{0,8},{8,0},{16,24},{24,16},{1,9},{9,1},{17,25},{25,17},{2,10},{10... | collective-permute-start | bytes 165896 | tf_op jit(solution)/shard_map/ppermute | solution.py:30
  30.1 4.1 %collective-permute-start.14 = (bf16[24,1024]{1,0:T(8,128)(2,1)S(1)}, bf16[24,1024]{1,0:T(8,128)(2,1)S(1)}, u32[]{:S(2)}, u32[]{:S(2)}) collective-permute-start(bf16[24,1024]{1,0:T(8,128)(2,1)S(1)} %slice.470), channel_id=1, source_target_pairs={{0,16},{8,24},{16,0},{24,8},{1,17},{9,25},{17,1},{25,9},{2,18},{10... | collective-permute-start | bytes 147464 | tf_op jit(solution)/shard_map/ppermute | solution.py:30
  31.7 5.3 %collective-permute-start.27 = (bf16[24,1152]{1,0:T(8,128)(2,1)S(1)}, bf16[24,1152]{1,0:T(8,128)(2,1)S(1)}, u32[]{:S(2)}, u32[]{:S(2)}) collective-permute-start(bf16[24,1152]{1,0:T(8,128)(2,1)S(1)} %slice.487), channel_id=1, source_target_pairs={{0,8},{8,0},{16,24},{24,16},{1,9},{9,1},{17,25},{25,17},{2,10},{10... | collective-permute-start | bytes 165896 | tf_op jit(solution)/shard_map/ppermute | solution.py:30
  32.9 4.1 %collective-permute-start.26 = (bf16[24,1024]{1,0:T(8,128)(2,1)S(1)}, bf16[24,1024]{1,0:T(8,128)(2,1)S(1)}, u32[]{:S(2)}, u32[]{:S(2)}) collective-permute-start(bf16[24,1024]{1,0:T(8,128)(2,1)S(1)} %slice.486), channel_id=1, source_target_pairs={{0,16},{8,24},{16,0},{24,8},{1,17},{9,25},{17,1},{25,9},{2,18},{10... | collective-permute-start | bytes 147464 | tf_op jit(solution)/shard_map/ppermute | solution.py:30
  34.2 22.6 %collective-permute-start.40 = (bf16[96,2048]{1,0:T(8,128)(2,1)S(1)}, bf16[96,2048]{1,0:T(8,128)(2,1)}, u32[]{:S(2)}, u32[]{:S(2)}) collective-permute-start(bf16[96,2048]{1,0:T(8,128)(2,1)S(1)} %slice.504), channel_id=1, source_target_pairs={{0,1},{1,0},{2,3},{3,2},{4,5},{5,4},{6,7},{7,6},{8,9},{9,8},{10,11... | collective-permute-start | bytes 1179656 | tf_op jit(solution)/shard_map/ppermute | solution.py:30
  40.1 20.1 %collective-permute-start.28 = (bf16[96,2048]{1,0:T(8,128)(2,1)S(1)}, bf16[96,2048]{1,0:T(8,128)(2,1)}, u32[]{:S(2)}, u32[]{:S(2)}) collective-permute-start(bf16[96,2048]{1,0:T(8,128)(2,1)S(1)} %slice.488), channel_id=1, source_target_pairs={{0,1},{1,0},{2,3},{3,2},{4,5},{5,4},{6,7},{7,6},{8,9},{9,8},{10,11... | collective-permute-start | bytes 1179656 | tf_op jit(solution)/shard_map/ppermute | solution.py:30
  40.9 22.7 %collective-permute-start.16 = (bf16[96,2048]{1,0:T(8,128)(2,1)S(1)}, bf16[96,2048]{1,0:T(8,128)(2,1)}, u32[]{:S(2)}, u32[]{:S(2)}) collective-permute-start(bf16[96,2048]{1,0:T(8,128)(2,1)S(1)} %slice.472), channel_id=1, source_target_pairs={{0,1},{1,0},{2,3},{3,2},{4,5},{5,4},{6,7},{7,6},{8,9},{9,8},{10,11... | collective-permute-start | bytes 1179656 | tf_op jit(solution)/shard_map/ppermute | solution.py:30
  56.8 15.1 %collective-permute-start.6 = (bf16[96,2048]{1,0:T(8,128)(2,1)S(1)}, bf16[96,2048]{1,0:T(8,128)(2,1)S(1)}, u32[]{:S(2)}, u32[]{:S(2)}) collective-permute-start(bf16[96,2048]{1,0:T(8,128)(2,1)S(1)} %broadcast_select_fusion.9), channel_id=1, source_target_pairs={{0,1},{1,0},{2,3},{3,2},{4,5},{5,4},{6,7},{7,6},{8,9},{9,8},{10,11... | collective-permute-start | bytes 1179656 | tf_op jit(solution)/shard_map/ppermute | solution.py:30
  68.5 10.7 %collective-permute-start.41 = (bf16[96,2048]{1,0:T(8,128)(2,1)S(1)}, bf16[96,2048]{1,0:T(8,128)(2,1)S(1)}, u32[]{:S(2)}, u32[]{:S(2)}) collective-permute-start(bf16[96,2048]{1,0:T(8,128)(2,1)S(1)} %broadcast_select_fusion), channel_id=1, source_target_pairs={{0,1},{1,0},{2,3},{3,2},{4,5},{5,4},{6,7},{7,6},{8,9},{9,8},{10,11... | collective-permute-start | bytes 1179656 | tf_op jit(solution)/shard_map/ppermute | solution.py:30
  70.5 10.1 %collective-permute-start.29 = (bf16[96,2048]{1,0:T(8,128)(2,1)S(1)}, bf16[96,2048]{1,0:T(8,128)(2,1)S(1)}, u32[]{:S(2)}, u32[]{:S(2)}) collective-permute-start(bf16[96,2048]{1,0:T(8,128)(2,1)S(1)} %broadcast_select_fusion.3), channel_id=1, source_target_pairs={{0,1},{1,0},{2,3},{3,2},{4,5},{5,4},{6,7},{7,6},{8,9},{9,8},{10,11... | collective-permute-start | bytes 1179656 | tf_op jit(solution)/shard_map/ppermute | solution.py:30
  72.1 4.2 %collective-permute-start.7 = (bf16[24,1024]{1,0:T(8,128)(2,1)S(1)}, bf16[24,1024]{1,0:T(8,128)(2,1)S(1)}, u32[]{:S(2)}, u32[]{:S(2)}) collective-permute-start(bf16[24,1024]{1,0:T(8,128)(2,1)S(1)} %get-tuple-element.16), channel_id=1, source_target_pairs={{0,16},{8,24},{16,0},{24,8},{1,17},{9,25},{17,1},{25,9},{2,18},{10... | collective-permute-start | bytes 147464 | tf_op jit(solution)/shard_map/ppermute | solution.py:30
  72.7 4.1 %collective-permute-start.9 = (bf16[24,1024]{1,0:T(8,128)(2,1)S(1)}, bf16[24,1024]{1,0:T(8,128)(2,1)S(1)}, u32[]{:S(2)}, u32[]{:S(2)}) collective-permute-start(bf16[24,1024]{1,0:T(8,128)(2,1)S(1)} %get-tuple-element.19), channel_id=1, source_target_pairs={{0,8},{8,0},{16,24},{24,16},{1,9},{9,1},{17,25},{25,17},{2,10},{10... | collective-permute-start | bytes 147464 | tf_op jit(solution)/shard_map/ppermute | solution.py:30
  74.1 7.3 %collective-permute-start.17 = (bf16[96,2048]{1,0:T(8,128)(2,1)S(1)}, bf16[96,2048]{1,0:T(8,128)(2,1)S(1)}, u32[]{:S(2)}, u32[]{:S(2)}) collective-permute-start(bf16[96,2048]{1,0:T(8,128)(2,1)S(1)} %broadcast_select_fusion.6), channel_id=1, source_target_pairs={{0,1},{1,0},{2,3},{3,2},{4,5},{5,4},{6,7},{7,6},{8,9},{9,8},{10,11... | collective-permute-start | bytes 1179656 | tf_op jit(solution)/shard_map/ppermute | solution.py:30
  76.8 25.6 %collective-permute-start.10 = (bf16[24,2048]{1,0:T(8,128)(2,1)S(1)}, bf16[24,2048]{1,0:T(8,128)(2,1)S(1)}, u32[]{:S(2)}, u32[]{:S(2)}) collective-permute-start(bf16[24,2048]{1,0:T(8,128)(2,1)S(1)} %pad_maximum_fusion.15), channel_id=1, source_target_pairs={{0,16},{8,24},{16,0},{24,8},{1,17},{9,25},{17,1},{25,9},{2,18},{10... | collective-permute-start | bytes 294920 | tf_op jit(solution)/shard_map/ppermute | solution.py:30
  78.4 24.1 %collective-permute-start.8 = (bf16[24,2048]{1,0:T(8,128)(2,1)S(1)}, bf16[24,2048]{1,0:T(8,128)(2,1)S(1)}, u32[]{:S(2)}, u32[]{:S(2)}) collective-permute-start(bf16[24,2048]{1,0:T(8,128)(2,1)S(1)} %pad_maximum_fusion.14), channel_id=1, source_target_pairs={{0,8},{8,0},{16,24},{24,16},{1,9},{9,1},{17,25},{25,17},{2,10},{10... | collective-permute-start | bytes 294920 | tf_op jit(solution)/shard_map/ppermute | solution.py:30
  79.4 4.2 %collective-permute-start.42 = (bf16[24,1024]{1,0:T(8,128)(2,1)S(1)}, bf16[24,1024]{1,0:T(8,128)(2,1)S(1)}, u32[]{:S(2)}, u32[]{:S(2)}) collective-permute-start(bf16[24,1024]{1,0:T(8,128)(2,1)S(1)} %get-tuple-element.34), channel_id=1, source_target_pairs={{0,16},{8,24},{16,0},{24,8},{1,17},{9,25},{17,1},{25,9},{2,18},{10... | collective-permute-start | bytes 147464 | tf_op jit(solution)/shard_map/ppermute | solution.py:30
  80.6 4.3 %collective-permute-start.44 = (bf16[24,1024]{1,0:T(8,128)(2,1)S(1)}, bf16[24,1024]{1,0:T(8,128)(2,1)S(1)}, u32[]{:S(2)}, u32[]{:S(2)}) collective-permute-start(bf16[24,1024]{1,0:T(8,128)(2,1)S(1)} %get-tuple-element.37), channel_id=1, source_target_pairs={{0,8},{8,0},{16,24},{24,16},{1,9},{9,1},{17,25},{25,17},{2,10},{10... | collective-permute-start | bytes 147464 | tf_op jit(solution)/shard_map/ppermute | solution.py:30
  81.4 4.7 %collective-permute-start.30 = (bf16[24,1024]{1,0:T(8,128)(2,1)S(1)}, bf16[24,1024]{1,0:T(8,128)(2,1)S(1)}, u32[]{:S(2)}, u32[]{:S(2)}) collective-permute-start(bf16[24,1024]{1,0:T(8,128)(2,1)S(1)} %get-tuple-element.28), channel_id=1, source_target_pairs={{0,16},{8,24},{16,0},{24,8},{1,17},{9,25},{17,1},{25,9},{2,18},{10... | collective-permute-start | bytes 147464 | tf_op jit(solution)/shard_map/ppermute | solution.py:30
  83.6 4.1 %collective-permute-start.32 = (bf16[24,1024]{1,0:T(8,128)(2,1)S(1)}, bf16[24,1024]{1,0:T(8,128)(2,1)S(1)}, u32[]{:S(2)}, u32[]{:S(2)}) collective-permute-start(bf16[24,1024]{1,0:T(8,128)(2,1)S(1)} %get-tuple-element.31), channel_id=1, source_target_pairs={{0,8},{8,0},{16,24},{24,16},{1,9},{9,1},{17,25},{25,17},{2,10},{10... | collective-permute-start | bytes 147464 | tf_op jit(solution)/shard_map/ppermute | solution.py:30
  84.8 4.5 %collective-permute-start.18 = (bf16[24,1024]{1,0:T(8,128)(2,1)S(1)}, bf16[24,1024]{1,0:T(8,128)(2,1)S(1)}, u32[]{:S(2)}, u32[]{:S(2)}) collective-permute-start(bf16[24,1024]{1,0:T(8,128)(2,1)S(1)} %get-tuple-element.22), channel_id=1, source_target_pairs={{0,16},{8,24},{16,0},{24,8},{1,17},{9,25},{17,1},{25,9},{2,18},{10... | collective-permute-start | bytes 147464 | tf_op jit(solution)/shard_map/ppermute | solution.py:30
  86.1 4.2 %collective-permute-start.20 = (bf16[24,1024]{1,0:T(8,128)(2,1)S(1)}, bf16[24,1024]{1,0:T(8,128)(2,1)S(1)}, u32[]{:S(2)}, u32[]{:S(2)}) collective-permute-start(bf16[24,1024]{1,0:T(8,128)(2,1)S(1)} %get-tuple-element.25), channel_id=1, source_target_pairs={{0,8},{8,0},{16,24},{24,16},{1,9},{9,1},{17,25},{25,17},{2,10},{10... | collective-permute-start | bytes 147464 | tf_op jit(solution)/shard_map/ppermute | solution.py:30
  87.7 4.6 %collective-permute-start.45 = (bf16[24,2048]{1,0:T(8,128)(2,1)S(1)}, bf16[24,2048]{1,0:T(8,128)(2,1)S(1)}, u32[]{:S(2)}, u32[]{:S(2)}) collective-permute-start(bf16[24,2048]{1,0:T(8,128)(2,1)S(1)} %pad_maximum_fusion.21), channel_id=1, source_target_pairs={{0,16},{8,24},{16,0},{24,8},{1,17},{9,25},{17,1},{25,9},{2,18},{10... | collective-permute-start | bytes 294920 | tf_op jit(solution)/shard_map/ppermute | solution.py:30
  89.4 5.6 %collective-permute-start.43 = (bf16[24,2048]{1,0:T(8,128)(2,1)S(1)}, bf16[24,2048]{1,0:T(8,128)(2,1)S(1)}, u32[]{:S(2)}, u32[]{:S(2)}) collective-permute-start(bf16[24,2048]{1,0:T(8,128)(2,1)S(1)} %pad_maximum_fusion.20), channel_id=1, source_target_pairs={{0,8},{8,0},{16,24},{24,16},{1,9},{9,1},{17,25},{25,17},{2,10},{10... | collective-permute-start | bytes 294920 | tf_op jit(solution)/shard_map/ppermute | solution.py:30
  90.2 5.8 %collective-permute-start.33 = (bf16[24,2048]{1,0:T(8,128)(2,1)S(1)}, bf16[24,2048]{1,0:T(8,128)(2,1)S(1)}, u32[]{:S(2)}, u32[]{:S(2)}) collective-permute-start(bf16[24,2048]{1,0:T(8,128)(2,1)S(1)} %pad_maximum_fusion.19), channel_id=1, source_target_pairs={{0,16},{8,24},{16,0},{24,8},{1,17},{9,25},{17,1},{25,9},{2,18},{10... | collective-permute-start | bytes 294920 | tf_op jit(solution)/shard_map/ppermute | solution.py:30
  92.3 4.6 %collective-permute-start.31 = (bf16[24,2048]{1,0:T(8,128)(2,1)S(1)}, bf16[24,2048]{1,0:T(8,128)(2,1)S(1)}, u32[]{:S(2)}, u32[]{:S(2)}) collective-permute-start(bf16[24,2048]{1,0:T(8,128)(2,1)S(1)} %pad_maximum_fusion.18), channel_id=1, source_target_pairs={{0,8},{8,0},{16,24},{24,16},{1,9},{9,1},{17,25},{25,17},{2,10},{10... | collective-permute-start | bytes 294920 | tf_op jit(solution)/shard_map/ppermute | solution.py:30
  95.0 5.0 %collective-permute-start.21 = (bf16[24,2048]{1,0:T(8,128)(2,1)S(1)}, bf16[24,2048]{1,0:T(8,128)(2,1)S(1)}, u32[]{:S(2)}, u32[]{:S(2)}) collective-permute-start(bf16[24,2048]{1,0:T(8,128)(2,1)S(1)} %pad_maximum_fusion.17), channel_id=1, source_target_pairs={{0,16},{8,24},{16,0},{24,8},{1,17},{9,25},{17,1},{25,9},{2,18},{10... | collective-permute-start | bytes 294920 | tf_op jit(solution)/shard_map/ppermute | solution.py:30
  96.1 4.7 %collective-permute-start.19 = (bf16[24,2048]{1,0:T(8,128)(2,1)S(1)}, bf16[24,2048]{1,0:T(8,128)(2,1)S(1)}, u32[]{:S(2)}, u32[]{:S(2)}) collective-permute-start(bf16[24,2048]{1,0:T(8,128)(2,1)S(1)} %pad_maximum_fusion.16), channel_id=1, source_target_pairs={{0,8},{8,0},{16,24},{24,16},{1,9},{9,1},{17,25},{25,17},{2,10},{10... | collective-permute-start | bytes 294920 | tf_op jit(solution)/shard_map/ppermute | solution.py:30
  96.9 6.4 %collective-permute-start.46 = (bf16[24,2048]{1,0:T(8,128)(2,1)S(1)}, bf16[24,2048]{1,0:T(8,128)(2,1)S(1)}, u32[]{:S(2)}, u32[]{:S(2)}) collective-permute-start(bf16[24,2048]{1,0:T(8,128)(2,1)S(1)} %add_convert_fusion.5), channel_id=1, source_target_pairs={{0,6},{2,4},{4,2},{6,0},{1,7},{3,5},{5,3},{7,1},{8,14},{10,12},{12... | collective-permute-start | bytes 294920 | tf_op jit(solution)/shard_map/ppermute | solution.py:30
  100.0 5.7 %collective-permute-start.34 = (bf16[24,2048]{1,0:T(8,128)(2,1)S(1)}, bf16[24,2048]{1,0:T(8,128)(2,1)S(1)}, u32[]{:S(2)}, u32[]{:S(2)}) collective-permute-start(bf16[24,2048]{1,0:T(8,128)(2,1)S(1)} %add_convert_fusion.6), channel_id=1, source_target_pairs={{0,4},{2,6},{4,0},{6,2},{1,5},{3,7},{5,1},{7,3},{8,12},{10,14},{12... | collective-permute-start | bytes 294920 | tf_op jit(solution)/shard_map/ppermute | solution.py:30
  100.8 5.7 %collective-permute-start.22 = (bf16[24,2048]{1,0:T(8,128)(2,1)S(1)}, bf16[24,2048]{1,0:T(8,128)(2,1)S(1)}, u32[]{:S(2)}, u32[]{:S(2)}) collective-permute-start(bf16[24,2048]{1,0:T(8,128)(2,1)S(1)} %add_convert_fusion.7), channel_id=1, source_target_pairs={{0,2},{2,0},{4,6},{6,4},{1,3},{3,1},{5,7},{7,5},{8,10},{10,8},{12,... | collective-permute-start | bytes 294920 | tf_op jit(solution)/shard_map/ppermute | solution.py:30
  106.6 1.3 %collective-permute-start.47 = (bf16[12,2048]{1,0:T(8,128)(2,1)S(1)}, bf16[12,2048]{1,0:T(8,128)(2,1)S(1)}, u32[]{:S(2)}, u32[]{:S(2)}) collective-permute-start(bf16[12,2048]{1,0:T(8,128)(2,1)S(1)} %broadcast_select_fusion.16), channel_id=1, source_target_pairs={{0,1},{1,0},{2,3},{3,2},{4,5},{5,4},{6,7},{7,6},{8,9},{9,8},{10,11... | collective-permute-start | bytes 147464 | tf_op jit(solution)/shard_map/ppermute | solution.py:30
  (8 other events, 66.2 us)

commit v4 on v3

v4 whole, which is shorter than its diff:
```python
import jax
import jax.numpy as jnp
from jax import lax
from jax.experimental.layout import Layout, with_layout_constraint
from jax.sharding import Mesh, PartitionSpec as P

LANES = 128
GATE_MOST = 5


def lookup_small(values_table, index_array):
    columns = jnp.arange(values_table.shape[0], dtype=jnp.int32)
    return jnp.sum(jnp.where(index_array[..., None] == columns, values_table, 0), -1)


def planned_holder(expert_index, swap_slot, per_device, owners):
    home = expert_index // per_device
    within = expert_index % per_device
    partner = (home + owners // 2) % owners
    moved = within == lookup_small(swap_slot, home)
    return jnp.where(moved, partner, home)


def row_major(value):
    return with_layout_constraint(value, Layout(major_to_minor=tuple(range(value.ndim))))


def swap(value, axis, distance):
    size = lax.axis_size(axis)
    pairs = [(i, i ^ distance) for i in range(size)]
    return row_major(lax.ppermute(row_major(value), axis, pairs))


def split_gates(gates):
    high = lax.reduce_precision(gates, 8, 7)
    middle = lax.reduce_precision(gates - high, 8, 7)
    return [part.astype(jnp.bfloat16) for part in (high, middle, gates - high - middle)]


def cut_of(block):
    return block.shape[1] // (2 * LANES) * LANES


def spread_near(block):
    size = lax.axis_size("dp")
    return [swap(block, "dp", k) for k in range(1, 3 if size == 4 else size)]


def spread_rest(near):
    if lax.axis_size("dp") != 4:
        return []
    cut = cut_of(near[0])
    return [swap(near[0][:, :cut], "dp", 2), swap(near[1][:, cut:], "dp", 1)]


def joined(halves):
    return [jnp.concatenate(halves, 1)] if halves else []


def behind(values, others):
    return lax.optimization_barrier((values, others))[0]


def wide(value):
    return value.astype(jnp.float32)


def with_fourth(blocks):
    if len(blocks) != 4:
        return blocks
    own, one, two, both = blocks
    cut = cut_of(own)
    upper = swap(both[:, :cut], "dp", 2)
    lower = swap(both[:, cut:], "dp", 1)
    one = jnp.concatenate(
        [(wide(one[:, :cut]) + wide(upper)).astype(jnp.bfloat16), one[:, cut:]], 1
    )
    two = jnp.concatenate(
        [two[:, :cut], (wide(two[:, cut:]) + wide(lower)).astype(jnp.bfloat16)], 1
    )
    return [own, one, two]


def collected(blocks):
    total = wide(blocks[0])
    for k, block in enumerate(blocks[1:], 1):
        total = total + wide(swap(block, "dp", k))
    return total.astype(jnp.bfloat16)


def on_device(tokens, expert_ids, gate_probs, in_weight, out_weight, swap_slot):
    groups, chips = lax.axis_size("dp"), lax.axis_size("chip")
    owners = 2 * chips
    per_device = in_weight.shape[0]
    rows, width = tokens.shape
    part = width // 2
    top_count = expert_ids.shape[1]
    experts_all = per_device * owners
    half_width = out_weight.shape[1]
    core = lax.axis_index("core")
    first = core == 0
    all_experts = jnp.arange(experts_all, dtype=jnp.int32)
    home = lax.axis_index("chip") * 2 + core

    routing = jnp.concatenate(
        [row_major(expert_ids).astype(jnp.bfloat16), *split_gates(row_major(gate_probs))], 1
    )
    routing = row_major(jnp.pad(routing, ((0, 0), (0, LANES - routing.shape[1]))))
    left, right = tokens[:, :part], tokens[:, part:]
    keep = jnp.concatenate([jnp.where(first, left, right), routing], 1)
    give = jnp.concatenate([jnp.where(first, right, left), routing], 1)
    taken = swap(give, "core", 1)
    chip_rows = row_major(
        jnp.concatenate([jnp.where(first, keep, taken), jnp.where(first, taken, keep)], 0)
    )

    def routes(meta):
        ids = meta[:, :top_count].astype(jnp.int32)
        gates = sum(
            wide(meta[:, (i + 1) * top_count : (i + 2) * top_count]) for i in range(3)
        )
        return ids, gates

    def own_sums(blocks):
        held = row_major(jnp.concatenate(blocks, 0))
        own_half = held[:, :part]
        other_half = swap(own_half, "core", 1)
        held_tokens = row_major(
            jnp.concatenate(
                [
                    jnp.where(first, own_half, other_half),
                    jnp.where(first, other_half, own_half),
                ],
                1,
            )
        )
        ids, gates = routes(held[:, part:])
        hidden = []
        for s in range(per_device):
            own_gate = jnp.sum(
                jnp.where(ids == home * per_device + s, gates, jnp.float32(0.0)), 1, keepdims=True
            )
            both = jnp.dot(held_tokens, in_weight[s], preferred_element_type=jnp.float32)
            unit = jax.nn.silu(both[:, :half_width]) * both[:, half_width:]
            hidden.append((unit * own_gate).astype(jnp.bfloat16))
        summed = jnp.dot(
            jnp.concatenate(hidden, 1),
            out_weight.reshape(per_device * half_width, width),
            preferred_element_type=jnp.float32,
        )
        return row_major(summed.astype(jnp.bfloat16))

    def chip_sums(summed, blocks):
        left, right = summed[:, :part], summed[:, part:]
        arrived = swap(jnp.where(first, right, left), "core", 1)
        chip_sum = (wide(jnp.where(first, left, right)) + wide(arrived)).astype(jnp.bfloat16)
        chip_sum = row_major(chip_sum)
        edges = [0]
        for block in blocks:
            edges.append(edges[-1] + block.shape[0])
        return [chip_sum[low:high] for low, high in zip(edges, edges[1:])]

    others = [swap(chip_rows, "chip", j) for j in range(1, chips)]
    near = [chip_rows, *spread_near(chip_rows)]
    near += joined(spread_rest(near[1:]))
    far = [row_major(jnp.concatenate(others, 0))]
    far += spread_near(far[0])
    first_blocks = [*near, far[0]]
    first_part = own_sums(first_blocks)
    far[1:] = behind(far[1:], first_part)
    rest = spread_rest(far[1:])
    first_sums = chip_sums(first_part, first_blocks)
    near_sums, far_sums = first_sums[:groups], first_sums[groups:]
    near_sums = with_fourth(near_sums)
    part_two = own_sums(far[1:])
    if rest:
        rest = joined(behind(rest, (part_two, near_sums)))
        part_three = own_sums(rest)
        far_sums += chip_sums(part_two, far[1:]) + chip_sums(part_three, rest)
    else:
        far_sums += chip_sums(part_two, far[1:])
    far += rest
    near_total = collected(near_sums)
    far_sums = with_fourth(far_sums)
    far_total = collected(far_sums)

    total = wide(near_total)
    for j in range(1, chips):
        block = far_total[(j - 1) * 2 * rows : j * 2 * rows]
        total = total + wide(swap(block, "chip", j))
    total = total.astype(jnp.bfloat16)
    upper, lower = total[:rows], total[rows:]
    arrived = swap(jnp.where(first, lower, upper), "core", 1)
    kept = jnp.where(first, upper, lower)
    mixed_out = row_major(
        jnp.concatenate([jnp.where(first, kept, arrived), jnp.where(first, arrived, kept)], 1)
    )

    ids, gates = routes(jnp.concatenate([block[:, part:] for block in near + far], 0))
    step = 2.0 ** (31 - (ids.shape[0] * GATE_MOST).bit_length())
    amounts = jnp.round(gates * step).astype(jnp.int32)
    totals = jnp.sum(jnp.where(ids[..., None] == all_experts, amounts[..., None], 0), (0, 1))
    totals = totals.astype(jnp.float32) * (1.0 / step)
    holder = planned_holder(all_experts, swap_slot, per_device, owners)
    owner_load = jnp.sum(
        jnp.where(
            holder == jnp.arange(owners, dtype=jnp.int32)[:, None], totals[None, :], jnp.float32(0.0)
        ),
        1,
    ) * (owners / ids.shape[0])
    return (mixed_out, owner_load)


def solution(mesh):
    groups, owners = mesh.devices.shape
    fine = Mesh(mesh.devices.reshape(groups, owners // 2, 2), ("dp", "chip", "core"))
    rows = P(("dp", "chip", "core"), None)
    return jax.shard_map(
        on_device,
        mesh=fine,
        in_specs=(
            rows,
            rows,
            rows,
            P(("chip", "core"), None, "dp"),
            P(("chip", "core"), "dp", None),
            P(),
        ),
        out_specs=(rows, P()),
        check_vma=False,
    )
```

time: 109 us -> 91.9 us (0.84)
  starting transfers between devices: 44.3 us -> 27.5 us
  waiting for transfers between devices: 21.3 us -> 29.1 us
  other arithmetic: 15.9 us -> 9.33 us
  local copies, waits for them, and re-layouts: 5.91 us -> 4.71 us
    ppermute x48 -> x30, starting transfers between devices: 44.3 us -> 27.5 us  [swap(): return row_major(lax.ppermute(row_major(value), axis, pairs))]
    ppermute x48 -> x30, waiting for transfers between devices: 21.3 us -> 29.1 us  [swap(): return row_major(lax.ppermute(row_major(value), axis, pairs))]
    reduce_sum x9 -> x4, other arithmetic: 4.3 us -> 0.84 us  [the longest x3 0.7 us: own_sums(): jnp.sum(jnp.where(ids == home * per_device + s, gates, jnp.float32(0.0)),...]
    select_n x8 -> x6, other arithmetic: 4.44 us -> 1.28 us  [the longest x3 0.98 us: chip_sums(): arrived = swap(jnp.where(first, right, left), 'core', 1)]
    unnamed x22 -> x23, local copies, waits for them, and re-layouts: 1.91 us -> 4.25 us
    reshape x4 -> x0, local copies, waits for them, and re-layouts: 2.17 us -> none  [on_device(): dense_gates.reshape(groups, 2 * rows, experts_all)]
    eq x3 -> x0, other arithmetic: 1.23 us -> none  [the longest x2 1.15 us: in_order(): match = here[:, None] ^ here[None, :] == lax.axis_index(axis)]
    concatenate x13 -> x5, other arithmetic: 0.25 us -> 1.38 us  [the longest x2 0.67 us: with_fourth(): jnp.concatenate([two[:, :cut], (wide(two[:, cut:]) + wide(lower)).astype(...]
  transfers between devices with their start and end apart: 48 -> 30, of which waited for: 23 -> 15; matrix products, arithmetic and copies ran while one was open for 35% -> 29% of each run, Pallas kernels for 0% -> 0%
where the time goes in v4:
time: 91.9 us; the launch traced here: 91.6 us
  waiting for transfers between devices  29.1 us (32%)
  starting transfers between devices  27.5 us (30%)
  matrix products  19.8 us (22%)
  other arithmetic  9.33 us (10%)
  local copies, waits for them, and re-layouts  4.71 us (5%)
  between operations  1.11 us (1%)
    ppermute x30, waiting for transfers between devices, swap(): return row_major(lax.ppermute(row_major(value), axis, pairs))  29.1 us
    ppermute x30, starting transfers between devices, swap(): return row_major(lax.ppermute(row_major(value), axis, pairs))  27.5 us
    dot_general x6, matrix products, own_sums(): jnp.dot(held_tokens, in_weight[s], preferred_element_type=jnp.float32)  16 us
    unnamed x23, local copies, waits for them, and re-layouts  4.25 us
    dot_general x3, matrix products, own_sums(): jnp.dot(jnp.concatenate(hidden, 1), out_weight.reshape(per_device * half_...  3.79 us
  transfers between devices with their start and end apart: 30, of which 15 were waited for; matrix products, arithmetic and copies ran while one was open for 29% of the time, Pallas kernels for 0%

profile of v4, /device:TPU:0, one launch (start us, length us, event | category | flops | bytes accessed | tf_op | source)
XLA Modules:
  0.0 91.6 jit_solution(10380885980696909270)
XLA Ops:
  0.6 0.8 copy.15
  1.4 0.8 copy.14
  2.2 0.9 broadcast_select_fusion.16
  3.7 0.7 select_reduce_fusion.8
  4.7 2.9 %collective-permute-start.1 = (bf16[24,2176]{1,0:T(8,128)(2,1)S(1)}, bf16[24,2176]{1,0:T(8,128)(2,1)S(1)}, u32[]{:S(2)}, u32[]{:S(2)}) collective-permute-start(bf16[24,2176]{1,0:T(8,128)(2,1)S(1)} %get-tuple-element.17), channel_id=1, source_target_pairs={{0,8},{8,0},{16,24},{24,16},{1,9},{9,1},{17,25},{25,17},{2,10},{10... | collective-permute-start | bytes 313352 | tf_op jit(solution)/shard_map/ppermute | solution.py:31
  7.6 1.5 %collective-permute-start.2 = (bf16[24,2176]{1,0:T(8,128)(2,1)S(1)}, bf16[24,2176]{1,0:T(8,128)(2,1)S(1)}, u32[]{:S(2)}, u32[]{:S(2)}) collective-permute-start(bf16[24,2176]{1,0:T(8,128)(2,1)S(1)} %get-tuple-element.17), channel_id=1, source_target_pairs={{0,16},{8,24},{16,0},{24,8},{1,17},{9,25},{17,1},{25,9},{2,18},{10... | collective-permute-start | bytes 313352 | tf_op jit(solution)/shard_map/ppermute | solution.py:31
  9.1 1.6 %collective-permute-start.5 = (bf16[24,2176]{1,0:T(8,128)(2,1)S(1)}, bf16[24,2176]{1,0:T(8,128)(2,1)S(1)}, u32[]{:S(2)}, u32[]{:S(2)}) collective-permute-start(bf16[24,2176]{1,0:T(8,128)(2,1)S(1)} %get-tuple-element.17), channel_id=1, source_target_pairs={{0,2},{2,0},{4,6},{6,4},{1,3},{3,1},{5,7},{7,5},{8,10},{10,8},{12,... | collective-permute-start | bytes 313352 | tf_op jit(solution)/shard_map/ppermute | solution.py:31
  10.7 2.6 %collective-permute-start.6 = (bf16[24,2176]{1,0:T(8,128)(2,1)S(1)}, bf16[24,2176]{1,0:T(8,128)(2,1)S(1)}, u32[]{:S(2)}, u32[]{:S(2)}) collective-permute-start(bf16[24,2176]{1,0:T(8,128)(2,1)S(1)} %get-tuple-element.17), channel_id=1, source_target_pairs={{0,4},{2,6},{4,0},{6,2},{1,5},{3,7},{5,1},{7,3},{8,12},{10,14},{12... | collective-permute-start | bytes 313352 | tf_op jit(solution)/shard_map/ppermute | solution.py:31
  13.5 0.6 collective-permute-start.4
  14.5 3.8 %collective-permute-done.3 = bf16[24,1024]{1,0:T(8,128)(2,1)S(1)} collective-permute-done((bf16[24,1024]{1,0:T(8,128)(2,1)S(1)}, bf16[24,1024]{1,0:T(8,128)(2,1)S(1)}, u32[]{:S(2)}, u32[]{:S(2)}) %collective-permute-start.3) | collective-permute-done | bytes 49184 | tf_op jit(solution)/shard_map/ppermute | solution.py:31
  18.3 3.0 %collective-permute-done.6 = bf16[24,2176]{1,0:T(8,128)(2,1)S(1)} collective-permute-done((bf16[24,2176]{1,0:T(8,128)(2,1)S(1)}, bf16[24,2176]{1,0:T(8,128)(2,1)S(1)}, u32[]{:S(2)}, u32[]{:S(2)}) %collective-permute-start.6) | collective-permute-done | bytes 104480 | tf_op jit(solution)/shard_map/ppermute | solution.py:31
  21.6 0.6 collective-permute-start.14
  22.9 0.7 collective-permute-done.8
  23.8 4.2 %fusion.10 = f32[168,768]{1,0:T(8,128)S(1)} fusion(bf16[2,4096,768]{2,1,0:T(8,128)(2,1)} %param.9, bf16[168,2048]{1,0:T(8,128)(2,1)S(1)} %get-tuple-element.19, bf16[168,2048]{1,0:T(8,128)(2,1)S(1)} %get-tuple-element.18), kind=kOutput, calls=%fused_computation.10 | convolution fusion | flops 1059717120 | bytes 8183808 | tf_op jit(solution)/shard_map/dot_general | solution.py:143
  28.0 2.1 %copy-done = bf16[2,4096,768]{2,1,0:T(8,128)(2,1)S(1)} copy-done((bf16[2,4096,768]{2,1,0:T(8,128)(2,1)S(1)}, bf16[2,4096,768]{2,1,0:T(8,128)(2,1)}, u32[]{:S(2)}) %copy-start) | copy-done | bytes 12582936
  30.1 1.3 %fusion.4 = f32[168,768]{1,0:T(8,128)S(1)} fusion(bf16[2,4096,768]{2,1,0:T(8,128)(2,1)S(1)} %copy-done, bf16[168,2048]{1,0:T(8,128)(2,1)S(1)} %get-tuple-element.19, bf16[168,2048]{1,0:T(8,128)(2,1)S(1)} %get-tuple-element.18), kind=kOutput, calls=%fused_computation.4 | convolution fusion | flops 1059717120 | bytes 8183808 | tf_op jit(solution)/shard_map/dot_general | solution.py:143
  32.1 1.2 %convolution_convert_fusion = bf16[168,4096]{1,0:T(8,128)(2,1)S(1)} fusion(bf16[768,4096]{1,0:T(8,128)(2,1)S(1)} %bitcast.20, bf16[168,384]{1,0:T(8,128)(2,1)S(1)} %get-tuple-element.54, bf16[168,384]{1,0:T(8,128)(2,1)S(1)} %get-tuple-element.55), kind=kOutput, calls=%fused_computation.12 | convolution fusion | flops 1058168832 | bytes 7925760 | tf_op jit(solution)/shard_map/dot_general | solution.py:146
  34.3 0.8 collective-permute-start.19
  35.0 1.5 %collective-permute-start.18 = (bf16[72,1024]{1,0:T(8,128)(2,1)S(1)}, bf16[72,1024]{1,0:T(8,128)(2,1)S(1)}, u32[]{:S(2)}, u32[]{:S(2)}) collective-permute-start(bf16[72,1024]{1,0:T(8,128)(2,1)S(1)} %slice.287), channel_id=1, source_target_pairs={{0,16},{8,24},{16,0},{24,8},{1,17},{9,25},{17,1},{25,9},{2,18},{10... | collective-permute-start | bytes 442376 | tf_op jit(solution)/shard_map/ppermute | solution.py:31
  36.9 1.1 %fusion.8 = f32[144,768]{1,0:T(8,128)S(1)} fusion(bf16[2,4096,768]{2,1,0:T(8,128)(2,1)S(1)} %copy-done, bf16[144,2048]{1,0:T(8,128)(2,1)S(1)} %get-tuple-element.21, bf16[144,2048]{1,0:T(8,128)(2,1)S(1)} %get-tuple-element.20), kind=kOutput, calls=%fused_computation.8 | convolution fusion | flops 908328960 | bytes 7913472 | tf_op jit(solution)/shard_map/dot_general | solution.py:143
  38.1 1.1 %fusion.2 = f32[144,768]{1,0:T(8,128)S(1)} fusion(bf16[2,4096,768]{2,1,0:T(8,128)(2,1)S(1)} %copy-done, bf16[144,2048]{1,0:T(8,128)(2,1)S(1)} %get-tuple-element.21, bf16[144,2048]{1,0:T(8,128)(2,1)S(1)} %get-tuple-element.20), kind=kOutput, calls=%fused_computation.2 | convolution fusion | flops 908328960 | bytes 7913472 | tf_op jit(solution)/shard_map/dot_general | solution.py:143
  39.4 1.1 %convolution_convert_fusion.1 = bf16[144,4096]{1,0:T(8,128)(2,1)S(1)} fusion(bf16[768,4096]{1,0:T(8,128)(2,1)S(1)} %bitcast.21, bf16[144,384]{1,0:T(8,128)(2,1)S(1)} %fusion.26, bf16[144,384]{1,0:T(8,128)(2,1)S(1)} %fusion.28), kind=kOutput, calls=%fused_computation.13 | convolution fusion | flops 907001856 | bytes 7692288 | tf_op jit(solution)/shard_map/dot_general | solution.py:146
  41.5 1.3 %collective-permute-start.12 = (bf16[24,1024]{1,0:T(8,128)(2,1)S(1)}, bf16[24,1024]{1,0:T(8,128)(2,1)S(1)}, u32[]{:S(2)}, u32[]{:S(2)}) collective-permute-start(bf16[24,1024]{1,0:T(8,128)(2,1)S(1)} %get-tuple-element.23), channel_id=1, source_target_pairs={{0,8},{8,0},{16,24},{24,16},{1,9},{9,1},{17,25},{25,17},{2,10},{10... | collective-permute-start | bytes 147464 | tf_op jit(solution)/shard_map/ppermute | solution.py:31
  42.7 0.9 broadcast_select_fusion.3
  43.6 1.4 %collective-permute-done.10 = bf16[24,1024]{1,0:T(8,128)(2,1)S(1)} collective-permute-done((bf16[24,1024]{1,0:T(8,128)(2,1)S(1)}, bf16[24,1024]{1,0:T(8,128)(2,1)S(1)}, u32[]{:S(2)}, u32[]{:S(2)}) %collective-permute-start.10) | collective-permute-done | bytes 49184 | tf_op jit(solution)/shard_map/ppermute | solution.py:31
  45.6 0.6 pad_maximum_fusion.15
  46.2 1.5 %collective-permute-start.13 = (bf16[24,2048]{1,0:T(8,128)(2,1)}, bf16[24,2048]{1,0:T(8,128)(2,1)}, u32[]{:S(2)}, u32[]{:S(2)}) collective-permute-start(bf16[24,2048]{1,0:T(8,128)(2,1)} %pad_maximum_fusion.15), channel_id=1, source_target_pairs={{0,16},{8,24},{16,0},{24,8},{1,17},{9,25},{17,1},{25,9},{2,18},{10... | collective-permute-start | bytes 294920 | tf_op jit(solution)/shard_map/ppermute | solution.py:31
  47.8 0.6 pad_maximum_fusion.14
  49.6 1.1 %collective-permute-done.20 = bf16[72,2048]{1,0:T(8,128)(2,1)S(1)} collective-permute-done((bf16[72,2048]{1,0:T(8,128)(2,1)S(1)}, bf16[72,2048]{1,0:T(8,128)(2,1)S(1)}, u32[]{:S(2)}, u32[]{:S(2)}) %collective-permute-start.20) | collective-permute-done | bytes 294944 | tf_op jit(solution)/shard_map/ppermute | solution.py:31
  50.8 4.1 %fusion.6 = f32[72,768]{1,0:T(8,128)S(1)} fusion(bf16[2,4096,768]{2,1,0:T(8,128)(2,1)} %param.9, bf16[72,2048]{1,0:T(8,128)(2,1)S(1)} %get-tuple-element.33, bf16[72,2048]{1,0:T(8,128)(2,1)S(1)} %get-tuple-element.32), kind=kOutput, calls=%fused_computation.6 | convolution fusion | flops 454164480 | bytes 7102464 | tf_op jit(solution)/shard_map/dot_general | solution.py:143
  55.0 4.1 %fusion = f32[72,768]{1,0:T(8,128)S(1)} fusion(bf16[2,4096,768]{2,1,0:T(8,128)(2,1)} %param.9, bf16[72,2048]{1,0:T(8,128)(2,1)S(1)} %get-tuple-element.33, bf16[72,2048]{1,0:T(8,128)(2,1)S(1)} %get-tuple-element.32), kind=kOutput, calls=%fused_computation | convolution fusion | flops 454164480 | bytes 7102464 | tf_op jit(solution)/shard_map/dot_general | solution.py:143
  59.3 1.4 %convolution_convert_fusion.2 = bf16[72,4096]{1,0:T(8,128)(2,1)S(1)} fusion(bf16[768,4096]{1,0:T(8,128)(2,1)S(1)} %bitcast.24, bf16[72,384]{1,0:T(8,128)(2,1)S(1)} %fusion.33, bf16[72,384]{1,0:T(8,128)(2,1)S(1)} %fusion.35), kind=kOutput, calls=%fused_computation.20 | convolution fusion | flops 453500928 | bytes 6991872 | tf_op jit(solution)/shard_map/dot_general | solution.py:146
  61.2 1.2 %collective-permute-done.21 = bf16[72,2048]{1,0:T(8,128)(2,1)S(1)} collective-permute-done((bf16[72,2048]{1,0:T(8,128)(2,1)S(1)}, bf16[72,2048]{1,0:T(8,128)(2,1)S(1)}, u32[]{:S(2)}, u32[]{:S(2)}) %collective-permute-start.21) | collective-permute-done | bytes 294944 | tf_op jit(solution)/shard_map/ppermute | solution.py:31
  62.5 1.3 %collective-permute-start.22 = (bf16[72,1024]{1,0:T(8,128)(2,1)S(1)}, bf16[72,1024]{1,0:T(8,128)(2,1)S(1)}, u32[]{:S(2)}, u32[]{:S(2)}) collective-permute-start(bf16[72,1024]{1,0:T(8,128)(2,1)S(1)} %get-tuple-element.37), channel_id=1, source_target_pairs={{0,16},{8,24},{16,0},{24,8},{1,17},{9,25},{17,1},{25,9},{2,18},{10... | collective-permute-start | bytes 442376 | tf_op jit(solution)/shard_map/ppermute | solution.py:31
  63.8 0.8 collective-permute-start.24
  64.6 3.9 %collective-permute-done.22 = bf16[72,1024]{1,0:T(8,128)(2,1)S(1)} collective-permute-done((bf16[72,1024]{1,0:T(8,128)(2,1)S(1)}, bf16[72,1024]{1,0:T(8,128)(2,1)S(1)}, u32[]{:S(2)}, u32[]{:S(2)}) %collective-permute-start.22) | collective-permute-done | bytes 147488 | tf_op jit(solution)/shard_map/ppermute | solution.py:31
  68.5 1.0 %collective-permute-done.24 = bf16[72,1024]{1,0:T(8,128)(2,1)S(1)} collective-permute-done((bf16[72,1024]{1,0:T(8,128)(2,1)S(1)}, bf16[72,1024]{1,0:T(8,128)(2,1)S(1)}, u32[]{:S(2)}, u32[]{:S(2)}) %collective-permute-start.24) | collective-permute-done | bytes 147488 | tf_op jit(solution)/shard_map/ppermute | solution.py:31
  69.6 0.8 collective-permute-start.23
  70.4 1.6 %collective-permute-start.25 = (bf16[72,2048]{1,0:T(8,128)(2,1)S(1)}, bf16[72,2048]{1,0:T(8,128)(2,1)S(1)}, u32[]{:S(2)}, u32[]{:S(2)}) collective-permute-start(bf16[72,2048]{1,0:T(8,128)(2,1)S(1)} %pad_maximum_fusion.11), channel_id=1, source_target_pairs={{0,16},{8,24},{16,0},{24,8},{1,17},{9,25},{17,1},{25,9},{2,18},{10... | collective-permute-start | bytes 884744 | tf_op jit(solution)/shard_map/ppermute | solution.py:31
  72.1 5.4 %collective-permute-done.23 = bf16[72,2048]{1,0:T(8,128)(2,1)S(1)} collective-permute-done((bf16[72,2048]{1,0:T(8,128)(2,1)S(1)}, bf16[72,2048]{1,0:T(8,128)(2,1)S(1)}, u32[]{:S(2)}, u32[]{:S(2)}) %collective-permute-start.23) | collective-permute-done | bytes 294944 | tf_op jit(solution)/shard_map/ppermute | solution.py:31
  77.5 0.7 collective-permute-done.25
  78.3 1.7 %collective-permute-start.26 = (bf16[24,2048]{1,0:T(8,128)(2,1)S(1)}, bf16[24,2048]{1,0:T(8,128)(2,1)S(1)}, u32[]{:S(2)}, u32[]{:S(2)}) collective-permute-start(bf16[24,2048]{1,0:T(8,128)(2,1)S(1)} %get-tuple-element.34), channel_id=1, source_target_pairs={{0,2},{2,0},{4,6},{6,4},{1,3},{3,1},{5,7},{7,5},{8,10},{10,8},{12,... | collective-permute-start | bytes 294920 | tf_op jit(solution)/shard_map/ppermute | solution.py:31
  80.1 1.4 %collective-permute-start.27 = (bf16[24,2048]{1,0:T(8,128)(2,1)S(1)}, bf16[24,2048]{1,0:T(8,128)(2,1)S(1)}, u32[]{:S(2)}, u32[]{:S(2)}) collective-permute-start(bf16[24,2048]{1,0:T(8,128)(2,1)S(1)} %get-tuple-element.36), channel_id=1, source_target_pairs={{0,4},{2,6},{4,0},{6,2},{1,5},{3,7},{5,1},{7,3},{8,12},{10,14},{12... | collective-permute-start | bytes 294920 | tf_op jit(solution)/shard_map/ppermute | solution.py:31
  81.5 1.3 %collective-permute-start.28 = (bf16[24,2048]{1,0:T(8,128)(2,1)S(1)}, bf16[24,2048]{1,0:T(8,128)(2,1)S(1)}, u32[]{:S(2)}, u32[]{:S(2)}) collective-permute-start(bf16[24,2048]{1,0:T(8,128)(2,1)S(1)} %get-tuple-element.35), channel_id=1, source_target_pairs={{0,6},{2,4},{4,2},{6,0},{1,7},{3,5},{5,3},{7,1},{8,14},{10,12},{12... | collective-permute-start | bytes 294920 | tf_op jit(solution)/shard_map/ppermute | solution.py:31
  83.2 5.3 %collective-permute-done.27 = bf16[24,2048]{1,0:T(8,128)(2,1)S(1)} collective-permute-done((bf16[24,2048]{1,0:T(8,128)(2,1)S(1)}, bf16[24,2048]{1,0:T(8,128)(2,1)S(1)}, u32[]{:S(2)}, u32[]{:S(2)}) %collective-permute-start.27) | collective-permute-done | bytes 98336 | tf_op jit(solution)/shard_map/ppermute | solution.py:31
  88.5 1.0 %add_convert_fusion.6 = bf16[24,2048]{1,0:T(8,128)(2,1)S(1)} fusion(bf16[24,2048]{1,0:T(8,128)(2,1)S(1)} %collective-permute-done.28, bf16[24,2048]{1,0:T(8,128)(2,1)S(1)} %collective-permute-done.27, bf16[24,2048]{1,0:T(8,128)(2,1)S(1)} %collective-permute-done.26, bf16[24,2048]{1,0:T(8,128)(2,1)} %collective-permute-done.13, ...), kind=kLoop, calls=%fused_computation.63 | loop fusion | flops 688128 | bytes 688128 | tf_op jit(solution)/shard_map/convert_element_type | solution.py:191
  90.2 0.7 collective-permute-done.29
  90.9 0.7 pad_maximum_fusion.12
  (108 shorter events, 9.7 us)
Async XLA Ops:
  3.2 1.4 %collective-permute-start = (bf16[12,2176]{1,0:T(8,128)(2,1)S(1)}, bf16[12,2176]{1,0:T(8,128)(2,1)S(1)}, u32[]{:S(2)}, u32[]{:S(2)}) collective-permute-start(bf16[12,2176]{1,0:T(8,128)(2,1)S(1)} %pad_maximum_fusion.16), channel_id=1, source_target_pairs={{0,1},{1,0},{2,3},{3,2},{4,5},{5,4},{6,7},{7,6},{8,9},{9,8},{10,11... | collective-permute-start | bytes 156680 | tf_op jit(solution)/shard_map/ppermute | solution.py:31
  4.7 9.5 %collective-permute-start.1 = (bf16[24,2176]{1,0:T(8,128)(2,1)S(1)}, bf16[24,2176]{1,0:T(8,128)(2,1)S(1)}, u32[]{:S(2)}, u32[]{:S(2)}) collective-permute-start(bf16[24,2176]{1,0:T(8,128)(2,1)S(1)} %get-tuple-element.17), channel_id=1, source_target_pairs={{0,8},{8,0},{16,24},{24,16},{1,9},{9,1},{17,25},{25,17},{2,10},{10... | collective-permute-start | bytes 313352 | tf_op jit(solution)/shard_map/ppermute | solution.py:31
  7.6 5.9 %collective-permute-start.2 = (bf16[24,2176]{1,0:T(8,128)(2,1)S(1)}, bf16[24,2176]{1,0:T(8,128)(2,1)S(1)}, u32[]{:S(2)}, u32[]{:S(2)}) collective-permute-start(bf16[24,2176]{1,0:T(8,128)(2,1)S(1)} %get-tuple-element.17), channel_id=1, source_target_pairs={{0,16},{8,24},{16,0},{24,8},{1,17},{9,25},{17,1},{25,9},{2,18},{10... | collective-permute-start | bytes 313352 | tf_op jit(solution)/shard_map/ppermute | solution.py:31
  9.1 9.2 %collective-permute-start.5 = (bf16[24,2176]{1,0:T(8,128)(2,1)S(1)}, bf16[24,2176]{1,0:T(8,128)(2,1)S(1)}, u32[]{:S(2)}, u32[]{:S(2)}) collective-permute-start(bf16[24,2176]{1,0:T(8,128)(2,1)S(1)} %get-tuple-element.17), channel_id=1, source_target_pairs={{0,2},{2,0},{4,6},{6,4},{1,3},{3,1},{5,7},{7,5},{8,10},{10,8},{12,... | collective-permute-start | bytes 313352 | tf_op jit(solution)/shard_map/ppermute | solution.py:31
  10.7 10.6 %collective-permute-start.6 = (bf16[24,2176]{1,0:T(8,128)(2,1)S(1)}, bf16[24,2176]{1,0:T(8,128)(2,1)S(1)}, u32[]{:S(2)}, u32[]{:S(2)}) collective-permute-start(bf16[24,2176]{1,0:T(8,128)(2,1)S(1)} %get-tuple-element.17), channel_id=1, source_target_pairs={{0,4},{2,6},{4,0},{6,2},{1,5},{3,7},{5,1},{7,3},{8,12},{10,14},{12... | collective-permute-start | bytes 313352 | tf_op jit(solution)/shard_map/ppermute | solution.py:31
  13.3 8.1 %collective-permute-start.7 = (bf16[24,2176]{1,0:T(8,128)(2,1)S(1)}, bf16[24,2176]{1,0:T(8,128)(2,1)S(1)}, u32[]{:S(2)}, u32[]{:S(2)}) collective-permute-start(bf16[24,2176]{1,0:T(8,128)(2,1)S(1)} %get-tuple-element.17), channel_id=1, source_target_pairs={{0,6},{2,4},{4,2},{6,0},{1,7},{3,5},{5,3},{7,1},{8,14},{10,12},{12... | collective-permute-start | bytes 313352 | tf_op jit(solution)/shard_map/ppermute | solution.py:31
  13.5 4.8 %collective-permute-start.4 = (bf16[24,1152]{1,0:T(8,128)(2,1)S(1)}, bf16[24,1152]{1,0:T(8,128)(2,1)S(1)}, u32[]{:S(2)}, u32[]{:S(2)}) collective-permute-start(bf16[24,1152]{1,0:T(8,128)(2,1)S(1)} %slice.327), channel_id=1, source_target_pairs={{0,8},{8,0},{16,24},{24,16},{1,9},{9,1},{17,25},{25,17},{2,10},{10... | collective-permute-start | bytes 165896 | tf_op jit(solution)/shard_map/ppermute | solution.py:31
  14.1 4.2 %collective-permute-start.3 = (bf16[24,1024]{1,0:T(8,128)(2,1)S(1)}, bf16[24,1024]{1,0:T(8,128)(2,1)S(1)}, u32[]{:S(2)}, u32[]{:S(2)}) collective-permute-start(bf16[24,1024]{1,0:T(8,128)(2,1)S(1)} %slice.326), channel_id=1, source_target_pairs={{0,16},{8,24},{16,0},{24,8},{1,17},{9,25},{17,1},{25,9},{2,18},{10... | collective-permute-start | bytes 147464 | tf_op jit(solution)/shard_map/ppermute | solution.py:31
  21.5 2.2 %collective-permute-start.8 = (bf16[168,2048]{1,0:T(8,128)(2,1)S(1)}, bf16[168,2048]{1,0:T(8,128)(2,1)S(1)}, u32[]{:S(2)}, u32[]{:S(2)}) collective-permute-start(bf16[168,2048]{1,0:T(8,128)(2,1)S(1)} %slice.328), channel_id=1, source_target_pairs={{0,1},{1,0},{2,3},{3,2},{4,5},{5,4},{6,7},{7,6},{8,9},{9,8},{10,11... | collective-permute-start | bytes 2064392 | tf_op jit(solution)/shard_map/ppermute | solution.py:31
  21.6 11.8 %collective-permute-start.14 = (bf16[72,2176]{1,0:T(8,128)(2,1)S(1)}, bf16[72,2176]{1,0:T(8,128)(2,1)S(1)}, u32[]{:S(2)}, u32[]{:S(2)}) collective-permute-start(bf16[72,2176]{1,0:T(8,128)(2,1)S(1)} %get-tuple-element.46), channel_id=1, source_target_pairs={{0,8},{8,0},{16,24},{24,16},{1,9},{9,1},{17,25},{25,17},{2,10},{10... | collective-permute-start | bytes 940040 | tf_op jit(solution)/shard_map/ppermute | solution.py:31
  22.2 11.2 %collective-permute-start.15 = (bf16[72,2176]{1,0:T(8,128)(2,1)S(1)}, bf16[72,2176]{1,0:T(8,128)(2,1)S(1)}, u32[]{:S(2)}, u32[]{:S(2)}) collective-permute-start(bf16[72,2176]{1,0:T(8,128)(2,1)S(1)} %get-tuple-element.46), channel_id=1, source_target_pairs={{0,16},{8,24},{16,0},{24,8},{1,17},{9,25},{17,1},{25,9},{2,18},{10... | collective-permute-start | bytes 940040 | tf_op jit(solution)/shard_map/ppermute | solution.py:31
  23.7 6.4 %copy-start = (bf16[2,4096,768]{2,1,0:T(8,128)(2,1)S(1)}, bf16[2,4096,768]{2,1,0:T(8,128)(2,1)}, u32[]{:S(2)}) copy-start(bf16[2,4096,768]{2,1,0:T(8,128)(2,1)} %param.9) | copy-start | bytes 37748740
  23.8 7.8 %slice-start = ((s8[6291456]{0:T(1024)(128)(4,1)}), s8[4194304]{0:T(1024)(128)(4,1)S(1)}, s32[]{:S(2)}) async-start(s8[6291456]{0:T(1024)(128)(4,1)} %bitcast.18), calls=%async_computation | async-start | bytes 8388608
  30.1 2.0 %slice-start.1 = ((s8[6291456]{0:T(1024)(128)(4,1)}), s8[2097152]{0:T(1024)(128)(4,1)S(1)}, s32[]{:S(2)}) async-start(s8[6291456]{0:T(1024)(128)(4,1)} %bitcast.18), calls=%async_computation.1 | async-start | bytes 4194304
  33.5 3.3 %collective-permute-start.16 = (bf16[144,2048]{1,0:T(8,128)(2,1)S(1)}, bf16[144,2048]{1,0:T(8,128)(2,1)S(1)}, u32[]{:S(2)}, u32[]{:S(2)}) collective-permute-start(bf16[144,2048]{1,0:T(8,128)(2,1)S(1)} %slice.347), channel_id=1, source_target_pairs={{0,1},{1,0},{2,3},{3,2},{4,5},{5,4},{6,7},{7,6},{8,9},{9,8},{10,11... | collective-permute-start | bytes 1769480 | tf_op jit(solution)/shard_map/ppermute | solution.py:31
  33.8 6.7 %collective-permute-start.9 = (bf16[168,2048]{1,0:T(8,128)(2,1)S(1)}, bf16[168,2048]{1,0:T(8,128)(2,1)S(1)}, u32[]{:S(2)}, u32[]{:S(2)}) collective-permute-start(bf16[168,2048]{1,0:T(8,128)(2,1)S(1)} %broadcast_select_fusion), channel_id=1, source_target_pairs={{0,1},{1,0},{2,3},{3,2},{4,5},{5,4},{6,7},{7,6},{8,9},{9,8},{10,11... | collective-permute-start | bytes 2064392 | tf_op jit(solution)/shard_map/ppermute | solution.py:31
  34.3 14.7 %collective-permute-start.19 = (bf16[72,1152]{1,0:T(8,128)(2,1)S(1)}, bf16[72,1152]{1,0:T(8,128)(2,1)S(1)}, u32[]{:S(2)}, u32[]{:S(2)}) collective-permute-start(bf16[72,1152]{1,0:T(8,128)(2,1)S(1)} %slice.288), channel_id=1, source_target_pairs={{0,8},{8,0},{16,24},{24,16},{1,9},{9,1},{17,25},{25,17},{2,10},{10... | collective-permute-start | bytes 497672 | tf_op jit(solution)/shard_map/ppermute | solution.py:31
  35.0 13.9 %collective-permute-start.18 = (bf16[72,1024]{1,0:T(8,128)(2,1)S(1)}, bf16[72,1024]{1,0:T(8,128)(2,1)S(1)}, u32[]{:S(2)}, u32[]{:S(2)}) collective-permute-start(bf16[72,1024]{1,0:T(8,128)(2,1)S(1)} %slice.287), channel_id=1, source_target_pairs={{0,16},{8,24},{16,0},{24,8},{1,17},{9,25},{17,1},{25,9},{2,18},{10... | collective-permute-start | bytes 442376 | tf_op jit(solution)/shard_map/ppermute | solution.py:31
  40.9 4.2 %collective-permute-start.10 = (bf16[24,1024]{1,0:T(8,128)(2,1)S(1)}, bf16[24,1024]{1,0:T(8,128)(2,1)S(1)}, u32[]{:S(2)}, u32[]{:S(2)}) collective-permute-start(bf16[24,1024]{1,0:T(8,128)(2,1)S(1)} %get-tuple-element.25), channel_id=1, source_target_pairs={{0,16},{8,24},{16,0},{24,8},{1,17},{9,25},{17,1},{25,9},{2,18},{10... | collective-permute-start | bytes 147464 | tf_op jit(solution)/shard_map/ppermute | solution.py:31
  41.5 4.1 %collective-permute-start.12 = (bf16[24,1024]{1,0:T(8,128)(2,1)S(1)}, bf16[24,1024]{1,0:T(8,128)(2,1)S(1)}, u32[]{:S(2)}, u32[]{:S(2)}) collective-permute-start(bf16[24,1024]{1,0:T(8,128)(2,1)S(1)} %get-tuple-element.23), channel_id=1, source_target_pairs={{0,8},{8,0},{16,24},{24,16},{1,9},{9,1},{17,25},{25,17},{2,10},{10... | collective-permute-start | bytes 147464 | tf_op jit(solution)/shard_map/ppermute | solution.py:31
  43.6 17.3 %collective-permute-start.17 = (bf16[144,2048]{1,0:T(8,128)(2,1)}, bf16[144,2048]{1,0:T(8,128)(2,1)S(1)}, u32[]{:S(2)}, u32[]{:S(2)}) collective-permute-start(bf16[144,2048]{1,0:T(8,128)(2,1)} %broadcast_select_fusion.3), channel_id=1, source_target_pairs={{0,1},{1,0},{2,3},{3,2},{4,5},{5,4},{6,7},{7,6},{8,9},{9,8},{10,11... | collective-permute-start | bytes 1769480 | tf_op jit(solution)/shard_map/ppermute | solution.py:31
  46.2 36.7 %collective-permute-start.13 = (bf16[24,2048]{1,0:T(8,128)(2,1)}, bf16[24,2048]{1,0:T(8,128)(2,1)}, u32[]{:S(2)}, u32[]{:S(2)}) collective-permute-start(bf16[24,2048]{1,0:T(8,128)(2,1)} %pad_maximum_fusion.15), channel_id=1, source_target_pairs={{0,16},{8,24},{16,0},{24,8},{1,17},{9,25},{17,1},{25,9},{2,18},{10... | collective-permute-start | bytes 294920 | tf_op jit(solution)/shard_map/ppermute | solution.py:31
  48.4 34.5 %collective-permute-start.11 = (bf16[24,2048]{1,0:T(8,128)(2,1)}, bf16[24,2048]{1,0:T(8,128)(2,1)}, u32[]{:S(2)}, u32[]{:S(2)}) collective-permute-start(bf16[24,2048]{1,0:T(8,128)(2,1)} %pad_maximum_fusion.14), channel_id=1, source_target_pairs={{0,8},{8,0},{16,24},{24,16},{1,9},{9,1},{17,25},{25,17},{2,10},{10... | collective-permute-start | bytes 294920 | tf_op jit(solution)/shard_map/ppermute | solution.py:31
  49.1 1.6 %collective-permute-start.20 = (bf16[72,2048]{1,0:T(8,128)(2,1)S(1)}, bf16[72,2048]{1,0:T(8,128)(2,1)S(1)}, u32[]{:S(2)}, u32[]{:S(2)}) collective-permute-start(bf16[72,2048]{1,0:T(8,128)(2,1)S(1)} %pad_maximum_fusion.9), channel_id=1, source_target_pairs={{0,1},{1,0},{2,3},{3,2},{4,5},{5,4},{6,7},{7,6},{8,9},{9,8},{10,11... | collective-permute-start | bytes 884744 | tf_op jit(solution)/shard_map/ppermute | solution.py:31
  50.8 8.4 %slice-start.2 = ((s8[6291456]{0:T(1024)(128)(4,1)}), s8[4194304]{0:T(1024)(128)(4,1)S(1)}, s32[]{:S(2)}) async-start(s8[6291456]{0:T(1024)(128)(4,1)} %bitcast.22), calls=%async_computation.2 | async-start | bytes 8388608
  55.0 4.3 %slice-start.3 = ((s8[6291456]{0:T(1024)(128)(4,1)}), s8[2097152]{0:T(1024)(128)(4,1)S(1)}, s32[]{:S(2)}) async-start(s8[6291456]{0:T(1024)(128)(4,1)} %bitcast.22), calls=%async_computation.3 | async-start | bytes 4194304
  60.7 1.6 %collective-permute-start.21 = (bf16[72,2048]{1,0:T(8,128)(2,1)S(1)}, bf16[72,2048]{1,0:T(8,128)(2,1)S(1)}, u32[]{:S(2)}, u32[]{:S(2)}) collective-permute-start(bf16[72,2048]{1,0:T(8,128)(2,1)S(1)} %broadcast_select_fusion.6), channel_id=1, source_target_pairs={{0,1},{1,0},{2,3},{3,2},{4,5},{5,4},{6,7},{7,6},{8,9},{9,8},{10,11... | collective-permute-start | bytes 884744 | tf_op jit(solution)/shard_map/ppermute | solution.py:31
  62.5 6.0 %collective-permute-start.22 = (bf16[72,1024]{1,0:T(8,128)(2,1)S(1)}, bf16[72,1024]{1,0:T(8,128)(2,1)S(1)}, u32[]{:S(2)}, u32[]{:S(2)}) collective-permute-start(bf16[72,1024]{1,0:T(8,128)(2,1)S(1)} %get-tuple-element.37), channel_id=1, source_target_pairs={{0,16},{8,24},{16,0},{24,8},{1,17},{9,25},{17,1},{25,9},{2,18},{10... | collective-permute-start | bytes 442376 | tf_op jit(solution)/shard_map/ppermute | solution.py:31
  63.8 5.6 %collective-permute-start.24 = (bf16[72,1024]{1,0:T(8,128)(2,1)S(1)}, bf16[72,1024]{1,0:T(8,128)(2,1)S(1)}, u32[]{:S(2)}, u32[]{:S(2)}) collective-permute-start(bf16[72,1024]{1,0:T(8,128)(2,1)S(1)} %get-tuple-element.38), channel_id=1, source_target_pairs={{0,8},{8,0},{16,24},{24,16},{1,9},{9,1},{17,25},{25,17},{2,10},{10... | collective-permute-start | bytes 442376 | tf_op jit(solution)/shard_map/ppermute | solution.py:31
  69.6 8.0 %collective-permute-start.23 = (bf16[72,2048]{1,0:T(8,128)(2,1)S(1)}, bf16[72,2048]{1,0:T(8,128)(2,1)S(1)}, u32[]{:S(2)}, u32[]{:S(2)}) collective-permute-start(bf16[72,2048]{1,0:T(8,128)(2,1)S(1)} %pad_maximum_fusion.10), channel_id=1, source_target_pairs={{0,8},{8,0},{16,24},{24,16},{1,9},{9,1},{17,25},{25,17},{2,10},{10... | collective-permute-start | bytes 884744 | tf_op jit(solution)/shard_map/ppermute | solution.py:31
  70.4 7.8 %collective-permute-start.25 = (bf16[72,2048]{1,0:T(8,128)(2,1)S(1)}, bf16[72,2048]{1,0:T(8,128)(2,1)S(1)}, u32[]{:S(2)}, u32[]{:S(2)}) collective-permute-start(bf16[72,2048]{1,0:T(8,128)(2,1)S(1)} %pad_maximum_fusion.11), channel_id=1, source_target_pairs={{0,16},{8,24},{16,0},{24,8},{1,17},{9,25},{17,1},{25,9},{2,18},{10... | collective-permute-start | bytes 884744 | tf_op jit(solution)/shard_map/ppermute | solution.py:31
  78.3 4.9 %collective-permute-start.26 = (bf16[24,2048]{1,0:T(8,128)(2,1)S(1)}, bf16[24,2048]{1,0:T(8,128)(2,1)S(1)}, u32[]{:S(2)}, u32[]{:S(2)}) collective-permute-start(bf16[24,2048]{1,0:T(8,128)(2,1)S(1)} %get-tuple-element.34), channel_id=1, source_target_pairs={{0,2},{2,0},{4,6},{6,4},{1,3},{3,1},{5,7},{7,5},{8,10},{10,8},{12,... | collective-permute-start | bytes 294920 | tf_op jit(solution)/shard_map/ppermute | solution.py:31
  80.1 8.5 %collective-permute-start.27 = (bf16[24,2048]{1,0:T(8,128)(2,1)S(1)}, bf16[24,2048]{1,0:T(8,128)(2,1)S(1)}, u32[]{:S(2)}, u32[]{:S(2)}) collective-permute-start(bf16[24,2048]{1,0:T(8,128)(2,1)S(1)} %get-tuple-element.36), channel_id=1, source_target_pairs={{0,4},{2,6},{4,0},{6,2},{1,5},{3,7},{5,1},{7,3},{8,12},{10,14},{12... | collective-permute-start | bytes 294920 | tf_op jit(solution)/shard_map/ppermute | solution.py:31
  81.5 7.1 %collective-permute-start.28 = (bf16[24,2048]{1,0:T(8,128)(2,1)S(1)}, bf16[24,2048]{1,0:T(8,128)(2,1)S(1)}, u32[]{:S(2)}, u32[]{:S(2)}) collective-permute-start(bf16[24,2048]{1,0:T(8,128)(2,1)S(1)} %get-tuple-element.35), channel_id=1, source_target_pairs={{0,6},{2,4},{4,2},{6,0},{1,7},{3,5},{5,3},{7,1},{8,14},{10,12},{12... | collective-permute-start | bytes 294920 | tf_op jit(solution)/shard_map/ppermute | solution.py:31
  89.6 1.3 %collective-permute-start.29 = (bf16[12,2048]{1,0:T(8,128)(2,1)S(1)}, bf16[12,2048]{1,0:T(8,128)(2,1)S(1)}, u32[]{:S(2)}, u32[]{:S(2)}) collective-permute-start(bf16[12,2048]{1,0:T(8,128)(2,1)S(1)} %broadcast_select_fusion.13), channel_id=1, source_target_pairs={{0,1},{1,0},{2,3},{3,2},{4,5},{5,4},{6,7},{7,6},{8,9},{9,8},{10,11... | collective-permute-start | bytes 147464 | tf_op jit(solution)/shard_map/ppermute | solution.py:31

commit v5 on v4

--- a/solution.py
+++ b/solution.py
@@ -1,6 +1,8 @@
 import jax
 import jax.numpy as jnp
 from jax import lax
+from jax.experimental import pallas as pl
+from jax.experimental.pallas import tpu as pltpu
 from jax.experimental.layout import Layout, with_layout_constraint
 from jax.sharding import Mesh, PartitionSpec as P
 
@@ -86,6 +88,30 @@
     for k, block in enumerate(blocks[1:], 1):
         total = total + wide(swap(block, "dp", k))
     return total.astype(jnp.bfloat16)
+
+
+def load_kernel(up_ref, down_ref, up_out, down_out, sems):
+    copies = [
+        pltpu.make_async_copy(up_ref, up_out, sems.at[0]),
+        pltpu.make_async_copy(down_ref, down_out, sems.at[1]),
+    ]
+    for copy in copies:
+        copy.start()
+    for copy in copies:
+        copy.wait()
+
+
+def loaded(up, down):
+    nbytes = up.nbytes + down.nbytes
+    return pl.pallas_call(
+        load_kernel,
+        in_specs=[pl.BlockSpec(memory_space=pl.ANY)] * 2,
+        out_specs=[pl.BlockSpec(memory_space=pltpu.VMEM)] * 2,
+        out_shape=[pltpu.VMEM(up.shape, up.dtype), pltpu.VMEM(down.shape, down.dtype)],
+        scratch_shapes=[pltpu.SemaphoreType.DMA((2,))],
+        compiler_params=pltpu.CompilerParams(vmem_limit_bytes=32 * 2**20),
+        cost_estimate=pl.CostEstimate(flops=0, bytes_accessed=nbytes, transcendentals=0),
+    )(up, down)
 
 
 def on_device(tokens, expert_ids, gate_probs, in_weight, out_weight, swap_slot):
@@ -161,33 +187,30 @@
         return [chip_sum[low:high] for low, high in zip(edges, edges[1:])]
 
     others = [swap(chip_rows, "chip", j) for j in range(1, chips)]
-    near = [chip_rows, *spread_near(chip_rows)]
+    near = [chip_rows, *spread_near(behind(chip_rows, others[0]))]
     near += joined(spread_rest(near[1:]))
+    in_weight, out_weight = loaded(*behind((in_weight, out_weight), near[1:3]))
     far = [row_major(jnp.concatenate(others, 0))]
     far += spread_near(far[0])
     first_blocks = [*near, far[0]]
     first_part = own_sums(first_blocks)
     far[1:] = behind(far[1:], first_part)
     rest = spread_rest(far[1:])
-    first_sums = chip_sums(first_part, first_blocks)
-    near_sums, far_sums = first_sums[:groups], first_sums[groups:]
-    near_sums = with_fourth(near_sums)
+    sums = chip_sums(first_part, first_blocks)
     part_two = own_sums(far[1:])
     if rest:
-        rest = joined(behind(rest, (part_two, near_sums)))
+        rest = joined(behind(rest, part_two))
         part_three = own_sums(rest)
-        far_sums += chip_sums(part_two, far[1:]) + chip_sums(part_three, rest)
+        sums += chip_sums(part_two, far[1:]) + chip_sums(part_three, rest)
     else:
-        far_sums += chip_sums(part_two, far[1:])
+        sums += chip_sums(part_two, far[1:])
     far += rest
-    near_total = collected(near_sums)
-    far_sums = with_fourth(far_sums)
-    far_total = collected(far_sums)
-
-    total = wide(near_total)
+    sums = [jnp.concatenate([sums[k], sums[groups + k]], 0) for k in range(groups)]
+    total = collected(with_fourth(sums))
+    blocks = [total[j * 2 * rows : (j + 1) * 2 * rows] for j in range(chips)]
+    total = wide(blocks[0])
     for j in range(1, chips):
-        block = far_total[(j - 1) * 2 * rows : j * 2 * rows]
-        total = total + wide(swap(block, "chip", j))
+        total = total + wide(swap(blocks[j], "chip", j))
     total = total.astype(jnp.bfloat16)
     upper, lower = total[:rows], total[rows:]
     arrived = swap(jnp.where(first, lower, upper), "core", 1)

time: 91.9 us -> 84.8 us (0.923)
  matrix products: 19.8 us -> 10.7 us
  Pallas kernels: 0 us -> 6.39 us
  other arithmetic: 9.33 us -> 6.29 us
  local copies, waits for them, and re-layouts: 4.71 us -> 2.2 us
    dot_general x6, matrix products: 16 us -> 7.05 us  [own_sums(): jnp.dot(held_tokens, in_weight[s], preferred_element_type=jnp.float32)]
    pallas_call x0 -> x1, Pallas kernels: none -> 6.39 us  [loaded(): pl.pallas_call(load_kernel, in_specs=[pl.BlockSpec(memory_space=pl.ANY)]...]
    unnamed x23 -> x13, local copies, waits for them, and re-layouts: 4.25 us -> 1.69 us
    convert_element_type x1, other arithmetic: 1.03 us -> 0.05 us  [on_device(): total = total.astype(jnp.bfloat16)]
    ppermute x30 -> x26, waiting for transfers between devices: 29.1 us -> 29.8 us  [swap(): return row_major(lax.ppermute(row_major(value), axis, pairs))]
    ppermute x30 -> x26, starting transfers between devices: 27.5 us -> 28.2 us  [swap(): return row_major(lax.ppermute(row_major(value), axis, pairs))]
  transfers between devices with their start and end apart: 30 -> 26, of which waited for: 15 -> 17; matrix products, arithmetic and copies ran while one was open for 29% -> 18% of each run, Pallas kernels for 0% -> 8%
where the time goes in v5:
time: 84.8 us; the launch traced here: 84.5 us
  waiting for transfers between devices  29.8 us (35%)
  starting transfers between devices  28.2 us (33%)
  matrix products  10.7 us (13%)
  Pallas kernels  6.39 us (8%)
  other arithmetic  6.29 us (7%)
  local copies, waits for them, and re-layouts  2.2 us (3%)
  between operations  1.09 us (1%)
    ppermute x26, waiting for transfers between devices, swap(): return row_major(lax.ppermute(row_major(value), axis, pairs))  29.8 us
    ppermute x26, starting transfers between devices, swap(): return row_major(lax.ppermute(row_major(value), axis, pairs))  28.2 us
    dot_general x6, matrix products, own_sums(): jnp.dot(held_tokens, in_weight[s], preferred_element_type=jnp.float32)  7.05 us
    pallas_call x1, Pallas kernels, loaded(): pl.pallas_call(load_kernel, in_specs=[pl.BlockSpec(memory_space=pl.ANY)]...  6.39 us
    dot_general x3, matrix products, own_sums(): jnp.dot(jnp.concatenate(hidden, 1), out_weight.reshape(per_device * half_...  3.61 us
  transfers between devices with their start and end apart: 26, of which 17 were waited for; matrix products, arithmetic and copies ran while one was open for 18% of the time, Pallas kernels for 8%

profile of v5, /device:TPU:0, one launch (start us, length us, event | category | flops | bytes accessed | tf_op | source)
XLA Modules:
  0.0 84.5 jit_solution(2831466998204476541)
XLA Ops:
  0.6 0.8 copy.14
  1.4 0.8 copy.15
  2.2 0.9 %broadcast_select_fusion.16 = (bf16[12,2048]{1,0:T(8,128)(2,1)S(1)}, bf16[12,2048]{1,0:T(8,128)(2,1)S(1)}) fusion(pred[]{:T(512)S(6)} %eq.88, bf16[12,4096]{1,0:T(8,128)(2,1)} %param.6), kind=kLoop, calls=%fused_computation.113 | loop fusion | flops 49152 | bytes 196609 | tf_op jit(solution)/shard_map/jit(_where)/select_n | solution.py:136
  3.2 0.5 collective-permute-start
  3.7 0.7 select_reduce_fusion.8
  4.7 3.0 %collective-permute-start.1 = (bf16[24,2176]{1,0:T(8,128)(2,1)S(1)}, bf16[24,2176]{1,0:T(8,128)(2,1)S(1)}, u32[]{:S(2)}, u32[]{:S(2)}) collective-permute-start(bf16[24,2176]{1,0:T(8,128)(2,1)S(1)} %get-tuple-element.11), channel_id=1, source_target_pairs={{0,2},{2,0},{4,6},{6,4},{1,3},{3,1},{5,7},{7,5},{8,10},{10,8},{12,... | collective-permute-start | bytes 313352 | tf_op jit(solution)/shard_map/ppermute | solution.py:33
  7.7 2.5 %collective-permute-start.7 = (bf16[24,2176]{1,0:T(8,128)(2,1)S(1)}, bf16[24,2176]{1,0:T(8,128)(2,1)S(1)}, u32[]{:S(2)}, u32[]{:S(2)}) collective-permute-start(bf16[24,2176]{1,0:T(8,128)(2,1)S(1)} %get-tuple-element.11), channel_id=1, source_target_pairs={{0,6},{2,4},{4,2},{6,0},{1,7},{3,5},{5,3},{7,1},{8,14},{10,12},{12... | collective-permute-start | bytes 313352 | tf_op jit(solution)/shard_map/ppermute | solution.py:33
  10.3 0.6 collective-permute-done.1
  10.9 1.7 %collective-permute-start.2 = (bf16[24,2176]{1,0:T(8,128)(2,1)S(1)}, bf16[24,2176]{1,0:T(8,128)(2,1)S(1)}, u32[]{:S(2)}, u32[]{:S(2)}) collective-permute-start(bf16[24,2176]{1,0:T(8,128)(2,1)S(1)} %get-tuple-element.11), channel_id=1, source_target_pairs={{0,8},{8,0},{16,24},{24,16},{1,9},{9,1},{17,25},{25,17},{2,10},{10... | collective-permute-start | bytes 313352 | tf_op jit(solution)/shard_map/ppermute | solution.py:33
  12.6 1.5 %collective-permute-start.3 = (bf16[24,2176]{1,0:T(8,128)(2,1)S(1)}, bf16[24,2176]{1,0:T(8,128)(2,1)S(1)}, u32[]{:S(2)}, u32[]{:S(2)}) collective-permute-start(bf16[24,2176]{1,0:T(8,128)(2,1)S(1)} %get-tuple-element.11), channel_id=1, source_target_pairs={{0,16},{8,24},{16,0},{24,8},{1,17},{9,25},{17,1},{25,9},{2,18},{10... | collective-permute-start | bytes 313352 | tf_op jit(solution)/shard_map/ppermute | solution.py:33
  14.1 1.5 %collective-permute-done.2 = bf16[24,2176]{1,0:T(8,128)(2,1)S(1)} collective-permute-done((bf16[24,2176]{1,0:T(8,128)(2,1)S(1)}, bf16[24,2176]{1,0:T(8,128)(2,1)S(1)}, u32[]{:S(2)}, u32[]{:S(2)}) %collective-permute-start.2) | collective-permute-done | bytes 104480 | tf_op jit(solution)/shard_map/ppermute | solution.py:33
  15.6 1.7 %collective-permute-start.4 = (bf16[24,1024]{1,0:T(8,128)(2,1)S(1)}, bf16[24,1024]{1,0:T(8,128)(2,1)S(1)}, u32[]{:S(2)}, u32[]{:S(2)}) collective-permute-start(bf16[24,1024]{1,0:T(8,128)(2,1)S(1)} %slice.311), channel_id=1, source_target_pairs={{0,16},{8,24},{16,0},{24,8},{1,17},{9,25},{17,1},{25,9},{2,18},{10... | collective-permute-start | bytes 147464 | tf_op jit(solution)/shard_map/ppermute | solution.py:33
  17.5 1.3 %collective-permute-start.5 = (bf16[24,1152]{1,0:T(8,128)(2,1)S(1)}, bf16[24,1152]{1,0:T(8,128)(2,1)S(1)}, u32[]{:S(2)}, u32[]{:S(2)}) collective-permute-start(bf16[24,1152]{1,0:T(8,128)(2,1)S(1)} %slice.312), channel_id=1, source_target_pairs={{0,8},{8,0},{16,24},{24,16},{1,9},{9,1},{17,25},{25,17},{2,10},{10... | collective-permute-start | bytes 165896 | tf_op jit(solution)/shard_map/ppermute | solution.py:33
  18.9 6.4 %shard_map.77 = (bf16[2,4096,768]{2,1,0:T(8,128)(2,1)S(1)}, bf16[2,384,4096]{2,1,0:T(8,128)(2,1)S(1)}) custom-call(bf16[2,4096,768]{2,1,0:T(8,128)(2,1)} %up_ref, bf16[2,384,4096]{2,1,0:T(8,128)(2,1)} %down_ref), custom_call_target="tpu_custom_call" | custom-call | bytes 18874368 | tf_op jit(solution)/shard_map/pallas_call | solution.py:106
  25.6 0.6 collective-permute-start.11
  26.2 1.9 %collective-permute-start.10 = (bf16[72,2176]{1,0:T(8,128)(2,1)S(1)}, bf16[72,2176]{1,0:T(8,128)(2,1)S(1)}, u32[]{:S(2)}, u32[]{:S(2)}) collective-permute-start(bf16[72,2176]{1,0:T(8,128)(2,1)S(1)} %get-tuple-element.52), channel_id=1, source_target_pairs={{0,8},{8,0},{16,24},{24,16},{1,9},{9,1},{17,25},{25,17},{2,10},{10... | collective-permute-start | bytes 940040 | tf_op jit(solution)/shard_map/ppermute | solution.py:33
  28.5 1.3 %fusion.4 = f32[168,768]{1,0:T(8,128)S(1)} fusion(bf16[2,4096,768]{2,1,0:T(8,128)(2,1)S(1)} %get-tuple-element.14, bf16[168,2048]{1,0:T(8,128)(2,1)S(1)} %get-tuple-element.29, bf16[168,2048]{1,0:T(8,128)(2,1)S(1)} %get-tuple-element.28), kind=kOutput, calls=%fused_computation.4 | convolution fusion | flops 1059717120 | bytes 8183808 | tf_op jit(solution)/shard_map/dot_general | solution.py:169
  29.7 1.3 %fusion.10 = f32[168,768]{1,0:T(8,128)S(1)} fusion(bf16[2,4096,768]{2,1,0:T(8,128)(2,1)S(1)} %get-tuple-element.14, bf16[168,2048]{1,0:T(8,128)(2,1)S(1)} %get-tuple-element.29, bf16[168,2048]{1,0:T(8,128)(2,1)S(1)} %get-tuple-element.28), kind=kOutput, calls=%fused_computation.10 | convolution fusion | flops 1059717120 | bytes 8183808 | tf_op jit(solution)/shard_map/dot_general | solution.py:169
  31.2 1.3 %convolution_convert_fusion = bf16[168,4096]{1,0:T(8,128)(2,1)S(1)} fusion(bf16[768,4096]{1,0:T(8,128)(2,1)S(1)} %bitcast.18, bf16[168,384]{1,0:T(8,128)(2,1)S(1)} %get-tuple-element.60, bf16[168,384]{1,0:T(8,128)(2,1)S(1)} %get-tuple-element.61), kind=kOutput, calls=%fused_computation.12 | convolution fusion | flops 1058168832 | bytes 7925760 | tf_op jit(solution)/shard_map/dot_general | solution.py:172
  32.4 3.0 %collective-permute-done.11 = bf16[72,2176]{1,0:T(8,128)(2,1)S(1)} collective-permute-done((bf16[72,2176]{1,0:T(8,128)(2,1)S(1)}, bf16[72,2176]{1,0:T(8,128)(2,1)S(1)}, u32[]{:S(2)}, u32[]{:S(2)}) %collective-permute-start.11) | collective-permute-done | bytes 313376 | tf_op jit(solution)/shard_map/ppermute | solution.py:33
  35.4 0.4 collective-permute-done.10
  36.1 1.4 %collective-permute-start.14 = (bf16[72,1024]{1,0:T(8,128)(2,1)S(1)}, bf16[72,1024]{1,0:T(8,128)(2,1)S(1)}, u32[]{:S(2)}, u32[]{:S(2)}) collective-permute-start(bf16[72,1024]{1,0:T(8,128)(2,1)S(1)} %slice.269), channel_id=1, source_target_pairs={{0,16},{8,24},{16,0},{24,8},{1,17},{9,25},{17,1},{25,9},{2,18},{10... | collective-permute-start | bytes 442376 | tf_op jit(solution)/shard_map/ppermute | solution.py:33
  37.5 0.7 collective-permute-start.15
  38.7 1.1 %fusion.8 = f32[144,768]{1,0:T(8,128)S(1)} fusion(bf16[2,4096,768]{2,1,0:T(8,128)(2,1)S(1)} %get-tuple-element.14, bf16[144,2048]{1,0:T(8,128)(2,1)S(1)} %get-tuple-element.31, bf16[144,2048]{1,0:T(8,128)(2,1)S(1)} %get-tuple-element.30), kind=kOutput, calls=%fused_computation.8 | convolution fusion | flops 908328960 | bytes 7913472 | tf_op jit(solution)/shard_map/dot_general | solution.py:169
  39.8 1.1 %fusion.2 = f32[144,768]{1,0:T(8,128)S(1)} fusion(bf16[2,4096,768]{2,1,0:T(8,128)(2,1)S(1)} %get-tuple-element.14, bf16[144,2048]{1,0:T(8,128)(2,1)S(1)} %get-tuple-element.31, bf16[144,2048]{1,0:T(8,128)(2,1)S(1)} %get-tuple-element.30), kind=kOutput, calls=%fused_computation.2 | convolution fusion | flops 908328960 | bytes 7913472 | tf_op jit(solution)/shard_map/dot_general | solution.py:169
  41.1 1.1 %convolution_convert_fusion.1 = bf16[144,4096]{1,0:T(8,128)(2,1)S(1)} fusion(bf16[768,4096]{1,0:T(8,128)(2,1)S(1)} %bitcast.19, bf16[144,384]{1,0:T(8,128)(2,1)S(1)} %fusion.30, bf16[144,384]{1,0:T(8,128)(2,1)S(1)} %fusion.32), kind=kOutput, calls=%fused_computation.13 | convolution fusion | flops 907001856 | bytes 7692288 | tf_op jit(solution)/shard_map/dot_general | solution.py:172
  42.4 1.5 %collective-permute-done.15 = bf16[72,1152]{1,0:T(8,128)(2,1)S(1)} collective-permute-done((bf16[72,1152]{1,0:T(8,128)(2,1)S(1)}, bf16[72,1152]{1,0:T(8,128)(2,1)S(1)}, u32[]{:S(2)}, u32[]{:S(2)}) %collective-permute-start.15) | collective-permute-done | bytes 165920 | tf_op jit(solution)/shard_map/ppermute | solution.py:33
  44.0 0.5 collective-permute-start.13
  45.2 0.4 collective-permute-done.16
  45.6 1.2 %fusion.6 = f32[72,768]{1,0:T(8,128)S(1)} fusion(bf16[2,4096,768]{2,1,0:T(8,128)(2,1)S(1)} %get-tuple-element.14, bf16[72,2048]{1,0:T(8,128)(2,1)S(1)} %get-tuple-element.39, bf16[72,2048]{1,0:T(8,128)(2,1)S(1)} %get-tuple-element.38), kind=kOutput, calls=%fused_computation.6 | convolution fusion | flops 454164480 | bytes 7102464 | tf_op jit(solution)/shard_map/dot_general | solution.py:169
  46.8 1.2 %fusion = f32[72,768]{1,0:T(8,128)S(1)} fusion(bf16[2,4096,768]{2,1,0:T(8,128)(2,1)S(1)} %get-tuple-element.14, bf16[72,2048]{1,0:T(8,128)(2,1)S(1)} %get-tuple-element.39, bf16[72,2048]{1,0:T(8,128)(2,1)S(1)} %get-tuple-element.38), kind=kOutput, calls=%fused_computation | convolution fusion | flops 454164480 | bytes 7102464 | tf_op jit(solution)/shard_map/dot_general | solution.py:169
  48.1 1.2 %convolution_convert_fusion.2 = bf16[72,4096]{1,0:T(8,128)(2,1)S(1)} fusion(bf16[768,4096]{1,0:T(8,128)(2,1)S(1)} %bitcast.20, bf16[72,384]{1,0:T(8,128)(2,1)S(1)} %fusion.40, bf16[72,384]{1,0:T(8,128)(2,1)S(1)} %fusion.42), kind=kOutput, calls=%fused_computation.20 | convolution fusion | flops 453500928 | bytes 6991872 | tf_op jit(solution)/shard_map/dot_general | solution.py:172
  49.6 1.4 %collective-permute-done.17 = bf16[72,2048]{1,0:T(8,128)(2,1)S(1)} collective-permute-done((bf16[72,2048]{1,0:T(8,128)(2,1)S(1)}, bf16[72,2048]{1,0:T(8,128)(2,1)S(1)}, u32[]{:S(2)}, u32[]{:S(2)}) %collective-permute-start.17) | collective-permute-done | bytes 294944 | tf_op jit(solution)/shard_map/ppermute | solution.py:33
  51.2 0.7 collective-permute-start.18
  51.9 1.7 %collective-permute-start.20 = (bf16[96,1024]{1,0:T(8,128)(2,1)S(1)}, bf16[96,1024]{1,0:T(8,128)(2,1)S(1)}, u32[]{:S(2)}, u32[]{:S(2)}) collective-permute-start(bf16[96,1024]{1,0:T(8,128)(2,1)S(1)} %get-tuple-element.44), channel_id=1, source_target_pairs={{0,8},{8,0},{16,24},{24,16},{1,9},{9,1},{17,25},{25,17},{2,10},{10... | collective-permute-start | bytes 589832 | tf_op jit(solution)/shard_map/ppermute | solution.py:33
  54.0 4.2 %collective-permute-done.18 = bf16[96,1024]{1,0:T(8,128)(2,1)S(1)} collective-permute-done((bf16[96,1024]{1,0:T(8,128)(2,1)S(1)}, bf16[96,1024]{1,0:T(8,128)(2,1)S(1)}, u32[]{:S(2)}, u32[]{:S(2)}) %collective-permute-start.18) | collective-permute-done | bytes 196640 | tf_op jit(solution)/shard_map/ppermute | solution.py:33
  58.7 1.4 %collective-permute-start.21 = (bf16[96,2048]{1,0:T(8,128)(2,1)S(1)}, bf16[96,2048]{1,0:T(8,128)(2,1)S(1)}, u32[]{:S(2)}, u32[]{:S(2)}) collective-permute-start(bf16[96,2048]{1,0:T(8,128)(2,1)S(1)} %pad_maximum_fusion.7), channel_id=1, source_target_pairs={{0,16},{8,24},{16,0},{24,8},{1,17},{9,25},{17,1},{25,9},{2,18},{10... | collective-permute-start | bytes 1179656 | tf_op jit(solution)/shard_map/ppermute | solution.py:33
  60.1 0.8 collective-permute-start.19
  61.3 7.5 %collective-permute-done.21 = bf16[96,2048]{1,0:T(8,128)(2,1)S(1)} collective-permute-done((bf16[96,2048]{1,0:T(8,128)(2,1)S(1)}, bf16[96,2048]{1,0:T(8,128)(2,1)S(1)}, u32[]{:S(2)}, u32[]{:S(2)}) %collective-permute-start.21) | collective-permute-done | bytes 393248 | tf_op jit(solution)/shard_map/ppermute | solution.py:33
  68.8 1.0 %collective-permute-done.19 = bf16[96,2048]{1,0:T(8,128)(2,1)S(1)} collective-permute-done((bf16[96,2048]{1,0:T(8,128)(2,1)S(1)}, bf16[96,2048]{1,0:T(8,128)(2,1)S(1)}, u32[]{:S(2)}, u32[]{:S(2)}) %collective-permute-start.19) | collective-permute-done | bytes 393248 | tf_op jit(solution)/shard_map/ppermute | solution.py:33
  70.0 1.6 %collective-permute-start.22 = (bf16[24,2048]{1,0:T(8,128)(2,1)S(1)}, bf16[24,2048]{1,0:T(8,128)(2,1)S(1)}, u32[]{:S(2)}, u32[]{:S(2)}) collective-permute-start(bf16[24,2048]{1,0:T(8,128)(2,1)S(1)} %get-tuple-element.40), channel_id=1, source_target_pairs={{0,2},{2,0},{4,6},{6,4},{1,3},{3,1},{5,7},{7,5},{8,10},{10,8},{12,... | collective-permute-start | bytes 294920 | tf_op jit(solution)/shard_map/ppermute | solution.py:33
  71.7 3.4 %collective-permute-start.24 = (bf16[24,2048]{1,0:T(8,128)(2,1)S(1)}, bf16[24,2048]{1,0:T(8,128)(2,1)S(1)}, u32[]{:S(2)}, u32[]{:S(2)}) collective-permute-start(bf16[24,2048]{1,0:T(8,128)(2,1)S(1)} %get-tuple-element.41), channel_id=1, source_target_pairs={{0,6},{2,4},{4,2},{6,0},{1,7},{3,5},{5,3},{7,1},{8,14},{10,12},{12... | collective-permute-start | bytes 294920 | tf_op jit(solution)/shard_map/ppermute | solution.py:33
  75.1 0.5 collective-permute-start.23
  75.7 3.8 %collective-permute-done.24 = bf16[24,2048]{1,0:T(8,128)(2,1)S(1)} collective-permute-done((bf16[24,2048]{1,0:T(8,128)(2,1)S(1)}, bf16[24,2048]{1,0:T(8,128)(2,1)S(1)}, u32[]{:S(2)}, u32[]{:S(2)}) %collective-permute-start.24) | collective-permute-done | bytes 98336 | tf_op jit(solution)/shard_map/ppermute | solution.py:33
  79.5 3.0 %collective-permute-done.23 = bf16[24,2048]{1,0:T(8,128)(2,1)S(1)} collective-permute-done((bf16[24,2048]{1,0:T(8,128)(2,1)S(1)}, bf16[24,2048]{1,0:T(8,128)(2,1)S(1)}, u32[]{:S(2)}, u32[]{:S(2)}) %collective-permute-start.23) | collective-permute-done | bytes 98336 | tf_op jit(solution)/shard_map/ppermute | solution.py:33
  82.6 0.5 broadcast_multiply_fusion
  83.1 0.7 collective-permute-done.25
  83.9 0.7 pad_maximum_fusion.13
  (89 shorter events, 5.7 us)
Async XLA Ops:
  3.2 1.4 %collective-permute-start = (bf16[12,2176]{1,0:T(8,128)(2,1)S(1)}, bf16[12,2176]{1,0:T(8,128)(2,1)S(1)}, u32[]{:S(2)}, u32[]{:S(2)}) collective-permute-start(bf16[12,2176]{1,0:T(8,128)(2,1)S(1)} %pad_maximum_fusion.15), channel_id=1, source_target_pairs={{0,1},{1,0},{2,3},{3,2},{4,5},{5,4},{6,7},{7,6},{8,9},{9,8},{10,11... | collective-permute-start | bytes 156680 | tf_op jit(solution)/shard_map/ppermute | solution.py:33
  4.7 6.2 %collective-permute-start.1 = (bf16[24,2176]{1,0:T(8,128)(2,1)S(1)}, bf16[24,2176]{1,0:T(8,128)(2,1)S(1)}, u32[]{:S(2)}, u32[]{:S(2)}) collective-permute-start(bf16[24,2176]{1,0:T(8,128)(2,1)S(1)} %get-tuple-element.11), channel_id=1, source_target_pairs={{0,2},{2,0},{4,6},{6,4},{1,3},{3,1},{5,7},{7,5},{8,10},{10,8},{12,... | collective-permute-start | bytes 313352 | tf_op jit(solution)/shard_map/ppermute | solution.py:33
  7.7 17.7 %collective-permute-start.7 = (bf16[24,2176]{1,0:T(8,128)(2,1)S(1)}, bf16[24,2176]{1,0:T(8,128)(2,1)S(1)}, u32[]{:S(2)}, u32[]{:S(2)}) collective-permute-start(bf16[24,2176]{1,0:T(8,128)(2,1)S(1)} %get-tuple-element.11), channel_id=1, source_target_pairs={{0,6},{2,4},{4,2},{6,0},{1,7},{3,5},{5,3},{7,1},{8,14},{10,12},{12... | collective-permute-start | bytes 313352 | tf_op jit(solution)/shard_map/ppermute | solution.py:33
  10.1 15.2 %collective-permute-start.6 = (bf16[24,2176]{1,0:T(8,128)(2,1)S(1)}, bf16[24,2176]{1,0:T(8,128)(2,1)S(1)}, u32[]{:S(2)}, u32[]{:S(2)}) collective-permute-start(bf16[24,2176]{1,0:T(8,128)(2,1)S(1)} %get-tuple-element.11), channel_id=1, source_target_pairs={{0,4},{2,6},{4,0},{6,2},{1,5},{3,7},{5,1},{7,3},{8,12},{10,14},{12... | collective-permute-start | bytes 313352 | tf_op jit(solution)/shard_map/ppermute | solution.py:33
  10.9 4.7 %collective-permute-start.2 = (bf16[24,2176]{1,0:T(8,128)(2,1)S(1)}, bf16[24,2176]{1,0:T(8,128)(2,1)S(1)}, u32[]{:S(2)}, u32[]{:S(2)}) collective-permute-start(bf16[24,2176]{1,0:T(8,128)(2,1)S(1)} %get-tuple-element.11), channel_id=1, source_target_pairs={{0,8},{8,0},{16,24},{24,16},{1,9},{9,1},{17,25},{25,17},{2,10},{10... | collective-permute-start | bytes 313352 | tf_op jit(solution)/shard_map/ppermute | solution.py:33
  12.6 5.0 %collective-permute-start.3 = (bf16[24,2176]{1,0:T(8,128)(2,1)S(1)}, bf16[24,2176]{1,0:T(8,128)(2,1)S(1)}, u32[]{:S(2)}, u32[]{:S(2)}) collective-permute-start(bf16[24,2176]{1,0:T(8,128)(2,1)S(1)} %get-tuple-element.11), channel_id=1, source_target_pairs={{0,16},{8,24},{16,0},{24,8},{1,17},{9,25},{17,1},{25,9},{2,18},{10... | collective-permute-start | bytes 313352 | tf_op jit(solution)/shard_map/ppermute | solution.py:33
  15.6 9.7 %collective-permute-start.4 = (bf16[24,1024]{1,0:T(8,128)(2,1)S(1)}, bf16[24,1024]{1,0:T(8,128)(2,1)S(1)}, u32[]{:S(2)}, u32[]{:S(2)}) collective-permute-start(bf16[24,1024]{1,0:T(8,128)(2,1)S(1)} %slice.311), channel_id=1, source_target_pairs={{0,16},{8,24},{16,0},{24,8},{1,17},{9,25},{17,1},{25,9},{2,18},{10... | collective-permute-start | bytes 147464 | tf_op jit(solution)/shard_map/ppermute | solution.py:33
  17.5 7.8 %collective-permute-start.5 = (bf16[24,1152]{1,0:T(8,128)(2,1)S(1)}, bf16[24,1152]{1,0:T(8,128)(2,1)S(1)}, u32[]{:S(2)}, u32[]{:S(2)}) collective-permute-start(bf16[24,1152]{1,0:T(8,128)(2,1)S(1)} %slice.312), channel_id=1, source_target_pairs={{0,8},{8,0},{16,24},{24,16},{1,9},{9,1},{17,25},{25,17},{2,10},{10... | collective-permute-start | bytes 165896 | tf_op jit(solution)/shard_map/ppermute | solution.py:33
  25.5 2.8 %collective-permute-start.8 = (bf16[168,2048]{1,0:T(8,128)(2,1)S(1)}, bf16[168,2048]{1,0:T(8,128)(2,1)S(1)}, u32[]{:S(2)}, u32[]{:S(2)}) collective-permute-start(bf16[168,2048]{1,0:T(8,128)(2,1)S(1)} %slice.313), channel_id=1, source_target_pairs={{0,1},{1,0},{2,3},{3,2},{4,5},{5,4},{6,7},{7,6},{8,9},{9,8},{10,11... | collective-permute-start | bytes 2064392 | tf_op jit(solution)/shard_map/ppermute | solution.py:33
  25.6 9.8 %collective-permute-start.11 = (bf16[72,2176]{1,0:T(8,128)(2,1)S(1)}, bf16[72,2176]{1,0:T(8,128)(2,1)S(1)}, u32[]{:S(2)}, u32[]{:S(2)}) collective-permute-start(bf16[72,2176]{1,0:T(8,128)(2,1)S(1)} %get-tuple-element.52), channel_id=1, source_target_pairs={{0,16},{8,24},{16,0},{24,8},{1,17},{9,25},{17,1},{25,9},{2,18},{10... | collective-permute-start | bytes 940040 | tf_op jit(solution)/shard_map/ppermute | solution.py:33
  26.2 9.6 %collective-permute-start.10 = (bf16[72,2176]{1,0:T(8,128)(2,1)S(1)}, bf16[72,2176]{1,0:T(8,128)(2,1)S(1)}, u32[]{:S(2)}, u32[]{:S(2)}) collective-permute-start(bf16[72,2176]{1,0:T(8,128)(2,1)S(1)} %get-tuple-element.52), channel_id=1, source_target_pairs={{0,8},{8,0},{16,24},{24,16},{1,9},{9,1},{17,25},{25,17},{2,10},{10... | collective-permute-start | bytes 940040 | tf_op jit(solution)/shard_map/ppermute | solution.py:33
  35.9 2.6 %collective-permute-start.12 = (bf16[144,2048]{1,0:T(8,128)(2,1)S(1)}, bf16[144,2048]{1,0:T(8,128)(2,1)S(1)}, u32[]{:S(2)}, u32[]{:S(2)}) collective-permute-start(bf16[144,2048]{1,0:T(8,128)(2,1)S(1)} %slice.327), channel_id=1, source_target_pairs={{0,1},{1,0},{2,3},{3,2},{4,5},{5,4},{6,7},{7,6},{8,9},{9,8},{10,11... | collective-permute-start | bytes 1769480 | tf_op jit(solution)/shard_map/ppermute | solution.py:33
  36.1 6.3 %collective-permute-start.14 = (bf16[72,1024]{1,0:T(8,128)(2,1)S(1)}, bf16[72,1024]{1,0:T(8,128)(2,1)S(1)}, u32[]{:S(2)}, u32[]{:S(2)}) collective-permute-start(bf16[72,1024]{1,0:T(8,128)(2,1)S(1)} %slice.269), channel_id=1, source_target_pairs={{0,16},{8,24},{16,0},{24,8},{1,17},{9,25},{17,1},{25,9},{2,18},{10... | collective-permute-start | bytes 442376 | tf_op jit(solution)/shard_map/ppermute | solution.py:33
  37.5 6.4 %collective-permute-start.15 = (bf16[72,1152]{1,0:T(8,128)(2,1)S(1)}, bf16[72,1152]{1,0:T(8,128)(2,1)S(1)}, u32[]{:S(2)}, u32[]{:S(2)}) collective-permute-start(bf16[72,1152]{1,0:T(8,128)(2,1)S(1)} %slice.270), channel_id=1, source_target_pairs={{0,8},{8,0},{16,24},{24,16},{1,9},{9,1},{17,25},{25,17},{2,10},{10... | collective-permute-start | bytes 497672 | tf_op jit(solution)/shard_map/ppermute | solution.py:33
  38.3 6.6 %collective-permute-start.9 = (bf16[168,2048]{1,0:T(8,128)(2,1)S(1)}, bf16[168,2048]{1,0:T(8,128)(2,1)S(1)}, u32[]{:S(2)}, u32[]{:S(2)}) collective-permute-start(bf16[168,2048]{1,0:T(8,128)(2,1)S(1)} %broadcast_select_fusion), channel_id=1, source_target_pairs={{0,1},{1,0},{2,3},{3,2},{4,5},{5,4},{6,7},{7,6},{8,9},{9,8},{10,11... | collective-permute-start | bytes 2064392 | tf_op jit(solution)/shard_map/ppermute | solution.py:33
  43.9 1.6 %collective-permute-start.16 = (bf16[72,2048]{1,0:T(8,128)(2,1)S(1)}, bf16[72,2048]{1,0:T(8,128)(2,1)S(1)}, u32[]{:S(2)}, u32[]{:S(2)}) collective-permute-start(bf16[72,2048]{1,0:T(8,128)(2,1)S(1)} %pad_maximum_fusion.10), channel_id=1, source_target_pairs={{0,1},{1,0},{2,3},{3,2},{4,5},{5,4},{6,7},{7,6},{8,9},{9,8},{10,11... | collective-permute-start | bytes 884744 | tf_op jit(solution)/shard_map/ppermute | solution.py:33
  44.0 9.7 %collective-permute-start.13 = (bf16[144,2048]{1,0:T(8,128)(2,1)S(1)}, bf16[144,2048]{1,0:T(8,128)(2,1)S(1)}, u32[]{:S(2)}, u32[]{:S(2)}) collective-permute-start(bf16[144,2048]{1,0:T(8,128)(2,1)S(1)} %broadcast_select_fusion.3), channel_id=1, source_target_pairs={{0,1},{1,0},{2,3},{3,2},{4,5},{5,4},{6,7},{7,6},{8,9},{9,8},{10,11... | collective-permute-start | bytes 1769480 | tf_op jit(solution)/shard_map/ppermute | solution.py:33
  49.4 1.6 %collective-permute-start.17 = (bf16[72,2048]{1,0:T(8,128)(2,1)S(1)}, bf16[72,2048]{1,0:T(8,128)(2,1)S(1)}, u32[]{:S(2)}, u32[]{:S(2)}) collective-permute-start(bf16[72,2048]{1,0:T(8,128)(2,1)S(1)} %broadcast_select_fusion.6), channel_id=1, source_target_pairs={{0,1},{1,0},{2,3},{3,2},{4,5},{5,4},{6,7},{7,6},{8,9},{9,8},{10,11... | collective-permute-start | bytes 884744 | tf_op jit(solution)/shard_map/ppermute | solution.py:33
  51.2 7.0 %collective-permute-start.18 = (bf16[96,1024]{1,0:T(8,128)(2,1)S(1)}, bf16[96,1024]{1,0:T(8,128)(2,1)S(1)}, u32[]{:S(2)}, u32[]{:S(2)}) collective-permute-start(bf16[96,1024]{1,0:T(8,128)(2,1)S(1)} %get-tuple-element.43), channel_id=1, source_target_pairs={{0,16},{8,24},{16,0},{24,8},{1,17},{9,25},{17,1},{25,9},{2,18},{10... | collective-permute-start | bytes 589832 | tf_op jit(solution)/shard_map/ppermute | solution.py:33
  51.9 6.7 %collective-permute-start.20 = (bf16[96,1024]{1,0:T(8,128)(2,1)S(1)}, bf16[96,1024]{1,0:T(8,128)(2,1)S(1)}, u32[]{:S(2)}, u32[]{:S(2)}) collective-permute-start(bf16[96,1024]{1,0:T(8,128)(2,1)S(1)} %get-tuple-element.44), channel_id=1, source_target_pairs={{0,8},{8,0},{16,24},{24,16},{1,9},{9,1},{17,25},{25,17},{2,10},{10... | collective-permute-start | bytes 589832 | tf_op jit(solution)/shard_map/ppermute | solution.py:33
  58.7 10.1 %collective-permute-start.21 = (bf16[96,2048]{1,0:T(8,128)(2,1)S(1)}, bf16[96,2048]{1,0:T(8,128)(2,1)S(1)}, u32[]{:S(2)}, u32[]{:S(2)}) collective-permute-start(bf16[96,2048]{1,0:T(8,128)(2,1)S(1)} %pad_maximum_fusion.7), channel_id=1, source_target_pairs={{0,16},{8,24},{16,0},{24,8},{1,17},{9,25},{17,1},{25,9},{2,18},{10... | collective-permute-start | bytes 1179656 | tf_op jit(solution)/shard_map/ppermute | solution.py:33
  60.1 9.7 %collective-permute-start.19 = (bf16[96,2048]{1,0:T(8,128)(2,1)S(1)}, bf16[96,2048]{1,0:T(8,128)(2,1)S(1)}, u32[]{:S(2)}, u32[]{:S(2)}) collective-permute-start(bf16[96,2048]{1,0:T(8,128)(2,1)S(1)} %fusion.21), channel_id=1, source_target_pairs={{0,8},{8,0},{16,24},{24,16},{1,9},{9,1},{17,25},{25,17},{2,10},{10... | collective-permute-start | bytes 1179656 | tf_op jit(solution)/shard_map/ppermute | solution.py:33
  70.0 5.7 %collective-permute-start.22 = (bf16[24,2048]{1,0:T(8,128)(2,1)S(1)}, bf16[24,2048]{1,0:T(8,128)(2,1)S(1)}, u32[]{:S(2)}, u32[]{:S(2)}) collective-permute-start(bf16[24,2048]{1,0:T(8,128)(2,1)S(1)} %get-tuple-element.40), channel_id=1, source_target_pairs={{0,2},{2,0},{4,6},{6,4},{1,3},{3,1},{5,7},{7,5},{8,10},{10,8},{12,... | collective-permute-start | bytes 294920 | tf_op jit(solution)/shard_map/ppermute | solution.py:33
  71.7 7.8 %collective-permute-start.24 = (bf16[24,2048]{1,0:T(8,128)(2,1)S(1)}, bf16[24,2048]{1,0:T(8,128)(2,1)S(1)}, u32[]{:S(2)}, u32[]{:S(2)}) collective-permute-start(bf16[24,2048]{1,0:T(8,128)(2,1)S(1)} %get-tuple-element.41), channel_id=1, source_target_pairs={{0,6},{2,4},{4,2},{6,0},{1,7},{3,5},{5,3},{7,1},{8,14},{10,12},{12... | collective-permute-start | bytes 294920 | tf_op jit(solution)/shard_map/ppermute | solution.py:33
  75.1 7.3 %collective-permute-start.23 = (bf16[24,2048]{1,0:T(8,128)(2,1)S(1)}, bf16[24,2048]{1,0:T(8,128)(2,1)S(1)}, u32[]{:S(2)}, u32[]{:S(2)}) collective-permute-start(bf16[24,2048]{1,0:T(8,128)(2,1)S(1)} %get-tuple-element.42), channel_id=1, source_target_pairs={{0,4},{2,6},{4,0},{6,2},{1,5},{3,7},{5,1},{7,3},{8,12},{10,14},{12... | collective-permute-start | bytes 294920 | tf_op jit(solution)/shard_map/ppermute | solution.py:33
  82.5 1.3 %collective-permute-start.25 = (bf16[12,2048]{1,0:T(8,128)(2,1)S(1)}, bf16[12,2048]{1,0:T(8,128)(2,1)S(1)}, u32[]{:S(2)}, u32[]{:S(2)}) collective-permute-start(bf16[12,2048]{1,0:T(8,128)(2,1)S(1)} %broadcast_select_fusion.13), channel_id=1, source_target_pairs={{0,1},{1,0},{2,3},{3,2},{4,5},{5,4},{6,7},{7,6},{8,9},{9,8},{10,11... | collective-permute-start | bytes 147464 | tf_op jit(solution)/shard_map/ppermute | solution.py:33

commit v6 on v5

--- a/solution.py
+++ b/solution.py
@@ -90,33 +90,31 @@
     return total.astype(jnp.bfloat16)
 
 
-def load_kernel(up_ref, down_ref, up_out, down_out, sems):
-    copies = [
-        pltpu.make_async_copy(up_ref, up_out, sems.at[0]),
-        pltpu.make_async_copy(down_ref, down_out, sems.at[1]),
-    ]
-    for copy in copies:
-        copy.start()
-    for copy in copies:
-        copy.wait()
-
-
-def loaded(up, down):
-    nbytes = up.nbytes + down.nbytes
+def load_kernel(hbm_ref, vmem_ref, sem):
+    copy = pltpu.make_async_copy(hbm_ref, vmem_ref, sem)
+    copy.start()
+    copy.wait()
+
+
+def loaded(weight):
+    weight = pltpu.with_memory_space_constraint(weight, pltpu.HBM)
     return pl.pallas_call(
         load_kernel,
-        in_specs=[pl.BlockSpec(memory_space=pl.ANY)] * 2,
-        out_specs=[pl.BlockSpec(memory_space=pltpu.VMEM)] * 2,
-        out_shape=[pltpu.VMEM(up.shape, up.dtype), pltpu.VMEM(down.shape, down.dtype)],
-        scratch_shapes=[pltpu.SemaphoreType.DMA((2,))],
-        compiler_params=pltpu.CompilerParams(vmem_limit_bytes=32 * 2**20),
-        cost_estimate=pl.CostEstimate(flops=0, bytes_accessed=nbytes, transcendentals=0),
-    )(up, down)
+        in_specs=[pl.BlockSpec(memory_space=pl.ANY)],
+        out_specs=pl.BlockSpec(memory_space=pltpu.VMEM),
+        out_shape=pltpu.VMEM(weight.shape, weight.dtype),
+        scratch_shapes=[pltpu.SemaphoreType.DMA],
+        compiler_params=pltpu.CompilerParams(vmem_limit_bytes=2 * 2**20),
+        cost_estimate=pl.CostEstimate(
+            flops=0, bytes_accessed=2 * weight.nbytes, transcendentals=0
+        ),
+    )(weight)
 
 
 def on_device(tokens, expert_ids, gate_probs, in_weight, out_weight, swap_slot):
     groups, chips = lax.axis_size("dp"), lax.axis_size("chip")
     owners = 2 * chips
+    near_chips = chips // 2
     per_device = in_weight.shape[0]
     rows, width = tokens.shape
     part = width // 2
@@ -189,9 +187,9 @@
     others = [swap(chip_rows, "chip", j) for j in range(1, chips)]
     near = [chip_rows, *spread_near(behind(chip_rows, others[0]))]
     near += joined(spread_rest(near[1:]))
-    in_weight, out_weight = loaded(*behind((in_weight, out_weight), near[1:3]))
     far = [row_major(jnp.concatenate(others, 0))]
     far += spread_near(far[0])
+    in_weight = loaded(behind(in_weight, far[0]))
     first_blocks = [*near, far[0]]
     first_part = own_sums(first_blocks)
     far[1:] = behind(far[1:], first_part)
@@ -206,8 +204,12 @@
         sums += chip_sums(part_two, far[1:])
     far += rest
     sums = [jnp.concatenate([sums[k], sums[groups + k]], 0) for k in range(groups)]
-    total = collected(with_fourth(sums))
-    blocks = [total[j * 2 * rows : (j + 1) * 2 * rows] for j in range(chips)]
+    sums = with_fourth(sums)
+    border = 2 * near_chips * rows
+    total = collected([block[border:] for block in sums])
+    blocks = [total[low : low + 2 * rows] for low in range(0, total.shape[0], 2 * rows)]
+    total = collected(behind([block[:border] for block in sums], total))
+    blocks = [total[low : low + 2 * rows] for low in range(0, border, 2 * rows)] + blocks
     total = wide(blocks[0])
     for j in range(1, chips):
         total = total + wide(swap(blocks[j], "chip", j))

time: 84.8 us -> 93.4 us (1.10)
  waiting for transfers between devices: 29.8 us -> 22.1 us
  matrix products: 10.7 us -> 16.8 us
  local copies, waits for them, and re-layouts: 2.2 us -> 6.89 us
  other arithmetic: 6.29 us -> 10.2 us
  starting transfers between devices: 28.2 us -> 31.1 us
  Pallas kernels: 6.39 us -> 4.58 us
    ppermute x26 -> x28, waiting for transfers between devices: 29.8 us -> 22.1 us  [swap(): return row_major(lax.ppermute(row_major(value), axis, pairs))]
    dot_general x6, matrix products: 7.05 us -> 13 us  [own_sums(): jnp.dot(held_tokens, in_weight[s], preferred_element_type=jnp.float32)]
    unnamed x13 -> x31, local copies, waits for them, and re-layouts: 1.69 us -> 6.36 us
    ppermute x26 -> x28, starting transfers between devices: 28.2 us -> 31.1 us  [swap(): return row_major(lax.ppermute(row_major(value), axis, pairs))]
    pallas_call x1, Pallas kernels: 6.39 us -> 4.58 us  [loaded(): pl.pallas_call(load_kernel, in_specs=[pl.BlockSpec(memory_space=pl.ANY)],...]
    convert_element_type x3, other arithmetic: 0.72 us -> 1.82 us  [chip_sums(): (wide(jnp.where(first, left, right)) + wide(arrived)).astype(jnp.bfloat16)]
    concatenate x1, other arithmetic: 0.02 us -> 1.03 us  [joined(): return [jnp.concatenate(halves, 1)] if halves else []]
    reduce_sum x3, other arithmetic: 0.67 us -> 1.61 us  [own_sums(): jnp.sum(jnp.where(ids == home * per_device + s, gates, jnp.float32(0.0)),...]
  transfers between devices with their start and end apart: 26 -> 28, of which waited for: 17 -> 15; matrix products, arithmetic and copies ran while one was open for 18% -> 28% of each run, Pallas kernels for 8% -> 5%
where the time goes in v6:
time: 93.4 us; the launch traced here: 93 us
  starting transfers between devices  31.1 us (33%)
  waiting for transfers between devices  22.1 us (24%)
  matrix products  16.8 us (18%)
  other arithmetic  10.2 us (11%)
  local copies, waits for them, and re-layouts  6.89 us (7%)
  Pallas kernels  4.58 us (5%)
  between operations  1.19 us (1%)
    ppermute x28, starting transfers between devices, swap(): return row_major(lax.ppermute(row_major(value), axis, pairs))  31.1 us
    ppermute x28, waiting for transfers between devices, swap(): return row_major(lax.ppermute(row_major(value), axis, pairs))  22.1 us
    dot_general x6, matrix products, own_sums(): jnp.dot(held_tokens, in_weight[s], preferred_element_type=jnp.float32)  13 us
    unnamed x31, local copies, waits for them, and re-layouts  6.36 us
    pallas_call x1, Pallas kernels, loaded(): pl.pallas_call(load_kernel, in_specs=[pl.BlockSpec(memory_space=pl.ANY)],...  4.58 us
    dot_general x3, matrix products, own_sums(): jnp.dot(jnp.concatenate(hidden, 1), out_weight.reshape(per_device * half_...  3.86 us
  transfers between devices with their start and end apart: 28, of which 15 were waited for; matrix products, arithmetic and copies ran while one was open for 28% of the time, Pallas kernels for 5%

profile of v6, /device:TPU:0, one launch (start us, length us, event | category | flops | bytes accessed | tf_op | source)
XLA Modules:
  0.0 93.0 jit_solution(15902374364363372984)
XLA Ops:
  0.6 0.8 copy.14
  1.4 0.8 copy.15
  2.2 0.9 broadcast_select_fusion.16
  3.7 0.7 select_reduce_fusion.8
  4.7 3.0 %collective-permute-start.1 = (bf16[24,2176]{1,0:T(8,128)(2,1)S(1)}, bf16[24,2176]{1,0:T(8,128)(2,1)S(1)}, u32[]{:S(2)}, u32[]{:S(2)}) collective-permute-start(bf16[24,2176]{1,0:T(8,128)(2,1)S(1)} %get-tuple-element.11), channel_id=1, source_target_pairs={{0,2},{2,0},{4,6},{6,4},{1,3},{3,1},{5,7},{7,5},{8,10},{10,8},{12,... | collective-permute-start | bytes 313352 | tf_op jit(solution)/shard_map/ppermute | solution.py:33
  7.7 2.5 %collective-permute-start.7 = (bf16[24,2176]{1,0:T(8,128)(2,1)S(1)}, bf16[24,2176]{1,0:T(8,128)(2,1)S(1)}, u32[]{:S(2)}, u32[]{:S(2)}) collective-permute-start(bf16[24,2176]{1,0:T(8,128)(2,1)S(1)} %get-tuple-element.11), channel_id=1, source_target_pairs={{0,6},{2,4},{4,2},{6,0},{1,7},{3,5},{5,3},{7,1},{8,14},{10,12},{12... | collective-permute-start | bytes 313352 | tf_op jit(solution)/shard_map/ppermute | solution.py:33
  10.9 1.7 %collective-permute-start.2 = (bf16[24,2176]{1,0:T(8,128)(2,1)S(1)}, bf16[24,2176]{1,0:T(8,128)(2,1)S(1)}, u32[]{:S(2)}, u32[]{:S(2)}) collective-permute-start(bf16[24,2176]{1,0:T(8,128)(2,1)S(1)} %get-tuple-element.11), channel_id=1, source_target_pairs={{0,8},{8,0},{16,24},{24,16},{1,9},{9,1},{17,25},{25,17},{2,10},{10... | collective-permute-start | bytes 313352 | tf_op jit(solution)/shard_map/ppermute | solution.py:33
  12.6 1.5 %collective-permute-start.3 = (bf16[24,2176]{1,0:T(8,128)(2,1)S(1)}, bf16[24,2176]{1,0:T(8,128)(2,1)S(1)}, u32[]{:S(2)}, u32[]{:S(2)}) collective-permute-start(bf16[24,2176]{1,0:T(8,128)(2,1)S(1)} %get-tuple-element.11), channel_id=1, source_target_pairs={{0,16},{8,24},{16,0},{24,8},{1,17},{9,25},{17,1},{25,9},{2,18},{10... | collective-permute-start | bytes 313352 | tf_op jit(solution)/shard_map/ppermute | solution.py:33
  14.1 1.5 %collective-permute-done.2 = bf16[24,2176]{1,0:T(8,128)(2,1)S(1)} collective-permute-done((bf16[24,2176]{1,0:T(8,128)(2,1)S(1)}, bf16[24,2176]{1,0:T(8,128)(2,1)S(1)}, u32[]{:S(2)}, u32[]{:S(2)}) %collective-permute-start.2) | collective-permute-done | bytes 104480 | tf_op jit(solution)/shard_map/ppermute | solution.py:33
  15.6 1.7 %collective-permute-start.4 = (bf16[24,1024]{1,0:T(8,128)(2,1)S(1)}, bf16[24,1024]{1,0:T(8,128)(2,1)S(1)}, u32[]{:S(2)}, u32[]{:S(2)}) collective-permute-start(bf16[24,1024]{1,0:T(8,128)(2,1)S(1)} %slice.336), channel_id=1, source_target_pairs={{0,16},{8,24},{16,0},{24,8},{1,17},{9,25},{17,1},{25,9},{2,18},{10... | collective-permute-start | bytes 147464 | tf_op jit(solution)/shard_map/ppermute | solution.py:33
  17.5 1.3 %collective-permute-start.5 = (bf16[24,1152]{1,0:T(8,128)(2,1)S(1)}, bf16[24,1152]{1,0:T(8,128)(2,1)S(1)}, u32[]{:S(2)}, u32[]{:S(2)}) collective-permute-start(bf16[24,1152]{1,0:T(8,128)(2,1)S(1)} %slice.337), channel_id=1, source_target_pairs={{0,8},{8,0},{16,24},{24,16},{1,9},{9,1},{17,25},{25,17},{2,10},{10... | collective-permute-start | bytes 165896 | tf_op jit(solution)/shard_map/ppermute | solution.py:33
  18.9 0.8 collective-permute-done.4
  19.7 2.0 %collective-permute-done.5 = bf16[24,1152]{1,0:T(8,128)(2,1)S(1)} collective-permute-done((bf16[24,1152]{1,0:T(8,128)(2,1)S(1)}, bf16[24,1152]{1,0:T(8,128)(2,1)S(1)}, u32[]{:S(2)}, u32[]{:S(2)}) %collective-permute-start.5) | collective-permute-done | bytes 55328 | tf_op jit(solution)/shard_map/ppermute | solution.py:33
  22.0 1.8 %collective-permute-start.11 = (bf16[72,2176]{1,0:T(8,128)(2,1)S(1)}, bf16[72,2176]{1,0:T(8,128)(2,1)S(1)}, u32[]{:S(2)}, u32[]{:S(2)}) collective-permute-start(bf16[72,2176]{1,0:T(8,128)(2,1)S(1)} %get-tuple-element.55), channel_id=1, source_target_pairs={{0,16},{8,24},{16,0},{24,8},{1,17},{9,25},{17,1},{25,9},{2,18},{10... | collective-permute-start | bytes 940040 | tf_op jit(solution)/shard_map/ppermute | solution.py:33
  23.9 4.6 %shard_map.77 = bf16[2,4096,768]{2,1,0:T(8,128)(2,1)S(1)} custom-call(bf16[2,4096,768]{2,1,0:T(8,128)(2,1)} %hbm_ref), custom_call_target="tpu_custom_call" | custom-call | bytes 25165824 | tf_op jit(solution)/shard_map/pallas_call | solution.py:101
  28.9 1.3 %fusion.5 = f32[168,768]{1,0:T(8,128)S(1)} fusion(bf16[2,4096,768]{2,1,0:T(8,128)(2,1)S(1)} %shard_map.77, bf16[168,2048]{1,0:T(8,128)(2,1)S(1)} %get-tuple-element.29, bf16[168,2048]{1,0:T(8,128)(2,1)S(1)} %get-tuple-element.28), kind=kOutput, calls=%fused_computation.9 | convolution fusion | flops 1059717120 | bytes 8183808 | tf_op jit(solution)/shard_map/dot_general | solution.py:167
  30.2 1.3 %fusion.2 = f32[168,768]{1,0:T(8,128)S(1)} fusion(bf16[2,4096,768]{2,1,0:T(8,128)(2,1)S(1)} %shard_map.77, bf16[168,2048]{1,0:T(8,128)(2,1)S(1)} %get-tuple-element.29, bf16[168,2048]{1,0:T(8,128)(2,1)S(1)} %get-tuple-element.28), kind=kOutput, calls=%fused_computation.6 | convolution fusion | flops 1059717120 | bytes 8183808 | tf_op jit(solution)/shard_map/dot_general | solution.py:167
  31.7 2.6 %slice-done = s8[4194304]{0:T(1024)(128)(4,1)S(1)} async-done(((s8[6291456]{0:T(1024)(128)(4,1)}), s8[4194304]{0:T(1024)(128)(4,1)S(1)}, s32[]{:S(2)}) %slice-start) | async-done | bytes 4194328
  34.2 1.6 %slice-done.1 = s8[2097152]{0:T(1024)(128)(4,1)S(1)} async-done(((s8[6291456]{0:T(1024)(128)(4,1)}), s8[2097152]{0:T(1024)(128)(4,1)S(1)}, s32[]{:S(2)}) %slice-start.1) | async-done | bytes 2097176
  35.8 1.2 %convolution_convert_fusion = bf16[168,4096]{1,0:T(8,128)(2,1)S(1)} fusion(bf16[768,4096]{1,0:T(8,128)(2,1)S(1)} %bitcast.16, bf16[168,384]{1,0:T(8,128)(2,1)S(1)} %get-tuple-element.63, bf16[168,384]{1,0:T(8,128)(2,1)S(1)} %get-tuple-element.64), kind=kOutput, calls=%fused_computation.2 | convolution fusion | flops 1058168832 | bytes 7925760 | tf_op jit(solution)/shard_map/dot_general | solution.py:170
  37.4 1.0 %broadcast_select_fusion = bf16[168,2048]{1,0:T(8,128)(2,1)} fusion(pred[]{:T(512)S(6)} %eq.88, bf16[168,4096]{1,0:T(8,128)(2,1)S(1)} %convolution_convert_fusion), kind=kLoop, calls=%fused_computation.18 | loop fusion | flops 344064 | bytes 2064385 | tf_op jit(solution)/shard_map/jit(_where)/select_n | solution.py:179
  38.4 1.6 %collective-permute-start.14 = (bf16[72,1024]{1,0:T(8,128)(2,1)S(1)}, bf16[72,1024]{1,0:T(8,128)(2,1)S(1)}, u32[]{:S(2)}, u32[]{:S(2)}) collective-permute-start(bf16[72,1024]{1,0:T(8,128)(2,1)S(1)} %slice.289), channel_id=1, source_target_pairs={{0,16},{8,24},{16,0},{24,8},{1,17},{9,25},{17,1},{25,9},{2,18},{10... | collective-permute-start | bytes 442376 | tf_op jit(solution)/shard_map/ppermute | solution.py:33
  39.9 0.7 collective-permute-start.15
  41.0 1.1 %fusion.1 = f32[144,768]{1,0:T(8,128)S(1)} fusion(bf16[2,4096,768]{2,1,0:T(8,128)(2,1)S(1)} %shard_map.77, bf16[144,2048]{1,0:T(8,128)(2,1)S(1)} %get-tuple-element.31, bf16[144,2048]{1,0:T(8,128)(2,1)S(1)} %get-tuple-element.30), kind=kOutput, calls=%fused_computation.5 | convolution fusion | flops 908328960 | bytes 7913472 | tf_op jit(solution)/shard_map/dot_general | solution.py:167
  42.1 1.1 %fusion.4 = f32[144,768]{1,0:T(8,128)S(1)} fusion(bf16[2,4096,768]{2,1,0:T(8,128)(2,1)S(1)} %shard_map.77, bf16[144,2048]{1,0:T(8,128)(2,1)S(1)} %get-tuple-element.31, bf16[144,2048]{1,0:T(8,128)(2,1)S(1)} %get-tuple-element.30), kind=kOutput, calls=%fused_computation.8 | convolution fusion | flops 908328960 | bytes 7913472 | tf_op jit(solution)/shard_map/dot_general | solution.py:167
  43.4 1.2 %convolution_convert_fusion.1 = bf16[144,4096]{1,0:T(8,128)(2,1)S(1)} fusion(bf16[768,4096]{1,0:T(8,128)(2,1)S(1)} %bitcast.17, bf16[144,384]{1,0:T(8,128)(2,1)S(1)} %fusion.18, bf16[144,384]{1,0:T(8,128)(2,1)S(1)} %fusion.20), kind=kOutput, calls=%fused_computation.3 | convolution fusion | flops 907001856 | bytes 7692288 | tf_op jit(solution)/shard_map/dot_general | solution.py:170
  44.6 1.6 %collective-permute-done.15 = bf16[72,1152]{1,0:T(8,128)(2,1)S(1)} collective-permute-done((bf16[72,1152]{1,0:T(8,128)(2,1)S(1)}, bf16[72,1152]{1,0:T(8,128)(2,1)S(1)}, u32[]{:S(2)}, u32[]{:S(2)}) %collective-permute-start.15) | collective-permute-done | bytes 165920 | tf_op jit(solution)/shard_map/ppermute | solution.py:33
  47.2 1.0 %pad_maximum_fusion.9 = bf16[72,2048]{1,0:T(8,128)(2,1)S(1)} fusion(bf16[72,1152]{1,0:T(8,128)(2,1)} %copy-done.3, bf16[72,1024]{1,0:T(8,128)(2,1)} %copy-done.4), kind=kLoop, calls=%fused_computation.40 | loop fusion | flops 589824 | bytes 608256 | tf_op jit(solution)/shard_map/concatenate | solution.py:59
  48.8 1.1 %select_reduce_fusion.6 = (f32[72]{0:T(128)S(1)}, f32[72]{0:T(128)S(1)}) fusion(s32[]{:T(128)S(6)} %mul.117, bf16[72,1152]{1,0:T(8,128)(2,1)} %copy-done.3, s32[]{:T(128)S(6)} %add.130), kind=kLoop, calls=%fused_computation.131 | loop fusion | flops 6768 | bytes 5192 | tf_op jit(solution)/shard_map/reduce_sum | solution.py:164
  50.1 1.4 %add_convert_fusion = bf16[168,2048]{1,0:T(8,128)(2,1)S(1)} fusion(bf16[168,2048]{1,0:T(8,128)(2,1)} %collective-permute-done.9, pred[]{:T(512)S(6)} %eq.88, bf16[168,4096]{1,0:T(8,128)(2,1)S(1)} %convolution_convert_fusion), kind=kLoop, calls=%fused_computation.12 | loop fusion | flops 1720320 | bytes 2752513 | tf_op jit(solution)/shard_map/convert_element_type | solution.py:180
  51.6 4.1 %fusion = f32[72,768]{1,0:T(8,128)S(1)} fusion(bf16[2,4096,768]{2,1,0:T(8,128)(2,1)} %copy-done, bf16[72,2048]{1,0:T(8,128)(2,1)S(1)} %get-tuple-element.39, bf16[72,2048]{1,0:T(8,128)(2,1)S(1)} %get-tuple-element.38), kind=kOutput, calls=%fused_computation.4 | convolution fusion | flops 454164480 | bytes 7102464 | tf_op jit(solution)/shard_map/dot_general | solution.py:167
  55.8 4.1 %fusion.3 = f32[72,768]{1,0:T(8,128)S(1)} fusion(bf16[2,4096,768]{2,1,0:T(8,128)(2,1)} %copy-done, bf16[72,2048]{1,0:T(8,128)(2,1)S(1)} %get-tuple-element.39, bf16[72,2048]{1,0:T(8,128)(2,1)S(1)} %get-tuple-element.38), kind=kOutput, calls=%fused_computation.7 | convolution fusion | flops 454164480 | bytes 7102464 | tf_op jit(solution)/shard_map/dot_general | solution.py:167
  60.1 1.4 %convolution_convert_fusion.2 = bf16[72,4096]{1,0:T(8,128)(2,1)S(1)} fusion(bf16[768,4096]{1,0:T(8,128)(2,1)S(1)} %bitcast.20, bf16[72,384]{1,0:T(8,128)(2,1)S(1)} %fusion.29, bf16[72,384]{1,0:T(8,128)(2,1)S(1)} %fusion.31), kind=kOutput, calls=%fused_computation.10 | convolution fusion | flops 453500928 | bytes 6991872 | tf_op jit(solution)/shard_map/dot_general | solution.py:170
  61.7 1.5 %collective-permute-done.17 = bf16[72,2048]{1,0:T(8,128)(2,1)S(1)} collective-permute-done((bf16[72,2048]{1,0:T(8,128)(2,1)S(1)}, bf16[72,2048]{1,0:T(8,128)(2,1)S(1)}, u32[]{:S(2)}, u32[]{:S(2)}) %collective-permute-start.17) | collective-permute-done | bytes 294944 | tf_op jit(solution)/shard_map/ppermute | solution.py:33
  63.3 0.7 collective-permute-start.18
  64.1 1.7 %collective-permute-start.19 = (bf16[96,1024]{1,0:T(8,128)(2,1)S(1)}, bf16[96,1024]{1,0:T(8,128)(2,1)S(1)}, u32[]{:S(2)}, u32[]{:S(2)}) collective-permute-start(bf16[96,1024]{1,0:T(8,128)(2,1)S(1)} %get-tuple-element.45), channel_id=1, source_target_pairs={{0,8},{8,0},{16,24},{24,16},{1,9},{9,1},{17,25},{25,17},{2,10},{10... | collective-permute-start | bytes 589832 | tf_op jit(solution)/shard_map/ppermute | solution.py:33
  66.2 4.2 %collective-permute-done.18 = bf16[96,1024]{1,0:T(8,128)(2,1)S(1)} collective-permute-done((bf16[96,1024]{1,0:T(8,128)(2,1)S(1)}, bf16[96,1024]{1,0:T(8,128)(2,1)S(1)}, u32[]{:S(2)}, u32[]{:S(2)}) %collective-permute-start.18) | collective-permute-done | bytes 196640 | tf_op jit(solution)/shard_map/ppermute | solution.py:33
  70.5 0.8 collective-permute-start.20
  71.4 1.7 %collective-permute-start.21 = (bf16[48,2048]{1,0:T(8,128)(2,1)S(1)}, bf16[48,2048]{1,0:T(8,128)(2,1)S(1)}, u32[]{:S(2)}, u32[]{:S(2)}) collective-permute-start(bf16[48,2048]{1,0:T(8,128)(2,1)S(1)} %get-tuple-element.41), channel_id=1, source_target_pairs={{0,16},{8,24},{16,0},{24,8},{1,17},{9,25},{17,1},{25,9},{2,18},{10... | collective-permute-start | bytes 589832 | tf_op jit(solution)/shard_map/ppermute | solution.py:33
  73.2 3.5 %collective-permute-done.20 = bf16[48,2048]{1,0:T(8,128)(2,1)S(1)} collective-permute-done((bf16[48,2048]{1,0:T(8,128)(2,1)S(1)}, bf16[48,2048]{1,0:T(8,128)(2,1)S(1)}, u32[]{:S(2)}, u32[]{:S(2)}) %collective-permute-start.20) | collective-permute-done | bytes 196640 | tf_op jit(solution)/shard_map/ppermute | solution.py:33
  77.4 1.3 %collective-permute-start.22 = (bf16[48,2048]{1,0:T(8,128)(2,1)S(1)}, bf16[48,2048]{1,0:T(8,128)(2,1)S(1)}, u32[]{:S(2)}, u32[]{:S(2)}) collective-permute-start(bf16[48,2048]{1,0:T(8,128)(2,1)S(1)} %get-tuple-element.18), channel_id=1, source_target_pairs={{0,8},{8,0},{16,24},{24,16},{1,9},{9,1},{17,25},{25,17},{2,10},{10... | collective-permute-start | bytes 589832 | tf_op jit(solution)/shard_map/ppermute | solution.py:33
  78.7 0.7 collective-permute-start.23
  79.4 3.7 %collective-permute-start.25 = (bf16[24,2048]{1,0:T(8,128)(2,1)S(1)}, bf16[24,2048]{1,0:T(8,128)(2,1)S(1)}, u32[]{:S(2)}, u32[]{:S(2)}) collective-permute-start(bf16[24,2048]{1,0:T(8,128)(2,1)S(1)} %get-tuple-element.46), channel_id=1, source_target_pairs={{0,4},{2,6},{4,0},{6,2},{1,5},{3,7},{5,1},{7,3},{8,12},{10,14},{12... | collective-permute-start | bytes 294920 | tf_op jit(solution)/shard_map/ppermute | solution.py:33
  83.2 1.6 %collective-permute-start.26 = (bf16[24,2048]{1,0:T(8,128)(2,1)S(1)}, bf16[24,2048]{1,0:T(8,128)(2,1)S(1)}, u32[]{:S(2)}, u32[]{:S(2)}) collective-permute-start(bf16[24,2048]{1,0:T(8,128)(2,1)S(1)} %get-tuple-element.47), channel_id=1, source_target_pairs={{0,6},{2,4},{4,2},{6,0},{1,7},{3,5},{5,3},{7,1},{8,14},{10,12},{12... | collective-permute-start | bytes 294920 | tf_op jit(solution)/shard_map/ppermute | solution.py:33
  84.9 1.2 %collective-permute-start.24 = (bf16[24,2048]{1,0:T(8,128)(2,1)S(1)}, bf16[24,2048]{1,0:T(8,128)(2,1)S(1)}, u32[]{:S(2)}, u32[]{:S(2)}) collective-permute-start(bf16[24,2048]{1,0:T(8,128)(2,1)S(1)} %slice.387), channel_id=1, source_target_pairs={{0,2},{2,0},{4,6},{6,4},{1,3},{3,1},{5,7},{7,5},{8,10},{10,8},{12,... | collective-permute-start | bytes 294920 | tf_op jit(solution)/shard_map/ppermute | solution.py:33
  86.3 3.7 %collective-permute-done.25 = bf16[24,2048]{1,0:T(8,128)(2,1)S(1)} collective-permute-done((bf16[24,2048]{1,0:T(8,128)(2,1)S(1)}, bf16[24,2048]{1,0:T(8,128)(2,1)S(1)}, u32[]{:S(2)}, u32[]{:S(2)}) %collective-permute-start.25) | collective-permute-done | bytes 98336 | tf_op jit(solution)/shard_map/ppermute | solution.py:33
  90.0 0.9 collective-permute-done.24
  91.5 0.7 collective-permute-done.27
  (118 shorter events, 8.8 us)
Async XLA Ops:
  3.2 1.4 %collective-permute-start = (bf16[12,2176]{1,0:T(8,128)(2,1)S(1)}, bf16[12,2176]{1,0:T(8,128)(2,1)S(1)}, u32[]{:S(2)}, u32[]{:S(2)}) collective-permute-start(bf16[12,2176]{1,0:T(8,128)(2,1)S(1)} %pad_maximum_fusion.16), channel_id=1, source_target_pairs={{0,1},{1,0},{2,3},{3,2},{4,5},{5,4},{6,7},{7,6},{8,9},{9,8},{10,11... | collective-permute-start | bytes 156680 | tf_op jit(solution)/shard_map/ppermute | solution.py:33
  4.7 6.2 %collective-permute-start.1 = (bf16[24,2176]{1,0:T(8,128)(2,1)S(1)}, bf16[24,2176]{1,0:T(8,128)(2,1)S(1)}, u32[]{:S(2)}, u32[]{:S(2)}) collective-permute-start(bf16[24,2176]{1,0:T(8,128)(2,1)S(1)} %get-tuple-element.11), channel_id=1, source_target_pairs={{0,2},{2,0},{4,6},{6,4},{1,3},{3,1},{5,7},{7,5},{8,10},{10,8},{12,... | collective-permute-start | bytes 313352 | tf_op jit(solution)/shard_map/ppermute | solution.py:33
  7.7 14.1 %collective-permute-start.7 = (bf16[24,2176]{1,0:T(8,128)(2,1)S(1)}, bf16[24,2176]{1,0:T(8,128)(2,1)S(1)}, u32[]{:S(2)}, u32[]{:S(2)}) collective-permute-start(bf16[24,2176]{1,0:T(8,128)(2,1)S(1)} %get-tuple-element.11), channel_id=1, source_target_pairs={{0,6},{2,4},{4,2},{6,0},{1,7},{3,5},{5,3},{7,1},{8,14},{10,12},{12... | collective-permute-start | bytes 313352 | tf_op jit(solution)/shard_map/ppermute | solution.py:33
  10.1 11.6 %collective-permute-start.6 = (bf16[24,2176]{1,0:T(8,128)(2,1)S(1)}, bf16[24,2176]{1,0:T(8,128)(2,1)S(1)}, u32[]{:S(2)}, u32[]{:S(2)}) collective-permute-start(bf16[24,2176]{1,0:T(8,128)(2,1)S(1)} %get-tuple-element.11), channel_id=1, source_target_pairs={{0,4},{2,6},{4,0},{6,2},{1,5},{3,7},{5,1},{7,3},{8,12},{10,14},{12... | collective-permute-start | bytes 313352 | tf_op jit(solution)/shard_map/ppermute | solution.py:33
  10.9 4.7 %collective-permute-start.2 = (bf16[24,2176]{1,0:T(8,128)(2,1)S(1)}, bf16[24,2176]{1,0:T(8,128)(2,1)S(1)}, u32[]{:S(2)}, u32[]{:S(2)}) collective-permute-start(bf16[24,2176]{1,0:T(8,128)(2,1)S(1)} %get-tuple-element.11), channel_id=1, source_target_pairs={{0,8},{8,0},{16,24},{24,16},{1,9},{9,1},{17,25},{25,17},{2,10},{10... | collective-permute-start | bytes 313352 | tf_op jit(solution)/shard_map/ppermute | solution.py:33
  12.6 5.0 %collective-permute-start.3 = (bf16[24,2176]{1,0:T(8,128)(2,1)S(1)}, bf16[24,2176]{1,0:T(8,128)(2,1)S(1)}, u32[]{:S(2)}, u32[]{:S(2)}) collective-permute-start(bf16[24,2176]{1,0:T(8,128)(2,1)S(1)} %get-tuple-element.11), channel_id=1, source_target_pairs={{0,16},{8,24},{16,0},{24,8},{1,17},{9,25},{17,1},{25,9},{2,18},{10... | collective-permute-start | bytes 313352 | tf_op jit(solution)/shard_map/ppermute | solution.py:33
  15.6 4.1 %collective-permute-start.4 = (bf16[24,1024]{1,0:T(8,128)(2,1)S(1)}, bf16[24,1024]{1,0:T(8,128)(2,1)S(1)}, u32[]{:S(2)}, u32[]{:S(2)}) collective-permute-start(bf16[24,1024]{1,0:T(8,128)(2,1)S(1)} %slice.336), channel_id=1, source_target_pairs={{0,16},{8,24},{16,0},{24,8},{1,17},{9,25},{17,1},{25,9},{2,18},{10... | collective-permute-start | bytes 147464 | tf_op jit(solution)/shard_map/ppermute | solution.py:33
  17.5 4.2 %collective-permute-start.5 = (bf16[24,1152]{1,0:T(8,128)(2,1)S(1)}, bf16[24,1152]{1,0:T(8,128)(2,1)S(1)}, u32[]{:S(2)}, u32[]{:S(2)}) collective-permute-start(bf16[24,1152]{1,0:T(8,128)(2,1)S(1)} %slice.337), channel_id=1, source_target_pairs={{0,8},{8,0},{16,24},{24,16},{1,9},{9,1},{17,25},{25,17},{2,10},{10... | collective-permute-start | bytes 165896 | tf_op jit(solution)/shard_map/ppermute | solution.py:33
  21.9 6.8 %collective-permute-start.8 = (bf16[168,2048]{1,0:T(8,128)(2,1)S(1)}, bf16[168,2048]{1,0:T(8,128)(2,1)S(1)}, u32[]{:S(2)}, u32[]{:S(2)}) collective-permute-start(bf16[168,2048]{1,0:T(8,128)(2,1)S(1)} %slice.338), channel_id=1, source_target_pairs={{0,1},{1,0},{2,3},{3,2},{4,5},{5,4},{6,7},{7,6},{8,9},{9,8},{10,11... | collective-permute-start | bytes 2064392 | tf_op jit(solution)/shard_map/ppermute | solution.py:33
  22.0 15.1 %collective-permute-start.11 = (bf16[72,2176]{1,0:T(8,128)(2,1)S(1)}, bf16[72,2176]{1,0:T(8,128)(2,1)S(1)}, u32[]{:S(2)}, u32[]{:S(2)}) collective-permute-start(bf16[72,2176]{1,0:T(8,128)(2,1)S(1)} %get-tuple-element.55), channel_id=1, source_target_pairs={{0,16},{8,24},{16,0},{24,8},{1,17},{9,25},{17,1},{25,9},{2,18},{10... | collective-permute-start | bytes 940040 | tf_op jit(solution)/shard_map/ppermute | solution.py:33
  23.7 13.4 %collective-permute-start.10 = (bf16[72,2176]{1,0:T(8,128)(2,1)S(1)}, bf16[72,2176]{1,0:T(8,128)(2,1)S(1)}, u32[]{:S(2)}, u32[]{:S(2)}) collective-permute-start(bf16[72,2176]{1,0:T(8,128)(2,1)S(1)} %get-tuple-element.55), channel_id=1, source_target_pairs={{0,8},{8,0},{16,24},{24,16},{1,9},{9,1},{17,25},{25,17},{2,10},{10... | collective-permute-start | bytes 940040 | tf_op jit(solution)/shard_map/ppermute | solution.py:33
  28.5 13.6 %copy-start = (bf16[2,4096,768]{2,1,0:T(8,128)(2,1)}, bf16[2,4096,768]{2,1,0:T(8,128)(2,1)S(1)}, u32[]{:S(2)}) copy-start(bf16[2,4096,768]{2,1,0:T(8,128)(2,1)S(1)} %shard_map.77) | copy-start | bytes 37748740
  28.9 5.4 %slice-start = ((s8[6291456]{0:T(1024)(128)(4,1)}), s8[4194304]{0:T(1024)(128)(4,1)S(1)}, s32[]{:S(2)}) async-start(s8[6291456]{0:T(1024)(128)(4,1)} %bitcast.14), calls=%async_computation | async-start | bytes 8388608
  30.2 5.7 %slice-start.1 = ((s8[6291456]{0:T(1024)(128)(4,1)}), s8[2097152]{0:T(1024)(128)(4,1)S(1)}, s32[]{:S(2)}) async-start(s8[6291456]{0:T(1024)(128)(4,1)} %bitcast.14), calls=%async_computation.1 | async-start | bytes 4194304
  37.2 3.7 %collective-permute-start.12 = (bf16[144,2048]{1,0:T(8,128)(2,1)S(1)}, bf16[144,2048]{1,0:T(8,128)(2,1)S(1)}, u32[]{:S(2)}, u32[]{:S(2)}) collective-permute-start(bf16[144,2048]{1,0:T(8,128)(2,1)S(1)} %slice.354), channel_id=1, source_target_pairs={{0,1},{1,0},{2,3},{3,2},{4,5},{5,4},{6,7},{7,6},{8,9},{9,8},{10,11... | collective-permute-start | bytes 1769480 | tf_op jit(solution)/shard_map/ppermute | solution.py:33
  38.4 6.3 %collective-permute-start.14 = (bf16[72,1024]{1,0:T(8,128)(2,1)S(1)}, bf16[72,1024]{1,0:T(8,128)(2,1)S(1)}, u32[]{:S(2)}, u32[]{:S(2)}) collective-permute-start(bf16[72,1024]{1,0:T(8,128)(2,1)S(1)} %slice.289), channel_id=1, source_target_pairs={{0,16},{8,24},{16,0},{24,8},{1,17},{9,25},{17,1},{25,9},{2,18},{10... | collective-permute-start | bytes 442376 | tf_op jit(solution)/shard_map/ppermute | solution.py:33
  39.9 6.4 %collective-permute-start.15 = (bf16[72,1152]{1,0:T(8,128)(2,1)S(1)}, bf16[72,1152]{1,0:T(8,128)(2,1)S(1)}, u32[]{:S(2)}, u32[]{:S(2)}) collective-permute-start(bf16[72,1152]{1,0:T(8,128)(2,1)S(1)} %slice.290), channel_id=1, source_target_pairs={{0,8},{8,0},{16,24},{24,16},{1,9},{9,1},{17,25},{25,17},{2,10},{10... | collective-permute-start | bytes 497672 | tf_op jit(solution)/shard_map/ppermute | solution.py:33
  40.6 9.4 %collective-permute-start.9 = (bf16[168,2048]{1,0:T(8,128)(2,1)}, bf16[168,2048]{1,0:T(8,128)(2,1)}, u32[]{:S(2)}, u32[]{:S(2)}) collective-permute-start(bf16[168,2048]{1,0:T(8,128)(2,1)} %broadcast_select_fusion), channel_id=1, source_target_pairs={{0,1},{1,0},{2,3},{3,2},{4,5},{5,4},{6,7},{7,6},{8,9},{9,8},{10,11... | collective-permute-start | bytes 2064392 | tf_op jit(solution)/shard_map/ppermute | solution.py:33
  44.6 1.8 %copy-start.4 = (bf16[72,1024]{1,0:T(8,128)(2,1)}, bf16[72,1024]{1,0:T(8,128)(2,1)S(1)}, u32[]{:S(2)}) copy-start(bf16[72,1024]{1,0:T(8,128)(2,1)S(1)} %collective-permute-done.14) | copy-start | bytes 442372
  46.3 0.7 copy-start.3
  48.2 3.3 %collective-permute-start.16 = (bf16[72,2048]{1,0:T(8,128)(2,1)S(1)}, bf16[72,2048]{1,0:T(8,128)(2,1)S(1)}, u32[]{:S(2)}, u32[]{:S(2)}) collective-permute-start(bf16[72,2048]{1,0:T(8,128)(2,1)S(1)} %pad_maximum_fusion.9), channel_id=1, source_target_pairs={{0,1},{1,0},{2,3},{3,2},{4,5},{5,4},{6,7},{7,6},{8,9},{9,8},{10,11... | collective-permute-start | bytes 884744 | tf_op jit(solution)/shard_map/ppermute | solution.py:33
  48.3 17.5 %collective-permute-start.13 = (bf16[144,2048]{1,0:T(8,128)(2,1)S(1)}, bf16[144,2048]{1,0:T(8,128)(2,1)S(1)}, u32[]{:S(2)}, u32[]{:S(2)}) collective-permute-start(bf16[144,2048]{1,0:T(8,128)(2,1)S(1)} %broadcast_select_fusion.3), channel_id=1, source_target_pairs={{0,1},{1,0},{2,3},{3,2},{4,5},{5,4},{6,7},{7,6},{8,9},{9,8},{10,11... | collective-permute-start | bytes 1769480 | tf_op jit(solution)/shard_map/ppermute | solution.py:33
  51.5 10.2 %copy-start.1 = (bf16[168,2048]{1,0:T(8,128)(2,1)}, bf16[168,2048]{1,0:T(8,128)(2,1)S(1)}, u32[]{:S(2)}) copy-start(bf16[168,2048]{1,0:T(8,128)(2,1)S(1)} %add_convert_fusion) | copy-start | bytes 2064388
  51.6 8.4 %slice-start.2 = ((s8[6291456]{0:T(1024)(128)(4,1)}), s8[4194304]{0:T(1024)(128)(4,1)S(1)}, s32[]{:S(2)}) async-start(s8[6291456]{0:T(1024)(128)(4,1)} %bitcast.18), calls=%async_computation.2 | async-start | bytes 8388608
  55.8 4.3 %slice-start.3 = ((s8[6291456]{0:T(1024)(128)(4,1)}), s8[2097152]{0:T(1024)(128)(4,1)S(1)}, s32[]{:S(2)}) async-start(s8[6291456]{0:T(1024)(128)(4,1)} %bitcast.18), calls=%async_computation.3 | async-start | bytes 4194304
  61.6 1.6 %collective-permute-start.17 = (bf16[72,2048]{1,0:T(8,128)(2,1)S(1)}, bf16[72,2048]{1,0:T(8,128)(2,1)S(1)}, u32[]{:S(2)}, u32[]{:S(2)}) collective-permute-start(bf16[72,2048]{1,0:T(8,128)(2,1)S(1)} %broadcast_select_fusion.6), channel_id=1, source_target_pairs={{0,1},{1,0},{2,3},{3,2},{4,5},{5,4},{6,7},{7,6},{8,9},{9,8},{10,11... | collective-permute-start | bytes 884744 | tf_op jit(solution)/shard_map/ppermute | solution.py:33
  63.3 7.0 %collective-permute-start.18 = (bf16[96,1024]{1,0:T(8,128)(2,1)S(1)}, bf16[96,1024]{1,0:T(8,128)(2,1)S(1)}, u32[]{:S(2)}, u32[]{:S(2)}) collective-permute-start(bf16[96,1024]{1,0:T(8,128)(2,1)S(1)} %get-tuple-element.44), channel_id=1, source_target_pairs={{0,16},{8,24},{16,0},{24,8},{1,17},{9,25},{17,1},{25,9},{2,18},{10... | collective-permute-start | bytes 589832 | tf_op jit(solution)/shard_map/ppermute | solution.py:33
  64.1 7.2 %collective-permute-start.19 = (bf16[96,1024]{1,0:T(8,128)(2,1)S(1)}, bf16[96,1024]{1,0:T(8,128)(2,1)S(1)}, u32[]{:S(2)}, u32[]{:S(2)}) collective-permute-start(bf16[96,1024]{1,0:T(8,128)(2,1)S(1)} %get-tuple-element.45), channel_id=1, source_target_pairs={{0,8},{8,0},{16,24},{24,16},{1,9},{9,1},{17,25},{25,17},{2,10},{10... | collective-permute-start | bytes 589832 | tf_op jit(solution)/shard_map/ppermute | solution.py:33
  66.2 7.0 %slice-start.4 = ((bf16[168,2048]{1,0:T(8,128)(2,1)}), bf16[72,2048]{1,0:T(8,128)(2,1)S(1)}, s32[]{:S(2)}) async-start(bf16[168,2048]{1,0:T(8,128)(2,1)} %copy-done.1), calls=%async_computation.4 | async-start | bytes 589824 | tf_op jit(solution)/shard_map/slice | solution.py:185
  70.4 6.9 %copy-start.2 = (bf16[168,2048]{1,0:T(8,128)(2,1)S(1)}, bf16[168,2048]{1,0:T(8,128)(2,1)}, u32[]{:S(2)}) copy-start(bf16[168,2048]{1,0:T(8,128)(2,1)} %copy-done.1) | copy-start | bytes 2064388
  70.5 6.2 %collective-permute-start.20 = (bf16[48,2048]{1,0:T(8,128)(2,1)S(1)}, bf16[48,2048]{1,0:T(8,128)(2,1)S(1)}, u32[]{:S(2)}, u32[]{:S(2)}) collective-permute-start(bf16[48,2048]{1,0:T(8,128)(2,1)S(1)} %get-tuple-element.43), channel_id=1, source_target_pairs={{0,8},{8,0},{16,24},{24,16},{1,9},{9,1},{17,25},{25,17},{2,10},{10... | collective-permute-start | bytes 589832 | tf_op jit(solution)/shard_map/ppermute | solution.py:33
  71.4 5.9 %collective-permute-start.21 = (bf16[48,2048]{1,0:T(8,128)(2,1)S(1)}, bf16[48,2048]{1,0:T(8,128)(2,1)S(1)}, u32[]{:S(2)}, u32[]{:S(2)}) collective-permute-start(bf16[48,2048]{1,0:T(8,128)(2,1)S(1)} %get-tuple-element.41), channel_id=1, source_target_pairs={{0,16},{8,24},{16,0},{24,8},{1,17},{9,25},{17,1},{25,9},{2,18},{10... | collective-permute-start | bytes 589832 | tf_op jit(solution)/shard_map/ppermute | solution.py:33
  77.4 7.4 %collective-permute-start.22 = (bf16[48,2048]{1,0:T(8,128)(2,1)S(1)}, bf16[48,2048]{1,0:T(8,128)(2,1)S(1)}, u32[]{:S(2)}, u32[]{:S(2)}) collective-permute-start(bf16[48,2048]{1,0:T(8,128)(2,1)S(1)} %get-tuple-element.18), channel_id=1, source_target_pairs={{0,8},{8,0},{16,24},{24,16},{1,9},{9,1},{17,25},{25,17},{2,10},{10... | collective-permute-start | bytes 589832 | tf_op jit(solution)/shard_map/ppermute | solution.py:33
  78.7 6.1 %collective-permute-start.23 = (bf16[48,2048]{1,0:T(8,128)(2,1)S(1)}, bf16[48,2048]{1,0:T(8,128)(2,1)S(1)}, u32[]{:S(2)}, u32[]{:S(2)}) collective-permute-start(bf16[48,2048]{1,0:T(8,128)(2,1)S(1)} %get-tuple-element.19), channel_id=1, source_target_pairs={{0,16},{8,24},{16,0},{24,8},{1,17},{9,25},{17,1},{25,9},{2,18},{10... | collective-permute-start | bytes 589832 | tf_op jit(solution)/shard_map/ppermute | solution.py:33
  79.4 10.5 %collective-permute-start.25 = (bf16[24,2048]{1,0:T(8,128)(2,1)S(1)}, bf16[24,2048]{1,0:T(8,128)(2,1)S(1)}, u32[]{:S(2)}, u32[]{:S(2)}) collective-permute-start(bf16[24,2048]{1,0:T(8,128)(2,1)S(1)} %get-tuple-element.46), channel_id=1, source_target_pairs={{0,4},{2,6},{4,0},{6,2},{1,5},{3,7},{5,1},{7,3},{8,12},{10,14},{12... | collective-permute-start | bytes 294920 | tf_op jit(solution)/shard_map/ppermute | solution.py:33
  83.2 6.8 %collective-permute-start.26 = (bf16[24,2048]{1,0:T(8,128)(2,1)S(1)}, bf16[24,2048]{1,0:T(8,128)(2,1)S(1)}, u32[]{:S(2)}, u32[]{:S(2)}) collective-permute-start(bf16[24,2048]{1,0:T(8,128)(2,1)S(1)} %get-tuple-element.47), channel_id=1, source_target_pairs={{0,6},{2,4},{4,2},{6,0},{1,7},{3,5},{5,3},{7,1},{8,14},{10,12},{12... | collective-permute-start | bytes 294920 | tf_op jit(solution)/shard_map/ppermute | solution.py:33
  84.9 5.9 %collective-permute-start.24 = (bf16[24,2048]{1,0:T(8,128)(2,1)S(1)}, bf16[24,2048]{1,0:T(8,128)(2,1)S(1)}, u32[]{:S(2)}, u32[]{:S(2)}) collective-permute-start(bf16[24,2048]{1,0:T(8,128)(2,1)S(1)} %slice.387), channel_id=1, source_target_pairs={{0,2},{2,0},{4,6},{6,4},{1,3},{3,1},{5,7},{7,5},{8,10},{10,8},{12,... | collective-permute-start | bytes 294920 | tf_op jit(solution)/shard_map/ppermute | solution.py:33
  90.9 1.3 %collective-permute-start.27 = (bf16[12,2048]{1,0:T(8,128)(2,1)S(1)}, bf16[12,2048]{1,0:T(8,128)(2,1)S(1)}, u32[]{:S(2)}, u32[]{:S(2)}) collective-permute-start(bf16[12,2048]{1,0:T(8,128)(2,1)S(1)} %broadcast_select_fusion.13), channel_id=1, source_target_pairs={{0,1},{1,0},{2,3},{3,2},{4,5},{5,4},{6,7},{7,6},{8,9},{9,8},{10,11... | collective-permute-start | bytes 147464 | tf_op jit(solution)/shard_map/ppermute | solution.py:33

commit v7 on v5

--- a/solution.py
+++ b/solution.py
@@ -111,12 +111,16 @@
         scratch_shapes=[pltpu.SemaphoreType.DMA((2,))],
         compiler_params=pltpu.CompilerParams(vmem_limit_bytes=32 * 2**20),
         cost_estimate=pl.CostEstimate(flops=0, bytes_accessed=nbytes, transcendentals=0),
-    )(up, down)
+    )(
+        pltpu.with_memory_space_constraint(up, pltpu.HBM),
+        pltpu.with_memory_space_constraint(down, pltpu.HBM),
+    )
 
 
 def on_device(tokens, expert_ids, gate_probs, in_weight, out_weight, swap_slot):
     groups, chips = lax.axis_size("dp"), lax.axis_size("chip")
     owners = 2 * chips
+    near_chips = chips // 2
     per_device = in_weight.shape[0]
     rows, width = tokens.shape
     part = width // 2
@@ -186,28 +190,27 @@
             edges.append(edges[-1] + block.shape[0])
         return [chip_sum[low:high] for low, high in zip(edges, edges[1:])]
 
-    others = [swap(chip_rows, "chip", j) for j in range(1, chips)]
-    near = [chip_rows, *spread_near(behind(chip_rows, others[0]))]
-    near += joined(spread_rest(near[1:]))
-    in_weight, out_weight = loaded(*behind((in_weight, out_weight), near[1:3]))
-    far = [row_major(jnp.concatenate(others, 0))]
-    far += spread_near(far[0])
-    first_blocks = [*near, far[0]]
-    first_part = own_sums(first_blocks)
-    far[1:] = behind(far[1:], first_part)
-    rest = spread_rest(far[1:])
-    sums = chip_sums(first_part, first_blocks)
-    part_two = own_sums(far[1:])
+    chip_blocks = [chip_rows] + [swap(chip_rows, "chip", j) for j in range(1, chips)]
+    in_weight, out_weight = loaded(*behind((in_weight, out_weight), chip_rows))
+    chip_blocks[1:] = behind(chip_blocks[1:], in_weight)
+    held = [row_major(jnp.concatenate(chip_blocks, 0))]
+    held += spread_near(held[0])
+    first_part = own_sums(held[:1])
+    held[1:] = behind(held[1:], first_part)
+    rest = spread_rest(held[1:])
+    sums = chip_sums(first_part, held[:1])
+    second_part = own_sums(held[1:])
+    sums += chip_sums(second_part, held[1:])
     if rest:
-        rest = joined(behind(rest, part_two))
-        part_three = own_sums(rest)
-        sums += chip_sums(part_two, far[1:]) + chip_sums(part_three, rest)
-    else:
-        sums += chip_sums(part_two, far[1:])
-    far += rest
-    sums = [jnp.concatenate([sums[k], sums[groups + k]], 0) for k in range(groups)]
-    total = collected(with_fourth(sums))
-    blocks = [total[j * 2 * rows : (j + 1) * 2 * rows] for j in range(chips)]
+        rest = joined(behind(rest, second_part))
+        sums += chip_sums(own_sums(rest), rest)
+    held += rest
+    sums = with_fourth(sums)
+    border = 2 * near_chips * rows
+    total = collected([block[border:] for block in sums])
+    blocks = [total[low : low + 2 * rows] for low in range(0, total.shape[0], 2 * rows)]
+    total = collected(behind([block[:border] for block in sums], total))
+    blocks = [total[low : low + 2 * rows] for low in range(0, border, 2 * rows)] + blocks
     total = wide(blocks[0])
     for j in range(1, chips):
         total = total + wide(swap(blocks[j], "chip", j))
@@ -219,7 +222,7 @@
         jnp.concatenate([jnp.where(first, kept, arrived), jnp.where(first, arrived, kept)], 1)
     )
 
-    ids, gates = routes(jnp.concatenate([block[:, part:] for block in near + far], 0))
+    ids, gates = routes(jnp.concatenate([block[:, part:] for block in held], 0))
     step = 2.0 ** (31 - (ids.shape[0] * GATE_MOST).bit_length())
     amounts = jnp.round(gates * step).astype(jnp.int32)
     totals = jnp.sum(jnp.where(ids[..., None] == all_experts, amounts[..., None], 0), (0, 1))

time: 84.8 us -> 89 us (1.050)
  matrix products: 10.7 us -> 22.8 us
  waiting for transfers between devices: 29.8 us -> 20.6 us
  local copies, waits for them, and re-layouts: 2.2 us -> 9.42 us
  starting transfers between devices: 28.2 us -> 22.7 us
    dot_general x6, matrix products: 7.05 us -> 19 us  [own_sums(): jnp.dot(held_tokens, in_weight[s], preferred_element_type=jnp.float32)]
    ppermute x26 -> x24, waiting for transfers between devices: 29.8 us -> 20.6 us  [swap(): return row_major(lax.ppermute(row_major(value), axis, pairs))]
    unnamed x13 -> x27, local copies, waits for them, and re-layouts: 1.69 us -> 8.97 us
    ppermute x26 -> x24, starting transfers between devices: 28.2 us -> 22.7 us  [swap(): return row_major(lax.ppermute(row_major(value), axis, pairs))]
  transfers between devices with their start and end apart: 26 -> 24, of which waited for: 17 -> 15; matrix products, arithmetic and copies ran while one was open for 18% -> 19% of each run, Pallas kernels for 8% -> 7%
where the time goes in v7:
time: 89 us; the launch traced here: 88.7 us
  matrix products  22.8 us (26%)
  starting transfers between devices  22.7 us (26%)
  waiting for transfers between devices  20.6 us (23%)
  local copies, waits for them, and re-layouts  9.42 us (11%)
  Pallas kernels  6.38 us (7%)
  other arithmetic  5.56 us (6%)
  between operations  1.22 us (1%)
    ppermute x24, starting transfers between devices, swap(): return row_major(lax.ppermute(row_major(value), axis, pairs))  22.7 us
    ppermute x24, waiting for transfers between devices, swap(): return row_major(lax.ppermute(row_major(value), axis, pairs))  20.6 us
    dot_general x6, matrix products, own_sums(): jnp.dot(held_tokens, in_weight[s], preferred_element_type=jnp.float32)  19 us
    unnamed x27, local copies, waits for them, and re-layouts  8.97 us
    pallas_call x1, Pallas kernels, loaded(): pl.pallas_call(load_kernel, in_specs=[pl.BlockSpec(memory_space=pl.ANY)]...  6.38 us
    dot_general x3, matrix products, own_sums(): jnp.dot(jnp.concatenate(hidden, 1), out_weight.reshape(per_device * half_...  3.76 us
  transfers between devices with their start and end apart: 24, of which 15 were waited for; matrix products, arithmetic and copies ran while one was open for 19% of the time, Pallas kernels for 7%

profile of v7, /device:TPU:0, one launch (start us, length us, event | category | flops | bytes accessed | tf_op | source)
XLA Modules:
  0.0 88.7 jit_solution(6856522856485408658)
XLA Ops:
  0.6 0.8 copy.14
  1.4 0.8 copy.15
  2.2 0.9 broadcast_select_fusion.16
  3.2 0.5 collective-permute-start
  3.7 0.9 %collective-permute-done = bf16[12,2176]{1,0:T(8,128)(2,1)S(1)} collective-permute-done((bf16[12,2176]{1,0:T(8,128)(2,1)S(1)}, bf16[12,2176]{1,0:T(8,128)(2,1)S(1)}, u32[]{:S(2)}, u32[]{:S(2)}) %collective-permute-start) | collective-permute-done | bytes 52256 | tf_op jit(solution)/shard_map/ppermute | solution.py:33
  4.7 3.0 %collective-permute-start.1 = (bf16[24,2176]{1,0:T(8,128)(2,1)S(1)}, bf16[24,2176]{1,0:T(8,128)(2,1)S(1)}, u32[]{:S(2)}, u32[]{:S(2)}) collective-permute-start(bf16[24,2176]{1,0:T(8,128)(2,1)S(1)} %pad_maximum_fusion.14), channel_id=1, source_target_pairs={{0,2},{2,0},{4,6},{6,4},{1,3},{3,1},{5,7},{7,5},{8,10},{10,8},{12,... | collective-permute-start | bytes 313352 | tf_op jit(solution)/shard_map/ppermute | solution.py:33
  7.7 2.5 %collective-permute-start.3 = (bf16[24,2176]{1,0:T(8,128)(2,1)S(1)}, bf16[24,2176]{1,0:T(8,128)(2,1)S(1)}, u32[]{:S(2)}, u32[]{:S(2)}) collective-permute-start(bf16[24,2176]{1,0:T(8,128)(2,1)S(1)} %pad_maximum_fusion.14), channel_id=1, source_target_pairs={{0,6},{2,4},{4,2},{6,0},{1,7},{3,5},{5,3},{7,1},{8,14},{10,12},{12... | collective-permute-start | bytes 313352 | tf_op jit(solution)/shard_map/ppermute | solution.py:33
  10.3 6.4 %shard_map.77 = (bf16[2,4096,768]{2,1,0:T(8,128)(2,1)S(1)}, bf16[2,384,4096]{2,1,0:T(8,128)(2,1)S(1)}) custom-call(bf16[2,4096,768]{2,1,0:T(8,128)(2,1)} %up_ref, bf16[2,384,4096]{2,1,0:T(8,128)(2,1)} %down_ref), custom_call_target="tpu_custom_call" | custom-call | bytes 18874368 | tf_op jit(solution)/shard_map/pallas_call | solution.py:106
  16.7 2.6 %copy-done = bf16[2,384,4096]{2,1,0:T(8,128)(2,1)} copy-done((bf16[2,384,4096]{2,1,0:T(8,128)(2,1)}, bf16[2,384,4096]{2,1,0:T(8,128)(2,1)S(1)}, u32[]{:S(2)}) %copy-start) | copy-done | bytes 6291480
  19.3 4.5 %copy-done.1 = bf16[2,4096,768]{2,1,0:T(8,128)(2,1)} copy-done((bf16[2,4096,768]{2,1,0:T(8,128)(2,1)}, bf16[2,4096,768]{2,1,0:T(8,128)(2,1)S(1)}, u32[]{:S(2)}) %copy-start.1) | copy-done | bytes 12582936
  24.1 1.5 %collective-permute-start.6 = (bf16[96,2176]{1,0:T(8,128)(2,1)S(1)}, bf16[96,2176]{1,0:T(8,128)(2,1)S(1)}, u32[]{:S(2)}, u32[]{:S(2)}) collective-permute-start(bf16[96,2176]{1,0:T(8,128)(2,1)S(1)} %pad_maximum_fusion.9), channel_id=1, source_target_pairs={{0,8},{8,0},{16,24},{24,16},{1,9},{9,1},{17,25},{25,17},{2,10},{10... | collective-permute-start | bytes 1253384 | tf_op jit(solution)/shard_map/ppermute | solution.py:33
  25.6 1.5 %collective-permute-start.7 = (bf16[96,2176]{1,0:T(8,128)(2,1)S(1)}, bf16[96,2176]{1,0:T(8,128)(2,1)S(1)}, u32[]{:S(2)}, u32[]{:S(2)}) collective-permute-start(bf16[96,2176]{1,0:T(8,128)(2,1)S(1)} %pad_maximum_fusion.9), channel_id=1, source_target_pairs={{0,16},{8,24},{16,0},{24,8},{1,17},{9,25},{17,1},{25,9},{2,18},{10... | collective-permute-start | bytes 1253384 | tf_op jit(solution)/shard_map/ppermute | solution.py:33
  27.4 4.1 %fusion.10 = f32[96,768]{1,0:T(8,128)S(1)} fusion(bf16[2,4096,768]{2,1,0:T(8,128)(2,1)} %copy-done.1, bf16[96,2048]{1,0:T(8,128)(2,1)S(1)} %get-tuple-element.39, bf16[96,2048]{1,0:T(8,128)(2,1)S(1)} %get-tuple-element.38), kind=kOutput, calls=%fused_computation.10 | convolution fusion | flops 605552640 | bytes 7372800 | tf_op jit(solution)/shard_map/dot_general | solution.py:173
  31.4 4.1 %fusion.4 = f32[96,768]{1,0:T(8,128)S(1)} fusion(bf16[2,4096,768]{2,1,0:T(8,128)(2,1)} %copy-done.1, bf16[96,2048]{1,0:T(8,128)(2,1)S(1)} %get-tuple-element.39, bf16[96,2048]{1,0:T(8,128)(2,1)S(1)} %get-tuple-element.38), kind=kOutput, calls=%fused_computation.4 | convolution fusion | flops 605552640 | bytes 7372800 | tf_op jit(solution)/shard_map/dot_general | solution.py:173
  35.7 1.2 %convolution_convert_fusion.2 = bf16[96,4096]{1,0:T(8,128)(2,1)S(1)} fusion(bf16[768,4096]{1,0:T(8,128)(2,1)S(1)} %bitcast.20, bf16[96,384]{1,0:T(8,128)(2,1)S(1)} %get-tuple-element.63, bf16[96,384]{1,0:T(8,128)(2,1)S(1)} %get-tuple-element.64), kind=kOutput, calls=%fused_computation.20 | convolution fusion | flops 604667904 | bytes 7225344 | tf_op jit(solution)/shard_map/dot_general | solution.py:176
  37.8 1.4 %collective-permute-start.10 = (bf16[96,1024]{1,0:T(8,128)(2,1)S(1)}, bf16[96,1024]{1,0:T(8,128)(2,1)S(1)}, u32[]{:S(2)}, u32[]{:S(2)}) collective-permute-start(bf16[96,1024]{1,0:T(8,128)(2,1)S(1)} %slice.248), channel_id=1, source_target_pairs={{0,16},{8,24},{16,0},{24,8},{1,17},{9,25},{17,1},{25,9},{2,18},{10... | collective-permute-start | bytes 589832 | tf_op jit(solution)/shard_map/ppermute | solution.py:33
  39.2 0.5 collective-permute-start.11
  40.6 1.4 %fusion.8 = f32[192,768]{1,0:T(8,128)S(1)} fusion(bf16[2,4096,768]{2,1,0:T(8,128)(2,1)S(1)} %bitcast.26, bf16[192,2048]{1,0:T(8,128)(2,1)S(1)} %get-tuple-element.37, bf16[192,2048]{1,0:T(8,128)(2,1)S(1)} %get-tuple-element.36), kind=kOutput, calls=%fused_computation.8 | convolution fusion | flops 1211105280 | bytes 8454144 | tf_op jit(solution)/shard_map/dot_general | solution.py:173
  42.0 1.4 %fusion.2 = f32[192,768]{1,0:T(8,128)S(1)} fusion(bf16[2,4096,768]{2,1,0:T(8,128)(2,1)S(1)} %bitcast.26, bf16[192,2048]{1,0:T(8,128)(2,1)S(1)} %get-tuple-element.37, bf16[192,2048]{1,0:T(8,128)(2,1)S(1)} %get-tuple-element.36), kind=kOutput, calls=%fused_computation.2 | convolution fusion | flops 1211105280 | bytes 8454144 | tf_op jit(solution)/shard_map/dot_general | solution.py:173
  43.7 1.4 %convolution_convert_fusion = bf16[192,4096]{1,0:T(8,128)(2,1)S(1)} fusion(bf16[768,4096]{1,0:T(8,128)(2,1)S(1)} %bitcast.21, bf16[192,384]{1,0:T(8,128)(2,1)S(1)} %fusion.19, bf16[192,384]{1,0:T(8,128)(2,1)S(1)} %fusion.21), kind=kOutput, calls=%fused_computation.12 | convolution fusion | flops 1209335808 | bytes 8159232 | tf_op jit(solution)/shard_map/dot_general | solution.py:176
  45.1 1.7 %collective-permute-done.11 = bf16[96,1152]{1,0:T(8,128)(2,1)S(1)} collective-permute-done((bf16[96,1152]{1,0:T(8,128)(2,1)S(1)}, bf16[96,1152]{1,0:T(8,128)(2,1)S(1)}, u32[]{:S(2)}, u32[]{:S(2)}) %collective-permute-start.11) | collective-permute-done | bytes 221216 | tf_op jit(solution)/shard_map/ppermute | solution.py:33
  47.5 1.1 %collective-permute-done.12 = bf16[96,2048]{1,0:T(8,128)(2,1)S(1)} collective-permute-done((bf16[96,2048]{1,0:T(8,128)(2,1)S(1)}, bf16[96,2048]{1,0:T(8,128)(2,1)S(1)}, u32[]{:S(2)}, u32[]{:S(2)}) %collective-permute-start.12) | collective-permute-done | bytes 393248 | tf_op jit(solution)/shard_map/ppermute | solution.py:33
  48.7 4.1 %fusion.6 = f32[96,768]{1,0:T(8,128)S(1)} fusion(bf16[2,4096,768]{2,1,0:T(8,128)(2,1)} %copy-done.1, bf16[96,2048]{1,0:T(8,128)(2,1)S(1)} %get-tuple-element.45, bf16[96,2048]{1,0:T(8,128)(2,1)S(1)} %get-tuple-element.44), kind=kOutput, calls=%fused_computation.6 | convolution fusion | flops 605552640 | bytes 7372800 | tf_op jit(solution)/shard_map/dot_general | solution.py:173
  52.7 4.1 %fusion = f32[96,768]{1,0:T(8,128)S(1)} fusion(bf16[2,4096,768]{2,1,0:T(8,128)(2,1)} %copy-done.1, bf16[96,2048]{1,0:T(8,128)(2,1)S(1)} %get-tuple-element.45, bf16[96,2048]{1,0:T(8,128)(2,1)S(1)} %get-tuple-element.44), kind=kOutput, calls=%fused_computation | convolution fusion | flops 605552640 | bytes 7372800 | tf_op jit(solution)/shard_map/dot_general | solution.py:173
  57.0 1.2 %convolution_convert_fusion.1 = bf16[96,4096]{1,0:T(8,128)(2,1)S(1)} fusion(bf16[768,4096]{1,0:T(8,128)(2,1)S(1)} %bitcast.24, bf16[96,384]{1,0:T(8,128)(2,1)S(1)} %fusion.28, bf16[96,384]{1,0:T(8,128)(2,1)S(1)} %fusion.30), kind=kOutput, calls=%fused_computation.19 | convolution fusion | flops 604667904 | bytes 7225344 | tf_op jit(solution)/shard_map/dot_general | solution.py:176
  58.5 0.4 collective-permute-start.9
  59.1 0.9 %collective-permute-done.13 = bf16[96,2048]{1,0:T(8,128)(2,1)S(1)} collective-permute-done((bf16[96,2048]{1,0:T(8,128)(2,1)S(1)}, bf16[96,2048]{1,0:T(8,128)(2,1)S(1)}, u32[]{:S(2)}, u32[]{:S(2)}) %collective-permute-start.13) | collective-permute-done | bytes 393248 | tf_op jit(solution)/shard_map/ppermute | solution.py:33
  60.2 0.6 collective-permute-start.14
  60.8 0.5 collective-permute-start.15
  61.3 0.4 add_convert_fusion
  61.8 5.5 %collective-permute-done.14 = bf16[96,1024]{1,0:T(8,128)(2,1)S(1)} collective-permute-done((bf16[96,1024]{1,0:T(8,128)(2,1)S(1)}, bf16[96,1024]{1,0:T(8,128)(2,1)S(1)}, u32[]{:S(2)}, u32[]{:S(2)}) %collective-permute-start.14) | collective-permute-done | bytes 196640 | tf_op jit(solution)/shard_map/ppermute | solution.py:33
  67.6 1.6 %collective-permute-start.17 = (bf16[48,2048]{1,0:T(8,128)(2,1)S(1)}, bf16[48,2048]{1,0:T(8,128)(2,1)S(1)}, u32[]{:S(2)}, u32[]{:S(2)}) collective-permute-start(bf16[48,2048]{1,0:T(8,128)(2,1)S(1)} %get-tuple-element.47), channel_id=1, source_target_pairs={{0,16},{8,24},{16,0},{24,8},{1,17},{9,25},{17,1},{25,9},{2,18},{10... | collective-permute-start | bytes 589832 | tf_op jit(solution)/shard_map/ppermute | solution.py:33
  69.3 0.6 collective-permute-start.16
  69.9 3.7 %collective-permute-done.17 = bf16[48,2048]{1,0:T(8,128)(2,1)S(1)} collective-permute-done((bf16[48,2048]{1,0:T(8,128)(2,1)S(1)}, bf16[48,2048]{1,0:T(8,128)(2,1)S(1)}, u32[]{:S(2)}, u32[]{:S(2)}) %collective-permute-start.17) | collective-permute-done | bytes 196640 | tf_op jit(solution)/shard_map/ppermute | solution.py:33
  73.6 1.4 %collective-permute-done.16 = bf16[48,2048]{1,0:T(8,128)(2,1)S(1)} collective-permute-done((bf16[48,2048]{1,0:T(8,128)(2,1)S(1)}, bf16[48,2048]{1,0:T(8,128)(2,1)S(1)}, u32[]{:S(2)}, u32[]{:S(2)}) %collective-permute-start.16) | collective-permute-done | bytes 196640 | tf_op jit(solution)/shard_map/ppermute | solution.py:33
  75.1 0.6 collective-permute-start.18
  75.7 0.5 collective-permute-start.19
  76.2 2.9 %collective-permute-start.21 = (bf16[24,2048]{1,0:T(8,128)(2,1)S(1)}, bf16[24,2048]{1,0:T(8,128)(2,1)S(1)}, u32[]{:S(2)}, u32[]{:S(2)}) collective-permute-start(bf16[24,2048]{1,0:T(8,128)(2,1)S(1)} %get-tuple-element.52), channel_id=1, source_target_pairs={{0,4},{2,6},{4,0},{6,2},{1,5},{3,7},{5,1},{7,3},{8,12},{10,14},{12... | collective-permute-start | bytes 294920 | tf_op jit(solution)/shard_map/ppermute | solution.py:33
  79.1 1.3 %collective-permute-start.22 = (bf16[24,2048]{1,0:T(8,128)(2,1)S(1)}, bf16[24,2048]{1,0:T(8,128)(2,1)S(1)}, u32[]{:S(2)}, u32[]{:S(2)}) collective-permute-start(bf16[24,2048]{1,0:T(8,128)(2,1)S(1)} %get-tuple-element.53), channel_id=1, source_target_pairs={{0,6},{2,4},{4,2},{6,0},{1,7},{3,5},{5,3},{7,1},{8,14},{10,12},{12... | collective-permute-start | bytes 294920 | tf_op jit(solution)/shard_map/ppermute | solution.py:33
  80.4 0.4 collective-permute-done.18
  80.8 0.5 collective-permute-done.19
  81.4 1.9 %collective-permute-start.20 = (bf16[24,2048]{1,0:T(8,128)(2,1)S(1)}, bf16[24,2048]{1,0:T(8,128)(2,1)S(1)}, u32[]{:S(2)}, u32[]{:S(2)}) collective-permute-start(bf16[24,2048]{1,0:T(8,128)(2,1)S(1)} %slice.330), channel_id=1, source_target_pairs={{0,2},{2,0},{4,6},{6,4},{1,3},{3,1},{5,7},{7,5},{8,10},{10,8},{12,... | collective-permute-start | bytes 294920 | tf_op jit(solution)/shard_map/ppermute | solution.py:33
  83.4 0.3 collective-permute-done.21
  83.7 1.9 %collective-permute-done.22 = bf16[24,2048]{1,0:T(8,128)(2,1)S(1)} collective-permute-done((bf16[24,2048]{1,0:T(8,128)(2,1)S(1)}, bf16[24,2048]{1,0:T(8,128)(2,1)S(1)}, u32[]{:S(2)}, u32[]{:S(2)}) %collective-permute-start.22) | collective-permute-done | bytes 98336 | tf_op jit(solution)/shard_map/ppermute | solution.py:33
  85.6 1.0 %collective-permute-done.20 = bf16[24,2048]{1,0:T(8,128)(2,1)S(1)} collective-permute-done((bf16[24,2048]{1,0:T(8,128)(2,1)S(1)}, bf16[24,2048]{1,0:T(8,128)(2,1)S(1)}, u32[]{:S(2)}, u32[]{:S(2)}) %collective-permute-start.20) | collective-permute-done | bytes 98336 | tf_op jit(solution)/shard_map/ppermute | solution.py:33
  86.8 0.5 broadcast_multiply_fusion
  87.3 0.7 collective-permute-done.23
  88.1 0.7 pad_maximum_fusion.13
  (103 shorter events, 5.3 us)
Async XLA Ops:
  3.2 1.4 %collective-permute-start = (bf16[12,2176]{1,0:T(8,128)(2,1)S(1)}, bf16[12,2176]{1,0:T(8,128)(2,1)S(1)}, u32[]{:S(2)}, u32[]{:S(2)}) collective-permute-start(bf16[12,2176]{1,0:T(8,128)(2,1)S(1)} %pad_maximum_fusion.16), channel_id=1, source_target_pairs={{0,1},{1,0},{2,3},{3,2},{4,5},{5,4},{6,7},{7,6},{8,9},{9,8},{10,11... | collective-permute-start | bytes 156680 | tf_op jit(solution)/shard_map/ppermute | solution.py:33
  4.7 19.3 %copy-start.4 = (s32[8]{0:T(128)S(1)}, s32[8]{0:T(128)}, u32[]{:S(2)}) copy-start(s32[8]{0:T(128)} %param.11) | copy-start | bytes 100
  4.7 19.1 %collective-permute-start.1 = (bf16[24,2176]{1,0:T(8,128)(2,1)S(1)}, bf16[24,2176]{1,0:T(8,128)(2,1)S(1)}, u32[]{:S(2)}, u32[]{:S(2)}) collective-permute-start(bf16[24,2176]{1,0:T(8,128)(2,1)S(1)} %pad_maximum_fusion.14), channel_id=1, source_target_pairs={{0,2},{2,0},{4,6},{6,4},{1,3},{3,1},{5,7},{7,5},{8,10},{10,8},{12,... | collective-permute-start | bytes 313352 | tf_op jit(solution)/shard_map/ppermute | solution.py:33
  7.7 16.1 %collective-permute-start.3 = (bf16[24,2176]{1,0:T(8,128)(2,1)S(1)}, bf16[24,2176]{1,0:T(8,128)(2,1)S(1)}, u32[]{:S(2)}, u32[]{:S(2)}) collective-permute-start(bf16[24,2176]{1,0:T(8,128)(2,1)S(1)} %pad_maximum_fusion.14), channel_id=1, source_target_pairs={{0,6},{2,4},{4,2},{6,0},{1,7},{3,5},{5,3},{7,1},{8,14},{10,12},{12... | collective-permute-start | bytes 313352 | tf_op jit(solution)/shard_map/ppermute | solution.py:33
  10.1 13.6 %collective-permute-start.2 = (bf16[24,2176]{1,0:T(8,128)(2,1)S(1)}, bf16[24,2176]{1,0:T(8,128)(2,1)S(1)}, u32[]{:S(2)}, u32[]{:S(2)}) collective-permute-start(bf16[24,2176]{1,0:T(8,128)(2,1)S(1)} %pad_maximum_fusion.14), channel_id=1, source_target_pairs={{0,4},{2,6},{4,0},{6,2},{1,5},{3,7},{5,1},{7,3},{8,12},{10,14},{12... | collective-permute-start | bytes 313352 | tf_op jit(solution)/shard_map/ppermute | solution.py:33
  16.7 2.6 %copy-start = (bf16[2,384,4096]{2,1,0:T(8,128)(2,1)}, bf16[2,384,4096]{2,1,0:T(8,128)(2,1)S(1)}, u32[]{:S(2)}) copy-start(bf16[2,384,4096]{2,1,0:T(8,128)(2,1)S(1)} %get-tuple-element.22) | copy-start | bytes 18874372
  19.3 4.5 %copy-start.1 = (bf16[2,4096,768]{2,1,0:T(8,128)(2,1)}, bf16[2,4096,768]{2,1,0:T(8,128)(2,1)S(1)}, u32[]{:S(2)}) copy-start(bf16[2,4096,768]{2,1,0:T(8,128)(2,1)S(1)} %get-tuple-element.18) | copy-start | bytes 37748740
  23.9 3.4 %collective-permute-start.4 = (bf16[96,2048]{1,0:T(8,128)(2,1)S(1)}, bf16[96,2048]{1,0:T(8,128)(2,1)S(1)}, u32[]{:S(2)}, u32[]{:S(2)}) collective-permute-start(bf16[96,2048]{1,0:T(8,128)(2,1)S(1)} %slice.289), channel_id=1, source_target_pairs={{0,1},{1,0},{2,3},{3,2},{4,5},{5,4},{6,7},{7,6},{8,9},{9,8},{10,11... | collective-permute-start | bytes 1179656 | tf_op jit(solution)/shard_map/ppermute | solution.py:33
  24.1 12.9 %collective-permute-start.6 = (bf16[96,2176]{1,0:T(8,128)(2,1)S(1)}, bf16[96,2176]{1,0:T(8,128)(2,1)S(1)}, u32[]{:S(2)}, u32[]{:S(2)}) collective-permute-start(bf16[96,2176]{1,0:T(8,128)(2,1)S(1)} %pad_maximum_fusion.9), channel_id=1, source_target_pairs={{0,8},{8,0},{16,24},{24,16},{1,9},{9,1},{17,25},{25,17},{2,10},{10... | collective-permute-start | bytes 1253384 | tf_op jit(solution)/shard_map/ppermute | solution.py:33
  25.6 11.7 %collective-permute-start.7 = (bf16[96,2176]{1,0:T(8,128)(2,1)S(1)}, bf16[96,2176]{1,0:T(8,128)(2,1)S(1)}, u32[]{:S(2)}, u32[]{:S(2)}) collective-permute-start(bf16[96,2176]{1,0:T(8,128)(2,1)S(1)} %pad_maximum_fusion.9), channel_id=1, source_target_pairs={{0,16},{8,24},{16,0},{24,8},{1,17},{9,25},{17,1},{25,9},{2,18},{10... | collective-permute-start | bytes 1253384 | tf_op jit(solution)/shard_map/ppermute | solution.py:33
  27.4 8.3 %slice-start = ((s8[6291456]{0:T(1024)(128)(4,1)}), s8[4194304]{0:T(1024)(128)(4,1)S(1)}, s32[]{:S(2)}) async-start(s8[6291456]{0:T(1024)(128)(4,1)} %bitcast.18), calls=%async_computation | async-start | bytes 8388608
  31.4 4.2 %slice-start.1 = ((s8[6291456]{0:T(1024)(128)(4,1)}), s8[2097152]{0:T(1024)(128)(4,1)S(1)}, s32[]{:S(2)}) async-start(s8[6291456]{0:T(1024)(128)(4,1)} %bitcast.18), calls=%async_computation.1 | async-start | bytes 4194304
  35.5 4.8 %slice-start.4 = ((s8[12582912]{0:T(1024)(128)(4,1)}), s8[4194304]{0:T(1024)(128)(4,1)S(1)}, s32[]{:S(2)}) async-start(s8[12582912]{0:T(1024)(128)(4,1)} %bitcast.25), calls=%async_computation.4 | async-start | bytes 8388608
  35.7 4.7 %slice-start.5 = ((s8[12582912]{0:T(1024)(128)(4,1)}), s8[4194304]{0:T(1024)(128)(4,1)S(1)}, s32[]{:S(2)}) async-start(s8[12582912]{0:T(1024)(128)(4,1)} %bitcast.25), calls=%async_computation.5 | async-start | bytes 8388608
  36.9 3.1 %collective-permute-start.5 = (bf16[96,2048]{1,0:T(8,128)(2,1)S(1)}, bf16[96,2048]{1,0:T(8,128)(2,1)S(1)}, u32[]{:S(2)}, u32[]{:S(2)}) collective-permute-start(bf16[96,2048]{1,0:T(8,128)(2,1)S(1)} %broadcast_select_fusion.6), channel_id=1, source_target_pairs={{0,1},{1,0},{2,3},{3,2},{4,5},{5,4},{6,7},{7,6},{8,9},{9,8},{10,11... | collective-permute-start | bytes 1179656 | tf_op jit(solution)/shard_map/ppermute | solution.py:33
  37.0 5.0 %copy-start.3 = (bf16[96,2176]{1,0:T(8,128)(2,1)}, bf16[96,2176]{1,0:T(8,128)(2,1)S(1)}, u32[]{:S(2)}) copy-start(bf16[96,2176]{1,0:T(8,128)(2,1)S(1)} %collective-permute-done.6) | copy-start | bytes 1253380
  37.3 4.7 %copy-start.2 = (bf16[96,2176]{1,0:T(8,128)(2,1)}, bf16[96,2176]{1,0:T(8,128)(2,1)S(1)}, u32[]{:S(2)}) copy-start(bf16[96,2176]{1,0:T(8,128)(2,1)S(1)} %collective-permute-done.7) | copy-start | bytes 1253380
  37.4 3.2 %slice-start.6 = ((s8[12582912]{0:T(1024)(128)(4,1)}), s8[4194304]{0:T(1024)(128)(4,1)S(1)}, s32[]{:S(2)}) async-start(s8[12582912]{0:T(1024)(128)(4,1)} %bitcast.25), calls=%async_computation.6 | async-start | bytes 8388608
  37.5 2.7 %collective-permute-start.8 = (bf16[192,2048]{1,0:T(8,128)(2,1)S(1)}, bf16[192,2048]{1,0:T(8,128)(2,1)S(1)}, u32[]{:S(2)}, u32[]{:S(2)}) collective-permute-start(bf16[192,2048]{1,0:T(8,128)(2,1)S(1)} %slice.301), channel_id=1, source_target_pairs={{0,1},{1,0},{2,3},{3,2},{4,5},{5,4},{6,7},{7,6},{8,9},{9,8},{10,11... | collective-permute-start | bytes 2359304 | tf_op jit(solution)/shard_map/ppermute | solution.py:33
  37.8 7.2 %collective-permute-start.10 = (bf16[96,1024]{1,0:T(8,128)(2,1)S(1)}, bf16[96,1024]{1,0:T(8,128)(2,1)S(1)}, u32[]{:S(2)}, u32[]{:S(2)}) collective-permute-start(bf16[96,1024]{1,0:T(8,128)(2,1)S(1)} %slice.248), channel_id=1, source_target_pairs={{0,16},{8,24},{16,0},{24,8},{1,17},{9,25},{17,1},{25,9},{2,18},{10... | collective-permute-start | bytes 589832 | tf_op jit(solution)/shard_map/ppermute | solution.py:33
  39.2 7.5 %collective-permute-start.11 = (bf16[96,1152]{1,0:T(8,128)(2,1)S(1)}, bf16[96,1152]{1,0:T(8,128)(2,1)S(1)}, u32[]{:S(2)}, u32[]{:S(2)}) collective-permute-start(bf16[96,1152]{1,0:T(8,128)(2,1)S(1)} %slice.249), channel_id=1, source_target_pairs={{0,8},{8,0},{16,24},{24,16},{1,9},{9,1},{17,25},{25,17},{2,10},{10... | collective-permute-start | bytes 663560 | tf_op jit(solution)/shard_map/ppermute | solution.py:33
  43.6 3.2 %slice-start.7 = ((bf16[96,2176]{1,0:T(8,128)(2,1)}), bf16[96,128]{1,0:T(8,128)(2,1)S(1)}, s32[]{:S(2)}) async-start(bf16[96,2176]{1,0:T(8,128)(2,1)} %copy-done.2), calls=%async_computation.7 | async-start | bytes 49152 | tf_op jit(solution)/shard_map/slice | solution.py:225
  43.6 3.2 %slice-start.8 = ((bf16[96,2176]{1,0:T(8,128)(2,1)}), bf16[96,128]{1,0:T(8,128)(2,1)S(1)}, s32[]{:S(2)}) async-start(bf16[96,2176]{1,0:T(8,128)(2,1)} %copy-done.3), calls=%async_computation.8 | async-start | bytes 49152 | tf_op jit(solution)/shard_map/slice | solution.py:225
  46.8 1.8 %collective-permute-start.12 = (bf16[96,2048]{1,0:T(8,128)(2,1)S(1)}, bf16[96,2048]{1,0:T(8,128)(2,1)S(1)}, u32[]{:S(2)}, u32[]{:S(2)}) collective-permute-start(bf16[96,2048]{1,0:T(8,128)(2,1)S(1)} %pad_maximum_fusion.10), channel_id=1, source_target_pairs={{0,1},{1,0},{2,3},{3,2},{4,5},{5,4},{6,7},{7,6},{8,9},{9,8},{10,11... | collective-permute-start | bytes 1179656 | tf_op jit(solution)/shard_map/ppermute | solution.py:33
  48.6 8.3 %slice-start.2 = ((s8[6291456]{0:T(1024)(128)(4,1)}), s8[4194304]{0:T(1024)(128)(4,1)S(1)}, s32[]{:S(2)}) async-start(s8[6291456]{0:T(1024)(128)(4,1)} %bitcast.22), calls=%async_computation.2 | async-start | bytes 8388608
  52.7 4.3 %slice-start.3 = ((s8[6291456]{0:T(1024)(128)(4,1)}), s8[2097152]{0:T(1024)(128)(4,1)S(1)}, s32[]{:S(2)}) async-start(s8[6291456]{0:T(1024)(128)(4,1)} %bitcast.22), calls=%async_computation.3 | async-start | bytes 4194304
  58.2 1.8 %collective-permute-start.13 = (bf16[96,2048]{1,0:T(8,128)(2,1)S(1)}, bf16[96,2048]{1,0:T(8,128)(2,1)S(1)}, u32[]{:S(2)}, u32[]{:S(2)}) collective-permute-start(bf16[96,2048]{1,0:T(8,128)(2,1)S(1)} %broadcast_select_fusion.3), channel_id=1, source_target_pairs={{0,1},{1,0},{2,3},{3,2},{4,5},{5,4},{6,7},{7,6},{8,9},{9,8},{10,11... | collective-permute-start | bytes 1179656 | tf_op jit(solution)/shard_map/ppermute | solution.py:33
  58.5 2.8 %collective-permute-start.9 = (bf16[192,2048]{1,0:T(8,128)(2,1)S(1)}, bf16[192,2048]{1,0:T(8,128)(2,1)S(1)}, u32[]{:S(2)}, u32[]{:S(2)}) collective-permute-start(bf16[192,2048]{1,0:T(8,128)(2,1)S(1)} %broadcast_select_fusion), channel_id=1, source_target_pairs={{0,1},{1,0},{2,3},{3,2},{4,5},{5,4},{6,7},{7,6},{8,9},{9,8},{10,11... | collective-permute-start | bytes 2359304 | tf_op jit(solution)/shard_map/ppermute | solution.py:33
  60.2 7.0 %collective-permute-start.14 = (bf16[96,1024]{1,0:T(8,128)(2,1)S(1)}, bf16[96,1024]{1,0:T(8,128)(2,1)S(1)}, u32[]{:S(2)}, u32[]{:S(2)}) collective-permute-start(bf16[96,1024]{1,0:T(8,128)(2,1)S(1)} %get-tuple-element.50), channel_id=1, source_target_pairs={{0,16},{8,24},{16,0},{24,8},{1,17},{9,25},{17,1},{25,9},{2,18},{10... | collective-permute-start | bytes 589832 | tf_op jit(solution)/shard_map/ppermute | solution.py:33
  60.8 6.7 %collective-permute-start.15 = (bf16[96,1024]{1,0:T(8,128)(2,1)S(1)}, bf16[96,1024]{1,0:T(8,128)(2,1)S(1)}, u32[]{:S(2)}, u32[]{:S(2)}) collective-permute-start(bf16[96,1024]{1,0:T(8,128)(2,1)S(1)} %get-tuple-element.51), channel_id=1, source_target_pairs={{0,8},{8,0},{16,24},{24,16},{1,9},{9,1},{17,25},{25,17},{2,10},{10... | collective-permute-start | bytes 589832 | tf_op jit(solution)/shard_map/ppermute | solution.py:33
  67.6 6.0 %collective-permute-start.17 = (bf16[48,2048]{1,0:T(8,128)(2,1)S(1)}, bf16[48,2048]{1,0:T(8,128)(2,1)S(1)}, u32[]{:S(2)}, u32[]{:S(2)}) collective-permute-start(bf16[48,2048]{1,0:T(8,128)(2,1)S(1)} %get-tuple-element.47), channel_id=1, source_target_pairs={{0,16},{8,24},{16,0},{24,8},{1,17},{9,25},{17,1},{25,9},{2,18},{10... | collective-permute-start | bytes 589832 | tf_op jit(solution)/shard_map/ppermute | solution.py:33
  69.3 5.7 %collective-permute-start.16 = (bf16[48,2048]{1,0:T(8,128)(2,1)S(1)}, bf16[48,2048]{1,0:T(8,128)(2,1)S(1)}, u32[]{:S(2)}, u32[]{:S(2)}) collective-permute-start(bf16[48,2048]{1,0:T(8,128)(2,1)S(1)} %get-tuple-element.49), channel_id=1, source_target_pairs={{0,8},{8,0},{16,24},{24,16},{1,9},{9,1},{17,25},{25,17},{2,10},{10... | collective-permute-start | bytes 589832 | tf_op jit(solution)/shard_map/ppermute | solution.py:33
  75.1 5.7 %collective-permute-start.18 = (bf16[48,2048]{1,0:T(8,128)(2,1)S(1)}, bf16[48,2048]{1,0:T(8,128)(2,1)S(1)}, u32[]{:S(2)}, u32[]{:S(2)}) collective-permute-start(bf16[48,2048]{1,0:T(8,128)(2,1)S(1)} %get-tuple-element.28), channel_id=1, source_target_pairs={{0,8},{8,0},{16,24},{24,16},{1,9},{9,1},{17,25},{25,17},{2,10},{10... | collective-permute-start | bytes 589832 | tf_op jit(solution)/shard_map/ppermute | solution.py:33
  75.7 5.7 %collective-permute-start.19 = (bf16[48,2048]{1,0:T(8,128)(2,1)S(1)}, bf16[48,2048]{1,0:T(8,128)(2,1)S(1)}, u32[]{:S(2)}, u32[]{:S(2)}) collective-permute-start(bf16[48,2048]{1,0:T(8,128)(2,1)S(1)} %get-tuple-element.29), channel_id=1, source_target_pairs={{0,16},{8,24},{16,0},{24,8},{1,17},{9,25},{17,1},{25,9},{2,18},{10... | collective-permute-start | bytes 589832 | tf_op jit(solution)/shard_map/ppermute | solution.py:33
  76.2 7.5 %collective-permute-start.21 = (bf16[24,2048]{1,0:T(8,128)(2,1)S(1)}, bf16[24,2048]{1,0:T(8,128)(2,1)S(1)}, u32[]{:S(2)}, u32[]{:S(2)}) collective-permute-start(bf16[24,2048]{1,0:T(8,128)(2,1)S(1)} %get-tuple-element.52), channel_id=1, source_target_pairs={{0,4},{2,6},{4,0},{6,2},{1,5},{3,7},{5,1},{7,3},{8,12},{10,14},{12... | collective-permute-start | bytes 294920 | tf_op jit(solution)/shard_map/ppermute | solution.py:33
  79.1 6.6 %collective-permute-start.22 = (bf16[24,2048]{1,0:T(8,128)(2,1)S(1)}, bf16[24,2048]{1,0:T(8,128)(2,1)S(1)}, u32[]{:S(2)}, u32[]{:S(2)}) collective-permute-start(bf16[24,2048]{1,0:T(8,128)(2,1)S(1)} %get-tuple-element.53), channel_id=1, source_target_pairs={{0,6},{2,4},{4,2},{6,0},{1,7},{3,5},{5,3},{7,1},{8,14},{10,12},{12... | collective-permute-start | bytes 294920 | tf_op jit(solution)/shard_map/ppermute | solution.py:33
  81.4 5.2 %collective-permute-start.20 = (bf16[24,2048]{1,0:T(8,128)(2,1)S(1)}, bf16[24,2048]{1,0:T(8,128)(2,1)S(1)}, u32[]{:S(2)}, u32[]{:S(2)}) collective-permute-start(bf16[24,2048]{1,0:T(8,128)(2,1)S(1)} %slice.330), channel_id=1, source_target_pairs={{0,2},{2,0},{4,6},{6,4},{1,3},{3,1},{5,7},{7,5},{8,10},{10,8},{12,... | collective-permute-start | bytes 294920 | tf_op jit(solution)/shard_map/ppermute | solution.py:33
  86.7 1.3 %collective-permute-start.23 = (bf16[12,2048]{1,0:T(8,128)(2,1)S(1)}, bf16[12,2048]{1,0:T(8,128)(2,1)S(1)}, u32[]{:S(2)}, u32[]{:S(2)}) collective-permute-start(bf16[12,2048]{1,0:T(8,128)(2,1)S(1)} %broadcast_select_fusion.13), channel_id=1, source_target_pairs={{0,1},{1,0},{2,3},{3,2},{4,5},{5,4},{6,7},{7,6},{8,9},{9,8},{10,11... | collective-permute-start | bytes 147464 | tf_op jit(solution)/shard_map/ppermute | solution.py:33

commit v8 on v7

--- a/solution.py
+++ b/solution.py
@@ -90,30 +90,37 @@
     return total.astype(jnp.bfloat16)
 
 
-def load_kernel(up_ref, down_ref, up_out, down_out, sems):
+def load_kernel(up_ref, down_ref, rows_ref, up_out, down_out, rows_out, sems):
     copies = [
         pltpu.make_async_copy(up_ref, up_out, sems.at[0]),
         pltpu.make_async_copy(down_ref, down_out, sems.at[1]),
     ]
     for copy in copies:
         copy.start()
+    rows_out[...] = rows_ref[...]
     for copy in copies:
         copy.wait()
 
 
-def loaded(up, down):
+def loaded(up, down, rows):
     nbytes = up.nbytes + down.nbytes
     return pl.pallas_call(
         load_kernel,
-        in_specs=[pl.BlockSpec(memory_space=pl.ANY)] * 2,
-        out_specs=[pl.BlockSpec(memory_space=pltpu.VMEM)] * 2,
-        out_shape=[pltpu.VMEM(up.shape, up.dtype), pltpu.VMEM(down.shape, down.dtype)],
+        in_specs=[pl.BlockSpec(memory_space=pl.ANY)] * 2
+        + [pl.BlockSpec(memory_space=pltpu.VMEM)],
+        out_specs=[pl.BlockSpec(memory_space=pltpu.VMEM)] * 3,
+        out_shape=[
+            pltpu.VMEM(up.shape, up.dtype),
+            pltpu.VMEM(down.shape, down.dtype),
+            jax.ShapeDtypeStruct(rows.shape, rows.dtype),
+        ],
         scratch_shapes=[pltpu.SemaphoreType.DMA((2,))],
         compiler_params=pltpu.CompilerParams(vmem_limit_bytes=32 * 2**20),
         cost_estimate=pl.CostEstimate(flops=0, bytes_accessed=nbytes, transcendentals=0),
     )(
         pltpu.with_memory_space_constraint(up, pltpu.HBM),
         pltpu.with_memory_space_constraint(down, pltpu.HBM),
+        rows,
     )
 
 
@@ -191,8 +198,7 @@
         return [chip_sum[low:high] for low, high in zip(edges, edges[1:])]
 
     chip_blocks = [chip_rows] + [swap(chip_rows, "chip", j) for j in range(1, chips)]
-    in_weight, out_weight = loaded(*behind((in_weight, out_weight), chip_rows))
-    chip_blocks[1:] = behind(chip_blocks[1:], in_weight)
+    in_weight, out_weight, chip_blocks[0] = loaded(in_weight, out_weight, chip_rows)
     held = [row_major(jnp.concatenate(chip_blocks, 0))]
     held += spread_near(held[0])
     first_part = own_sums(held[:1])

time: 89 us -> 88.7 us (level)
  starting transfers between devices: 22.7 us -> 21.2 us
  waiting for transfers between devices: 20.6 us -> 21.9 us
    ppermute x24, starting transfers between devices: 22.7 us -> 21.2 us  [swap(): return row_major(lax.ppermute(row_major(value), axis, pairs))]
    ppermute x24, waiting for transfers between devices: 20.6 us -> 21.9 us  [swap(): return row_major(lax.ppermute(row_major(value), axis, pairs))]
    unnamed x27 -> x30, local copies, waits for them, and re-layouts: 8.97 us -> 9.01 us
  transfers between devices with their start and end apart: 24 -> 24, of which waited for: 15 -> 14; matrix products, arithmetic and copies ran while one was open for 19% -> 19% of each run, Pallas kernels for 7% -> 7%
where the time goes in v8:
time: 88.7 us; the launch traced here: 88.5 us
  matrix products  22.8 us (26%)
  waiting for transfers between devices  21.9 us (25%)
  starting transfers between devices  21.2 us (24%)
  local copies, waits for them, and re-layouts  9.47 us (11%)
  Pallas kernels  6.38 us (7%)
  other arithmetic  5.52 us (6%)
  between operations  1.25 us (1%)
    ppermute x24, waiting for transfers between devices, swap(): return row_major(lax.ppermute(row_major(value), axis, pairs))  21.9 us
    ppermute x24, starting transfers between devices, swap(): return row_major(lax.ppermute(row_major(value), axis, pairs))  21.2 us
    dot_general x6, matrix products, own_sums(): jnp.dot(held_tokens, in_weight[s], preferred_element_type=jnp.float32)  19 us
    unnamed x30, local copies, waits for them, and re-layouts  9.01 us
    pallas_call x1, Pallas kernels, loaded(): pl.pallas_call(load_kernel, in_specs=[pl.BlockSpec(memory_space=pl.ANY)]...  6.38 us
    dot_general x3, matrix products, own_sums(): jnp.dot(jnp.concatenate(hidden, 1), out_weight.reshape(per_device * half_...  3.76 us
  transfers between devices with their start and end apart: 24, of which 14 were waited for; matrix products, arithmetic and copies ran while one was open for 19% of the time, Pallas kernels for 7%

profile of v8, /device:TPU:0, one launch (start us, length us, event | category | flops | bytes accessed | tf_op | source)
XLA Modules:
  0.0 88.5 jit_solution(7578881180652320152)
XLA Ops:
  0.6 0.8 copy.14
  1.4 0.8 copy.15
  2.2 0.9 broadcast_select_fusion.16
  3.2 0.5 collective-permute-start
  3.7 0.9 %collective-permute-done = bf16[12,2176]{1,0:T(8,128)(2,1)S(1)} collective-permute-done((bf16[12,2176]{1,0:T(8,128)(2,1)S(1)}, bf16[12,2176]{1,0:T(8,128)(2,1)S(1)}, u32[]{:S(2)}, u32[]{:S(2)}) %collective-permute-start) | collective-permute-done | bytes 52256 | tf_op jit(solution)/shard_map/ppermute | solution.py:33
  4.7 4.0 %collective-permute-start.2 = (bf16[24,2176]{1,0:T(8,128)(2,1)S(1)}, bf16[24,2176]{1,0:T(8,128)(2,1)S(1)}, u32[]{:S(2)}, u32[]{:S(2)}) collective-permute-start(bf16[24,2176]{1,0:T(8,128)(2,1)S(1)} %pad_maximum_fusion.13.rows_ref), channel_id=1, source_target_pairs={{0,4},{2,6},{4,0},{6,2},{1,5},{3,7},{5,1},{7,3},{8,12},{10,14},{12... | collective-permute-start | bytes 313352 | tf_op jit(solution)/shard_map/ppermute | solution.py:33
  8.7 1.6 %collective-permute-start.1 = (bf16[24,2176]{1,0:T(8,128)(2,1)S(1)}, bf16[24,2176]{1,0:T(8,128)(2,1)S(1)}, u32[]{:S(2)}, u32[]{:S(2)}) collective-permute-start(bf16[24,2176]{1,0:T(8,128)(2,1)S(1)} %pad_maximum_fusion.13.rows_ref), channel_id=1, source_target_pairs={{0,2},{2,0},{4,6},{6,4},{1,3},{3,1},{5,7},{7,5},{8,10},{10,8},{12,... | collective-permute-start | bytes 313352 | tf_op jit(solution)/shard_map/ppermute | solution.py:33
  10.3 6.4 %shard_map.77 = (bf16[2,4096,768]{2,1,0:T(8,128)(2,1)S(1)}, bf16[2,384,4096]{2,1,0:T(8,128)(2,1)S(1)}, bf16[24,2176]{1,0:T(8,128)(2,1)S(1)}) custom-call(bf16[2,4096,768]{2,1,0:T(8,128)(2,1)} %up_ref.1, bf16[2,384,4096]{2,1,0:T(8,128)(2,1)} %down_ref.1, bf16[24,2176]{1,0:T(8,128)(2,1)S(1)} %pad_maximum_fusion.13.rows_ref), custom_call_target="tpu_custom_call" | custom-call | bytes 18874368 | tf_op jit(solution)/shard_map/pallas_call | solution.py:107
  16.7 2.6 %copy-done = bf16[2,384,4096]{2,1,0:T(8,128)(2,1)} copy-done((bf16[2,384,4096]{2,1,0:T(8,128)(2,1)}, bf16[2,384,4096]{2,1,0:T(8,128)(2,1)S(1)}, u32[]{:S(2)}) %copy-start) | copy-done | bytes 6291480
  19.3 4.5 %copy-done.1 = bf16[2,4096,768]{2,1,0:T(8,128)(2,1)} copy-done((bf16[2,4096,768]{2,1,0:T(8,128)(2,1)}, bf16[2,4096,768]{2,1,0:T(8,128)(2,1)S(1)}, u32[]{:S(2)}) %copy-start.1) | copy-done | bytes 12582936
  24.1 1.7 %collective-permute-start.6 = (bf16[96,2176]{1,0:T(8,128)(2,1)S(1)}, bf16[96,2176]{1,0:T(8,128)(2,1)S(1)}, u32[]{:S(2)}, u32[]{:S(2)}) collective-permute-start(bf16[96,2176]{1,0:T(8,128)(2,1)S(1)} %constant_dynamic-update-slice_fusion), channel_id=1, source_target_pairs={{0,8},{8,0},{16,24},{24,16},{1,9},{9,1},{17,25},{25,17},{2,10},{10... | collective-permute-start | bytes 1253384 | tf_op jit(solution)/shard_map/ppermute | solution.py:33
  25.8 1.5 %collective-permute-start.7 = (bf16[96,2176]{1,0:T(8,128)(2,1)S(1)}, bf16[96,2176]{1,0:T(8,128)(2,1)S(1)}, u32[]{:S(2)}, u32[]{:S(2)}) collective-permute-start(bf16[96,2176]{1,0:T(8,128)(2,1)S(1)} %constant_dynamic-update-slice_fusion), channel_id=1, source_target_pairs={{0,16},{8,24},{16,0},{24,8},{1,17},{9,25},{17,1},{25,9},{2,18},{10... | collective-permute-start | bytes 1253384 | tf_op jit(solution)/shard_map/ppermute | solution.py:33
  27.6 4.1 %fusion.10 = f32[96,768]{1,0:T(8,128)S(1)} fusion(bf16[2,4096,768]{2,1,0:T(8,128)(2,1)} %copy-done.1, bf16[96,2048]{1,0:T(8,128)(2,1)S(1)} %get-tuple-element.31, bf16[96,2048]{1,0:T(8,128)(2,1)S(1)} %get-tuple-element.30), kind=kOutput, calls=%fused_computation.10 | convolution fusion | flops 605552640 | bytes 7372800 | tf_op jit(solution)/shard_map/dot_general | solution.py:180
  31.7 4.1 %fusion.4 = f32[96,768]{1,0:T(8,128)S(1)} fusion(bf16[2,4096,768]{2,1,0:T(8,128)(2,1)} %copy-done.1, bf16[96,2048]{1,0:T(8,128)(2,1)S(1)} %get-tuple-element.31, bf16[96,2048]{1,0:T(8,128)(2,1)S(1)} %get-tuple-element.30), kind=kOutput, calls=%fused_computation.4 | convolution fusion | flops 605552640 | bytes 7372800 | tf_op jit(solution)/shard_map/dot_general | solution.py:180
  35.9 1.2 %convolution_convert_fusion.2 = bf16[96,4096]{1,0:T(8,128)(2,1)S(1)} fusion(bf16[768,4096]{1,0:T(8,128)(2,1)S(1)} %bitcast.20, bf16[96,384]{1,0:T(8,128)(2,1)S(1)} %get-tuple-element.55, bf16[96,384]{1,0:T(8,128)(2,1)S(1)} %get-tuple-element.56), kind=kOutput, calls=%fused_computation.20 | convolution fusion | flops 604667904 | bytes 7225344 | tf_op jit(solution)/shard_map/dot_general | solution.py:183
  37.3 0.3 collective-permute-done.7
  38.1 1.4 %collective-permute-start.10 = (bf16[96,1024]{1,0:T(8,128)(2,1)S(1)}, bf16[96,1024]{1,0:T(8,128)(2,1)S(1)}, u32[]{:S(2)}, u32[]{:S(2)}) collective-permute-start(bf16[96,1024]{1,0:T(8,128)(2,1)S(1)} %slice.248), channel_id=1, source_target_pairs={{0,16},{8,24},{16,0},{24,8},{1,17},{9,25},{17,1},{25,9},{2,18},{10... | collective-permute-start | bytes 589832 | tf_op jit(solution)/shard_map/ppermute | solution.py:33
  39.5 0.5 collective-permute-start.11
  40.9 1.4 %fusion.8 = f32[192,768]{1,0:T(8,128)S(1)} fusion(bf16[2,4096,768]{2,1,0:T(8,128)(2,1)S(1)} %bitcast.26, bf16[192,2048]{1,0:T(8,128)(2,1)S(1)} %get-tuple-element.29, bf16[192,2048]{1,0:T(8,128)(2,1)S(1)} %get-tuple-element.28), kind=kOutput, calls=%fused_computation.8 | convolution fusion | flops 1211105280 | bytes 8454144 | tf_op jit(solution)/shard_map/dot_general | solution.py:180
  42.3 1.4 %fusion.2 = f32[192,768]{1,0:T(8,128)S(1)} fusion(bf16[2,4096,768]{2,1,0:T(8,128)(2,1)S(1)} %bitcast.26, bf16[192,2048]{1,0:T(8,128)(2,1)S(1)} %get-tuple-element.29, bf16[192,2048]{1,0:T(8,128)(2,1)S(1)} %get-tuple-element.28), kind=kOutput, calls=%fused_computation.2 | convolution fusion | flops 1211105280 | bytes 8454144 | tf_op jit(solution)/shard_map/dot_general | solution.py:180
  43.9 1.4 %convolution_convert_fusion = bf16[192,4096]{1,0:T(8,128)(2,1)S(1)} fusion(bf16[768,4096]{1,0:T(8,128)(2,1)S(1)} %bitcast.21, bf16[192,384]{1,0:T(8,128)(2,1)S(1)} %fusion.19, bf16[192,384]{1,0:T(8,128)(2,1)S(1)} %fusion.21), kind=kOutput, calls=%fused_computation.12 | convolution fusion | flops 1209335808 | bytes 8159232 | tf_op jit(solution)/shard_map/dot_general | solution.py:183
  45.3 1.7 %collective-permute-done.11 = bf16[96,1152]{1,0:T(8,128)(2,1)S(1)} collective-permute-done((bf16[96,1152]{1,0:T(8,128)(2,1)S(1)}, bf16[96,1152]{1,0:T(8,128)(2,1)S(1)}, u32[]{:S(2)}, u32[]{:S(2)}) %collective-permute-start.11) | collective-permute-done | bytes 221216 | tf_op jit(solution)/shard_map/ppermute | solution.py:33
  47.7 1.1 %collective-permute-done.12 = bf16[96,2048]{1,0:T(8,128)(2,1)S(1)} collective-permute-done((bf16[96,2048]{1,0:T(8,128)(2,1)S(1)}, bf16[96,2048]{1,0:T(8,128)(2,1)S(1)}, u32[]{:S(2)}, u32[]{:S(2)}) %collective-permute-start.12) | collective-permute-done | bytes 393248 | tf_op jit(solution)/shard_map/ppermute | solution.py:33
  48.9 4.1 %fusion.6 = f32[96,768]{1,0:T(8,128)S(1)} fusion(bf16[2,4096,768]{2,1,0:T(8,128)(2,1)} %copy-done.1, bf16[96,2048]{1,0:T(8,128)(2,1)S(1)} %get-tuple-element.37, bf16[96,2048]{1,0:T(8,128)(2,1)S(1)} %get-tuple-element.36), kind=kOutput, calls=%fused_computation.6 | convolution fusion | flops 605552640 | bytes 7372800 | tf_op jit(solution)/shard_map/dot_general | solution.py:180
  53.0 4.1 %fusion = f32[96,768]{1,0:T(8,128)S(1)} fusion(bf16[2,4096,768]{2,1,0:T(8,128)(2,1)} %copy-done.1, bf16[96,2048]{1,0:T(8,128)(2,1)S(1)} %get-tuple-element.37, bf16[96,2048]{1,0:T(8,128)(2,1)S(1)} %get-tuple-element.36), kind=kOutput, calls=%fused_computation | convolution fusion | flops 605552640 | bytes 7372800 | tf_op jit(solution)/shard_map/dot_general | solution.py:180
  57.3 1.2 %convolution_convert_fusion.1 = bf16[96,4096]{1,0:T(8,128)(2,1)S(1)} fusion(bf16[768,4096]{1,0:T(8,128)(2,1)S(1)} %bitcast.24, bf16[96,384]{1,0:T(8,128)(2,1)S(1)} %fusion.28, bf16[96,384]{1,0:T(8,128)(2,1)S(1)} %fusion.30), kind=kOutput, calls=%fused_computation.19 | convolution fusion | flops 604667904 | bytes 7225344 | tf_op jit(solution)/shard_map/dot_general | solution.py:183
  58.8 0.4 collective-permute-start.9
  59.4 0.9 %collective-permute-done.13 = bf16[96,2048]{1,0:T(8,128)(2,1)S(1)} collective-permute-done((bf16[96,2048]{1,0:T(8,128)(2,1)S(1)}, bf16[96,2048]{1,0:T(8,128)(2,1)S(1)}, u32[]{:S(2)}, u32[]{:S(2)}) %collective-permute-start.13) | collective-permute-done | bytes 393248 | tf_op jit(solution)/shard_map/ppermute | solution.py:33
  60.5 0.6 collective-permute-start.14
  61.1 0.4 collective-permute-start.15
  61.4 0.4 add_convert_fusion
  61.9 5.6 %collective-permute-done.14 = bf16[96,1024]{1,0:T(8,128)(2,1)S(1)} collective-permute-done((bf16[96,1024]{1,0:T(8,128)(2,1)S(1)}, bf16[96,1024]{1,0:T(8,128)(2,1)S(1)}, u32[]{:S(2)}, u32[]{:S(2)}) %collective-permute-start.14) | collective-permute-done | bytes 196640 | tf_op jit(solution)/shard_map/ppermute | solution.py:33
  67.9 1.6 %collective-permute-start.17 = (bf16[48,2048]{1,0:T(8,128)(2,1)S(1)}, bf16[48,2048]{1,0:T(8,128)(2,1)S(1)}, u32[]{:S(2)}, u32[]{:S(2)}) collective-permute-start(bf16[48,2048]{1,0:T(8,128)(2,1)S(1)} %get-tuple-element.39), channel_id=1, source_target_pairs={{0,16},{8,24},{16,0},{24,8},{1,17},{9,25},{17,1},{25,9},{2,18},{10... | collective-permute-start | bytes 589832 | tf_op jit(solution)/shard_map/ppermute | solution.py:33
  69.5 0.6 collective-permute-start.16
  70.1 3.7 %collective-permute-done.17 = bf16[48,2048]{1,0:T(8,128)(2,1)S(1)} collective-permute-done((bf16[48,2048]{1,0:T(8,128)(2,1)S(1)}, bf16[48,2048]{1,0:T(8,128)(2,1)S(1)}, u32[]{:S(2)}, u32[]{:S(2)}) %collective-permute-start.17) | collective-permute-done | bytes 196640 | tf_op jit(solution)/shard_map/ppermute | solution.py:33
  73.9 1.4 %collective-permute-done.16 = bf16[48,2048]{1,0:T(8,128)(2,1)S(1)} collective-permute-done((bf16[48,2048]{1,0:T(8,128)(2,1)S(1)}, bf16[48,2048]{1,0:T(8,128)(2,1)S(1)}, u32[]{:S(2)}, u32[]{:S(2)}) %collective-permute-start.16) | collective-permute-done | bytes 196640 | tf_op jit(solution)/shard_map/ppermute | solution.py:33
  75.3 0.6 collective-permute-start.18
  75.9 0.4 collective-permute-start.19
  76.4 1.8 %collective-permute-start.21 = (bf16[24,2048]{1,0:T(8,128)(2,1)S(1)}, bf16[24,2048]{1,0:T(8,128)(2,1)S(1)}, u32[]{:S(2)}, u32[]{:S(2)}) collective-permute-start(bf16[24,2048]{1,0:T(8,128)(2,1)S(1)} %get-tuple-element.44), channel_id=1, source_target_pairs={{0,4},{2,6},{4,0},{6,2},{1,5},{3,7},{5,1},{7,3},{8,12},{10,14},{12... | collective-permute-start | bytes 294920 | tf_op jit(solution)/shard_map/ppermute | solution.py:33
  78.2 2.0 %collective-permute-start.22 = (bf16[24,2048]{1,0:T(8,128)(2,1)S(1)}, bf16[24,2048]{1,0:T(8,128)(2,1)S(1)}, u32[]{:S(2)}, u32[]{:S(2)}) collective-permute-start(bf16[24,2048]{1,0:T(8,128)(2,1)S(1)} %get-tuple-element.45), channel_id=1, source_target_pairs={{0,6},{2,4},{4,2},{6,0},{1,7},{3,5},{5,3},{7,1},{8,14},{10,12},{12... | collective-permute-start | bytes 294920 | tf_op jit(solution)/shard_map/ppermute | solution.py:33
  80.2 0.9 collective-permute-done.18
  81.1 0.5 collective-permute-done.19
  81.7 0.7 collective-permute-start.20
  82.6 2.4 %collective-permute-done.21 = bf16[24,2048]{1,0:T(8,128)(2,1)S(1)} collective-permute-done((bf16[24,2048]{1,0:T(8,128)(2,1)S(1)}, bf16[24,2048]{1,0:T(8,128)(2,1)S(1)}, u32[]{:S(2)}, u32[]{:S(2)}) %collective-permute-start.21) | collective-permute-done | bytes 98336 | tf_op jit(solution)/shard_map/ppermute | solution.py:33
  85.0 1.4 %collective-permute-done.20 = bf16[24,2048]{1,0:T(8,128)(2,1)S(1)} collective-permute-done((bf16[24,2048]{1,0:T(8,128)(2,1)S(1)}, bf16[24,2048]{1,0:T(8,128)(2,1)S(1)}, u32[]{:S(2)}, u32[]{:S(2)}) %collective-permute-start.20) | collective-permute-done | bytes 98336 | tf_op jit(solution)/shard_map/ppermute | solution.py:33
  86.5 0.5 broadcast_multiply_fusion
  87.1 0.7 collective-permute-done.23
  87.8 0.7 pad_maximum_fusion.12
  (106 shorter events, 4.9 us)
Async XLA Ops:
  3.2 1.4 %collective-permute-start = (bf16[12,2176]{1,0:T(8,128)(2,1)S(1)}, bf16[12,2176]{1,0:T(8,128)(2,1)S(1)}, u32[]{:S(2)}, u32[]{:S(2)}) collective-permute-start(bf16[12,2176]{1,0:T(8,128)(2,1)S(1)} %pad_maximum_fusion.15), channel_id=1, source_target_pairs={{0,1},{1,0},{2,3},{3,2},{4,5},{5,4},{6,7},{7,6},{8,9},{9,8},{10,11... | collective-permute-start | bytes 156680 | tf_op jit(solution)/shard_map/ppermute | solution.py:33
  4.7 19.3 %copy-start.4 = (s32[8]{0:T(128)S(1)}, s32[8]{0:T(128)}, u32[]{:S(2)}) copy-start(s32[8]{0:T(128)} %param.11) | copy-start | bytes 100
  4.7 19.1 %collective-permute-start.2 = (bf16[24,2176]{1,0:T(8,128)(2,1)S(1)}, bf16[24,2176]{1,0:T(8,128)(2,1)S(1)}, u32[]{:S(2)}, u32[]{:S(2)}) collective-permute-start(bf16[24,2176]{1,0:T(8,128)(2,1)S(1)} %pad_maximum_fusion.13.rows_ref), channel_id=1, source_target_pairs={{0,4},{2,6},{4,0},{6,2},{1,5},{3,7},{5,1},{7,3},{8,12},{10,14},{12... | collective-permute-start | bytes 313352 | tf_op jit(solution)/shard_map/ppermute | solution.py:33
  8.7 15.1 %collective-permute-start.1 = (bf16[24,2176]{1,0:T(8,128)(2,1)S(1)}, bf16[24,2176]{1,0:T(8,128)(2,1)S(1)}, u32[]{:S(2)}, u32[]{:S(2)}) collective-permute-start(bf16[24,2176]{1,0:T(8,128)(2,1)S(1)} %pad_maximum_fusion.13.rows_ref), channel_id=1, source_target_pairs={{0,2},{2,0},{4,6},{6,4},{1,3},{3,1},{5,7},{7,5},{8,10},{10,8},{12,... | collective-permute-start | bytes 313352 | tf_op jit(solution)/shard_map/ppermute | solution.py:33
  10.3 13.6 %collective-permute-start.3 = (bf16[24,2176]{1,0:T(8,128)(2,1)S(1)}, bf16[24,2176]{1,0:T(8,128)(2,1)S(1)}, u32[]{:S(2)}, u32[]{:S(2)}) collective-permute-start(bf16[24,2176]{1,0:T(8,128)(2,1)S(1)} %pad_maximum_fusion.13.rows_ref), channel_id=1, source_target_pairs={{0,6},{2,4},{4,2},{6,0},{1,7},{3,5},{5,3},{7,1},{8,14},{10,12},{12... | collective-permute-start | bytes 313352 | tf_op jit(solution)/shard_map/ppermute | solution.py:33
  16.7 2.6 %copy-start = (bf16[2,384,4096]{2,1,0:T(8,128)(2,1)}, bf16[2,384,4096]{2,1,0:T(8,128)(2,1)S(1)}, u32[]{:S(2)}) copy-start(bf16[2,384,4096]{2,1,0:T(8,128)(2,1)S(1)} %get-tuple-element.14) | copy-start | bytes 18874372
  19.3 4.5 %copy-start.1 = (bf16[2,4096,768]{2,1,0:T(8,128)(2,1)}, bf16[2,4096,768]{2,1,0:T(8,128)(2,1)S(1)}, u32[]{:S(2)}) copy-start(bf16[2,4096,768]{2,1,0:T(8,128)(2,1)S(1)} %get-tuple-element.13) | copy-start | bytes 37748740
  23.9 3.6 %collective-permute-start.4 = (bf16[96,2048]{1,0:T(8,128)(2,1)S(1)}, bf16[96,2048]{1,0:T(8,128)(2,1)S(1)}, u32[]{:S(2)}, u32[]{:S(2)}) collective-permute-start(bf16[96,2048]{1,0:T(8,128)(2,1)S(1)} %slice.289), channel_id=1, source_target_pairs={{0,1},{1,0},{2,3},{3,2},{4,5},{5,4},{6,7},{7,6},{8,9},{9,8},{10,11... | collective-permute-start | bytes 1179656 | tf_op jit(solution)/shard_map/ppermute | solution.py:33
  24.1 13.1 %collective-permute-start.6 = (bf16[96,2176]{1,0:T(8,128)(2,1)S(1)}, bf16[96,2176]{1,0:T(8,128)(2,1)S(1)}, u32[]{:S(2)}, u32[]{:S(2)}) collective-permute-start(bf16[96,2176]{1,0:T(8,128)(2,1)S(1)} %constant_dynamic-update-slice_fusion), channel_id=1, source_target_pairs={{0,8},{8,0},{16,24},{24,16},{1,9},{9,1},{17,25},{25,17},{2,10},{10... | collective-permute-start | bytes 1253384 | tf_op jit(solution)/shard_map/ppermute | solution.py:33
  25.8 11.7 %collective-permute-start.7 = (bf16[96,2176]{1,0:T(8,128)(2,1)S(1)}, bf16[96,2176]{1,0:T(8,128)(2,1)S(1)}, u32[]{:S(2)}, u32[]{:S(2)}) collective-permute-start(bf16[96,2176]{1,0:T(8,128)(2,1)S(1)} %constant_dynamic-update-slice_fusion), channel_id=1, source_target_pairs={{0,16},{8,24},{16,0},{24,8},{1,17},{9,25},{17,1},{25,9},{2,18},{10... | collective-permute-start | bytes 1253384 | tf_op jit(solution)/shard_map/ppermute | solution.py:33
  27.6 8.3 %slice-start = ((s8[6291456]{0:T(1024)(128)(4,1)}), s8[4194304]{0:T(1024)(128)(4,1)S(1)}, s32[]{:S(2)}) async-start(s8[6291456]{0:T(1024)(128)(4,1)} %bitcast.18), calls=%async_computation | async-start | bytes 8388608
  31.7 4.2 %slice-start.1 = ((s8[6291456]{0:T(1024)(128)(4,1)}), s8[2097152]{0:T(1024)(128)(4,1)S(1)}, s32[]{:S(2)}) async-start(s8[6291456]{0:T(1024)(128)(4,1)} %bitcast.18), calls=%async_computation.1 | async-start | bytes 4194304
  35.8 4.8 %slice-start.4 = ((s8[12582912]{0:T(1024)(128)(4,1)}), s8[4194304]{0:T(1024)(128)(4,1)S(1)}, s32[]{:S(2)}) async-start(s8[12582912]{0:T(1024)(128)(4,1)} %bitcast.25), calls=%async_computation.4 | async-start | bytes 8388608
  35.9 4.7 %slice-start.5 = ((s8[12582912]{0:T(1024)(128)(4,1)}), s8[4194304]{0:T(1024)(128)(4,1)S(1)}, s32[]{:S(2)}) async-start(s8[12582912]{0:T(1024)(128)(4,1)} %bitcast.25), calls=%async_computation.5 | async-start | bytes 8388608
  37.2 3.1 %collective-permute-start.5 = (bf16[96,2048]{1,0:T(8,128)(2,1)S(1)}, bf16[96,2048]{1,0:T(8,128)(2,1)S(1)}, u32[]{:S(2)}, u32[]{:S(2)}) collective-permute-start(bf16[96,2048]{1,0:T(8,128)(2,1)S(1)} %broadcast_select_fusion.6), channel_id=1, source_target_pairs={{0,1},{1,0},{2,3},{3,2},{4,5},{5,4},{6,7},{7,6},{8,9},{9,8},{10,11... | collective-permute-start | bytes 1179656 | tf_op jit(solution)/shard_map/ppermute | solution.py:33
  37.3 5.0 %copy-start.3 = (bf16[96,2176]{1,0:T(8,128)(2,1)}, bf16[96,2176]{1,0:T(8,128)(2,1)S(1)}, u32[]{:S(2)}) copy-start(bf16[96,2176]{1,0:T(8,128)(2,1)S(1)} %collective-permute-done.6) | copy-start | bytes 1253380
  37.6 4.7 %copy-start.2 = (bf16[96,2176]{1,0:T(8,128)(2,1)}, bf16[96,2176]{1,0:T(8,128)(2,1)S(1)}, u32[]{:S(2)}) copy-start(bf16[96,2176]{1,0:T(8,128)(2,1)S(1)} %collective-permute-done.7) | copy-start | bytes 1253380
  37.6 3.2 %slice-start.6 = ((s8[12582912]{0:T(1024)(128)(4,1)}), s8[4194304]{0:T(1024)(128)(4,1)S(1)}, s32[]{:S(2)}) async-start(s8[12582912]{0:T(1024)(128)(4,1)} %bitcast.25), calls=%async_computation.6 | async-start | bytes 8388608
  37.8 2.7 %collective-permute-start.8 = (bf16[192,2048]{1,0:T(8,128)(2,1)S(1)}, bf16[192,2048]{1,0:T(8,128)(2,1)S(1)}, u32[]{:S(2)}, u32[]{:S(2)}) collective-permute-start(bf16[192,2048]{1,0:T(8,128)(2,1)S(1)} %slice.301), channel_id=1, source_target_pairs={{0,1},{1,0},{2,3},{3,2},{4,5},{5,4},{6,7},{7,6},{8,9},{9,8},{10,11... | collective-permute-start | bytes 2359304 | tf_op jit(solution)/shard_map/ppermute | solution.py:33
  38.1 7.2 %collective-permute-start.10 = (bf16[96,1024]{1,0:T(8,128)(2,1)S(1)}, bf16[96,1024]{1,0:T(8,128)(2,1)S(1)}, u32[]{:S(2)}, u32[]{:S(2)}) collective-permute-start(bf16[96,1024]{1,0:T(8,128)(2,1)S(1)} %slice.248), channel_id=1, source_target_pairs={{0,16},{8,24},{16,0},{24,8},{1,17},{9,25},{17,1},{25,9},{2,18},{10... | collective-permute-start | bytes 589832 | tf_op jit(solution)/shard_map/ppermute | solution.py:33
  39.5 7.5 %collective-permute-start.11 = (bf16[96,1152]{1,0:T(8,128)(2,1)S(1)}, bf16[96,1152]{1,0:T(8,128)(2,1)S(1)}, u32[]{:S(2)}, u32[]{:S(2)}) collective-permute-start(bf16[96,1152]{1,0:T(8,128)(2,1)S(1)} %slice.249), channel_id=1, source_target_pairs={{0,8},{8,0},{16,24},{24,16},{1,9},{9,1},{17,25},{25,17},{2,10},{10... | collective-permute-start | bytes 663560 | tf_op jit(solution)/shard_map/ppermute | solution.py:33
  43.9 3.2 %slice-start.7 = ((bf16[96,2176]{1,0:T(8,128)(2,1)}), bf16[96,128]{1,0:T(8,128)(2,1)S(1)}, s32[]{:S(2)}) async-start(bf16[96,2176]{1,0:T(8,128)(2,1)} %copy-done.2), calls=%async_computation.7 | async-start | bytes 49152 | tf_op jit(solution)/shard_map/slice | solution.py:231
  43.9 3.2 %slice-start.8 = ((bf16[96,2176]{1,0:T(8,128)(2,1)}), bf16[96,128]{1,0:T(8,128)(2,1)S(1)}, s32[]{:S(2)}) async-start(bf16[96,2176]{1,0:T(8,128)(2,1)} %copy-done.3), calls=%async_computation.8 | async-start | bytes 49152 | tf_op jit(solution)/shard_map/slice | solution.py:231
  47.1 1.8 %collective-permute-start.12 = (bf16[96,2048]{1,0:T(8,128)(2,1)S(1)}, bf16[96,2048]{1,0:T(8,128)(2,1)S(1)}, u32[]{:S(2)}, u32[]{:S(2)}) collective-permute-start(bf16[96,2048]{1,0:T(8,128)(2,1)S(1)} %pad_maximum_fusion.9), channel_id=1, source_target_pairs={{0,1},{1,0},{2,3},{3,2},{4,5},{5,4},{6,7},{7,6},{8,9},{9,8},{10,11... | collective-permute-start | bytes 1179656 | tf_op jit(solution)/shard_map/ppermute | solution.py:33
  48.9 8.3 %slice-start.2 = ((s8[6291456]{0:T(1024)(128)(4,1)}), s8[4194304]{0:T(1024)(128)(4,1)S(1)}, s32[]{:S(2)}) async-start(s8[6291456]{0:T(1024)(128)(4,1)} %bitcast.22), calls=%async_computation.2 | async-start | bytes 8388608
  53.0 4.3 %slice-start.3 = ((s8[6291456]{0:T(1024)(128)(4,1)}), s8[2097152]{0:T(1024)(128)(4,1)S(1)}, s32[]{:S(2)}) async-start(s8[6291456]{0:T(1024)(128)(4,1)} %bitcast.22), calls=%async_computation.3 | async-start | bytes 4194304
  58.5 1.8 %collective-permute-start.13 = (bf16[96,2048]{1,0:T(8,128)(2,1)S(1)}, bf16[96,2048]{1,0:T(8,128)(2,1)S(1)}, u32[]{:S(2)}, u32[]{:S(2)}) collective-permute-start(bf16[96,2048]{1,0:T(8,128)(2,1)S(1)} %broadcast_select_fusion.3), channel_id=1, source_target_pairs={{0,1},{1,0},{2,3},{3,2},{4,5},{5,4},{6,7},{7,6},{8,9},{9,8},{10,11... | collective-permute-start | bytes 1179656 | tf_op jit(solution)/shard_map/ppermute | solution.py:33
  58.8 2.6 %collective-permute-start.9 = (bf16[192,2048]{1,0:T(8,128)(2,1)S(1)}, bf16[192,2048]{1,0:T(8,128)(2,1)S(1)}, u32[]{:S(2)}, u32[]{:S(2)}) collective-permute-start(bf16[192,2048]{1,0:T(8,128)(2,1)S(1)} %broadcast_select_fusion), channel_id=1, source_target_pairs={{0,1},{1,0},{2,3},{3,2},{4,5},{5,4},{6,7},{7,6},{8,9},{9,8},{10,11... | collective-permute-start | bytes 2359304 | tf_op jit(solution)/shard_map/ppermute | solution.py:33
  60.5 7.0 %collective-permute-start.14 = (bf16[96,1024]{1,0:T(8,128)(2,1)S(1)}, bf16[96,1024]{1,0:T(8,128)(2,1)S(1)}, u32[]{:S(2)}, u32[]{:S(2)}) collective-permute-start(bf16[96,1024]{1,0:T(8,128)(2,1)S(1)} %get-tuple-element.42), channel_id=1, source_target_pairs={{0,16},{8,24},{16,0},{24,8},{1,17},{9,25},{17,1},{25,9},{2,18},{10... | collective-permute-start | bytes 589832 | tf_op jit(solution)/shard_map/ppermute | solution.py:33
  61.1 6.7 %collective-permute-start.15 = (bf16[96,1024]{1,0:T(8,128)(2,1)S(1)}, bf16[96,1024]{1,0:T(8,128)(2,1)S(1)}, u32[]{:S(2)}, u32[]{:S(2)}) collective-permute-start(bf16[96,1024]{1,0:T(8,128)(2,1)S(1)} %get-tuple-element.43), channel_id=1, source_target_pairs={{0,8},{8,0},{16,24},{24,16},{1,9},{9,1},{17,25},{25,17},{2,10},{10... | collective-permute-start | bytes 589832 | tf_op jit(solution)/shard_map/ppermute | solution.py:33
  67.9 6.0 %collective-permute-start.17 = (bf16[48,2048]{1,0:T(8,128)(2,1)S(1)}, bf16[48,2048]{1,0:T(8,128)(2,1)S(1)}, u32[]{:S(2)}, u32[]{:S(2)}) collective-permute-start(bf16[48,2048]{1,0:T(8,128)(2,1)S(1)} %get-tuple-element.39), channel_id=1, source_target_pairs={{0,16},{8,24},{16,0},{24,8},{1,17},{9,25},{17,1},{25,9},{2,18},{10... | collective-permute-start | bytes 589832 | tf_op jit(solution)/shard_map/ppermute | solution.py:33
  69.5 5.7 %collective-permute-start.16 = (bf16[48,2048]{1,0:T(8,128)(2,1)S(1)}, bf16[48,2048]{1,0:T(8,128)(2,1)S(1)}, u32[]{:S(2)}, u32[]{:S(2)}) collective-permute-start(bf16[48,2048]{1,0:T(8,128)(2,1)S(1)} %get-tuple-element.41), channel_id=1, source_target_pairs={{0,8},{8,0},{16,24},{24,16},{1,9},{9,1},{17,25},{25,17},{2,10},{10... | collective-permute-start | bytes 589832 | tf_op jit(solution)/shard_map/ppermute | solution.py:33
  75.3 5.7 %collective-permute-start.18 = (bf16[48,2048]{1,0:T(8,128)(2,1)S(1)}, bf16[48,2048]{1,0:T(8,128)(2,1)S(1)}, u32[]{:S(2)}, u32[]{:S(2)}) collective-permute-start(bf16[48,2048]{1,0:T(8,128)(2,1)S(1)} %get-tuple-element.20), channel_id=1, source_target_pairs={{0,8},{8,0},{16,24},{24,16},{1,9},{9,1},{17,25},{25,17},{2,10},{10... | collective-permute-start | bytes 589832 | tf_op jit(solution)/shard_map/ppermute | solution.py:33
  75.9 5.7 %collective-permute-start.19 = (bf16[48,2048]{1,0:T(8,128)(2,1)S(1)}, bf16[48,2048]{1,0:T(8,128)(2,1)S(1)}, u32[]{:S(2)}, u32[]{:S(2)}) collective-permute-start(bf16[48,2048]{1,0:T(8,128)(2,1)S(1)} %get-tuple-element.21), channel_id=1, source_target_pairs={{0,16},{8,24},{16,0},{24,8},{1,17},{9,25},{17,1},{25,9},{2,18},{10... | collective-permute-start | bytes 589832 | tf_op jit(solution)/shard_map/ppermute | solution.py:33
  76.4 8.6 %collective-permute-start.21 = (bf16[24,2048]{1,0:T(8,128)(2,1)S(1)}, bf16[24,2048]{1,0:T(8,128)(2,1)S(1)}, u32[]{:S(2)}, u32[]{:S(2)}) collective-permute-start(bf16[24,2048]{1,0:T(8,128)(2,1)S(1)} %get-tuple-element.44), channel_id=1, source_target_pairs={{0,4},{2,6},{4,0},{6,2},{1,5},{3,7},{5,1},{7,3},{8,12},{10,14},{12... | collective-permute-start | bytes 294920 | tf_op jit(solution)/shard_map/ppermute | solution.py:33
  78.2 6.8 %collective-permute-start.22 = (bf16[24,2048]{1,0:T(8,128)(2,1)S(1)}, bf16[24,2048]{1,0:T(8,128)(2,1)S(1)}, u32[]{:S(2)}, u32[]{:S(2)}) collective-permute-start(bf16[24,2048]{1,0:T(8,128)(2,1)S(1)} %get-tuple-element.45), channel_id=1, source_target_pairs={{0,6},{2,4},{4,2},{6,0},{1,7},{3,5},{5,3},{7,1},{8,14},{10,12},{12... | collective-permute-start | bytes 294920 | tf_op jit(solution)/shard_map/ppermute | solution.py:33
  81.7 4.7 %collective-permute-start.20 = (bf16[24,2048]{1,0:T(8,128)(2,1)S(1)}, bf16[24,2048]{1,0:T(8,128)(2,1)S(1)}, u32[]{:S(2)}, u32[]{:S(2)}) collective-permute-start(bf16[24,2048]{1,0:T(8,128)(2,1)S(1)} %slice.330), channel_id=1, source_target_pairs={{0,2},{2,0},{4,6},{6,4},{1,3},{3,1},{5,7},{7,5},{8,10},{10,8},{12,... | collective-permute-start | bytes 294920 | tf_op jit(solution)/shard_map/ppermute | solution.py:33
  86.5 1.3 %collective-permute-start.23 = (bf16[12,2048]{1,0:T(8,128)(2,1)S(1)}, bf16[12,2048]{1,0:T(8,128)(2,1)S(1)}, u32[]{:S(2)}, u32[]{:S(2)}) collective-permute-start(bf16[12,2048]{1,0:T(8,128)(2,1)S(1)} %broadcast_select_fusion.13), channel_id=1, source_target_pairs={{0,1},{1,0},{2,3},{3,2},{4,5},{5,4},{6,7},{7,6},{8,9},{9,8},{10,11... | collective-permute-start | bytes 147464 | tf_op jit(solution)/shard_map/ppermute | solution.py:33

commit v9 on v6

--- a/solution.py
+++ b/solution.py
@@ -7,6 +7,10 @@
 from jax.sharding import Mesh, PartitionSpec as P
 
 LANES = 128
+TOP_LANES = 8
+CHUNK = 1024
+TILE = 512
+VMEM_LIMIT = 12 * 2**20
 GATE_MOST = 5
 
 
@@ -53,10 +57,6 @@
         return []
     cut = cut_of(near[0])
     return [swap(near[0][:, :cut], "dp", 2), swap(near[1][:, cut:], "dp", 1)]
-
-
-def joined(halves):
-    return [jnp.concatenate(halves, 1)] if halves else []
 
 
 def behind(values, others):
@@ -90,25 +90,121 @@
     return total.astype(jnp.bfloat16)
 
 
-def load_kernel(hbm_ref, vmem_ref, sem):
-    copy = pltpu.make_async_copy(hbm_ref, vmem_ref, sem)
-    copy.start()
-    copy.wait()
-
-
-def loaded(weight):
-    weight = pltpu.with_memory_space_constraint(weight, pltpu.HBM)
+def sums_kernel(layout, filling, *refs):
+    widths, block_count = layout
+    refs = list(refs)
+    place = refs.pop(0)
+    sides = [[[refs.pop(0) for _ in range(block_count)] for _ in widths] for _ in range(2)]
+    if filling:
+        up_hbm, down_hbm, keep_ref, give_ref, up, down, acc, hidden, sems = refs
+    else:
+        up, down, keep_ref, give_ref, acc, hidden = refs
+    core, first_expert = place[0], place[1]
+    per_device, width, both_width = up.shape
+    half_width = both_width // 2
+    part = width // 2
+    bases = [core * part, (1 - core) * part]
+    arrivals = {}
+    if filling:
+        copies = []
+        for side in range(2):
+            for low in range(0, part, CHUNK):
+                for s in range(per_device):
+                    at = pl.ds(pl.multiple_of(bases[side] + low, CHUNK), CHUNK)
+                    copies.append((up_hbm.at[s, at], up.at[s, at], (side, low)))
+        deep = down.shape[0]
+        for low in range(0, deep, half_width):
+            at = pl.ds(low, half_width)
+            copies.append((down_hbm.at[at], down.at[at], "down"))
+        for number, (source, target, key) in enumerate(copies):
+            copy = pltpu.make_async_copy(source, target, sems.at[number])
+            copy.start()
+            arrivals.setdefault(key, []).append(copy)
+
+    def arrive(key):
+        for copy in arrivals.get(key, ()):
+            copy.wait()
+
+    acc[...] = jnp.zeros_like(acc)
+    for side in range(2):
+        offset = 0
+        for blocks, seg_width in zip(sides[side], widths):
+            for low in range(0, seg_width, CHUNK):
+                arrive((side, offset + low))
+
+                @pl.loop(0, CHUNK // TILE)
+                def _(step, blocks=blocks, low=low, at=bases[side] + offset + low):
+                    columns = pl.ds(pl.multiple_of(low + step * TILE, TILE), TILE)
+                    held = [block[:, columns] for block in blocks]
+                    held = held[0] if len(held) == 1 else jnp.concatenate(held, 0)
+                    rows = pl.ds(pl.multiple_of(at + step * TILE, TILE), TILE)
+                    for s in range(per_device):
+                        acc[s] += jnp.dot(held, up[s, rows], preferred_element_type=jnp.float32)
+
+            offset += seg_width
+
+    last = widths[-1]
+    meta = [block[:, last:].astype(jnp.float32) for block in sides[0][-1]]
+    meta = meta[0] if len(meta) == 1 else jnp.concatenate(meta, 0)
+    gates = sum(pltpu.roll(meta, LANES - k * TOP_LANES, 1) for k in (1, 2, 3))
+    lanes = lax.broadcasted_iota(jnp.int32, meta.shape, 1)
+    for s in range(per_device):
+        chosen = (meta.astype(jnp.int32) == first_expert + s) & (lanes < TOP_LANES)
+        own_gate = jnp.sum(jnp.where(chosen, gates, 0.0), 1, keepdims=True)
+        gate_half, up_half = acc[s, :, :half_width], acc[s, :, half_width:]
+        unit = gate_half * (1.0 / (1.0 + jnp.exp(-gate_half))) * up_half
+        hidden[:, s * half_width : (s + 1) * half_width] = (unit * own_gate).astype(jnp.bfloat16)
+
+    arrive("down")
+    for base, out in ((bases[1], give_ref), (bases[0], keep_ref)):
+
+        @pl.loop(0, part // TILE)
+        def _(step, base=base, out=out):
+            columns = pl.ds(pl.multiple_of(base + step * TILE, TILE), TILE)
+            target = pl.ds(pl.multiple_of(step * TILE, TILE), TILE)
+            out[:, target] = jnp.dot(
+                hidden[...], down[:, columns], preferred_element_type=jnp.float32
+            ).astype(jnp.bfloat16)
+
+
+def gated_sums(place, own, other, up, down, filling):
+    widths = tuple(segment[0].shape[1] for segment in other)
+    block_count = len(own[0])
+    count = sum(block.shape[0] for block in own[0])
+    per_device, width, both_width = up.shape
+    operands = [block for segments in (own, other) for segment in segments for block in segment]
+    in_vmem = pl.BlockSpec(memory_space=pltpu.VMEM)
+    operands = [pltpu.with_memory_space_constraint(x, pltpu.VMEM) for x in operands]
+    out_shape = [pltpu.VMEM((count, width // 2), jnp.bfloat16)] * 2
+    scratch = [
+        pltpu.VMEM((per_device, count, both_width), jnp.float32),
+        pltpu.VMEM((count, down.shape[0]), jnp.bfloat16),
+    ]
+    if filling:
+        weights = [pltpu.with_memory_space_constraint(w, pltpu.HBM) for w in (up, down)]
+        weight_specs = [pl.BlockSpec(memory_space=pl.ANY)] * 2
+        out_shape += [pltpu.VMEM(up.shape, up.dtype), pltpu.VMEM(down.shape, down.dtype)]
+        scratch += [pltpu.SemaphoreType.DMA((per_device * (width // CHUNK + 1),))]
+        moved = up.nbytes + down.nbytes
+    else:
+        weights = [pltpu.with_memory_space_constraint(w, pltpu.VMEM) for w in (up, down)]
+        weight_specs = [in_vmem] * 2
+        moved = 0
     return pl.pallas_call(
-        load_kernel,
-        in_specs=[pl.BlockSpec(memory_space=pl.ANY)],
-        out_specs=pl.BlockSpec(memory_space=pltpu.VMEM),
-        out_shape=pltpu.VMEM(weight.shape, weight.dtype),
-        scratch_shapes=[pltpu.SemaphoreType.DMA],
-        compiler_params=pltpu.CompilerParams(vmem_limit_bytes=2 * 2**20),
+        lambda *refs: sums_kernel((widths, block_count), filling, *refs),
+        in_specs=[pl.BlockSpec(memory_space=pltpu.SMEM)]
+        + [in_vmem] * len(operands)
+        + weight_specs,
+        out_specs=[in_vmem] * len(out_shape),
+        out_shape=out_shape,
+        scratch_shapes=scratch,
+        compiler_params=pltpu.CompilerParams(vmem_limit_bytes=VMEM_LIMIT),
         cost_estimate=pl.CostEstimate(
-            flops=0, bytes_accessed=2 * weight.nbytes, transcendentals=0
+            flops=2 * count * (up.size + down.size),
+            bytes_accessed=moved,
+            transcendentals=count * down.shape[0],
         ),
-    )(weight)
+    )(place, *operands, *weights)
 
 
 def on_device(tokens, expert_ids, gate_probs, in_weight, out_weight, swap_slot):
@@ -124,7 +220,8 @@
     core = lax.axis_index("core")
     first = core == 0
     all_experts = jnp.arange(experts_all, dtype=jnp.int32)
-    home = lax.axis_index("chip") * 2 + core
+    first_expert = (lax.axis_index("chip") * 2 + core) * per_device
+    place = jnp.stack([core, first_expert]).astype(jnp.int32)
 
     routing = jnp.concatenate(
         [row_major(expert_ids).astype(jnp.bfloat16), *split_gates(row_major(gate_probs))], 1
@@ -145,65 +242,39 @@
         )
         return ids, gates
 
-    def own_sums(blocks):
-        held = row_major(jnp.concatenate(blocks, 0))
-        own_half = held[:, :part]
-        other_half = swap(own_half, "core", 1)
-        held_tokens = row_major(
-            jnp.concatenate(
-                [
-                    jnp.where(first, own_half, other_half),
-                    jnp.where(first, other_half, own_half),
-                ],
-                1,
-            )
-        )
-        ids, gates = routes(held[:, part:])
-        hidden = []
-        for s in range(per_device):
-            own_gate = jnp.sum(
-                jnp.where(ids == home * per_device + s, gates, jnp.float32(0.0)), 1, keepdims=True
-            )
-            both = jnp.dot(held_tokens, in_weight[s], preferred_element_type=jnp.float32)
-            unit = jax.nn.silu(both[:, :half_width]) * both[:, half_width:]
-            hidden.append((unit * own_gate).astype(jnp.bfloat16))
-        summed = jnp.dot(
-            jnp.concatenate(hidden, 1),
-            out_weight.reshape(per_device * half_width, width),
-            preferred_element_type=jnp.float32,
-        )
-        return row_major(summed.astype(jnp.bfloat16))
-
-    def chip_sums(summed, blocks):
-        left, right = summed[:, :part], summed[:, part:]
-        arrived = swap(jnp.where(first, right, left), "core", 1)
-        chip_sum = (wide(jnp.where(first, left, right)) + wide(arrived)).astype(jnp.bfloat16)
-        chip_sum = row_major(chip_sum)
-        edges = [0]
-        for block in blocks:
-            edges.append(edges[-1] + block.shape[0])
-        return [chip_sum[low:high] for low, high in zip(edges, edges[1:])]
-
-    others = [swap(chip_rows, "chip", j) for j in range(1, chips)]
-    near = [chip_rows, *spread_near(behind(chip_rows, others[0]))]
-    near += joined(spread_rest(near[1:]))
-    far = [row_major(jnp.concatenate(others, 0))]
-    far += spread_near(far[0])
-    in_weight = loaded(behind(in_weight, far[0]))
-    first_blocks = [*near, far[0]]
-    first_part = own_sums(first_blocks)
-    far[1:] = behind(far[1:], first_part)
-    rest = spread_rest(far[1:])
-    sums = chip_sums(first_part, first_blocks)
-    part_two = own_sums(far[1:])
+    def sums_of(own, weights, filling=False):
+        last = len(own) - 1
+        bare = [
+            [block[:, : block.shape[1] - (LANES if i == last else 0)] for block in segment]
+            for i, segment in enumerate(own)
+        ]
+        other = [[swap(block, "core", 1) for block in segment] for segment in bare]
+        keep, give, *filled = gated_sums(place, own, other, *weights, filling)
+        return keep, give, filled or weights
+
+    def chip_sums(keep, give):
+        return (wide(keep) + wide(swap(give, "core", 1))).astype(jnp.bfloat16)
+
+    chip_blocks = [chip_rows] + [swap(chip_rows, "chip", j) for j in range(1, chips)]
+    held = [row_major(jnp.concatenate(chip_blocks, 0))]
+    near = spread_near(held[0])
+    weights = (in_weight, out_weight.reshape(per_device * half_width, width))
+    keep, give, weights = sums_of([held], weights, filling=True)
+    near = behind(near, give)
+    rest = spread_rest(near)
+    sums = [chip_sums(keep, give)]
     if rest:
-        rest = joined(behind(rest, part_two))
-        part_three = own_sums(rest)
-        sums += chip_sums(part_two, far[1:]) + chip_sums(part_three, rest)
+        keep, give, _ = sums_of([near], weights)
+        pair = chip_sums(keep, give)
+        sums += [pair[: pair.shape[0] // 2], pair[pair.shape[0] // 2 :]]
+        rest = behind(rest, give)
+        keep, give, _ = sums_of([[half] for half in rest], weights)
+        sums += [chip_sums(keep, give)]
     else:
-        sums += chip_sums(part_two, far[1:])
-    far += rest
-    sums = [jnp.concatenate([sums[k], sums[groups + k]], 0) for k in range(groups)]
+        for block in near:
+            keep, give, _ = sums_of([[block]], weights)
+            sums += [chip_sums(keep, give)]
+    metas = [block[:, block.shape[1] - LANES :] for block in held + near + rest[1:]]
     sums = with_fourth(sums)
     border = 2 * near_chips * rows
     total = collected([block[border:] for block in sums])
@@ -221,7 +292,7 @@
         jnp.concatenate([jnp.where(first, kept, arrived), jnp.where(first, arrived, kept)], 1)
     )
 
-    ids, gates = routes(jnp.concatenate([block[:, part:] for block in near + far], 0))
+    ids, gates = routes(jnp.concatenate(metas, 0))
     step = 2.0 ** (31 - (ids.shape[0] * GATE_MOST).bit_length())
     amounts = jnp.round(gates * step).astype(jnp.int32)
     totals = jnp.sum(jnp.where(ids[..., None] == all_experts, amounts[..., None], 0), (0, 1))

time: 93.4 us -> 83.6 us (0.90)
  Pallas kernels: 4.58 us -> 23 us
  matrix products: 16.8 us -> 0 us
  local copies, waits for them, and re-layouts: 6.89 us -> 1.93 us
  starting transfers between devices: 31.1 us -> 26.2 us
  other arithmetic: 10.2 us -> 5.97 us
  waiting for transfers between devices: 22.1 us -> 25.2 us
    pallas_call x1 -> x3, Pallas kernels: 4.58 us -> 23 us  [gated_sums(): pl.pallas_call(lambda *refs: sums_kernel((widths, block_count), filling,...]
    dot_general x9 -> x0, matrix products: 16.8 us -> none  [the longest x6 13 us: own_sums(): jnp.dot(held_tokens, in_weight[s], preferred_element_type=jnp.float32)]
    ppermute x28 -> x26, starting transfers between devices: 31.1 us -> 26.2 us  [swap(): return row_major(lax.ppermute(row_major(value), axis, pairs))]
    unnamed x31 -> x4, local copies, waits for them, and re-layouts: 6.36 us -> 1.54 us
    ppermute x28 -> x26, waiting for transfers between devices: 22.1 us -> 25.2 us  [swap(): return row_major(lax.ppermute(row_major(value), axis, pairs))]
    reduce_sum x3 -> x0, other arithmetic: 1.61 us -> none  [own_sums(): jnp.sum(jnp.where(ids == home * per_device + s, gates, jnp.float32(0.0)),...]
    select_n x6 -> x0, other arithmetic: 1.33 us -> none  [the longest x3 1.06 us: chip_sums(): arrived = swap(jnp.where(first, right, left), 'core', 1)]
    concatenate x4 -> x3, other arithmetic: 1.09 us -> 0.09 us  [the longest x1 0.04 us: on_device(): held = [row_major(jnp.concatenate(chip_blocks, 0))]]
  transfers between devices with their start and end apart: 28 -> 26, of which waited for: 15 -> 16; matrix products, arithmetic and copies ran while one was open for 28% -> 5% of each run, Pallas kernels for 5% -> 28%
where the time goes in v9:
time: 83.6 us; the launch traced here: 83.3 us
  starting transfers between devices  26.2 us (31%)
  waiting for transfers between devices  25.2 us (30%)
  Pallas kernels  23 us (28%)
  other arithmetic  5.97 us (7%)
  local copies, waits for them, and re-layouts  1.93 us (2%)
  between operations  0.94 us (1%)
    ppermute x26, starting transfers between devices, swap(): return row_major(lax.ppermute(row_major(value), axis, pairs))  26.2 us
    ppermute x26, waiting for transfers between devices, swap(): return row_major(lax.ppermute(row_major(value), axis, pairs))  25.2 us
    pallas_call x3, Pallas kernels, gated_sums(): pl.pallas_call(lambda *refs: sums_kernel((widths, block_count), filling,...  23 us
    convert_element_type x3, other arithmetic, chip_sums(): return (wide(keep) + wide(swap(give, 'core', 1))).astype(jnp.bfloat16)  2.58 us
  transfers between devices with their start and end apart: 26, of which 16 were waited for; matrix products, arithmetic and copies ran while one was open for 5% of the time, Pallas kernels for 28%

profile of v9, /device:TPU:0, one launch (start us, length us, event | category | flops | bytes accessed | tf_op | source)
XLA Modules:
  0.0 83.3 jit_solution(1191965349989323210)
XLA Ops:
  0.6 0.8 copy.15
  1.4 0.8 copy.14
  2.2 0.9 %broadcast_select_fusion.7 = (bf16[12,2048]{1,0:T(8,128)(2,1)S(1)}, bf16[12,2048]{1,0:T(8,128)(2,1)S(1)}) fusion(pred[]{:T(512)S(6)} %eq.52, bf16[12,4096]{1,0:T(8,128)(2,1)} %param.6), kind=kLoop, calls=%fused_computation.33 | loop fusion | flops 49152 | bytes 196609 | tf_op jit(solution)/shard_map/jit(_where)/select_n | solution.py:231
  3.2 0.5 collective-permute-start
  3.7 0.9 %collective-permute-done = bf16[12,2176]{1,0:T(8,128)(2,1)S(1)} collective-permute-done((bf16[12,2176]{1,0:T(8,128)(2,1)S(1)}, bf16[12,2176]{1,0:T(8,128)(2,1)S(1)}, u32[]{:S(2)}, u32[]{:S(2)}) %collective-permute-start) | collective-permute-done | bytes 52256 | tf_op jit(solution)/shard_map/ppermute | solution.py:37
  4.7 3.0 %collective-permute-start.1 = (bf16[24,2176]{1,0:T(8,128)(2,1)S(1)}, bf16[24,2176]{1,0:T(8,128)(2,1)S(1)}, u32[]{:S(2)}, u32[]{:S(2)}) collective-permute-start(bf16[24,2176]{1,0:T(8,128)(2,1)S(1)} %pad_maximum_fusion.4), channel_id=1, source_target_pairs={{0,2},{2,0},{4,6},{6,4},{1,3},{3,1},{5,7},{7,5},{8,10},{10,8},{12,... | collective-permute-start | bytes 313352 | tf_op jit(solution)/shard_map/ppermute | solution.py:37
  7.7 2.6 %collective-permute-start.2 = (bf16[24,2176]{1,0:T(8,128)(2,1)S(1)}, bf16[24,2176]{1,0:T(8,128)(2,1)S(1)}, u32[]{:S(2)}, u32[]{:S(2)}) collective-permute-start(bf16[24,2176]{1,0:T(8,128)(2,1)S(1)} %pad_maximum_fusion.4), channel_id=1, source_target_pairs={{0,4},{2,6},{4,0},{6,2},{1,5},{3,7},{5,1},{7,3},{8,12},{10,14},{12... | collective-permute-start | bytes 313352 | tf_op jit(solution)/shard_map/ppermute | solution.py:37
  10.3 0.7 collective-permute-done.1
  10.9 7.8 %collective-permute-done.2 = bf16[24,2176]{1,0:T(8,128)(2,1)S(1)} collective-permute-done((bf16[24,2176]{1,0:T(8,128)(2,1)S(1)}, bf16[24,2176]{1,0:T(8,128)(2,1)S(1)}, u32[]{:S(2)}, u32[]{:S(2)}) %collective-permute-start.2) | collective-permute-done | bytes 104480 | tf_op jit(solution)/shard_map/ppermute | solution.py:37
  18.9 1.6 %collective-permute-start.6 = (bf16[96,2176]{1,0:T(8,128)(2,1)S(1)}, bf16[96,2176]{1,0:T(8,128)(2,1)S(1)}, u32[]{:S(2)}, u32[]{:S(2)}) collective-permute-start(bf16[96,2176]{1,0:T(8,128)(2,1)S(1)} %pad_maximum_fusion.refs_1_), channel_id=1, source_target_pairs={{0,8},{8,0},{16,24},{24,16},{1,9},{9,1},{17,25},{25,17},{2,10},{10... | collective-permute-start | bytes 1253384 | tf_op jit(solution)/shard_map/ppermute | solution.py:37
  20.4 1.5 %collective-permute-start.7 = (bf16[96,2176]{1,0:T(8,128)(2,1)S(1)}, bf16[96,2176]{1,0:T(8,128)(2,1)S(1)}, u32[]{:S(2)}, u32[]{:S(2)}) collective-permute-start(bf16[96,2176]{1,0:T(8,128)(2,1)S(1)} %pad_maximum_fusion.refs_1_), channel_id=1, source_target_pairs={{0,16},{8,24},{16,0},{24,8},{1,17},{9,25},{17,1},{25,9},{2,18},{10... | collective-permute-start | bytes 1253384 | tf_op jit(solution)/shard_map/ppermute | solution.py:37
  22.0 9.3 %shard_map.77 = (bf16[96,2048]{1,0:T(8,128)(2,1)S(1)}, bf16[96,2048]{1,0:T(8,128)(2,1)S(1)}, bf16[2,4096,768]{2,1,0:T(8,128)(2,1)S(1)}, bf16[768,4096]{1,0:T(8,128)(2,1)S(1)}) custom-call(s32[2]{0:T(128)S(1)} %pad_add_fusion.refs_0_, bf16[96,2176]{1,0:T(8,128)(2,1)S(1)} %pad_maximum_fusion.refs_1_, bf16[96,2048]{1,0:T(8,128)(2,1)S(1)} %collective-permute-done.4.refs_2_, ...), custom_call_target="tpu_custom_call" | custom-call | flops 1811939328 | bytes 18874368 | tf_op jit(solution)/shard_map/pallas_call | solution.py:193
  31.3 0.8 collective-permute-done.7.refs_2_
  32.3 0.6 collective-permute-start.9
  33.0 0.6 collective-permute-start.12
  33.6 1.5 %collective-permute-start.11 = (bf16[96,1024]{1,0:T(8,128)(2,1)S(1)}, bf16[96,1024]{1,0:T(8,128)(2,1)S(1)}, u32[]{:S(2)}, u32[]{:S(2)}) collective-permute-start(bf16[96,1024]{1,0:T(8,128)(2,1)S(1)} %slice.115), channel_id=1, source_target_pairs={{0,16},{8,24},{16,0},{24,8},{1,17},{9,25},{17,1},{25,9},{2,18},{10... | collective-permute-start | bytes 589832 | tf_op jit(solution)/shard_map/ppermute | solution.py:37
  35.2 7.6 %shard_map.78 = (bf16[192,2048]{1,0:T(8,128)(2,1)S(1)}, bf16[192,2048]{1,0:T(8,128)(2,1)S(1)}) custom-call(s32[2]{0:T(128)S(1)} %pad_add_fusion.refs_0_, bf16[96,2176]{1,0:T(8,128)(2,1)S(1)} %collective-permute-done.6.refs_1_, bf16[96,2176]{1,0:T(8,128)(2,1)S(1)} %collective-permute-done.7.refs_2_, bf16[96,2048]{1,0:T(8,128)(2,1)S(1)} %collective-permute-done.8.refs_3_, ...), custom_call_target="tpu_custom_call" | custom-call | flops 3623878656 | tf_op jit(solution)/shard_map/pallas_call | solution.py:193
  42.9 0.5 collective-permute-start.13
  43.6 0.1 collective-permute-start.10
  43.7 0.6 collective-permute-done.14.refs_4_
  44.4 0.3 collective-permute-done.13.refs_3_
  44.6 6.1 %shard_map.79 = (bf16[96,2048]{1,0:T(8,128)(2,1)S(1)}, bf16[96,2048]{1,0:T(8,128)(2,1)S(1)}) custom-call(s32[2]{0:T(128)S(1)} %pad_add_fusion.refs_0_, bf16[96,1024]{1,0:T(8,128)(2,1)S(1)} %collective-permute-done.11.refs_1_, bf16[96,1152]{1,0:T(8,128)(2,1)S(1)} %collective-permute-done.12.refs_2_, bf16[96,1024]{1,0:T(8,128)(2,1)S(1)} %collective-permute-done.13.refs_3_, ...), custom_call_target="tpu_custom_call" | custom-call | flops 1811939328 | tf_op jit(solution)/shard_map/pallas_call | solution.py:193
  50.8 0.3 collective-permute-start.15
  51.2 0.2 round-nearest-even_convert_fusion
  51.4 0.2 select_reduce_fusion
  51.6 1.1 %collective-permute-done.15 = bf16[96,2048]{1,0:T(8,128)(2,1)} collective-permute-done((bf16[96,2048]{1,0:T(8,128)(2,1)S(1)}, bf16[96,2048]{1,0:T(8,128)(2,1)}, u32[]{:S(2)}, u32[]{:S(2)}) %collective-permute-start.15) | collective-permute-done | bytes 393248 | tf_op jit(solution)/shard_map/ppermute | solution.py:37
  52.7 1.1 %add_convert_fusion.1 = bf16[96,2048]{1,0:T(8,128)(2,1)S(1)} fusion(bf16[96,2048]{1,0:T(8,128)(2,1)} %collective-permute-done.15, bf16[96,2048]{1,0:T(8,128)(2,1)S(1)} %get-tuple-element.27), kind=kLoop, calls=%fused_computation.1 | loop fusion | flops 786432 | bytes 1179648 | tf_op jit(solution)/shard_map/convert_element_type | solution.py:256
  53.8 0.9 %collective-permute-start.16 = (bf16[96,1024]{1,0:T(8,128)(2,1)S(1)}, bf16[96,1024]{1,0:T(8,128)(2,1)S(1)}, u32[]{:S(2)}, u32[]{:S(2)}) collective-permute-start(bf16[96,1024]{1,0:T(8,128)(2,1)S(1)} %get-tuple-element.40), channel_id=1, source_target_pairs={{0,16},{8,24},{16,0},{24,8},{1,17},{9,25},{17,1},{25,9},{2,18},{10... | collective-permute-start | bytes 589832 | tf_op jit(solution)/shard_map/ppermute | solution.py:37
  54.8 1.1 %collective-permute-start.17 = (bf16[96,1024]{1,0:T(8,128)(2,1)S(1)}, bf16[96,1024]{1,0:T(8,128)(2,1)S(1)}, u32[]{:S(2)}, u32[]{:S(2)}) collective-permute-start(bf16[96,1024]{1,0:T(8,128)(2,1)S(1)} %get-tuple-element.41), channel_id=1, source_target_pairs={{0,8},{8,0},{16,24},{24,16},{1,9},{9,1},{17,25},{25,17},{2,10},{10... | collective-permute-start | bytes 589832 | tf_op jit(solution)/shard_map/ppermute | solution.py:37
  55.9 1.4 %add_convert_fusion = bf16[192,2048]{1,0:T(8,128)(2,1)S(1)} fusion(bf16[192,2048]{1,0:T(8,128)(2,1)} %collective-permute-done.10, bf16[192,2048]{1,0:T(8,128)(2,1)S(1)} %get-tuple-element.23), kind=kLoop, calls=%fused_computation | loop fusion | flops 1572864 | bytes 2359296 | tf_op jit(solution)/shard_map/convert_element_type | solution.py:256
  57.3 3.6 %collective-permute-done.16 = bf16[96,1024]{1,0:T(8,128)(2,1)S(1)} collective-permute-done((bf16[96,1024]{1,0:T(8,128)(2,1)S(1)}, bf16[96,1024]{1,0:T(8,128)(2,1)S(1)}, u32[]{:S(2)}, u32[]{:S(2)}) %collective-permute-start.16) | collective-permute-done | bytes 196640 | tf_op jit(solution)/shard_map/ppermute | solution.py:37
  60.9 0.6 collective-permute-done.17
  61.7 1.2 %collective-permute-start.18 = (bf16[48,2048]{1,0:T(8,128)(2,1)S(1)}, bf16[48,2048]{1,0:T(8,128)(2,1)S(1)}, u32[]{:S(2)}, u32[]{:S(2)}) collective-permute-start(bf16[48,2048]{1,0:T(8,128)(2,1)S(1)} %get-tuple-element.39), channel_id=1, source_target_pairs={{0,8},{8,0},{16,24},{24,16},{1,9},{9,1},{17,25},{25,17},{2,10},{10... | collective-permute-start | bytes 589832 | tf_op jit(solution)/shard_map/ppermute | solution.py:37
  62.9 1.6 %collective-permute-start.19 = (bf16[48,2048]{1,0:T(8,128)(2,1)S(1)}, bf16[48,2048]{1,0:T(8,128)(2,1)S(1)}, u32[]{:S(2)}, u32[]{:S(2)}) collective-permute-start(bf16[48,2048]{1,0:T(8,128)(2,1)S(1)} %get-tuple-element.37), channel_id=1, source_target_pairs={{0,16},{8,24},{16,0},{24,8},{1,17},{9,25},{17,1},{25,9},{2,18},{10... | collective-permute-start | bytes 589832 | tf_op jit(solution)/shard_map/ppermute | solution.py:37
  64.5 3.2 %collective-permute-done.18 = bf16[48,2048]{1,0:T(8,128)(2,1)S(1)} collective-permute-done((bf16[48,2048]{1,0:T(8,128)(2,1)S(1)}, bf16[48,2048]{1,0:T(8,128)(2,1)S(1)}, u32[]{:S(2)}, u32[]{:S(2)}) %collective-permute-start.18) | collective-permute-done | bytes 196640 | tf_op jit(solution)/shard_map/ppermute | solution.py:37
  67.7 1.0 %collective-permute-done.19 = bf16[48,2048]{1,0:T(8,128)(2,1)S(1)} collective-permute-done((bf16[48,2048]{1,0:T(8,128)(2,1)S(1)}, bf16[48,2048]{1,0:T(8,128)(2,1)S(1)}, u32[]{:S(2)}, u32[]{:S(2)}) %collective-permute-start.19) | collective-permute-done | bytes 196640 | tf_op jit(solution)/shard_map/ppermute | solution.py:37
  68.8 0.9 %collective-permute-start.20 = (bf16[48,2048]{1,0:T(8,128)(2,1)S(1)}, bf16[48,2048]{1,0:T(8,128)(2,1)S(1)}, u32[]{:S(2)}, u32[]{:S(2)}) collective-permute-start(bf16[48,2048]{1,0:T(8,128)(2,1)S(1)} %get-tuple-element.30), channel_id=1, source_target_pairs={{0,8},{8,0},{16,24},{24,16},{1,9},{9,1},{17,25},{25,17},{2,10},{10... | collective-permute-start | bytes 589832 | tf_op jit(solution)/shard_map/ppermute | solution.py:37
  69.7 1.2 %collective-permute-start.21 = (bf16[48,2048]{1,0:T(8,128)(2,1)S(1)}, bf16[48,2048]{1,0:T(8,128)(2,1)S(1)}, u32[]{:S(2)}, u32[]{:S(2)}) collective-permute-start(bf16[48,2048]{1,0:T(8,128)(2,1)S(1)} %get-tuple-element.31), channel_id=1, source_target_pairs={{0,16},{8,24},{16,0},{24,8},{1,17},{9,25},{17,1},{25,9},{2,18},{10... | collective-permute-start | bytes 589832 | tf_op jit(solution)/shard_map/ppermute | solution.py:37
  70.9 3.0 %collective-permute-start.23 = (bf16[24,2048]{1,0:T(8,128)(2,1)S(1)}, bf16[24,2048]{1,0:T(8,128)(2,1)S(1)}, u32[]{:S(2)}, u32[]{:S(2)}) collective-permute-start(bf16[24,2048]{1,0:T(8,128)(2,1)S(1)} %get-tuple-element.42), channel_id=1, source_target_pairs={{0,4},{2,6},{4,0},{6,2},{1,5},{3,7},{5,1},{7,3},{8,12},{10,14},{12... | collective-permute-start | bytes 294920 | tf_op jit(solution)/shard_map/ppermute | solution.py:37
  73.9 1.3 %collective-permute-start.24 = (bf16[24,2048]{1,0:T(8,128)(2,1)S(1)}, bf16[24,2048]{1,0:T(8,128)(2,1)S(1)}, u32[]{:S(2)}, u32[]{:S(2)}) collective-permute-start(bf16[24,2048]{1,0:T(8,128)(2,1)S(1)} %get-tuple-element.43), channel_id=1, source_target_pairs={{0,6},{2,4},{4,2},{6,0},{1,7},{3,5},{5,3},{7,1},{8,14},{10,12},{12... | collective-permute-start | bytes 294920 | tf_op jit(solution)/shard_map/ppermute | solution.py:37
  75.2 0.2 collective-permute-done.21
  75.5 1.9 %collective-permute-start.22 = (bf16[24,2048]{1,0:T(8,128)(2,1)S(1)}, bf16[24,2048]{1,0:T(8,128)(2,1)S(1)}, u32[]{:S(2)}, u32[]{:S(2)}) collective-permute-start(bf16[24,2048]{1,0:T(8,128)(2,1)S(1)} %slice.156), channel_id=1, source_target_pairs={{0,2},{2,0},{4,6},{6,4},{1,3},{3,1},{5,7},{7,5},{8,10},{10,8},{12,... | collective-permute-start | bytes 294920 | tf_op jit(solution)/shard_map/ppermute | solution.py:37
  77.5 1.1 %collective-permute-done.23 = bf16[24,2048]{1,0:T(8,128)(2,1)S(1)} collective-permute-done((bf16[24,2048]{1,0:T(8,128)(2,1)S(1)}, bf16[24,2048]{1,0:T(8,128)(2,1)S(1)}, u32[]{:S(2)}, u32[]{:S(2)}) %collective-permute-start.23) | collective-permute-done | bytes 98336 | tf_op jit(solution)/shard_map/ppermute | solution.py:37
  78.6 1.9 %collective-permute-done.24 = bf16[24,2048]{1,0:T(8,128)(2,1)S(1)} collective-permute-done((bf16[24,2048]{1,0:T(8,128)(2,1)S(1)}, bf16[24,2048]{1,0:T(8,128)(2,1)S(1)}, u32[]{:S(2)}, u32[]{:S(2)}) %collective-permute-start.24) | collective-permute-done | bytes 98336 | tf_op jit(solution)/shard_map/ppermute | solution.py:37
  80.4 0.8 collective-permute-done.22
  81.4 0.5 broadcast_multiply_fusion
  81.9 0.7 collective-permute-done.25
  82.7 0.7 pad_maximum_fusion.3
  (59 shorter events, 1.8 us)
Async XLA Ops:
  3.2 1.4 %collective-permute-start = (bf16[12,2176]{1,0:T(8,128)(2,1)S(1)}, bf16[12,2176]{1,0:T(8,128)(2,1)S(1)}, u32[]{:S(2)}, u32[]{:S(2)}) collective-permute-start(bf16[12,2176]{1,0:T(8,128)(2,1)S(1)} %pad_maximum_fusion.6), channel_id=1, source_target_pairs={{0,1},{1,0},{2,3},{3,2},{4,5},{5,4},{6,7},{7,6},{8,9},{9,8},{10,11... | collective-permute-start | bytes 156680 | tf_op jit(solution)/shard_map/ppermute | solution.py:37
  4.7 6.2 %collective-permute-start.1 = (bf16[24,2176]{1,0:T(8,128)(2,1)S(1)}, bf16[24,2176]{1,0:T(8,128)(2,1)S(1)}, u32[]{:S(2)}, u32[]{:S(2)}) collective-permute-start(bf16[24,2176]{1,0:T(8,128)(2,1)S(1)} %pad_maximum_fusion.4), channel_id=1, source_target_pairs={{0,2},{2,0},{4,6},{6,4},{1,3},{3,1},{5,7},{7,5},{8,10},{10,8},{12,... | collective-permute-start | bytes 313352 | tf_op jit(solution)/shard_map/ppermute | solution.py:37
  7.7 11.0 %collective-permute-start.2 = (bf16[24,2176]{1,0:T(8,128)(2,1)S(1)}, bf16[24,2176]{1,0:T(8,128)(2,1)S(1)}, u32[]{:S(2)}, u32[]{:S(2)}) collective-permute-start(bf16[24,2176]{1,0:T(8,128)(2,1)S(1)} %pad_maximum_fusion.4), channel_id=1, source_target_pairs={{0,4},{2,6},{4,0},{6,2},{1,5},{3,7},{5,1},{7,3},{8,12},{10,14},{12... | collective-permute-start | bytes 313352 | tf_op jit(solution)/shard_map/ppermute | solution.py:37
  10.3 8.4 %collective-permute-start.3 = (bf16[24,2176]{1,0:T(8,128)(2,1)S(1)}, bf16[24,2176]{1,0:T(8,128)(2,1)S(1)}, u32[]{:S(2)}, u32[]{:S(2)}) collective-permute-start(bf16[24,2176]{1,0:T(8,128)(2,1)S(1)} %pad_maximum_fusion.4), channel_id=1, source_target_pairs={{0,6},{2,4},{4,2},{6,0},{1,7},{3,5},{5,3},{7,1},{8,14},{10,12},{12... | collective-permute-start | bytes 313352 | tf_op jit(solution)/shard_map/ppermute | solution.py:37
  18.8 3.2 %collective-permute-start.4 = (bf16[96,2048]{1,0:T(8,128)(2,1)S(1)}, bf16[96,2048]{1,0:T(8,128)(2,1)S(1)}, u32[]{:S(2)}, u32[]{:S(2)}) collective-permute-start(bf16[96,2048]{1,0:T(8,128)(2,1)S(1)} %slice.142), channel_id=1, source_target_pairs={{0,1},{1,0},{2,3},{3,2},{4,5},{5,4},{6,7},{7,6},{8,9},{9,8},{10,11... | collective-permute-start | bytes 1179656 | tf_op jit(solution)/shard_map/ppermute | solution.py:37
  18.9 12.4 %collective-permute-start.6 = (bf16[96,2176]{1,0:T(8,128)(2,1)S(1)}, bf16[96,2176]{1,0:T(8,128)(2,1)S(1)}, u32[]{:S(2)}, u32[]{:S(2)}) collective-permute-start(bf16[96,2176]{1,0:T(8,128)(2,1)S(1)} %pad_maximum_fusion.refs_1_), channel_id=1, source_target_pairs={{0,8},{8,0},{16,24},{24,16},{1,9},{9,1},{17,25},{25,17},{2,10},{10... | collective-permute-start | bytes 1253384 | tf_op jit(solution)/shard_map/ppermute | solution.py:37
  20.4 11.7 %collective-permute-start.7 = (bf16[96,2176]{1,0:T(8,128)(2,1)S(1)}, bf16[96,2176]{1,0:T(8,128)(2,1)S(1)}, u32[]{:S(2)}, u32[]{:S(2)}) collective-permute-start(bf16[96,2176]{1,0:T(8,128)(2,1)S(1)} %pad_maximum_fusion.refs_1_), channel_id=1, source_target_pairs={{0,16},{8,24},{16,0},{24,8},{1,17},{9,25},{17,1},{25,9},{2,18},{10... | collective-permute-start | bytes 1253384 | tf_op jit(solution)/shard_map/ppermute | solution.py:37
  22.0 10.8 %copy-start = (s32[8]{0:T(128)S(1)}, s32[8]{0:T(128)}, u32[]{:S(2)}) copy-start(s32[8]{0:T(128)} %param.11) | copy-start | bytes 100
  32.2 3.0 %collective-permute-start.8 = (bf16[96,2048]{1,0:T(8,128)(2,1)S(1)}, bf16[96,2048]{1,0:T(8,128)(2,1)S(1)}, u32[]{:S(2)}, u32[]{:S(2)}) collective-permute-start(bf16[96,2048]{1,0:T(8,128)(2,1)S(1)} %slice.112), channel_id=1, source_target_pairs={{0,1},{1,0},{2,3},{3,2},{4,5},{5,4},{6,7},{7,6},{8,9},{9,8},{10,11... | collective-permute-start | bytes 1179656 | tf_op jit(solution)/shard_map/ppermute | solution.py:37
  32.3 2.9 %collective-permute-start.9 = (bf16[96,2048]{1,0:T(8,128)(2,1)S(1)}, bf16[96,2048]{1,0:T(8,128)(2,1)S(1)}, u32[]{:S(2)}, u32[]{:S(2)}) collective-permute-start(bf16[96,2048]{1,0:T(8,128)(2,1)S(1)} %slice.113), channel_id=1, source_target_pairs={{0,1},{1,0},{2,3},{3,2},{4,5},{5,4},{6,7},{7,6},{8,9},{9,8},{10,11... | collective-permute-start | bytes 1179656 | tf_op jit(solution)/shard_map/ppermute | solution.py:37
  32.9 10.5 %collective-permute-start.5 = (bf16[96,2048]{1,0:T(8,128)(2,1)S(1)}, bf16[96,2048]{1,0:T(8,128)(2,1)S(1)}, u32[]{:S(2)}, u32[]{:S(2)}) collective-permute-start(bf16[96,2048]{1,0:T(8,128)(2,1)S(1)} %get-tuple-element.18), channel_id=1, source_target_pairs={{0,1},{1,0},{2,3},{3,2},{4,5},{5,4},{6,7},{7,6},{8,9},{9,8},{10,11... | collective-permute-start | bytes 1179656 | tf_op jit(solution)/shard_map/ppermute | solution.py:37
  33.0 9.8 %collective-permute-start.12 = (bf16[96,1152]{1,0:T(8,128)(2,1)S(1)}, bf16[96,1152]{1,0:T(8,128)(2,1)S(1)}, u32[]{:S(2)}, u32[]{:S(2)}) collective-permute-start(bf16[96,1152]{1,0:T(8,128)(2,1)S(1)} %slice.116), channel_id=1, source_target_pairs={{0,8},{8,0},{16,24},{24,16},{1,9},{9,1},{17,25},{25,17},{2,10},{10... | collective-permute-start | bytes 663560 | tf_op jit(solution)/shard_map/ppermute | solution.py:37
  33.6 9.2 %collective-permute-start.11 = (bf16[96,1024]{1,0:T(8,128)(2,1)S(1)}, bf16[96,1024]{1,0:T(8,128)(2,1)S(1)}, u32[]{:S(2)}, u32[]{:S(2)}) collective-permute-start(bf16[96,1024]{1,0:T(8,128)(2,1)S(1)} %slice.115), channel_id=1, source_target_pairs={{0,16},{8,24},{16,0},{24,8},{1,17},{9,25},{17,1},{25,9},{2,18},{10... | collective-permute-start | bytes 589832 | tf_op jit(solution)/shard_map/ppermute | solution.py:37
  42.8 1.5 %collective-permute-start.14 = (bf16[96,1024]{1,0:T(8,128)(2,1)S(1)}, bf16[96,1024]{1,0:T(8,128)(2,1)S(1)}, u32[]{:S(2)}, u32[]{:S(2)}) collective-permute-start(bf16[96,1024]{1,0:T(8,128)(2,1)S(1)} %slice.117), channel_id=1, source_target_pairs={{0,1},{1,0},{2,3},{3,2},{4,5},{5,4},{6,7},{7,6},{8,9},{9,8},{10,11... | collective-permute-start | bytes 589832 | tf_op jit(solution)/shard_map/ppermute | solution.py:37
  42.9 1.7 %collective-permute-start.13 = (bf16[96,1024]{1,0:T(8,128)(2,1)S(1)}, bf16[96,1024]{1,0:T(8,128)(2,1)S(1)}, u32[]{:S(2)}, u32[]{:S(2)}) collective-permute-start(bf16[96,1024]{1,0:T(8,128)(2,1)S(1)} %collective-permute-done.11.refs_1_), channel_id=1, source_target_pairs={{0,1},{1,0},{2,3},{3,2},{4,5},{5,4},{6,7},{7,6},{8,9},{9,8},{10,11... | collective-permute-start | bytes 589832 | tf_op jit(solution)/shard_map/ppermute | solution.py:37
  43.6 12.3 %collective-permute-start.10 = (bf16[192,2048]{1,0:T(8,128)(2,1)S(1)}, bf16[192,2048]{1,0:T(8,128)(2,1)}, u32[]{:S(2)}, u32[]{:S(2)}) collective-permute-start(bf16[192,2048]{1,0:T(8,128)(2,1)S(1)} %get-tuple-element.24), channel_id=1, source_target_pairs={{0,1},{1,0},{2,3},{3,2},{4,5},{5,4},{6,7},{7,6},{8,9},{9,8},{10,11... | collective-permute-start | bytes 2359304 | tf_op jit(solution)/shard_map/ppermute | solution.py:37
  50.8 1.9 %collective-permute-start.15 = (bf16[96,2048]{1,0:T(8,128)(2,1)S(1)}, bf16[96,2048]{1,0:T(8,128)(2,1)}, u32[]{:S(2)}, u32[]{:S(2)}) collective-permute-start(bf16[96,2048]{1,0:T(8,128)(2,1)S(1)} %get-tuple-element.28), channel_id=1, source_target_pairs={{0,1},{1,0},{2,3},{3,2},{4,5},{5,4},{6,7},{7,6},{8,9},{9,8},{10,11... | collective-permute-start | bytes 1179656 | tf_op jit(solution)/shard_map/ppermute | solution.py:37
  53.8 7.1 %collective-permute-start.16 = (bf16[96,1024]{1,0:T(8,128)(2,1)S(1)}, bf16[96,1024]{1,0:T(8,128)(2,1)S(1)}, u32[]{:S(2)}, u32[]{:S(2)}) collective-permute-start(bf16[96,1024]{1,0:T(8,128)(2,1)S(1)} %get-tuple-element.40), channel_id=1, source_target_pairs={{0,16},{8,24},{16,0},{24,8},{1,17},{9,25},{17,1},{25,9},{2,18},{10... | collective-permute-start | bytes 589832 | tf_op jit(solution)/shard_map/ppermute | solution.py:37
  54.8 6.8 %collective-permute-start.17 = (bf16[96,1024]{1,0:T(8,128)(2,1)S(1)}, bf16[96,1024]{1,0:T(8,128)(2,1)S(1)}, u32[]{:S(2)}, u32[]{:S(2)}) collective-permute-start(bf16[96,1024]{1,0:T(8,128)(2,1)S(1)} %get-tuple-element.41), channel_id=1, source_target_pairs={{0,8},{8,0},{16,24},{24,16},{1,9},{9,1},{17,25},{25,17},{2,10},{10... | collective-permute-start | bytes 589832 | tf_op jit(solution)/shard_map/ppermute | solution.py:37
  61.7 6.0 %collective-permute-start.18 = (bf16[48,2048]{1,0:T(8,128)(2,1)S(1)}, bf16[48,2048]{1,0:T(8,128)(2,1)S(1)}, u32[]{:S(2)}, u32[]{:S(2)}) collective-permute-start(bf16[48,2048]{1,0:T(8,128)(2,1)S(1)} %get-tuple-element.39), channel_id=1, source_target_pairs={{0,8},{8,0},{16,24},{24,16},{1,9},{9,1},{17,25},{25,17},{2,10},{10... | collective-permute-start | bytes 589832 | tf_op jit(solution)/shard_map/ppermute | solution.py:37
  62.9 5.8 %collective-permute-start.19 = (bf16[48,2048]{1,0:T(8,128)(2,1)S(1)}, bf16[48,2048]{1,0:T(8,128)(2,1)S(1)}, u32[]{:S(2)}, u32[]{:S(2)}) collective-permute-start(bf16[48,2048]{1,0:T(8,128)(2,1)S(1)} %get-tuple-element.37), channel_id=1, source_target_pairs={{0,16},{8,24},{16,0},{24,8},{1,17},{9,25},{17,1},{25,9},{2,18},{10... | collective-permute-start | bytes 589832 | tf_op jit(solution)/shard_map/ppermute | solution.py:37
  68.8 6.4 %collective-permute-start.20 = (bf16[48,2048]{1,0:T(8,128)(2,1)S(1)}, bf16[48,2048]{1,0:T(8,128)(2,1)S(1)}, u32[]{:S(2)}, u32[]{:S(2)}) collective-permute-start(bf16[48,2048]{1,0:T(8,128)(2,1)S(1)} %get-tuple-element.30), channel_id=1, source_target_pairs={{0,8},{8,0},{16,24},{24,16},{1,9},{9,1},{17,25},{25,17},{2,10},{10... | collective-permute-start | bytes 589832 | tf_op jit(solution)/shard_map/ppermute | solution.py:37
  69.7 5.7 %collective-permute-start.21 = (bf16[48,2048]{1,0:T(8,128)(2,1)S(1)}, bf16[48,2048]{1,0:T(8,128)(2,1)S(1)}, u32[]{:S(2)}, u32[]{:S(2)}) collective-permute-start(bf16[48,2048]{1,0:T(8,128)(2,1)S(1)} %get-tuple-element.31), channel_id=1, source_target_pairs={{0,16},{8,24},{16,0},{24,8},{1,17},{9,25},{17,1},{25,9},{2,18},{10... | collective-permute-start | bytes 589832 | tf_op jit(solution)/shard_map/ppermute | solution.py:37
  70.9 7.7 %collective-permute-start.23 = (bf16[24,2048]{1,0:T(8,128)(2,1)S(1)}, bf16[24,2048]{1,0:T(8,128)(2,1)S(1)}, u32[]{:S(2)}, u32[]{:S(2)}) collective-permute-start(bf16[24,2048]{1,0:T(8,128)(2,1)S(1)} %get-tuple-element.42), channel_id=1, source_target_pairs={{0,4},{2,6},{4,0},{6,2},{1,5},{3,7},{5,1},{7,3},{8,12},{10,14},{12... | collective-permute-start | bytes 294920 | tf_op jit(solution)/shard_map/ppermute | solution.py:37
  73.9 6.6 %collective-permute-start.24 = (bf16[24,2048]{1,0:T(8,128)(2,1)S(1)}, bf16[24,2048]{1,0:T(8,128)(2,1)S(1)}, u32[]{:S(2)}, u32[]{:S(2)}) collective-permute-start(bf16[24,2048]{1,0:T(8,128)(2,1)S(1)} %get-tuple-element.43), channel_id=1, source_target_pairs={{0,6},{2,4},{4,2},{6,0},{1,7},{3,5},{5,3},{7,1},{8,14},{10,12},{12... | collective-permute-start | bytes 294920 | tf_op jit(solution)/shard_map/ppermute | solution.py:37
  75.5 5.7 %collective-permute-start.22 = (bf16[24,2048]{1,0:T(8,128)(2,1)S(1)}, bf16[24,2048]{1,0:T(8,128)(2,1)S(1)}, u32[]{:S(2)}, u32[]{:S(2)}) collective-permute-start(bf16[24,2048]{1,0:T(8,128)(2,1)S(1)} %slice.156), channel_id=1, source_target_pairs={{0,2},{2,0},{4,6},{6,4},{1,3},{3,1},{5,7},{7,5},{8,10},{10,8},{12,... | collective-permute-start | bytes 294920 | tf_op jit(solution)/shard_map/ppermute | solution.py:37
  81.3 1.3 %collective-permute-start.25 = (bf16[12,2048]{1,0:T(8,128)(2,1)S(1)}, bf16[12,2048]{1,0:T(8,128)(2,1)S(1)}, u32[]{:S(2)}, u32[]{:S(2)}) collective-permute-start(bf16[12,2048]{1,0:T(8,128)(2,1)S(1)} %broadcast_select_fusion.4), channel_id=1, source_target_pairs={{0,1},{1,0},{2,3},{3,2},{4,5},{5,4},{6,7},{7,6},{8,9},{9,8},{10,11... | collective-permute-start | bytes 147464 | tf_op jit(solution)/shard_map/ppermute | solution.py:37

commit v10 on v9

--- a/solution.py
+++ b/solution.py
@@ -7,9 +7,7 @@
 from jax.sharding import Mesh, PartitionSpec as P
 
 LANES = 128
-TOP_LANES = 8
 CHUNK = 1024
-TILE = 512
 VMEM_LIMIT = 12 * 2**20
 GATE_MOST = 5
 
@@ -37,12 +35,6 @@
     return row_major(lax.ppermute(row_major(value), axis, pairs))
 
 
-def split_gates(gates):
-    high = lax.reduce_precision(gates, 8, 7)
-    middle = lax.reduce_precision(gates - high, 8, 7)
-    return [part.astype(jnp.bfloat16) for part in (high, middle, gates - high - middle)]
-
-
 def cut_of(block):
     return block.shape[1] // (2 * LANES) * LANES
 
@@ -67,13 +59,10 @@
     return value.astype(jnp.float32)
 
 
-def with_fourth(blocks):
-    if len(blocks) != 4:
-        return blocks
-    own, one, two, both = blocks
+def with_fourth(blocks, halves):
+    own, one, two = blocks
     cut = cut_of(own)
-    upper = swap(both[:, :cut], "dp", 2)
-    lower = swap(both[:, cut:], "dp", 1)
+    upper, lower = swap(halves[0], "dp", 2), swap(halves[1], "dp", 1)
     one = jnp.concatenate(
         [(wide(one[:, :cut]) + wide(upper)).astype(jnp.bfloat16), one[:, cut:]], 1
     )
@@ -91,7 +80,7 @@
 
 
 def sums_kernel(layout, filling, *refs):
-    widths, block_count = layout
+    widths, block_count, top_count = layout
     refs = list(refs)
     place = refs.pop(0)
     sides = [[[refs.pop(0) for _ in range(block_count)] for _ in widths] for _ in range(2)]
@@ -131,25 +120,20 @@
         for blocks, seg_width in zip(sides[side], widths):
             for low in range(0, seg_width, CHUNK):
                 arrive((side, offset + low))
-
-                @pl.loop(0, CHUNK // TILE)
-                def _(step, blocks=blocks, low=low, at=bases[side] + offset + low):
-                    columns = pl.ds(pl.multiple_of(low + step * TILE, TILE), TILE)
-                    held = [block[:, columns] for block in blocks]
-                    held = held[0] if len(held) == 1 else jnp.concatenate(held, 0)
-                    rows = pl.ds(pl.multiple_of(at + step * TILE, TILE), TILE)
-                    for s in range(per_device):
-                        acc[s] += jnp.dot(held, up[s, rows], preferred_element_type=jnp.float32)
-
+                held = [block[:, low : low + CHUNK] for block in blocks]
+                held = held[0] if len(held) == 1 else jnp.concatenate(held, 0)
+                rows = pl.ds(pl.multiple_of(bases[side] + offset + low, CHUNK), CHUNK)
+                for s in range(per_device):
+                    acc[s] += jnp.dot(held, up[s, rows], preferred_element_type=jnp.float32)
             offset += seg_width
 
     last = widths[-1]
     meta = [block[:, last:].astype(jnp.float32) for block in sides[0][-1]]
     meta = meta[0] if len(meta) == 1 else jnp.concatenate(meta, 0)
-    gates = sum(pltpu.roll(meta, LANES - k * TOP_LANES, 1) for k in (1, 2, 3))
+    gates = sum(pltpu.roll(meta, LANES - k * top_count, 1) for k in (1, 2, 3))
     lanes = lax.broadcasted_iota(jnp.int32, meta.shape, 1)
     for s in range(per_device):
-        chosen = (meta.astype(jnp.int32) == first_expert + s) & (lanes < TOP_LANES)
+        chosen = (meta.astype(jnp.int32) == first_expert + s) & (lanes < top_count)
         own_gate = jnp.sum(jnp.where(chosen, gates, 0.0), 1, keepdims=True)
         gate_half, up_half = acc[s, :, :half_width], acc[s, :, half_width:]
         unit = gate_half * (1.0 / (1.0 + jnp.exp(-gate_half))) * up_half
@@ -157,17 +141,14 @@
 
     arrive("down")
     for base, out in ((bases[1], give_ref), (bases[0], keep_ref)):
-
-        @pl.loop(0, part // TILE)
-        def _(step, base=base, out=out):
-            columns = pl.ds(pl.multiple_of(base + step * TILE, TILE), TILE)
-            target = pl.ds(pl.multiple_of(step * TILE, TILE), TILE)
-            out[:, target] = jnp.dot(
+        for low in range(0, part, CHUNK):
+            columns = pl.ds(pl.multiple_of(base + low, CHUNK), CHUNK)
+            out[:, low : low + CHUNK] = jnp.dot(
                 hidden[...], down[:, columns], preferred_element_type=jnp.float32
             ).astype(jnp.bfloat16)
 
 
-def gated_sums(place, own, other, up, down, filling):
+def gated_sums(place, top_count, own, other, up, down, filling):
     widths = tuple(segment[0].shape[1] for segment in other)
     block_count = len(own[0])
     count = sum(block.shape[0] for block in own[0])
@@ -191,7 +172,7 @@
         weight_specs = [in_vmem] * 2
         moved = 0
     return pl.pallas_call(
-        lambda *refs: sums_kernel((widths, block_count), filling, *refs),
+        lambda *refs: sums_kernel((widths, block_count, top_count), filling, *refs),
         in_specs=[pl.BlockSpec(memory_space=pltpu.SMEM)]
         + [in_vmem] * len(operands)
         + weight_specs,
@@ -205,6 +186,70 @@
             transcendentals=count * down.shape[0],
         ),
     )(place, *operands, *weights)
+
+
+def first_kernel(place, *refs):
+    sources, (keep_ref, give_ref, tokens, ids, gates, turned, sems) = refs[:3], refs[3:]
+    copies = [
+        pltpu.make_async_copy(source, target, sems.at[number])
+        for number, (source, target) in enumerate(zip(sources, (tokens, ids, gates)))
+    ]
+    for copy in copies:
+        copy.start()
+    for copy in copies:
+        copy.wait()
+    core = place[0]
+    part = tokens.shape[1] // 2
+    top_count, rows = ids.shape
+    turned[...] = jnp.zeros_like(turned)
+    left = gates[...]
+    parts = [ids[...].astype(jnp.float32)]
+    for _ in range(3):
+        parts.append(left.astype(jnp.bfloat16).astype(jnp.float32))
+        left = left - parts[-1]
+    for number, values in enumerate(parts):
+        turned[number * top_count : (number + 1) * top_count, :rows] = values
+    routing = turned[...].T[:rows].astype(jnp.bfloat16)
+    for half, out in ((core, keep_ref), (1 - core, give_ref)):
+        out[:, :part] = tokens[:, pl.ds(pl.multiple_of(half * part, LANES), part)]
+        out[:, part:] = routing
+
+
+def first_halves(place, tokens, expert_ids, gate_probs):
+    rows, width = tokens.shape
+    sources = [tokens, expert_ids.T, gate_probs.T]
+    return pl.pallas_call(
+        first_kernel,
+        in_specs=[pl.BlockSpec(memory_space=pltpu.SMEM)]
+        + [pl.BlockSpec(memory_space=pl.ANY)] * 3,
+        out_specs=[pl.BlockSpec(memory_space=pltpu.VMEM)] * 2,
+        out_shape=[pltpu.VMEM((rows, width // 2 + LANES), jnp.bfloat16)] * 2,
+        scratch_shapes=[pltpu.VMEM(x.shape, x.dtype) for x in sources]
+        + [pltpu.VMEM((LANES, LANES), jnp.float32), pltpu.SemaphoreType.DMA((3,))],
+        compiler_params=pltpu.CompilerParams(vmem_limit_bytes=VMEM_LIMIT),
+    )(place, *(pltpu.with_memory_space_constraint(x, pltpu.HBM) for x in sources))
+
+
+def added_kernel(kept_ref, taken_ref, left_ref, right_ref):
+    total = kept_ref[...].astype(jnp.float32) + taken_ref[...].astype(jnp.float32)
+    cut = left_ref.shape[1]
+    left_ref[...] = total[:, :cut].astype(jnp.bfloat16)
+    right_ref[...] = total[:, cut:].astype(jnp.bfloat16)
+
+
+def added(kept, taken, cut):
+    in_vmem = pl.BlockSpec(memory_space=pltpu.VMEM)
+    count, width = kept.shape
+    return pl.pallas_call(
+        added_kernel,
+        in_specs=[in_vmem] * 2,
+        out_specs=[in_vmem] * 2,
+        out_shape=[
+            pltpu.VMEM((count, cut), jnp.bfloat16),
+            pltpu.VMEM((count, width - cut), jnp.bfloat16),
+        ],
+        compiler_params=pltpu.CompilerParams(vmem_limit_bytes=VMEM_LIMIT),
+    )(*(pltpu.with_memory_space_constraint(x, pltpu.VMEM) for x in (kept, taken)))
 
 
 def on_device(tokens, expert_ids, gate_probs, in_weight, out_weight, swap_slot):
@@ -223,13 +268,7 @@
     first_expert = (lax.axis_index("chip") * 2 + core) * per_device
     place = jnp.stack([core, first_expert]).astype(jnp.int32)
 
-    routing = jnp.concatenate(
-        [row_major(expert_ids).astype(jnp.bfloat16), *split_gates(row_major(gate_probs))], 1
-    )
-    routing = row_major(jnp.pad(routing, ((0, 0), (0, LANES - routing.shape[1]))))
-    left, right = tokens[:, :part], tokens[:, part:]
-    keep = jnp.concatenate([jnp.where(first, left, right), routing], 1)
-    give = jnp.concatenate([jnp.where(first, right, left), routing], 1)
+    keep, give = first_halves(place, tokens, expert_ids, gate_probs)
     taken = swap(give, "core", 1)
     chip_rows = row_major(
         jnp.concatenate([jnp.where(first, keep, taken), jnp.where(first, taken, keep)], 0)
@@ -249,33 +288,52 @@
             for i, segment in enumerate(own)
         ]
         other = [[swap(block, "core", 1) for block in segment] for segment in bare]
-        keep, give, *filled = gated_sums(place, own, other, *weights, filling)
+        keep, give, *filled = gated_sums(
+            place, top_count, own, other, *weights, filling
+        )
         return keep, give, filled or weights
 
     def chip_sums(keep, give):
         return (wide(keep) + wide(swap(give, "core", 1))).astype(jnp.bfloat16)
 
     chip_blocks = [chip_rows] + [swap(chip_rows, "chip", j) for j in range(1, chips)]
-    held = [row_major(jnp.concatenate(chip_blocks, 0))]
-    near = spread_near(held[0])
+    direct = [swap(chip_rows, "dp", k) for k in range(1, groups)]
+    far = row_major(jnp.concatenate(chip_blocks[1:], 0))
+    held = row_major(jnp.concatenate([*chip_blocks, *direct], 0))
+    near = spread_near(far)
     weights = (in_weight, out_weight.reshape(per_device * half_width, width))
-    keep, give, weights = sums_of([held], weights, filling=True)
+    keep, give, weights = sums_of([[held]], weights, filling=True)
     near = behind(near, give)
     rest = spread_rest(near)
-    sums = [chip_sums(keep, give)]
+    first_sum = chip_sums(keep, give)
+    own_sum = first_sum[: chips * 2 * rows]
+    direct_sums = [
+        first_sum[low : low + 2 * rows]
+        for low in range(chips * 2 * rows, first_sum.shape[0], 2 * rows)
+    ]
     if rest:
-        keep, give, _ = sums_of([near], weights)
+        near = row_major(jnp.concatenate(near, 0))
+        keep, give, _ = sums_of([[near]], weights)
         pair = chip_sums(keep, give)
-        sums += [pair[: pair.shape[0] // 2], pair[pair.shape[0] // 2 :]]
+        sums = [pair[: far.shape[0]], pair[far.shape[0] :]]
         rest = behind(rest, give)
         keep, give, _ = sums_of([[half] for half in rest], weights)
-        sums += [chip_sums(keep, give)]
+        cut = rest[0].shape[1]
+        diagonal = added(keep, swap(give, "core", 1), cut)
+        diagonal = [
+            jnp.concatenate([block, half], 0)
+            for block, half in zip((direct_sums[2][:, :cut], direct_sums[2][:, cut:]), diagonal)
+        ]
+        sums = [jnp.concatenate([o, s], 0) for o, s in zip(direct_sums, sums)]
+        sums = with_fourth([own_sum, *sums], diagonal)
+        metas = [held, near, rest[1]]
     else:
-        for block in near:
+        sums = [own_sum]
+        for block, o in zip(near, direct_sums):
             keep, give, _ = sums_of([[block]], weights)
-            sums += [chip_sums(keep, give)]
-    metas = [block[:, block.shape[1] - LANES :] for block in held + near + rest[1:]]
-    sums = with_fourth(sums)
+            sums += [jnp.concatenate([o, chip_sums(keep, give)], 0)]
+        metas = [held, *near]
+    metas = [block[:, block.shape[1] - LANES :] for block in metas]
     border = 2 * near_chips * rows
     total = collected([block[border:] for block in sums])
     blocks = [total[low : low + 2 * rows] for low in range(0, total.shape[0], 2 * rows)]

time: 83.6 us -> 90 us (1.077)
  local copies, waits for them, and re-layouts: 1.93 us -> 16.2 us
  Pallas kernels: 23 us -> 17.6 us
  starting transfers between devices: 26.2 us -> 25 us
  other arithmetic: 5.97 us -> 4.91 us
    unnamed x4 -> x16, local copies, waits for them, and re-layouts: 1.54 us -> 15 us
    pallas_call x3 -> x5, Pallas kernels: 23 us -> 17.6 us  [the longest x3 16 us: gated_sums(): pl.pallas_call(lambda *refs: sums_kernel((widths, block_count, top_count)...]
    ppermute x26 -> x28, starting transfers between devices: 26.2 us -> 25 us  [swap(): return row_major(lax.ppermute(row_major(value), axis, pairs))]
    ppermute x26 -> x28, waiting for transfers between devices: 25.2 us -> 25 us  [swap(): return row_major(lax.ppermute(row_major(value), axis, pairs))]
    convert_element_type x3 -> x2, other arithmetic: 2.58 us -> 2.54 us  [chip_sums(): return (wide(keep) + wide(swap(give, 'core', 1))).astype(jnp.bfloat16)]
  transfers between devices with their start and end apart: 26 -> 28, of which waited for: 16 -> 12; matrix products, arithmetic and copies ran while one was open for 5% -> 5% of each run, Pallas kernels for 28% -> 18%
where the time goes in v10:
time: 90 us; the launch traced here: 89.7 us
  starting transfers between devices  25 us (28%)
  waiting for transfers between devices  25 us (28%)
  Pallas kernels  17.6 us (20%)
  local copies, waits for them, and re-layouts  16.2 us (18%)
  other arithmetic  4.91 us (5%)
  between operations  1.03 us (1%)
    ppermute x28, starting transfers between devices, swap(): return row_major(lax.ppermute(row_major(value), axis, pairs))  25 us
    ppermute x28, waiting for transfers between devices, swap(): return row_major(lax.ppermute(row_major(value), axis, pairs))  25 us
    pallas_call x3, Pallas kernels, gated_sums(): pl.pallas_call(lambda *refs: sums_kernel((widths, block_count, top_count)...  16 us
    unnamed x16, local copies, waits for them, and re-layouts  15 us
    convert_element_type x2, other arithmetic, chip_sums(): return (wide(keep) + wide(swap(give, 'core', 1))).astype(jnp.bfloat16)  2.54 us
  transfers between devices with their start and end apart: 28, of which 12 were waited for; matrix products, arithmetic and copies ran while one was open for 5% of the time, Pallas kernels for 18%

profile of v10, /device:TPU:0, one launch (start us, length us, event | category | flops | bytes accessed | tf_op | source)
XLA Modules:
  0.0 89.7 jit_solution(12390075348468026057)
XLA Ops:
  0.7 1.6 %shard_map.77 = (bf16[12,2176]{1,0:T(8,128)(2,1)S(1)}, bf16[12,2176]{1,0:T(8,128)(2,1)S(1)}) custom-call(s32[2]{0:T(128)S(1)} %pad_add_fusion.place.refs_0_, bf16[12,4096]{1,0:T(8,128)(2,1)} %refs_0_.1, s32[8,12]{1,0:T(8,128)} %bitcast.6, f32[8,12]{1,0:T(8,128)} %bitcast.7), custom_call_target="tpu_custom_call" | custom-call | tf_op jit(solution)/shard_map/pallas_call | solution.py:221
  2.3 0.5 collective-permute-start
  2.8 0.9 %collective-permute-done = bf16[12,2176]{1,0:T(8,128)(2,1)S(1)} collective-permute-done((bf16[12,2176]{1,0:T(8,128)(2,1)S(1)}, bf16[12,2176]{1,0:T(8,128)(2,1)S(1)}, u32[]{:S(2)}, u32[]{:S(2)}) %collective-permute-start) | collective-permute-done | bytes 52256 | tf_op jit(solution)/shard_map/ppermute | solution.py:35
  3.8 3.0 %collective-permute-start.1 = (bf16[24,2176]{1,0:T(8,128)(2,1)S(1)}, bf16[24,2176]{1,0:T(8,128)(2,1)S(1)}, u32[]{:S(2)}, u32[]{:S(2)}) collective-permute-start(bf16[24,2176]{1,0:T(8,128)(2,1)S(1)} %get-tuple-element.41), channel_id=1, source_target_pairs={{0,2},{2,0},{4,6},{6,4},{1,3},{3,1},{5,7},{7,5},{8,10},{10,8},{12,... | collective-permute-start | bytes 313352 | tf_op jit(solution)/shard_map/ppermute | solution.py:35
  6.8 2.5 %collective-permute-start.3 = (bf16[24,2176]{1,0:T(8,128)(2,1)S(1)}, bf16[24,2176]{1,0:T(8,128)(2,1)S(1)}, u32[]{:S(2)}, u32[]{:S(2)}) collective-permute-start(bf16[24,2176]{1,0:T(8,128)(2,1)S(1)} %get-tuple-element.41), channel_id=1, source_target_pairs={{0,6},{2,4},{4,2},{6,0},{1,7},{3,5},{5,3},{7,1},{8,14},{10,12},{12... | collective-permute-start | bytes 313352 | tf_op jit(solution)/shard_map/ppermute | solution.py:35
  9.3 2.4 %collective-permute-start.6 = (bf16[24,2176]{1,0:T(8,128)(2,1)S(1)}, bf16[24,2176]{1,0:T(8,128)(2,1)S(1)}, u32[]{:S(2)}, u32[]{:S(2)}) collective-permute-start(bf16[24,2176]{1,0:T(8,128)(2,1)S(1)} %get-tuple-element.41), channel_id=1, source_target_pairs={{0,24},{8,16},{16,8},{24,0},{1,25},{9,17},{17,9},{25,1},{2,26},{10... | collective-permute-start | bytes 313352 | tf_op jit(solution)/shard_map/ppermute | solution.py:35
  11.8 0.5 collective-permute-start.5
  12.3 0.5 collective-permute-start.4
  12.9 6.2 %collective-permute-done.2 = bf16[24,2176]{1,0:T(8,128)(2,1)S(1)} collective-permute-done((bf16[24,2176]{1,0:T(8,128)(2,1)S(1)}, bf16[24,2176]{1,0:T(8,128)(2,1)S(1)}, u32[]{:S(2)}, u32[]{:S(2)}) %collective-permute-start.2) | collective-permute-done | bytes 104480 | tf_op jit(solution)/shard_map/ppermute | solution.py:35
  19.3 1.6 %collective-permute-start.9 = (bf16[72,2176]{1,0:T(8,128)(2,1)S(1)}, bf16[72,2176]{1,0:T(8,128)(2,1)S(1)}, u32[]{:S(2)}, u32[]{:S(2)}) collective-permute-start(bf16[72,2176]{1,0:T(8,128)(2,1)S(1)} %get-tuple-element.59), channel_id=1, source_target_pairs={{0,8},{8,0},{16,24},{24,16},{1,9},{9,1},{17,25},{25,17},{2,10},{10... | collective-permute-start | bytes 940040 | tf_op jit(solution)/shard_map/ppermute | solution.py:35
  20.9 1.5 %collective-permute-start.10 = (bf16[72,2176]{1,0:T(8,128)(2,1)S(1)}, bf16[72,2176]{1,0:T(8,128)(2,1)S(1)}, u32[]{:S(2)}, u32[]{:S(2)}) collective-permute-start(bf16[72,2176]{1,0:T(8,128)(2,1)S(1)} %get-tuple-element.59), channel_id=1, source_target_pairs={{0,16},{8,24},{16,0},{24,8},{1,17},{9,25},{17,1},{25,9},{2,18},{10... | collective-permute-start | bytes 940040 | tf_op jit(solution)/shard_map/ppermute | solution.py:35
  22.4 8.4 %shard_map.78 = (bf16[168,2048]{1,0:T(8,128)(2,1)S(1)}, bf16[168,2048]{1,0:T(8,128)(2,1)S(1)}, bf16[2,4096,768]{2,1,0:T(8,128)(2,1)S(1)}, bf16[768,4096]{1,0:T(8,128)(2,1)S(1)}) custom-call(s32[2]{0:T(128)S(1)} %pad_add_fusion.place.refs_0_, bf16[168,2176]{1,0:T(8,128)(2,1)S(1)} %constant_dynamic-update-slice_fusion.refs_1_, ...), custom_call_target="tpu_custom_call" | custom-call | flops 3170893824 | bytes 18874368 | tf_op jit(solution)/shard_map/pallas_call | solution.py:174
  31.1 0.4 copy-done.4
  31.6 0.2 collective-permute-start.8
  31.8 1.0 %collective-permute-start.13 = (bf16[72,1024]{1,0:T(8,128)(2,1)S(1)}, bf16[72,1024]{1,0:T(8,128)(2,1)S(1)}, u32[]{:S(2)}, u32[]{:S(2)}) collective-permute-start(bf16[72,1024]{1,0:T(8,128)(2,1)S(1)} %slice.115), channel_id=1, source_target_pairs={{0,16},{8,24},{16,0},{24,8},{1,17},{9,25},{17,1},{25,9},{2,18},{10... | collective-permute-start | bytes 442376 | tf_op jit(solution)/shard_map/ppermute | solution.py:35
  32.8 1.1 %collective-permute-start.14 = (bf16[72,1152]{1,0:T(8,128)(2,1)S(1)}, bf16[72,1152]{1,0:T(8,128)(2,1)S(1)}, u32[]{:S(2)}, u32[]{:S(2)}) collective-permute-start(bf16[72,1152]{1,0:T(8,128)(2,1)S(1)} %slice.116), channel_id=1, source_target_pairs={{0,8},{8,0},{16,24},{24,16},{1,9},{9,1},{17,25},{25,17},{2,10},{10... | collective-permute-start | bytes 497672 | tf_op jit(solution)/shard_map/ppermute | solution.py:35
  33.9 3.5 %shard_map.79 = (bf16[144,2048]{1,0:T(8,128)(2,1)S(1)}, bf16[144,2048]{1,0:T(8,128)(2,1)S(1)}) custom-call(s32[2]{0:T(128)S(1)} %pad_add_fusion.place.refs_0_, bf16[144,2176]{1,0:T(8,128)(2,1)S(1)} %constant_dynamic-update-slice_fusion.10.refs_1_, bf16[144,2048]{1,0:T(8,128)(2,1)S(1)} %collective-permute-done.11.refs_2_, ...), custom_call_target="tpu_custom_call" | custom-call | flops 2717908992 | tf_op jit(solution)/shard_map/pallas_call | solution.py:174
  37.5 4.5 %copy-done = bf16[2,4096,768]{2,1,0:T(8,128)(2,1)} copy-done((bf16[2,4096,768]{2,1,0:T(8,128)(2,1)}, bf16[2,4096,768]{2,1,0:T(8,128)(2,1)S(1)}, u32[]{:S(2)}) %copy-start) | copy-done | bytes 12582936
  42.0 2.6 %copy-done.2 = bf16[768,4096]{1,0:T(8,128)(2,1)} copy-done((bf16[768,4096]{1,0:T(8,128)(2,1)}, bf16[768,4096]{1,0:T(8,128)(2,1)S(1)}, u32[]{:S(2)}) %copy-start.2) | copy-done | bytes 6291480
  44.6 0.7 slice.117
  45.3 0.5 collective-permute-start.16
  46.2 0.2 select_reduce_fusion
  46.4 1.3 %add_convert_fusion = bf16[168,2048]{1,0:T(8,128)(2,1)S(1)} fusion(bf16[168,2048]{1,0:T(8,128)(2,1)} %collective-permute-done.8, bf16[168,2048]{1,0:T(8,128)(2,1)S(1)} %get-tuple-element.23), kind=kLoop, calls=%fused_computation | loop fusion | flops 1376256 | bytes 2064384 | tf_op jit(solution)/shard_map/convert_element_type | solution.py:297
  47.7 4.6 %copy-done.1 = bf16[2,4096,768]{2,1,0:T(8,128)(2,1)S(1)} copy-done((bf16[2,4096,768]{2,1,0:T(8,128)(2,1)S(1)}, bf16[2,4096,768]{2,1,0:T(8,128)(2,1)}, u32[]{:S(2)}) %copy-start.1) | copy-done | bytes 12582936
  52.3 2.8 %copy-done.3 = bf16[768,4096]{1,0:T(8,128)(2,1)S(1)} copy-done((bf16[768,4096]{1,0:T(8,128)(2,1)S(1)}, bf16[768,4096]{1,0:T(8,128)(2,1)}, u32[]{:S(2)}) %copy-start.3) | copy-done | bytes 6291480
  55.1 4.0 %shard_map.80 = (bf16[72,2048]{1,0:T(8,128)(2,1)S(1)}, bf16[72,2048]{1,0:T(8,128)(2,1)S(1)}) custom-call(s32[2]{0:T(128)S(1)} %pad_add_fusion.place.refs_0_, bf16[72,1024]{1,0:T(8,128)(2,1)S(1)} %collective-permute-done.13.refs_1_, bf16[72,1152]{1,0:T(8,128)(2,1)S(1)} %collective-permute-done.14.refs_2_, ...), custom_call_target="tpu_custom_call" | custom-call | flops 1358954496 | tf_op jit(solution)/shard_map/pallas_call | solution.py:174
  59.1 0.6 collective-permute-start.17
  59.7 1.2 %collective-permute-done.17.taken_ref = bf16[72,2048]{1,0:T(8,128)(2,1)S(1)} collective-permute-done((bf16[72,2048]{1,0:T(8,128)(2,1)S(1)}, bf16[72,2048]{1,0:T(8,128)(2,1)S(1)}, u32[]{:S(2)}, u32[]{:S(2)}) %collective-permute-start.17) | collective-permute-done | bytes 294944 | tf_op jit(solution)/shard_map/ppermute | solution.py:35
  61.0 1.0 %collective-permute-start.19 = (bf16[96,1024]{1,0:T(8,128)(2,1)S(1)}, bf16[96,1024]{1,0:T(8,128)(2,1)S(1)}, u32[]{:S(2)}, u32[]{:S(2)}) collective-permute-start(bf16[96,1024]{1,0:T(8,128)(2,1)S(1)} %pad_maximum_fusion.3), channel_id=1, source_target_pairs={{0,8},{8,0},{16,24},{24,16},{1,9},{9,1},{17,25},{25,17},{2,10},{10... | collective-permute-start | bytes 589832 | tf_op jit(solution)/shard_map/ppermute | solution.py:35
  62.0 1.1 %collective-permute-start.18 = (bf16[96,1024]{1,0:T(8,128)(2,1)S(1)}, bf16[96,1024]{1,0:T(8,128)(2,1)S(1)}, u32[]{:S(2)}, u32[]{:S(2)}) collective-permute-start(bf16[96,1024]{1,0:T(8,128)(2,1)S(1)} %pad_maximum_fusion.2), channel_id=1, source_target_pairs={{0,16},{8,24},{16,0},{24,8},{1,17},{9,25},{17,1},{25,9},{2,18},{10... | collective-permute-start | bytes 589832 | tf_op jit(solution)/shard_map/ppermute | solution.py:35
  63.1 1.2 %add_convert_fusion.1 = bf16[144,2048]{1,0:T(8,128)(2,1)S(1)} fusion(bf16[144,2048]{1,0:T(8,128)(2,1)} %collective-permute-done.12, bf16[144,2048]{1,0:T(8,128)(2,1)S(1)} %get-tuple-element.29), kind=kLoop, calls=%fused_computation.1 | loop fusion | flops 1179648 | bytes 1769472 | tf_op jit(solution)/shard_map/convert_element_type | solution.py:297
  64.3 3.9 %collective-permute-done.19 = bf16[96,1024]{1,0:T(8,128)(2,1)S(1)} collective-permute-done((bf16[96,1024]{1,0:T(8,128)(2,1)S(1)}, bf16[96,1024]{1,0:T(8,128)(2,1)S(1)}, u32[]{:S(2)}, u32[]{:S(2)}) %collective-permute-start.19) | collective-permute-done | bytes 196640 | tf_op jit(solution)/shard_map/ppermute | solution.py:35
  68.2 0.7 collective-permute-done.18
  69.2 1.1 %collective-permute-start.21 = (bf16[48,2048]{1,0:T(8,128)(2,1)S(1)}, bf16[48,2048]{1,0:T(8,128)(2,1)S(1)}, u32[]{:S(2)}, u32[]{:S(2)}) collective-permute-start(bf16[48,2048]{1,0:T(8,128)(2,1)S(1)} %get-tuple-element.49), channel_id=1, source_target_pairs={{0,16},{8,24},{16,0},{24,8},{1,17},{9,25},{17,1},{25,9},{2,18},{10... | collective-permute-start | bytes 589832 | tf_op jit(solution)/shard_map/ppermute | solution.py:35
  70.2 0.6 collective-permute-start.20
  70.9 4.4 %collective-permute-done.21 = bf16[48,2048]{1,0:T(8,128)(2,1)S(1)} collective-permute-done((bf16[48,2048]{1,0:T(8,128)(2,1)S(1)}, bf16[48,2048]{1,0:T(8,128)(2,1)S(1)}, u32[]{:S(2)}, u32[]{:S(2)}) %collective-permute-start.21) | collective-permute-done | bytes 196640 | tf_op jit(solution)/shard_map/ppermute | solution.py:35
  75.3 0.7 collective-permute-done.20
  76.1 0.7 collective-permute-start.22
  76.8 1.5 %collective-permute-start.23 = (bf16[48,2048]{1,0:T(8,128)(2,1)S(1)}, bf16[48,2048]{1,0:T(8,128)(2,1)S(1)}, u32[]{:S(2)}, u32[]{:S(2)}) collective-permute-start(bf16[48,2048]{1,0:T(8,128)(2,1)S(1)} %get-tuple-element.39), channel_id=1, source_target_pairs={{0,16},{8,24},{16,0},{24,8},{1,17},{9,25},{17,1},{25,9},{2,18},{10... | collective-permute-start | bytes 589832 | tf_op jit(solution)/shard_map/ppermute | solution.py:35
  78.3 0.5 collective-permute-start.25
  78.8 2.3 %collective-permute-start.26 = (bf16[24,2048]{1,0:T(8,128)(2,1)S(1)}, bf16[24,2048]{1,0:T(8,128)(2,1)S(1)}, u32[]{:S(2)}, u32[]{:S(2)}) collective-permute-start(bf16[24,2048]{1,0:T(8,128)(2,1)S(1)} %get-tuple-element.53), channel_id=1, source_target_pairs={{0,6},{2,4},{4,2},{6,0},{1,7},{3,5},{5,3},{7,1},{8,14},{10,12},{12... | collective-permute-start | bytes 294920 | tf_op jit(solution)/shard_map/ppermute | solution.py:35
  81.1 0.7 collective-permute-done.22
  81.8 0.6 collective-permute-done.23
  82.7 4.1 %collective-permute-done.25 = bf16[24,2048]{1,0:T(8,128)(2,1)S(1)} collective-permute-done((bf16[24,2048]{1,0:T(8,128)(2,1)S(1)}, bf16[24,2048]{1,0:T(8,128)(2,1)S(1)}, u32[]{:S(2)}, u32[]{:S(2)}) %collective-permute-start.25) | collective-permute-done | bytes 98336 | tf_op jit(solution)/shard_map/ppermute | solution.py:35
  86.8 0.8 collective-permute-done.24
  87.8 0.5 broadcast_multiply_fusion
  88.3 0.7 collective-permute-done.27
  89.0 0.7 pad_maximum_fusion.4
  (75 shorter events, 2.2 us)
Async XLA Ops:
  2.3 1.4 %collective-permute-start = (bf16[12,2176]{1,0:T(8,128)(2,1)S(1)}, bf16[12,2176]{1,0:T(8,128)(2,1)S(1)}, u32[]{:S(2)}, u32[]{:S(2)}) collective-permute-start(bf16[12,2176]{1,0:T(8,128)(2,1)S(1)} %get-tuple-element.22), channel_id=1, source_target_pairs={{0,1},{1,0},{2,3},{3,2},{4,5},{5,4},{6,7},{7,6},{8,9},{9,8},{10,11... | collective-permute-start | bytes 156680 | tf_op jit(solution)/shard_map/ppermute | solution.py:35
  3.8 8.5 %collective-permute-start.1 = (bf16[24,2176]{1,0:T(8,128)(2,1)S(1)}, bf16[24,2176]{1,0:T(8,128)(2,1)S(1)}, u32[]{:S(2)}, u32[]{:S(2)}) collective-permute-start(bf16[24,2176]{1,0:T(8,128)(2,1)S(1)} %get-tuple-element.41), channel_id=1, source_target_pairs={{0,2},{2,0},{4,6},{6,4},{1,3},{3,1},{5,7},{7,5},{8,10},{10,8},{12,... | collective-permute-start | bytes 313352 | tf_op jit(solution)/shard_map/ppermute | solution.py:35
  6.8 12.3 %collective-permute-start.3 = (bf16[24,2176]{1,0:T(8,128)(2,1)S(1)}, bf16[24,2176]{1,0:T(8,128)(2,1)S(1)}, u32[]{:S(2)}, u32[]{:S(2)}) collective-permute-start(bf16[24,2176]{1,0:T(8,128)(2,1)S(1)} %get-tuple-element.41), channel_id=1, source_target_pairs={{0,6},{2,4},{4,2},{6,0},{1,7},{3,5},{5,3},{7,1},{8,14},{10,12},{12... | collective-permute-start | bytes 313352 | tf_op jit(solution)/shard_map/ppermute | solution.py:35
  9.2 9.8 %collective-permute-start.2 = (bf16[24,2176]{1,0:T(8,128)(2,1)S(1)}, bf16[24,2176]{1,0:T(8,128)(2,1)S(1)}, u32[]{:S(2)}, u32[]{:S(2)}) collective-permute-start(bf16[24,2176]{1,0:T(8,128)(2,1)S(1)} %get-tuple-element.41), channel_id=1, source_target_pairs={{0,4},{2,6},{4,0},{6,2},{1,5},{3,7},{5,1},{7,3},{8,12},{10,14},{12... | collective-permute-start | bytes 313352 | tf_op jit(solution)/shard_map/ppermute | solution.py:35
  9.3 9.8 %collective-permute-start.6 = (bf16[24,2176]{1,0:T(8,128)(2,1)S(1)}, bf16[24,2176]{1,0:T(8,128)(2,1)S(1)}, u32[]{:S(2)}, u32[]{:S(2)}) collective-permute-start(bf16[24,2176]{1,0:T(8,128)(2,1)S(1)} %get-tuple-element.41), channel_id=1, source_target_pairs={{0,24},{8,16},{16,8},{24,0},{1,25},{9,17},{17,9},{25,1},{2,26},{10... | collective-permute-start | bytes 313352 | tf_op jit(solution)/shard_map/ppermute | solution.py:35
  11.8 7.3 %collective-permute-start.5 = (bf16[24,2176]{1,0:T(8,128)(2,1)S(1)}, bf16[24,2176]{1,0:T(8,128)(2,1)S(1)}, u32[]{:S(2)}, u32[]{:S(2)}) collective-permute-start(bf16[24,2176]{1,0:T(8,128)(2,1)S(1)} %get-tuple-element.41), channel_id=1, source_target_pairs={{0,16},{8,24},{16,0},{24,8},{1,17},{9,25},{17,1},{25,9},{2,18},{10... | collective-permute-start | bytes 313352 | tf_op jit(solution)/shard_map/ppermute | solution.py:35
  12.3 6.8 %collective-permute-start.4 = (bf16[24,2176]{1,0:T(8,128)(2,1)S(1)}, bf16[24,2176]{1,0:T(8,128)(2,1)S(1)}, u32[]{:S(2)}, u32[]{:S(2)}) collective-permute-start(bf16[24,2176]{1,0:T(8,128)(2,1)S(1)} %get-tuple-element.41), channel_id=1, source_target_pairs={{0,8},{8,0},{16,24},{24,16},{1,9},{9,1},{17,25},{25,17},{2,10},{10... | collective-permute-start | bytes 313352 | tf_op jit(solution)/shard_map/ppermute | solution.py:35
  19.3 3.2 %collective-permute-start.7 = (bf16[168,2048]{1,0:T(8,128)(2,1)S(1)}, bf16[168,2048]{1,0:T(8,128)(2,1)S(1)}, u32[]{:S(2)}, u32[]{:S(2)}) collective-permute-start(bf16[168,2048]{1,0:T(8,128)(2,1)S(1)} %slice.142), channel_id=1, source_target_pairs={{0,1},{1,0},{2,3},{3,2},{4,5},{5,4},{6,7},{7,6},{8,9},{9,8},{10,11... | collective-permute-start | bytes 2064392 | tf_op jit(solution)/shard_map/ppermute | solution.py:35
  19.3 11.5 %collective-permute-start.9 = (bf16[72,2176]{1,0:T(8,128)(2,1)S(1)}, bf16[72,2176]{1,0:T(8,128)(2,1)S(1)}, u32[]{:S(2)}, u32[]{:S(2)}) collective-permute-start(bf16[72,2176]{1,0:T(8,128)(2,1)S(1)} %get-tuple-element.59), channel_id=1, source_target_pairs={{0,8},{8,0},{16,24},{24,16},{1,9},{9,1},{17,25},{25,17},{2,10},{10... | collective-permute-start | bytes 940040 | tf_op jit(solution)/shard_map/ppermute | solution.py:35
  20.9 10.0 %collective-permute-start.10 = (bf16[72,2176]{1,0:T(8,128)(2,1)S(1)}, bf16[72,2176]{1,0:T(8,128)(2,1)S(1)}, u32[]{:S(2)}, u32[]{:S(2)}) collective-permute-start(bf16[72,2176]{1,0:T(8,128)(2,1)S(1)} %get-tuple-element.59), channel_id=1, source_target_pairs={{0,16},{8,24},{16,0},{24,8},{1,17},{9,25},{17,1},{25,9},{2,18},{10... | collective-permute-start | bytes 940040 | tf_op jit(solution)/shard_map/ppermute | solution.py:35
  30.8 0.7 copy-start.4
  31.0 2.9 %collective-permute-start.11 = (bf16[144,2048]{1,0:T(8,128)(2,1)S(1)}, bf16[144,2048]{1,0:T(8,128)(2,1)S(1)}, u32[]{:S(2)}, u32[]{:S(2)}) collective-permute-start(bf16[144,2048]{1,0:T(8,128)(2,1)S(1)} %slice.145), channel_id=1, source_target_pairs={{0,1},{1,0},{2,3},{3,2},{4,5},{5,4},{6,7},{7,6},{8,9},{9,8},{10,11... | collective-permute-start | bytes 1769480 | tf_op jit(solution)/shard_map/ppermute | solution.py:35
  31.6 14.7 %collective-permute-start.8 = (bf16[168,2048]{1,0:T(8,128)(2,1)S(1)}, bf16[168,2048]{1,0:T(8,128)(2,1)}, u32[]{:S(2)}, u32[]{:S(2)}) collective-permute-start(bf16[168,2048]{1,0:T(8,128)(2,1)S(1)} %get-tuple-element.24), channel_id=1, source_target_pairs={{0,1},{1,0},{2,3},{3,2},{4,5},{5,4},{6,7},{7,6},{8,9},{9,8},{10,11... | collective-permute-start | bytes 2064392 | tf_op jit(solution)/shard_map/ppermute | solution.py:35
  31.8 12.8 %collective-permute-start.13 = (bf16[72,1024]{1,0:T(8,128)(2,1)S(1)}, bf16[72,1024]{1,0:T(8,128)(2,1)S(1)}, u32[]{:S(2)}, u32[]{:S(2)}) collective-permute-start(bf16[72,1024]{1,0:T(8,128)(2,1)S(1)} %slice.115), channel_id=1, source_target_pairs={{0,16},{8,24},{16,0},{24,8},{1,17},{9,25},{17,1},{25,9},{2,18},{10... | collective-permute-start | bytes 442376 | tf_op jit(solution)/shard_map/ppermute | solution.py:35
  32.8 11.8 %collective-permute-start.14 = (bf16[72,1152]{1,0:T(8,128)(2,1)S(1)}, bf16[72,1152]{1,0:T(8,128)(2,1)S(1)}, u32[]{:S(2)}, u32[]{:S(2)}) collective-permute-start(bf16[72,1152]{1,0:T(8,128)(2,1)S(1)} %slice.116), channel_id=1, source_target_pairs={{0,8},{8,0},{16,24},{24,16},{1,9},{9,1},{17,25},{25,17},{2,10},{10... | collective-permute-start | bytes 497672 | tf_op jit(solution)/shard_map/ppermute | solution.py:35
  37.5 4.5 %copy-start = (bf16[2,4096,768]{2,1,0:T(8,128)(2,1)}, bf16[2,4096,768]{2,1,0:T(8,128)(2,1)S(1)}, u32[]{:S(2)}) copy-start(bf16[2,4096,768]{2,1,0:T(8,128)(2,1)S(1)} %get-tuple-element.27.refs_3_.refs_5_) | copy-start | bytes 37748740
  42.0 2.6 %copy-start.2 = (bf16[768,4096]{1,0:T(8,128)(2,1)}, bf16[768,4096]{1,0:T(8,128)(2,1)S(1)}, u32[]{:S(2)}) copy-start(bf16[768,4096]{1,0:T(8,128)(2,1)S(1)} %get-tuple-element.28.refs_4_.refs_6_) | copy-start | bytes 18874372
  45.3 17.8 %collective-permute-start.12 = (bf16[144,2048]{1,0:T(8,128)(2,1)S(1)}, bf16[144,2048]{1,0:T(8,128)(2,1)}, u32[]{:S(2)}, u32[]{:S(2)}) collective-permute-start(bf16[144,2048]{1,0:T(8,128)(2,1)S(1)} %get-tuple-element.30), channel_id=1, source_target_pairs={{0,1},{1,0},{2,3},{3,2},{4,5},{5,4},{6,7},{7,6},{8,9},{9,8},{10,11... | collective-permute-start | bytes 1769480 | tf_op jit(solution)/shard_map/ppermute | solution.py:35
  45.3 2.4 %collective-permute-start.16 = (bf16[72,1024]{1,0:T(8,128)(2,1)}, bf16[72,1024]{1,0:T(8,128)(2,1)S(1)}, u32[]{:S(2)}, u32[]{:S(2)}) collective-permute-start(bf16[72,1024]{1,0:T(8,128)(2,1)} %slice.117), channel_id=1, source_target_pairs={{0,1},{1,0},{2,3},{3,2},{4,5},{5,4},{6,7},{7,6},{8,9},{9,8},{10,11... | collective-permute-start | bytes 442376 | tf_op jit(solution)/shard_map/ppermute | solution.py:35
  45.8 1.9 %collective-permute-start.15 = (bf16[72,1024]{1,0:T(8,128)(2,1)S(1)}, bf16[72,1024]{1,0:T(8,128)(2,1)S(1)}, u32[]{:S(2)}, u32[]{:S(2)}) collective-permute-start(bf16[72,1024]{1,0:T(8,128)(2,1)S(1)} %collective-permute-done.13.refs_1_), channel_id=1, source_target_pairs={{0,1},{1,0},{2,3},{3,2},{4,5},{5,4},{6,7},{7,6},{8,9},{9,8},{10,11... | collective-permute-start | bytes 442376 | tf_op jit(solution)/shard_map/ppermute | solution.py:35
  47.7 4.6 %copy-start.1 = (bf16[2,4096,768]{2,1,0:T(8,128)(2,1)S(1)}, bf16[2,4096,768]{2,1,0:T(8,128)(2,1)}, u32[]{:S(2)}) copy-start(bf16[2,4096,768]{2,1,0:T(8,128)(2,1)} %copy-done) | copy-start | bytes 37748740
  52.3 2.8 %copy-start.3 = (bf16[768,4096]{1,0:T(8,128)(2,1)S(1)}, bf16[768,4096]{1,0:T(8,128)(2,1)}, u32[]{:S(2)}) copy-start(bf16[768,4096]{1,0:T(8,128)(2,1)} %copy-done.2) | copy-start | bytes 18874372
  59.1 1.8 %collective-permute-start.17 = (bf16[72,2048]{1,0:T(8,128)(2,1)S(1)}, bf16[72,2048]{1,0:T(8,128)(2,1)S(1)}, u32[]{:S(2)}, u32[]{:S(2)}) collective-permute-start(bf16[72,2048]{1,0:T(8,128)(2,1)S(1)} %get-tuple-element.34), channel_id=1, source_target_pairs={{0,1},{1,0},{2,3},{3,2},{4,5},{5,4},{6,7},{7,6},{8,9},{9,8},{10,11... | collective-permute-start | bytes 884744 | tf_op jit(solution)/shard_map/ppermute | solution.py:35
  61.0 7.2 %collective-permute-start.19 = (bf16[96,1024]{1,0:T(8,128)(2,1)S(1)}, bf16[96,1024]{1,0:T(8,128)(2,1)S(1)}, u32[]{:S(2)}, u32[]{:S(2)}) collective-permute-start(bf16[96,1024]{1,0:T(8,128)(2,1)S(1)} %pad_maximum_fusion.3), channel_id=1, source_target_pairs={{0,8},{8,0},{16,24},{24,16},{1,9},{9,1},{17,25},{25,17},{2,10},{10... | collective-permute-start | bytes 589832 | tf_op jit(solution)/shard_map/ppermute | solution.py:35
  62.0 7.0 %collective-permute-start.18 = (bf16[96,1024]{1,0:T(8,128)(2,1)S(1)}, bf16[96,1024]{1,0:T(8,128)(2,1)S(1)}, u32[]{:S(2)}, u32[]{:S(2)}) collective-permute-start(bf16[96,1024]{1,0:T(8,128)(2,1)S(1)} %pad_maximum_fusion.2), channel_id=1, source_target_pairs={{0,16},{8,24},{16,0},{24,8},{1,17},{9,25},{17,1},{25,9},{2,18},{10... | collective-permute-start | bytes 589832 | tf_op jit(solution)/shard_map/ppermute | solution.py:35
  69.2 6.1 %collective-permute-start.21 = (bf16[48,2048]{1,0:T(8,128)(2,1)S(1)}, bf16[48,2048]{1,0:T(8,128)(2,1)S(1)}, u32[]{:S(2)}, u32[]{:S(2)}) collective-permute-start(bf16[48,2048]{1,0:T(8,128)(2,1)S(1)} %get-tuple-element.49), channel_id=1, source_target_pairs={{0,16},{8,24},{16,0},{24,8},{1,17},{9,25},{17,1},{25,9},{2,18},{10... | collective-permute-start | bytes 589832 | tf_op jit(solution)/shard_map/ppermute | solution.py:35
  70.2 5.8 %collective-permute-start.20 = (bf16[48,2048]{1,0:T(8,128)(2,1)S(1)}, bf16[48,2048]{1,0:T(8,128)(2,1)S(1)}, u32[]{:S(2)}, u32[]{:S(2)}) collective-permute-start(bf16[48,2048]{1,0:T(8,128)(2,1)S(1)} %get-tuple-element.51), channel_id=1, source_target_pairs={{0,8},{8,0},{16,24},{24,16},{1,9},{9,1},{17,25},{25,17},{2,10},{10... | collective-permute-start | bytes 589832 | tf_op jit(solution)/shard_map/ppermute | solution.py:35
  76.1 5.7 %collective-permute-start.22 = (bf16[48,2048]{1,0:T(8,128)(2,1)S(1)}, bf16[48,2048]{1,0:T(8,128)(2,1)S(1)}, u32[]{:S(2)}, u32[]{:S(2)}) collective-permute-start(bf16[48,2048]{1,0:T(8,128)(2,1)S(1)} %get-tuple-element.38), channel_id=1, source_target_pairs={{0,8},{8,0},{16,24},{24,16},{1,9},{9,1},{17,25},{25,17},{2,10},{10... | collective-permute-start | bytes 589832 | tf_op jit(solution)/shard_map/ppermute | solution.py:35
  76.8 5.7 %collective-permute-start.23 = (bf16[48,2048]{1,0:T(8,128)(2,1)S(1)}, bf16[48,2048]{1,0:T(8,128)(2,1)S(1)}, u32[]{:S(2)}, u32[]{:S(2)}) collective-permute-start(bf16[48,2048]{1,0:T(8,128)(2,1)S(1)} %get-tuple-element.39), channel_id=1, source_target_pairs={{0,16},{8,24},{16,0},{24,8},{1,17},{9,25},{17,1},{25,9},{2,18},{10... | collective-permute-start | bytes 589832 | tf_op jit(solution)/shard_map/ppermute | solution.py:35
  78.3 8.5 %collective-permute-start.25 = (bf16[24,2048]{1,0:T(8,128)(2,1)S(1)}, bf16[24,2048]{1,0:T(8,128)(2,1)S(1)}, u32[]{:S(2)}, u32[]{:S(2)}) collective-permute-start(bf16[24,2048]{1,0:T(8,128)(2,1)S(1)} %get-tuple-element.52), channel_id=1, source_target_pairs={{0,4},{2,6},{4,0},{6,2},{1,5},{3,7},{5,1},{7,3},{8,12},{10,14},{12... | collective-permute-start | bytes 294920 | tf_op jit(solution)/shard_map/ppermute | solution.py:35
  78.8 8.0 %collective-permute-start.26 = (bf16[24,2048]{1,0:T(8,128)(2,1)S(1)}, bf16[24,2048]{1,0:T(8,128)(2,1)S(1)}, u32[]{:S(2)}, u32[]{:S(2)}) collective-permute-start(bf16[24,2048]{1,0:T(8,128)(2,1)S(1)} %get-tuple-element.53), channel_id=1, source_target_pairs={{0,6},{2,4},{4,2},{6,0},{1,7},{3,5},{5,3},{7,1},{8,14},{10,12},{12... | collective-permute-start | bytes 294920 | tf_op jit(solution)/shard_map/ppermute | solution.py:35
  82.5 5.1 %collective-permute-start.24 = (bf16[24,2048]{1,0:T(8,128)(2,1)S(1)}, bf16[24,2048]{1,0:T(8,128)(2,1)S(1)}, u32[]{:S(2)}, u32[]{:S(2)}) collective-permute-start(bf16[24,2048]{1,0:T(8,128)(2,1)S(1)} %slice.161), channel_id=1, source_target_pairs={{0,2},{2,0},{4,6},{6,4},{1,3},{3,1},{5,7},{7,5},{8,10},{10,8},{12,... | collective-permute-start | bytes 294920 | tf_op jit(solution)/shard_map/ppermute | solution.py:35
  87.7 1.3 %collective-permute-start.27 = (bf16[12,2048]{1,0:T(8,128)(2,1)S(1)}, bf16[12,2048]{1,0:T(8,128)(2,1)S(1)}, u32[]{:S(2)}, u32[]{:S(2)}) collective-permute-start(bf16[12,2048]{1,0:T(8,128)(2,1)S(1)} %broadcast_select_fusion.4), channel_id=1, source_target_pairs={{0,1},{1,0},{2,3},{3,2},{4,5},{5,4},{6,7},{7,6},{8,9},{9,8},{10,11... | collective-permute-start | bytes 147464 | tf_op jit(solution)/shard_map/ppermute | solution.py:35

commit v11 on v10

--- a/solution.py
+++ b/solution.py
@@ -7,22 +7,10 @@
 from jax.sharding import Mesh, PartitionSpec as P
 
 LANES = 128
+PART = 1024.0
 CHUNK = 1024
 VMEM_LIMIT = 12 * 2**20
 GATE_MOST = 5
-
-
-def lookup_small(values_table, index_array):
-    columns = jnp.arange(values_table.shape[0], dtype=jnp.int32)
-    return jnp.sum(jnp.where(index_array[..., None] == columns, values_table, 0), -1)
-
-
-def planned_holder(expert_index, swap_slot, per_device, owners):
-    home = expert_index // per_device
-    within = expert_index % per_device
-    partner = (home + owners // 2) % owners
-    moved = within == lookup_small(swap_slot, home)
-    return jnp.where(moved, partner, home)
 
 
 def row_major(value):
@@ -252,6 +240,56 @@
     )(*(pltpu.with_memory_space_constraint(x, pltpu.VMEM) for x in (kept, taken)))
 
 
+def load_kernel(layout, swap_slot, *refs):
+    owners, per_device, top_count, step, scale = layout
+    *metas, load_ref = refs
+    experts_all = owners * per_device
+    high, low = [], []
+    for meta in metas:
+        values = meta[...].astype(jnp.float32)
+        lanes = lax.broadcasted_iota(jnp.int32, values.shape, 1)
+        gates = sum(pltpu.roll(values, LANES - k * top_count, 1) for k in (1, 2, 3))
+        amounts = jnp.round(gates * step)
+        upper = jnp.floor(amounts * (1.0 / PART))
+        lower = amounts - upper * PART
+        ids = jnp.where(lanes < top_count, values, -1.0)
+        high.append([])
+        low.append([])
+        for e in range(experts_all):
+            chosen = ids == e
+            high[-1].append(jnp.sum(jnp.where(chosen, upper, 0.0), 0, keepdims=True))
+            low[-1].append(jnp.sum(jnp.where(chosen, lower, 0.0), 0, keepdims=True))
+    sums = []
+    for part in (high, low):
+        rows = [sum(block[e] for block in part) for e in range(experts_all)]
+        sums.append(jnp.sum(jnp.concatenate(rows, 0), 1, keepdims=True))
+    totals = (sums[0] * PART + sums[1]) * (1.0 / step)
+    expert = lax.broadcasted_iota(jnp.int32, (experts_all, LANES), 0)
+    owner = lax.broadcasted_iota(jnp.int32, (experts_all, LANES), 1)
+    home = expert // per_device
+    slot = jnp.zeros_like(home)
+    for h in range(owners):
+        slot = jnp.where(home == h, swap_slot[h], slot)
+    partner = (home + owners // 2) % owners
+    holder = jnp.where(expert % per_device == slot, partner, home)
+    load_ref[...] = jnp.sum(jnp.where(holder == owner, totals, 0.0), 0, keepdims=True) * scale
+
+
+def planned_load(metas, swap_slot, owners, per_device, top_count):
+    count = sum(meta.shape[0] for meta in metas)
+    step = 2.0 ** (31 - (count * GATE_MOST).bit_length())
+    layout = (owners, per_device, top_count, step, owners / count)
+    in_vmem = pl.BlockSpec(memory_space=pltpu.VMEM)
+    load = pl.pallas_call(
+        lambda *refs: load_kernel(layout, *refs),
+        in_specs=[pl.BlockSpec(memory_space=pltpu.SMEM)] + [in_vmem] * len(metas),
+        out_specs=in_vmem,
+        out_shape=jax.ShapeDtypeStruct((1, LANES), jnp.float32),
+        compiler_params=pltpu.CompilerParams(vmem_limit_bytes=VMEM_LIMIT),
+    )(swap_slot, *metas)
+    return load[0, :owners]
+
+
 def on_device(tokens, expert_ids, gate_probs, in_weight, out_weight, swap_slot):
     groups, chips = lax.axis_size("dp"), lax.axis_size("chip")
     owners = 2 * chips
@@ -260,11 +298,9 @@
     rows, width = tokens.shape
     part = width // 2
     top_count = expert_ids.shape[1]
-    experts_all = per_device * owners
     half_width = out_weight.shape[1]
     core = lax.axis_index("core")
     first = core == 0
-    all_experts = jnp.arange(experts_all, dtype=jnp.int32)
     first_expert = (lax.axis_index("chip") * 2 + core) * per_device
     place = jnp.stack([core, first_expert]).astype(jnp.int32)
 
@@ -273,13 +309,6 @@
     chip_rows = row_major(
         jnp.concatenate([jnp.where(first, keep, taken), jnp.where(first, taken, keep)], 0)
     )
-
-    def routes(meta):
-        ids = meta[:, :top_count].astype(jnp.int32)
-        gates = sum(
-            wide(meta[:, (i + 1) * top_count : (i + 2) * top_count]) for i in range(3)
-        )
-        return ids, gates
 
     def sums_of(own, weights, filling=False):
         last = len(own) - 1
@@ -350,18 +379,7 @@
         jnp.concatenate([jnp.where(first, kept, arrived), jnp.where(first, arrived, kept)], 1)
     )
 
-    ids, gates = routes(jnp.concatenate(metas, 0))
-    step = 2.0 ** (31 - (ids.shape[0] * GATE_MOST).bit_length())
-    amounts = jnp.round(gates * step).astype(jnp.int32)
-    totals = jnp.sum(jnp.where(ids[..., None] == all_experts, amounts[..., None], 0), (0, 1))
-    totals = totals.astype(jnp.float32) * (1.0 / step)
-    holder = planned_holder(all_experts, swap_slot, per_device, owners)
-    owner_load = jnp.sum(
-        jnp.where(
-            holder == jnp.arange(owners, dtype=jnp.int32)[:, None], totals[None, :], jnp.float32(0.0)
-        ),
-        1,
-    ) * (owners / ids.shape[0])
+    owner_load = planned_load(metas, swap_slot, owners, per_device, top_count)
     return (mixed_out, owner_load)
 
 

time: 90 us -> 74.9 us (0.83)
  local copies, waits for them, and re-layouts: 16.2 us -> 0.98 us
  other arithmetic: 4.91 us -> 1.64 us
  Pallas kernels: 17.6 us -> 19.1 us
  waiting for transfers between devices: 25 us -> 26.5 us
    unnamed x16 -> x8, local copies, waits for them, and re-layouts: 15 us -> 0.13 us
    convert_element_type x2, other arithmetic: 2.54 us -> 0.37 us  [chip_sums(): return (wide(keep) + wide(swap(give, 'core', 1))).astype(jnp.bfloat16)]
    ppermute x28, waiting for transfers between devices: 25 us -> 26.5 us  [swap(): return row_major(lax.ppermute(row_major(value), axis, pairs))]
    pallas_call x0 -> x1, Pallas kernels: none -> 1.47 us  [planned_load(): pl.pallas_call(lambda *refs: load_kernel(layout, *refs), in_specs=[pl.Blo...]
  transfers between devices with their start and end apart: 28 -> 28, of which waited for: 12 -> 16; matrix products, arithmetic and copies ran while one was open for 5% -> 2% of each run, Pallas kernels for 18% -> 23%
where the time goes in v11:
time: 74.9 us; the launch traced here: 74.8 us
  waiting for transfers between devices  26.5 us (35%)
  starting transfers between devices  25.6 us (34%)
  Pallas kernels  19.1 us (26%)
  other arithmetic  1.64 us (2%)
  between operations  1 us (1%)
  local copies, waits for them, and re-layouts  0.98 us (1%)
    ppermute x28, waiting for transfers between devices, swap(): return row_major(lax.ppermute(row_major(value), axis, pairs))  26.5 us
    ppermute x28, starting transfers between devices, swap(): return row_major(lax.ppermute(row_major(value), axis, pairs))  25.6 us
    pallas_call x3, Pallas kernels, gated_sums(): pl.pallas_call(lambda *refs: sums_kernel((widths, block_count, top_count)...  16 us
    pallas_call x1, Pallas kernels, first_halves(): pl.pallas_call(first_kernel, in_specs=[pl.BlockSpec(memory_space=pltpu.SM...  1.56 us
  transfers between devices with their start and end apart: 28, of which 16 were waited for; matrix products, arithmetic and copies ran while one was open for 2% of the time, Pallas kernels for 23%

profile of v11, /device:TPU:0, one launch (start us, length us, event | category | flops | bytes accessed | tf_op | source)
XLA Modules:
  0.0 74.8 jit_solution(333924280247846907)
XLA Ops:
  0.7 1.6 %shard_map.77 = (bf16[12,2176]{1,0:T(8,128)(2,1)S(1)}, bf16[12,2176]{1,0:T(8,128)(2,1)S(1)}) custom-call(s32[2]{0:T(128)S(1)} %pad_add_fusion.place.refs_0_, bf16[12,4096]{1,0:T(8,128)(2,1)} %refs_0_.2, s32[8,12]{1,0:T(8,128)} %bitcast.8, f32[8,12]{1,0:T(8,128)} %bitcast.9), custom_call_target="tpu_custom_call" | custom-call | tf_op jit(solution)/shard_map/pallas_call | solution.py:209
  2.3 0.5 collective-permute-start
  2.8 0.9 %collective-permute-done = bf16[12,2176]{1,0:T(8,128)(2,1)S(1)} collective-permute-done((bf16[12,2176]{1,0:T(8,128)(2,1)S(1)}, bf16[12,2176]{1,0:T(8,128)(2,1)S(1)}, u32[]{:S(2)}, u32[]{:S(2)}) %collective-permute-start) | collective-permute-done | bytes 52256 | tf_op jit(solution)/shard_map/ppermute | solution.py:23
  3.8 3.0 %collective-permute-start.1 = (bf16[24,2176]{1,0:T(8,128)(2,1)S(1)}, bf16[24,2176]{1,0:T(8,128)(2,1)S(1)}, u32[]{:S(2)}, u32[]{:S(2)}) collective-permute-start(bf16[24,2176]{1,0:T(8,128)(2,1)S(1)} %get-tuple-element.41), channel_id=1, source_target_pairs={{0,2},{2,0},{4,6},{6,4},{1,3},{3,1},{5,7},{7,5},{8,10},{10,8},{12,... | collective-permute-start | bytes 313352 | tf_op jit(solution)/shard_map/ppermute | solution.py:23
  6.8 2.5 %collective-permute-start.3 = (bf16[24,2176]{1,0:T(8,128)(2,1)S(1)}, bf16[24,2176]{1,0:T(8,128)(2,1)S(1)}, u32[]{:S(2)}, u32[]{:S(2)}) collective-permute-start(bf16[24,2176]{1,0:T(8,128)(2,1)S(1)} %get-tuple-element.41), channel_id=1, source_target_pairs={{0,6},{2,4},{4,2},{6,0},{1,7},{3,5},{5,3},{7,1},{8,14},{10,12},{12... | collective-permute-start | bytes 313352 | tf_op jit(solution)/shard_map/ppermute | solution.py:23
  9.2 0.1 collective-permute-start.2
  9.3 2.4 %collective-permute-start.6 = (bf16[24,2176]{1,0:T(8,128)(2,1)S(1)}, bf16[24,2176]{1,0:T(8,128)(2,1)S(1)}, u32[]{:S(2)}, u32[]{:S(2)}) collective-permute-start(bf16[24,2176]{1,0:T(8,128)(2,1)S(1)} %get-tuple-element.41), channel_id=1, source_target_pairs={{0,24},{8,16},{16,8},{24,0},{1,25},{9,17},{17,9},{25,1},{2,26},{10... | collective-permute-start | bytes 313352 | tf_op jit(solution)/shard_map/ppermute | solution.py:23
  11.8 0.5 collective-permute-start.5
  12.3 0.5 collective-permute-start.4
  12.9 6.2 %collective-permute-done.2 = bf16[24,2176]{1,0:T(8,128)(2,1)S(1)} collective-permute-done((bf16[24,2176]{1,0:T(8,128)(2,1)S(1)}, bf16[24,2176]{1,0:T(8,128)(2,1)S(1)}, u32[]{:S(2)}, u32[]{:S(2)}) %collective-permute-start.2) | collective-permute-done | bytes 104480 | tf_op jit(solution)/shard_map/ppermute | solution.py:23
  19.3 1.6 %collective-permute-start.9 = (bf16[72,2176]{1,0:T(8,128)(2,1)S(1)}, bf16[72,2176]{1,0:T(8,128)(2,1)S(1)}, u32[]{:S(2)}, u32[]{:S(2)}) collective-permute-start(bf16[72,2176]{1,0:T(8,128)(2,1)S(1)} %get-tuple-element.59), channel_id=1, source_target_pairs={{0,8},{8,0},{16,24},{24,16},{1,9},{9,1},{17,25},{25,17},{2,10},{10... | collective-permute-start | bytes 940040 | tf_op jit(solution)/shard_map/ppermute | solution.py:23
  20.9 1.5 %collective-permute-start.10 = (bf16[72,2176]{1,0:T(8,128)(2,1)S(1)}, bf16[72,2176]{1,0:T(8,128)(2,1)S(1)}, u32[]{:S(2)}, u32[]{:S(2)}) collective-permute-start(bf16[72,2176]{1,0:T(8,128)(2,1)S(1)} %get-tuple-element.59), channel_id=1, source_target_pairs={{0,16},{8,24},{16,0},{24,8},{1,17},{9,25},{17,1},{25,9},{2,18},{10... | collective-permute-start | bytes 940040 | tf_op jit(solution)/shard_map/ppermute | solution.py:23
  22.4 8.4 %shard_map.78 = (bf16[168,2048]{1,0:T(8,128)(2,1)S(1)}, bf16[168,2048]{1,0:T(8,128)(2,1)S(1)}, bf16[2,4096,768]{2,1,0:T(8,128)(2,1)S(1)}, bf16[768,4096]{1,0:T(8,128)(2,1)S(1)}) custom-call(s32[2]{0:T(128)S(1)} %pad_add_fusion.place.refs_0_, bf16[168,2176]{1,0:T(8,128)(2,1)S(1)} %constant_dynamic-update-slice_fusion.refs_1_, ...), custom_call_target="tpu_custom_call" | custom-call | flops 3170893824 | bytes 18874368 | tf_op jit(solution)/shard_map/pallas_call | solution.py:162
  31.0 0.5 collective-permute-start.8
  31.6 1.1 %collective-permute-start.13 = (bf16[72,1024]{1,0:T(8,128)(2,1)S(1)}, bf16[72,1024]{1,0:T(8,128)(2,1)S(1)}, u32[]{:S(2)}, u32[]{:S(2)}) collective-permute-start(bf16[72,1024]{1,0:T(8,128)(2,1)S(1)} %slice.106), channel_id=1, source_target_pairs={{0,16},{8,24},{16,0},{24,8},{1,17},{9,25},{17,1},{25,9},{2,18},{10... | collective-permute-start | bytes 442376 | tf_op jit(solution)/shard_map/ppermute | solution.py:23
  32.7 1.0 %collective-permute-start.14 = (bf16[72,1152]{1,0:T(8,128)(2,1)S(1)}, bf16[72,1152]{1,0:T(8,128)(2,1)S(1)}, u32[]{:S(2)}, u32[]{:S(2)}) collective-permute-start(bf16[72,1152]{1,0:T(8,128)(2,1)S(1)} %slice.107), channel_id=1, source_target_pairs={{0,8},{8,0},{16,24},{24,16},{1,9},{9,1},{17,25},{25,17},{2,10},{10... | collective-permute-start | bytes 497672 | tf_op jit(solution)/shard_map/ppermute | solution.py:23
  33.7 3.6 %shard_map.79 = (bf16[144,2048]{1,0:T(8,128)(2,1)S(1)}, bf16[144,2048]{1,0:T(8,128)(2,1)S(1)}) custom-call(s32[2]{0:T(128)S(1)} %pad_add_fusion.place.refs_0_, bf16[144,2176]{1,0:T(8,128)(2,1)S(1)} %constant_dynamic-update-slice_fusion.10.refs_1_, bf16[144,2048]{1,0:T(8,128)(2,1)S(1)} %collective-permute-done.11.refs_2_, ...), custom_call_target="tpu_custom_call" | custom-call | flops 2717908992 | tf_op jit(solution)/shard_map/pallas_call | solution.py:162
  37.4 0.1 collective-permute-done.13.refs_1_
  37.5 1.2 %collective-permute-done.14.refs_2_ = bf16[72,1152]{1,0:T(8,128)(2,1)S(1)} collective-permute-done((bf16[72,1152]{1,0:T(8,128)(2,1)S(1)}, bf16[72,1152]{1,0:T(8,128)(2,1)S(1)}, u32[]{:S(2)}, u32[]{:S(2)}) %collective-permute-start.14) | collective-permute-done | bytes 165920 | tf_op jit(solution)/shard_map/ppermute | solution.py:23
  38.7 0.5 collective-permute-start.15
  39.2 0.2 add_convert_fusion
  39.5 0.6 collective-permute-done.16.refs_4_
  40.1 0.2 collective-permute-done.15.refs_3_
  40.3 4.0 %shard_map.80 = (bf16[72,2048]{1,0:T(8,128)(2,1)S(1)}, bf16[72,2048]{1,0:T(8,128)(2,1)S(1)}) custom-call(s32[2]{0:T(128)S(1)} %pad_add_fusion.place.refs_0_, bf16[72,1024]{1,0:T(8,128)(2,1)S(1)} %collective-permute-done.13.refs_1_, bf16[72,1152]{1,0:T(8,128)(2,1)S(1)} %collective-permute-done.14.refs_2_, ...), custom_call_target="tpu_custom_call" | custom-call | flops 1358954496 | tf_op jit(solution)/shard_map/pallas_call | solution.py:162
  44.3 0.4 collective-permute-start.17
  44.7 1.2 %collective-permute-done.17.taken_ref = bf16[72,2048]{1,0:T(8,128)(2,1)S(1)} collective-permute-done((bf16[72,2048]{1,0:T(8,128)(2,1)S(1)}, bf16[72,2048]{1,0:T(8,128)(2,1)S(1)}, u32[]{:S(2)}, u32[]{:S(2)}) %collective-permute-start.17) | collective-permute-done | bytes 294944 | tf_op jit(solution)/shard_map/ppermute | solution.py:23
  46.0 1.2 %collective-permute-start.19 = (bf16[96,1024]{1,0:T(8,128)(2,1)S(1)}, bf16[96,1024]{1,0:T(8,128)(2,1)S(1)}, u32[]{:S(2)}, u32[]{:S(2)}) collective-permute-start(bf16[96,1024]{1,0:T(8,128)(2,1)S(1)} %pad_maximum_fusion.3), channel_id=1, source_target_pairs={{0,8},{8,0},{16,24},{24,16},{1,9},{9,1},{17,25},{25,17},{2,10},{10... | collective-permute-start | bytes 589832 | tf_op jit(solution)/shard_map/ppermute | solution.py:23
  47.2 0.6 collective-permute-start.18
  47.8 0.1 add_convert_fusion.1
  48.0 5.2 %collective-permute-done.19 = bf16[96,1024]{1,0:T(8,128)(2,1)S(1)} collective-permute-done((bf16[96,1024]{1,0:T(8,128)(2,1)S(1)}, bf16[96,1024]{1,0:T(8,128)(2,1)S(1)}, u32[]{:S(2)}, u32[]{:S(2)}) %collective-permute-start.19) | collective-permute-done | bytes 196640 | tf_op jit(solution)/shard_map/ppermute | solution.py:23
  53.2 0.9 %collective-permute-done.18 = bf16[96,1024]{1,0:T(8,128)(2,1)S(1)} collective-permute-done((bf16[96,1024]{1,0:T(8,128)(2,1)S(1)}, bf16[96,1024]{1,0:T(8,128)(2,1)S(1)}, u32[]{:S(2)}, u32[]{:S(2)}) %collective-permute-start.18) | collective-permute-done | bytes 196640 | tf_op jit(solution)/shard_map/ppermute | solution.py:23
  54.1 0.1 add_convert_fusion.4
  54.3 0.6 collective-permute-start.21
  54.9 1.4 %collective-permute-start.20 = (bf16[48,2048]{1,0:T(8,128)(2,1)S(1)}, bf16[48,2048]{1,0:T(8,128)(2,1)S(1)}, u32[]{:S(2)}, u32[]{:S(2)}) collective-permute-start(bf16[48,2048]{1,0:T(8,128)(2,1)S(1)} %get-tuple-element.51), channel_id=1, source_target_pairs={{0,8},{8,0},{16,24},{24,16},{1,9},{9,1},{17,25},{25,17},{2,10},{10... | collective-permute-start | bytes 589832 | tf_op jit(solution)/shard_map/ppermute | solution.py:23
  56.3 4.0 %collective-permute-done.21 = bf16[48,2048]{1,0:T(8,128)(2,1)S(1)} collective-permute-done((bf16[48,2048]{1,0:T(8,128)(2,1)S(1)}, bf16[48,2048]{1,0:T(8,128)(2,1)S(1)}, u32[]{:S(2)}, u32[]{:S(2)}) %collective-permute-start.21) | collective-permute-done | bytes 196640 | tf_op jit(solution)/shard_map/ppermute | solution.py:23
  60.4 0.2 collective-permute-done.20
  60.7 1.5 %collective-permute-start.22 = (bf16[48,2048]{1,0:T(8,128)(2,1)S(1)}, bf16[48,2048]{1,0:T(8,128)(2,1)S(1)}, u32[]{:S(2)}, u32[]{:S(2)}) collective-permute-start(bf16[48,2048]{1,0:T(8,128)(2,1)S(1)} %get-tuple-element.38), channel_id=1, source_target_pairs={{0,8},{8,0},{16,24},{24,16},{1,9},{9,1},{17,25},{25,17},{2,10},{10... | collective-permute-start | bytes 589832 | tf_op jit(solution)/shard_map/ppermute | solution.py:23
  62.2 1.0 %collective-permute-start.23 = (bf16[48,2048]{1,0:T(8,128)(2,1)S(1)}, bf16[48,2048]{1,0:T(8,128)(2,1)S(1)}, u32[]{:S(2)}, u32[]{:S(2)}) collective-permute-start(bf16[48,2048]{1,0:T(8,128)(2,1)S(1)} %get-tuple-element.39), channel_id=1, source_target_pairs={{0,16},{8,24},{16,0},{24,8},{1,17},{9,25},{17,1},{25,9},{2,18},{10... | collective-permute-start | bytes 589832 | tf_op jit(solution)/shard_map/ppermute | solution.py:23
  63.2 0.5 collective-permute-start.25
  63.7 2.3 %collective-permute-start.26 = (bf16[24,2048]{1,0:T(8,128)(2,1)S(1)}, bf16[24,2048]{1,0:T(8,128)(2,1)S(1)}, u32[]{:S(2)}, u32[]{:S(2)}) collective-permute-start(bf16[24,2048]{1,0:T(8,128)(2,1)S(1)} %get-tuple-element.53), channel_id=1, source_target_pairs={{0,6},{2,4},{4,2},{6,0},{1,7},{3,5},{5,3},{7,1},{8,14},{10,12},{12... | collective-permute-start | bytes 294920 | tf_op jit(solution)/shard_map/ppermute | solution.py:23
  66.0 0.4 collective-permute-done.22
  66.4 1.4 %collective-permute-done.23 = bf16[48,2048]{1,0:T(8,128)(2,1)S(1)} collective-permute-done((bf16[48,2048]{1,0:T(8,128)(2,1)S(1)}, bf16[48,2048]{1,0:T(8,128)(2,1)S(1)}, u32[]{:S(2)}, u32[]{:S(2)}) %collective-permute-start.23) | collective-permute-done | bytes 196640 | tf_op jit(solution)/shard_map/ppermute | solution.py:23
  68.1 1.5 %shard_map.82 = f32[1,128]{1,0:T(1,128)S(1)} custom-call(s32[8]{0:T(128)S(1)} %copy-done, bf16[168,128]{1,0:T(8,128)(2,1)S(1)} %slice.154.refs_1_, bf16[144,128]{1,0:T(8,128)(2,1)S(1)} %slice.155.refs_2_, bf16[72,128]{1,0:T(8,128)(2,1)S(1)} %slice.128.refs_3_), custom_call_target="tpu_custom_call" | custom-call | tf_op jit(solution)/shard_map/pallas_call | solution.py:283
  69.5 2.1 %collective-permute-done.25 = bf16[24,2048]{1,0:T(8,128)(2,1)S(1)} collective-permute-done((bf16[24,2048]{1,0:T(8,128)(2,1)S(1)}, bf16[24,2048]{1,0:T(8,128)(2,1)S(1)}, u32[]{:S(2)}, u32[]{:S(2)}) %collective-permute-start.25) | collective-permute-done | bytes 98336 | tf_op jit(solution)/shard_map/ppermute | solution.py:23
  71.6 1.0 %collective-permute-done.24 = bf16[24,2048]{1,0:T(8,128)(2,1)S(1)} collective-permute-done((bf16[24,2048]{1,0:T(8,128)(2,1)S(1)}, bf16[24,2048]{1,0:T(8,128)(2,1)S(1)}, u32[]{:S(2)}, u32[]{:S(2)}) %collective-permute-start.24) | collective-permute-done | bytes 98336 | tf_op jit(solution)/shard_map/ppermute | solution.py:23
  72.8 0.5 slice_bitcast_fusion
  73.3 0.7 collective-permute-done.27
  74.1 0.7 pad_maximum_fusion.4
  (57 shorter events, 1.5 us)
Async XLA Ops:
  2.3 1.4 %collective-permute-start = (bf16[12,2176]{1,0:T(8,128)(2,1)S(1)}, bf16[12,2176]{1,0:T(8,128)(2,1)S(1)}, u32[]{:S(2)}, u32[]{:S(2)}) collective-permute-start(bf16[12,2176]{1,0:T(8,128)(2,1)S(1)} %get-tuple-element.22), channel_id=1, source_target_pairs={{0,1},{1,0},{2,3},{3,2},{4,5},{5,4},{6,7},{7,6},{8,9},{9,8},{10,11... | collective-permute-start | bytes 156680 | tf_op jit(solution)/shard_map/ppermute | solution.py:23
  3.8 8.5 %collective-permute-start.1 = (bf16[24,2176]{1,0:T(8,128)(2,1)S(1)}, bf16[24,2176]{1,0:T(8,128)(2,1)S(1)}, u32[]{:S(2)}, u32[]{:S(2)}) collective-permute-start(bf16[24,2176]{1,0:T(8,128)(2,1)S(1)} %get-tuple-element.41), channel_id=1, source_target_pairs={{0,2},{2,0},{4,6},{6,4},{1,3},{3,1},{5,7},{7,5},{8,10},{10,8},{12,... | collective-permute-start | bytes 313352 | tf_op jit(solution)/shard_map/ppermute | solution.py:23
  6.8 12.3 %collective-permute-start.3 = (bf16[24,2176]{1,0:T(8,128)(2,1)S(1)}, bf16[24,2176]{1,0:T(8,128)(2,1)S(1)}, u32[]{:S(2)}, u32[]{:S(2)}) collective-permute-start(bf16[24,2176]{1,0:T(8,128)(2,1)S(1)} %get-tuple-element.41), channel_id=1, source_target_pairs={{0,6},{2,4},{4,2},{6,0},{1,7},{3,5},{5,3},{7,1},{8,14},{10,12},{12... | collective-permute-start | bytes 313352 | tf_op jit(solution)/shard_map/ppermute | solution.py:23
  9.2 9.8 %collective-permute-start.2 = (bf16[24,2176]{1,0:T(8,128)(2,1)S(1)}, bf16[24,2176]{1,0:T(8,128)(2,1)S(1)}, u32[]{:S(2)}, u32[]{:S(2)}) collective-permute-start(bf16[24,2176]{1,0:T(8,128)(2,1)S(1)} %get-tuple-element.41), channel_id=1, source_target_pairs={{0,4},{2,6},{4,0},{6,2},{1,5},{3,7},{5,1},{7,3},{8,12},{10,14},{12... | collective-permute-start | bytes 313352 | tf_op jit(solution)/shard_map/ppermute | solution.py:23
  9.3 9.8 %collective-permute-start.6 = (bf16[24,2176]{1,0:T(8,128)(2,1)S(1)}, bf16[24,2176]{1,0:T(8,128)(2,1)S(1)}, u32[]{:S(2)}, u32[]{:S(2)}) collective-permute-start(bf16[24,2176]{1,0:T(8,128)(2,1)S(1)} %get-tuple-element.41), channel_id=1, source_target_pairs={{0,24},{8,16},{16,8},{24,0},{1,25},{9,17},{17,9},{25,1},{2,26},{10... | collective-permute-start | bytes 313352 | tf_op jit(solution)/shard_map/ppermute | solution.py:23
  11.8 7.3 %collective-permute-start.5 = (bf16[24,2176]{1,0:T(8,128)(2,1)S(1)}, bf16[24,2176]{1,0:T(8,128)(2,1)S(1)}, u32[]{:S(2)}, u32[]{:S(2)}) collective-permute-start(bf16[24,2176]{1,0:T(8,128)(2,1)S(1)} %get-tuple-element.41), channel_id=1, source_target_pairs={{0,16},{8,24},{16,0},{24,8},{1,17},{9,25},{17,1},{25,9},{2,18},{10... | collective-permute-start | bytes 313352 | tf_op jit(solution)/shard_map/ppermute | solution.py:23
  12.3 6.8 %collective-permute-start.4 = (bf16[24,2176]{1,0:T(8,128)(2,1)S(1)}, bf16[24,2176]{1,0:T(8,128)(2,1)S(1)}, u32[]{:S(2)}, u32[]{:S(2)}) collective-permute-start(bf16[24,2176]{1,0:T(8,128)(2,1)S(1)} %get-tuple-element.41), channel_id=1, source_target_pairs={{0,8},{8,0},{16,24},{24,16},{1,9},{9,1},{17,25},{25,17},{2,10},{10... | collective-permute-start | bytes 313352 | tf_op jit(solution)/shard_map/ppermute | solution.py:23
  19.2 3.2 %collective-permute-start.7 = (bf16[168,2048]{1,0:T(8,128)(2,1)S(1)}, bf16[168,2048]{1,0:T(8,128)(2,1)S(1)}, u32[]{:S(2)}, u32[]{:S(2)}) collective-permute-start(bf16[168,2048]{1,0:T(8,128)(2,1)S(1)} %slice.130), channel_id=1, source_target_pairs={{0,1},{1,0},{2,3},{3,2},{4,5},{5,4},{6,7},{7,6},{8,9},{9,8},{10,11... | collective-permute-start | bytes 2064392 | tf_op jit(solution)/shard_map/ppermute | solution.py:23
  19.3 11.5 %collective-permute-start.9 = (bf16[72,2176]{1,0:T(8,128)(2,1)S(1)}, bf16[72,2176]{1,0:T(8,128)(2,1)S(1)}, u32[]{:S(2)}, u32[]{:S(2)}) collective-permute-start(bf16[72,2176]{1,0:T(8,128)(2,1)S(1)} %get-tuple-element.59), channel_id=1, source_target_pairs={{0,8},{8,0},{16,24},{24,16},{1,9},{9,1},{17,25},{25,17},{2,10},{10... | collective-permute-start | bytes 940040 | tf_op jit(solution)/shard_map/ppermute | solution.py:23
  20.9 9.9 %collective-permute-start.10 = (bf16[72,2176]{1,0:T(8,128)(2,1)S(1)}, bf16[72,2176]{1,0:T(8,128)(2,1)S(1)}, u32[]{:S(2)}, u32[]{:S(2)}) collective-permute-start(bf16[72,2176]{1,0:T(8,128)(2,1)S(1)} %get-tuple-element.59), channel_id=1, source_target_pairs={{0,16},{8,24},{16,0},{24,8},{1,17},{9,25},{17,1},{25,9},{2,18},{10... | collective-permute-start | bytes 940040 | tf_op jit(solution)/shard_map/ppermute | solution.py:23
  31.0 2.7 %collective-permute-start.11 = (bf16[144,2048]{1,0:T(8,128)(2,1)S(1)}, bf16[144,2048]{1,0:T(8,128)(2,1)S(1)}, u32[]{:S(2)}, u32[]{:S(2)}) collective-permute-start(bf16[144,2048]{1,0:T(8,128)(2,1)S(1)} %slice.133), channel_id=1, source_target_pairs={{0,1},{1,0},{2,3},{3,2},{4,5},{5,4},{6,7},{7,6},{8,9},{9,8},{10,11... | collective-permute-start | bytes 1769480 | tf_op jit(solution)/shard_map/ppermute | solution.py:23
  31.0 8.2 %collective-permute-start.8 = (bf16[168,2048]{1,0:T(8,128)(2,1)S(1)}, bf16[168,2048]{1,0:T(8,128)(2,1)S(1)}, u32[]{:S(2)}, u32[]{:S(2)}) collective-permute-start(bf16[168,2048]{1,0:T(8,128)(2,1)S(1)} %get-tuple-element.24), channel_id=1, source_target_pairs={{0,1},{1,0},{2,3},{3,2},{4,5},{5,4},{6,7},{7,6},{8,9},{9,8},{10,11... | collective-permute-start | bytes 2064392 | tf_op jit(solution)/shard_map/ppermute | solution.py:23
  31.6 5.9 %collective-permute-start.13 = (bf16[72,1024]{1,0:T(8,128)(2,1)S(1)}, bf16[72,1024]{1,0:T(8,128)(2,1)S(1)}, u32[]{:S(2)}, u32[]{:S(2)}) collective-permute-start(bf16[72,1024]{1,0:T(8,128)(2,1)S(1)} %slice.106), channel_id=1, source_target_pairs={{0,16},{8,24},{16,0},{24,8},{1,17},{9,25},{17,1},{25,9},{2,18},{10... | collective-permute-start | bytes 442376 | tf_op jit(solution)/shard_map/ppermute | solution.py:23
  32.7 5.9 %collective-permute-start.14 = (bf16[72,1152]{1,0:T(8,128)(2,1)S(1)}, bf16[72,1152]{1,0:T(8,128)(2,1)S(1)}, u32[]{:S(2)}, u32[]{:S(2)}) collective-permute-start(bf16[72,1152]{1,0:T(8,128)(2,1)S(1)} %slice.107), channel_id=1, source_target_pairs={{0,8},{8,0},{16,24},{24,16},{1,9},{9,1},{17,25},{25,17},{2,10},{10... | collective-permute-start | bytes 497672 | tf_op jit(solution)/shard_map/ppermute | solution.py:23
  37.3 10.5 %collective-permute-start.12 = (bf16[144,2048]{1,0:T(8,128)(2,1)S(1)}, bf16[144,2048]{1,0:T(8,128)(2,1)S(1)}, u32[]{:S(2)}, u32[]{:S(2)}) collective-permute-start(bf16[144,2048]{1,0:T(8,128)(2,1)S(1)} %get-tuple-element.30), channel_id=1, source_target_pairs={{0,1},{1,0},{2,3},{3,2},{4,5},{5,4},{6,7},{7,6},{8,9},{9,8},{10,11... | collective-permute-start | bytes 1769480 | tf_op jit(solution)/shard_map/ppermute | solution.py:23
  38.6 1.4 %collective-permute-start.16 = (bf16[72,1024]{1,0:T(8,128)(2,1)S(1)}, bf16[72,1024]{1,0:T(8,128)(2,1)S(1)}, u32[]{:S(2)}, u32[]{:S(2)}) collective-permute-start(bf16[72,1024]{1,0:T(8,128)(2,1)S(1)} %slice.108), channel_id=1, source_target_pairs={{0,1},{1,0},{2,3},{3,2},{4,5},{5,4},{6,7},{7,6},{8,9},{9,8},{10,11... | collective-permute-start | bytes 442376 | tf_op jit(solution)/shard_map/ppermute | solution.py:23
  38.7 1.6 %collective-permute-start.15 = (bf16[72,1024]{1,0:T(8,128)(2,1)S(1)}, bf16[72,1024]{1,0:T(8,128)(2,1)S(1)}, u32[]{:S(2)}, u32[]{:S(2)}) collective-permute-start(bf16[72,1024]{1,0:T(8,128)(2,1)S(1)} %collective-permute-done.13.refs_1_), channel_id=1, source_target_pairs={{0,1},{1,0},{2,3},{3,2},{4,5},{5,4},{6,7},{7,6},{8,9},{9,8},{10,11... | collective-permute-start | bytes 442376 | tf_op jit(solution)/shard_map/ppermute | solution.py:23
  44.3 1.6 %collective-permute-start.17 = (bf16[72,2048]{1,0:T(8,128)(2,1)S(1)}, bf16[72,2048]{1,0:T(8,128)(2,1)S(1)}, u32[]{:S(2)}, u32[]{:S(2)}) collective-permute-start(bf16[72,2048]{1,0:T(8,128)(2,1)S(1)} %get-tuple-element.34), channel_id=1, source_target_pairs={{0,1},{1,0},{2,3},{3,2},{4,5},{5,4},{6,7},{7,6},{8,9},{9,8},{10,11... | collective-permute-start | bytes 884744 | tf_op jit(solution)/shard_map/ppermute | solution.py:23
  46.0 7.2 %collective-permute-start.19 = (bf16[96,1024]{1,0:T(8,128)(2,1)S(1)}, bf16[96,1024]{1,0:T(8,128)(2,1)S(1)}, u32[]{:S(2)}, u32[]{:S(2)}) collective-permute-start(bf16[96,1024]{1,0:T(8,128)(2,1)S(1)} %pad_maximum_fusion.3), channel_id=1, source_target_pairs={{0,8},{8,0},{16,24},{24,16},{1,9},{9,1},{17,25},{25,17},{2,10},{10... | collective-permute-start | bytes 589832 | tf_op jit(solution)/shard_map/ppermute | solution.py:23
  47.2 6.9 %collective-permute-start.18 = (bf16[96,1024]{1,0:T(8,128)(2,1)S(1)}, bf16[96,1024]{1,0:T(8,128)(2,1)S(1)}, u32[]{:S(2)}, u32[]{:S(2)}) collective-permute-start(bf16[96,1024]{1,0:T(8,128)(2,1)S(1)} %pad_maximum_fusion.2), channel_id=1, source_target_pairs={{0,16},{8,24},{16,0},{24,8},{1,17},{9,25},{17,1},{25,9},{2,18},{10... | collective-permute-start | bytes 589832 | tf_op jit(solution)/shard_map/ppermute | solution.py:23
  54.3 6.0 %collective-permute-start.21 = (bf16[48,2048]{1,0:T(8,128)(2,1)S(1)}, bf16[48,2048]{1,0:T(8,128)(2,1)S(1)}, u32[]{:S(2)}, u32[]{:S(2)}) collective-permute-start(bf16[48,2048]{1,0:T(8,128)(2,1)S(1)} %get-tuple-element.49), channel_id=1, source_target_pairs={{0,16},{8,24},{16,0},{24,8},{1,17},{9,25},{17,1},{25,9},{2,18},{10... | collective-permute-start | bytes 589832 | tf_op jit(solution)/shard_map/ppermute | solution.py:23
  54.9 13.2 %copy-start = (s32[8]{0:T(128)S(1)}, s32[8]{0:T(128)}, u32[]{:S(2)}) copy-start(s32[8]{0:T(128)} %refs_0_.3) | copy-start | bytes 100
  54.9 5.7 %collective-permute-start.20 = (bf16[48,2048]{1,0:T(8,128)(2,1)S(1)}, bf16[48,2048]{1,0:T(8,128)(2,1)S(1)}, u32[]{:S(2)}, u32[]{:S(2)}) collective-permute-start(bf16[48,2048]{1,0:T(8,128)(2,1)S(1)} %get-tuple-element.51), channel_id=1, source_target_pairs={{0,8},{8,0},{16,24},{24,16},{1,9},{9,1},{17,25},{25,17},{2,10},{10... | collective-permute-start | bytes 589832 | tf_op jit(solution)/shard_map/ppermute | solution.py:23
  60.7 5.7 %collective-permute-start.22 = (bf16[48,2048]{1,0:T(8,128)(2,1)S(1)}, bf16[48,2048]{1,0:T(8,128)(2,1)S(1)}, u32[]{:S(2)}, u32[]{:S(2)}) collective-permute-start(bf16[48,2048]{1,0:T(8,128)(2,1)S(1)} %get-tuple-element.38), channel_id=1, source_target_pairs={{0,8},{8,0},{16,24},{24,16},{1,9},{9,1},{17,25},{25,17},{2,10},{10... | collective-permute-start | bytes 589832 | tf_op jit(solution)/shard_map/ppermute | solution.py:23
  62.2 5.7 %collective-permute-start.23 = (bf16[48,2048]{1,0:T(8,128)(2,1)S(1)}, bf16[48,2048]{1,0:T(8,128)(2,1)S(1)}, u32[]{:S(2)}, u32[]{:S(2)}) collective-permute-start(bf16[48,2048]{1,0:T(8,128)(2,1)S(1)} %get-tuple-element.39), channel_id=1, source_target_pairs={{0,16},{8,24},{16,0},{24,8},{1,17},{9,25},{17,1},{25,9},{2,18},{10... | collective-permute-start | bytes 589832 | tf_op jit(solution)/shard_map/ppermute | solution.py:23
  63.2 8.4 %collective-permute-start.25 = (bf16[24,2048]{1,0:T(8,128)(2,1)S(1)}, bf16[24,2048]{1,0:T(8,128)(2,1)S(1)}, u32[]{:S(2)}, u32[]{:S(2)}) collective-permute-start(bf16[24,2048]{1,0:T(8,128)(2,1)S(1)} %get-tuple-element.52), channel_id=1, source_target_pairs={{0,4},{2,6},{4,0},{6,2},{1,5},{3,7},{5,1},{7,3},{8,12},{10,14},{12... | collective-permute-start | bytes 294920 | tf_op jit(solution)/shard_map/ppermute | solution.py:23
  63.7 7.9 %collective-permute-start.26 = (bf16[24,2048]{1,0:T(8,128)(2,1)S(1)}, bf16[24,2048]{1,0:T(8,128)(2,1)S(1)}, u32[]{:S(2)}, u32[]{:S(2)}) collective-permute-start(bf16[24,2048]{1,0:T(8,128)(2,1)S(1)} %get-tuple-element.53), channel_id=1, source_target_pairs={{0,6},{2,4},{4,2},{6,0},{1,7},{3,5},{5,3},{7,1},{8,14},{10,12},{12... | collective-permute-start | bytes 294920 | tf_op jit(solution)/shard_map/ppermute | solution.py:23
  67.9 4.7 %collective-permute-start.24 = (bf16[24,2048]{1,0:T(8,128)(2,1)S(1)}, bf16[24,2048]{1,0:T(8,128)(2,1)S(1)}, u32[]{:S(2)}, u32[]{:S(2)}) collective-permute-start(bf16[24,2048]{1,0:T(8,128)(2,1)S(1)} %slice.149), channel_id=1, source_target_pairs={{0,2},{2,0},{4,6},{6,4},{1,3},{3,1},{5,7},{7,5},{8,10},{10,8},{12,... | collective-permute-start | bytes 294920 | tf_op jit(solution)/shard_map/ppermute | solution.py:23
  72.7 1.3 %collective-permute-start.27 = (bf16[12,2048]{1,0:T(8,128)(2,1)S(1)}, bf16[12,2048]{1,0:T(8,128)(2,1)S(1)}, u32[]{:S(2)}, u32[]{:S(2)}) collective-permute-start(bf16[12,2048]{1,0:T(8,128)(2,1)S(1)} %broadcast_select_fusion.4), channel_id=1, source_target_pairs={{0,1},{1,0},{2,3},{3,2},{4,5},{5,4},{6,7},{7,6},{8,9},{9,8},{10,11... | collective-permute-start | bytes 147464 | tf_op jit(solution)/shard_map/ppermute | solution.py:23

commit v12 on v11

--- a/solution.py
+++ b/solution.py
@@ -9,6 +9,7 @@
 LANES = 128
 PART = 1024.0
 CHUNK = 1024
+MOST_ROWS = 512
 VMEM_LIMIT = 12 * 2**20
 GATE_MOST = 5
 
@@ -23,41 +24,12 @@
     return row_major(lax.ppermute(row_major(value), axis, pairs))
 
 
-def cut_of(block):
-    return block.shape[1] // (2 * LANES) * LANES
-
-
-def spread_near(block):
-    size = lax.axis_size("dp")
-    return [swap(block, "dp", k) for k in range(1, 3 if size == 4 else size)]
-
-
-def spread_rest(near):
-    if lax.axis_size("dp") != 4:
-        return []
-    cut = cut_of(near[0])
-    return [swap(near[0][:, :cut], "dp", 2), swap(near[1][:, cut:], "dp", 1)]
-
-
 def behind(values, others):
     return lax.optimization_barrier((values, others))[0]
 
 
 def wide(value):
     return value.astype(jnp.float32)
-
-
-def with_fourth(blocks, halves):
-    own, one, two = blocks
-    cut = cut_of(own)
-    upper, lower = swap(halves[0], "dp", 2), swap(halves[1], "dp", 1)
-    one = jnp.concatenate(
-        [(wide(one[:, :cut]) + wide(upper)).astype(jnp.bfloat16), one[:, cut:]], 1
-    )
-    two = jnp.concatenate(
-        [two[:, :cut], (wide(two[:, cut:]) + wide(lower)).astype(jnp.bfloat16)], 1
-    )
-    return [own, one, two]
 
 
 def collected(blocks):
@@ -218,24 +190,22 @@
     )(place, *(pltpu.with_memory_space_constraint(x, pltpu.HBM) for x in sources))
 
 
-def added_kernel(kept_ref, taken_ref, left_ref, right_ref):
-    total = kept_ref[...].astype(jnp.float32) + taken_ref[...].astype(jnp.float32)
-    cut = left_ref.shape[1]
-    left_ref[...] = total[:, :cut].astype(jnp.bfloat16)
-    right_ref[...] = total[:, cut:].astype(jnp.bfloat16)
-
-
-def added(kept, taken, cut):
+def added_kernel(kept_ref, taken_ref, *blocks):
+    low = 0
+    for block in blocks:
+        rows = slice(low, low + block.shape[0])
+        total = kept_ref[rows].astype(jnp.float32) + taken_ref[rows].astype(jnp.float32)
+        block[...] = total.astype(jnp.bfloat16)
+        low += block.shape[0]
+
+
+def added(kept, taken, counts):
     in_vmem = pl.BlockSpec(memory_space=pltpu.VMEM)
-    count, width = kept.shape
     return pl.pallas_call(
         added_kernel,
         in_specs=[in_vmem] * 2,
-        out_specs=[in_vmem] * 2,
-        out_shape=[
-            pltpu.VMEM((count, cut), jnp.bfloat16),
-            pltpu.VMEM((count, width - cut), jnp.bfloat16),
-        ],
+        out_specs=[in_vmem] * len(counts),
+        out_shape=[pltpu.VMEM((count, kept.shape[1]), jnp.bfloat16) for count in counts],
         compiler_params=pltpu.CompilerParams(vmem_limit_bytes=VMEM_LIMIT),
     )(*(pltpu.with_memory_space_constraint(x, pltpu.VMEM) for x in (kept, taken)))
 
@@ -310,64 +280,37 @@
         jnp.concatenate([jnp.where(first, keep, taken), jnp.where(first, taken, keep)], 0)
     )
 
-    def sums_of(own, weights, filling=False):
-        last = len(own) - 1
-        bare = [
-            [block[:, : block.shape[1] - (LANES if i == last else 0)] for block in segment]
-            for i, segment in enumerate(own)
-        ]
-        other = [[swap(block, "core", 1) for block in segment] for segment in bare]
+    def sums_of(blocks, weights, filling=False):
+        own = row_major(jnp.concatenate(blocks, 0))
+        other = swap(own[:, :part], "core", 1)
         keep, give, *filled = gated_sums(
-            place, top_count, own, other, *weights, filling
+            place, top_count, [[own]], [[other]], *weights, filling
         )
         return keep, give, filled or weights
 
-    def chip_sums(keep, give):
-        return (wide(keep) + wide(swap(give, "core", 1))).astype(jnp.bfloat16)
+    def chip_sums(keep, give, blocks):
+        return added(keep, swap(give, "core", 1), [block.shape[0] for block in blocks])
 
     chip_blocks = [chip_rows] + [swap(chip_rows, "chip", j) for j in range(1, chips)]
-    direct = [swap(chip_rows, "dp", k) for k in range(1, groups)]
-    far = row_major(jnp.concatenate(chip_blocks[1:], 0))
-    held = row_major(jnp.concatenate([*chip_blocks, *direct], 0))
-    near = spread_near(far)
+    low = [row_major(jnp.concatenate(chip_blocks[:near_chips], 0))]
+    low += [swap(low[0], "dp", k) for k in range(1, groups)]
+    high = [row_major(jnp.concatenate(chip_blocks[near_chips:], 0))]
+    high += [swap(high[0], "dp", k) for k in range(1, groups)]
+    sets = [[*low, high[0]], high[1:]]
+    if sum(block.shape[0] for block in sets[0]) > MOST_ROWS:
+        sets = [[block] for blocks in sets for block in blocks]
     weights = (in_weight, out_weight.reshape(per_device * half_width, width))
-    keep, give, weights = sums_of([[held]], weights, filling=True)
-    near = behind(near, give)
-    rest = spread_rest(near)
-    first_sum = chip_sums(keep, give)
-    own_sum = first_sum[: chips * 2 * rows]
-    direct_sums = [
-        first_sum[low : low + 2 * rows]
-        for low in range(chips * 2 * rows, first_sum.shape[0], 2 * rows)
-    ]
-    if rest:
-        near = row_major(jnp.concatenate(near, 0))
-        keep, give, _ = sums_of([[near]], weights)
-        pair = chip_sums(keep, give)
-        sums = [pair[: far.shape[0]], pair[far.shape[0] :]]
-        rest = behind(rest, give)
-        keep, give, _ = sums_of([[half] for half in rest], weights)
-        cut = rest[0].shape[1]
-        diagonal = added(keep, swap(give, "core", 1), cut)
-        diagonal = [
-            jnp.concatenate([block, half], 0)
-            for block, half in zip((direct_sums[2][:, :cut], direct_sums[2][:, cut:]), diagonal)
-        ]
-        sums = [jnp.concatenate([o, s], 0) for o, s in zip(direct_sums, sums)]
-        sums = with_fourth([own_sum, *sums], diagonal)
-        metas = [held, near, rest[1]]
-    else:
-        sums = [own_sum]
-        for block, o in zip(near, direct_sums):
-            keep, give, _ = sums_of([[block]], weights)
-            sums += [jnp.concatenate([o, chip_sums(keep, give)], 0)]
-        metas = [held, *near]
-    metas = [block[:, block.shape[1] - LANES :] for block in metas]
-    border = 2 * near_chips * rows
-    total = collected([block[border:] for block in sums])
-    blocks = [total[low : low + 2 * rows] for low in range(0, total.shape[0], 2 * rows)]
-    total = collected(behind([block[:border] for block in sums], total))
-    blocks = [total[low : low + 2 * rows] for low in range(0, border, 2 * rows)] + blocks
+    sums, give = [], None
+    for number, blocks in enumerate(sets):
+        if number:
+            blocks = behind(blocks, give)
+        keep, give, weights = sums_of(blocks, weights, filling=number == 0)
+        sums += chip_sums(keep, give, blocks)
+    total = collected(sums[groups:])
+    blocks = [total[at : at + 2 * rows] for at in range(0, total.shape[0], 2 * rows)]
+    total = collected(behind(sums[:groups], total))
+    blocks = [total[at : at + 2 * rows] for at in range(0, total.shape[0], 2 * rows)] + blocks
+    metas = [block[:, part:] for block in low + high]
     total = wide(blocks[0])
     for j in range(1, chips):
         total = total + wide(swap(blocks[j], "chip", j))

time: 74.9 us -> 78.7 us (1.051)
  waiting for transfers between devices: 26.5 us -> 33.6 us
  Pallas kernels: 19.1 us -> 16 us
    ppermute x28 -> x24, waiting for transfers between devices: 26.5 us -> 33.6 us  [swap(): return row_major(lax.ppermute(row_major(value), axis, pairs))]
    pallas_call x3 -> x2, Pallas kernels: 16 us -> 12.4 us  [gated_sums(): pl.pallas_call(lambda *refs: sums_kernel((widths, block_count, top_count)...]
    ppermute x28 -> x24, starting transfers between devices: 25.6 us -> 26 us  [swap(): return row_major(lax.ppermute(row_major(value), axis, pairs))]
  transfers between devices with their start and end apart: 28 -> 24, of which waited for: 16 -> 13; matrix products, arithmetic and copies ran while one was open for 2% -> 1% of each run, Pallas kernels for 23% -> 18%
where the time goes in v12:
time: 78.7 us; the launch traced here: 78.5 us
  waiting for transfers between devices  33.6 us (43%)
  starting transfers between devices  26 us (33%)
  Pallas kernels  16 us (20%)
  other arithmetic  1.15 us (1%)
  local copies, waits for them, and re-layouts  0.9 us (1%)
  between operations  0.89 us (1%)
    ppermute x24, waiting for transfers between devices, swap(): return row_major(lax.ppermute(row_major(value), axis, pairs))  33.6 us
    ppermute x24, starting transfers between devices, swap(): return row_major(lax.ppermute(row_major(value), axis, pairs))  26 us
    pallas_call x2, Pallas kernels, gated_sums(): pl.pallas_call(lambda *refs: sums_kernel((widths, block_count, top_count)...  12.4 us
    pallas_call x1, Pallas kernels, planned_load(): pl.pallas_call(lambda *refs: load_kernel(layout, *refs), in_specs=[pl.Blo...  1.58 us
  transfers between devices with their start and end apart: 24, of which 13 were waited for; matrix products, arithmetic and copies ran while one was open for 1% of the time, Pallas kernels for 18%

profile of v12, /device:TPU:0, one launch (start us, length us, event | category | flops | bytes accessed | tf_op | source)
XLA Modules:
  0.0 78.5 jit_solution(10595213460741610536)
XLA Ops:
  0.6 0.1 pad_add_fusion.place.refs_0_
  0.7 1.6 %shard_map.77 = (bf16[12,2176]{1,0:T(8,128)(2,1)S(1)}, bf16[12,2176]{1,0:T(8,128)(2,1)S(1)}) custom-call(s32[2]{0:T(128)S(1)} %pad_add_fusion.place.refs_0_, bf16[12,4096]{1,0:T(8,128)(2,1)} %refs_0_.2, s32[8,12]{1,0:T(8,128)} %bitcast.8, f32[8,12]{1,0:T(8,128)} %bitcast.9), custom_call_target="tpu_custom_call" | custom-call | tf_op jit(solution)/shard_map/pallas_call | solution.py:181
  2.3 0.5 collective-permute-start
  2.8 0.9 %collective-permute-done = bf16[12,2176]{1,0:T(8,128)(2,1)S(1)} collective-permute-done((bf16[12,2176]{1,0:T(8,128)(2,1)S(1)}, bf16[12,2176]{1,0:T(8,128)(2,1)S(1)}, u32[]{:S(2)}, u32[]{:S(2)}) %collective-permute-start) | collective-permute-done | bytes 52256 | tf_op jit(solution)/shard_map/ppermute | solution.py:24
  3.8 3.0 %collective-permute-start.1 = (bf16[24,2176]{1,0:T(8,128)(2,1)S(1)}, bf16[24,2176]{1,0:T(8,128)(2,1)S(1)}, u32[]{:S(2)}, u32[]{:S(2)}) collective-permute-start(bf16[24,2176]{1,0:T(8,128)(2,1)S(1)} %pad_maximum_fusion.2), channel_id=1, source_target_pairs={{0,2},{2,0},{4,6},{6,4},{1,3},{3,1},{5,7},{7,5},{8,10},{10,8},{12,... | collective-permute-start | bytes 313352 | tf_op jit(solution)/shard_map/ppermute | solution.py:24
  6.8 3.2 %collective-permute-done.1 = bf16[24,2176]{1,0:T(8,128)(2,1)S(1)} collective-permute-done((bf16[24,2176]{1,0:T(8,128)(2,1)S(1)}, bf16[24,2176]{1,0:T(8,128)(2,1)S(1)}, u32[]{:S(2)}, u32[]{:S(2)}) %collective-permute-start.1) | collective-permute-done | bytes 104480 | tf_op jit(solution)/shard_map/ppermute | solution.py:24
  10.1 1.7 %collective-permute-start.2 = (bf16[48,2176]{1,0:T(8,128)(2,1)S(1)}, bf16[48,2176]{1,0:T(8,128)(2,1)S(1)}, u32[]{:S(2)}, u32[]{:S(2)}) collective-permute-start(bf16[48,2176]{1,0:T(8,128)(2,1)S(1)} %get-tuple-element.49), channel_id=1, source_target_pairs={{0,8},{8,0},{16,24},{24,16},{1,9},{9,1},{17,25},{25,17},{2,10},{10... | collective-permute-start | bytes 626696 | tf_op jit(solution)/shard_map/ppermute | solution.py:24
  11.8 3.6 %collective-permute-start.6 = (bf16[24,2176]{1,0:T(8,128)(2,1)S(1)}, bf16[24,2176]{1,0:T(8,128)(2,1)S(1)}, u32[]{:S(2)}, u32[]{:S(2)}) collective-permute-start(bf16[24,2176]{1,0:T(8,128)(2,1)S(1)} %pad_maximum_fusion.2), channel_id=1, source_target_pairs={{0,6},{2,4},{4,2},{6,0},{1,7},{3,5},{5,3},{7,1},{8,14},{10,12},{12... | collective-permute-start | bytes 313352 | tf_op jit(solution)/shard_map/ppermute | solution.py:24
  15.4 1.5 %collective-permute-start.3 = (bf16[48,2176]{1,0:T(8,128)(2,1)S(1)}, bf16[48,2176]{1,0:T(8,128)(2,1)S(1)}, u32[]{:S(2)}, u32[]{:S(2)}) collective-permute-start(bf16[48,2176]{1,0:T(8,128)(2,1)S(1)} %get-tuple-element.49), channel_id=1, source_target_pairs={{0,16},{8,24},{16,0},{24,8},{1,17},{9,25},{17,1},{25,9},{2,18},{10... | collective-permute-start | bytes 626696 | tf_op jit(solution)/shard_map/ppermute | solution.py:24
  16.9 0.5 collective-permute-start.4
  17.4 8.3 %collective-permute-done.3 = bf16[48,2176]{1,0:T(8,128)(2,1)S(1)} collective-permute-done((bf16[48,2176]{1,0:T(8,128)(2,1)S(1)}, bf16[48,2176]{1,0:T(8,128)(2,1)S(1)}, u32[]{:S(2)}, u32[]{:S(2)}) %collective-permute-start.3) | collective-permute-done | bytes 208928 | tf_op jit(solution)/shard_map/ppermute | solution.py:24
  25.8 0.1 slice.68
  25.9 0.1 collective-permute-start.7
  26.0 0.6 collective-permute-start.9
  26.6 2.4 %collective-permute-start.11 = (bf16[48,2176]{1,0:T(8,128)(2,1)S(1)}, bf16[48,2176]{1,0:T(8,128)(2,1)S(1)}, u32[]{:S(2)}, u32[]{:S(2)}) collective-permute-start(bf16[48,2176]{1,0:T(8,128)(2,1)S(1)} %get-tuple-element.57), channel_id=1, source_target_pairs={{0,24},{8,16},{16,8},{24,0},{1,25},{9,17},{17,9},{25,1},{2,26},{10... | collective-permute-start | bytes 626696 | tf_op jit(solution)/shard_map/ppermute | solution.py:24
  29.1 0.5 collective-permute-start.10
  29.6 8.8 %shard_map.78 = (bf16[240,2048]{1,0:T(8,128)(2,1)S(1)}, bf16[240,2048]{1,0:T(8,128)(2,1)S(1)}, bf16[2,4096,768]{2,1,0:T(8,128)(2,1)S(1)}, bf16[768,4096]{1,0:T(8,128)(2,1)S(1)}) custom-call(s32[2]{0:T(128)S(1)} %pad_add_fusion.place.refs_0_, bf16[240,2176]{1,0:T(8,128)(2,1)S(1)} %get-tuple-element.56.refs_1_, ...), custom_call_target="tpu_custom_call" | custom-call | flops 4529848320 | bytes 18874368 | tf_op jit(solution)/shard_map/pallas_call | solution.py:134
  38.4 0.7 collective-permute-done.11
  39.1 1.4 %collective-permute-done.10 = bf16[48,2176]{1,0:T(8,128)(2,1)S(1)} collective-permute-done((bf16[48,2176]{1,0:T(8,128)(2,1)S(1)}, bf16[48,2176]{1,0:T(8,128)(2,1)S(1)}, u32[]{:S(2)}, u32[]{:S(2)}) %collective-permute-start.10) | collective-permute-done | bytes 208928 | tf_op jit(solution)/shard_map/ppermute | solution.py:24
  40.6 0.1 collective-permute-start.12
  40.7 0.5 collective-permute-start.8
  41.2 1.5 %collective-permute-done.12.refs_2_ = bf16[144,2048]{1,0:T(8,128)(2,1)S(1)} collective-permute-done((bf16[144,2048]{1,0:T(8,128)(2,1)S(1)}, bf16[144,2048]{1,0:T(8,128)(2,1)S(1)}, u32[]{:S(2)}, u32[]{:S(2)}) %collective-permute-start.12) | collective-permute-done | bytes 589856 | tf_op jit(solution)/shard_map/ppermute | solution.py:24
  42.7 3.6 %shard_map.80 = (bf16[144,2048]{1,0:T(8,128)(2,1)S(1)}, bf16[144,2048]{1,0:T(8,128)(2,1)S(1)}) custom-call(s32[2]{0:T(128)S(1)} %pad_add_fusion.place.refs_0_, bf16[144,2176]{1,0:T(8,128)(2,1)S(1)} %constant_dynamic-update-slice_fusion.8.refs_1_, bf16[144,2048]{1,0:T(8,128)(2,1)S(1)} %collective-permute-done.12.refs_2_, ...), custom_call_target="tpu_custom_call" | custom-call | flops 2717908992 | tf_op jit(solution)/shard_map/pallas_call | solution.py:134
  46.4 0.2 collective-permute-start.13
  46.6 1.8 %collective-permute-done.13.taken_ref = bf16[144,2048]{1,0:T(8,128)(2,1)S(1)} collective-permute-done((bf16[144,2048]{1,0:T(8,128)(2,1)S(1)}, bf16[144,2048]{1,0:T(8,128)(2,1)S(1)}, u32[]{:S(2)}, u32[]{:S(2)}) %collective-permute-start.13) | collective-permute-done | bytes 589856 | tf_op jit(solution)/shard_map/ppermute | solution.py:24
  48.4 0.1 shard_map.81
  48.6 0.6 collective-permute-start.14
  49.2 0.5 collective-permute-start.15
  49.7 2.4 %collective-permute-start.16 = (bf16[48,2048]{1,0:T(8,128)(2,1)S(1)}, bf16[48,2048]{1,0:T(8,128)(2,1)S(1)}, u32[]{:S(2)}, u32[]{:S(2)}) collective-permute-start(bf16[48,2048]{1,0:T(8,128)(2,1)S(1)} %get-tuple-element.43), channel_id=1, source_target_pairs={{0,24},{8,16},{16,8},{24,0},{1,25},{9,17},{17,9},{25,1},{2,26},{10... | collective-permute-start | bytes 589832 | tf_op jit(solution)/shard_map/ppermute | solution.py:24
  52.1 0.3 shard_map.79
  52.4 4.0 %collective-permute-done.14 = bf16[48,2048]{1,0:T(8,128)(2,1)S(1)} collective-permute-done((bf16[48,2048]{1,0:T(8,128)(2,1)S(1)}, bf16[48,2048]{1,0:T(8,128)(2,1)S(1)}, u32[]{:S(2)}, u32[]{:S(2)}) %collective-permute-start.14) | collective-permute-done | bytes 196640 | tf_op jit(solution)/shard_map/ppermute | solution.py:24
  56.4 3.7 %collective-permute-done.15 = bf16[48,2048]{1,0:T(8,128)(2,1)S(1)} collective-permute-done((bf16[48,2048]{1,0:T(8,128)(2,1)S(1)}, bf16[48,2048]{1,0:T(8,128)(2,1)S(1)}, u32[]{:S(2)}, u32[]{:S(2)}) %collective-permute-start.15) | collective-permute-done | bytes 196640 | tf_op jit(solution)/shard_map/ppermute | solution.py:24
  60.1 0.1 add_convert_fusion.1
  60.2 1.6 %collective-permute-start.17 = (bf16[48,2048]{1,0:T(8,128)(2,1)S(1)}, bf16[48,2048]{1,0:T(8,128)(2,1)S(1)}, u32[]{:S(2)}, u32[]{:S(2)}) collective-permute-start(bf16[48,2048]{1,0:T(8,128)(2,1)S(1)} %get-tuple-element.45), channel_id=1, source_target_pairs={{0,8},{8,0},{16,24},{24,16},{1,9},{9,1},{17,25},{25,17},{2,10},{10... | collective-permute-start | bytes 589832 | tf_op jit(solution)/shard_map/ppermute | solution.py:24
  61.7 0.5 collective-permute-start.18
  62.2 1.5 %collective-permute-start.19 = (bf16[48,2048]{1,0:T(8,128)(2,1)S(1)}, bf16[48,2048]{1,0:T(8,128)(2,1)S(1)}, u32[]{:S(2)}, u32[]{:S(2)}) collective-permute-start(bf16[48,2048]{1,0:T(8,128)(2,1)S(1)} %get-tuple-element.47), channel_id=1, source_target_pairs={{0,24},{8,16},{16,8},{24,0},{1,25},{9,17},{17,9},{25,1},{2,26},{10... | collective-permute-start | bytes 589832 | tf_op jit(solution)/shard_map/ppermute | solution.py:24
  63.8 2.7 %collective-permute-start.21 = (bf16[24,2048]{1,0:T(8,128)(2,1)S(1)}, bf16[24,2048]{1,0:T(8,128)(2,1)S(1)}, u32[]{:S(2)}, u32[]{:S(2)}) collective-permute-start(bf16[24,2048]{1,0:T(8,128)(2,1)S(1)} %get-tuple-element.50), channel_id=1, source_target_pairs={{0,4},{2,6},{4,0},{6,2},{1,5},{3,7},{5,1},{7,3},{8,12},{10,14},{12... | collective-permute-start | bytes 294920 | tf_op jit(solution)/shard_map/ppermute | solution.py:24
  66.5 0.3 collective-permute-start.22
  66.7 1.2 %collective-permute-done.17 = bf16[48,2048]{1,0:T(8,128)(2,1)S(1)} collective-permute-done((bf16[48,2048]{1,0:T(8,128)(2,1)S(1)}, bf16[48,2048]{1,0:T(8,128)(2,1)S(1)}, u32[]{:S(2)}, u32[]{:S(2)}) %collective-permute-start.17) | collective-permute-done | bytes 196640 | tf_op jit(solution)/shard_map/ppermute | solution.py:24
  68.0 3.6 %collective-permute-done.18 = bf16[48,2048]{1,0:T(8,128)(2,1)S(1)} collective-permute-done((bf16[48,2048]{1,0:T(8,128)(2,1)S(1)}, bf16[48,2048]{1,0:T(8,128)(2,1)S(1)}, u32[]{:S(2)}, u32[]{:S(2)}) %collective-permute-start.18) | collective-permute-done | bytes 196640 | tf_op jit(solution)/shard_map/ppermute | solution.py:24
  71.6 0.1 add_convert_fusion
  71.8 0.6 collective-permute-start.20
  72.4 1.6 %shard_map.82 = f32[1,128]{1,0:T(1,128)S(1)} custom-call(s32[8]{0:T(128)S(1)} %copy-done, bf16[48,128]{1,0:T(8,128)(2,1)S(1)} %slice.76.refs_1_, bf16[48,128]{1,0:T(8,128)(2,1)S(1)} %slice.77.refs_2_, bf16[48,128]{1,0:T(8,128)(2,1)S(1)} %slice.78.refs_3_, bf16[48,128]{1,0:T(8,128)(2,1)S(1)} %slice.79.refs_4_, bf16[48,128]{1,0:T(8,128)(2,1)S(1)} %slice.80.refs_5_, ...), custom_call_target="tpu_custom_call" | custom-call | tf_op jit(solution)/shard_map/pallas_call | solution.py:253
  74.0 2.4 %collective-permute-done.20 = bf16[24,2048]{1,0:T(8,128)(2,1)S(1)} collective-permute-done((bf16[24,2048]{1,0:T(8,128)(2,1)S(1)}, bf16[24,2048]{1,0:T(8,128)(2,1)S(1)}, u32[]{:S(2)}, u32[]{:S(2)}) %collective-permute-start.20) | collective-permute-done | bytes 98336 | tf_op jit(solution)/shard_map/ppermute | solution.py:24
  76.5 0.1 collective-permute-start.23
  76.6 0.5 slice_bitcast_fusion
  77.1 0.7 collective-permute-done.23
  77.9 0.7 pad_maximum_fusion.1
  (39 shorter events, 0.5 us)
Async XLA Ops:
  2.3 1.4 %collective-permute-start = (bf16[12,2176]{1,0:T(8,128)(2,1)S(1)}, bf16[12,2176]{1,0:T(8,128)(2,1)S(1)}, u32[]{:S(2)}, u32[]{:S(2)}) collective-permute-start(bf16[12,2176]{1,0:T(8,128)(2,1)S(1)} %get-tuple-element.26), channel_id=1, source_target_pairs={{0,1},{1,0},{2,3},{3,2},{4,5},{5,4},{6,7},{7,6},{8,9},{9,8},{10,11... | collective-permute-start | bytes 156680 | tf_op jit(solution)/shard_map/ppermute | solution.py:24
  3.8 6.2 %collective-permute-start.1 = (bf16[24,2176]{1,0:T(8,128)(2,1)S(1)}, bf16[24,2176]{1,0:T(8,128)(2,1)S(1)}, u32[]{:S(2)}, u32[]{:S(2)}) collective-permute-start(bf16[24,2176]{1,0:T(8,128)(2,1)S(1)} %pad_maximum_fusion.2), channel_id=1, source_target_pairs={{0,2},{2,0},{4,6},{6,4},{1,3},{3,1},{5,7},{7,5},{8,10},{10,8},{12,... | collective-permute-start | bytes 313352 | tf_op jit(solution)/shard_map/ppermute | solution.py:24
  10.1 7.3 %collective-permute-start.2 = (bf16[48,2176]{1,0:T(8,128)(2,1)S(1)}, bf16[48,2176]{1,0:T(8,128)(2,1)S(1)}, u32[]{:S(2)}, u32[]{:S(2)}) collective-permute-start(bf16[48,2176]{1,0:T(8,128)(2,1)S(1)} %get-tuple-element.49), channel_id=1, source_target_pairs={{0,8},{8,0},{16,24},{24,16},{1,9},{9,1},{17,25},{25,17},{2,10},{10... | collective-permute-start | bytes 626696 | tf_op jit(solution)/shard_map/ppermute | solution.py:24
  11.8 14.0 %collective-permute-start.6 = (bf16[24,2176]{1,0:T(8,128)(2,1)S(1)}, bf16[24,2176]{1,0:T(8,128)(2,1)S(1)}, u32[]{:S(2)}, u32[]{:S(2)}) collective-permute-start(bf16[24,2176]{1,0:T(8,128)(2,1)S(1)} %pad_maximum_fusion.2), channel_id=1, source_target_pairs={{0,6},{2,4},{4,2},{6,0},{1,7},{3,5},{5,3},{7,1},{8,14},{10,12},{12... | collective-permute-start | bytes 313352 | tf_op jit(solution)/shard_map/ppermute | solution.py:24
  15.4 10.4 %collective-permute-start.5 = (bf16[24,2176]{1,0:T(8,128)(2,1)S(1)}, bf16[24,2176]{1,0:T(8,128)(2,1)S(1)}, u32[]{:S(2)}, u32[]{:S(2)}) collective-permute-start(bf16[24,2176]{1,0:T(8,128)(2,1)S(1)} %pad_maximum_fusion.2), channel_id=1, source_target_pairs={{0,4},{2,6},{4,0},{6,2},{1,5},{3,7},{5,1},{7,3},{8,12},{10,14},{12... | collective-permute-start | bytes 313352 | tf_op jit(solution)/shard_map/ppermute | solution.py:24
  15.4 10.3 %collective-permute-start.3 = (bf16[48,2176]{1,0:T(8,128)(2,1)S(1)}, bf16[48,2176]{1,0:T(8,128)(2,1)S(1)}, u32[]{:S(2)}, u32[]{:S(2)}) collective-permute-start(bf16[48,2176]{1,0:T(8,128)(2,1)S(1)} %get-tuple-element.49), channel_id=1, source_target_pairs={{0,16},{8,24},{16,0},{24,8},{1,17},{9,25},{17,1},{25,9},{2,18},{10... | collective-permute-start | bytes 626696 | tf_op jit(solution)/shard_map/ppermute | solution.py:24
  16.9 8.8 %collective-permute-start.4 = (bf16[48,2176]{1,0:T(8,128)(2,1)S(1)}, bf16[48,2176]{1,0:T(8,128)(2,1)S(1)}, u32[]{:S(2)}, u32[]{:S(2)}) collective-permute-start(bf16[48,2176]{1,0:T(8,128)(2,1)S(1)} %get-tuple-element.49), channel_id=1, source_target_pairs={{0,24},{8,16},{16,8},{24,0},{1,25},{9,17},{17,9},{25,1},{2,26},{10... | collective-permute-start | bytes 626696 | tf_op jit(solution)/shard_map/ppermute | solution.py:24
  25.9 3.6 %collective-permute-start.7 = (bf16[240,2048]{1,0:T(8,128)(2,1)S(1)}, bf16[240,2048]{1,0:T(8,128)(2,1)S(1)}, u32[]{:S(2)}, u32[]{:S(2)}) collective-permute-start(bf16[240,2048]{1,0:T(8,128)(2,1)S(1)} %slice.68), channel_id=1, source_target_pairs={{0,1},{1,0},{2,3},{3,2},{4,5},{5,4},{6,7},{7,6},{8,9},{9,8},{10,11... | collective-permute-start | bytes 2949128 | tf_op jit(solution)/shard_map/ppermute | solution.py:24
  26.0 12.4 %collective-permute-start.9 = (bf16[48,2176]{1,0:T(8,128)(2,1)S(1)}, bf16[48,2176]{1,0:T(8,128)(2,1)S(1)}, u32[]{:S(2)}, u32[]{:S(2)}) collective-permute-start(bf16[48,2176]{1,0:T(8,128)(2,1)S(1)} %get-tuple-element.57), channel_id=1, source_target_pairs={{0,8},{8,0},{16,24},{24,16},{1,9},{9,1},{17,25},{25,17},{2,10},{10... | collective-permute-start | bytes 626696 | tf_op jit(solution)/shard_map/ppermute | solution.py:24
  26.6 12.5 %collective-permute-start.11 = (bf16[48,2176]{1,0:T(8,128)(2,1)S(1)}, bf16[48,2176]{1,0:T(8,128)(2,1)S(1)}, u32[]{:S(2)}, u32[]{:S(2)}) collective-permute-start(bf16[48,2176]{1,0:T(8,128)(2,1)S(1)} %get-tuple-element.57), channel_id=1, source_target_pairs={{0,24},{8,16},{16,8},{24,0},{1,25},{9,17},{17,9},{25,1},{2,26},{10... | collective-permute-start | bytes 626696 | tf_op jit(solution)/shard_map/ppermute | solution.py:24
  29.1 11.4 %collective-permute-start.10 = (bf16[48,2176]{1,0:T(8,128)(2,1)S(1)}, bf16[48,2176]{1,0:T(8,128)(2,1)S(1)}, u32[]{:S(2)}, u32[]{:S(2)}) collective-permute-start(bf16[48,2176]{1,0:T(8,128)(2,1)S(1)} %get-tuple-element.57), channel_id=1, source_target_pairs={{0,16},{8,24},{16,0},{24,8},{1,17},{9,25},{17,1},{25,9},{2,18},{10... | collective-permute-start | bytes 626696 | tf_op jit(solution)/shard_map/ppermute | solution.py:24
  40.6 2.1 %collective-permute-start.12 = (bf16[144,2048]{1,0:T(8,128)(2,1)S(1)}, bf16[144,2048]{1,0:T(8,128)(2,1)S(1)}, u32[]{:S(2)}, u32[]{:S(2)}) collective-permute-start(bf16[144,2048]{1,0:T(8,128)(2,1)S(1)} %slice.69), channel_id=1, source_target_pairs={{0,1},{1,0},{2,3},{3,2},{4,5},{5,4},{6,7},{7,6},{8,9},{9,8},{10,11... | collective-permute-start | bytes 1769480 | tf_op jit(solution)/shard_map/ppermute | solution.py:24
  40.7 11.4 %collective-permute-start.8 = (bf16[240,2048]{1,0:T(8,128)(2,1)S(1)}, bf16[240,2048]{1,0:T(8,128)(2,1)S(1)}, u32[]{:S(2)}, u32[]{:S(2)}) collective-permute-start(bf16[240,2048]{1,0:T(8,128)(2,1)S(1)} %get-tuple-element.28), channel_id=1, source_target_pairs={{0,1},{1,0},{2,3},{3,2},{4,5},{5,4},{6,7},{7,6},{8,9},{9,8},{10,11... | collective-permute-start | bytes 2949128 | tf_op jit(solution)/shard_map/ppermute | solution.py:24
  42.7 29.7 %copy-start = (s32[8]{0:T(128)S(1)}, s32[8]{0:T(128)}, u32[]{:S(2)}) copy-start(s32[8]{0:T(128)} %refs_0_.3) | copy-start | bytes 100
  46.4 2.1 %collective-permute-start.13 = (bf16[144,2048]{1,0:T(8,128)(2,1)S(1)}, bf16[144,2048]{1,0:T(8,128)(2,1)S(1)}, u32[]{:S(2)}, u32[]{:S(2)}) collective-permute-start(bf16[144,2048]{1,0:T(8,128)(2,1)S(1)} %get-tuple-element.40), channel_id=1, source_target_pairs={{0,1},{1,0},{2,3},{3,2},{4,5},{5,4},{6,7},{7,6},{8,9},{9,8},{10,11... | collective-permute-start | bytes 1769480 | tf_op jit(solution)/shard_map/ppermute | solution.py:24
  48.6 7.8 %collective-permute-start.14 = (bf16[48,2048]{1,0:T(8,128)(2,1)S(1)}, bf16[48,2048]{1,0:T(8,128)(2,1)S(1)}, u32[]{:S(2)}, u32[]{:S(2)}) collective-permute-start(bf16[48,2048]{1,0:T(8,128)(2,1)S(1)} %get-tuple-element.41), channel_id=1, source_target_pairs={{0,8},{8,0},{16,24},{24,16},{1,9},{9,1},{17,25},{25,17},{2,10},{10... | collective-permute-start | bytes 589832 | tf_op jit(solution)/shard_map/ppermute | solution.py:24
  49.2 10.9 %collective-permute-start.15 = (bf16[48,2048]{1,0:T(8,128)(2,1)S(1)}, bf16[48,2048]{1,0:T(8,128)(2,1)S(1)}, u32[]{:S(2)}, u32[]{:S(2)}) collective-permute-start(bf16[48,2048]{1,0:T(8,128)(2,1)S(1)} %get-tuple-element.42), channel_id=1, source_target_pairs={{0,16},{8,24},{16,0},{24,8},{1,17},{9,25},{17,1},{25,9},{2,18},{10... | collective-permute-start | bytes 589832 | tf_op jit(solution)/shard_map/ppermute | solution.py:24
  49.7 10.4 %collective-permute-start.16 = (bf16[48,2048]{1,0:T(8,128)(2,1)S(1)}, bf16[48,2048]{1,0:T(8,128)(2,1)S(1)}, u32[]{:S(2)}, u32[]{:S(2)}) collective-permute-start(bf16[48,2048]{1,0:T(8,128)(2,1)S(1)} %get-tuple-element.43), channel_id=1, source_target_pairs={{0,24},{8,16},{16,8},{24,0},{1,25},{9,17},{17,9},{25,1},{2,26},{10... | collective-permute-start | bytes 589832 | tf_op jit(solution)/shard_map/ppermute | solution.py:24
  60.2 7.8 %collective-permute-start.17 = (bf16[48,2048]{1,0:T(8,128)(2,1)S(1)}, bf16[48,2048]{1,0:T(8,128)(2,1)S(1)}, u32[]{:S(2)}, u32[]{:S(2)}) collective-permute-start(bf16[48,2048]{1,0:T(8,128)(2,1)S(1)} %get-tuple-element.45), channel_id=1, source_target_pairs={{0,8},{8,0},{16,24},{24,16},{1,9},{9,1},{17,25},{25,17},{2,10},{10... | collective-permute-start | bytes 589832 | tf_op jit(solution)/shard_map/ppermute | solution.py:24
  61.7 9.9 %collective-permute-start.18 = (bf16[48,2048]{1,0:T(8,128)(2,1)S(1)}, bf16[48,2048]{1,0:T(8,128)(2,1)S(1)}, u32[]{:S(2)}, u32[]{:S(2)}) collective-permute-start(bf16[48,2048]{1,0:T(8,128)(2,1)S(1)} %get-tuple-element.46), channel_id=1, source_target_pairs={{0,16},{8,24},{16,0},{24,8},{1,17},{9,25},{17,1},{25,9},{2,18},{10... | collective-permute-start | bytes 589832 | tf_op jit(solution)/shard_map/ppermute | solution.py:24
  62.2 9.4 %collective-permute-start.19 = (bf16[48,2048]{1,0:T(8,128)(2,1)S(1)}, bf16[48,2048]{1,0:T(8,128)(2,1)S(1)}, u32[]{:S(2)}, u32[]{:S(2)}) collective-permute-start(bf16[48,2048]{1,0:T(8,128)(2,1)S(1)} %get-tuple-element.47), channel_id=1, source_target_pairs={{0,24},{8,16},{16,8},{24,0},{1,25},{9,17},{17,9},{25,1},{2,26},{10... | collective-permute-start | bytes 589832 | tf_op jit(solution)/shard_map/ppermute | solution.py:24
  63.8 10.3 %collective-permute-start.21 = (bf16[24,2048]{1,0:T(8,128)(2,1)S(1)}, bf16[24,2048]{1,0:T(8,128)(2,1)S(1)}, u32[]{:S(2)}, u32[]{:S(2)}) collective-permute-start(bf16[24,2048]{1,0:T(8,128)(2,1)S(1)} %get-tuple-element.50), channel_id=1, source_target_pairs={{0,4},{2,6},{4,0},{6,2},{1,5},{3,7},{5,1},{7,3},{8,12},{10,14},{12... | collective-permute-start | bytes 294920 | tf_op jit(solution)/shard_map/ppermute | solution.py:24
  66.5 7.6 %collective-permute-start.22 = (bf16[24,2048]{1,0:T(8,128)(2,1)S(1)}, bf16[24,2048]{1,0:T(8,128)(2,1)S(1)}, u32[]{:S(2)}, u32[]{:S(2)}) collective-permute-start(bf16[24,2048]{1,0:T(8,128)(2,1)S(1)} %get-tuple-element.51), channel_id=1, source_target_pairs={{0,6},{2,4},{4,2},{6,0},{1,7},{3,5},{5,3},{7,1},{8,14},{10,12},{12... | collective-permute-start | bytes 294920 | tf_op jit(solution)/shard_map/ppermute | solution.py:24
  71.8 4.7 %collective-permute-start.20 = (bf16[24,2048]{1,0:T(8,128)(2,1)S(1)}, bf16[24,2048]{1,0:T(8,128)(2,1)S(1)}, u32[]{:S(2)}, u32[]{:S(2)}) collective-permute-start(bf16[24,2048]{1,0:T(8,128)(2,1)S(1)} %slice.71), channel_id=1, source_target_pairs={{0,2},{2,0},{4,6},{6,4},{1,3},{3,1},{5,7},{7,5},{8,10},{10,8},{12,... | collective-permute-start | bytes 294920 | tf_op jit(solution)/shard_map/ppermute | solution.py:24
  76.5 1.3 %collective-permute-start.23 = (bf16[12,2048]{1,0:T(8,128)(2,1)S(1)}, bf16[12,2048]{1,0:T(8,128)(2,1)S(1)}, u32[]{:S(2)}, u32[]{:S(2)}) collective-permute-start(bf16[12,2048]{1,0:T(8,128)(2,1)S(1)} %broadcast_select_fusion.4), channel_id=1, source_target_pairs={{0,1},{1,0},{2,3},{3,2},{4,5},{5,4},{6,7},{7,6},{8,9},{9,8},{10,11... | collective-permute-start | bytes 147464 | tf_op jit(solution)/shard_map/ppermute | solution.py:24

commit v13 on v11

--- a/solution.py
+++ b/solution.py
@@ -9,6 +9,7 @@
 LANES = 128
 PART = 1024.0
 CHUNK = 1024
+MOST_ROWS = 512
 VMEM_LIMIT = 12 * 2**20
 GATE_MOST = 5
 
@@ -67,113 +68,164 @@
     return total.astype(jnp.bfloat16)
 
 
-def sums_kernel(layout, filling, *refs):
-    widths, block_count, top_count = layout
-    refs = list(refs)
-    place = refs.pop(0)
-    sides = [[[refs.pop(0) for _ in range(block_count)] for _ in widths] for _ in range(2)]
-    if filling:
-        up_hbm, down_hbm, keep_ref, give_ref, up, down, acc, hidden, sems = refs
-    else:
-        up, down, keep_ref, give_ref, acc, hidden = refs
-    core, first_expert = place[0], place[1]
-    per_device, width, both_width = up.shape
-    half_width = both_width // 2
-    part = width // 2
-    bases = [core * part, (1 - core) * part]
-    arrivals = {}
-    if filling:
-        copies = []
-        for side in range(2):
-            for low in range(0, part, CHUNK):
-                for s in range(per_device):
-                    at = pl.ds(pl.multiple_of(bases[side] + low, CHUNK), CHUNK)
-                    copies.append((up_hbm.at[s, at], up.at[s, at], (side, low)))
-        deep = down.shape[0]
-        for low in range(0, deep, half_width):
-            at = pl.ds(low, half_width)
-            copies.append((down_hbm.at[at], down.at[at], "down"))
-        for number, (source, target, key) in enumerate(copies):
-            copy = pltpu.make_async_copy(source, target, sems.at[number])
-            copy.start()
-            arrivals.setdefault(key, []).append(copy)
-
-    def arrive(key):
-        for copy in arrivals.get(key, ()):
-            copy.wait()
-
-    acc[...] = jnp.zeros_like(acc)
-    for side in range(2):
-        offset = 0
-        for blocks, seg_width in zip(sides[side], widths):
-            for low in range(0, seg_width, CHUNK):
-                arrive((side, offset + low))
-                held = [block[:, low : low + CHUNK] for block in blocks]
-                held = held[0] if len(held) == 1 else jnp.concatenate(held, 0)
-                rows = pl.ds(pl.multiple_of(bases[side] + offset + low, CHUNK), CHUNK)
-                for s in range(per_device):
-                    acc[s] += jnp.dot(held, up[s, rows], preferred_element_type=jnp.float32)
-            offset += seg_width
-
-    last = widths[-1]
-    meta = [block[:, last:].astype(jnp.float32) for block in sides[0][-1]]
-    meta = meta[0] if len(meta) == 1 else jnp.concatenate(meta, 0)
+def load_weights_kernel(up_ref, down_ref, _, up_out, down_out, mark_ref, sems):
+    copies = [
+        pltpu.make_async_copy(up_ref, up_out, sems.at[0]),
+        pltpu.make_async_copy(down_ref, down_out, sems.at[1]),
+    ]
+    for copy in copies:
+        copy.start()
+    mark_ref[...] = jnp.zeros_like(mark_ref)
+    for copy in copies:
+        copy.wait()
+
+
+def loaded(up, down, after):
+    return pl.pallas_call(
+        load_weights_kernel,
+        in_specs=[pl.BlockSpec(memory_space=pl.ANY)] * 3,
+        out_specs=[pl.BlockSpec(memory_space=pltpu.VMEM)] * 3,
+        out_shape=[
+            pltpu.VMEM(up.shape, up.dtype),
+            pltpu.VMEM(down.shape, down.dtype),
+            pltpu.VMEM((8, LANES), jnp.float32),
+        ],
+        scratch_shapes=[pltpu.SemaphoreType.DMA((2,))],
+        compiler_params=pltpu.CompilerParams(vmem_limit_bytes=VMEM_LIMIT),
+        cost_estimate=pl.CostEstimate(
+            flops=0, bytes_accessed=up.nbytes + down.nbytes, transcendentals=0
+        ),
+    )(*(pltpu.with_memory_space_constraint(x, pltpu.HBM) for x in (up, down)), after)
+
+
+def joined(blocks):
+    return blocks[0] if len(blocks) == 1 else jnp.concatenate(blocks, 0)
+
+
+def add_up(acc, segments, widths, up, base):
+    for blocks, width in zip(segments, widths):
+        for low in range(0, width, CHUNK):
+            held = joined([block[:, low : low + CHUNK] for block in blocks])
+            rows = pl.ds(pl.multiple_of(base, CHUNK), CHUNK)
+            for s in range(up.shape[0]):
+                acc[s] += jnp.dot(held, up[s, rows], preferred_element_type=jnp.float32)
+            base = base + CHUNK
+
+
+def make_hidden(hidden, acc, routed, width, first_expert, top_count):
+    meta = joined([block[:, width:].astype(jnp.float32) for block in routed])
     gates = sum(pltpu.roll(meta, LANES - k * top_count, 1) for k in (1, 2, 3))
     lanes = lax.broadcasted_iota(jnp.int32, meta.shape, 1)
-    for s in range(per_device):
+    half_width = acc.shape[2] // 2
+    for s in range(acc.shape[0]):
         chosen = (meta.astype(jnp.int32) == first_expert + s) & (lanes < top_count)
         own_gate = jnp.sum(jnp.where(chosen, gates, 0.0), 1, keepdims=True)
         gate_half, up_half = acc[s, :, :half_width], acc[s, :, half_width:]
         unit = gate_half * (1.0 / (1.0 + jnp.exp(-gate_half))) * up_half
         hidden[:, s * half_width : (s + 1) * half_width] = (unit * own_gate).astype(jnp.bfloat16)
 
-    arrive("down")
-    for base, out in ((bases[1], give_ref), (bases[0], keep_ref)):
-        for low in range(0, part, CHUNK):
-            columns = pl.ds(pl.multiple_of(base + low, CHUNK), CHUNK)
-            out[:, low : low + CHUNK] = jnp.dot(
-                hidden[...], down[:, columns], preferred_element_type=jnp.float32
-            ).astype(jnp.bfloat16)
-
-
-def gated_sums(place, top_count, own, other, up, down, filling):
-    widths = tuple(segment[0].shape[1] for segment in other)
-    block_count = len(own[0])
-    count = sum(block.shape[0] for block in own[0])
-    per_device, width, both_width = up.shape
-    operands = [block for segments in (own, other) for segment in segments for block in segment]
+
+def multiply_down(out, hidden, down, base):
+    for low in range(0, out.shape[1], CHUNK):
+        columns = pl.ds(pl.multiple_of(base + low, CHUNK), CHUNK)
+        out[:, low : low + CHUNK] = jnp.dot(
+            hidden[...], down[:, columns], preferred_element_type=jnp.float32
+        ).astype(jnp.bfloat16)
+
+
+def sums_kernel(top_count, place, own, other, up, down, mark, keep_ref, give_ref, acc, hidden):
+    part = other.shape[1]
+    bases = [place[0] * part, (1 - place[0]) * part]
+    acc[...] = jnp.zeros_like(acc)
+    add_up(acc, [[own]], [part], up, bases[0])
+    add_up(acc, [[other]], [part], up, bases[1])
+    make_hidden(hidden, acc, [own], part, place[1], top_count)
+    multiply_down(give_ref, hidden, down, bases[1])
+    multiply_down(keep_ref, hidden, down, bases[0])
+
+
+def own_kernel(place, first, second, up, acc):
+    cut = first.shape[1]
+    acc[...] = jnp.zeros_like(acc)
+    add_up(acc, [[first], [second]], [cut, cut], up, place[0] * 2 * cut)
+
+
+def give_kernel(top_count, place, routed, first, second, held, up, down, give_ref, hidden, acc):
+    cut = first.shape[1]
+    base = (1 - place[0]) * 2 * cut
+    acc[...] = held[...]
+    add_up(acc, [[first], [second]], [cut, cut], up, base)
+    make_hidden(hidden, acc, [routed], cut, place[1], top_count)
+    multiply_down(give_ref, hidden, down, base)
+
+
+def keep_kernel(place, hidden, down, keep_ref):
+    multiply_down(keep_ref, hidden, down, place[0] * keep_ref.shape[1])
+
+
+def call(kernel, operands, out_shape, scratch_shapes=(), flops=0, unplaced=0):
     in_vmem = pl.BlockSpec(memory_space=pltpu.VMEM)
-    operands = [pltpu.with_memory_space_constraint(x, pltpu.VMEM) for x in operands]
-    out_shape = [pltpu.VMEM((count, width // 2), jnp.bfloat16)] * 2
-    scratch = [
-        pltpu.VMEM((per_device, count, both_width), jnp.float32),
-        pltpu.VMEM((count, down.shape[0]), jnp.bfloat16),
-    ]
-    if filling:
-        weights = [pltpu.with_memory_space_constraint(w, pltpu.HBM) for w in (up, down)]
-        weight_specs = [pl.BlockSpec(memory_space=pl.ANY)] * 2
-        out_shape += [pltpu.VMEM(up.shape, up.dtype), pltpu.VMEM(down.shape, down.dtype)]
-        scratch += [pltpu.SemaphoreType.DMA((per_device * (width // CHUNK + 1),))]
-        moved = up.nbytes + down.nbytes
-    else:
-        weights = [pltpu.with_memory_space_constraint(w, pltpu.VMEM) for w in (up, down)]
-        weight_specs = [in_vmem] * 2
-        moved = 0
+    place, *arrays = operands
+    split = len(arrays) - unplaced
     return pl.pallas_call(
-        lambda *refs: sums_kernel((widths, block_count, top_count), filling, *refs),
+        kernel,
         in_specs=[pl.BlockSpec(memory_space=pltpu.SMEM)]
-        + [in_vmem] * len(operands)
-        + weight_specs,
+        + [in_vmem] * split
+        + [pl.BlockSpec(memory_space=pl.ANY)] * unplaced,
         out_specs=[in_vmem] * len(out_shape),
         out_shape=out_shape,
-        scratch_shapes=scratch,
+        scratch_shapes=list(scratch_shapes),
         compiler_params=pltpu.CompilerParams(vmem_limit_bytes=VMEM_LIMIT),
-        cost_estimate=pl.CostEstimate(
-            flops=2 * count * (up.size + down.size),
-            bytes_accessed=moved,
-            transcendentals=count * down.shape[0],
-        ),
-    )(place, *operands, *weights)
+        cost_estimate=pl.CostEstimate(flops=flops, bytes_accessed=0, transcendentals=0),
+    )(
+        place,
+        *(pltpu.with_memory_space_constraint(x, pltpu.VMEM) for x in arrays[:split]),
+        *arrays[split:],
+    )
+
+
+def gated_sums(place, top_count, own, other, up, down, mark):
+    count, part = other.shape
+    out = pltpu.VMEM((count, part), jnp.bfloat16)
+    return call(
+        lambda *refs: sums_kernel(top_count, *refs),
+        [place, own, other, up, down, mark],
+        [out, out],
+        [
+            pltpu.VMEM((up.shape[0], count, up.shape[2]), jnp.float32),
+            pltpu.VMEM((count, down.shape[0]), jnp.bfloat16),
+        ],
+        flops=2 * count * (up.size + down.size),
+        unplaced=1,
+    )
+
+
+def gated_sums_in_halves(place, top_count, own, other, up, down):
+    count, cut = own[0].shape
+    acc_shape = (up.shape[0], count, up.shape[2])
+    (held,) = call(
+        own_kernel,
+        [place, own[0], own[1][:, :cut], up],
+        [pltpu.VMEM(acc_shape, jnp.float32)],
+        flops=count * up.size,
+    )
+    give, hidden = call(
+        lambda *refs: give_kernel(top_count, *refs),
+        [place, own[1], *other, held, up, down],
+        [
+            pltpu.VMEM((count, 2 * cut), jnp.bfloat16),
+            pltpu.VMEM((count, down.shape[0]), jnp.bfloat16),
+        ],
+        [pltpu.VMEM(acc_shape, jnp.float32)],
+        flops=count * (up.size + down.size),
+    )
+    (keep,) = call(
+        keep_kernel,
+        [place, hidden, down],
+        [pltpu.VMEM((count, 2 * cut), jnp.bfloat16)],
+        flops=count * down.size,
+    )
+    return keep, give
 
 
 def first_kernel(place, *refs):
@@ -310,28 +362,27 @@
         jnp.concatenate([jnp.where(first, keep, taken), jnp.where(first, taken, keep)], 0)
     )
 
-    def sums_of(own, weights, filling=False):
-        last = len(own) - 1
-        bare = [
-            [block[:, : block.shape[1] - (LANES if i == last else 0)] for block in segment]
-            for i, segment in enumerate(own)
-        ]
-        other = [[swap(block, "core", 1) for block in segment] for segment in bare]
-        keep, give, *filled = gated_sums(
-            place, top_count, own, other, *weights, filling
-        )
-        return keep, give, filled or weights
+    def sums_of(own):
+        other = swap(own[:, :part], "core", 1)
+        return gated_sums(place, top_count, own, other, *weights, mark)
 
     def chip_sums(keep, give):
         return (wide(keep) + wide(swap(give, "core", 1))).astype(jnp.bfloat16)
 
     chip_blocks = [chip_rows] + [swap(chip_rows, "chip", j) for j in range(1, chips)]
     direct = [swap(chip_rows, "dp", k) for k in range(1, groups)]
+    *weights, mark = loaded(
+        in_weight, out_weight.reshape(per_device * half_width, width), chip_blocks[1]
+    )
+    chip_blocks[1:], mark = lax.optimization_barrier((chip_blocks[1:], mark))
     far = row_major(jnp.concatenate(chip_blocks[1:], 0))
     held = row_major(jnp.concatenate([*chip_blocks, *direct], 0))
     near = spread_near(far)
-    weights = (in_weight, out_weight.reshape(per_device * half_width, width))
-    keep, give, weights = sums_of([[held]], weights, filling=True)
+    if held.shape[0] > MOST_ROWS:
+        pieces = [sums_of(block) for block in (jnp.concatenate(chip_blocks, 0), *direct)]
+        keep, give = (jnp.concatenate(piece, 0) for piece in zip(*pieces))
+    else:
+        keep, give = sums_of(held)
     near = behind(near, give)
     rest = spread_rest(near)
     first_sum = chip_sums(keep, give)
@@ -342,12 +393,13 @@
     ]
     if rest:
         near = row_major(jnp.concatenate(near, 0))
-        keep, give, _ = sums_of([[near]], weights)
+        keep, give = sums_of(near)
         pair = chip_sums(keep, give)
         sums = [pair[: far.shape[0]], pair[far.shape[0] :]]
         rest = behind(rest, give)
-        keep, give, _ = sums_of([[half] for half in rest], weights)
         cut = rest[0].shape[1]
+        other = [swap(half[:, :cut], "core", 1) for half in rest]
+        keep, give = gated_sums_in_halves(place, top_count, rest, other, *weights)
         diagonal = added(keep, swap(give, "core", 1), cut)
         diagonal = [
             jnp.concatenate([block, half], 0)
@@ -359,7 +411,7 @@
     else:
         sums = [own_sum]
         for block, o in zip(near, direct_sums):
-            keep, give, _ = sums_of([[block]], weights)
+            keep, give = sums_of(block)
             sums += [jnp.concatenate([o, chip_sums(keep, give)], 0)]
         metas = [held, *near]
     metas = [block[:, block.shape[1] - LANES :] for block in metas]

time: 74.9 us -> 75 us (level)
  waiting for transfers between devices: 26.5 us -> 20 us
  Pallas kernels: 19.1 us -> 22.7 us
  starting transfers between devices: 25.6 us -> 28.6 us
    ppermute x28, waiting for transfers between devices: 26.5 us -> 20 us  [swap(): return row_major(lax.ppermute(row_major(value), axis, pairs))]
    pallas_call x3 -> x6, Pallas kernels: 16 us -> 19.6 us  [the longest x5 13.2 us: call(): pl.pallas_call(kernel, in_specs=[pl.BlockSpec(memory_space=pltpu.SMEM)] +...]
    ppermute x28, starting transfers between devices: 25.6 us -> 28.6 us  [swap(): return row_major(lax.ppermute(row_major(value), axis, pairs))]
  transfers between devices with their start and end apart: 28 -> 28, of which waited for: 16 -> 12; matrix products, arithmetic and copies ran while one was open for 2% -> 2% of each run, Pallas kernels for 23% -> 28%
where the time goes in v13:
time: 75 us; the launch traced here: 74.8 us
  starting transfers between devices  28.6 us (38%)
  Pallas kernels  22.7 us (30%)
  waiting for transfers between devices  20 us (27%)
  other arithmetic  1.66 us (2%)
  between operations  1.01 us (1%)
  local copies, waits for them, and re-layouts  0.98 us (1%)
    ppermute x28, starting transfers between devices, swap(): return row_major(lax.ppermute(row_major(value), axis, pairs))  28.6 us
    ppermute x28, waiting for transfers between devices, swap(): return row_major(lax.ppermute(row_major(value), axis, pairs))  20 us
    pallas_call x5, Pallas kernels, call(): pl.pallas_call(kernel, in_specs=[pl.BlockSpec(memory_space=pltpu.SMEM)] +...  13.2 us
    pallas_call x1, Pallas kernels, loaded(): pl.pallas_call(load_weights_kernel, in_specs=[pl.BlockSpec(memory_space=p...  6.38 us
    pallas_call x1, Pallas kernels, first_halves(): pl.pallas_call(first_kernel, in_specs=[pl.BlockSpec(memory_space=pltpu.SM...  1.56 us
  transfers between devices with their start and end apart: 28, of which 12 were waited for; matrix products, arithmetic and copies ran while one was open for 2% of the time, Pallas kernels for 28%

profile of v13, /device:TPU:0, one launch (start us, length us, event | category | flops | bytes accessed | tf_op | source)
XLA Modules:
  0.0 74.8 jit_solution(2799993818253493094)
XLA Ops:
  0.7 1.6 %shard_map.77 = (bf16[12,2176]{1,0:T(8,128)(2,1)S(1)}, bf16[12,2176]{1,0:T(8,128)(2,1)S(1)}) custom-call(s32[2]{0:T(128)S(1)} %pad_add_fusion.place.refs_0_, bf16[12,4096]{1,0:T(8,128)(2,1)} %refs_0_.2, s32[8,12]{1,0:T(8,128)} %bitcast.8, f32[8,12]{1,0:T(8,128)} %bitcast.9), custom_call_target="tpu_custom_call" | custom-call | tf_op jit(solution)/shard_map/pallas_call | solution.py:261
  2.3 0.5 collective-permute-start
  2.8 0.9 %collective-permute-done = bf16[12,2176]{1,0:T(8,128)(2,1)S(1)} collective-permute-done((bf16[12,2176]{1,0:T(8,128)(2,1)S(1)}, bf16[12,2176]{1,0:T(8,128)(2,1)S(1)}, u32[]{:S(2)}, u32[]{:S(2)}) %collective-permute-start) | collective-permute-done | bytes 52256 | tf_op jit(solution)/shard_map/ppermute | solution.py:24
  3.8 3.0 %collective-permute-start.1 = (bf16[24,2176]{1,0:T(8,128)(2,1)S(1)}, bf16[24,2176]{1,0:T(8,128)(2,1)S(1)}, u32[]{:S(2)}, u32[]{:S(2)}) collective-permute-start(bf16[24,2176]{1,0:T(8,128)(2,1)S(1)} %get-tuple-element.51), channel_id=1, source_target_pairs={{0,2},{2,0},{4,6},{6,4},{1,3},{3,1},{5,7},{7,5},{8,10},{10,8},{12,... | collective-permute-start | bytes 313352 | tf_op jit(solution)/shard_map/ppermute | solution.py:24
  6.8 2.5 %collective-permute-start.3 = (bf16[24,2176]{1,0:T(8,128)(2,1)S(1)}, bf16[24,2176]{1,0:T(8,128)(2,1)S(1)}, u32[]{:S(2)}, u32[]{:S(2)}) collective-permute-start(bf16[24,2176]{1,0:T(8,128)(2,1)S(1)} %get-tuple-element.51), channel_id=1, source_target_pairs={{0,6},{2,4},{4,2},{6,0},{1,7},{3,5},{5,3},{7,1},{8,14},{10,12},{12... | collective-permute-start | bytes 313352 | tf_op jit(solution)/shard_map/ppermute | solution.py:24
  9.2 0.1 collective-permute-start.2
  9.3 2.4 %collective-permute-start.6 = (bf16[24,2176]{1,0:T(8,128)(2,1)S(1)}, bf16[24,2176]{1,0:T(8,128)(2,1)S(1)}, u32[]{:S(2)}, u32[]{:S(2)}) collective-permute-start(bf16[24,2176]{1,0:T(8,128)(2,1)S(1)} %get-tuple-element.51), channel_id=1, source_target_pairs={{0,24},{8,16},{16,8},{24,0},{1,25},{9,17},{17,9},{25,1},{2,26},{10... | collective-permute-start | bytes 313352 | tf_op jit(solution)/shard_map/ppermute | solution.py:24
  11.8 0.5 collective-permute-start.5
  12.3 0.5 collective-permute-start.4
  12.8 6.4 %shard_map.78 = (bf16[2,4096,768]{2,1,0:T(8,128)(2,1)S(1)}, bf16[768,4096]{1,0:T(8,128)(2,1)S(1)}, f32[8,128]{1,0:T(8,128)S(1)}) custom-call(bf16[2,4096,768]{2,1,0:T(8,128)(2,1)} %up_ref.1, bf16[768,4096]{1,0:T(8,128)(2,1)} %bitcast.7, bf16[24,2176]{1,0:T(8,128)(2,1)S(1)} %collective-permute-done.1._), custom_call_target="tpu_custom_call" | custom-call | bytes 18874368 | tf_op jit(solution)/shard_map/pallas_call | solution.py:84
  19.6 1.6 %collective-permute-start.9 = (bf16[72,2176]{1,0:T(8,128)(2,1)S(1)}, bf16[72,2176]{1,0:T(8,128)(2,1)S(1)}, u32[]{:S(2)}, u32[]{:S(2)}) collective-permute-start(bf16[72,2176]{1,0:T(8,128)(2,1)S(1)} %get-tuple-element.69), channel_id=1, source_target_pairs={{0,8},{8,0},{16,24},{24,16},{1,9},{9,1},{17,25},{25,17},{2,10},{10... | collective-permute-start | bytes 940040 | tf_op jit(solution)/shard_map/ppermute | solution.py:24
  21.1 1.5 %collective-permute-start.10 = (bf16[72,2176]{1,0:T(8,128)(2,1)S(1)}, bf16[72,2176]{1,0:T(8,128)(2,1)S(1)}, u32[]{:S(2)}, u32[]{:S(2)}) collective-permute-start(bf16[72,2176]{1,0:T(8,128)(2,1)S(1)} %get-tuple-element.69), channel_id=1, source_target_pairs={{0,16},{8,24},{16,0},{24,8},{1,17},{9,25},{17,1},{25,9},{2,18},{10... | collective-permute-start | bytes 940040 | tf_op jit(solution)/shard_map/ppermute | solution.py:24
  22.7 4.2 %shard_map.79 = (bf16[168,2048]{1,0:T(8,128)(2,1)S(1)}, bf16[168,2048]{1,0:T(8,128)(2,1)S(1)}) custom-call(s32[2]{0:T(128)S(1)} %pad_add_fusion.place.refs_0_, bf16[168,2176]{1,0:T(8,128)(2,1)S(1)} %constant_dynamic-update-slice_fusion.refs_1_, bf16[168,2048]{1,0:T(8,128)(2,1)S(1)} %collective-permute-done.7.refs_2_, ...), custom_call_target="tpu_custom_call" | custom-call | flops 3170893824 | tf_op jit(solution)/shard_map/pallas_call | solution.py:170
  26.9 2.5 %collective-permute-done.9 = bf16[72,2176]{1,0:T(8,128)(2,1)S(1)} collective-permute-done((bf16[72,2176]{1,0:T(8,128)(2,1)S(1)}, bf16[72,2176]{1,0:T(8,128)(2,1)S(1)}, u32[]{:S(2)}, u32[]{:S(2)}) %collective-permute-start.9) | collective-permute-done | bytes 313376 | tf_op jit(solution)/shard_map/ppermute | solution.py:24
  29.4 1.2 %collective-permute-done.10 = bf16[72,2176]{1,0:T(8,128)(2,1)S(1)} collective-permute-done((bf16[72,2176]{1,0:T(8,128)(2,1)S(1)}, bf16[72,2176]{1,0:T(8,128)(2,1)S(1)}, u32[]{:S(2)}, u32[]{:S(2)}) %collective-permute-start.10) | collective-permute-done | bytes 313376 | tf_op jit(solution)/shard_map/ppermute | solution.py:24
  30.8 0.5 collective-permute-start.8
  31.3 1.6 %collective-permute-start.13 = (bf16[72,1024]{1,0:T(8,128)(2,1)S(1)}, bf16[72,1024]{1,0:T(8,128)(2,1)S(1)}, u32[]{:S(2)}, u32[]{:S(2)}) collective-permute-start(bf16[72,1024]{1,0:T(8,128)(2,1)S(1)} %slice.107), channel_id=1, source_target_pairs={{0,16},{8,24},{16,0},{24,8},{1,17},{9,25},{17,1},{25,9},{2,18},{10... | collective-permute-start | bytes 442376 | tf_op jit(solution)/shard_map/ppermute | solution.py:24
  32.9 0.5 collective-permute-start.14
  33.5 3.6 %shard_map.80 = (bf16[144,2048]{1,0:T(8,128)(2,1)S(1)}, bf16[144,2048]{1,0:T(8,128)(2,1)S(1)}) custom-call(s32[2]{0:T(128)S(1)} %pad_add_fusion.place.refs_0_, bf16[144,2176]{1,0:T(8,128)(2,1)S(1)} %constant_dynamic-update-slice_fusion.10.refs_1_, bf16[144,2048]{1,0:T(8,128)(2,1)S(1)} %collective-permute-done.11.refs_2_, ...), custom_call_target="tpu_custom_call" | custom-call | flops 2717908992 | tf_op jit(solution)/shard_map/pallas_call | solution.py:170
  37.2 1.6 %collective-permute-done.14.refs_1_ = bf16[72,1152]{1,0:T(8,128)(2,1)S(1)} collective-permute-done((bf16[72,1152]{1,0:T(8,128)(2,1)S(1)}, bf16[72,1152]{1,0:T(8,128)(2,1)S(1)}, u32[]{:S(2)}, u32[]{:S(2)}) %collective-permute-start.14) | collective-permute-done | bytes 165920 | tf_op jit(solution)/shard_map/ppermute | solution.py:24
  39.0 0.5 collective-permute-start.15
  39.5 1.7 %shard_map.81.refs_4_ = f32[2,72,768]{2,1,0:T(8,128)S(1)} custom-call(s32[2]{0:T(128)S(1)} %pad_add_fusion.place.refs_0_, bf16[72,1024]{1,0:T(8,128)(2,1)S(1)} %collective-permute-done.13.first, bf16[72,1024]{1,0:T(8,128)(2,1)S(1)} %slice.109.second, bf16[2,4096,768]{2,1,0:T(8,128)(2,1)S(1)} %get-tuple-element.32.refs_3_.up.refs_5_), custom_call_target="tpu_custom_call" | custom-call | flops 452984832 | tf_op jit(solution)/shard_map/pallas_call | solution.py:170
  41.2 0.2 add_convert_fusion
  41.5 2.4 %shard_map.82 = (bf16[72,2048]{1,0:T(8,128)(2,1)S(1)}, bf16[72,768]{1,0:T(8,128)(2,1)S(1)}) custom-call(s32[2]{0:T(128)S(1)} %pad_add_fusion.place.refs_0_, bf16[72,1152]{1,0:T(8,128)(2,1)S(1)} %collective-permute-done.14.refs_1_, bf16[72,1024]{1,0:T(8,128)(2,1)S(1)} %collective-permute-done.15.refs_2_, ...), custom_call_target="tpu_custom_call" | custom-call | flops 679477248 | tf_op jit(solution)/shard_map/pallas_call | solution.py:170
  43.9 0.1 collective-permute-start.17
  44.0 1.2 %shard_map.83.kept_ref = bf16[72,2048]{1,0:T(8,128)(2,1)S(1)} custom-call(s32[2]{0:T(128)S(1)} %pad_add_fusion.place.refs_0_, bf16[72,768]{1,0:T(8,128)(2,1)S(1)} %get-tuple-element.43.hidden, bf16[768,4096]{1,0:T(8,128)(2,1)S(1)} %get-tuple-element.33.refs_4_.refs_6_.down), custom_call_target="tpu_custom_call" | custom-call | flops 226492416 | tf_op jit(solution)/shard_map/pallas_call | solution.py:170
  45.3 0.2 collective-permute-done.17.taken_ref
  45.6 0.6 collective-permute-start.19
  46.2 0.6 collective-permute-start.18
  46.8 0.1 add_convert_fusion.1
  47.0 5.7 %collective-permute-done.19 = bf16[96,1024]{1,0:T(8,128)(2,1)S(1)} collective-permute-done((bf16[96,1024]{1,0:T(8,128)(2,1)S(1)}, bf16[96,1024]{1,0:T(8,128)(2,1)S(1)}, u32[]{:S(2)}, u32[]{:S(2)}) %collective-permute-start.19) | collective-permute-done | bytes 196640 | tf_op jit(solution)/shard_map/ppermute | solution.py:24
  52.7 0.3 collective-permute-done.18
  53.0 0.1 add_convert_fusion.4
  53.3 0.6 collective-permute-start.21
  53.8 1.5 %collective-permute-start.20 = (bf16[48,2048]{1,0:T(8,128)(2,1)S(1)}, bf16[48,2048]{1,0:T(8,128)(2,1)S(1)}, u32[]{:S(2)}, u32[]{:S(2)}) collective-permute-start(bf16[48,2048]{1,0:T(8,128)(2,1)S(1)} %get-tuple-element.61), channel_id=1, source_target_pairs={{0,8},{8,0},{16,24},{24,16},{1,9},{9,1},{17,25},{25,17},{2,10},{10... | collective-permute-start | bytes 589832 | tf_op jit(solution)/shard_map/ppermute | solution.py:24
  55.3 3.9 %collective-permute-done.21 = bf16[48,2048]{1,0:T(8,128)(2,1)S(1)} collective-permute-done((bf16[48,2048]{1,0:T(8,128)(2,1)S(1)}, bf16[48,2048]{1,0:T(8,128)(2,1)S(1)}, u32[]{:S(2)}, u32[]{:S(2)}) %collective-permute-start.21) | collective-permute-done | bytes 196640 | tf_op jit(solution)/shard_map/ppermute | solution.py:24
  59.2 0.3 collective-permute-done.20
  59.6 1.6 %collective-permute-start.22 = (bf16[48,2048]{1,0:T(8,128)(2,1)S(1)}, bf16[48,2048]{1,0:T(8,128)(2,1)S(1)}, u32[]{:S(2)}, u32[]{:S(2)}) collective-permute-start(bf16[48,2048]{1,0:T(8,128)(2,1)S(1)} %get-tuple-element.48), channel_id=1, source_target_pairs={{0,8},{8,0},{16,24},{24,16},{1,9},{9,1},{17,25},{25,17},{2,10},{10... | collective-permute-start | bytes 589832 | tf_op jit(solution)/shard_map/ppermute | solution.py:24
  61.1 1.5 %collective-permute-start.23 = (bf16[48,2048]{1,0:T(8,128)(2,1)S(1)}, bf16[48,2048]{1,0:T(8,128)(2,1)S(1)}, u32[]{:S(2)}, u32[]{:S(2)}) collective-permute-start(bf16[48,2048]{1,0:T(8,128)(2,1)S(1)} %get-tuple-element.49), channel_id=1, source_target_pairs={{0,16},{8,24},{16,0},{24,8},{1,17},{9,25},{17,1},{25,9},{2,18},{10... | collective-permute-start | bytes 589832 | tf_op jit(solution)/shard_map/ppermute | solution.py:24
  62.7 2.9 %collective-permute-start.25 = (bf16[24,2048]{1,0:T(8,128)(2,1)S(1)}, bf16[24,2048]{1,0:T(8,128)(2,1)S(1)}, u32[]{:S(2)}, u32[]{:S(2)}) collective-permute-start(bf16[24,2048]{1,0:T(8,128)(2,1)S(1)} %get-tuple-element.62), channel_id=1, source_target_pairs={{0,4},{2,6},{4,0},{6,2},{1,5},{3,7},{5,1},{7,3},{8,12},{10,14},{12... | collective-permute-start | bytes 294920 | tf_op jit(solution)/shard_map/ppermute | solution.py:24
  65.6 1.4 %collective-permute-start.26 = (bf16[24,2048]{1,0:T(8,128)(2,1)S(1)}, bf16[24,2048]{1,0:T(8,128)(2,1)S(1)}, u32[]{:S(2)}, u32[]{:S(2)}) collective-permute-start(bf16[24,2048]{1,0:T(8,128)(2,1)S(1)} %get-tuple-element.63), channel_id=1, source_target_pairs={{0,6},{2,4},{4,2},{6,0},{1,7},{3,5},{5,3},{7,1},{8,14},{10,12},{12... | collective-permute-start | bytes 294920 | tf_op jit(solution)/shard_map/ppermute | solution.py:24
  67.0 1.8 %collective-permute-start.24 = (bf16[24,2048]{1,0:T(8,128)(2,1)S(1)}, bf16[24,2048]{1,0:T(8,128)(2,1)S(1)}, u32[]{:S(2)}, u32[]{:S(2)}) collective-permute-start(bf16[24,2048]{1,0:T(8,128)(2,1)S(1)} %slice.150), channel_id=1, source_target_pairs={{0,2},{2,0},{4,6},{6,4},{1,3},{3,1},{5,7},{7,5},{8,10},{10,8},{12,... | collective-permute-start | bytes 294920 | tf_op jit(solution)/shard_map/ppermute | solution.py:24
  68.8 1.5 %shard_map.85 = f32[1,128]{1,0:T(1,128)S(1)} custom-call(s32[8]{0:T(128)S(1)} %copy-done, bf16[168,128]{1,0:T(8,128)(2,1)S(1)} %slice.155.refs_1_, bf16[144,128]{1,0:T(8,128)(2,1)S(1)} %slice.156.refs_2_, bf16[72,128]{1,0:T(8,128)(2,1)S(1)} %slice.129.refs_3_), custom_call_target="tpu_custom_call" | custom-call | tf_op jit(solution)/shard_map/pallas_call | solution.py:335
  70.3 1.8 %collective-permute-done.26 = bf16[24,2048]{1,0:T(8,128)(2,1)S(1)} collective-permute-done((bf16[24,2048]{1,0:T(8,128)(2,1)S(1)}, bf16[24,2048]{1,0:T(8,128)(2,1)S(1)}, u32[]{:S(2)}, u32[]{:S(2)}) %collective-permute-start.26) | collective-permute-done | bytes 98336 | tf_op jit(solution)/shard_map/ppermute | solution.py:24
  72.1 0.6 collective-permute-done.24
  72.9 0.5 slice_bitcast_fusion
  73.4 0.7 collective-permute-done.27
  74.2 0.7 pad_maximum_fusion.4
  (60 shorter events, 1.5 us)
Async XLA Ops:
  2.3 1.4 %collective-permute-start = (bf16[12,2176]{1,0:T(8,128)(2,1)S(1)}, bf16[12,2176]{1,0:T(8,128)(2,1)S(1)}, u32[]{:S(2)}, u32[]{:S(2)}) collective-permute-start(bf16[12,2176]{1,0:T(8,128)(2,1)S(1)} %get-tuple-element.27), channel_id=1, source_target_pairs={{0,1},{1,0},{2,3},{3,2},{4,5},{5,4},{6,7},{7,6},{8,9},{9,8},{10,11... | collective-permute-start | bytes 156680 | tf_op jit(solution)/shard_map/ppermute | solution.py:24
  3.8 8.5 %collective-permute-start.1 = (bf16[24,2176]{1,0:T(8,128)(2,1)S(1)}, bf16[24,2176]{1,0:T(8,128)(2,1)S(1)}, u32[]{:S(2)}, u32[]{:S(2)}) collective-permute-start(bf16[24,2176]{1,0:T(8,128)(2,1)S(1)} %get-tuple-element.51), channel_id=1, source_target_pairs={{0,2},{2,0},{4,6},{6,4},{1,3},{3,1},{5,7},{7,5},{8,10},{10,8},{12,... | collective-permute-start | bytes 313352 | tf_op jit(solution)/shard_map/ppermute | solution.py:24
  6.8 12.5 %collective-permute-start.3 = (bf16[24,2176]{1,0:T(8,128)(2,1)S(1)}, bf16[24,2176]{1,0:T(8,128)(2,1)S(1)}, u32[]{:S(2)}, u32[]{:S(2)}) collective-permute-start(bf16[24,2176]{1,0:T(8,128)(2,1)S(1)} %get-tuple-element.51), channel_id=1, source_target_pairs={{0,6},{2,4},{4,2},{6,0},{1,7},{3,5},{5,3},{7,1},{8,14},{10,12},{12... | collective-permute-start | bytes 313352 | tf_op jit(solution)/shard_map/ppermute | solution.py:24
  9.2 10.0 %collective-permute-start.2 = (bf16[24,2176]{1,0:T(8,128)(2,1)S(1)}, bf16[24,2176]{1,0:T(8,128)(2,1)S(1)}, u32[]{:S(2)}, u32[]{:S(2)}) collective-permute-start(bf16[24,2176]{1,0:T(8,128)(2,1)S(1)} %get-tuple-element.51), channel_id=1, source_target_pairs={{0,4},{2,6},{4,0},{6,2},{1,5},{3,7},{5,1},{7,3},{8,12},{10,14},{12... | collective-permute-start | bytes 313352 | tf_op jit(solution)/shard_map/ppermute | solution.py:24
  9.3 10.0 %collective-permute-start.6 = (bf16[24,2176]{1,0:T(8,128)(2,1)S(1)}, bf16[24,2176]{1,0:T(8,128)(2,1)S(1)}, u32[]{:S(2)}, u32[]{:S(2)}) collective-permute-start(bf16[24,2176]{1,0:T(8,128)(2,1)S(1)} %get-tuple-element.51), channel_id=1, source_target_pairs={{0,24},{8,16},{16,8},{24,0},{1,25},{9,17},{17,9},{25,1},{2,26},{10... | collective-permute-start | bytes 313352 | tf_op jit(solution)/shard_map/ppermute | solution.py:24
  11.8 7.6 %collective-permute-start.5 = (bf16[24,2176]{1,0:T(8,128)(2,1)S(1)}, bf16[24,2176]{1,0:T(8,128)(2,1)S(1)}, u32[]{:S(2)}, u32[]{:S(2)}) collective-permute-start(bf16[24,2176]{1,0:T(8,128)(2,1)S(1)} %get-tuple-element.51), channel_id=1, source_target_pairs={{0,16},{8,24},{16,0},{24,8},{1,17},{9,25},{17,1},{25,9},{2,18},{10... | collective-permute-start | bytes 313352 | tf_op jit(solution)/shard_map/ppermute | solution.py:24
  12.3 7.0 %collective-permute-start.4 = (bf16[24,2176]{1,0:T(8,128)(2,1)S(1)}, bf16[24,2176]{1,0:T(8,128)(2,1)S(1)}, u32[]{:S(2)}, u32[]{:S(2)}) collective-permute-start(bf16[24,2176]{1,0:T(8,128)(2,1)S(1)} %get-tuple-element.51), channel_id=1, source_target_pairs={{0,8},{8,0},{16,24},{24,16},{1,9},{9,1},{17,25},{25,17},{2,10},{10... | collective-permute-start | bytes 313352 | tf_op jit(solution)/shard_map/ppermute | solution.py:24
  19.5 3.2 %collective-permute-start.7 = (bf16[168,2048]{1,0:T(8,128)(2,1)S(1)}, bf16[168,2048]{1,0:T(8,128)(2,1)S(1)}, u32[]{:S(2)}, u32[]{:S(2)}) collective-permute-start(bf16[168,2048]{1,0:T(8,128)(2,1)S(1)} %slice.131), channel_id=1, source_target_pairs={{0,1},{1,0},{2,3},{3,2},{4,5},{5,4},{6,7},{7,6},{8,9},{9,8},{10,11... | collective-permute-start | bytes 2064392 | tf_op jit(solution)/shard_map/ppermute | solution.py:24
  19.6 9.8 %collective-permute-start.9 = (bf16[72,2176]{1,0:T(8,128)(2,1)S(1)}, bf16[72,2176]{1,0:T(8,128)(2,1)S(1)}, u32[]{:S(2)}, u32[]{:S(2)}) collective-permute-start(bf16[72,2176]{1,0:T(8,128)(2,1)S(1)} %get-tuple-element.69), channel_id=1, source_target_pairs={{0,8},{8,0},{16,24},{24,16},{1,9},{9,1},{17,25},{25,17},{2,10},{10... | collective-permute-start | bytes 940040 | tf_op jit(solution)/shard_map/ppermute | solution.py:24
  21.1 9.5 %collective-permute-start.10 = (bf16[72,2176]{1,0:T(8,128)(2,1)S(1)}, bf16[72,2176]{1,0:T(8,128)(2,1)S(1)}, u32[]{:S(2)}, u32[]{:S(2)}) collective-permute-start(bf16[72,2176]{1,0:T(8,128)(2,1)S(1)} %get-tuple-element.69), channel_id=1, source_target_pairs={{0,16},{8,24},{16,0},{24,8},{1,17},{9,25},{17,1},{25,9},{2,18},{10... | collective-permute-start | bytes 940040 | tf_op jit(solution)/shard_map/ppermute | solution.py:24
  30.7 2.7 %collective-permute-start.11 = (bf16[144,2048]{1,0:T(8,128)(2,1)S(1)}, bf16[144,2048]{1,0:T(8,128)(2,1)S(1)}, u32[]{:S(2)}, u32[]{:S(2)}) collective-permute-start(bf16[144,2048]{1,0:T(8,128)(2,1)S(1)} %slice.134), channel_id=1, source_target_pairs={{0,1},{1,0},{2,3},{3,2},{4,5},{5,4},{6,7},{7,6},{8,9},{9,8},{10,11... | collective-permute-start | bytes 1769480 | tf_op jit(solution)/shard_map/ppermute | solution.py:24
  30.8 10.4 %collective-permute-start.8 = (bf16[168,2048]{1,0:T(8,128)(2,1)S(1)}, bf16[168,2048]{1,0:T(8,128)(2,1)S(1)}, u32[]{:S(2)}, u32[]{:S(2)}) collective-permute-start(bf16[168,2048]{1,0:T(8,128)(2,1)S(1)} %get-tuple-element.36), channel_id=1, source_target_pairs={{0,1},{1,0},{2,3},{3,2},{4,5},{5,4},{6,7},{7,6},{8,9},{9,8},{10,11... | collective-permute-start | bytes 2064392 | tf_op jit(solution)/shard_map/ppermute | solution.py:24
  31.3 5.9 %collective-permute-start.13 = (bf16[72,1024]{1,0:T(8,128)(2,1)S(1)}, bf16[72,1024]{1,0:T(8,128)(2,1)S(1)}, u32[]{:S(2)}, u32[]{:S(2)}) collective-permute-start(bf16[72,1024]{1,0:T(8,128)(2,1)S(1)} %slice.107), channel_id=1, source_target_pairs={{0,16},{8,24},{16,0},{24,8},{1,17},{9,25},{17,1},{25,9},{2,18},{10... | collective-permute-start | bytes 442376 | tf_op jit(solution)/shard_map/ppermute | solution.py:24
  32.9 5.9 %collective-permute-start.14 = (bf16[72,1152]{1,0:T(8,128)(2,1)S(1)}, bf16[72,1152]{1,0:T(8,128)(2,1)S(1)}, u32[]{:S(2)}, u32[]{:S(2)}) collective-permute-start(bf16[72,1152]{1,0:T(8,128)(2,1)S(1)} %slice.108), channel_id=1, source_target_pairs={{0,8},{8,0},{16,24},{24,16},{1,9},{9,1},{17,25},{25,17},{2,10},{10... | collective-permute-start | bytes 497672 | tf_op jit(solution)/shard_map/ppermute | solution.py:24
  37.1 9.7 %collective-permute-start.12 = (bf16[144,2048]{1,0:T(8,128)(2,1)S(1)}, bf16[144,2048]{1,0:T(8,128)(2,1)S(1)}, u32[]{:S(2)}, u32[]{:S(2)}) collective-permute-start(bf16[144,2048]{1,0:T(8,128)(2,1)S(1)} %get-tuple-element.40), channel_id=1, source_target_pairs={{0,1},{1,0},{2,3},{3,2},{4,5},{5,4},{6,7},{7,6},{8,9},{9,8},{10,11... | collective-permute-start | bytes 1769480 | tf_op jit(solution)/shard_map/ppermute | solution.py:24
  38.9 2.6 %collective-permute-start.16 = (bf16[72,1024]{1,0:T(8,128)(2,1)S(1)}, bf16[72,1024]{1,0:T(8,128)(2,1)S(1)}, u32[]{:S(2)}, u32[]{:S(2)}) collective-permute-start(bf16[72,1024]{1,0:T(8,128)(2,1)S(1)} %slice.109.second), channel_id=1, source_target_pairs={{0,1},{1,0},{2,3},{3,2},{4,5},{5,4},{6,7},{7,6},{8,9},{9,8},{10,11... | collective-permute-start | bytes 442376 | tf_op jit(solution)/shard_map/ppermute | solution.py:24
  39.0 2.5 %collective-permute-start.15 = (bf16[72,1024]{1,0:T(8,128)(2,1)S(1)}, bf16[72,1024]{1,0:T(8,128)(2,1)S(1)}, u32[]{:S(2)}, u32[]{:S(2)}) collective-permute-start(bf16[72,1024]{1,0:T(8,128)(2,1)S(1)} %collective-permute-done.13.first), channel_id=1, source_target_pairs={{0,1},{1,0},{2,3},{3,2},{4,5},{5,4},{6,7},{7,6},{8,9},{9,8},{10,11... | collective-permute-start | bytes 442376 | tf_op jit(solution)/shard_map/ppermute | solution.py:24
  43.9 1.6 %collective-permute-start.17 = (bf16[72,2048]{1,0:T(8,128)(2,1)S(1)}, bf16[72,2048]{1,0:T(8,128)(2,1)S(1)}, u32[]{:S(2)}, u32[]{:S(2)}) collective-permute-start(bf16[72,2048]{1,0:T(8,128)(2,1)S(1)} %get-tuple-element.44), channel_id=1, source_target_pairs={{0,1},{1,0},{2,3},{3,2},{4,5},{5,4},{6,7},{7,6},{8,9},{9,8},{10,11... | collective-permute-start | bytes 884744 | tf_op jit(solution)/shard_map/ppermute | solution.py:24
  45.6 7.1 %collective-permute-start.19 = (bf16[96,1024]{1,0:T(8,128)(2,1)S(1)}, bf16[96,1024]{1,0:T(8,128)(2,1)S(1)}, u32[]{:S(2)}, u32[]{:S(2)}) collective-permute-start(bf16[96,1024]{1,0:T(8,128)(2,1)S(1)} %pad_maximum_fusion.3), channel_id=1, source_target_pairs={{0,8},{8,0},{16,24},{24,16},{1,9},{9,1},{17,25},{25,17},{2,10},{10... | collective-permute-start | bytes 589832 | tf_op jit(solution)/shard_map/ppermute | solution.py:24
  46.2 6.8 %collective-permute-start.18 = (bf16[96,1024]{1,0:T(8,128)(2,1)S(1)}, bf16[96,1024]{1,0:T(8,128)(2,1)S(1)}, u32[]{:S(2)}, u32[]{:S(2)}) collective-permute-start(bf16[96,1024]{1,0:T(8,128)(2,1)S(1)} %pad_maximum_fusion.2), channel_id=1, source_target_pairs={{0,16},{8,24},{16,0},{24,8},{1,17},{9,25},{17,1},{25,9},{2,18},{10... | collective-permute-start | bytes 589832 | tf_op jit(solution)/shard_map/ppermute | solution.py:24
  53.3 5.9 %collective-permute-start.21 = (bf16[48,2048]{1,0:T(8,128)(2,1)S(1)}, bf16[48,2048]{1,0:T(8,128)(2,1)S(1)}, u32[]{:S(2)}, u32[]{:S(2)}) collective-permute-start(bf16[48,2048]{1,0:T(8,128)(2,1)S(1)} %get-tuple-element.59), channel_id=1, source_target_pairs={{0,16},{8,24},{16,0},{24,8},{1,17},{9,25},{17,1},{25,9},{2,18},{10... | collective-permute-start | bytes 589832 | tf_op jit(solution)/shard_map/ppermute | solution.py:24
  53.8 15.0 %copy-start = (s32[8]{0:T(128)S(1)}, s32[8]{0:T(128)}, u32[]{:S(2)}) copy-start(s32[8]{0:T(128)} %refs_0_.3) | copy-start | bytes 100
  53.8 5.7 %collective-permute-start.20 = (bf16[48,2048]{1,0:T(8,128)(2,1)S(1)}, bf16[48,2048]{1,0:T(8,128)(2,1)S(1)}, u32[]{:S(2)}, u32[]{:S(2)}) collective-permute-start(bf16[48,2048]{1,0:T(8,128)(2,1)S(1)} %get-tuple-element.61), channel_id=1, source_target_pairs={{0,8},{8,0},{16,24},{24,16},{1,9},{9,1},{17,25},{25,17},{2,10},{10... | collective-permute-start | bytes 589832 | tf_op jit(solution)/shard_map/ppermute | solution.py:24
  59.6 7.3 %collective-permute-start.22 = (bf16[48,2048]{1,0:T(8,128)(2,1)S(1)}, bf16[48,2048]{1,0:T(8,128)(2,1)S(1)}, u32[]{:S(2)}, u32[]{:S(2)}) collective-permute-start(bf16[48,2048]{1,0:T(8,128)(2,1)S(1)} %get-tuple-element.48), channel_id=1, source_target_pairs={{0,8},{8,0},{16,24},{24,16},{1,9},{9,1},{17,25},{25,17},{2,10},{10... | collective-permute-start | bytes 589832 | tf_op jit(solution)/shard_map/ppermute | solution.py:24
  61.1 5.8 %collective-permute-start.23 = (bf16[48,2048]{1,0:T(8,128)(2,1)S(1)}, bf16[48,2048]{1,0:T(8,128)(2,1)S(1)}, u32[]{:S(2)}, u32[]{:S(2)}) collective-permute-start(bf16[48,2048]{1,0:T(8,128)(2,1)S(1)} %get-tuple-element.49), channel_id=1, source_target_pairs={{0,16},{8,24},{16,0},{24,8},{1,17},{9,25},{17,1},{25,9},{2,18},{10... | collective-permute-start | bytes 589832 | tf_op jit(solution)/shard_map/ppermute | solution.py:24
  62.7 7.6 %collective-permute-start.25 = (bf16[24,2048]{1,0:T(8,128)(2,1)S(1)}, bf16[24,2048]{1,0:T(8,128)(2,1)S(1)}, u32[]{:S(2)}, u32[]{:S(2)}) collective-permute-start(bf16[24,2048]{1,0:T(8,128)(2,1)S(1)} %get-tuple-element.62), channel_id=1, source_target_pairs={{0,4},{2,6},{4,0},{6,2},{1,5},{3,7},{5,1},{7,3},{8,12},{10,14},{12... | collective-permute-start | bytes 294920 | tf_op jit(solution)/shard_map/ppermute | solution.py:24
  65.6 6.6 %collective-permute-start.26 = (bf16[24,2048]{1,0:T(8,128)(2,1)S(1)}, bf16[24,2048]{1,0:T(8,128)(2,1)S(1)}, u32[]{:S(2)}, u32[]{:S(2)}) collective-permute-start(bf16[24,2048]{1,0:T(8,128)(2,1)S(1)} %get-tuple-element.63), channel_id=1, source_target_pairs={{0,6},{2,4},{4,2},{6,0},{1,7},{3,5},{5,3},{7,1},{8,14},{10,12},{12... | collective-permute-start | bytes 294920 | tf_op jit(solution)/shard_map/ppermute | solution.py:24
  67.0 5.7 %collective-permute-start.24 = (bf16[24,2048]{1,0:T(8,128)(2,1)S(1)}, bf16[24,2048]{1,0:T(8,128)(2,1)S(1)}, u32[]{:S(2)}, u32[]{:S(2)}) collective-permute-start(bf16[24,2048]{1,0:T(8,128)(2,1)S(1)} %slice.150), channel_id=1, source_target_pairs={{0,2},{2,0},{4,6},{6,4},{1,3},{3,1},{5,7},{7,5},{8,10},{10,8},{12,... | collective-permute-start | bytes 294920 | tf_op jit(solution)/shard_map/ppermute | solution.py:24
  72.8 1.3 %collective-permute-start.27 = (bf16[12,2048]{1,0:T(8,128)(2,1)S(1)}, bf16[12,2048]{1,0:T(8,128)(2,1)S(1)}, u32[]{:S(2)}, u32[]{:S(2)}) collective-permute-start(bf16[12,2048]{1,0:T(8,128)(2,1)S(1)} %broadcast_select_fusion.4), channel_id=1, source_target_pairs={{0,1},{1,0},{2,3},{3,2},{4,5},{5,4},{6,7},{7,6},{8,9},{9,8},{10,11... | collective-permute-start | bytes 147464 | tf_op jit(solution)/shard_map/ppermute | solution.py:24

commit v14 on v13

--- a/solution.py
+++ b/solution.py
@@ -61,41 +61,34 @@
     return [own, one, two]
 
 
-def collected(blocks):
-    total = wide(blocks[0])
-    for k, block in enumerate(blocks[1:], 1):
-        total = total + wide(swap(block, "dp", k))
-    return total.astype(jnp.bfloat16)
-
-
-def load_weights_kernel(up_ref, down_ref, _, up_out, down_out, mark_ref, sems):
-    copies = [
-        pltpu.make_async_copy(up_ref, up_out, sems.at[0]),
-        pltpu.make_async_copy(down_ref, down_out, sems.at[1]),
-    ]
-    for copy in copies:
-        copy.start()
+def received(blocks):
+    return [swap(block, "dp", k) for k, block in enumerate(blocks[1:], 1)]
+
+
+def collected(own, others):
+    return sum([wide(block) for block in others], wide(own)).astype(jnp.bfloat16)
+
+
+def load_weight_kernel(weight_ref, _, weight_out, mark_ref, sem):
+    copy = pltpu.make_async_copy(weight_ref, weight_out, sem)
+    copy.start()
     mark_ref[...] = jnp.zeros_like(mark_ref)
-    for copy in copies:
-        copy.wait()
-
-
-def loaded(up, down, after):
+    copy.wait()
+
+
+def loaded(weight, after):
     return pl.pallas_call(
-        load_weights_kernel,
-        in_specs=[pl.BlockSpec(memory_space=pl.ANY)] * 3,
-        out_specs=[pl.BlockSpec(memory_space=pltpu.VMEM)] * 3,
+        load_weight_kernel,
+        in_specs=[pl.BlockSpec(memory_space=pl.ANY)] * 2,
+        out_specs=[pl.BlockSpec(memory_space=pltpu.VMEM)] * 2,
         out_shape=[
-            pltpu.VMEM(up.shape, up.dtype),
-            pltpu.VMEM(down.shape, down.dtype),
+            pltpu.VMEM(weight.shape, weight.dtype),
             pltpu.VMEM((8, LANES), jnp.float32),
         ],
-        scratch_shapes=[pltpu.SemaphoreType.DMA((2,))],
+        scratch_shapes=[pltpu.SemaphoreType.DMA],
         compiler_params=pltpu.CompilerParams(vmem_limit_bytes=VMEM_LIMIT),
-        cost_estimate=pl.CostEstimate(
-            flops=0, bytes_accessed=up.nbytes + down.nbytes, transcendentals=0
-        ),
-    )(*(pltpu.with_memory_space_constraint(x, pltpu.HBM) for x in (up, down)), after)
+        cost_estimate=pl.CostEstimate(flops=0, bytes_accessed=weight.nbytes, transcendentals=0),
+    )(pltpu.with_memory_space_constraint(weight, pltpu.HBM), after)
 
 
 def joined(blocks):
@@ -133,13 +126,21 @@
         ).astype(jnp.bfloat16)
 
 
-def sums_kernel(top_count, place, own, other, up, down, mark, keep_ref, give_ref, acc, hidden):
+def sums_kernel(top_count, filling, place, own, other, up, *refs):
+    if filling:
+        down_ref, _, keep_ref, give_ref, down, acc, hidden, sem = refs
+        copy = pltpu.make_async_copy(down_ref, down, sem)
+        copy.start()
+    else:
+        down, keep_ref, give_ref, acc, hidden = refs
     part = other.shape[1]
     bases = [place[0] * part, (1 - place[0]) * part]
     acc[...] = jnp.zeros_like(acc)
     add_up(acc, [[own]], [part], up, bases[0])
     add_up(acc, [[other]], [part], up, bases[1])
     make_hidden(hidden, acc, [own], part, place[1], top_count)
+    if filling:
+        copy.wait()
     multiply_down(give_ref, hidden, down, bases[1])
     multiply_down(keep_ref, hidden, down, bases[0])
 
@@ -184,19 +185,27 @@
     )
 
 
-def gated_sums(place, top_count, own, other, up, down, mark):
+def gated_sums(place, top_count, own, other, up, down, mark=None):
     count, part = other.shape
+    filling = mark is not None
     out = pltpu.VMEM((count, part), jnp.bfloat16)
+    out_shape = [out, out]
+    scratch = [
+        pltpu.VMEM((up.shape[0], count, up.shape[2]), jnp.float32),
+        pltpu.VMEM((count, down.shape[0]), jnp.bfloat16),
+    ]
+    operands = [place, own, other, up, down]
+    if filling:
+        operands[-1:] = [pltpu.with_memory_space_constraint(down, pltpu.HBM), mark]
+        out_shape.append(pltpu.VMEM(down.shape, down.dtype))
+        scratch.append(pltpu.SemaphoreType.DMA)
     return call(
-        lambda *refs: sums_kernel(top_count, *refs),
-        [place, own, other, up, down, mark],
-        [out, out],
-        [
-            pltpu.VMEM((up.shape[0], count, up.shape[2]), jnp.float32),
-            pltpu.VMEM((count, down.shape[0]), jnp.bfloat16),
-        ],
+        lambda *refs: sums_kernel(top_count, filling, *refs),
+        operands,
+        out_shape,
+        scratch,
         flops=2 * count * (up.size + down.size),
-        unplaced=1,
+        unplaced=2 if filling else 0,
     )
 
 
@@ -294,7 +303,7 @@
 
 def load_kernel(layout, swap_slot, *refs):
     owners, per_device, top_count, step, scale = layout
-    *metas, load_ref = refs
+    *metas, _, load_ref = refs
     experts_all = owners * per_device
     high, low = [], []
     for meta in metas:
@@ -327,19 +336,24 @@
     load_ref[...] = jnp.sum(jnp.where(holder == owner, totals, 0.0), 0, keepdims=True) * scale
 
 
-def planned_load(metas, swap_slot, owners, per_device, top_count):
+def planned_load(metas, swap_slot, owners, per_device, top_count, after):
     count = sum(meta.shape[0] for meta in metas)
     step = 2.0 ** (31 - (count * GATE_MOST).bit_length())
     layout = (owners, per_device, top_count, step, owners / count)
     in_vmem = pl.BlockSpec(memory_space=pltpu.VMEM)
     load = pl.pallas_call(
         lambda *refs: load_kernel(layout, *refs),
-        in_specs=[pl.BlockSpec(memory_space=pltpu.SMEM)] + [in_vmem] * len(metas),
+        in_specs=[pl.BlockSpec(memory_space=pltpu.SMEM)]
+        + [in_vmem] * len(metas)
+        + [pl.BlockSpec(memory_space=pl.ANY)],
         out_specs=in_vmem,
         out_shape=jax.ShapeDtypeStruct((1, LANES), jnp.float32),
         compiler_params=pltpu.CompilerParams(vmem_limit_bytes=VMEM_LIMIT),
-    )(swap_slot, *metas)
-    return load[0, :owners]
+        cost_estimate=pl.CostEstimate(
+            flops=0, bytes_accessed=sum(meta.nbytes for meta in metas), transcendentals=0
+        ),
+    )(swap_slot, *metas, after)
+    return load
 
 
 def on_device(tokens, expert_ids, gate_probs, in_weight, out_weight, swap_slot):
@@ -362,30 +376,31 @@
         jnp.concatenate([jnp.where(first, keep, taken), jnp.where(first, taken, keep)], 0)
     )
 
-    def sums_of(own):
+    def sums_of(own, weights, *mark):
         other = swap(own[:, :part], "core", 1)
-        return gated_sums(place, top_count, own, other, *weights, mark)
+        return gated_sums(place, top_count, own, other, *weights, *mark)
 
     def chip_sums(keep, give):
         return (wide(keep) + wide(swap(give, "core", 1))).astype(jnp.bfloat16)
 
     chip_blocks = [chip_rows] + [swap(chip_rows, "chip", j) for j in range(1, chips)]
     direct = [swap(chip_rows, "dp", k) for k in range(1, groups)]
-    *weights, mark = loaded(
-        in_weight, out_weight.reshape(per_device * half_width, width), chip_blocks[1]
-    )
+    up, mark = loaded(in_weight, chip_blocks[1])
     chip_blocks[1:], mark = lax.optimization_barrier((chip_blocks[1:], mark))
     far = row_major(jnp.concatenate(chip_blocks[1:], 0))
     held = row_major(jnp.concatenate([*chip_blocks, *direct], 0))
     near = spread_near(far)
+    weights = [up, out_weight.reshape(per_device * half_width, width)]
+    pieces = [held]
     if held.shape[0] > MOST_ROWS:
-        pieces = [sums_of(block) for block in (jnp.concatenate(chip_blocks, 0), *direct)]
-        keep, give = (jnp.concatenate(piece, 0) for piece in zip(*pieces))
-    else:
-        keep, give = sums_of(held)
+        pieces = [row_major(jnp.concatenate(chip_blocks, 0)), *direct]
+    keep, give, weights[1] = sums_of(pieces[0], weights, mark)
+    later = [sums_of(piece, weights) for piece in pieces[1:]]
+    if later:
+        keep, give = (jnp.concatenate(x, 0) for x in zip((keep, give), *later))
+    first_sum = chip_sums(keep, give)
     near = behind(near, give)
     rest = spread_rest(near)
-    first_sum = chip_sums(keep, give)
     own_sum = first_sum[: chips * 2 * rows]
     direct_sums = [
         first_sum[low : low + 2 * rows]
@@ -393,7 +408,7 @@
     ]
     if rest:
         near = row_major(jnp.concatenate(near, 0))
-        keep, give = sums_of(near)
+        keep, give = sums_of(near, weights)
         pair = chip_sums(keep, give)
         sums = [pair[: far.shape[0]], pair[far.shape[0] :]]
         rest = behind(rest, give)
@@ -411,15 +426,19 @@
     else:
         sums = [own_sum]
         for block, o in zip(near, direct_sums):
-            keep, give = sums_of(block)
+            keep, give = sums_of(block, weights)
             sums += [jnp.concatenate([o, chip_sums(keep, give)], 0)]
         metas = [held, *near]
     metas = [block[:, block.shape[1] - LANES :] for block in metas]
     border = 2 * near_chips * rows
-    total = collected([block[border:] for block in sums])
-    blocks = [total[low : low + 2 * rows] for low in range(0, total.shape[0], 2 * rows)]
-    total = collected(behind([block[:border] for block in sums], total))
-    blocks = [total[low : low + 2 * rows] for low in range(0, border, 2 * rows)] + blocks
+    high = [block[border:] for block in sums]
+    low = [block[:border] for block in sums]
+    total = collected(high[0], received(high))
+    blocks = [total[at : at + 2 * rows] for at in range(0, total.shape[0], 2 * rows)]
+    load = planned_load(metas, swap_slot, owners, per_device, top_count, blocks[0])
+    low = behind(low, total)
+    total = collected(low[0], received(low))
+    blocks = [total[at : at + 2 * rows] for at in range(0, border, 2 * rows)] + blocks
     total = wide(blocks[0])
     for j in range(1, chips):
         total = total + wide(swap(blocks[j], "chip", j))
@@ -431,8 +450,7 @@
         jnp.concatenate([jnp.where(first, kept, arrived), jnp.where(first, arrived, kept)], 1)
     )
 
-    owner_load = planned_load(metas, swap_slot, owners, per_device, top_count)
-    return (mixed_out, owner_load)
+    return (mixed_out, load[0, :owners])
 
 
 def solution(mesh):

time: 75 us -> 74.9 us (level)
  starting transfers between devices: 28.6 us -> 25.7 us
  waiting for transfers between devices: 20 us -> 22.2 us
    ppermute x28, starting transfers between devices: 28.6 us -> 25.7 us  [swap(): return row_major(lax.ppermute(row_major(value), axis, pairs))]
    ppermute x28, waiting for transfers between devices: 20 us -> 22.2 us  [swap(): return row_major(lax.ppermute(row_major(value), axis, pairs))]
    pallas_call x5, Pallas kernels: 13.2 us -> 15.4 us  [call(): pl.pallas_call(kernel, in_specs=[pl.BlockSpec(memory_space=pltpu.SMEM)] +...]
    pallas_call x1, Pallas kernels: 6.38 us -> 4.58 us  [loaded(): pl.pallas_call(load_weight_kernel, in_specs=[pl.BlockSpec(memory_space=pl...]
  transfers between devices with their start and end apart: 28 -> 28, of which waited for: 12 -> 15; matrix products, arithmetic and copies ran while one was open for 2% -> 2% of each run, Pallas kernels for 28% -> 29%
where the time goes in v14:
time: 74.9 us; the launch traced here: 74.7 us
  starting transfers between devices  25.7 us (34%)
  Pallas kernels  23.1 us (31%)
  waiting for transfers between devices  22.2 us (30%)
  other arithmetic  1.65 us (2%)
  between operations  1 us (1%)
  local copies, waits for them, and re-layouts  0.98 us (1%)
    ppermute x28, starting transfers between devices, swap(): return row_major(lax.ppermute(row_major(value), axis, pairs))  25.7 us
    ppermute x28, waiting for transfers between devices, swap(): return row_major(lax.ppermute(row_major(value), axis, pairs))  22.2 us
    pallas_call x5, Pallas kernels, call(): pl.pallas_call(kernel, in_specs=[pl.BlockSpec(memory_space=pltpu.SMEM)] +...  15.4 us
    pallas_call x1, Pallas kernels, loaded(): pl.pallas_call(load_weight_kernel, in_specs=[pl.BlockSpec(memory_space=pl...  4.58 us
    pallas_call x1, Pallas kernels, first_halves(): pl.pallas_call(first_kernel, in_specs=[pl.BlockSpec(memory_space=pltpu.SM...  1.56 us
  transfers between devices with their start and end apart: 28, of which 15 were waited for; matrix products, arithmetic and copies ran while one was open for 2% of the time, Pallas kernels for 29%

profile of v14, /device:TPU:0, one launch (start us, length us, event | category | flops | bytes accessed | tf_op | source)
XLA Modules:
  0.0 74.7 jit_solution(13875346429811799601)
XLA Ops:
  0.7 1.6 %shard_map.77 = (bf16[12,2176]{1,0:T(8,128)(2,1)S(1)}, bf16[12,2176]{1,0:T(8,128)(2,1)S(1)}) custom-call(s32[2]{0:T(128)S(1)} %pad_add_fusion.place.refs_0_, bf16[12,4096]{1,0:T(8,128)(2,1)} %refs_0_.2, s32[8,12]{1,0:T(8,128)} %bitcast.8, f32[8,12]{1,0:T(8,128)} %bitcast.9), custom_call_target="tpu_custom_call" | custom-call | tf_op jit(solution)/shard_map/pallas_call | solution.py:270
  2.3 0.5 collective-permute-start
  2.8 0.9 %collective-permute-done = bf16[12,2176]{1,0:T(8,128)(2,1)S(1)} collective-permute-done((bf16[12,2176]{1,0:T(8,128)(2,1)S(1)}, bf16[12,2176]{1,0:T(8,128)(2,1)S(1)}, u32[]{:S(2)}, u32[]{:S(2)}) %collective-permute-start) | collective-permute-done | bytes 52256 | tf_op jit(solution)/shard_map/ppermute | solution.py:24
  3.8 3.0 %collective-permute-start.1 = (bf16[24,2176]{1,0:T(8,128)(2,1)S(1)}, bf16[24,2176]{1,0:T(8,128)(2,1)S(1)}, u32[]{:S(2)}, u32[]{:S(2)}) collective-permute-start(bf16[24,2176]{1,0:T(8,128)(2,1)S(1)} %get-tuple-element.51), channel_id=1, source_target_pairs={{0,2},{2,0},{4,6},{6,4},{1,3},{3,1},{5,7},{7,5},{8,10},{10,8},{12,... | collective-permute-start | bytes 313352 | tf_op jit(solution)/shard_map/ppermute | solution.py:24
  6.8 2.5 %collective-permute-start.3 = (bf16[24,2176]{1,0:T(8,128)(2,1)S(1)}, bf16[24,2176]{1,0:T(8,128)(2,1)S(1)}, u32[]{:S(2)}, u32[]{:S(2)}) collective-permute-start(bf16[24,2176]{1,0:T(8,128)(2,1)S(1)} %get-tuple-element.51), channel_id=1, source_target_pairs={{0,6},{2,4},{4,2},{6,0},{1,7},{3,5},{5,3},{7,1},{8,14},{10,12},{12... | collective-permute-start | bytes 313352 | tf_op jit(solution)/shard_map/ppermute | solution.py:24
  9.3 2.4 %collective-permute-start.6 = (bf16[24,2176]{1,0:T(8,128)(2,1)S(1)}, bf16[24,2176]{1,0:T(8,128)(2,1)S(1)}, u32[]{:S(2)}, u32[]{:S(2)}) collective-permute-start(bf16[24,2176]{1,0:T(8,128)(2,1)S(1)} %get-tuple-element.51), channel_id=1, source_target_pairs={{0,24},{8,16},{16,8},{24,0},{1,25},{9,17},{17,9},{25,1},{2,26},{10... | collective-permute-start | bytes 313352 | tf_op jit(solution)/shard_map/ppermute | solution.py:24
  11.8 0.5 collective-permute-start.5
  12.3 0.5 collective-permute-start.4
  12.8 4.6 %shard_map.78 = (bf16[2,4096,768]{2,1,0:T(8,128)(2,1)S(1)}, f32[8,128]{1,0:T(8,128)S(1)}) custom-call(bf16[2,4096,768]{2,1,0:T(8,128)(2,1)} %weight_ref.1, bf16[24,2176]{1,0:T(8,128)(2,1)S(1)} %collective-permute-done.1._), custom_call_target="tpu_custom_call" | custom-call | bytes 12582912 | tf_op jit(solution)/shard_map/pallas_call | solution.py:80
  17.4 1.6 %collective-permute-done.2 = bf16[24,2176]{1,0:T(8,128)(2,1)S(1)} collective-permute-done((bf16[24,2176]{1,0:T(8,128)(2,1)S(1)}, bf16[24,2176]{1,0:T(8,128)(2,1)S(1)}, u32[]{:S(2)}, u32[]{:S(2)}) %collective-permute-start.2) | collective-permute-done | bytes 104480 | tf_op jit(solution)/shard_map/ppermute | solution.py:24
  19.3 1.6 %collective-permute-start.9 = (bf16[72,2176]{1,0:T(8,128)(2,1)S(1)}, bf16[72,2176]{1,0:T(8,128)(2,1)S(1)}, u32[]{:S(2)}, u32[]{:S(2)}) collective-permute-start(bf16[72,2176]{1,0:T(8,128)(2,1)S(1)} %get-tuple-element.69), channel_id=1, source_target_pairs={{0,8},{8,0},{16,24},{24,16},{1,9},{9,1},{17,25},{25,17},{2,10},{10... | collective-permute-start | bytes 940040 | tf_op jit(solution)/shard_map/ppermute | solution.py:24
  20.9 1.5 %collective-permute-start.10 = (bf16[72,2176]{1,0:T(8,128)(2,1)S(1)}, bf16[72,2176]{1,0:T(8,128)(2,1)S(1)}, u32[]{:S(2)}, u32[]{:S(2)}) collective-permute-start(bf16[72,2176]{1,0:T(8,128)(2,1)S(1)} %get-tuple-element.69), channel_id=1, source_target_pairs={{0,16},{8,24},{16,0},{24,8},{1,17},{9,25},{17,1},{25,9},{2,18},{10... | collective-permute-start | bytes 940040 | tf_op jit(solution)/shard_map/ppermute | solution.py:24
  22.4 6.4 %shard_map.79 = (bf16[168,2048]{1,0:T(8,128)(2,1)S(1)}, bf16[168,2048]{1,0:T(8,128)(2,1)S(1)}, bf16[768,4096]{1,0:T(8,128)(2,1)S(1)}) custom-call(s32[2]{0:T(128)S(1)} %pad_add_fusion.place.refs_0_, bf16[168,2176]{1,0:T(8,128)(2,1)S(1)} %constant_dynamic-update-slice_fusion.refs_1_, bf16[168,2048]{1,0:T(8,128)(2,1)S(1)} %collective-permute-done.7.refs_2_, ...), custom_call_target="tpu_custom_call" | custom-call | flops 3170893824 | tf_op jit(solution)/shard_map/pallas_call | solution.py:171
  28.9 0.3 collective-permute-done.9
  29.2 1.2 %collective-permute-done.10 = bf16[72,2176]{1,0:T(8,128)(2,1)S(1)} collective-permute-done((bf16[72,2176]{1,0:T(8,128)(2,1)S(1)}, bf16[72,2176]{1,0:T(8,128)(2,1)S(1)}, u32[]{:S(2)}, u32[]{:S(2)}) %collective-permute-start.10) | collective-permute-done | bytes 313376 | tf_op jit(solution)/shard_map/ppermute | solution.py:24
  30.6 0.5 collective-permute-start.8
  31.1 1.6 %collective-permute-start.13 = (bf16[72,1024]{1,0:T(8,128)(2,1)S(1)}, bf16[72,1024]{1,0:T(8,128)(2,1)S(1)}, u32[]{:S(2)}, u32[]{:S(2)}) collective-permute-start(bf16[72,1024]{1,0:T(8,128)(2,1)S(1)} %slice.107), channel_id=1, source_target_pairs={{0,16},{8,24},{16,0},{24,8},{1,17},{9,25},{17,1},{25,9},{2,18},{10... | collective-permute-start | bytes 442376 | tf_op jit(solution)/shard_map/ppermute | solution.py:24
  32.7 0.5 collective-permute-start.14
  33.2 3.6 %shard_map.80 = (bf16[144,2048]{1,0:T(8,128)(2,1)S(1)}, bf16[144,2048]{1,0:T(8,128)(2,1)S(1)}) custom-call(s32[2]{0:T(128)S(1)} %pad_add_fusion.place.refs_0_, bf16[144,2176]{1,0:T(8,128)(2,1)S(1)} %constant_dynamic-update-slice_fusion.10.refs_1_, bf16[144,2048]{1,0:T(8,128)(2,1)S(1)} %collective-permute-done.11.refs_2_, ...), custom_call_target="tpu_custom_call" | custom-call | flops 2717908992 | tf_op jit(solution)/shard_map/pallas_call | solution.py:171
  37.0 1.6 %collective-permute-done.14.refs_1_ = bf16[72,1152]{1,0:T(8,128)(2,1)S(1)} collective-permute-done((bf16[72,1152]{1,0:T(8,128)(2,1)S(1)}, bf16[72,1152]{1,0:T(8,128)(2,1)S(1)}, u32[]{:S(2)}, u32[]{:S(2)}) %collective-permute-start.14) | collective-permute-done | bytes 165920 | tf_op jit(solution)/shard_map/ppermute | solution.py:24
  38.7 0.5 collective-permute-start.15
  39.2 1.7 %shard_map.81.refs_4_ = f32[2,72,768]{2,1,0:T(8,128)S(1)} custom-call(s32[2]{0:T(128)S(1)} %pad_add_fusion.place.refs_0_, bf16[72,1024]{1,0:T(8,128)(2,1)S(1)} %collective-permute-done.13.first, bf16[72,1024]{1,0:T(8,128)(2,1)S(1)} %slice.109.second, bf16[2,4096,768]{2,1,0:T(8,128)(2,1)S(1)} %get-tuple-element.32.refs_3_.up.refs_5_), custom_call_target="tpu_custom_call" | custom-call | flops 452984832 | tf_op jit(solution)/shard_map/pallas_call | solution.py:171
  41.0 0.2 add_convert_fusion
  41.3 2.4 %shard_map.82 = (bf16[72,2048]{1,0:T(8,128)(2,1)S(1)}, bf16[72,768]{1,0:T(8,128)(2,1)S(1)}) custom-call(s32[2]{0:T(128)S(1)} %pad_add_fusion.place.refs_0_, bf16[72,1152]{1,0:T(8,128)(2,1)S(1)} %collective-permute-done.14.refs_1_, bf16[72,1024]{1,0:T(8,128)(2,1)S(1)} %collective-permute-done.15.refs_2_, ...), custom_call_target="tpu_custom_call" | custom-call | flops 679477248 | tf_op jit(solution)/shard_map/pallas_call | solution.py:171
  43.6 0.1 collective-permute-start.17
  43.8 1.2 %shard_map.83.kept_ref = bf16[72,2048]{1,0:T(8,128)(2,1)S(1)} custom-call(s32[2]{0:T(128)S(1)} %pad_add_fusion.place.refs_0_, bf16[72,768]{1,0:T(8,128)(2,1)S(1)} %get-tuple-element.43.hidden, bf16[768,4096]{1,0:T(8,128)(2,1)S(1)} %get-tuple-element.38.refs_4_.refs_6_.down), custom_call_target="tpu_custom_call" | custom-call | flops 226492416 | tf_op jit(solution)/shard_map/pallas_call | solution.py:171
  45.0 0.2 collective-permute-done.17.taken_ref
  45.4 0.6 collective-permute-start.19
  46.0 0.6 collective-permute-start.18
  46.6 0.1 add_convert_fusion.1
  46.8 5.7 %collective-permute-done.19 = bf16[96,1024]{1,0:T(8,128)(2,1)S(1)} collective-permute-done((bf16[96,1024]{1,0:T(8,128)(2,1)S(1)}, bf16[96,1024]{1,0:T(8,128)(2,1)S(1)}, u32[]{:S(2)}, u32[]{:S(2)}) %collective-permute-start.19) | collective-permute-done | bytes 196640 | tf_op jit(solution)/shard_map/ppermute | solution.py:24
  52.4 0.3 collective-permute-done.18
  53.0 0.6 collective-permute-start.21
  53.6 1.5 %collective-permute-start.20 = (bf16[48,2048]{1,0:T(8,128)(2,1)S(1)}, bf16[48,2048]{1,0:T(8,128)(2,1)S(1)}, u32[]{:S(2)}, u32[]{:S(2)}) collective-permute-start(bf16[48,2048]{1,0:T(8,128)(2,1)S(1)} %get-tuple-element.61), channel_id=1, source_target_pairs={{0,8},{8,0},{16,24},{24,16},{1,9},{9,1},{17,25},{25,17},{2,10},{10... | collective-permute-start | bytes 589832 | tf_op jit(solution)/shard_map/ppermute | solution.py:24
  55.1 3.9 %collective-permute-done.21 = bf16[48,2048]{1,0:T(8,128)(2,1)S(1)} collective-permute-done((bf16[48,2048]{1,0:T(8,128)(2,1)S(1)}, bf16[48,2048]{1,0:T(8,128)(2,1)S(1)}, u32[]{:S(2)}, u32[]{:S(2)}) %collective-permute-start.21) | collective-permute-done | bytes 196640 | tf_op jit(solution)/shard_map/ppermute | solution.py:24
  59.0 0.3 collective-permute-done.20
  59.4 1.6 %collective-permute-start.22 = (bf16[48,2048]{1,0:T(8,128)(2,1)S(1)}, bf16[48,2048]{1,0:T(8,128)(2,1)S(1)}, u32[]{:S(2)}, u32[]{:S(2)}) collective-permute-start(bf16[48,2048]{1,0:T(8,128)(2,1)S(1)} %get-tuple-element.48), channel_id=1, source_target_pairs={{0,8},{8,0},{16,24},{24,16},{1,9},{9,1},{17,25},{25,17},{2,10},{10... | collective-permute-start | bytes 589832 | tf_op jit(solution)/shard_map/ppermute | solution.py:24
  60.9 1.5 %collective-permute-start.23 = (bf16[48,2048]{1,0:T(8,128)(2,1)S(1)}, bf16[48,2048]{1,0:T(8,128)(2,1)S(1)}, u32[]{:S(2)}, u32[]{:S(2)}) collective-permute-start(bf16[48,2048]{1,0:T(8,128)(2,1)S(1)} %get-tuple-element.49), channel_id=1, source_target_pairs={{0,16},{8,24},{16,0},{24,8},{1,17},{9,25},{17,1},{25,9},{2,18},{10... | collective-permute-start | bytes 589832 | tf_op jit(solution)/shard_map/ppermute | solution.py:24
  62.4 2.7 %collective-permute-start.26 = (bf16[24,2048]{1,0:T(8,128)(2,1)S(1)}, bf16[24,2048]{1,0:T(8,128)(2,1)S(1)}, u32[]{:S(2)}, u32[]{:S(2)}) collective-permute-start(bf16[24,2048]{1,0:T(8,128)(2,1)S(1)} %get-tuple-element.63), channel_id=1, source_target_pairs={{0,6},{2,4},{4,2},{6,0},{1,7},{3,5},{5,3},{7,1},{8,14},{10,12},{12... | collective-permute-start | bytes 294920 | tf_op jit(solution)/shard_map/ppermute | solution.py:24
  65.2 1.4 %collective-permute-done.23 = bf16[48,2048]{1,0:T(8,128)(2,1)S(1)} collective-permute-done((bf16[48,2048]{1,0:T(8,128)(2,1)S(1)}, bf16[48,2048]{1,0:T(8,128)(2,1)S(1)}, u32[]{:S(2)}, u32[]{:S(2)}) %collective-permute-start.23) | collective-permute-done | bytes 196640 | tf_op jit(solution)/shard_map/ppermute | solution.py:24
  66.7 0.4 collective-permute-start.24
  67.1 1.5 %shard_map.85 = f32[1,128]{1,0:T(1,128)S(1)} custom-call(s32[8]{0:T(128)S(1)} %copy-done, bf16[168,128]{1,0:T(8,128)(2,1)S(1)} %slice.155.refs_1_, bf16[144,128]{1,0:T(8,128)(2,1)S(1)} %slice.156.refs_2_, bf16[72,128]{1,0:T(8,128)(2,1)S(1)} %slice.129.refs_3_, bf16[24,2048]{1,0:T(8,128)(2,1)S(1)} %get-tuple-element.62.refs_4_), custom_call_target="tpu_custom_call" | custom-call | bytes 98304 | tf_op jit(solution)/shard_map/pallas_call | solution.py:344
  68.6 0.6 collective-permute-done.26
  69.2 2.6 %collective-permute-done.25 = bf16[24,2048]{1,0:T(8,128)(2,1)S(1)} collective-permute-done((bf16[24,2048]{1,0:T(8,128)(2,1)S(1)}, bf16[24,2048]{1,0:T(8,128)(2,1)S(1)}, u32[]{:S(2)}, u32[]{:S(2)}) %collective-permute-start.25) | collective-permute-done | bytes 98336 | tf_op jit(solution)/shard_map/ppermute | solution.py:24
  71.8 0.8 %collective-permute-done.24 = bf16[24,2048]{1,0:T(8,128)(2,1)S(1)} collective-permute-done((bf16[24,2048]{1,0:T(8,128)(2,1)S(1)}, bf16[24,2048]{1,0:T(8,128)(2,1)S(1)}, u32[]{:S(2)}, u32[]{:S(2)}) %collective-permute-start.24) | collective-permute-done | bytes 98336 | tf_op jit(solution)/shard_map/ppermute | solution.py:24
  72.7 0.5 slice_bitcast_fusion
  73.2 0.7 collective-permute-done.27
  74.0 0.7 pad_maximum_fusion.4
  (60 shorter events, 1.7 us)
Async XLA Ops:
  2.3 1.4 %collective-permute-start = (bf16[12,2176]{1,0:T(8,128)(2,1)S(1)}, bf16[12,2176]{1,0:T(8,128)(2,1)S(1)}, u32[]{:S(2)}, u32[]{:S(2)}) collective-permute-start(bf16[12,2176]{1,0:T(8,128)(2,1)S(1)} %get-tuple-element.27), channel_id=1, source_target_pairs={{0,1},{1,0},{2,3},{3,2},{4,5},{5,4},{6,7},{7,6},{8,9},{9,8},{10,11... | collective-permute-start | bytes 156680 | tf_op jit(solution)/shard_map/ppermute | solution.py:24
  3.8 8.5 %collective-permute-start.1 = (bf16[24,2176]{1,0:T(8,128)(2,1)S(1)}, bf16[24,2176]{1,0:T(8,128)(2,1)S(1)}, u32[]{:S(2)}, u32[]{:S(2)}) collective-permute-start(bf16[24,2176]{1,0:T(8,128)(2,1)S(1)} %get-tuple-element.51), channel_id=1, source_target_pairs={{0,2},{2,0},{4,6},{6,4},{1,3},{3,1},{5,7},{7,5},{8,10},{10,8},{12,... | collective-permute-start | bytes 313352 | tf_op jit(solution)/shard_map/ppermute | solution.py:24
  6.8 10.7 %collective-permute-start.3 = (bf16[24,2176]{1,0:T(8,128)(2,1)S(1)}, bf16[24,2176]{1,0:T(8,128)(2,1)S(1)}, u32[]{:S(2)}, u32[]{:S(2)}) collective-permute-start(bf16[24,2176]{1,0:T(8,128)(2,1)S(1)} %get-tuple-element.51), channel_id=1, source_target_pairs={{0,6},{2,4},{4,2},{6,0},{1,7},{3,5},{5,3},{7,1},{8,14},{10,12},{12... | collective-permute-start | bytes 313352 | tf_op jit(solution)/shard_map/ppermute | solution.py:24
  9.2 9.8 %collective-permute-start.2 = (bf16[24,2176]{1,0:T(8,128)(2,1)S(1)}, bf16[24,2176]{1,0:T(8,128)(2,1)S(1)}, u32[]{:S(2)}, u32[]{:S(2)}) collective-permute-start(bf16[24,2176]{1,0:T(8,128)(2,1)S(1)} %get-tuple-element.51), channel_id=1, source_target_pairs={{0,4},{2,6},{4,0},{6,2},{1,5},{3,7},{5,1},{7,3},{8,12},{10,14},{12... | collective-permute-start | bytes 313352 | tf_op jit(solution)/shard_map/ppermute | solution.py:24
  9.3 9.8 %collective-permute-start.6 = (bf16[24,2176]{1,0:T(8,128)(2,1)S(1)}, bf16[24,2176]{1,0:T(8,128)(2,1)S(1)}, u32[]{:S(2)}, u32[]{:S(2)}) collective-permute-start(bf16[24,2176]{1,0:T(8,128)(2,1)S(1)} %get-tuple-element.51), channel_id=1, source_target_pairs={{0,24},{8,16},{16,8},{24,0},{1,25},{9,17},{17,9},{25,1},{2,26},{10... | collective-permute-start | bytes 313352 | tf_op jit(solution)/shard_map/ppermute | solution.py:24
  11.8 7.3 %collective-permute-start.5 = (bf16[24,2176]{1,0:T(8,128)(2,1)S(1)}, bf16[24,2176]{1,0:T(8,128)(2,1)S(1)}, u32[]{:S(2)}, u32[]{:S(2)}) collective-permute-start(bf16[24,2176]{1,0:T(8,128)(2,1)S(1)} %get-tuple-element.51), channel_id=1, source_target_pairs={{0,16},{8,24},{16,0},{24,8},{1,17},{9,25},{17,1},{25,9},{2,18},{10... | collective-permute-start | bytes 313352 | tf_op jit(solution)/shard_map/ppermute | solution.py:24
  12.3 6.8 %collective-permute-start.4 = (bf16[24,2176]{1,0:T(8,128)(2,1)S(1)}, bf16[24,2176]{1,0:T(8,128)(2,1)S(1)}, u32[]{:S(2)}, u32[]{:S(2)}) collective-permute-start(bf16[24,2176]{1,0:T(8,128)(2,1)S(1)} %get-tuple-element.51), channel_id=1, source_target_pairs={{0,8},{8,0},{16,24},{24,16},{1,9},{9,1},{17,25},{25,17},{2,10},{10... | collective-permute-start | bytes 313352 | tf_op jit(solution)/shard_map/ppermute | solution.py:24
  19.3 3.2 %collective-permute-start.7 = (bf16[168,2048]{1,0:T(8,128)(2,1)S(1)}, bf16[168,2048]{1,0:T(8,128)(2,1)S(1)}, u32[]{:S(2)}, u32[]{:S(2)}) collective-permute-start(bf16[168,2048]{1,0:T(8,128)(2,1)S(1)} %slice.131), channel_id=1, source_target_pairs={{0,1},{1,0},{2,3},{3,2},{4,5},{5,4},{6,7},{7,6},{8,9},{9,8},{10,11... | collective-permute-start | bytes 2064392 | tf_op jit(solution)/shard_map/ppermute | solution.py:24
  19.3 9.8 %collective-permute-start.9 = (bf16[72,2176]{1,0:T(8,128)(2,1)S(1)}, bf16[72,2176]{1,0:T(8,128)(2,1)S(1)}, u32[]{:S(2)}, u32[]{:S(2)}) collective-permute-start(bf16[72,2176]{1,0:T(8,128)(2,1)S(1)} %get-tuple-element.69), channel_id=1, source_target_pairs={{0,8},{8,0},{16,24},{24,16},{1,9},{9,1},{17,25},{25,17},{2,10},{10... | collective-permute-start | bytes 940040 | tf_op jit(solution)/shard_map/ppermute | solution.py:24
  20.9 9.5 %collective-permute-start.10 = (bf16[72,2176]{1,0:T(8,128)(2,1)S(1)}, bf16[72,2176]{1,0:T(8,128)(2,1)S(1)}, u32[]{:S(2)}, u32[]{:S(2)}) collective-permute-start(bf16[72,2176]{1,0:T(8,128)(2,1)S(1)} %get-tuple-element.69), channel_id=1, source_target_pairs={{0,16},{8,24},{16,0},{24,8},{1,17},{9,25},{17,1},{25,9},{2,18},{10... | collective-permute-start | bytes 940040 | tf_op jit(solution)/shard_map/ppermute | solution.py:24
  30.5 2.7 %collective-permute-start.11 = (bf16[144,2048]{1,0:T(8,128)(2,1)S(1)}, bf16[144,2048]{1,0:T(8,128)(2,1)S(1)}, u32[]{:S(2)}, u32[]{:S(2)}) collective-permute-start(bf16[144,2048]{1,0:T(8,128)(2,1)S(1)} %slice.134), channel_id=1, source_target_pairs={{0,1},{1,0},{2,3},{3,2},{4,5},{5,4},{6,7},{7,6},{8,9},{9,8},{10,11... | collective-permute-start | bytes 1769480 | tf_op jit(solution)/shard_map/ppermute | solution.py:24
  30.6 10.4 %collective-permute-start.8 = (bf16[168,2048]{1,0:T(8,128)(2,1)S(1)}, bf16[168,2048]{1,0:T(8,128)(2,1)S(1)}, u32[]{:S(2)}, u32[]{:S(2)}) collective-permute-start(bf16[168,2048]{1,0:T(8,128)(2,1)S(1)} %get-tuple-element.35), channel_id=1, source_target_pairs={{0,1},{1,0},{2,3},{3,2},{4,5},{5,4},{6,7},{7,6},{8,9},{9,8},{10,11... | collective-permute-start | bytes 2064392 | tf_op jit(solution)/shard_map/ppermute | solution.py:24
  31.1 5.9 %collective-permute-start.13 = (bf16[72,1024]{1,0:T(8,128)(2,1)S(1)}, bf16[72,1024]{1,0:T(8,128)(2,1)S(1)}, u32[]{:S(2)}, u32[]{:S(2)}) collective-permute-start(bf16[72,1024]{1,0:T(8,128)(2,1)S(1)} %slice.107), channel_id=1, source_target_pairs={{0,16},{8,24},{16,0},{24,8},{1,17},{9,25},{17,1},{25,9},{2,18},{10... | collective-permute-start | bytes 442376 | tf_op jit(solution)/shard_map/ppermute | solution.py:24
  32.7 5.9 %collective-permute-start.14 = (bf16[72,1152]{1,0:T(8,128)(2,1)S(1)}, bf16[72,1152]{1,0:T(8,128)(2,1)S(1)}, u32[]{:S(2)}, u32[]{:S(2)}) collective-permute-start(bf16[72,1152]{1,0:T(8,128)(2,1)S(1)} %slice.108), channel_id=1, source_target_pairs={{0,8},{8,0},{16,24},{24,16},{1,9},{9,1},{17,25},{25,17},{2,10},{10... | collective-permute-start | bytes 497672 | tf_op jit(solution)/shard_map/ppermute | solution.py:24
  36.9 9.7 %collective-permute-start.12 = (bf16[144,2048]{1,0:T(8,128)(2,1)S(1)}, bf16[144,2048]{1,0:T(8,128)(2,1)S(1)}, u32[]{:S(2)}, u32[]{:S(2)}) collective-permute-start(bf16[144,2048]{1,0:T(8,128)(2,1)S(1)} %get-tuple-element.40), channel_id=1, source_target_pairs={{0,1},{1,0},{2,3},{3,2},{4,5},{5,4},{6,7},{7,6},{8,9},{9,8},{10,11... | collective-permute-start | bytes 1769480 | tf_op jit(solution)/shard_map/ppermute | solution.py:24
  38.7 2.6 %collective-permute-start.16 = (bf16[72,1024]{1,0:T(8,128)(2,1)S(1)}, bf16[72,1024]{1,0:T(8,128)(2,1)S(1)}, u32[]{:S(2)}, u32[]{:S(2)}) collective-permute-start(bf16[72,1024]{1,0:T(8,128)(2,1)S(1)} %slice.109.second), channel_id=1, source_target_pairs={{0,1},{1,0},{2,3},{3,2},{4,5},{5,4},{6,7},{7,6},{8,9},{9,8},{10,11... | collective-permute-start | bytes 442376 | tf_op jit(solution)/shard_map/ppermute | solution.py:24
  38.7 2.5 %collective-permute-start.15 = (bf16[72,1024]{1,0:T(8,128)(2,1)S(1)}, bf16[72,1024]{1,0:T(8,128)(2,1)S(1)}, u32[]{:S(2)}, u32[]{:S(2)}) collective-permute-start(bf16[72,1024]{1,0:T(8,128)(2,1)S(1)} %collective-permute-done.13.first), channel_id=1, source_target_pairs={{0,1},{1,0},{2,3},{3,2},{4,5},{5,4},{6,7},{7,6},{8,9},{9,8},{10,11... | collective-permute-start | bytes 442376 | tf_op jit(solution)/shard_map/ppermute | solution.py:24
  43.6 1.6 %collective-permute-start.17 = (bf16[72,2048]{1,0:T(8,128)(2,1)S(1)}, bf16[72,2048]{1,0:T(8,128)(2,1)S(1)}, u32[]{:S(2)}, u32[]{:S(2)}) collective-permute-start(bf16[72,2048]{1,0:T(8,128)(2,1)S(1)} %get-tuple-element.44), channel_id=1, source_target_pairs={{0,1},{1,0},{2,3},{3,2},{4,5},{5,4},{6,7},{7,6},{8,9},{9,8},{10,11... | collective-permute-start | bytes 884744 | tf_op jit(solution)/shard_map/ppermute | solution.py:24
  45.4 7.1 %collective-permute-start.19 = (bf16[96,1024]{1,0:T(8,128)(2,1)S(1)}, bf16[96,1024]{1,0:T(8,128)(2,1)S(1)}, u32[]{:S(2)}, u32[]{:S(2)}) collective-permute-start(bf16[96,1024]{1,0:T(8,128)(2,1)S(1)} %pad_maximum_fusion.3), channel_id=1, source_target_pairs={{0,8},{8,0},{16,24},{24,16},{1,9},{9,1},{17,25},{25,17},{2,10},{10... | collective-permute-start | bytes 589832 | tf_op jit(solution)/shard_map/ppermute | solution.py:24
  46.0 6.8 %collective-permute-start.18 = (bf16[96,1024]{1,0:T(8,128)(2,1)S(1)}, bf16[96,1024]{1,0:T(8,128)(2,1)S(1)}, u32[]{:S(2)}, u32[]{:S(2)}) collective-permute-start(bf16[96,1024]{1,0:T(8,128)(2,1)S(1)} %pad_maximum_fusion.2), channel_id=1, source_target_pairs={{0,16},{8,24},{16,0},{24,8},{1,17},{9,25},{17,1},{25,9},{2,18},{10... | collective-permute-start | bytes 589832 | tf_op jit(solution)/shard_map/ppermute | solution.py:24
  53.0 5.9 %collective-permute-start.21 = (bf16[48,2048]{1,0:T(8,128)(2,1)S(1)}, bf16[48,2048]{1,0:T(8,128)(2,1)S(1)}, u32[]{:S(2)}, u32[]{:S(2)}) collective-permute-start(bf16[48,2048]{1,0:T(8,128)(2,1)S(1)} %get-tuple-element.59), channel_id=1, source_target_pairs={{0,16},{8,24},{16,0},{24,8},{1,17},{9,25},{17,1},{25,9},{2,18},{10... | collective-permute-start | bytes 589832 | tf_op jit(solution)/shard_map/ppermute | solution.py:24
  53.6 13.5 %copy-start = (s32[8]{0:T(128)S(1)}, s32[8]{0:T(128)}, u32[]{:S(2)}) copy-start(s32[8]{0:T(128)} %refs_0_.3) | copy-start | bytes 100
  53.6 5.7 %collective-permute-start.20 = (bf16[48,2048]{1,0:T(8,128)(2,1)S(1)}, bf16[48,2048]{1,0:T(8,128)(2,1)S(1)}, u32[]{:S(2)}, u32[]{:S(2)}) collective-permute-start(bf16[48,2048]{1,0:T(8,128)(2,1)S(1)} %get-tuple-element.61), channel_id=1, source_target_pairs={{0,8},{8,0},{16,24},{24,16},{1,9},{9,1},{17,25},{25,17},{2,10},{10... | collective-permute-start | bytes 589832 | tf_op jit(solution)/shard_map/ppermute | solution.py:24
  59.4 5.8 %collective-permute-start.22 = (bf16[48,2048]{1,0:T(8,128)(2,1)S(1)}, bf16[48,2048]{1,0:T(8,128)(2,1)S(1)}, u32[]{:S(2)}, u32[]{:S(2)}) collective-permute-start(bf16[48,2048]{1,0:T(8,128)(2,1)S(1)} %get-tuple-element.48), channel_id=1, source_target_pairs={{0,8},{8,0},{16,24},{24,16},{1,9},{9,1},{17,25},{25,17},{2,10},{10... | collective-permute-start | bytes 589832 | tf_op jit(solution)/shard_map/ppermute | solution.py:24
  60.9 5.7 %collective-permute-start.23 = (bf16[48,2048]{1,0:T(8,128)(2,1)S(1)}, bf16[48,2048]{1,0:T(8,128)(2,1)S(1)}, u32[]{:S(2)}, u32[]{:S(2)}) collective-permute-start(bf16[48,2048]{1,0:T(8,128)(2,1)S(1)} %get-tuple-element.49), channel_id=1, source_target_pairs={{0,16},{8,24},{16,0},{24,8},{1,17},{9,25},{17,1},{25,9},{2,18},{10... | collective-permute-start | bytes 589832 | tf_op jit(solution)/shard_map/ppermute | solution.py:24
  62.4 6.8 %collective-permute-start.26 = (bf16[24,2048]{1,0:T(8,128)(2,1)S(1)}, bf16[24,2048]{1,0:T(8,128)(2,1)S(1)}, u32[]{:S(2)}, u32[]{:S(2)}) collective-permute-start(bf16[24,2048]{1,0:T(8,128)(2,1)S(1)} %get-tuple-element.63), channel_id=1, source_target_pairs={{0,6},{2,4},{4,2},{6,0},{1,7},{3,5},{5,3},{7,1},{8,14},{10,12},{12... | collective-permute-start | bytes 294920 | tf_op jit(solution)/shard_map/ppermute | solution.py:24
  65.2 6.6 %collective-permute-start.25 = (bf16[24,2048]{1,0:T(8,128)(2,1)S(1)}, bf16[24,2048]{1,0:T(8,128)(2,1)S(1)}, u32[]{:S(2)}, u32[]{:S(2)}) collective-permute-start(bf16[24,2048]{1,0:T(8,128)(2,1)S(1)} %get-tuple-element.62.refs_4_), channel_id=1, source_target_pairs={{0,4},{2,6},{4,0},{6,2},{1,5},{3,7},{5,1},{7,3},{8,12},{10,14},{12... | collective-permute-start | bytes 294920 | tf_op jit(solution)/shard_map/ppermute | solution.py:24
  66.7 5.9 %collective-permute-start.24 = (bf16[24,2048]{1,0:T(8,128)(2,1)S(1)}, bf16[24,2048]{1,0:T(8,128)(2,1)S(1)}, u32[]{:S(2)}, u32[]{:S(2)}) collective-permute-start(bf16[24,2048]{1,0:T(8,128)(2,1)S(1)} %slice.150), channel_id=1, source_target_pairs={{0,2},{2,0},{4,6},{6,4},{1,3},{3,1},{5,7},{7,5},{8,10},{10,8},{12,... | collective-permute-start | bytes 294920 | tf_op jit(solution)/shard_map/ppermute | solution.py:24
  72.6 1.3 %collective-permute-start.27 = (bf16[12,2048]{1,0:T(8,128)(2,1)S(1)}, bf16[12,2048]{1,0:T(8,128)(2,1)S(1)}, u32[]{:S(2)}, u32[]{:S(2)}) collective-permute-start(bf16[12,2048]{1,0:T(8,128)(2,1)S(1)} %broadcast_select_fusion.4), channel_id=1, source_target_pairs={{0,1},{1,0},{2,3},{3,2},{4,5},{5,4},{6,7},{7,6},{8,9},{9,8},{10,11... | collective-permute-start | bytes 147464 | tf_op jit(solution)/shard_map/ppermute | solution.py:24

commit v15 on v14

--- a/solution.py
+++ b/solution.py
@@ -24,20 +24,16 @@
     return row_major(lax.ppermute(row_major(value), axis, pairs))
 
 
-def cut_of(block):
-    return block.shape[1] // (2 * LANES) * LANES
-
-
 def spread_near(block):
     size = lax.axis_size("dp")
     return [swap(block, "dp", k) for k in range(1, 3 if size == 4 else size)]
 
 
-def spread_rest(near):
-    if lax.axis_size("dp") != 4:
-        return []
-    cut = cut_of(near[0])
-    return [swap(near[0][:, :cut], "dp", 2), swap(near[1][:, cut:], "dp", 1)]
+def cross(value):
+    pairs = []
+    for i in range(4):
+        pairs += [(2 * i, 2 * (i ^ 2)), (2 * i + 1, 2 * (i ^ 1) + 1)]
+    return row_major(lax.ppermute(row_major(value), ("dp", "core"), pairs))
 
 
 def behind(values, others):
@@ -48,17 +44,12 @@
     return value.astype(jnp.float32)
 
 
-def with_fourth(blocks, halves):
-    own, one, two = blocks
-    cut = cut_of(own)
-    upper, lower = swap(halves[0], "dp", 2), swap(halves[1], "dp", 1)
-    one = jnp.concatenate(
-        [(wide(one[:, :cut]) + wide(upper)).astype(jnp.bfloat16), one[:, cut:]], 1
-    )
-    two = jnp.concatenate(
-        [two[:, :cut], (wide(two[:, cut:]) + wide(lower)).astype(jnp.bfloat16)], 1
-    )
-    return [own, one, two]
+def with_fourth(one, two, fourth, first):
+    came = wide(cross(fourth))
+    return (
+        jnp.where(first, wide(one) + came, wide(one)).astype(jnp.bfloat16),
+        jnp.where(first, wide(two), wide(two) + came).astype(jnp.bfloat16),
+    )
 
 
 def received(blocks):
@@ -145,18 +136,18 @@
     multiply_down(keep_ref, hidden, down, bases[0])
 
 
-def own_kernel(place, first, second, up, acc):
-    cut = first.shape[1]
+def own_kernel(place, own, up, acc):
+    part = up.shape[1] // 2
     acc[...] = jnp.zeros_like(acc)
-    add_up(acc, [[first], [second]], [cut, cut], up, place[0] * 2 * cut)
-
-
-def give_kernel(top_count, place, routed, first, second, held, up, down, give_ref, hidden, acc):
-    cut = first.shape[1]
-    base = (1 - place[0]) * 2 * cut
+    add_up(acc, [[own]], [part], up, place[0] * part)
+
+
+def give_kernel(top_count, place, own, other, held, up, down, give_ref, hidden, acc):
+    part = other.shape[1]
+    base = (1 - place[0]) * part
     acc[...] = held[...]
-    add_up(acc, [[first], [second]], [cut, cut], up, base)
-    make_hidden(hidden, acc, [routed], cut, place[1], top_count)
+    add_up(acc, [[other]], [part], up, base)
+    make_hidden(hidden, acc, [own], part, place[1], top_count)
     multiply_down(give_ref, hidden, down, base)
 
 
@@ -209,20 +200,20 @@
     )
 
 
-def gated_sums_in_halves(place, top_count, own, other, up, down):
-    count, cut = own[0].shape
+def gated_sums_in_steps(place, top_count, own, other, up, down):
+    count, part = other.shape
     acc_shape = (up.shape[0], count, up.shape[2])
     (held,) = call(
         own_kernel,
-        [place, own[0], own[1][:, :cut], up],
+        [place, own, up],
         [pltpu.VMEM(acc_shape, jnp.float32)],
         flops=count * up.size,
     )
     give, hidden = call(
         lambda *refs: give_kernel(top_count, *refs),
-        [place, own[1], *other, held, up, down],
+        [place, own, other, held, up, down],
         [
-            pltpu.VMEM((count, 2 * cut), jnp.bfloat16),
+            pltpu.VMEM((count, part), jnp.bfloat16),
             pltpu.VMEM((count, down.shape[0]), jnp.bfloat16),
         ],
         [pltpu.VMEM(acc_shape, jnp.float32)],
@@ -231,7 +222,7 @@
     (keep,) = call(
         keep_kernel,
         [place, hidden, down],
-        [pltpu.VMEM((count, 2 * cut), jnp.bfloat16)],
+        [pltpu.VMEM((count, part), jnp.bfloat16)],
         flops=count * down.size,
     )
     return keep, give
@@ -279,24 +270,18 @@
     )(place, *(pltpu.with_memory_space_constraint(x, pltpu.HBM) for x in sources))
 
 
-def added_kernel(kept_ref, taken_ref, left_ref, right_ref):
+def added_kernel(kept_ref, taken_ref, total_ref):
     total = kept_ref[...].astype(jnp.float32) + taken_ref[...].astype(jnp.float32)
-    cut = left_ref.shape[1]
-    left_ref[...] = total[:, :cut].astype(jnp.bfloat16)
-    right_ref[...] = total[:, cut:].astype(jnp.bfloat16)
-
-
-def added(kept, taken, cut):
+    total_ref[...] = total.astype(jnp.bfloat16)
+
+
+def added(kept, taken):
     in_vmem = pl.BlockSpec(memory_space=pltpu.VMEM)
-    count, width = kept.shape
     return pl.pallas_call(
         added_kernel,
         in_specs=[in_vmem] * 2,
-        out_specs=[in_vmem] * 2,
-        out_shape=[
-            pltpu.VMEM((count, cut), jnp.bfloat16),
-            pltpu.VMEM((count, width - cut), jnp.bfloat16),
-        ],
+        out_specs=in_vmem,
+        out_shape=pltpu.VMEM(kept.shape, jnp.bfloat16),
         compiler_params=pltpu.CompilerParams(vmem_limit_bytes=VMEM_LIMIT),
     )(*(pltpu.with_memory_space_constraint(x, pltpu.VMEM) for x in (kept, taken)))
 
@@ -400,29 +385,23 @@
         keep, give = (jnp.concatenate(x, 0) for x in zip((keep, give), *later))
     first_sum = chip_sums(keep, give)
     near = behind(near, give)
-    rest = spread_rest(near)
     own_sum = first_sum[: chips * 2 * rows]
     direct_sums = [
         first_sum[low : low + 2 * rows]
         for low in range(chips * 2 * rows, first_sum.shape[0], 2 * rows)
     ]
-    if rest:
+    if groups == 4:
+        rest = cross(jnp.where(first, near[0], near[1]))
         near = row_major(jnp.concatenate(near, 0))
         keep, give = sums_of(near, weights)
         pair = chip_sums(keep, give)
-        sums = [pair[: far.shape[0]], pair[far.shape[0] :]]
         rest = behind(rest, give)
-        cut = rest[0].shape[1]
-        other = [swap(half[:, :cut], "core", 1) for half in rest]
-        keep, give = gated_sums_in_halves(place, top_count, rest, other, *weights)
-        diagonal = added(keep, swap(give, "core", 1), cut)
-        diagonal = [
-            jnp.concatenate([block, half], 0)
-            for block, half in zip((direct_sums[2][:, :cut], direct_sums[2][:, cut:]), diagonal)
-        ]
+        other = swap(rest[:, :part], "core", 1)
+        keep, give = gated_sums_in_steps(place, top_count, rest, other, *weights)
+        sums = [pair[: far.shape[0]], pair[far.shape[0] :], added(keep, swap(give, "core", 1))]
         sums = [jnp.concatenate([o, s], 0) for o, s in zip(direct_sums, sums)]
-        sums = with_fourth([own_sum, *sums], diagonal)
-        metas = [held, near, rest[1]]
+        sums = [own_sum, *with_fourth(*sums, first)]
+        metas = [held, near, rest]
     else:
         sums = [own_sum]
         for block, o in zip(near, direct_sums):

time: 74.9 us -> 74.9 us (level)
    ppermute x0 -> x2, waiting for transfers between devices: none -> 7.63 us  [cross(): return row_major(lax.ppermute(row_major(value), ('dp', 'core'), pairs))]
    ppermute x28 -> x23, waiting for transfers between devices: 22.2 us -> 14.6 us  [swap(): return row_major(lax.ppermute(row_major(value), axis, pairs))]
    ppermute x28 -> x23, starting transfers between devices: 25.7 us -> 22.5 us  [swap(): return row_major(lax.ppermute(row_major(value), axis, pairs))]
    ppermute x0 -> x2, starting transfers between devices: none -> 3.11 us  [cross(): return row_major(lax.ppermute(row_major(value), ('dp', 'core'), pairs))]
  transfers between devices with their start and end apart: 28 -> 25, of which waited for: 15 -> 13; matrix products, arithmetic and copies ran while one was open for 2% -> 2% of each run, Pallas kernels for 29% -> 29%
where the time goes in v15:
time: 74.9 us; the launch traced here: 74.7 us
  starting transfers between devices  25.6 us (34%)
  Pallas kernels  23.1 us (31%)
  waiting for transfers between devices  22.3 us (30%)
  other arithmetic  1.77 us (2%)
  local copies, waits for them, and re-layouts  0.96 us (1%)
  between operations  0.96 us (1%)
    ppermute x23, starting transfers between devices, swap(): return row_major(lax.ppermute(row_major(value), axis, pairs))  22.5 us
    pallas_call x5, Pallas kernels, call(): pl.pallas_call(kernel, in_specs=[pl.BlockSpec(memory_space=pltpu.SMEM)] +...  15.4 us
    ppermute x23, waiting for transfers between devices, swap(): return row_major(lax.ppermute(row_major(value), axis, pairs))  14.6 us
    ppermute x2, waiting for transfers between devices, cross(): return row_major(lax.ppermute(row_major(value), ('dp', 'core'), pairs))  7.63 us
    pallas_call x1, Pallas kernels, loaded(): pl.pallas_call(load_weight_kernel, in_specs=[pl.BlockSpec(memory_space=pl...  4.58 us
    ppermute x2, starting transfers between devices, cross(): return row_major(lax.ppermute(row_major(value), ('dp', 'core'), pairs))  3.11 us
    pallas_call x1, Pallas kernels, first_halves(): pl.pallas_call(first_kernel, in_specs=[pl.BlockSpec(memory_space=pltpu.SM...  1.56 us
  transfers between devices with their start and end apart: 25, of which 13 were waited for; matrix products, arithmetic and copies ran while one was open for 2% of the time, Pallas kernels for 29%

profile of v15, /device:TPU:0, one launch (start us, length us, event | category | flops | bytes accessed | tf_op | source)
XLA Modules:
  0.0 74.7 jit_solution(903409813185835358)
XLA Ops:
  0.7 1.6 %shard_map.77 = (bf16[12,2176]{1,0:T(8,128)(2,1)S(1)}, bf16[12,2176]{1,0:T(8,128)(2,1)S(1)}) custom-call(s32[2]{0:T(128)S(1)} %pad_add_fusion.place.refs_0_, bf16[12,4096]{1,0:T(8,128)(2,1)} %refs_0_.2, s32[8,12]{1,0:T(8,128)} %bitcast.8, f32[8,12]{1,0:T(8,128)} %bitcast.9), custom_call_target="tpu_custom_call" | custom-call | tf_op jit(solution)/shard_map/pallas_call | solution.py:261
  2.3 0.5 collective-permute-start
  2.8 0.9 %collective-permute-done = bf16[12,2176]{1,0:T(8,128)(2,1)S(1)} collective-permute-done((bf16[12,2176]{1,0:T(8,128)(2,1)S(1)}, bf16[12,2176]{1,0:T(8,128)(2,1)S(1)}, u32[]{:S(2)}, u32[]{:S(2)}) %collective-permute-start) | collective-permute-done | bytes 52256 | tf_op jit(solution)/shard_map/ppermute | solution.py:24
  3.8 3.0 %collective-permute-start.1 = (bf16[24,2176]{1,0:T(8,128)(2,1)S(1)}, bf16[24,2176]{1,0:T(8,128)(2,1)S(1)}, u32[]{:S(2)}, u32[]{:S(2)}) collective-permute-start(bf16[24,2176]{1,0:T(8,128)(2,1)S(1)} %get-tuple-element.45), channel_id=1, source_target_pairs={{0,2},{2,0},{4,6},{6,4},{1,3},{3,1},{5,7},{7,5},{8,10},{10,8},{12,... | collective-permute-start | bytes 313352 | tf_op jit(solution)/shard_map/ppermute | solution.py:24
  6.8 2.5 %collective-permute-start.3 = (bf16[24,2176]{1,0:T(8,128)(2,1)S(1)}, bf16[24,2176]{1,0:T(8,128)(2,1)S(1)}, u32[]{:S(2)}, u32[]{:S(2)}) collective-permute-start(bf16[24,2176]{1,0:T(8,128)(2,1)S(1)} %get-tuple-element.45), channel_id=1, source_target_pairs={{0,6},{2,4},{4,2},{6,0},{1,7},{3,5},{5,3},{7,1},{8,14},{10,12},{12... | collective-permute-start | bytes 313352 | tf_op jit(solution)/shard_map/ppermute | solution.py:24
  9.2 0.1 collective-permute-start.2
  9.3 2.4 %collective-permute-start.6 = (bf16[24,2176]{1,0:T(8,128)(2,1)S(1)}, bf16[24,2176]{1,0:T(8,128)(2,1)S(1)}, u32[]{:S(2)}, u32[]{:S(2)}) collective-permute-start(bf16[24,2176]{1,0:T(8,128)(2,1)S(1)} %get-tuple-element.45), channel_id=1, source_target_pairs={{0,24},{8,16},{16,8},{24,0},{1,25},{9,17},{17,9},{25,1},{2,26},{10... | collective-permute-start | bytes 313352 | tf_op jit(solution)/shard_map/ppermute | solution.py:24
  11.8 0.5 collective-permute-start.5
  12.3 0.5 collective-permute-start.4
  12.8 4.6 %shard_map.78 = (bf16[2,4096,768]{2,1,0:T(8,128)(2,1)S(1)}, f32[8,128]{1,0:T(8,128)S(1)}) custom-call(bf16[2,4096,768]{2,1,0:T(8,128)(2,1)} %weight_ref.1, bf16[24,2176]{1,0:T(8,128)(2,1)S(1)} %collective-permute-done.1._), custom_call_target="tpu_custom_call" | custom-call | bytes 12582912 | tf_op jit(solution)/shard_map/pallas_call | solution.py:71
  17.4 1.6 %collective-permute-done.2 = bf16[24,2176]{1,0:T(8,128)(2,1)S(1)} collective-permute-done((bf16[24,2176]{1,0:T(8,128)(2,1)S(1)}, bf16[24,2176]{1,0:T(8,128)(2,1)S(1)}, u32[]{:S(2)}, u32[]{:S(2)}) %collective-permute-start.2) | collective-permute-done | bytes 104480 | tf_op jit(solution)/shard_map/ppermute | solution.py:24
  19.3 1.6 %collective-permute-start.9 = (bf16[72,2176]{1,0:T(8,128)(2,1)S(1)}, bf16[72,2176]{1,0:T(8,128)(2,1)S(1)}, u32[]{:S(2)}, u32[]{:S(2)}) collective-permute-start(bf16[72,2176]{1,0:T(8,128)(2,1)S(1)} %get-tuple-element.66), channel_id=1, source_target_pairs={{0,8},{8,0},{16,24},{24,16},{1,9},{9,1},{17,25},{25,17},{2,10},{10... | collective-permute-start | bytes 940040 | tf_op jit(solution)/shard_map/ppermute | solution.py:24
  20.9 1.5 %collective-permute-start.10 = (bf16[72,2176]{1,0:T(8,128)(2,1)S(1)}, bf16[72,2176]{1,0:T(8,128)(2,1)S(1)}, u32[]{:S(2)}, u32[]{:S(2)}) collective-permute-start(bf16[72,2176]{1,0:T(8,128)(2,1)S(1)} %get-tuple-element.66), channel_id=1, source_target_pairs={{0,16},{8,24},{16,0},{24,8},{1,17},{9,25},{17,1},{25,9},{2,18},{10... | collective-permute-start | bytes 940040 | tf_op jit(solution)/shard_map/ppermute | solution.py:24
  22.4 6.4 %shard_map.79 = (bf16[168,2048]{1,0:T(8,128)(2,1)S(1)}, bf16[168,2048]{1,0:T(8,128)(2,1)S(1)}, bf16[768,4096]{1,0:T(8,128)(2,1)S(1)}) custom-call(s32[2]{0:T(128)S(1)} %pad_add_fusion.place.refs_0_, bf16[168,2176]{1,0:T(8,128)(2,1)S(1)} %constant_dynamic-update-slice_fusion.refs_1_, bf16[168,2048]{1,0:T(8,128)(2,1)S(1)} %collective-permute-done.7.refs_2_, ...), custom_call_target="tpu_custom_call" | custom-call | flops 3170893824 | tf_op jit(solution)/shard_map/pallas_call | solution.py:162
  28.9 0.3 collective-permute-done.9
  29.2 1.2 %collective-permute-done.10 = bf16[72,2176]{1,0:T(8,128)(2,1)S(1)} collective-permute-done((bf16[72,2176]{1,0:T(8,128)(2,1)S(1)}, bf16[72,2176]{1,0:T(8,128)(2,1)S(1)}, u32[]{:S(2)}, u32[]{:S(2)}) %collective-permute-start.10) | collective-permute-done | bytes 313376 | tf_op jit(solution)/shard_map/ppermute | solution.py:24
  30.4 0.1 constant_dynamic-update-slice_fusion.10
  30.6 0.5 collective-permute-start.8
  31.1 1.5 %collective-permute-start.13 = (bf16[72,2176]{1,0:T(8,128)(2,1)S(1)}, bf16[72,2176]{1,0:T(8,128)(2,1)S(1)}, u32[]{:S(2)}, u32[]{:S(2)}) collective-permute-start(bf16[72,2176]{1,0:T(8,128)(2,1)S(1)} %get-tuple-element.58), channel_id=1, source_target_pairs={{0,16},{1,9},{8,24},{9,1},{16,0},{17,25},{24,8},{25,17},{2,18},{3,... | collective-permute-start | bytes 940040 | tf_op jit(solution)/shard_map/ppermute | solution.py:36
  32.7 3.6 %shard_map.80 = (bf16[144,2048]{1,0:T(8,128)(2,1)S(1)}, bf16[144,2048]{1,0:T(8,128)(2,1)S(1)}) custom-call(s32[2]{0:T(128)S(1)} %pad_add_fusion.place.refs_0_, bf16[144,2176]{1,0:T(8,128)(2,1)S(1)} %get-tuple-element.57.refs_1_, bf16[144,2048]{1,0:T(8,128)(2,1)S(1)} %collective-permute-done.11.refs_2_, ...), custom_call_target="tpu_custom_call" | custom-call | flops 2717908992 | tf_op jit(solution)/shard_map/pallas_call | solution.py:162
  36.3 0.2 collective-permute-start.12
  36.5 1.6 %collective-permute-done.13.own.refs_1_ = bf16[72,2176]{1,0:T(8,128)(2,1)S(1)} collective-permute-done((bf16[72,2176]{1,0:T(8,128)(2,1)S(1)}, bf16[72,2176]{1,0:T(8,128)(2,1)S(1)}, u32[]{:S(2)}, u32[]{:S(2)}) %collective-permute-start.13) | collective-permute-done | bytes 313376 | tf_op jit(solution)/shard_map/ppermute | solution.py:36
  38.2 1.8 %shard_map.81.refs_3_ = f32[2,72,768]{2,1,0:T(8,128)S(1)} custom-call(s32[2]{0:T(128)S(1)} %pad_add_fusion.place.refs_0_, bf16[72,2176]{1,0:T(8,128)(2,1)S(1)} %collective-permute-done.13.own.refs_1_, bf16[2,4096,768]{2,1,0:T(8,128)(2,1)S(1)} %get-tuple-element.29.refs_3_.up.refs_4_), custom_call_target="tpu_custom_call" | custom-call | flops 452984832 | tf_op jit(solution)/shard_map/pallas_call | solution.py:162
  39.9 0.2 add_convert_fusion
  40.2 2.4 %shard_map.82 = (bf16[72,2048]{1,0:T(8,128)(2,1)S(1)}, bf16[72,768]{1,0:T(8,128)(2,1)S(1)}) custom-call(s32[2]{0:T(128)S(1)} %pad_add_fusion.place.refs_0_, bf16[72,2176]{1,0:T(8,128)(2,1)S(1)} %collective-permute-done.13.own.refs_1_, bf16[72,2048]{1,0:T(8,128)(2,1)S(1)} %collective-permute-done.14.refs_2_, f32[2,72,768]{2,1,0:T(8,128)S(1)} %shard_map.81.refs_3_, ...), custom_call_target="tpu_custom_call" | custom-call | flops 679477248 | tf_op jit(solution)/shard_map/pallas_call | solution.py:162
  42.6 0.6 collective-permute-start.15
  43.1 1.2 %shard_map.83.kept_ref = bf16[72,2048]{1,0:T(8,128)(2,1)S(1)} custom-call(s32[2]{0:T(128)S(1)} %pad_add_fusion.place.refs_0_, bf16[72,768]{1,0:T(8,128)(2,1)S(1)} %get-tuple-element.39.hidden, bf16[768,4096]{1,0:T(8,128)(2,1)S(1)} %get-tuple-element.35.refs_4_.refs_5_.down), custom_call_target="tpu_custom_call" | custom-call | flops 226492416 | tf_op jit(solution)/shard_map/pallas_call | solution.py:162
  44.5 1.6 %collective-permute-start.16 = (bf16[96,2048]{1,0:T(8,128)(2,1)S(1)}, bf16[96,2048]{1,0:T(8,128)(2,1)S(1)}, u32[]{:S(2)}, u32[]{:S(2)}) collective-permute-start(bf16[96,2048]{1,0:T(8,128)(2,1)S(1)} %pad_maximum_fusion), channel_id=1, source_target_pairs={{0,16},{1,9},{8,24},{9,1},{16,0},{17,25},{24,8},{25,17},{2,18},{3,... | collective-permute-start | bytes 1179656 | tf_op jit(solution)/shard_map/ppermute | solution.py:36
  46.1 0.1 add_convert_fusion.1
  46.3 6.1 %collective-permute-done.16 = bf16[96,2048]{1,0:T(8,128)(2,1)S(1)} collective-permute-done((bf16[96,2048]{1,0:T(8,128)(2,1)S(1)}, bf16[96,2048]{1,0:T(8,128)(2,1)S(1)}, u32[]{:S(2)}, u32[]{:S(2)}) %collective-permute-start.16) | collective-permute-done | bytes 393248 | tf_op jit(solution)/shard_map/ppermute | solution.py:36
  52.3 0.2 fusion
  52.6 0.6 collective-permute-start.17
  53.2 1.6 %collective-permute-start.18 = (bf16[48,2048]{1,0:T(8,128)(2,1)S(1)}, bf16[48,2048]{1,0:T(8,128)(2,1)S(1)}, u32[]{:S(2)}, u32[]{:S(2)}) collective-permute-start(bf16[48,2048]{1,0:T(8,128)(2,1)S(1)} %get-tuple-element.52), channel_id=1, source_target_pairs={{0,16},{8,24},{16,0},{24,8},{1,17},{9,25},{17,1},{25,9},{2,18},{10... | collective-permute-start | bytes 589832 | tf_op jit(solution)/shard_map/ppermute | solution.py:24
  54.8 4.1 %collective-permute-done.17 = bf16[48,2048]{1,0:T(8,128)(2,1)S(1)} collective-permute-done((bf16[48,2048]{1,0:T(8,128)(2,1)S(1)}, bf16[48,2048]{1,0:T(8,128)(2,1)S(1)}, u32[]{:S(2)}, u32[]{:S(2)}) %collective-permute-start.17) | collective-permute-done | bytes 196640 | tf_op jit(solution)/shard_map/ppermute | solution.py:24
  58.9 0.4 collective-permute-done.18
  59.3 0.1 add_convert_fusion.3
  59.4 1.6 %collective-permute-start.19 = (bf16[48,2048]{1,0:T(8,128)(2,1)S(1)}, bf16[48,2048]{1,0:T(8,128)(2,1)S(1)}, u32[]{:S(2)}, u32[]{:S(2)}) collective-permute-start(bf16[48,2048]{1,0:T(8,128)(2,1)S(1)} %get-tuple-element.42), channel_id=1, source_target_pairs={{0,8},{8,0},{16,24},{24,16},{1,9},{9,1},{17,25},{25,17},{2,10},{10... | collective-permute-start | bytes 589832 | tf_op jit(solution)/shard_map/ppermute | solution.py:24
  60.9 1.5 %collective-permute-start.20 = (bf16[48,2048]{1,0:T(8,128)(2,1)S(1)}, bf16[48,2048]{1,0:T(8,128)(2,1)S(1)}, u32[]{:S(2)}, u32[]{:S(2)}) collective-permute-start(bf16[48,2048]{1,0:T(8,128)(2,1)S(1)} %get-tuple-element.43), channel_id=1, source_target_pairs={{0,16},{8,24},{16,0},{24,8},{1,17},{9,25},{17,1},{25,9},{2,18},{10... | collective-permute-start | bytes 589832 | tf_op jit(solution)/shard_map/ppermute | solution.py:24
  62.5 2.7 %collective-permute-start.23 = (bf16[24,2048]{1,0:T(8,128)(2,1)S(1)}, bf16[24,2048]{1,0:T(8,128)(2,1)S(1)}, u32[]{:S(2)}, u32[]{:S(2)}) collective-permute-start(bf16[24,2048]{1,0:T(8,128)(2,1)S(1)} %get-tuple-element.60), channel_id=1, source_target_pairs={{0,6},{2,4},{4,2},{6,0},{1,7},{3,5},{5,3},{7,1},{8,14},{10,12},{12... | collective-permute-start | bytes 294920 | tf_op jit(solution)/shard_map/ppermute | solution.py:24
  65.2 1.4 %collective-permute-done.20 = bf16[48,2048]{1,0:T(8,128)(2,1)S(1)} collective-permute-done((bf16[48,2048]{1,0:T(8,128)(2,1)S(1)}, bf16[48,2048]{1,0:T(8,128)(2,1)S(1)}, u32[]{:S(2)}, u32[]{:S(2)}) %collective-permute-start.20) | collective-permute-done | bytes 196640 | tf_op jit(solution)/shard_map/ppermute | solution.py:24
  66.7 0.4 collective-permute-start.21
  67.1 1.5 %shard_map.85 = f32[1,128]{1,0:T(1,128)S(1)} custom-call(s32[8]{0:T(128)S(1)} %copy-done, bf16[168,128]{1,0:T(8,128)(2,1)S(1)} %slice.118.refs_1_, bf16[144,128]{1,0:T(8,128)(2,1)S(1)} %slice.119.refs_2_, bf16[72,128]{1,0:T(8,128)(2,1)S(1)} %slice.97.refs_3_, bf16[24,2048]{1,0:T(8,128)(2,1)S(1)} %get-tuple-element.59.refs_4_), custom_call_target="tpu_custom_call" | custom-call | bytes 98304 | tf_op jit(solution)/shard_map/pallas_call | solution.py:329
  68.6 0.9 %collective-permute-done.23 = bf16[24,2048]{1,0:T(8,128)(2,1)S(1)} collective-permute-done((bf16[24,2048]{1,0:T(8,128)(2,1)S(1)}, bf16[24,2048]{1,0:T(8,128)(2,1)S(1)}, u32[]{:S(2)}, u32[]{:S(2)}) %collective-permute-start.23) | collective-permute-done | bytes 98336 | tf_op jit(solution)/shard_map/ppermute | solution.py:24
  69.5 2.6 %collective-permute-done.22 = bf16[24,2048]{1,0:T(8,128)(2,1)S(1)} collective-permute-done((bf16[24,2048]{1,0:T(8,128)(2,1)S(1)}, bf16[24,2048]{1,0:T(8,128)(2,1)S(1)}, u32[]{:S(2)}, u32[]{:S(2)}) %collective-permute-start.22) | collective-permute-done | bytes 98336 | tf_op jit(solution)/shard_map/ppermute | solution.py:24
  72.1 0.5 collective-permute-done.21
  72.8 0.5 slice_bitcast_fusion
  73.3 0.7 collective-permute-done.24
  74.1 0.7 pad_maximum_fusion.1
  (48 shorter events, 1.2 us)
Async XLA Ops:
  2.3 1.4 %collective-permute-start = (bf16[12,2176]{1,0:T(8,128)(2,1)S(1)}, bf16[12,2176]{1,0:T(8,128)(2,1)S(1)}, u32[]{:S(2)}, u32[]{:S(2)}) collective-permute-start(bf16[12,2176]{1,0:T(8,128)(2,1)S(1)} %get-tuple-element.24), channel_id=1, source_target_pairs={{0,1},{1,0},{2,3},{3,2},{4,5},{5,4},{6,7},{7,6},{8,9},{9,8},{10,11... | collective-permute-start | bytes 156680 | tf_op jit(solution)/shard_map/ppermute | solution.py:24
  3.8 8.5 %collective-permute-start.1 = (bf16[24,2176]{1,0:T(8,128)(2,1)S(1)}, bf16[24,2176]{1,0:T(8,128)(2,1)S(1)}, u32[]{:S(2)}, u32[]{:S(2)}) collective-permute-start(bf16[24,2176]{1,0:T(8,128)(2,1)S(1)} %get-tuple-element.45), channel_id=1, source_target_pairs={{0,2},{2,0},{4,6},{6,4},{1,3},{3,1},{5,7},{7,5},{8,10},{10,8},{12,... | collective-permute-start | bytes 313352 | tf_op jit(solution)/shard_map/ppermute | solution.py:24
  6.8 10.7 %collective-permute-start.3 = (bf16[24,2176]{1,0:T(8,128)(2,1)S(1)}, bf16[24,2176]{1,0:T(8,128)(2,1)S(1)}, u32[]{:S(2)}, u32[]{:S(2)}) collective-permute-start(bf16[24,2176]{1,0:T(8,128)(2,1)S(1)} %get-tuple-element.45), channel_id=1, source_target_pairs={{0,6},{2,4},{4,2},{6,0},{1,7},{3,5},{5,3},{7,1},{8,14},{10,12},{12... | collective-permute-start | bytes 313352 | tf_op jit(solution)/shard_map/ppermute | solution.py:24
  9.2 9.8 %collective-permute-start.2 = (bf16[24,2176]{1,0:T(8,128)(2,1)S(1)}, bf16[24,2176]{1,0:T(8,128)(2,1)S(1)}, u32[]{:S(2)}, u32[]{:S(2)}) collective-permute-start(bf16[24,2176]{1,0:T(8,128)(2,1)S(1)} %get-tuple-element.45), channel_id=1, source_target_pairs={{0,4},{2,6},{4,0},{6,2},{1,5},{3,7},{5,1},{7,3},{8,12},{10,14},{12... | collective-permute-start | bytes 313352 | tf_op jit(solution)/shard_map/ppermute | solution.py:24
  9.3 9.8 %collective-permute-start.6 = (bf16[24,2176]{1,0:T(8,128)(2,1)S(1)}, bf16[24,2176]{1,0:T(8,128)(2,1)S(1)}, u32[]{:S(2)}, u32[]{:S(2)}) collective-permute-start(bf16[24,2176]{1,0:T(8,128)(2,1)S(1)} %get-tuple-element.45), channel_id=1, source_target_pairs={{0,24},{8,16},{16,8},{24,0},{1,25},{9,17},{17,9},{25,1},{2,26},{10... | collective-permute-start | bytes 313352 | tf_op jit(solution)/shard_map/ppermute | solution.py:24
  11.8 7.3 %collective-permute-start.5 = (bf16[24,2176]{1,0:T(8,128)(2,1)S(1)}, bf16[24,2176]{1,0:T(8,128)(2,1)S(1)}, u32[]{:S(2)}, u32[]{:S(2)}) collective-permute-start(bf16[24,2176]{1,0:T(8,128)(2,1)S(1)} %get-tuple-element.45), channel_id=1, source_target_pairs={{0,16},{8,24},{16,0},{24,8},{1,17},{9,25},{17,1},{25,9},{2,18},{10... | collective-permute-start | bytes 313352 | tf_op jit(solution)/shard_map/ppermute | solution.py:24
  12.3 6.8 %collective-permute-start.4 = (bf16[24,2176]{1,0:T(8,128)(2,1)S(1)}, bf16[24,2176]{1,0:T(8,128)(2,1)S(1)}, u32[]{:S(2)}, u32[]{:S(2)}) collective-permute-start(bf16[24,2176]{1,0:T(8,128)(2,1)S(1)} %get-tuple-element.45), channel_id=1, source_target_pairs={{0,8},{8,0},{16,24},{24,16},{1,9},{9,1},{17,25},{25,17},{2,10},{10... | collective-permute-start | bytes 313352 | tf_op jit(solution)/shard_map/ppermute | solution.py:24
  19.3 3.2 %collective-permute-start.7 = (bf16[168,2048]{1,0:T(8,128)(2,1)S(1)}, bf16[168,2048]{1,0:T(8,128)(2,1)S(1)}, u32[]{:S(2)}, u32[]{:S(2)}) collective-permute-start(bf16[168,2048]{1,0:T(8,128)(2,1)S(1)} %slice.99), channel_id=1, source_target_pairs={{0,1},{1,0},{2,3},{3,2},{4,5},{5,4},{6,7},{7,6},{8,9},{9,8},{10,11... | collective-permute-start | bytes 2064392 | tf_op jit(solution)/shard_map/ppermute | solution.py:24
  19.3 9.8 %collective-permute-start.9 = (bf16[72,2176]{1,0:T(8,128)(2,1)S(1)}, bf16[72,2176]{1,0:T(8,128)(2,1)S(1)}, u32[]{:S(2)}, u32[]{:S(2)}) collective-permute-start(bf16[72,2176]{1,0:T(8,128)(2,1)S(1)} %get-tuple-element.66), channel_id=1, source_target_pairs={{0,8},{8,0},{16,24},{24,16},{1,9},{9,1},{17,25},{25,17},{2,10},{10... | collective-permute-start | bytes 940040 | tf_op jit(solution)/shard_map/ppermute | solution.py:24
  20.9 9.5 %collective-permute-start.10 = (bf16[72,2176]{1,0:T(8,128)(2,1)S(1)}, bf16[72,2176]{1,0:T(8,128)(2,1)S(1)}, u32[]{:S(2)}, u32[]{:S(2)}) collective-permute-start(bf16[72,2176]{1,0:T(8,128)(2,1)S(1)} %get-tuple-element.66), channel_id=1, source_target_pairs={{0,16},{8,24},{16,0},{24,8},{1,17},{9,25},{17,1},{25,9},{2,18},{10... | collective-permute-start | bytes 940040 | tf_op jit(solution)/shard_map/ppermute | solution.py:24
  30.6 2.1 %collective-permute-start.11 = (bf16[144,2048]{1,0:T(8,128)(2,1)S(1)}, bf16[144,2048]{1,0:T(8,128)(2,1)S(1)}, u32[]{:S(2)}, u32[]{:S(2)}) collective-permute-start(bf16[144,2048]{1,0:T(8,128)(2,1)S(1)} %slice.102), channel_id=1, source_target_pairs={{0,1},{1,0},{2,3},{3,2},{4,5},{5,4},{6,7},{7,6},{8,9},{9,8},{10,11... | collective-permute-start | bytes 1769480 | tf_op jit(solution)/shard_map/ppermute | solution.py:24
  30.6 9.3 %collective-permute-start.8 = (bf16[168,2048]{1,0:T(8,128)(2,1)S(1)}, bf16[168,2048]{1,0:T(8,128)(2,1)S(1)}, u32[]{:S(2)}, u32[]{:S(2)}) collective-permute-start(bf16[168,2048]{1,0:T(8,128)(2,1)S(1)} %get-tuple-element.32), channel_id=1, source_target_pairs={{0,1},{1,0},{2,3},{3,2},{4,5},{5,4},{6,7},{7,6},{8,9},{9,8},{10,11... | collective-permute-start | bytes 2064392 | tf_op jit(solution)/shard_map/ppermute | solution.py:24
  31.1 6.9 %collective-permute-start.13 = (bf16[72,2176]{1,0:T(8,128)(2,1)S(1)}, bf16[72,2176]{1,0:T(8,128)(2,1)S(1)}, u32[]{:S(2)}, u32[]{:S(2)}) collective-permute-start(bf16[72,2176]{1,0:T(8,128)(2,1)S(1)} %get-tuple-element.58), channel_id=1, source_target_pairs={{0,16},{1,9},{8,24},{9,1},{16,0},{17,25},{24,8},{25,17},{2,18},{3,... | collective-permute-start | bytes 940040 | tf_op jit(solution)/shard_map/ppermute | solution.py:36
  36.3 9.8 %collective-permute-start.12 = (bf16[144,2048]{1,0:T(8,128)(2,1)S(1)}, bf16[144,2048]{1,0:T(8,128)(2,1)S(1)}, u32[]{:S(2)}, u32[]{:S(2)}) collective-permute-start(bf16[144,2048]{1,0:T(8,128)(2,1)S(1)} %get-tuple-element.37), channel_id=1, source_target_pairs={{0,1},{1,0},{2,3},{3,2},{4,5},{5,4},{6,7},{7,6},{8,9},{9,8},{10,11... | collective-permute-start | bytes 1769480 | tf_op jit(solution)/shard_map/ppermute | solution.py:24
  38.1 2.1 %collective-permute-start.14 = (bf16[72,2048]{1,0:T(8,128)(2,1)S(1)}, bf16[72,2048]{1,0:T(8,128)(2,1)S(1)}, u32[]{:S(2)}, u32[]{:S(2)}) collective-permute-start(bf16[72,2048]{1,0:T(8,128)(2,1)S(1)} %slice.81), channel_id=1, source_target_pairs={{0,1},{1,0},{2,3},{3,2},{4,5},{5,4},{6,7},{7,6},{8,9},{9,8},{10,11... | collective-permute-start | bytes 884744 | tf_op jit(solution)/shard_map/ppermute | solution.py:24
  42.6 1.8 %collective-permute-start.15 = (bf16[72,2048]{1,0:T(8,128)(2,1)S(1)}, bf16[72,2048]{1,0:T(8,128)(2,1)S(1)}, u32[]{:S(2)}, u32[]{:S(2)}) collective-permute-start(bf16[72,2048]{1,0:T(8,128)(2,1)S(1)} %get-tuple-element.40), channel_id=1, source_target_pairs={{0,1},{1,0},{2,3},{3,2},{4,5},{5,4},{6,7},{7,6},{8,9},{9,8},{10,11... | collective-permute-start | bytes 884744 | tf_op jit(solution)/shard_map/ppermute | solution.py:24
  44.5 7.8 %collective-permute-start.16 = (bf16[96,2048]{1,0:T(8,128)(2,1)S(1)}, bf16[96,2048]{1,0:T(8,128)(2,1)S(1)}, u32[]{:S(2)}, u32[]{:S(2)}) collective-permute-start(bf16[96,2048]{1,0:T(8,128)(2,1)S(1)} %pad_maximum_fusion), channel_id=1, source_target_pairs={{0,16},{1,9},{8,24},{9,1},{16,0},{17,25},{24,8},{25,17},{2,18},{3,... | collective-permute-start | bytes 1179656 | tf_op jit(solution)/shard_map/ppermute | solution.py:36
  52.6 6.3 %collective-permute-start.17 = (bf16[48,2048]{1,0:T(8,128)(2,1)S(1)}, bf16[48,2048]{1,0:T(8,128)(2,1)S(1)}, u32[]{:S(2)}, u32[]{:S(2)}) collective-permute-start(bf16[48,2048]{1,0:T(8,128)(2,1)S(1)} %get-tuple-element.54), channel_id=1, source_target_pairs={{0,8},{8,0},{16,24},{24,16},{1,9},{9,1},{17,25},{25,17},{2,10},{10... | collective-permute-start | bytes 589832 | tf_op jit(solution)/shard_map/ppermute | solution.py:24
  53.2 13.9 %copy-start = (s32[8]{0:T(128)S(1)}, s32[8]{0:T(128)}, u32[]{:S(2)}) copy-start(s32[8]{0:T(128)} %refs_0_.3) | copy-start | bytes 100
  53.2 6.1 %collective-permute-start.18 = (bf16[48,2048]{1,0:T(8,128)(2,1)S(1)}, bf16[48,2048]{1,0:T(8,128)(2,1)S(1)}, u32[]{:S(2)}, u32[]{:S(2)}) collective-permute-start(bf16[48,2048]{1,0:T(8,128)(2,1)S(1)} %get-tuple-element.52), channel_id=1, source_target_pairs={{0,16},{8,24},{16,0},{24,8},{1,17},{9,25},{17,1},{25,9},{2,18},{10... | collective-permute-start | bytes 589832 | tf_op jit(solution)/shard_map/ppermute | solution.py:24
  59.4 5.8 %collective-permute-start.19 = (bf16[48,2048]{1,0:T(8,128)(2,1)S(1)}, bf16[48,2048]{1,0:T(8,128)(2,1)S(1)}, u32[]{:S(2)}, u32[]{:S(2)}) collective-permute-start(bf16[48,2048]{1,0:T(8,128)(2,1)S(1)} %get-tuple-element.42), channel_id=1, source_target_pairs={{0,8},{8,0},{16,24},{24,16},{1,9},{9,1},{17,25},{25,17},{2,10},{10... | collective-permute-start | bytes 589832 | tf_op jit(solution)/shard_map/ppermute | solution.py:24
  60.9 5.7 %collective-permute-start.20 = (bf16[48,2048]{1,0:T(8,128)(2,1)S(1)}, bf16[48,2048]{1,0:T(8,128)(2,1)S(1)}, u32[]{:S(2)}, u32[]{:S(2)}) collective-permute-start(bf16[48,2048]{1,0:T(8,128)(2,1)S(1)} %get-tuple-element.43), channel_id=1, source_target_pairs={{0,16},{8,24},{16,0},{24,8},{1,17},{9,25},{17,1},{25,9},{2,18},{10... | collective-permute-start | bytes 589832 | tf_op jit(solution)/shard_map/ppermute | solution.py:24
  62.5 7.1 %collective-permute-start.23 = (bf16[24,2048]{1,0:T(8,128)(2,1)S(1)}, bf16[24,2048]{1,0:T(8,128)(2,1)S(1)}, u32[]{:S(2)}, u32[]{:S(2)}) collective-permute-start(bf16[24,2048]{1,0:T(8,128)(2,1)S(1)} %get-tuple-element.60), channel_id=1, source_target_pairs={{0,6},{2,4},{4,2},{6,0},{1,7},{3,5},{5,3},{7,1},{8,14},{10,12},{12... | collective-permute-start | bytes 294920 | tf_op jit(solution)/shard_map/ppermute | solution.py:24
  65.2 6.9 %collective-permute-start.22 = (bf16[24,2048]{1,0:T(8,128)(2,1)S(1)}, bf16[24,2048]{1,0:T(8,128)(2,1)S(1)}, u32[]{:S(2)}, u32[]{:S(2)}) collective-permute-start(bf16[24,2048]{1,0:T(8,128)(2,1)S(1)} %get-tuple-element.59.refs_4_), channel_id=1, source_target_pairs={{0,4},{2,6},{4,0},{6,2},{1,5},{3,7},{5,1},{7,3},{8,12},{10,14},{12... | collective-permute-start | bytes 294920 | tf_op jit(solution)/shard_map/ppermute | solution.py:24
  66.7 5.9 %collective-permute-start.21 = (bf16[24,2048]{1,0:T(8,128)(2,1)S(1)}, bf16[24,2048]{1,0:T(8,128)(2,1)S(1)}, u32[]{:S(2)}, u32[]{:S(2)}) collective-permute-start(bf16[24,2048]{1,0:T(8,128)(2,1)S(1)} %slice.113), channel_id=1, source_target_pairs={{0,2},{2,0},{4,6},{6,4},{1,3},{3,1},{5,7},{7,5},{8,10},{10,8},{12,... | collective-permute-start | bytes 294920 | tf_op jit(solution)/shard_map/ppermute | solution.py:24
  72.7 1.3 %collective-permute-start.24 = (bf16[12,2048]{1,0:T(8,128)(2,1)S(1)}, bf16[12,2048]{1,0:T(8,128)(2,1)S(1)}, u32[]{:S(2)}, u32[]{:S(2)}) collective-permute-start(bf16[12,2048]{1,0:T(8,128)(2,1)S(1)} %broadcast_select_fusion.5), channel_id=1, source_target_pairs={{0,1},{1,0},{2,3},{3,2},{4,5},{5,4},{6,7},{7,6},{8,9},{9,8},{10,11... | collective-permute-start | bytes 147464 | tf_op jit(solution)/shard_map/ppermute | solution.py:24

commit v16 on v15

--- a/solution.py
+++ b/solution.py
@@ -344,7 +344,6 @@
 def on_device(tokens, expert_ids, gate_probs, in_weight, out_weight, swap_slot):
     groups, chips = lax.axis_size("dp"), lax.axis_size("chip")
     owners = 2 * chips
-    near_chips = chips // 2
     per_device = in_weight.shape[0]
     rows, width = tokens.shape
     part = width // 2
@@ -368,9 +367,10 @@
     def chip_sums(keep, give):
         return (wide(keep) + wide(swap(give, "core", 1))).astype(jnp.bfloat16)
 
-    chip_blocks = [chip_rows] + [swap(chip_rows, "chip", j) for j in range(1, chips)]
+    chip_blocks = [swap(chip_rows, "chip", j) for j in range(chips - 1, 0, -1)]
+    chip_blocks = [chip_rows, *chip_blocks[::-1]]
     direct = [swap(chip_rows, "dp", k) for k in range(1, groups)]
-    up, mark = loaded(in_weight, chip_blocks[1])
+    up, mark = loaded(in_weight, direct[0])
     chip_blocks[1:], mark = lax.optimization_barrier((chip_blocks[1:], mark))
     far = row_major(jnp.concatenate(chip_blocks[1:], 0))
     held = row_major(jnp.concatenate([*chip_blocks, *direct], 0))
@@ -385,11 +385,12 @@
         keep, give = (jnp.concatenate(x, 0) for x in zip((keep, give), *later))
     first_sum = chip_sums(keep, give)
     near = behind(near, give)
-    own_sum = first_sum[: chips * 2 * rows]
-    direct_sums = [
-        first_sum[low : low + 2 * rows]
-        for low in range(chips * 2 * rows, first_sum.shape[0], 2 * rows)
+    border = chips * 2 * rows
+    near_sums = [first_sum[: 2 * rows]]
+    near_sums += [
+        first_sum[low : low + 2 * rows] for low in range(border, first_sum.shape[0], 2 * rows)
     ]
+    far_sums = [first_sum[2 * rows : border]]
     if groups == 4:
         rest = cross(jnp.where(first, near[0], near[1]))
         near = row_major(jnp.concatenate(near, 0))
@@ -398,30 +399,21 @@
         rest = behind(rest, give)
         other = swap(rest[:, :part], "core", 1)
         keep, give = gated_sums_in_steps(place, top_count, rest, other, *weights)
-        sums = [pair[: far.shape[0]], pair[far.shape[0] :], added(keep, swap(give, "core", 1))]
-        sums = [jnp.concatenate([o, s], 0) for o, s in zip(direct_sums, sums)]
-        sums = [own_sum, *with_fourth(*sums, first)]
+        fourth = added(keep, swap(give, "core", 1))
+        count = far.shape[0]
+        far_sums += with_fourth(pair[:count], pair[count:], fourth, first)
         metas = [held, near, rest]
     else:
-        sums = [own_sum]
-        for block, o in zip(near, direct_sums):
-            keep, give = sums_of(block, weights)
-            sums += [jnp.concatenate([o, chip_sums(keep, give)], 0)]
+        far_sums += [chip_sums(*sums_of(block, weights)) for block in near]
         metas = [held, *near]
     metas = [block[:, block.shape[1] - LANES :] for block in metas]
-    border = 2 * near_chips * rows
-    high = [block[border:] for block in sums]
-    low = [block[:border] for block in sums]
-    total = collected(high[0], received(high))
+    total = collected(far_sums[0], received(far_sums))
     blocks = [total[at : at + 2 * rows] for at in range(0, total.shape[0], 2 * rows)]
+    came = [swap(blocks[j - 1], "chip", j) for j in range(chips - 1, 0, -1)]
+    near_sums = behind(near_sums, came[-1])
+    came += received(near_sums)
     load = planned_load(metas, swap_slot, owners, per_device, top_count, blocks[0])
-    low = behind(low, total)
-    total = collected(low[0], received(low))
-    blocks = [total[at : at + 2 * rows] for at in range(0, border, 2 * rows)] + blocks
-    total = wide(blocks[0])
-    for j in range(1, chips):
-        total = total + wide(swap(blocks[j], "chip", j))
-    total = total.astype(jnp.bfloat16)
+    total = collected(near_sums[0], came)
     upper, lower = total[:rows], total[rows:]
     arrived = swap(jnp.where(first, lower, upper), "core", 1)
     kept = jnp.where(first, upper, lower)

time: 74.9 us -> 75.9 us (1.013)
  starting transfers between devices: 25.6 us -> 26.4 us
    ppermute x23 -> x24, waiting for transfers between devices: 14.6 us -> 16.3 us  [swap(): return row_major(lax.ppermute(row_major(value), axis, pairs))]
    ppermute x2, waiting for transfers between devices: 7.63 us -> 6.4 us  [cross(): return row_major(lax.ppermute(row_major(value), ('dp', 'core'), pairs))]
    ppermute x23 -> x24, starting transfers between devices: 22.5 us -> 23.2 us  [swap(): return row_major(lax.ppermute(row_major(value), axis, pairs))]
  transfers between devices with their start and end apart: 25 -> 26, of which waited for: 13 -> 13; matrix products, arithmetic and copies ran while one was open for 2% -> 2% of each run, Pallas kernels for 29% -> 28%
where the time goes in v16:
time: 75.9 us; the launch traced here: 75.7 us
  starting transfers between devices  26.4 us (35%)
  Pallas kernels  23.1 us (30%)
  waiting for transfers between devices  22.7 us (30%)
  other arithmetic  1.67 us (2%)
  between operations  0.92 us (1%)
  local copies, waits for them, and re-layouts  0.86 us (1%)
    ppermute x24, starting transfers between devices, swap(): return row_major(lax.ppermute(row_major(value), axis, pairs))  23.2 us
    ppermute x24, waiting for transfers between devices, swap(): return row_major(lax.ppermute(row_major(value), axis, pairs))  16.3 us
    pallas_call x5, Pallas kernels, call(): pl.pallas_call(kernel, in_specs=[pl.BlockSpec(memory_space=pltpu.SMEM)] +...  15.4 us
    ppermute x2, waiting for transfers between devices, cross(): return row_major(lax.ppermute(row_major(value), ('dp', 'core'), pairs))  6.4 us
    pallas_call x1, Pallas kernels, loaded(): pl.pallas_call(load_weight_kernel, in_specs=[pl.BlockSpec(memory_space=pl...  4.58 us
    ppermute x2, starting transfers between devices, cross(): return row_major(lax.ppermute(row_major(value), ('dp', 'core'), pairs))  3.17 us
    pallas_call x1, Pallas kernels, first_halves(): pl.pallas_call(first_kernel, in_specs=[pl.BlockSpec(memory_space=pltpu.SM...  1.56 us
  transfers between devices with their start and end apart: 26, of which 13 were waited for; matrix products, arithmetic and copies ran while one was open for 2% of the time, Pallas kernels for 28%

profile of v16, /device:TPU:0, one launch (start us, length us, event | category | flops | bytes accessed | tf_op | source)
XLA Modules:
  0.0 75.7 jit_solution(381970863191305522)
XLA Ops:
  0.7 1.6 %shard_map.77 = (bf16[12,2176]{1,0:T(8,128)(2,1)S(1)}, bf16[12,2176]{1,0:T(8,128)(2,1)S(1)}) custom-call(s32[2]{0:T(128)S(1)} %pad_add_fusion.place.refs_0_, bf16[12,4096]{1,0:T(8,128)(2,1)} %refs_0_.2, s32[8,12]{1,0:T(8,128)} %bitcast.8, f32[8,12]{1,0:T(8,128)} %bitcast.9), custom_call_target="tpu_custom_call" | custom-call | tf_op jit(solution)/shard_map/pallas_call | solution.py:261
  2.3 0.5 collective-permute-start
  2.8 0.9 %collective-permute-done = bf16[12,2176]{1,0:T(8,128)(2,1)S(1)} collective-permute-done((bf16[12,2176]{1,0:T(8,128)(2,1)S(1)}, bf16[12,2176]{1,0:T(8,128)(2,1)S(1)}, u32[]{:S(2)}, u32[]{:S(2)}) %collective-permute-start) | collective-permute-done | bytes 52256 | tf_op jit(solution)/shard_map/ppermute | solution.py:24
  3.8 2.9 %collective-permute-start.4 = (bf16[24,2176]{1,0:T(8,128)(2,1)S(1)}, bf16[24,2176]{1,0:T(8,128)(2,1)S(1)}, u32[]{:S(2)}, u32[]{:S(2)}) collective-permute-start(bf16[24,2176]{1,0:T(8,128)(2,1)S(1)} %get-tuple-element.47), channel_id=1, source_target_pairs={{0,8},{8,0},{16,24},{24,16},{1,9},{9,1},{17,25},{25,17},{2,10},{10... | collective-permute-start | bytes 313352 | tf_op jit(solution)/shard_map/ppermute | solution.py:24
  6.7 3.6 %collective-permute-start.3 = (bf16[24,2176]{1,0:T(8,128)(2,1)S(1)}, bf16[24,2176]{1,0:T(8,128)(2,1)S(1)}, u32[]{:S(2)}, u32[]{:S(2)}) collective-permute-start(bf16[24,2176]{1,0:T(8,128)(2,1)S(1)} %get-tuple-element.47), channel_id=1, source_target_pairs={{0,6},{2,4},{4,2},{6,0},{1,7},{3,5},{5,3},{7,1},{8,14},{10,12},{12... | collective-permute-start | bytes 313352 | tf_op jit(solution)/shard_map/ppermute | solution.py:24
  10.3 0.8 %collective-permute-start.1 = (bf16[24,2176]{1,0:T(8,128)(2,1)S(1)}, bf16[24,2176]{1,0:T(8,128)(2,1)S(1)}, u32[]{:S(2)}, u32[]{:S(2)}) collective-permute-start(bf16[24,2176]{1,0:T(8,128)(2,1)S(1)} %get-tuple-element.47), channel_id=1, source_target_pairs={{0,2},{2,0},{4,6},{6,4},{1,3},{3,1},{5,7},{7,5},{8,10},{10,8},{12,... | collective-permute-start | bytes 313352 | tf_op jit(solution)/shard_map/ppermute | solution.py:24
  11.1 1.5 %collective-permute-start.6 = (bf16[24,2176]{1,0:T(8,128)(2,1)S(1)}, bf16[24,2176]{1,0:T(8,128)(2,1)S(1)}, u32[]{:S(2)}, u32[]{:S(2)}) collective-permute-start(bf16[24,2176]{1,0:T(8,128)(2,1)S(1)} %get-tuple-element.47), channel_id=1, source_target_pairs={{0,24},{8,16},{16,8},{24,0},{1,25},{9,17},{17,9},{25,1},{2,26},{10... | collective-permute-start | bytes 313352 | tf_op jit(solution)/shard_map/ppermute | solution.py:24
  12.6 0.3 collective-permute-start.5
  12.8 4.6 %shard_map.78 = (bf16[2,4096,768]{2,1,0:T(8,128)(2,1)S(1)}, f32[8,128]{1,0:T(8,128)S(1)}) custom-call(bf16[2,4096,768]{2,1,0:T(8,128)(2,1)} %weight_ref.1, bf16[24,2176]{1,0:T(8,128)(2,1)S(1)} %collective-permute-done.4._), custom_call_target="tpu_custom_call" | custom-call | bytes 12582912 | tf_op jit(solution)/shard_map/pallas_call | solution.py:71
  17.4 1.7 %collective-permute-done.2 = bf16[24,2176]{1,0:T(8,128)(2,1)S(1)} collective-permute-done((bf16[24,2176]{1,0:T(8,128)(2,1)S(1)}, bf16[24,2176]{1,0:T(8,128)(2,1)S(1)}, u32[]{:S(2)}, u32[]{:S(2)}) %collective-permute-start.2) | collective-permute-done | bytes 104480 | tf_op jit(solution)/shard_map/ppermute | solution.py:24
  19.4 0.6 collective-permute-start.9
  20.0 1.5 %collective-permute-start.10 = (bf16[72,2176]{1,0:T(8,128)(2,1)S(1)}, bf16[72,2176]{1,0:T(8,128)(2,1)S(1)}, u32[]{:S(2)}, u32[]{:S(2)}) collective-permute-start(bf16[72,2176]{1,0:T(8,128)(2,1)S(1)} %get-tuple-element.63), channel_id=1, source_target_pairs={{0,16},{8,24},{16,0},{24,8},{1,17},{9,25},{17,1},{25,9},{2,18},{10... | collective-permute-start | bytes 940040 | tf_op jit(solution)/shard_map/ppermute | solution.py:24
  21.6 6.4 %shard_map.79 = (bf16[168,2048]{1,0:T(8,128)(2,1)S(1)}, bf16[168,2048]{1,0:T(8,128)(2,1)S(1)}, bf16[768,4096]{1,0:T(8,128)(2,1)S(1)}) custom-call(s32[2]{0:T(128)S(1)} %pad_add_fusion.place.refs_0_, bf16[168,2176]{1,0:T(8,128)(2,1)S(1)} %constant_dynamic-update-slice_fusion.refs_1_, bf16[168,2048]{1,0:T(8,128)(2,1)S(1)} %collective-permute-done.7.refs_2_, ...), custom_call_target="tpu_custom_call" | custom-call | flops 3170893824 | tf_op jit(solution)/shard_map/pallas_call | solution.py:162
  28.0 1.2 %collective-permute-done.9 = bf16[72,2176]{1,0:T(8,128)(2,1)S(1)} collective-permute-done((bf16[72,2176]{1,0:T(8,128)(2,1)S(1)}, bf16[72,2176]{1,0:T(8,128)(2,1)S(1)}, u32[]{:S(2)}, u32[]{:S(2)}) %collective-permute-start.9) | collective-permute-done | bytes 313376 | tf_op jit(solution)/shard_map/ppermute | solution.py:24
  29.2 0.3 collective-permute-done.10
  29.8 1.6 %collective-permute-start.13 = (bf16[72,2176]{1,0:T(8,128)(2,1)S(1)}, bf16[72,2176]{1,0:T(8,128)(2,1)S(1)}, u32[]{:S(2)}, u32[]{:S(2)}) collective-permute-start(bf16[72,2176]{1,0:T(8,128)(2,1)S(1)} %get-tuple-element.55), channel_id=1, source_target_pairs={{0,16},{1,9},{8,24},{9,1},{16,0},{17,25},{24,8},{25,17},{2,18},{3,... | collective-permute-start | bytes 940040 | tf_op jit(solution)/shard_map/ppermute | solution.py:36
  31.4 0.4 collective-permute-done.11.refs_2_
  31.8 3.6 %shard_map.80 = (bf16[144,2048]{1,0:T(8,128)(2,1)S(1)}, bf16[144,2048]{1,0:T(8,128)(2,1)S(1)}) custom-call(s32[2]{0:T(128)S(1)} %pad_add_fusion.place.refs_0_, bf16[144,2176]{1,0:T(8,128)(2,1)S(1)} %get-tuple-element.54.refs_1_, bf16[144,2048]{1,0:T(8,128)(2,1)S(1)} %collective-permute-done.11.refs_2_, ...), custom_call_target="tpu_custom_call" | custom-call | flops 2717908992 | tf_op jit(solution)/shard_map/pallas_call | solution.py:162
  35.4 1.4 %collective-permute-done.13.own.refs_1_ = bf16[72,2176]{1,0:T(8,128)(2,1)S(1)} collective-permute-done((bf16[72,2176]{1,0:T(8,128)(2,1)S(1)}, bf16[72,2176]{1,0:T(8,128)(2,1)S(1)}, u32[]{:S(2)}, u32[]{:S(2)}) %collective-permute-start.13) | collective-permute-done | bytes 313376 | tf_op jit(solution)/shard_map/ppermute | solution.py:36
  36.9 0.5 collective-permute-start.12
  37.4 1.8 %shard_map.81.refs_3_ = f32[2,72,768]{2,1,0:T(8,128)S(1)} custom-call(s32[2]{0:T(128)S(1)} %pad_add_fusion.place.refs_0_, bf16[72,2176]{1,0:T(8,128)(2,1)S(1)} %collective-permute-done.13.own.refs_1_, bf16[2,4096,768]{2,1,0:T(8,128)(2,1)S(1)} %get-tuple-element.30.refs_3_.up.refs_4_), custom_call_target="tpu_custom_call" | custom-call | flops 452984832 | tf_op jit(solution)/shard_map/pallas_call | solution.py:162
  39.1 2.4 %shard_map.82 = (bf16[72,2048]{1,0:T(8,128)(2,1)S(1)}, bf16[72,768]{1,0:T(8,128)(2,1)S(1)}) custom-call(s32[2]{0:T(128)S(1)} %pad_add_fusion.place.refs_0_, bf16[72,2176]{1,0:T(8,128)(2,1)S(1)} %collective-permute-done.13.own.refs_1_, bf16[72,2048]{1,0:T(8,128)(2,1)S(1)} %collective-permute-done.14.refs_2_, f32[2,72,768]{2,1,0:T(8,128)S(1)} %shard_map.81.refs_3_, ...), custom_call_target="tpu_custom_call" | custom-call | flops 679477248 | tf_op jit(solution)/shard_map/pallas_call | solution.py:162
  41.5 0.1 collective-permute-start.15
  41.6 0.4 collective-permute-start.8
  42.1 1.2 %shard_map.83.kept_ref = bf16[72,2048]{1,0:T(8,128)(2,1)S(1)} custom-call(s32[2]{0:T(128)S(1)} %pad_add_fusion.place.refs_0_, bf16[72,768]{1,0:T(8,128)(2,1)S(1)} %get-tuple-element.40.hidden, bf16[768,4096]{1,0:T(8,128)(2,1)S(1)} %get-tuple-element.36.refs_4_.refs_5_.down), custom_call_target="tpu_custom_call" | custom-call | flops 226492416 | tf_op jit(solution)/shard_map/pallas_call | solution.py:162
  43.4 1.6 %collective-permute-start.16 = (bf16[72,2048]{1,0:T(8,128)(2,1)S(1)}, bf16[72,2048]{1,0:T(8,128)(2,1)S(1)}, u32[]{:S(2)}, u32[]{:S(2)}) collective-permute-start(bf16[72,2048]{1,0:T(8,128)(2,1)S(1)} %shard_map.84), channel_id=1, source_target_pairs={{0,16},{1,9},{8,24},{9,1},{16,0},{17,25},{24,8},{25,17},{2,18},{3,... | collective-permute-start | bytes 884744 | tf_op jit(solution)/shard_map/ppermute | solution.py:36
  45.0 0.1 add_convert_fusion.1
  45.1 5.0 %collective-permute-done.16 = bf16[72,2048]{1,0:T(8,128)(2,1)S(1)} collective-permute-done((bf16[72,2048]{1,0:T(8,128)(2,1)S(1)}, bf16[72,2048]{1,0:T(8,128)(2,1)S(1)}, u32[]{:S(2)}, u32[]{:S(2)}) %collective-permute-start.16) | collective-permute-done | bytes 294944 | tf_op jit(solution)/shard_map/ppermute | solution.py:36
  50.2 0.2 fusion
  50.3 1.6 %collective-permute-start.17 = (bf16[72,2048]{1,0:T(8,128)(2,1)S(1)}, bf16[72,2048]{1,0:T(8,128)(2,1)S(1)}, u32[]{:S(2)}, u32[]{:S(2)}) collective-permute-start(bf16[72,2048]{1,0:T(8,128)(2,1)S(1)} %get-tuple-element.48), channel_id=1, source_target_pairs={{0,8},{8,0},{16,24},{24,16},{1,9},{9,1},{17,25},{25,17},{2,10},{10... | collective-permute-start | bytes 884744 | tf_op jit(solution)/shard_map/ppermute | solution.py:24
  51.9 1.5 %collective-permute-start.18 = (bf16[72,2048]{1,0:T(8,128)(2,1)S(1)}, bf16[72,2048]{1,0:T(8,128)(2,1)S(1)}, u32[]{:S(2)}, u32[]{:S(2)}) collective-permute-start(bf16[72,2048]{1,0:T(8,128)(2,1)S(1)} %get-tuple-element.49), channel_id=1, source_target_pairs={{0,16},{8,24},{16,0},{24,8},{1,17},{9,25},{17,1},{25,9},{2,18},{10... | collective-permute-start | bytes 884744 | tf_op jit(solution)/shard_map/ppermute | solution.py:24
  53.4 0.2 add_convert_fusion
  53.7 4.9 %collective-permute-done.17 = bf16[72,2048]{1,0:T(8,128)(2,1)S(1)} collective-permute-done((bf16[72,2048]{1,0:T(8,128)(2,1)S(1)}, bf16[72,2048]{1,0:T(8,128)(2,1)S(1)}, u32[]{:S(2)}, u32[]{:S(2)}) %collective-permute-start.17) | collective-permute-done | bytes 294944 | tf_op jit(solution)/shard_map/ppermute | solution.py:24
  58.5 1.2 %collective-permute-done.18 = bf16[72,2048]{1,0:T(8,128)(2,1)S(1)} collective-permute-done((bf16[72,2048]{1,0:T(8,128)(2,1)S(1)}, bf16[72,2048]{1,0:T(8,128)(2,1)S(1)}, u32[]{:S(2)}, u32[]{:S(2)}) %collective-permute-start.18) | collective-permute-done | bytes 294944 | tf_op jit(solution)/shard_map/ppermute | solution.py:24
  59.8 0.1 add_convert_fusion.2
  59.9 0.5 collective-permute-start.19
  60.4 2.4 %collective-permute-start.20 = (bf16[24,2048]{1,0:T(8,128)(2,1)S(1)}, bf16[24,2048]{1,0:T(8,128)(2,1)S(1)}, u32[]{:S(2)}, u32[]{:S(2)}) collective-permute-start(bf16[24,2048]{1,0:T(8,128)(2,1)S(1)} %get-tuple-element.56), channel_id=1, source_target_pairs={{0,6},{2,4},{4,2},{6,0},{1,7},{3,5},{5,3},{7,1},{8,14},{10,12},{12... | collective-permute-start | bytes 294920 | tf_op jit(solution)/shard_map/ppermute | solution.py:24
  62.8 0.8 collective-permute-start.21
  63.5 1.9 %collective-permute-done.19 = bf16[24,2048]{1,0:T(8,128)(2,1)S(1)} collective-permute-done((bf16[24,2048]{1,0:T(8,128)(2,1)S(1)}, bf16[24,2048]{1,0:T(8,128)(2,1)S(1)}, u32[]{:S(2)}, u32[]{:S(2)}) %collective-permute-start.19) | collective-permute-done | bytes 98336 | tf_op jit(solution)/shard_map/ppermute | solution.py:24
  65.4 1.1 %collective-permute-start.22 = (bf16[24,2048]{1,0:T(8,128)(2,1)S(1)}, bf16[24,2048]{1,0:T(8,128)(2,1)S(1)}, u32[]{:S(2)}, u32[]{:S(2)}) collective-permute-start(bf16[24,2048]{1,0:T(8,128)(2,1)S(1)} %get-tuple-element.43), channel_id=1, source_target_pairs={{0,8},{8,0},{16,24},{24,16},{1,9},{9,1},{17,25},{25,17},{2,10},{10... | collective-permute-start | bytes 294920 | tf_op jit(solution)/shard_map/ppermute | solution.py:24
  66.5 1.5 %collective-permute-start.23 = (bf16[24,2048]{1,0:T(8,128)(2,1)S(1)}, bf16[24,2048]{1,0:T(8,128)(2,1)S(1)}, u32[]{:S(2)}, u32[]{:S(2)}) collective-permute-start(bf16[24,2048]{1,0:T(8,128)(2,1)S(1)} %get-tuple-element.44), channel_id=1, source_target_pairs={{0,16},{8,24},{16,0},{24,8},{1,17},{9,25},{17,1},{25,9},{2,18},{10... | collective-permute-start | bytes 294920 | tf_op jit(solution)/shard_map/ppermute | solution.py:24
  68.0 0.9 %collective-permute-start.24 = (bf16[24,2048]{1,0:T(8,128)(2,1)S(1)}, bf16[24,2048]{1,0:T(8,128)(2,1)S(1)}, u32[]{:S(2)}, u32[]{:S(2)}) collective-permute-start(bf16[24,2048]{1,0:T(8,128)(2,1)S(1)} %get-tuple-element.45), channel_id=1, source_target_pairs={{0,24},{8,16},{16,8},{24,0},{1,25},{9,17},{17,9},{25,1},{2,26},{10... | collective-permute-start | bytes 294920 | tf_op jit(solution)/shard_map/ppermute | solution.py:24
  69.0 1.5 %shard_map.85 = f32[1,128]{1,0:T(1,128)S(1)} custom-call(s32[8]{0:T(128)S(1)} %copy-done, bf16[168,128]{1,0:T(8,128)(2,1)S(1)} %slice.90.refs_1_, bf16[144,128]{1,0:T(8,128)(2,1)S(1)} %slice.91.refs_2_, bf16[72,128]{1,0:T(8,128)(2,1)S(1)} %slice.74.refs_3_, bf16[24,2048]{1,0:T(8,128)(2,1)S(1)} %get-tuple-element.58.refs_4_), custom_call_target="tpu_custom_call" | custom-call | bytes 98304 | tf_op jit(solution)/shard_map/pallas_call | solution.py:329
  70.5 0.7 collective-permute-done.23
  71.1 2.4 %collective-permute-done.24 = bf16[24,2048]{1,0:T(8,128)(2,1)S(1)} collective-permute-done((bf16[24,2048]{1,0:T(8,128)(2,1)S(1)}, bf16[24,2048]{1,0:T(8,128)(2,1)S(1)}, u32[]{:S(2)}, u32[]{:S(2)}) %collective-permute-start.24) | collective-permute-done | bytes 98336 | tf_op jit(solution)/shard_map/ppermute | solution.py:24
  73.8 0.5 slice_bitcast_fusion
  74.3 0.7 collective-permute-done.25
  75.0 0.7 pad_maximum_fusion
  (43 shorter events, 1.1 us)
Async XLA Ops:
  2.3 1.4 %collective-permute-start = (bf16[12,2176]{1,0:T(8,128)(2,1)S(1)}, bf16[12,2176]{1,0:T(8,128)(2,1)S(1)}, u32[]{:S(2)}, u32[]{:S(2)}) collective-permute-start(bf16[12,2176]{1,0:T(8,128)(2,1)S(1)} %get-tuple-element.25), channel_id=1, source_target_pairs={{0,1},{1,0},{2,3},{3,2},{4,5},{5,4},{6,7},{7,6},{8,9},{9,8},{10,11... | collective-permute-start | bytes 156680 | tf_op jit(solution)/shard_map/ppermute | solution.py:24
  3.8 8.8 %collective-permute-start.4 = (bf16[24,2176]{1,0:T(8,128)(2,1)S(1)}, bf16[24,2176]{1,0:T(8,128)(2,1)S(1)}, u32[]{:S(2)}, u32[]{:S(2)}) collective-permute-start(bf16[24,2176]{1,0:T(8,128)(2,1)S(1)} %get-tuple-element.47), channel_id=1, source_target_pairs={{0,8},{8,0},{16,24},{24,16},{1,9},{9,1},{17,25},{25,17},{2,10},{10... | collective-permute-start | bytes 313352 | tf_op jit(solution)/shard_map/ppermute | solution.py:24
  6.7 10.8 %collective-permute-start.3 = (bf16[24,2176]{1,0:T(8,128)(2,1)S(1)}, bf16[24,2176]{1,0:T(8,128)(2,1)S(1)}, u32[]{:S(2)}, u32[]{:S(2)}) collective-permute-start(bf16[24,2176]{1,0:T(8,128)(2,1)S(1)} %get-tuple-element.47), channel_id=1, source_target_pairs={{0,6},{2,4},{4,2},{6,0},{1,7},{3,5},{5,3},{7,1},{8,14},{10,12},{12... | collective-permute-start | bytes 313352 | tf_op jit(solution)/shard_map/ppermute | solution.py:24
  10.3 8.8 %collective-permute-start.2 = (bf16[24,2176]{1,0:T(8,128)(2,1)S(1)}, bf16[24,2176]{1,0:T(8,128)(2,1)S(1)}, u32[]{:S(2)}, u32[]{:S(2)}) collective-permute-start(bf16[24,2176]{1,0:T(8,128)(2,1)S(1)} %get-tuple-element.47), channel_id=1, source_target_pairs={{0,4},{2,6},{4,0},{6,2},{1,5},{3,7},{5,1},{7,3},{8,12},{10,14},{12... | collective-permute-start | bytes 313352 | tf_op jit(solution)/shard_map/ppermute | solution.py:24
  10.3 8.8 %collective-permute-start.1 = (bf16[24,2176]{1,0:T(8,128)(2,1)S(1)}, bf16[24,2176]{1,0:T(8,128)(2,1)S(1)}, u32[]{:S(2)}, u32[]{:S(2)}) collective-permute-start(bf16[24,2176]{1,0:T(8,128)(2,1)S(1)} %get-tuple-element.47), channel_id=1, source_target_pairs={{0,2},{2,0},{4,6},{6,4},{1,3},{3,1},{5,7},{7,5},{8,10},{10,8},{12,... | collective-permute-start | bytes 313352 | tf_op jit(solution)/shard_map/ppermute | solution.py:24
  11.1 8.2 %collective-permute-start.6 = (bf16[24,2176]{1,0:T(8,128)(2,1)S(1)}, bf16[24,2176]{1,0:T(8,128)(2,1)S(1)}, u32[]{:S(2)}, u32[]{:S(2)}) collective-permute-start(bf16[24,2176]{1,0:T(8,128)(2,1)S(1)} %get-tuple-element.47), channel_id=1, source_target_pairs={{0,24},{8,16},{16,8},{24,0},{1,25},{9,17},{17,9},{25,1},{2,26},{10... | collective-permute-start | bytes 313352 | tf_op jit(solution)/shard_map/ppermute | solution.py:24
  12.6 6.7 %collective-permute-start.5 = (bf16[24,2176]{1,0:T(8,128)(2,1)S(1)}, bf16[24,2176]{1,0:T(8,128)(2,1)S(1)}, u32[]{:S(2)}, u32[]{:S(2)}) collective-permute-start(bf16[24,2176]{1,0:T(8,128)(2,1)S(1)} %get-tuple-element.47), channel_id=1, source_target_pairs={{0,16},{8,24},{16,0},{24,8},{1,17},{9,25},{17,1},{25,9},{2,18},{10... | collective-permute-start | bytes 313352 | tf_op jit(solution)/shard_map/ppermute | solution.py:24
  19.3 2.2 %collective-permute-start.7 = (bf16[168,2048]{1,0:T(8,128)(2,1)S(1)}, bf16[168,2048]{1,0:T(8,128)(2,1)S(1)}, u32[]{:S(2)}, u32[]{:S(2)}) collective-permute-start(bf16[168,2048]{1,0:T(8,128)(2,1)S(1)} %slice.76), channel_id=1, source_target_pairs={{0,1},{1,0},{2,3},{3,2},{4,5},{5,4},{6,7},{7,6},{8,9},{9,8},{10,11... | collective-permute-start | bytes 2064392 | tf_op jit(solution)/shard_map/ppermute | solution.py:24
  19.4 9.8 %collective-permute-start.9 = (bf16[72,2176]{1,0:T(8,128)(2,1)S(1)}, bf16[72,2176]{1,0:T(8,128)(2,1)S(1)}, u32[]{:S(2)}, u32[]{:S(2)}) collective-permute-start(bf16[72,2176]{1,0:T(8,128)(2,1)S(1)} %get-tuple-element.63), channel_id=1, source_target_pairs={{0,8},{8,0},{16,24},{24,16},{1,9},{9,1},{17,25},{25,17},{2,10},{10... | collective-permute-start | bytes 940040 | tf_op jit(solution)/shard_map/ppermute | solution.py:24
  20.0 9.5 %collective-permute-start.10 = (bf16[72,2176]{1,0:T(8,128)(2,1)S(1)}, bf16[72,2176]{1,0:T(8,128)(2,1)S(1)}, u32[]{:S(2)}, u32[]{:S(2)}) collective-permute-start(bf16[72,2176]{1,0:T(8,128)(2,1)S(1)} %get-tuple-element.63), channel_id=1, source_target_pairs={{0,16},{8,24},{16,0},{24,8},{1,17},{9,25},{17,1},{25,9},{2,18},{10... | collective-permute-start | bytes 940040 | tf_op jit(solution)/shard_map/ppermute | solution.py:24
  29.7 2.1 %collective-permute-start.11 = (bf16[144,2048]{1,0:T(8,128)(2,1)S(1)}, bf16[144,2048]{1,0:T(8,128)(2,1)S(1)}, u32[]{:S(2)}, u32[]{:S(2)}) collective-permute-start(bf16[144,2048]{1,0:T(8,128)(2,1)S(1)} %slice.82), channel_id=1, source_target_pairs={{0,1},{1,0},{2,3},{3,2},{4,5},{5,4},{6,7},{7,6},{8,9},{9,8},{10,11... | collective-permute-start | bytes 1769480 | tf_op jit(solution)/shard_map/ppermute | solution.py:24
  29.8 7.0 %collective-permute-start.13 = (bf16[72,2176]{1,0:T(8,128)(2,1)S(1)}, bf16[72,2176]{1,0:T(8,128)(2,1)S(1)}, u32[]{:S(2)}, u32[]{:S(2)}) collective-permute-start(bf16[72,2176]{1,0:T(8,128)(2,1)S(1)} %get-tuple-element.55), channel_id=1, source_target_pairs={{0,16},{1,9},{8,24},{9,1},{16,0},{17,25},{24,8},{25,17},{2,18},{3,... | collective-permute-start | bytes 940040 | tf_op jit(solution)/shard_map/ppermute | solution.py:36
  36.8 2.3 %collective-permute-start.14 = (bf16[72,2048]{1,0:T(8,128)(2,1)S(1)}, bf16[72,2048]{1,0:T(8,128)(2,1)S(1)}, u32[]{:S(2)}, u32[]{:S(2)}) collective-permute-start(bf16[72,2048]{1,0:T(8,128)(2,1)S(1)} %slice.65), channel_id=1, source_target_pairs={{0,1},{1,0},{2,3},{3,2},{4,5},{5,4},{6,7},{7,6},{8,9},{9,8},{10,11... | collective-permute-start | bytes 884744 | tf_op jit(solution)/shard_map/ppermute | solution.py:24
  36.9 8.1 %collective-permute-start.12 = (bf16[144,2048]{1,0:T(8,128)(2,1)S(1)}, bf16[144,2048]{1,0:T(8,128)(2,1)S(1)}, u32[]{:S(2)}, u32[]{:S(2)}) collective-permute-start(bf16[144,2048]{1,0:T(8,128)(2,1)S(1)} %get-tuple-element.38), channel_id=1, source_target_pairs={{0,1},{1,0},{2,3},{3,2},{4,5},{5,4},{6,7},{7,6},{8,9},{9,8},{10,11... | collective-permute-start | bytes 1769480 | tf_op jit(solution)/shard_map/ppermute | solution.py:24
  41.5 1.8 %collective-permute-start.15 = (bf16[72,2048]{1,0:T(8,128)(2,1)S(1)}, bf16[72,2048]{1,0:T(8,128)(2,1)S(1)}, u32[]{:S(2)}, u32[]{:S(2)}) collective-permute-start(bf16[72,2048]{1,0:T(8,128)(2,1)S(1)} %get-tuple-element.41), channel_id=1, source_target_pairs={{0,1},{1,0},{2,3},{3,2},{4,5},{5,4},{6,7},{7,6},{8,9},{9,8},{10,11... | collective-permute-start | bytes 884744 | tf_op jit(solution)/shard_map/ppermute | solution.py:24
  41.6 11.8 %collective-permute-start.8 = (bf16[168,2048]{1,0:T(8,128)(2,1)S(1)}, bf16[168,2048]{1,0:T(8,128)(2,1)S(1)}, u32[]{:S(2)}, u32[]{:S(2)}) collective-permute-start(bf16[168,2048]{1,0:T(8,128)(2,1)S(1)} %get-tuple-element.33), channel_id=1, source_target_pairs={{0,1},{1,0},{2,3},{3,2},{4,5},{5,4},{6,7},{7,6},{8,9},{9,8},{10,11... | collective-permute-start | bytes 2064392 | tf_op jit(solution)/shard_map/ppermute | solution.py:24
  43.4 6.8 %collective-permute-start.16 = (bf16[72,2048]{1,0:T(8,128)(2,1)S(1)}, bf16[72,2048]{1,0:T(8,128)(2,1)S(1)}, u32[]{:S(2)}, u32[]{:S(2)}) collective-permute-start(bf16[72,2048]{1,0:T(8,128)(2,1)S(1)} %shard_map.84), channel_id=1, source_target_pairs={{0,16},{1,9},{8,24},{9,1},{16,0},{17,25},{24,8},{25,17},{2,18},{3,... | collective-permute-start | bytes 884744 | tf_op jit(solution)/shard_map/ppermute | solution.py:36
  50.3 8.2 %collective-permute-start.17 = (bf16[72,2048]{1,0:T(8,128)(2,1)S(1)}, bf16[72,2048]{1,0:T(8,128)(2,1)S(1)}, u32[]{:S(2)}, u32[]{:S(2)}) collective-permute-start(bf16[72,2048]{1,0:T(8,128)(2,1)S(1)} %get-tuple-element.48), channel_id=1, source_target_pairs={{0,8},{8,0},{16,24},{24,16},{1,9},{9,1},{17,25},{25,17},{2,10},{10... | collective-permute-start | bytes 884744 | tf_op jit(solution)/shard_map/ppermute | solution.py:24
  51.9 7.9 %collective-permute-start.18 = (bf16[72,2048]{1,0:T(8,128)(2,1)S(1)}, bf16[72,2048]{1,0:T(8,128)(2,1)S(1)}, u32[]{:S(2)}, u32[]{:S(2)}) collective-permute-start(bf16[72,2048]{1,0:T(8,128)(2,1)S(1)} %get-tuple-element.49), channel_id=1, source_target_pairs={{0,16},{8,24},{16,0},{24,8},{1,17},{9,25},{17,1},{25,9},{2,18},{10... | collective-permute-start | bytes 884744 | tf_op jit(solution)/shard_map/ppermute | solution.py:24
  53.7 15.3 %copy-start = (s32[8]{0:T(128)S(1)}, s32[8]{0:T(128)}, u32[]{:S(2)}) copy-start(s32[8]{0:T(128)} %refs_0_.3) | copy-start | bytes 100
  59.9 5.5 %collective-permute-start.19 = (bf16[24,2048]{1,0:T(8,128)(2,1)S(1)}, bf16[24,2048]{1,0:T(8,128)(2,1)S(1)}, u32[]{:S(2)}, u32[]{:S(2)}) collective-permute-start(bf16[24,2048]{1,0:T(8,128)(2,1)S(1)} %get-tuple-element.58.refs_4_), channel_id=1, source_target_pairs={{0,2},{2,0},{4,6},{6,4},{1,3},{3,1},{5,7},{7,5},{8,10},{10,8},{12,... | collective-permute-start | bytes 294920 | tf_op jit(solution)/shard_map/ppermute | solution.py:24
  60.4 10.0 %collective-permute-start.20 = (bf16[24,2048]{1,0:T(8,128)(2,1)S(1)}, bf16[24,2048]{1,0:T(8,128)(2,1)S(1)}, u32[]{:S(2)}, u32[]{:S(2)}) collective-permute-start(bf16[24,2048]{1,0:T(8,128)(2,1)S(1)} %get-tuple-element.56), channel_id=1, source_target_pairs={{0,6},{2,4},{4,2},{6,0},{1,7},{3,5},{5,3},{7,1},{8,14},{10,12},{12... | collective-permute-start | bytes 294920 | tf_op jit(solution)/shard_map/ppermute | solution.py:24
  62.8 7.7 %collective-permute-start.21 = (bf16[24,2048]{1,0:T(8,128)(2,1)S(1)}, bf16[24,2048]{1,0:T(8,128)(2,1)S(1)}, u32[]{:S(2)}, u32[]{:S(2)}) collective-permute-start(bf16[24,2048]{1,0:T(8,128)(2,1)S(1)} %get-tuple-element.57), channel_id=1, source_target_pairs={{0,4},{2,6},{4,0},{6,2},{1,5},{3,7},{5,1},{7,3},{8,12},{10,14},{12... | collective-permute-start | bytes 294920 | tf_op jit(solution)/shard_map/ppermute | solution.py:24
  65.4 5.0 %collective-permute-start.22 = (bf16[24,2048]{1,0:T(8,128)(2,1)S(1)}, bf16[24,2048]{1,0:T(8,128)(2,1)S(1)}, u32[]{:S(2)}, u32[]{:S(2)}) collective-permute-start(bf16[24,2048]{1,0:T(8,128)(2,1)S(1)} %get-tuple-element.43), channel_id=1, source_target_pairs={{0,8},{8,0},{16,24},{24,16},{1,9},{9,1},{17,25},{25,17},{2,10},{10... | collective-permute-start | bytes 294920 | tf_op jit(solution)/shard_map/ppermute | solution.py:24
  66.5 4.6 %collective-permute-start.23 = (bf16[24,2048]{1,0:T(8,128)(2,1)S(1)}, bf16[24,2048]{1,0:T(8,128)(2,1)S(1)}, u32[]{:S(2)}, u32[]{:S(2)}) collective-permute-start(bf16[24,2048]{1,0:T(8,128)(2,1)S(1)} %get-tuple-element.44), channel_id=1, source_target_pairs={{0,16},{8,24},{16,0},{24,8},{1,17},{9,25},{17,1},{25,9},{2,18},{10... | collective-permute-start | bytes 294920 | tf_op jit(solution)/shard_map/ppermute | solution.py:24
  68.0 5.5 %collective-permute-start.24 = (bf16[24,2048]{1,0:T(8,128)(2,1)S(1)}, bf16[24,2048]{1,0:T(8,128)(2,1)S(1)}, u32[]{:S(2)}, u32[]{:S(2)}) collective-permute-start(bf16[24,2048]{1,0:T(8,128)(2,1)S(1)} %get-tuple-element.45), channel_id=1, source_target_pairs={{0,24},{8,16},{16,8},{24,0},{1,25},{9,17},{17,9},{25,1},{2,26},{10... | collective-permute-start | bytes 294920 | tf_op jit(solution)/shard_map/ppermute | solution.py:24
  73.7 1.3 %collective-permute-start.25 = (bf16[12,2048]{1,0:T(8,128)(2,1)S(1)}, bf16[12,2048]{1,0:T(8,128)(2,1)S(1)}, u32[]{:S(2)}, u32[]{:S(2)}) collective-permute-start(bf16[12,2048]{1,0:T(8,128)(2,1)S(1)} %broadcast_select_fusion.5), channel_id=1, source_target_pairs={{0,1},{1,0},{2,3},{3,2},{4,5},{5,4},{6,7},{7,6},{8,9},{9,8},{10,11... | collective-permute-start | bytes 147464 | tf_op jit(solution)/shard_map/ppermute | solution.py:24

commit v17 on v16

--- a/solution.py
+++ b/solution.py
@@ -42,14 +42,6 @@
 
 def wide(value):
     return value.astype(jnp.float32)
-
-
-def with_fourth(one, two, fourth, first):
-    came = wide(cross(fourth))
-    return (
-        jnp.where(first, wide(one) + came, wide(one)).astype(jnp.bfloat16),
-        jnp.where(first, wide(two), wide(two) + came).astype(jnp.bfloat16),
-    )
 
 
 def received(blocks):
@@ -391,29 +383,35 @@
         first_sum[low : low + 2 * rows] for low in range(border, first_sum.shape[0], 2 * rows)
     ]
     far_sums = [first_sum[2 * rows : border]]
+
+    def parts(block):
+        return [block[low : low + 2 * rows] for low in range(0, block.shape[0], 2 * rows)]
+
+    def along_chips(blocks):
+        return [swap(blocks[j - 1], "chip", j) for j in range(chips - 1, 0, -1)]
+
     if groups == 4:
         rest = cross(jnp.where(first, near[0], near[1]))
         near = row_major(jnp.concatenate(near, 0))
         keep, give = sums_of(near, weights)
-        pair = chip_sums(keep, give)
+        far_sums += [*jnp.split(chip_sums(keep, give), 2)]
+        whole = [jnp.concatenate(pair, 0) for pair in zip(near_sums, far_sums)]
         rest = behind(rest, give)
-        other = swap(rest[:, :part], "core", 1)
+        other = behind(swap(rest[:, :part], "core", 1), whole[1:3])
         keep, give = gated_sums_in_steps(place, top_count, rest, other, *weights)
-        fourth = added(keep, swap(give, "core", 1))
-        count = far.shape[0]
-        far_sums += with_fourth(pair[:count], pair[count:], fourth, first)
+        fourth = parts(added(keep, swap(give, "core", 1)))
+        fourth = collected(near_sums[3], along_chips(fourth))
+        came = [swap(fourth, "dp", 3)]
         metas = [held, near, rest]
     else:
         far_sums += [chip_sums(*sums_of(block, weights)) for block in near]
+        whole = [jnp.concatenate(pair, 0) for pair in zip(near_sums, far_sums)]
+        came = []
         metas = [held, *near]
     metas = [block[:, block.shape[1] - LANES :] for block in metas]
-    total = collected(far_sums[0], received(far_sums))
-    blocks = [total[at : at + 2 * rows] for at in range(0, total.shape[0], 2 * rows)]
-    came = [swap(blocks[j - 1], "chip", j) for j in range(chips - 1, 0, -1)]
-    near_sums = behind(near_sums, came[-1])
-    came += received(near_sums)
-    load = planned_load(metas, swap_slot, owners, per_device, top_count, blocks[0])
-    total = collected(near_sums[0], came)
+    total = parts(collected(whole[0], received(whole)))
+    load = planned_load(metas, swap_slot, owners, per_device, top_count, total[0])
+    total = collected(total[0], along_chips(total[1:]) + came)
     upper, lower = total[:rows], total[rows:]
     arrived = swap(jnp.where(first, lower, upper), "core", 1)
     kept = jnp.where(first, upper, lower)

time: 75.9 us -> 73.3 us (0.966)
  waiting for transfers between devices: 22.7 us -> 17.8 us
  starting transfers between devices: 26.4 us -> 28.7 us
    ppermute x2 -> x1, waiting for transfers between devices: 6.4 us -> 1.58 us  [cross(): return row_major(lax.ppermute(row_major(value), ('dp', 'core'), pairs))]
    ppermute x24 -> x25, starting transfers between devices: 23.2 us -> 27.2 us  [swap(): return row_major(lax.ppermute(row_major(value), axis, pairs))]
    ppermute x2 -> x1, starting transfers between devices: 3.17 us -> 1.52 us  [cross(): return row_major(lax.ppermute(row_major(value), ('dp', 'core'), pairs))]
    ppermute x24 -> x25, waiting for transfers between devices: 16.3 us -> 16.2 us  [swap(): return row_major(lax.ppermute(row_major(value), axis, pairs))]
  transfers between devices with their start and end apart: 26 -> 26, of which waited for: 13 -> 13; matrix products, arithmetic and copies ran while one was open for 2% -> 2% of each run, Pallas kernels for 28% -> 26%
where the time goes in v17:
time: 73.3 us; the launch traced here: 73.1 us
  starting transfers between devices  28.7 us (39%)
  Pallas kernels  23.1 us (32%)
  waiting for transfers between devices  17.8 us (24%)
  other arithmetic  1.64 us (2%)
  between operations  0.96 us (1%)
  local copies, waits for them, and re-layouts  0.91 us (1%)
    ppermute x25, starting transfers between devices, swap(): return row_major(lax.ppermute(row_major(value), axis, pairs))  27.2 us
    ppermute x25, waiting for transfers between devices, swap(): return row_major(lax.ppermute(row_major(value), axis, pairs))  16.2 us
    pallas_call x5, Pallas kernels, call(): pl.pallas_call(kernel, in_specs=[pl.BlockSpec(memory_space=pltpu.SMEM)] +...  15.4 us
    pallas_call x1, Pallas kernels, loaded(): pl.pallas_call(load_weight_kernel, in_specs=[pl.BlockSpec(memory_space=pl...  4.58 us
    ppermute x1, waiting for transfers between devices, cross(): return row_major(lax.ppermute(row_major(value), ('dp', 'core'), pairs))  1.58 us
    pallas_call x1, Pallas kernels, first_halves(): pl.pallas_call(first_kernel, in_specs=[pl.BlockSpec(memory_space=pltpu.SM...  1.56 us
    ppermute x1, starting transfers between devices, cross(): return row_major(lax.ppermute(row_major(value), ('dp', 'core'), pairs))  1.52 us
    pallas_call x1, Pallas kernels, planned_load(): pl.pallas_call(lambda *refs: load_kernel(layout, *refs), in_specs=[pl.Blo...  1.47 us
  transfers between devices with their start and end apart: 26, of which 13 were waited for; matrix products, arithmetic and copies ran while one was open for 2% of the time, Pallas kernels for 26%

profile of v17, /device:TPU:0, one launch (start us, length us, event | category | flops | bytes accessed | tf_op | source)
XLA Modules:
  0.0 73.1 jit_solution(312167787763130048)
XLA Ops:
  0.6 0.1 pad_add_fusion.place.refs_0_
  0.7 1.6 %shard_map.77 = (bf16[12,2176]{1,0:T(8,128)(2,1)S(1)}, bf16[12,2176]{1,0:T(8,128)(2,1)S(1)}) custom-call(s32[2]{0:T(128)S(1)} %pad_add_fusion.place.refs_0_, bf16[12,4096]{1,0:T(8,128)(2,1)} %refs_0_.2, s32[8,12]{1,0:T(8,128)} %bitcast.8, f32[8,12]{1,0:T(8,128)} %bitcast.9), custom_call_target="tpu_custom_call" | custom-call | tf_op jit(solution)/shard_map/pallas_call | solution.py:253
  2.3 0.5 collective-permute-start
  2.8 0.9 %collective-permute-done = bf16[12,2176]{1,0:T(8,128)(2,1)S(1)} collective-permute-done((bf16[12,2176]{1,0:T(8,128)(2,1)S(1)}, bf16[12,2176]{1,0:T(8,128)(2,1)S(1)}, u32[]{:S(2)}, u32[]{:S(2)}) %collective-permute-start) | collective-permute-done | bytes 52256 | tf_op jit(solution)/shard_map/ppermute | solution.py:24
  3.8 2.9 %collective-permute-start.4 = (bf16[24,2176]{1,0:T(8,128)(2,1)S(1)}, bf16[24,2176]{1,0:T(8,128)(2,1)S(1)}, u32[]{:S(2)}, u32[]{:S(2)}) collective-permute-start(bf16[24,2176]{1,0:T(8,128)(2,1)S(1)} %get-tuple-element.41), channel_id=1, source_target_pairs={{0,8},{8,0},{16,24},{24,16},{1,9},{9,1},{17,25},{25,17},{2,10},{10... | collective-permute-start | bytes 313352 | tf_op jit(solution)/shard_map/ppermute | solution.py:24
  6.7 3.6 %collective-permute-start.3 = (bf16[24,2176]{1,0:T(8,128)(2,1)S(1)}, bf16[24,2176]{1,0:T(8,128)(2,1)S(1)}, u32[]{:S(2)}, u32[]{:S(2)}) collective-permute-start(bf16[24,2176]{1,0:T(8,128)(2,1)S(1)} %get-tuple-element.41), channel_id=1, source_target_pairs={{0,6},{2,4},{4,2},{6,0},{1,7},{3,5},{5,3},{7,1},{8,14},{10,12},{12... | collective-permute-start | bytes 313352 | tf_op jit(solution)/shard_map/ppermute | solution.py:24
  10.3 0.8 %collective-permute-start.1 = (bf16[24,2176]{1,0:T(8,128)(2,1)S(1)}, bf16[24,2176]{1,0:T(8,128)(2,1)S(1)}, u32[]{:S(2)}, u32[]{:S(2)}) collective-permute-start(bf16[24,2176]{1,0:T(8,128)(2,1)S(1)} %get-tuple-element.41), channel_id=1, source_target_pairs={{0,2},{2,0},{4,6},{6,4},{1,3},{3,1},{5,7},{7,5},{8,10},{10,8},{12,... | collective-permute-start | bytes 313352 | tf_op jit(solution)/shard_map/ppermute | solution.py:24
  11.1 1.5 %collective-permute-start.6 = (bf16[24,2176]{1,0:T(8,128)(2,1)S(1)}, bf16[24,2176]{1,0:T(8,128)(2,1)S(1)}, u32[]{:S(2)}, u32[]{:S(2)}) collective-permute-start(bf16[24,2176]{1,0:T(8,128)(2,1)S(1)} %get-tuple-element.41), channel_id=1, source_target_pairs={{0,24},{8,16},{16,8},{24,0},{1,25},{9,17},{17,9},{25,1},{2,26},{10... | collective-permute-start | bytes 313352 | tf_op jit(solution)/shard_map/ppermute | solution.py:24
  12.6 0.3 collective-permute-start.5
  12.8 4.6 %shard_map.78 = (bf16[2,4096,768]{2,1,0:T(8,128)(2,1)S(1)}, f32[8,128]{1,0:T(8,128)S(1)}) custom-call(bf16[2,4096,768]{2,1,0:T(8,128)(2,1)} %weight_ref.1, bf16[24,2176]{1,0:T(8,128)(2,1)S(1)} %collective-permute-done.4._), custom_call_target="tpu_custom_call" | custom-call | bytes 12582912 | tf_op jit(solution)/shard_map/pallas_call | solution.py:63
  17.4 1.7 %collective-permute-done.2 = bf16[24,2176]{1,0:T(8,128)(2,1)S(1)} collective-permute-done((bf16[24,2176]{1,0:T(8,128)(2,1)S(1)}, bf16[24,2176]{1,0:T(8,128)(2,1)S(1)}, u32[]{:S(2)}, u32[]{:S(2)}) %collective-permute-start.2) | collective-permute-done | bytes 104480 | tf_op jit(solution)/shard_map/ppermute | solution.py:24
  19.3 0.1 collective-permute-start.7
  19.4 0.6 collective-permute-start.9
  20.0 1.5 %collective-permute-start.10 = (bf16[72,2176]{1,0:T(8,128)(2,1)S(1)}, bf16[72,2176]{1,0:T(8,128)(2,1)S(1)}, u32[]{:S(2)}, u32[]{:S(2)}) collective-permute-start(bf16[72,2176]{1,0:T(8,128)(2,1)S(1)} %get-tuple-element.60), channel_id=1, source_target_pairs={{0,16},{8,24},{16,0},{24,8},{1,17},{9,25},{17,1},{25,9},{2,18},{10... | collective-permute-start | bytes 940040 | tf_op jit(solution)/shard_map/ppermute | solution.py:24
  21.6 6.4 %shard_map.79 = (bf16[168,2048]{1,0:T(8,128)(2,1)S(1)}, bf16[168,2048]{1,0:T(8,128)(2,1)S(1)}, bf16[768,4096]{1,0:T(8,128)(2,1)S(1)}) custom-call(s32[2]{0:T(128)S(1)} %pad_add_fusion.place.refs_0_, bf16[168,2176]{1,0:T(8,128)(2,1)S(1)} %constant_dynamic-update-slice_fusion.refs_1_, bf16[168,2048]{1,0:T(8,128)(2,1)S(1)} %collective-permute-done.7.refs_2_, ...), custom_call_target="tpu_custom_call" | custom-call | flops 3170893824 | tf_op jit(solution)/shard_map/pallas_call | solution.py:154
  28.0 1.2 %collective-permute-done.9 = bf16[72,2176]{1,0:T(8,128)(2,1)S(1)} collective-permute-done((bf16[72,2176]{1,0:T(8,128)(2,1)S(1)}, bf16[72,2176]{1,0:T(8,128)(2,1)S(1)}, u32[]{:S(2)}, u32[]{:S(2)}) %collective-permute-start.9) | collective-permute-done | bytes 313376 | tf_op jit(solution)/shard_map/ppermute | solution.py:24
  29.2 0.3 collective-permute-done.10
  29.5 0.1 constant_dynamic-update-slice_fusion.10
  29.8 0.5 collective-permute-start.8
  30.3 1.5 %collective-permute-start.18 = (bf16[72,2176]{1,0:T(8,128)(2,1)S(1)}, bf16[72,2176]{1,0:T(8,128)(2,1)S(1)}, u32[]{:S(2)}, u32[]{:S(2)}) collective-permute-start(bf16[72,2176]{1,0:T(8,128)(2,1)S(1)} %get-tuple-element.51), channel_id=1, source_target_pairs={{0,16},{1,9},{8,24},{9,1},{16,0},{17,25},{24,8},{25,17},{2,18},{3,... | collective-permute-start | bytes 940040 | tf_op jit(solution)/shard_map/ppermute | solution.py:36
  31.8 3.6 %shard_map.80 = (bf16[144,2048]{1,0:T(8,128)(2,1)S(1)}, bf16[144,2048]{1,0:T(8,128)(2,1)S(1)}) custom-call(s32[2]{0:T(128)S(1)} %pad_add_fusion.place.refs_0_, bf16[144,2176]{1,0:T(8,128)(2,1)S(1)} %get-tuple-element.50.refs_1_, bf16[144,2048]{1,0:T(8,128)(2,1)S(1)} %collective-permute-done.11.refs_2_, ...), custom_call_target="tpu_custom_call" | custom-call | flops 2717908992 | tf_op jit(solution)/shard_map/pallas_call | solution.py:154
  35.4 0.2 collective-permute-start.12
  35.6 1.6 %collective-permute-done.18.own.refs_1_ = bf16[72,2176]{1,0:T(8,128)(2,1)S(1)} collective-permute-done((bf16[72,2176]{1,0:T(8,128)(2,1)S(1)}, bf16[72,2176]{1,0:T(8,128)(2,1)S(1)}, u32[]{:S(2)}, u32[]{:S(2)}) %collective-permute-start.18) | collective-permute-done | bytes 313376 | tf_op jit(solution)/shard_map/ppermute | solution.py:36
  37.3 1.8 %shard_map.81.refs_3_ = f32[2,72,768]{2,1,0:T(8,128)S(1)} custom-call(s32[2]{0:T(128)S(1)} %pad_add_fusion.place.refs_0_, bf16[72,2176]{1,0:T(8,128)(2,1)S(1)} %collective-permute-done.18.own.refs_1_, bf16[2,4096,768]{2,1,0:T(8,128)(2,1)S(1)} %get-tuple-element.27.refs_3_.up.refs_4_), custom_call_target="tpu_custom_call" | custom-call | flops 452984832 | tf_op jit(solution)/shard_map/pallas_call | solution.py:154
  39.1 0.2 add_convert_fusion
  39.3 0.1 add_convert_fusion.1
  39.6 2.4 %shard_map.82 = (bf16[72,2048]{1,0:T(8,128)(2,1)S(1)}, bf16[72,768]{1,0:T(8,128)(2,1)S(1)}) custom-call(s32[2]{0:T(128)S(1)} %pad_add_fusion.place.refs_0_, bf16[72,2176]{1,0:T(8,128)(2,1)S(1)} %collective-permute-done.18.own.refs_1_, bf16[72,2048]{1,0:T(8,128)(2,1)S(1)} %collective-permute-done.19.refs_2_, f32[2,72,768]{2,1,0:T(8,128)S(1)} %shard_map.81.refs_3_, ...), custom_call_target="tpu_custom_call" | custom-call | flops 679477248 | tf_op jit(solution)/shard_map/pallas_call | solution.py:154
  42.0 0.6 collective-permute-start.20
  42.5 1.2 %shard_map.83.kept_ref = bf16[72,2048]{1,0:T(8,128)(2,1)S(1)} custom-call(s32[2]{0:T(128)S(1)} %pad_add_fusion.place.refs_0_, bf16[72,768]{1,0:T(8,128)(2,1)S(1)} %get-tuple-element.38.hidden, bf16[768,4096]{1,0:T(8,128)(2,1)S(1)} %get-tuple-element.33.refs_4_.refs_5_.down), custom_call_target="tpu_custom_call" | custom-call | flops 226492416 | tf_op jit(solution)/shard_map/pallas_call | solution.py:154
  43.8 0.1 shard_map.84
  43.9 3.2 %collective-permute-start.21 = (bf16[24,2048]{1,0:T(8,128)(2,1)S(1)}, bf16[24,2048]{1,0:T(8,128)(2,1)S(1)}, u32[]{:S(2)}, u32[]{:S(2)}) collective-permute-start(bf16[24,2048]{1,0:T(8,128)(2,1)S(1)} %get-tuple-element.52), channel_id=1, source_target_pairs={{0,6},{2,4},{4,2},{6,0},{1,7},{3,5},{5,3},{7,1},{8,14},{10,12},{12... | collective-permute-start | bytes 294920 | tf_op jit(solution)/shard_map/ppermute | solution.py:24
  47.1 1.2 %collective-permute-start.22 = (bf16[24,2048]{1,0:T(8,128)(2,1)S(1)}, bf16[24,2048]{1,0:T(8,128)(2,1)S(1)}, u32[]{:S(2)}, u32[]{:S(2)}) collective-permute-start(bf16[24,2048]{1,0:T(8,128)(2,1)S(1)} %get-tuple-element.54), channel_id=1, source_target_pairs={{0,4},{2,6},{4,0},{6,2},{1,5},{3,7},{5,1},{7,3},{8,12},{10,14},{12... | collective-permute-start | bytes 294920 | tf_op jit(solution)/shard_map/ppermute | solution.py:24
  48.3 1.5 %collective-permute-start.13 = (bf16[96,2048]{1,0:T(8,128)(2,1)S(1)}, bf16[96,2048]{1,0:T(8,128)(2,1)S(1)}, u32[]{:S(2)}, u32[]{:S(2)}) collective-permute-start(bf16[96,2048]{1,0:T(8,128)(2,1)S(1)} %pad_maximum_fusion), channel_id=1, source_target_pairs={{0,8},{8,0},{16,24},{24,16},{1,9},{9,1},{17,25},{25,17},{2,10},{10... | collective-permute-start | bytes 1179656 | tf_op jit(solution)/shard_map/ppermute | solution.py:24
  49.8 1.5 %collective-permute-start.14 = (bf16[96,2048]{1,0:T(8,128)(2,1)S(1)}, bf16[96,2048]{1,0:T(8,128)(2,1)S(1)}, u32[]{:S(2)}, u32[]{:S(2)}) collective-permute-start(bf16[96,2048]{1,0:T(8,128)(2,1)S(1)} %pad_maximum_fusion.1), channel_id=1, source_target_pairs={{0,16},{8,24},{16,0},{24,8},{1,17},{9,25},{17,1},{25,9},{2,18},{10... | collective-permute-start | bytes 1179656 | tf_op jit(solution)/shard_map/ppermute | solution.py:24
  51.4 3.3 %collective-permute-done.23 = bf16[24,2048]{1,0:T(8,128)(2,1)S(1)} collective-permute-done((bf16[24,2048]{1,0:T(8,128)(2,1)S(1)}, bf16[24,2048]{1,0:T(8,128)(2,1)S(1)}, u32[]{:S(2)}, u32[]{:S(2)}) %collective-permute-start.23) | collective-permute-done | bytes 98336 | tf_op jit(solution)/shard_map/ppermute | solution.py:24
  54.7 0.8 %collective-permute-done.22 = bf16[24,2048]{1,0:T(8,128)(2,1)S(1)} collective-permute-done((bf16[24,2048]{1,0:T(8,128)(2,1)S(1)}, bf16[24,2048]{1,0:T(8,128)(2,1)S(1)}, u32[]{:S(2)}, u32[]{:S(2)}) %collective-permute-start.22) | collective-permute-done | bytes 98336 | tf_op jit(solution)/shard_map/ppermute | solution.py:24
  55.6 2.1 %collective-permute-start.24 = (bf16[24,2048]{1,0:T(8,128)(2,1)S(1)}, bf16[24,2048]{1,0:T(8,128)(2,1)S(1)}, u32[]{:S(2)}, u32[]{:S(2)}) collective-permute-start(bf16[24,2048]{1,0:T(8,128)(2,1)S(1)} %add_convert_fusion.4), channel_id=1, source_target_pairs={{0,24},{8,16},{16,8},{24,0},{1,25},{9,17},{17,9},{25,1},{2,26},{10... | collective-permute-start | bytes 294920 | tf_op jit(solution)/shard_map/ppermute | solution.py:24
  57.7 1.2 %collective-permute-done.13 = bf16[96,2048]{1,0:T(8,128)(2,1)S(1)} collective-permute-done((bf16[96,2048]{1,0:T(8,128)(2,1)S(1)}, bf16[96,2048]{1,0:T(8,128)(2,1)S(1)}, u32[]{:S(2)}, u32[]{:S(2)}) %collective-permute-start.13) | collective-permute-done | bytes 393248 | tf_op jit(solution)/shard_map/ppermute | solution.py:24
  58.9 3.3 %collective-permute-done.14 = bf16[96,2048]{1,0:T(8,128)(2,1)S(1)} collective-permute-done((bf16[96,2048]{1,0:T(8,128)(2,1)S(1)}, bf16[96,2048]{1,0:T(8,128)(2,1)S(1)}, u32[]{:S(2)}, u32[]{:S(2)}) %collective-permute-start.14) | collective-permute-done | bytes 393248 | tf_op jit(solution)/shard_map/ppermute | solution.py:24
  62.2 0.1 add_convert_fusion.2
  62.4 2.1 %collective-permute-start.16 = (bf16[24,2048]{1,0:T(8,128)(2,1)S(1)}, bf16[24,2048]{1,0:T(8,128)(2,1)S(1)}, u32[]{:S(2)}, u32[]{:S(2)}) collective-permute-start(bf16[24,2048]{1,0:T(8,128)(2,1)S(1)} %get-tuple-element.48), channel_id=1, source_target_pairs={{0,4},{2,6},{4,0},{6,2},{1,5},{3,7},{5,1},{7,3},{8,12},{10,14},{12... | collective-permute-start | bytes 294920 | tf_op jit(solution)/shard_map/ppermute | solution.py:24
  64.5 2.3 %collective-permute-start.15 = (bf16[24,2048]{1,0:T(8,128)(2,1)S(1)}, bf16[24,2048]{1,0:T(8,128)(2,1)S(1)}, u32[]{:S(2)}, u32[]{:S(2)}) collective-permute-start(bf16[24,2048]{1,0:T(8,128)(2,1)S(1)} %get-tuple-element.49), channel_id=1, source_target_pairs={{0,6},{2,4},{4,2},{6,0},{1,7},{3,5},{5,3},{7,1},{8,14},{10,12},{12... | collective-permute-start | bytes 294920 | tf_op jit(solution)/shard_map/ppermute | solution.py:24
  66.8 1.5 %shard_map.85 = f32[1,128]{1,0:T(1,128)S(1)} custom-call(s32[8]{0:T(128)S(1)} %copy-done, bf16[168,128]{1,0:T(8,128)(2,1)S(1)} %slice.93.refs_1_, bf16[144,128]{1,0:T(8,128)(2,1)S(1)} %slice.94.refs_2_, bf16[72,128]{1,0:T(8,128)(2,1)S(1)} %slice.77.refs_3_, bf16[24,2048]{1,0:T(8,128)(2,1)S(1)} %get-tuple-element.46.refs_4_), custom_call_target="tpu_custom_call" | custom-call | bytes 98304 | tf_op jit(solution)/shard_map/pallas_call | solution.py:321
  68.3 0.4 collective-permute-done.17
  68.8 2.3 %collective-permute-done.15 = bf16[24,2048]{1,0:T(8,128)(2,1)S(1)} collective-permute-done((bf16[24,2048]{1,0:T(8,128)(2,1)S(1)}, bf16[24,2048]{1,0:T(8,128)(2,1)S(1)}, u32[]{:S(2)}, u32[]{:S(2)}) %collective-permute-start.15) | collective-permute-done | bytes 98336 | tf_op jit(solution)/shard_map/ppermute | solution.py:24
  71.2 0.5 slice_bitcast_fusion
  71.7 0.7 collective-permute-done.25
  72.5 0.7 pad_maximum_fusion.2
  (47 shorter events, 1.1 us)
Async XLA Ops:
  2.3 1.4 %collective-permute-start = (bf16[12,2176]{1,0:T(8,128)(2,1)S(1)}, bf16[12,2176]{1,0:T(8,128)(2,1)S(1)}, u32[]{:S(2)}, u32[]{:S(2)}) collective-permute-start(bf16[12,2176]{1,0:T(8,128)(2,1)S(1)} %get-tuple-element.22), channel_id=1, source_target_pairs={{0,1},{1,0},{2,3},{3,2},{4,5},{5,4},{6,7},{7,6},{8,9},{9,8},{10,11... | collective-permute-start | bytes 156680 | tf_op jit(solution)/shard_map/ppermute | solution.py:24
  3.8 8.8 %collective-permute-start.4 = (bf16[24,2176]{1,0:T(8,128)(2,1)S(1)}, bf16[24,2176]{1,0:T(8,128)(2,1)S(1)}, u32[]{:S(2)}, u32[]{:S(2)}) collective-permute-start(bf16[24,2176]{1,0:T(8,128)(2,1)S(1)} %get-tuple-element.41), channel_id=1, source_target_pairs={{0,8},{8,0},{16,24},{24,16},{1,9},{9,1},{17,25},{25,17},{2,10},{10... | collective-permute-start | bytes 313352 | tf_op jit(solution)/shard_map/ppermute | solution.py:24
  6.7 10.8 %collective-permute-start.3 = (bf16[24,2176]{1,0:T(8,128)(2,1)S(1)}, bf16[24,2176]{1,0:T(8,128)(2,1)S(1)}, u32[]{:S(2)}, u32[]{:S(2)}) collective-permute-start(bf16[24,2176]{1,0:T(8,128)(2,1)S(1)} %get-tuple-element.41), channel_id=1, source_target_pairs={{0,6},{2,4},{4,2},{6,0},{1,7},{3,5},{5,3},{7,1},{8,14},{10,12},{12... | collective-permute-start | bytes 313352 | tf_op jit(solution)/shard_map/ppermute | solution.py:24
  10.3 8.8 %collective-permute-start.2 = (bf16[24,2176]{1,0:T(8,128)(2,1)S(1)}, bf16[24,2176]{1,0:T(8,128)(2,1)S(1)}, u32[]{:S(2)}, u32[]{:S(2)}) collective-permute-start(bf16[24,2176]{1,0:T(8,128)(2,1)S(1)} %get-tuple-element.41), channel_id=1, source_target_pairs={{0,4},{2,6},{4,0},{6,2},{1,5},{3,7},{5,1},{7,3},{8,12},{10,14},{12... | collective-permute-start | bytes 313352 | tf_op jit(solution)/shard_map/ppermute | solution.py:24
  10.3 8.8 %collective-permute-start.1 = (bf16[24,2176]{1,0:T(8,128)(2,1)S(1)}, bf16[24,2176]{1,0:T(8,128)(2,1)S(1)}, u32[]{:S(2)}, u32[]{:S(2)}) collective-permute-start(bf16[24,2176]{1,0:T(8,128)(2,1)S(1)} %get-tuple-element.41), channel_id=1, source_target_pairs={{0,2},{2,0},{4,6},{6,4},{1,3},{3,1},{5,7},{7,5},{8,10},{10,8},{12,... | collective-permute-start | bytes 313352 | tf_op jit(solution)/shard_map/ppermute | solution.py:24
  11.1 8.2 %collective-permute-start.6 = (bf16[24,2176]{1,0:T(8,128)(2,1)S(1)}, bf16[24,2176]{1,0:T(8,128)(2,1)S(1)}, u32[]{:S(2)}, u32[]{:S(2)}) collective-permute-start(bf16[24,2176]{1,0:T(8,128)(2,1)S(1)} %get-tuple-element.41), channel_id=1, source_target_pairs={{0,24},{8,16},{16,8},{24,0},{1,25},{9,17},{17,9},{25,1},{2,26},{10... | collective-permute-start | bytes 313352 | tf_op jit(solution)/shard_map/ppermute | solution.py:24
  12.6 6.7 %collective-permute-start.5 = (bf16[24,2176]{1,0:T(8,128)(2,1)S(1)}, bf16[24,2176]{1,0:T(8,128)(2,1)S(1)}, u32[]{:S(2)}, u32[]{:S(2)}) collective-permute-start(bf16[24,2176]{1,0:T(8,128)(2,1)S(1)} %get-tuple-element.41), channel_id=1, source_target_pairs={{0,16},{8,24},{16,0},{24,8},{1,17},{9,25},{17,1},{25,9},{2,18},{10... | collective-permute-start | bytes 313352 | tf_op jit(solution)/shard_map/ppermute | solution.py:24
  19.3 2.2 %collective-permute-start.7 = (bf16[168,2048]{1,0:T(8,128)(2,1)S(1)}, bf16[168,2048]{1,0:T(8,128)(2,1)S(1)}, u32[]{:S(2)}, u32[]{:S(2)}) collective-permute-start(bf16[168,2048]{1,0:T(8,128)(2,1)S(1)} %slice.79), channel_id=1, source_target_pairs={{0,1},{1,0},{2,3},{3,2},{4,5},{5,4},{6,7},{7,6},{8,9},{9,8},{10,11... | collective-permute-start | bytes 2064392 | tf_op jit(solution)/shard_map/ppermute | solution.py:24
  19.4 9.8 %collective-permute-start.9 = (bf16[72,2176]{1,0:T(8,128)(2,1)S(1)}, bf16[72,2176]{1,0:T(8,128)(2,1)S(1)}, u32[]{:S(2)}, u32[]{:S(2)}) collective-permute-start(bf16[72,2176]{1,0:T(8,128)(2,1)S(1)} %get-tuple-element.60), channel_id=1, source_target_pairs={{0,8},{8,0},{16,24},{24,16},{1,9},{9,1},{17,25},{25,17},{2,10},{10... | collective-permute-start | bytes 940040 | tf_op jit(solution)/shard_map/ppermute | solution.py:24
  20.0 9.5 %collective-permute-start.10 = (bf16[72,2176]{1,0:T(8,128)(2,1)S(1)}, bf16[72,2176]{1,0:T(8,128)(2,1)S(1)}, u32[]{:S(2)}, u32[]{:S(2)}) collective-permute-start(bf16[72,2176]{1,0:T(8,128)(2,1)S(1)} %get-tuple-element.60), channel_id=1, source_target_pairs={{0,16},{8,24},{16,0},{24,8},{1,17},{9,25},{17,1},{25,9},{2,18},{10... | collective-permute-start | bytes 940040 | tf_op jit(solution)/shard_map/ppermute | solution.py:24
  29.7 2.1 %collective-permute-start.11 = (bf16[144,2048]{1,0:T(8,128)(2,1)S(1)}, bf16[144,2048]{1,0:T(8,128)(2,1)S(1)}, u32[]{:S(2)}, u32[]{:S(2)}) collective-permute-start(bf16[144,2048]{1,0:T(8,128)(2,1)S(1)} %slice.81), channel_id=1, source_target_pairs={{0,1},{1,0},{2,3},{3,2},{4,5},{5,4},{6,7},{7,6},{8,9},{9,8},{10,11... | collective-permute-start | bytes 1769480 | tf_op jit(solution)/shard_map/ppermute | solution.py:24
  29.8 9.3 %collective-permute-start.8 = (bf16[168,2048]{1,0:T(8,128)(2,1)S(1)}, bf16[168,2048]{1,0:T(8,128)(2,1)S(1)}, u32[]{:S(2)}, u32[]{:S(2)}) collective-permute-start(bf16[168,2048]{1,0:T(8,128)(2,1)S(1)} %get-tuple-element.30), channel_id=1, source_target_pairs={{0,1},{1,0},{2,3},{3,2},{4,5},{5,4},{6,7},{7,6},{8,9},{9,8},{10,11... | collective-permute-start | bytes 2064392 | tf_op jit(solution)/shard_map/ppermute | solution.py:24
  30.3 6.9 %collective-permute-start.18 = (bf16[72,2176]{1,0:T(8,128)(2,1)S(1)}, bf16[72,2176]{1,0:T(8,128)(2,1)S(1)}, u32[]{:S(2)}, u32[]{:S(2)}) collective-permute-start(bf16[72,2176]{1,0:T(8,128)(2,1)S(1)} %get-tuple-element.51), channel_id=1, source_target_pairs={{0,16},{1,9},{8,24},{9,1},{16,0},{17,25},{24,8},{25,17},{2,18},{3,... | collective-permute-start | bytes 940040 | tf_op jit(solution)/shard_map/ppermute | solution.py:36
  35.4 3.9 %collective-permute-start.12 = (bf16[144,2048]{1,0:T(8,128)(2,1)S(1)}, bf16[144,2048]{1,0:T(8,128)(2,1)S(1)}, u32[]{:S(2)}, u32[]{:S(2)}) collective-permute-start(bf16[144,2048]{1,0:T(8,128)(2,1)S(1)} %get-tuple-element.35), channel_id=1, source_target_pairs={{0,1},{1,0},{2,3},{3,2},{4,5},{5,4},{6,7},{7,6},{8,9},{9,8},{10,11... | collective-permute-start | bytes 1769480 | tf_op jit(solution)/shard_map/ppermute | solution.py:24
  37.2 2.4 %collective-permute-start.19 = (bf16[72,2048]{1,0:T(8,128)(2,1)S(1)}, bf16[72,2048]{1,0:T(8,128)(2,1)S(1)}, u32[]{:S(2)}, u32[]{:S(2)}) collective-permute-start(bf16[72,2048]{1,0:T(8,128)(2,1)S(1)} %slice.69), channel_id=1, source_target_pairs={{0,1},{1,0},{2,3},{3,2},{4,5},{5,4},{6,7},{7,6},{8,9},{9,8},{10,11... | collective-permute-start | bytes 884744 | tf_op jit(solution)/shard_map/ppermute | solution.py:24
  42.0 1.8 %collective-permute-start.20 = (bf16[72,2048]{1,0:T(8,128)(2,1)S(1)}, bf16[72,2048]{1,0:T(8,128)(2,1)S(1)}, u32[]{:S(2)}, u32[]{:S(2)}) collective-permute-start(bf16[72,2048]{1,0:T(8,128)(2,1)S(1)} %get-tuple-element.39), channel_id=1, source_target_pairs={{0,1},{1,0},{2,3},{3,2},{4,5},{5,4},{6,7},{7,6},{8,9},{9,8},{10,11... | collective-permute-start | bytes 884744 | tf_op jit(solution)/shard_map/ppermute | solution.py:24
  43.9 7.5 %collective-permute-start.21 = (bf16[24,2048]{1,0:T(8,128)(2,1)S(1)}, bf16[24,2048]{1,0:T(8,128)(2,1)S(1)}, u32[]{:S(2)}, u32[]{:S(2)}) collective-permute-start(bf16[24,2048]{1,0:T(8,128)(2,1)S(1)} %get-tuple-element.52), channel_id=1, source_target_pairs={{0,6},{2,4},{4,2},{6,0},{1,7},{3,5},{5,3},{7,1},{8,14},{10,12},{12... | collective-permute-start | bytes 294920 | tf_op jit(solution)/shard_map/ppermute | solution.py:24
  47.1 7.6 %collective-permute-start.23 = (bf16[24,2048]{1,0:T(8,128)(2,1)S(1)}, bf16[24,2048]{1,0:T(8,128)(2,1)S(1)}, u32[]{:S(2)}, u32[]{:S(2)}) collective-permute-start(bf16[24,2048]{1,0:T(8,128)(2,1)S(1)} %get-tuple-element.53), channel_id=1, source_target_pairs={{0,2},{2,0},{4,6},{6,4},{1,3},{3,1},{5,7},{7,5},{8,10},{10,8},{12,... | collective-permute-start | bytes 294920 | tf_op jit(solution)/shard_map/ppermute | solution.py:24
  47.1 8.4 %collective-permute-start.22 = (bf16[24,2048]{1,0:T(8,128)(2,1)S(1)}, bf16[24,2048]{1,0:T(8,128)(2,1)S(1)}, u32[]{:S(2)}, u32[]{:S(2)}) collective-permute-start(bf16[24,2048]{1,0:T(8,128)(2,1)S(1)} %get-tuple-element.54), channel_id=1, source_target_pairs={{0,4},{2,6},{4,0},{6,2},{1,5},{3,7},{5,1},{7,3},{8,12},{10,14},{12... | collective-permute-start | bytes 294920 | tf_op jit(solution)/shard_map/ppermute | solution.py:24
  48.3 10.5 %collective-permute-start.13 = (bf16[96,2048]{1,0:T(8,128)(2,1)S(1)}, bf16[96,2048]{1,0:T(8,128)(2,1)S(1)}, u32[]{:S(2)}, u32[]{:S(2)}) collective-permute-start(bf16[96,2048]{1,0:T(8,128)(2,1)S(1)} %pad_maximum_fusion), channel_id=1, source_target_pairs={{0,8},{8,0},{16,24},{24,16},{1,9},{9,1},{17,25},{25,17},{2,10},{10... | collective-permute-start | bytes 1179656 | tf_op jit(solution)/shard_map/ppermute | solution.py:24
  49.8 12.3 %collective-permute-start.14 = (bf16[96,2048]{1,0:T(8,128)(2,1)S(1)}, bf16[96,2048]{1,0:T(8,128)(2,1)S(1)}, u32[]{:S(2)}, u32[]{:S(2)}) collective-permute-start(bf16[96,2048]{1,0:T(8,128)(2,1)S(1)} %pad_maximum_fusion.1), channel_id=1, source_target_pairs={{0,16},{8,24},{16,0},{24,8},{1,17},{9,25},{17,1},{25,9},{2,18},{10... | collective-permute-start | bytes 1179656 | tf_op jit(solution)/shard_map/ppermute | solution.py:24
  55.6 11.3 %copy-start = (s32[8]{0:T(128)S(1)}, s32[8]{0:T(128)}, u32[]{:S(2)}) copy-start(s32[8]{0:T(128)} %refs_0_.3) | copy-start | bytes 100
  55.6 12.7 %collective-permute-start.24 = (bf16[24,2048]{1,0:T(8,128)(2,1)S(1)}, bf16[24,2048]{1,0:T(8,128)(2,1)S(1)}, u32[]{:S(2)}, u32[]{:S(2)}) collective-permute-start(bf16[24,2048]{1,0:T(8,128)(2,1)S(1)} %add_convert_fusion.4), channel_id=1, source_target_pairs={{0,24},{8,16},{16,8},{24,0},{1,25},{9,17},{17,9},{25,1},{2,26},{10... | collective-permute-start | bytes 294920 | tf_op jit(solution)/shard_map/ppermute | solution.py:24
  62.4 6.4 %collective-permute-start.17 = (bf16[24,2048]{1,0:T(8,128)(2,1)S(1)}, bf16[24,2048]{1,0:T(8,128)(2,1)S(1)}, u32[]{:S(2)}, u32[]{:S(2)}) collective-permute-start(bf16[24,2048]{1,0:T(8,128)(2,1)S(1)} %get-tuple-element.47), channel_id=1, source_target_pairs={{0,2},{2,0},{4,6},{6,4},{1,3},{3,1},{5,7},{7,5},{8,10},{10,8},{12,... | collective-permute-start | bytes 294920 | tf_op jit(solution)/shard_map/ppermute | solution.py:24
  62.4 6.3 %collective-permute-start.16 = (bf16[24,2048]{1,0:T(8,128)(2,1)S(1)}, bf16[24,2048]{1,0:T(8,128)(2,1)S(1)}, u32[]{:S(2)}, u32[]{:S(2)}) collective-permute-start(bf16[24,2048]{1,0:T(8,128)(2,1)S(1)} %get-tuple-element.48), channel_id=1, source_target_pairs={{0,4},{2,6},{4,0},{6,2},{1,5},{3,7},{5,1},{7,3},{8,12},{10,14},{12... | collective-permute-start | bytes 294920 | tf_op jit(solution)/shard_map/ppermute | solution.py:24
  64.5 6.5 %collective-permute-start.15 = (bf16[24,2048]{1,0:T(8,128)(2,1)S(1)}, bf16[24,2048]{1,0:T(8,128)(2,1)S(1)}, u32[]{:S(2)}, u32[]{:S(2)}) collective-permute-start(bf16[24,2048]{1,0:T(8,128)(2,1)S(1)} %get-tuple-element.49), channel_id=1, source_target_pairs={{0,6},{2,4},{4,2},{6,0},{1,7},{3,5},{5,3},{7,1},{8,14},{10,12},{12... | collective-permute-start | bytes 294920 | tf_op jit(solution)/shard_map/ppermute | solution.py:24
  71.1 1.3 %collective-permute-start.25 = (bf16[12,2048]{1,0:T(8,128)(2,1)S(1)}, bf16[12,2048]{1,0:T(8,128)(2,1)S(1)}, u32[]{:S(2)}, u32[]{:S(2)}) collective-permute-start(bf16[12,2048]{1,0:T(8,128)(2,1)S(1)} %broadcast_select_fusion.5), channel_id=1, source_target_pairs={{0,1},{1,0},{2,3},{3,2},{4,5},{5,4},{6,7},{7,6},{8,9},{9,8},{10,11... | collective-permute-start | bytes 147464 | tf_op jit(solution)/shard_map/ppermute | solution.py:24

commit v18 on v17

--- a/solution.py
+++ b/solution.py
@@ -400,16 +400,20 @@
         other = behind(swap(rest[:, :part], "core", 1), whole[1:3])
         keep, give = gated_sums_in_steps(place, top_count, rest, other, *weights)
         fourth = parts(added(keep, swap(give, "core", 1)))
-        fourth = collected(near_sums[3], along_chips(fourth))
-        came = [swap(fourth, "dp", 3)]
+        fourth = along_chips(fourth)
         metas = [held, near, rest]
     else:
         far_sums += [chip_sums(*sums_of(block, weights)) for block in near]
         whole = [jnp.concatenate(pair, 0) for pair in zip(near_sums, far_sums)]
-        came = []
+        fourth = []
         metas = [held, *near]
     metas = [block[:, block.shape[1] - LANES :] for block in metas]
-    total = parts(collected(whole[0], received(whole)))
+    total = collected(whole[0], received(whole))
+    came = []
+    if fourth:
+        fourth = collected(near_sums[3], behind(fourth, total))
+        came = [swap(fourth, "dp", 3)]
+    total = parts(total)
     load = planned_load(metas, swap_slot, owners, per_device, top_count, total[0])
     total = collected(total[0], along_chips(total[1:]) + came)
     upper, lower = total[:rows], total[rows:]

time: 73.3 us -> 71.7 us (0.978)
  starting transfers between devices: 28.7 us -> 27.7 us
    ppermute x25, starting transfers between devices: 27.2 us -> 26.2 us  [swap(): return row_major(lax.ppermute(row_major(value), axis, pairs))]
  transfers between devices with their start and end apart: 26 -> 26, of which waited for: 13 -> 10; matrix products, arithmetic and copies ran while one was open for 2% -> 2% of each run, Pallas kernels for 26% -> 27%
where the time goes in v18:
time: 71.7 us; the launch traced here: 71.5 us
  starting transfers between devices  27.7 us (39%)
  Pallas kernels  23.1 us (32%)
  waiting for transfers between devices  17.2 us (24%)
  other arithmetic  1.64 us (2%)
  between operations  0.97 us (1%)
  local copies, waits for them, and re-layouts  0.91 us (1%)
    ppermute x25, starting transfers between devices, swap(): return row_major(lax.ppermute(row_major(value), axis, pairs))  26.2 us
    ppermute x25, waiting for transfers between devices, swap(): return row_major(lax.ppermute(row_major(value), axis, pairs))  15.6 us
    pallas_call x5, Pallas kernels, call(): pl.pallas_call(kernel, in_specs=[pl.BlockSpec(memory_space=pltpu.SMEM)] +...  15.4 us
    pallas_call x1, Pallas kernels, loaded(): pl.pallas_call(load_weight_kernel, in_specs=[pl.BlockSpec(memory_space=pl...  4.58 us
    ppermute x1, waiting for transfers between devices, cross(): return row_major(lax.ppermute(row_major(value), ('dp', 'core'), pairs))  1.58 us
    pallas_call x1, Pallas kernels, first_halves(): pl.pallas_call(first_kernel, in_specs=[pl.BlockSpec(memory_space=pltpu.SM...  1.56 us
    ppermute x1, starting transfers between devices, cross(): return row_major(lax.ppermute(row_major(value), ('dp', 'core'), pairs))  1.52 us
    pallas_call x1, Pallas kernels, planned_load(): pl.pallas_call(lambda *refs: load_kernel(layout, *refs), in_specs=[pl.Blo...  1.47 us
  transfers between devices with their start and end apart: 26, of which 10 were waited for; matrix products, arithmetic and copies ran while one was open for 2% of the time, Pallas kernels for 27%

profile of v18, /device:TPU:0, one launch (start us, length us, event | category | flops | bytes accessed | tf_op | source)
XLA Modules:
  0.0 71.5 jit_solution(65028733344911687)
XLA Ops:
  0.6 0.1 pad_add_fusion.place.refs_0_
  0.7 1.6 %shard_map.77 = (bf16[12,2176]{1,0:T(8,128)(2,1)S(1)}, bf16[12,2176]{1,0:T(8,128)(2,1)S(1)}) custom-call(s32[2]{0:T(128)S(1)} %pad_add_fusion.place.refs_0_, bf16[12,4096]{1,0:T(8,128)(2,1)} %refs_0_.2, s32[8,12]{1,0:T(8,128)} %bitcast.8, f32[8,12]{1,0:T(8,128)} %bitcast.9), custom_call_target="tpu_custom_call" | custom-call | tf_op jit(solution)/shard_map/pallas_call | solution.py:253
  2.3 0.5 collective-permute-start
  2.8 0.9 %collective-permute-done = bf16[12,2176]{1,0:T(8,128)(2,1)S(1)} collective-permute-done((bf16[12,2176]{1,0:T(8,128)(2,1)S(1)}, bf16[12,2176]{1,0:T(8,128)(2,1)S(1)}, u32[]{:S(2)}, u32[]{:S(2)}) %collective-permute-start) | collective-permute-done | bytes 52256 | tf_op jit(solution)/shard_map/ppermute | solution.py:24
  3.8 2.9 %collective-permute-start.4 = (bf16[24,2176]{1,0:T(8,128)(2,1)S(1)}, bf16[24,2176]{1,0:T(8,128)(2,1)S(1)}, u32[]{:S(2)}, u32[]{:S(2)}) collective-permute-start(bf16[24,2176]{1,0:T(8,128)(2,1)S(1)} %get-tuple-element.47), channel_id=1, source_target_pairs={{0,8},{8,0},{16,24},{24,16},{1,9},{9,1},{17,25},{25,17},{2,10},{10... | collective-permute-start | bytes 313352 | tf_op jit(solution)/shard_map/ppermute | solution.py:24
  6.7 3.6 %collective-permute-start.3 = (bf16[24,2176]{1,0:T(8,128)(2,1)S(1)}, bf16[24,2176]{1,0:T(8,128)(2,1)S(1)}, u32[]{:S(2)}, u32[]{:S(2)}) collective-permute-start(bf16[24,2176]{1,0:T(8,128)(2,1)S(1)} %get-tuple-element.47), channel_id=1, source_target_pairs={{0,6},{2,4},{4,2},{6,0},{1,7},{3,5},{5,3},{7,1},{8,14},{10,12},{12... | collective-permute-start | bytes 313352 | tf_op jit(solution)/shard_map/ppermute | solution.py:24
  10.3 0.8 %collective-permute-start.1 = (bf16[24,2176]{1,0:T(8,128)(2,1)S(1)}, bf16[24,2176]{1,0:T(8,128)(2,1)S(1)}, u32[]{:S(2)}, u32[]{:S(2)}) collective-permute-start(bf16[24,2176]{1,0:T(8,128)(2,1)S(1)} %get-tuple-element.47), channel_id=1, source_target_pairs={{0,2},{2,0},{4,6},{6,4},{1,3},{3,1},{5,7},{7,5},{8,10},{10,8},{12,... | collective-permute-start | bytes 313352 | tf_op jit(solution)/shard_map/ppermute | solution.py:24
  11.1 1.5 %collective-permute-start.6 = (bf16[24,2176]{1,0:T(8,128)(2,1)S(1)}, bf16[24,2176]{1,0:T(8,128)(2,1)S(1)}, u32[]{:S(2)}, u32[]{:S(2)}) collective-permute-start(bf16[24,2176]{1,0:T(8,128)(2,1)S(1)} %get-tuple-element.47), channel_id=1, source_target_pairs={{0,24},{8,16},{16,8},{24,0},{1,25},{9,17},{17,9},{25,1},{2,26},{10... | collective-permute-start | bytes 313352 | tf_op jit(solution)/shard_map/ppermute | solution.py:24
  12.6 0.3 collective-permute-start.5
  12.8 4.6 %shard_map.78 = (bf16[2,4096,768]{2,1,0:T(8,128)(2,1)S(1)}, f32[8,128]{1,0:T(8,128)S(1)}) custom-call(bf16[2,4096,768]{2,1,0:T(8,128)(2,1)} %weight_ref.1, bf16[24,2176]{1,0:T(8,128)(2,1)S(1)} %collective-permute-done.4._), custom_call_target="tpu_custom_call" | custom-call | bytes 12582912 | tf_op jit(solution)/shard_map/pallas_call | solution.py:63
  17.4 1.7 %collective-permute-done.2 = bf16[24,2176]{1,0:T(8,128)(2,1)S(1)} collective-permute-done((bf16[24,2176]{1,0:T(8,128)(2,1)S(1)}, bf16[24,2176]{1,0:T(8,128)(2,1)S(1)}, u32[]{:S(2)}, u32[]{:S(2)}) %collective-permute-start.2) | collective-permute-done | bytes 104480 | tf_op jit(solution)/shard_map/ppermute | solution.py:24
  19.3 0.1 collective-permute-start.7
  19.4 0.6 collective-permute-start.9
  20.0 1.5 %collective-permute-start.10 = (bf16[72,2176]{1,0:T(8,128)(2,1)S(1)}, bf16[72,2176]{1,0:T(8,128)(2,1)S(1)}, u32[]{:S(2)}, u32[]{:S(2)}) collective-permute-start(bf16[72,2176]{1,0:T(8,128)(2,1)S(1)} %get-tuple-element.66), channel_id=1, source_target_pairs={{0,16},{8,24},{16,0},{24,8},{1,17},{9,25},{17,1},{25,9},{2,18},{10... | collective-permute-start | bytes 940040 | tf_op jit(solution)/shard_map/ppermute | solution.py:24
  21.6 6.4 %shard_map.79 = (bf16[168,2048]{1,0:T(8,128)(2,1)S(1)}, bf16[168,2048]{1,0:T(8,128)(2,1)S(1)}, bf16[768,4096]{1,0:T(8,128)(2,1)S(1)}) custom-call(s32[2]{0:T(128)S(1)} %pad_add_fusion.place.refs_0_, bf16[168,2176]{1,0:T(8,128)(2,1)S(1)} %constant_dynamic-update-slice_fusion.refs_1_, bf16[168,2048]{1,0:T(8,128)(2,1)S(1)} %collective-permute-done.7.refs_2_, ...), custom_call_target="tpu_custom_call" | custom-call | flops 3170893824 | tf_op jit(solution)/shard_map/pallas_call | solution.py:154
  28.0 1.2 %collective-permute-done.9 = bf16[72,2176]{1,0:T(8,128)(2,1)S(1)} collective-permute-done((bf16[72,2176]{1,0:T(8,128)(2,1)S(1)}, bf16[72,2176]{1,0:T(8,128)(2,1)S(1)}, u32[]{:S(2)}, u32[]{:S(2)}) %collective-permute-start.9) | collective-permute-done | bytes 313376 | tf_op jit(solution)/shard_map/ppermute | solution.py:24
  29.2 0.3 collective-permute-done.10
  29.5 0.1 constant_dynamic-update-slice_fusion.10
  29.8 0.5 collective-permute-start.8
  30.3 1.5 %collective-permute-start.18 = (bf16[72,2176]{1,0:T(8,128)(2,1)S(1)}, bf16[72,2176]{1,0:T(8,128)(2,1)S(1)}, u32[]{:S(2)}, u32[]{:S(2)}) collective-permute-start(bf16[72,2176]{1,0:T(8,128)(2,1)S(1)} %get-tuple-element.57), channel_id=1, source_target_pairs={{0,16},{1,9},{8,24},{9,1},{16,0},{17,25},{24,8},{25,17},{2,18},{3,... | collective-permute-start | bytes 940040 | tf_op jit(solution)/shard_map/ppermute | solution.py:36
  31.8 3.6 %shard_map.80 = (bf16[144,2048]{1,0:T(8,128)(2,1)S(1)}, bf16[144,2048]{1,0:T(8,128)(2,1)S(1)}) custom-call(s32[2]{0:T(128)S(1)} %pad_add_fusion.place.refs_0_, bf16[144,2176]{1,0:T(8,128)(2,1)S(1)} %get-tuple-element.56.refs_1_, bf16[144,2048]{1,0:T(8,128)(2,1)S(1)} %collective-permute-done.11.refs_2_, ...), custom_call_target="tpu_custom_call" | custom-call | flops 2717908992 | tf_op jit(solution)/shard_map/pallas_call | solution.py:154
  35.4 0.2 collective-permute-start.12
  35.6 1.6 %collective-permute-done.18.own.refs_1_ = bf16[72,2176]{1,0:T(8,128)(2,1)S(1)} collective-permute-done((bf16[72,2176]{1,0:T(8,128)(2,1)S(1)}, bf16[72,2176]{1,0:T(8,128)(2,1)S(1)}, u32[]{:S(2)}, u32[]{:S(2)}) %collective-permute-start.18) | collective-permute-done | bytes 313376 | tf_op jit(solution)/shard_map/ppermute | solution.py:36
  37.3 1.8 %shard_map.81.refs_3_ = f32[2,72,768]{2,1,0:T(8,128)S(1)} custom-call(s32[2]{0:T(128)S(1)} %pad_add_fusion.place.refs_0_, bf16[72,2176]{1,0:T(8,128)(2,1)S(1)} %collective-permute-done.18.own.refs_1_, bf16[2,4096,768]{2,1,0:T(8,128)(2,1)S(1)} %get-tuple-element.30.refs_3_.up.refs_4_), custom_call_target="tpu_custom_call" | custom-call | flops 452984832 | tf_op jit(solution)/shard_map/pallas_call | solution.py:154
  39.1 0.2 add_convert_fusion
  39.3 0.1 add_convert_fusion.1
  39.6 2.4 %shard_map.82 = (bf16[72,2048]{1,0:T(8,128)(2,1)S(1)}, bf16[72,768]{1,0:T(8,128)(2,1)S(1)}) custom-call(s32[2]{0:T(128)S(1)} %pad_add_fusion.place.refs_0_, bf16[72,2176]{1,0:T(8,128)(2,1)S(1)} %collective-permute-done.18.own.refs_1_, bf16[72,2048]{1,0:T(8,128)(2,1)S(1)} %collective-permute-done.19.refs_2_, f32[2,72,768]{2,1,0:T(8,128)S(1)} %shard_map.81.refs_3_, ...), custom_call_target="tpu_custom_call" | custom-call | flops 679477248 | tf_op jit(solution)/shard_map/pallas_call | solution.py:154
  42.0 0.6 collective-permute-start.20
  42.5 1.5 %collective-permute-start.13 = (bf16[96,2048]{1,0:T(8,128)(2,1)S(1)}, bf16[96,2048]{1,0:T(8,128)(2,1)S(1)}, u32[]{:S(2)}, u32[]{:S(2)}) collective-permute-start(bf16[96,2048]{1,0:T(8,128)(2,1)S(1)} %pad_maximum_fusion), channel_id=1, source_target_pairs={{0,8},{8,0},{16,24},{24,16},{1,9},{9,1},{17,25},{25,17},{2,10},{10... | collective-permute-start | bytes 1179656 | tf_op jit(solution)/shard_map/ppermute | solution.py:24
  44.0 1.5 %collective-permute-start.14 = (bf16[96,2048]{1,0:T(8,128)(2,1)S(1)}, bf16[96,2048]{1,0:T(8,128)(2,1)S(1)}, u32[]{:S(2)}, u32[]{:S(2)}) collective-permute-start(bf16[96,2048]{1,0:T(8,128)(2,1)S(1)} %pad_maximum_fusion.1), channel_id=1, source_target_pairs={{0,16},{8,24},{16,0},{24,8},{1,17},{9,25},{17,1},{25,9},{2,18},{10... | collective-permute-start | bytes 1179656 | tf_op jit(solution)/shard_map/ppermute | solution.py:24
  45.5 1.2 %shard_map.83.kept_ref = bf16[72,2048]{1,0:T(8,128)(2,1)S(1)} custom-call(s32[2]{0:T(128)S(1)} %pad_add_fusion.place.refs_0_, bf16[72,768]{1,0:T(8,128)(2,1)S(1)} %get-tuple-element.41.hidden, bf16[768,4096]{1,0:T(8,128)(2,1)S(1)} %get-tuple-element.36.refs_4_.refs_5_.down), custom_call_target="tpu_custom_call" | custom-call | flops 226492416 | tf_op jit(solution)/shard_map/pallas_call | solution.py:154
  46.8 0.1 shard_map.84
  46.9 0.5 collective-permute-start.23
  47.3 2.6 %collective-permute-start.22 = (bf16[24,2048]{1,0:T(8,128)(2,1)S(1)}, bf16[24,2048]{1,0:T(8,128)(2,1)S(1)}, u32[]{:S(2)}, u32[]{:S(2)}) collective-permute-start(bf16[24,2048]{1,0:T(8,128)(2,1)S(1)} %get-tuple-element.59), channel_id=1, source_target_pairs={{0,4},{2,6},{4,0},{6,2},{1,5},{3,7},{5,1},{7,3},{8,12},{10,14},{12... | collective-permute-start | bytes 294920 | tf_op jit(solution)/shard_map/ppermute | solution.py:24
  50.0 1.3 %collective-permute-start.21 = (bf16[24,2048]{1,0:T(8,128)(2,1)S(1)}, bf16[24,2048]{1,0:T(8,128)(2,1)S(1)}, u32[]{:S(2)}, u32[]{:S(2)}) collective-permute-start(bf16[24,2048]{1,0:T(8,128)(2,1)S(1)} %get-tuple-element.60), channel_id=1, source_target_pairs={{0,6},{2,4},{4,2},{6,0},{1,7},{3,5},{5,3},{7,1},{8,14},{10,12},{12... | collective-permute-start | bytes 294920 | tf_op jit(solution)/shard_map/ppermute | solution.py:24
  51.3 2.3 %collective-permute-done.13 = bf16[96,2048]{1,0:T(8,128)(2,1)S(1)} collective-permute-done((bf16[96,2048]{1,0:T(8,128)(2,1)S(1)}, bf16[96,2048]{1,0:T(8,128)(2,1)S(1)}, u32[]{:S(2)}, u32[]{:S(2)}) %collective-permute-start.13) | collective-permute-done | bytes 393248 | tf_op jit(solution)/shard_map/ppermute | solution.py:24
  53.6 1.2 %collective-permute-done.14 = bf16[96,2048]{1,0:T(8,128)(2,1)S(1)} collective-permute-done((bf16[96,2048]{1,0:T(8,128)(2,1)S(1)}, bf16[96,2048]{1,0:T(8,128)(2,1)S(1)}, u32[]{:S(2)}, u32[]{:S(2)}) %collective-permute-start.14) | collective-permute-done | bytes 393248 | tf_op jit(solution)/shard_map/ppermute | solution.py:24
  54.8 0.1 add_convert_fusion.2
  55.0 2.5 %collective-permute-done.22 = bf16[24,2048]{1,0:T(8,128)(2,1)S(1)} collective-permute-done((bf16[24,2048]{1,0:T(8,128)(2,1)S(1)}, bf16[24,2048]{1,0:T(8,128)(2,1)S(1)}, u32[]{:S(2)}, u32[]{:S(2)}) %collective-permute-start.22) | collective-permute-done | bytes 98336 | tf_op jit(solution)/shard_map/ppermute | solution.py:24
  57.6 1.1 %collective-permute-start.24 = (bf16[24,2048]{1,0:T(8,128)(2,1)S(1)}, bf16[24,2048]{1,0:T(8,128)(2,1)S(1)}, u32[]{:S(2)}, u32[]{:S(2)}) collective-permute-start(bf16[24,2048]{1,0:T(8,128)(2,1)S(1)} %add_convert_fusion.4), channel_id=1, source_target_pairs={{0,24},{8,16},{16,8},{24,0},{1,25},{9,17},{17,9},{25,1},{2,26},{10... | collective-permute-start | bytes 294920 | tf_op jit(solution)/shard_map/ppermute | solution.py:24
  58.7 1.6 %collective-permute-start.17 = (bf16[24,2048]{1,0:T(8,128)(2,1)S(1)}, bf16[24,2048]{1,0:T(8,128)(2,1)S(1)}, u32[]{:S(2)}, u32[]{:S(2)}) collective-permute-start(bf16[24,2048]{1,0:T(8,128)(2,1)S(1)} %get-tuple-element.53), channel_id=1, source_target_pairs={{0,2},{2,0},{4,6},{6,4},{1,3},{3,1},{5,7},{7,5},{8,10},{10,8},{12,... | collective-permute-start | bytes 294920 | tf_op jit(solution)/shard_map/ppermute | solution.py:24
  60.3 1.4 %collective-permute-start.16 = (bf16[24,2048]{1,0:T(8,128)(2,1)S(1)}, bf16[24,2048]{1,0:T(8,128)(2,1)S(1)}, u32[]{:S(2)}, u32[]{:S(2)}) collective-permute-start(bf16[24,2048]{1,0:T(8,128)(2,1)S(1)} %get-tuple-element.54), channel_id=1, source_target_pairs={{0,4},{2,6},{4,0},{6,2},{1,5},{3,7},{5,1},{7,3},{8,12},{10,14},{12... | collective-permute-start | bytes 294920 | tf_op jit(solution)/shard_map/ppermute | solution.py:24
  61.7 1.4 %collective-permute-start.15 = (bf16[24,2048]{1,0:T(8,128)(2,1)S(1)}, bf16[24,2048]{1,0:T(8,128)(2,1)S(1)}, u32[]{:S(2)}, u32[]{:S(2)}) collective-permute-start(bf16[24,2048]{1,0:T(8,128)(2,1)S(1)} %get-tuple-element.55), channel_id=1, source_target_pairs={{0,6},{2,4},{4,2},{6,0},{1,7},{3,5},{5,3},{7,1},{8,14},{10,12},{12... | collective-permute-start | bytes 294920 | tf_op jit(solution)/shard_map/ppermute | solution.py:24
  63.1 1.5 %shard_map.85 = f32[1,128]{1,0:T(1,128)S(1)} custom-call(s32[8]{0:T(128)S(1)} %copy-done, bf16[168,128]{1,0:T(8,128)(2,1)S(1)} %slice.93.refs_1_, bf16[144,128]{1,0:T(8,128)(2,1)S(1)} %slice.94.refs_2_, bf16[72,128]{1,0:T(8,128)(2,1)S(1)} %slice.77.refs_3_, bf16[24,2048]{1,0:T(8,128)(2,1)S(1)} %get-tuple-element.52.refs_4_), custom_call_target="tpu_custom_call" | custom-call | bytes 98304 | tf_op jit(solution)/shard_map/pallas_call | solution.py:321
  64.6 4.7 %collective-permute-done.16 = bf16[24,2048]{1,0:T(8,128)(2,1)S(1)} collective-permute-done((bf16[24,2048]{1,0:T(8,128)(2,1)S(1)}, bf16[24,2048]{1,0:T(8,128)(2,1)S(1)}, u32[]{:S(2)}, u32[]{:S(2)}) %collective-permute-start.16) | collective-permute-done | bytes 98336 | tf_op jit(solution)/shard_map/ppermute | solution.py:24
  69.5 0.5 slice_bitcast_fusion
  70.0 0.7 %collective-permute-done.25 = bf16[12,2048]{1,0:T(8,128)(2,1)S(1)} collective-permute-done((bf16[12,2048]{1,0:T(8,128)(2,1)S(1)}, bf16[12,2048]{1,0:T(8,128)(2,1)S(1)}, u32[]{:S(2)}, u32[]{:S(2)}) %collective-permute-start.25) | collective-permute-done | bytes 49184 | tf_op jit(solution)/shard_map/ppermute | solution.py:24
  70.8 0.7 pad_maximum_fusion.2
  (47 shorter events, 0.9 us)
Async XLA Ops:
  2.3 1.4 %collective-permute-start = (bf16[12,2176]{1,0:T(8,128)(2,1)S(1)}, bf16[12,2176]{1,0:T(8,128)(2,1)S(1)}, u32[]{:S(2)}, u32[]{:S(2)}) collective-permute-start(bf16[12,2176]{1,0:T(8,128)(2,1)S(1)} %get-tuple-element.25), channel_id=1, source_target_pairs={{0,1},{1,0},{2,3},{3,2},{4,5},{5,4},{6,7},{7,6},{8,9},{9,8},{10,11... | collective-permute-start | bytes 156680 | tf_op jit(solution)/shard_map/ppermute | solution.py:24
  3.8 8.8 %collective-permute-start.4 = (bf16[24,2176]{1,0:T(8,128)(2,1)S(1)}, bf16[24,2176]{1,0:T(8,128)(2,1)S(1)}, u32[]{:S(2)}, u32[]{:S(2)}) collective-permute-start(bf16[24,2176]{1,0:T(8,128)(2,1)S(1)} %get-tuple-element.47), channel_id=1, source_target_pairs={{0,8},{8,0},{16,24},{24,16},{1,9},{9,1},{17,25},{25,17},{2,10},{10... | collective-permute-start | bytes 313352 | tf_op jit(solution)/shard_map/ppermute | solution.py:24
  6.7 10.8 %collective-permute-start.3 = (bf16[24,2176]{1,0:T(8,128)(2,1)S(1)}, bf16[24,2176]{1,0:T(8,128)(2,1)S(1)}, u32[]{:S(2)}, u32[]{:S(2)}) collective-permute-start(bf16[24,2176]{1,0:T(8,128)(2,1)S(1)} %get-tuple-element.47), channel_id=1, source_target_pairs={{0,6},{2,4},{4,2},{6,0},{1,7},{3,5},{5,3},{7,1},{8,14},{10,12},{12... | collective-permute-start | bytes 313352 | tf_op jit(solution)/shard_map/ppermute | solution.py:24
  10.3 8.8 %collective-permute-start.2 = (bf16[24,2176]{1,0:T(8,128)(2,1)S(1)}, bf16[24,2176]{1,0:T(8,128)(2,1)S(1)}, u32[]{:S(2)}, u32[]{:S(2)}) collective-permute-start(bf16[24,2176]{1,0:T(8,128)(2,1)S(1)} %get-tuple-element.47), channel_id=1, source_target_pairs={{0,4},{2,6},{4,0},{6,2},{1,5},{3,7},{5,1},{7,3},{8,12},{10,14},{12... | collective-permute-start | bytes 313352 | tf_op jit(solution)/shard_map/ppermute | solution.py:24
  10.3 8.8 %collective-permute-start.1 = (bf16[24,2176]{1,0:T(8,128)(2,1)S(1)}, bf16[24,2176]{1,0:T(8,128)(2,1)S(1)}, u32[]{:S(2)}, u32[]{:S(2)}) collective-permute-start(bf16[24,2176]{1,0:T(8,128)(2,1)S(1)} %get-tuple-element.47), channel_id=1, source_target_pairs={{0,2},{2,0},{4,6},{6,4},{1,3},{3,1},{5,7},{7,5},{8,10},{10,8},{12,... | collective-permute-start | bytes 313352 | tf_op jit(solution)/shard_map/ppermute | solution.py:24
  11.1 8.2 %collective-permute-start.6 = (bf16[24,2176]{1,0:T(8,128)(2,1)S(1)}, bf16[24,2176]{1,0:T(8,128)(2,1)S(1)}, u32[]{:S(2)}, u32[]{:S(2)}) collective-permute-start(bf16[24,2176]{1,0:T(8,128)(2,1)S(1)} %get-tuple-element.47), channel_id=1, source_target_pairs={{0,24},{8,16},{16,8},{24,0},{1,25},{9,17},{17,9},{25,1},{2,26},{10... | collective-permute-start | bytes 313352 | tf_op jit(solution)/shard_map/ppermute | solution.py:24
  12.6 6.7 %collective-permute-start.5 = (bf16[24,2176]{1,0:T(8,128)(2,1)S(1)}, bf16[24,2176]{1,0:T(8,128)(2,1)S(1)}, u32[]{:S(2)}, u32[]{:S(2)}) collective-permute-start(bf16[24,2176]{1,0:T(8,128)(2,1)S(1)} %get-tuple-element.47), channel_id=1, source_target_pairs={{0,16},{8,24},{16,0},{24,8},{1,17},{9,25},{17,1},{25,9},{2,18},{10... | collective-permute-start | bytes 313352 | tf_op jit(solution)/shard_map/ppermute | solution.py:24
  19.3 2.2 %collective-permute-start.7 = (bf16[168,2048]{1,0:T(8,128)(2,1)S(1)}, bf16[168,2048]{1,0:T(8,128)(2,1)S(1)}, u32[]{:S(2)}, u32[]{:S(2)}) collective-permute-start(bf16[168,2048]{1,0:T(8,128)(2,1)S(1)} %slice.79), channel_id=1, source_target_pairs={{0,1},{1,0},{2,3},{3,2},{4,5},{5,4},{6,7},{7,6},{8,9},{9,8},{10,11... | collective-permute-start | bytes 2064392 | tf_op jit(solution)/shard_map/ppermute | solution.py:24
  19.4 9.8 %collective-permute-start.9 = (bf16[72,2176]{1,0:T(8,128)(2,1)S(1)}, bf16[72,2176]{1,0:T(8,128)(2,1)S(1)}, u32[]{:S(2)}, u32[]{:S(2)}) collective-permute-start(bf16[72,2176]{1,0:T(8,128)(2,1)S(1)} %get-tuple-element.66), channel_id=1, source_target_pairs={{0,8},{8,0},{16,24},{24,16},{1,9},{9,1},{17,25},{25,17},{2,10},{10... | collective-permute-start | bytes 940040 | tf_op jit(solution)/shard_map/ppermute | solution.py:24
  20.0 9.5 %collective-permute-start.10 = (bf16[72,2176]{1,0:T(8,128)(2,1)S(1)}, bf16[72,2176]{1,0:T(8,128)(2,1)S(1)}, u32[]{:S(2)}, u32[]{:S(2)}) collective-permute-start(bf16[72,2176]{1,0:T(8,128)(2,1)S(1)} %get-tuple-element.66), channel_id=1, source_target_pairs={{0,16},{8,24},{16,0},{24,8},{1,17},{9,25},{17,1},{25,9},{2,18},{10... | collective-permute-start | bytes 940040 | tf_op jit(solution)/shard_map/ppermute | solution.py:24
  29.7 2.1 %collective-permute-start.11 = (bf16[144,2048]{1,0:T(8,128)(2,1)S(1)}, bf16[144,2048]{1,0:T(8,128)(2,1)S(1)}, u32[]{:S(2)}, u32[]{:S(2)}) collective-permute-start(bf16[144,2048]{1,0:T(8,128)(2,1)S(1)} %slice.81), channel_id=1, source_target_pairs={{0,1},{1,0},{2,3},{3,2},{4,5},{5,4},{6,7},{7,6},{8,9},{9,8},{10,11... | collective-permute-start | bytes 1769480 | tf_op jit(solution)/shard_map/ppermute | solution.py:24
  29.8 9.3 %collective-permute-start.8 = (bf16[168,2048]{1,0:T(8,128)(2,1)S(1)}, bf16[168,2048]{1,0:T(8,128)(2,1)S(1)}, u32[]{:S(2)}, u32[]{:S(2)}) collective-permute-start(bf16[168,2048]{1,0:T(8,128)(2,1)S(1)} %get-tuple-element.33), channel_id=1, source_target_pairs={{0,1},{1,0},{2,3},{3,2},{4,5},{5,4},{6,7},{7,6},{8,9},{9,8},{10,11... | collective-permute-start | bytes 2064392 | tf_op jit(solution)/shard_map/ppermute | solution.py:24
  30.3 6.9 %collective-permute-start.18 = (bf16[72,2176]{1,0:T(8,128)(2,1)S(1)}, bf16[72,2176]{1,0:T(8,128)(2,1)S(1)}, u32[]{:S(2)}, u32[]{:S(2)}) collective-permute-start(bf16[72,2176]{1,0:T(8,128)(2,1)S(1)} %get-tuple-element.57), channel_id=1, source_target_pairs={{0,16},{1,9},{8,24},{9,1},{16,0},{17,25},{24,8},{25,17},{2,18},{3,... | collective-permute-start | bytes 940040 | tf_op jit(solution)/shard_map/ppermute | solution.py:36
  35.4 3.9 %collective-permute-start.12 = (bf16[144,2048]{1,0:T(8,128)(2,1)S(1)}, bf16[144,2048]{1,0:T(8,128)(2,1)S(1)}, u32[]{:S(2)}, u32[]{:S(2)}) collective-permute-start(bf16[144,2048]{1,0:T(8,128)(2,1)S(1)} %get-tuple-element.38), channel_id=1, source_target_pairs={{0,1},{1,0},{2,3},{3,2},{4,5},{5,4},{6,7},{7,6},{8,9},{9,8},{10,11... | collective-permute-start | bytes 1769480 | tf_op jit(solution)/shard_map/ppermute | solution.py:24
  37.2 2.4 %collective-permute-start.19 = (bf16[72,2048]{1,0:T(8,128)(2,1)S(1)}, bf16[72,2048]{1,0:T(8,128)(2,1)S(1)}, u32[]{:S(2)}, u32[]{:S(2)}) collective-permute-start(bf16[72,2048]{1,0:T(8,128)(2,1)S(1)} %slice.69), channel_id=1, source_target_pairs={{0,1},{1,0},{2,3},{3,2},{4,5},{5,4},{6,7},{7,6},{8,9},{9,8},{10,11... | collective-permute-start | bytes 884744 | tf_op jit(solution)/shard_map/ppermute | solution.py:24
  42.0 4.8 %collective-permute-start.20 = (bf16[72,2048]{1,0:T(8,128)(2,1)S(1)}, bf16[72,2048]{1,0:T(8,128)(2,1)S(1)}, u32[]{:S(2)}, u32[]{:S(2)}) collective-permute-start(bf16[72,2048]{1,0:T(8,128)(2,1)S(1)} %get-tuple-element.42), channel_id=1, source_target_pairs={{0,1},{1,0},{2,3},{3,2},{4,5},{5,4},{6,7},{7,6},{8,9},{9,8},{10,11... | collective-permute-start | bytes 884744 | tf_op jit(solution)/shard_map/ppermute | solution.py:24
  42.5 11.1 %collective-permute-start.13 = (bf16[96,2048]{1,0:T(8,128)(2,1)S(1)}, bf16[96,2048]{1,0:T(8,128)(2,1)S(1)}, u32[]{:S(2)}, u32[]{:S(2)}) collective-permute-start(bf16[96,2048]{1,0:T(8,128)(2,1)S(1)} %pad_maximum_fusion), channel_id=1, source_target_pairs={{0,8},{8,0},{16,24},{24,16},{1,9},{9,1},{17,25},{25,17},{2,10},{10... | collective-permute-start | bytes 1179656 | tf_op jit(solution)/shard_map/ppermute | solution.py:24
  44.0 10.8 %collective-permute-start.14 = (bf16[96,2048]{1,0:T(8,128)(2,1)S(1)}, bf16[96,2048]{1,0:T(8,128)(2,1)S(1)}, u32[]{:S(2)}, u32[]{:S(2)}) collective-permute-start(bf16[96,2048]{1,0:T(8,128)(2,1)S(1)} %pad_maximum_fusion.1), channel_id=1, source_target_pairs={{0,16},{8,24},{16,0},{24,8},{1,17},{9,25},{17,1},{25,9},{2,18},{10... | collective-permute-start | bytes 1179656 | tf_op jit(solution)/shard_map/ppermute | solution.py:24
  46.9 8.1 %collective-permute-start.23 = (bf16[24,2048]{1,0:T(8,128)(2,1)S(1)}, bf16[24,2048]{1,0:T(8,128)(2,1)S(1)}, u32[]{:S(2)}, u32[]{:S(2)}) collective-permute-start(bf16[24,2048]{1,0:T(8,128)(2,1)S(1)} %get-tuple-element.58), channel_id=1, source_target_pairs={{0,2},{2,0},{4,6},{6,4},{1,3},{3,1},{5,7},{7,5},{8,10},{10,8},{12,... | collective-permute-start | bytes 294920 | tf_op jit(solution)/shard_map/ppermute | solution.py:24
  47.3 10.2 %collective-permute-start.22 = (bf16[24,2048]{1,0:T(8,128)(2,1)S(1)}, bf16[24,2048]{1,0:T(8,128)(2,1)S(1)}, u32[]{:S(2)}, u32[]{:S(2)}) collective-permute-start(bf16[24,2048]{1,0:T(8,128)(2,1)S(1)} %get-tuple-element.59), channel_id=1, source_target_pairs={{0,4},{2,6},{4,0},{6,2},{1,5},{3,7},{5,1},{7,3},{8,12},{10,14},{12... | collective-permute-start | bytes 294920 | tf_op jit(solution)/shard_map/ppermute | solution.py:24
  50.0 13.1 %copy-start = (s32[8]{0:T(128)S(1)}, s32[8]{0:T(128)}, u32[]{:S(2)}) copy-start(s32[8]{0:T(128)} %refs_0_.3) | copy-start | bytes 100
  50.0 7.6 %collective-permute-start.21 = (bf16[24,2048]{1,0:T(8,128)(2,1)S(1)}, bf16[24,2048]{1,0:T(8,128)(2,1)S(1)}, u32[]{:S(2)}, u32[]{:S(2)}) collective-permute-start(bf16[24,2048]{1,0:T(8,128)(2,1)S(1)} %get-tuple-element.60), channel_id=1, source_target_pairs={{0,6},{2,4},{4,2},{6,0},{1,7},{3,5},{5,3},{7,1},{8,14},{10,12},{12... | collective-permute-start | bytes 294920 | tf_op jit(solution)/shard_map/ppermute | solution.py:24
  57.6 7.0 %collective-permute-start.24 = (bf16[24,2048]{1,0:T(8,128)(2,1)S(1)}, bf16[24,2048]{1,0:T(8,128)(2,1)S(1)}, u32[]{:S(2)}, u32[]{:S(2)}) collective-permute-start(bf16[24,2048]{1,0:T(8,128)(2,1)S(1)} %add_convert_fusion.4), channel_id=1, source_target_pairs={{0,24},{8,16},{16,8},{24,0},{1,25},{9,17},{17,9},{25,1},{2,26},{10... | collective-permute-start | bytes 294920 | tf_op jit(solution)/shard_map/ppermute | solution.py:24
  58.7 5.9 %collective-permute-start.17 = (bf16[24,2048]{1,0:T(8,128)(2,1)S(1)}, bf16[24,2048]{1,0:T(8,128)(2,1)S(1)}, u32[]{:S(2)}, u32[]{:S(2)}) collective-permute-start(bf16[24,2048]{1,0:T(8,128)(2,1)S(1)} %get-tuple-element.53), channel_id=1, source_target_pairs={{0,2},{2,0},{4,6},{6,4},{1,3},{3,1},{5,7},{7,5},{8,10},{10,8},{12,... | collective-permute-start | bytes 294920 | tf_op jit(solution)/shard_map/ppermute | solution.py:24
  60.3 9.0 %collective-permute-start.16 = (bf16[24,2048]{1,0:T(8,128)(2,1)S(1)}, bf16[24,2048]{1,0:T(8,128)(2,1)S(1)}, u32[]{:S(2)}, u32[]{:S(2)}) collective-permute-start(bf16[24,2048]{1,0:T(8,128)(2,1)S(1)} %get-tuple-element.54), channel_id=1, source_target_pairs={{0,4},{2,6},{4,0},{6,2},{1,5},{3,7},{5,1},{7,3},{8,12},{10,14},{12... | collective-permute-start | bytes 294920 | tf_op jit(solution)/shard_map/ppermute | solution.py:24
  61.7 7.6 %collective-permute-start.15 = (bf16[24,2048]{1,0:T(8,128)(2,1)S(1)}, bf16[24,2048]{1,0:T(8,128)(2,1)S(1)}, u32[]{:S(2)}, u32[]{:S(2)}) collective-permute-start(bf16[24,2048]{1,0:T(8,128)(2,1)S(1)} %get-tuple-element.55), channel_id=1, source_target_pairs={{0,6},{2,4},{4,2},{6,0},{1,7},{3,5},{5,3},{7,1},{8,14},{10,12},{12... | collective-permute-start | bytes 294920 | tf_op jit(solution)/shard_map/ppermute | solution.py:24
  69.4 1.3 %collective-permute-start.25 = (bf16[12,2048]{1,0:T(8,128)(2,1)S(1)}, bf16[12,2048]{1,0:T(8,128)(2,1)S(1)}, u32[]{:S(2)}, u32[]{:S(2)}) collective-permute-start(bf16[12,2048]{1,0:T(8,128)(2,1)S(1)} %broadcast_select_fusion.5), channel_id=1, source_target_pairs={{0,1},{1,0},{2,3},{3,2},{4,5},{5,4},{6,7},{7,6},{8,9},{9,8},{10,11... | collective-permute-start | bytes 147464 | tf_op jit(solution)/shard_map/ppermute | solution.py:24

commit v19 on v18

--- a/solution.py
+++ b/solution.py
@@ -27,13 +27,6 @@
 def spread_near(block):
     size = lax.axis_size("dp")
     return [swap(block, "dp", k) for k in range(1, 3 if size == 4 else size)]
-
-
-def cross(value):
-    pairs = []
-    for i in range(4):
-        pairs += [(2 * i, 2 * (i ^ 2)), (2 * i + 1, 2 * (i ^ 1) + 1)]
-    return row_major(lax.ppermute(row_major(value), ("dp", "core"), pairs))
 
 
 def behind(values, others):
@@ -367,6 +360,9 @@
     far = row_major(jnp.concatenate(chip_blocks[1:], 0))
     held = row_major(jnp.concatenate([*chip_blocks, *direct], 0))
     near = spread_near(far)
+    if groups == 4:
+        fourth_rows = [swap(direct[2], "chip", j) for j in range(chips - 1, 0, -1)]
+        fourth_rows = jnp.concatenate(fourth_rows[::-1], 0)
     weights = [up, out_weight.reshape(per_device * half_width, width)]
     pieces = [held]
     if held.shape[0] > MOST_ROWS:
@@ -391,17 +387,15 @@
         return [swap(blocks[j - 1], "chip", j) for j in range(chips - 1, 0, -1)]
 
     if groups == 4:
-        rest = cross(jnp.where(first, near[0], near[1]))
-        near = row_major(jnp.concatenate(near, 0))
-        keep, give = sums_of(near, weights)
-        far_sums += [*jnp.split(chip_sums(keep, give), 2)]
-        whole = [jnp.concatenate(pair, 0) for pair in zip(near_sums, far_sums)]
-        rest = behind(rest, give)
-        other = behind(swap(rest[:, :part], "core", 1), whole[1:3])
+        rest = row_major(jnp.concatenate([*near, fourth_rows], 0))
+        other = swap(rest[:, :part], "core", 1)
         keep, give = gated_sums_in_steps(place, top_count, rest, other, *weights)
-        fourth = parts(added(keep, swap(give, "core", 1)))
+        pair = added(keep, swap(give, "core", 1))
+        far_sums += [*jnp.split(pair, 3)]
+        whole = [jnp.concatenate(blocks, 0) for blocks in zip(near_sums, far_sums[:3])]
+        fourth = parts(far_sums[3])
         fourth = along_chips(fourth)
-        metas = [held, near, rest]
+        metas = [held, rest]
     else:
         far_sums += [chip_sums(*sums_of(block, weights)) for block in near]
         whole = [jnp.concatenate(pair, 0) for pair in zip(near_sums, far_sums)]

time: 71.7 us -> 70.4 us (0.982)
  Pallas kernels: 23.1 us -> 20.8 us
  starting transfers between devices: 27.7 us -> 29.6 us
  waiting for transfers between devices: 17.2 us -> 16.4 us
    ppermute x25 -> x26, starting transfers between devices: 26.2 us -> 29.6 us  [swap(): return row_major(lax.ppermute(row_major(value), axis, pairs))]
    pallas_call x5 -> x4, Pallas kernels: 15.4 us -> 13 us  [call(): pl.pallas_call(kernel, in_specs=[pl.BlockSpec(memory_space=pltpu.SMEM)] +...]
    ppermute x1 -> x0, waiting for transfers between devices: 1.58 us -> none  [cross(): return row_major(lax.ppermute(row_major(value), ('dp', 'core'), pairs))]
    ppermute x1 -> x0, starting transfers between devices: 1.52 us -> none  [cross(): return row_major(lax.ppermute(row_major(value), ('dp', 'core'), pairs))]
    ppermute x25 -> x26, waiting for transfers between devices: 15.6 us -> 16.4 us  [swap(): return row_major(lax.ppermute(row_major(value), axis, pairs))]
  transfers between devices with their start and end apart: 26 -> 26, of which waited for: 10 -> 8; matrix products, arithmetic and copies ran while one was open for 2% -> 2% of each run, Pallas kernels for 27% -> 27%
where the time goes in v19:
time: 70.4 us; the launch traced here: 70.2 us
  starting transfers between devices  29.6 us (42%)
  Pallas kernels  20.8 us (30%)
  waiting for transfers between devices  16.4 us (23%)
  other arithmetic  1.4 us (2%)
  local copies, waits for them, and re-layouts  1.02 us (1%)
  between operations  0.98 us (1%)
    ppermute x26, starting transfers between devices, swap(): return row_major(lax.ppermute(row_major(value), axis, pairs))  29.6 us
    ppermute x26, waiting for transfers between devices, swap(): return row_major(lax.ppermute(row_major(value), axis, pairs))  16.4 us
    pallas_call x4, Pallas kernels, call(): pl.pallas_call(kernel, in_specs=[pl.BlockSpec(memory_space=pltpu.SMEM)] +...  13 us
    pallas_call x1, Pallas kernels, loaded(): pl.pallas_call(load_weight_kernel, in_specs=[pl.BlockSpec(memory_space=pl...  4.58 us
    pallas_call x1, Pallas kernels, first_halves(): pl.pallas_call(first_kernel, in_specs=[pl.BlockSpec(memory_space=pltpu.SM...  1.56 us
    pallas_call x1, Pallas kernels, planned_load(): pl.pallas_call(lambda *refs: load_kernel(layout, *refs), in_specs=[pl.Blo...  1.44 us
  transfers between devices with their start and end apart: 26, of which 8 were waited for; matrix products, arithmetic and copies ran while one was open for 2% of the time, Pallas kernels for 27%

profile of v19, /device:TPU:0, one launch (start us, length us, event | category | flops | bytes accessed | tf_op | source)
XLA Modules:
  0.0 70.2 jit_solution(2800299417636480668)
XLA Ops:
  0.6 0.1 pad_add_fusion.place.refs_0_
  0.7 1.6 %shard_map.77 = (bf16[12,2176]{1,0:T(8,128)(2,1)S(1)}, bf16[12,2176]{1,0:T(8,128)(2,1)S(1)}) custom-call(s32[2]{0:T(128)S(1)} %pad_add_fusion.place.refs_0_, bf16[12,4096]{1,0:T(8,128)(2,1)} %refs_0_.2, s32[8,12]{1,0:T(8,128)} %bitcast.8, f32[8,12]{1,0:T(8,128)} %bitcast.9), custom_call_target="tpu_custom_call" | custom-call | tf_op jit(solution)/shard_map/pallas_call | solution.py:246
  2.3 0.5 collective-permute-start
  2.8 0.9 %collective-permute-done = bf16[12,2176]{1,0:T(8,128)(2,1)S(1)} collective-permute-done((bf16[12,2176]{1,0:T(8,128)(2,1)S(1)}, bf16[12,2176]{1,0:T(8,128)(2,1)S(1)}, u32[]{:S(2)}, u32[]{:S(2)}) %collective-permute-start) | collective-permute-done | bytes 52256 | tf_op jit(solution)/shard_map/ppermute | solution.py:24
  3.8 2.9 %collective-permute-start.4 = (bf16[24,2176]{1,0:T(8,128)(2,1)S(1)}, bf16[24,2176]{1,0:T(8,128)(2,1)S(1)}, u32[]{:S(2)}, u32[]{:S(2)}) collective-permute-start(bf16[24,2176]{1,0:T(8,128)(2,1)S(1)} %get-tuple-element.39), channel_id=1, source_target_pairs={{0,8},{8,0},{16,24},{24,16},{1,9},{9,1},{17,25},{25,17},{2,10},{10... | collective-permute-start | bytes 313352 | tf_op jit(solution)/shard_map/ppermute | solution.py:24
  6.7 3.6 %collective-permute-start.3 = (bf16[24,2176]{1,0:T(8,128)(2,1)S(1)}, bf16[24,2176]{1,0:T(8,128)(2,1)S(1)}, u32[]{:S(2)}, u32[]{:S(2)}) collective-permute-start(bf16[24,2176]{1,0:T(8,128)(2,1)S(1)} %get-tuple-element.39), channel_id=1, source_target_pairs={{0,6},{2,4},{4,2},{6,0},{1,7},{3,5},{5,3},{7,1},{8,14},{10,12},{12... | collective-permute-start | bytes 313352 | tf_op jit(solution)/shard_map/ppermute | solution.py:24
  10.3 0.8 %collective-permute-start.1 = (bf16[24,2176]{1,0:T(8,128)(2,1)S(1)}, bf16[24,2176]{1,0:T(8,128)(2,1)S(1)}, u32[]{:S(2)}, u32[]{:S(2)}) collective-permute-start(bf16[24,2176]{1,0:T(8,128)(2,1)S(1)} %get-tuple-element.39), channel_id=1, source_target_pairs={{0,2},{2,0},{4,6},{6,4},{1,3},{3,1},{5,7},{7,5},{8,10},{10,8},{12,... | collective-permute-start | bytes 313352 | tf_op jit(solution)/shard_map/ppermute | solution.py:24
  11.1 1.5 %collective-permute-start.6 = (bf16[24,2176]{1,0:T(8,128)(2,1)S(1)}, bf16[24,2176]{1,0:T(8,128)(2,1)S(1)}, u32[]{:S(2)}, u32[]{:S(2)}) collective-permute-start(bf16[24,2176]{1,0:T(8,128)(2,1)S(1)} %get-tuple-element.39), channel_id=1, source_target_pairs={{0,24},{8,16},{16,8},{24,0},{1,25},{9,17},{17,9},{25,1},{2,26},{10... | collective-permute-start | bytes 313352 | tf_op jit(solution)/shard_map/ppermute | solution.py:24
  12.6 0.3 collective-permute-start.5
  12.8 4.6 %shard_map.78 = (bf16[2,4096,768]{2,1,0:T(8,128)(2,1)S(1)}, f32[8,128]{1,0:T(8,128)S(1)}) custom-call(bf16[2,4096,768]{2,1,0:T(8,128)(2,1)} %weight_ref.1, bf16[24,2176]{1,0:T(8,128)(2,1)S(1)} %collective-permute-done.4._), custom_call_target="tpu_custom_call" | custom-call | bytes 12582912 | tf_op jit(solution)/shard_map/pallas_call | solution.py:56
  17.4 1.7 %collective-permute-done.2 = bf16[24,2176]{1,0:T(8,128)(2,1)S(1)} collective-permute-done((bf16[24,2176]{1,0:T(8,128)(2,1)S(1)}, bf16[24,2176]{1,0:T(8,128)(2,1)S(1)}, u32[]{:S(2)}, u32[]{:S(2)}) %collective-permute-start.2) | collective-permute-done | bytes 104480 | tf_op jit(solution)/shard_map/ppermute | solution.py:24
  19.3 0.1 collective-permute-start.7
  19.4 0.6 collective-permute-start.9
  20.0 1.5 %collective-permute-start.10 = (bf16[72,2176]{1,0:T(8,128)(2,1)S(1)}, bf16[72,2176]{1,0:T(8,128)(2,1)S(1)}, u32[]{:S(2)}, u32[]{:S(2)}) collective-permute-start(bf16[72,2176]{1,0:T(8,128)(2,1)S(1)} %get-tuple-element.56), channel_id=1, source_target_pairs={{0,16},{8,24},{16,0},{24,8},{1,17},{9,25},{17,1},{25,9},{2,18},{10... | collective-permute-start | bytes 940040 | tf_op jit(solution)/shard_map/ppermute | solution.py:24
  21.5 1.7 %collective-permute-start.12 = (bf16[24,2176]{1,0:T(8,128)(2,1)S(1)}, bf16[24,2176]{1,0:T(8,128)(2,1)S(1)}, u32[]{:S(2)}, u32[]{:S(2)}) collective-permute-start(bf16[24,2176]{1,0:T(8,128)(2,1)S(1)} %collective-permute-done.6), channel_id=1, source_target_pairs={{0,4},{2,6},{4,0},{6,2},{1,5},{3,7},{5,1},{7,3},{8,12},{10,14},{12... | collective-permute-start | bytes 313352 | tf_op jit(solution)/shard_map/ppermute | solution.py:24
  23.2 2.0 %collective-permute-start.11 = (bf16[24,2176]{1,0:T(8,128)(2,1)S(1)}, bf16[24,2176]{1,0:T(8,128)(2,1)S(1)}, u32[]{:S(2)}, u32[]{:S(2)}) collective-permute-start(bf16[24,2176]{1,0:T(8,128)(2,1)S(1)} %collective-permute-done.6), channel_id=1, source_target_pairs={{0,2},{2,0},{4,6},{6,4},{1,3},{3,1},{5,7},{7,5},{8,10},{10,8},{12,... | collective-permute-start | bytes 313352 | tf_op jit(solution)/shard_map/ppermute | solution.py:24
  25.2 0.7 collective-permute-start.13
  25.9 6.5 %shard_map.79 = (bf16[168,2048]{1,0:T(8,128)(2,1)S(1)}, bf16[168,2048]{1,0:T(8,128)(2,1)S(1)}, bf16[768,4096]{1,0:T(8,128)(2,1)S(1)}) custom-call(s32[2]{0:T(128)S(1)} %pad_add_fusion.place.refs_0_, bf16[168,2176]{1,0:T(8,128)(2,1)S(1)} %constant_dynamic-update-slice_fusion.refs_1_, bf16[168,2048]{1,0:T(8,128)(2,1)S(1)} %collective-permute-done.7.refs_2_, ...), custom_call_target="tpu_custom_call" | custom-call | flops 3170893824 | tf_op jit(solution)/shard_map/pallas_call | solution.py:147
  32.6 0.1 slice.76
  32.7 0.1 collective-permute-start.14
  32.8 0.5 collective-permute-start.8
  33.3 2.1 %shard_map.80.refs_3_ = f32[2,216,768]{2,1,0:T(8,128)S(1)} custom-call(s32[2]{0:T(128)S(1)} %pad_add_fusion.place.refs_0_, bf16[216,2176]{1,0:T(8,128)(2,1)S(1)} %constant_dynamic-update-slice_fusion.10.own.refs_1_, bf16[2,4096,768]{2,1,0:T(8,128)(2,1)S(1)} %get-tuple-element.26.refs_3_.up.refs_4_), custom_call_target="tpu_custom_call" | custom-call | flops 1358954496 | tf_op jit(solution)/shard_map/pallas_call | solution.py:147
  35.4 3.0 %shard_map.81 = (bf16[216,2048]{1,0:T(8,128)(2,1)S(1)}, bf16[216,768]{1,0:T(8,128)(2,1)S(1)}) custom-call(s32[2]{0:T(128)S(1)} %pad_add_fusion.place.refs_0_, bf16[216,2176]{1,0:T(8,128)(2,1)S(1)} %constant_dynamic-update-slice_fusion.10.own.refs_1_, bf16[216,2048]{1,0:T(8,128)(2,1)S(1)} %collective-permute-done.14.refs_2_, ...), custom_call_target="tpu_custom_call" | custom-call | flops 2038431744 | tf_op jit(solution)/shard_map/pallas_call | solution.py:147
  38.4 0.1 collective-permute-start.15
  38.6 0.2 add_convert_fusion
  38.8 1.4 %shard_map.82.kept_ref = bf16[216,2048]{1,0:T(8,128)(2,1)S(1)} custom-call(s32[2]{0:T(128)S(1)} %pad_add_fusion.place.refs_0_, bf16[216,768]{1,0:T(8,128)(2,1)S(1)} %get-tuple-element.33.hidden, bf16[768,4096]{1,0:T(8,128)(2,1)S(1)} %get-tuple-element.32.refs_5_.down), custom_call_target="tpu_custom_call" | custom-call | flops 679477248 | tf_op jit(solution)/shard_map/pallas_call | solution.py:147
  40.3 0.6 collective-permute-done.15.taken_ref
  40.9 0.2 shard_map.83
  41.2 0.6 collective-permute-start.17
  41.8 1.6 %collective-permute-start.16 = (bf16[96,2048]{1,0:T(8,128)(2,1)S(1)}, bf16[96,2048]{1,0:T(8,128)(2,1)S(1)}, u32[]{:S(2)}, u32[]{:S(2)}) collective-permute-start(bf16[96,2048]{1,0:T(8,128)(2,1)S(1)} %pad_maximum_fusion), channel_id=1, source_target_pairs={{0,8},{8,0},{16,24},{24,16},{1,9},{9,1},{17,25},{25,17},{2,10},{10... | collective-permute-start | bytes 1179656 | tf_op jit(solution)/shard_map/ppermute | solution.py:24
  43.4 1.8 %collective-permute-start.23 = (bf16[24,2048]{1,0:T(8,128)(2,1)S(1)}, bf16[24,2048]{1,0:T(8,128)(2,1)S(1)}, u32[]{:S(2)}, u32[]{:S(2)}) collective-permute-start(bf16[24,2048]{1,0:T(8,128)(2,1)S(1)} %get-tuple-element.42), channel_id=1, source_target_pairs={{0,2},{2,0},{4,6},{6,4},{1,3},{3,1},{5,7},{7,5},{8,10},{10,8},{12,... | collective-permute-start | bytes 294920 | tf_op jit(solution)/shard_map/ppermute | solution.py:24
  45.2 1.3 %collective-permute-start.22 = (bf16[24,2048]{1,0:T(8,128)(2,1)S(1)}, bf16[24,2048]{1,0:T(8,128)(2,1)S(1)}, u32[]{:S(2)}, u32[]{:S(2)}) collective-permute-start(bf16[24,2048]{1,0:T(8,128)(2,1)S(1)} %get-tuple-element.43), channel_id=1, source_target_pairs={{0,4},{2,6},{4,0},{6,2},{1,5},{3,7},{5,1},{7,3},{8,12},{10,14},{12... | collective-permute-start | bytes 294920 | tf_op jit(solution)/shard_map/ppermute | solution.py:24
  46.5 1.3 %collective-permute-start.21 = (bf16[24,2048]{1,0:T(8,128)(2,1)S(1)}, bf16[24,2048]{1,0:T(8,128)(2,1)S(1)}, u32[]{:S(2)}, u32[]{:S(2)}) collective-permute-start(bf16[24,2048]{1,0:T(8,128)(2,1)S(1)} %get-tuple-element.44), channel_id=1, source_target_pairs={{0,6},{2,4},{4,2},{6,0},{1,7},{3,5},{5,3},{7,1},{8,14},{10,12},{12... | collective-permute-start | bytes 294920 | tf_op jit(solution)/shard_map/ppermute | solution.py:24
  47.8 4.6 %collective-permute-done.17 = bf16[96,2048]{1,0:T(8,128)(2,1)S(1)} collective-permute-done((bf16[96,2048]{1,0:T(8,128)(2,1)S(1)}, bf16[96,2048]{1,0:T(8,128)(2,1)S(1)}, u32[]{:S(2)}, u32[]{:S(2)}) %collective-permute-start.17) | collective-permute-done | bytes 393248 | tf_op jit(solution)/shard_map/ppermute | solution.py:24
  52.4 0.3 collective-permute-done.16
  52.7 0.1 add_convert_fusion.1
  52.9 2.4 %collective-permute-done.22 = bf16[24,2048]{1,0:T(8,128)(2,1)S(1)} collective-permute-done((bf16[24,2048]{1,0:T(8,128)(2,1)S(1)}, bf16[24,2048]{1,0:T(8,128)(2,1)S(1)}, u32[]{:S(2)}, u32[]{:S(2)}) %collective-permute-start.22) | collective-permute-done | bytes 98336 | tf_op jit(solution)/shard_map/ppermute | solution.py:24
  55.4 1.7 %collective-permute-start.24 = (bf16[24,2048]{1,0:T(8,128)(2,1)S(1)}, bf16[24,2048]{1,0:T(8,128)(2,1)S(1)}, u32[]{:S(2)}, u32[]{:S(2)}) collective-permute-start(bf16[24,2048]{1,0:T(8,128)(2,1)S(1)} %add_convert_fusion.3), channel_id=1, source_target_pairs={{0,24},{8,16},{16,8},{24,0},{1,25},{9,17},{17,9},{25,1},{2,26},{10... | collective-permute-start | bytes 294920 | tf_op jit(solution)/shard_map/ppermute | solution.py:24
  57.1 1.6 %collective-permute-start.20 = (bf16[24,2048]{1,0:T(8,128)(2,1)S(1)}, bf16[24,2048]{1,0:T(8,128)(2,1)S(1)}, u32[]{:S(2)}, u32[]{:S(2)}) collective-permute-start(bf16[24,2048]{1,0:T(8,128)(2,1)S(1)} %get-tuple-element.48), channel_id=1, source_target_pairs={{0,2},{2,0},{4,6},{6,4},{1,3},{3,1},{5,7},{7,5},{8,10},{10,8},{12,... | collective-permute-start | bytes 294920 | tf_op jit(solution)/shard_map/ppermute | solution.py:24
  58.7 1.5 %collective-permute-start.19 = (bf16[24,2048]{1,0:T(8,128)(2,1)S(1)}, bf16[24,2048]{1,0:T(8,128)(2,1)S(1)}, u32[]{:S(2)}, u32[]{:S(2)}) collective-permute-start(bf16[24,2048]{1,0:T(8,128)(2,1)S(1)} %get-tuple-element.49), channel_id=1, source_target_pairs={{0,4},{2,6},{4,0},{6,2},{1,5},{3,7},{5,1},{7,3},{8,12},{10,14},{12... | collective-permute-start | bytes 294920 | tf_op jit(solution)/shard_map/ppermute | solution.py:24
  60.2 1.3 %collective-permute-start.18 = (bf16[24,2048]{1,0:T(8,128)(2,1)S(1)}, bf16[24,2048]{1,0:T(8,128)(2,1)S(1)}, u32[]{:S(2)}, u32[]{:S(2)}) collective-permute-start(bf16[24,2048]{1,0:T(8,128)(2,1)S(1)} %get-tuple-element.50), channel_id=1, source_target_pairs={{0,6},{2,4},{4,2},{6,0},{1,7},{3,5},{5,3},{7,1},{8,14},{10,12},{12... | collective-permute-start | bytes 294920 | tf_op jit(solution)/shard_map/ppermute | solution.py:24
  61.5 1.4 %shard_map.84 = f32[1,128]{1,0:T(1,128)S(1)} custom-call(s32[8]{0:T(128)S(1)} %copy-done, bf16[168,128]{1,0:T(8,128)(2,1)S(1)} %slice.88.refs_1_, bf16[216,128]{1,0:T(8,128)(2,1)S(1)} %slice.89.refs_2_, bf16[24,2048]{1,0:T(8,128)(2,1)S(1)} %get-tuple-element.47.refs_3_), custom_call_target="tpu_custom_call" | custom-call | bytes 98304 | tf_op jit(solution)/shard_map/pallas_call | solution.py:314
  63.0 5.1 %collective-permute-done.19 = bf16[24,2048]{1,0:T(8,128)(2,1)S(1)} collective-permute-done((bf16[24,2048]{1,0:T(8,128)(2,1)S(1)}, bf16[24,2048]{1,0:T(8,128)(2,1)S(1)}, u32[]{:S(2)}, u32[]{:S(2)}) %collective-permute-start.19) | collective-permute-done | bytes 98336 | tf_op jit(solution)/shard_map/ppermute | solution.py:24
  68.1 0.1 add_convert_fusion.2
  68.2 0.1 collective-permute-start.25
  68.2 0.5 slice_bitcast_fusion
  68.8 0.7 %collective-permute-done.25 = bf16[12,2048]{1,0:T(8,128)(2,1)S(1)} collective-permute-done((bf16[12,2048]{1,0:T(8,128)(2,1)S(1)}, bf16[12,2048]{1,0:T(8,128)(2,1)S(1)}, u32[]{:S(2)}, u32[]{:S(2)}) %collective-permute-start.25) | collective-permute-done | bytes 49184 | tf_op jit(solution)/shard_map/ppermute | solution.py:24
  69.5 0.7 pad_maximum_fusion.2
  (46 shorter events, 0.7 us)
Async XLA Ops:
  2.3 1.4 %collective-permute-start = (bf16[12,2176]{1,0:T(8,128)(2,1)S(1)}, bf16[12,2176]{1,0:T(8,128)(2,1)S(1)}, u32[]{:S(2)}, u32[]{:S(2)}) collective-permute-start(bf16[12,2176]{1,0:T(8,128)(2,1)S(1)} %get-tuple-element.21), channel_id=1, source_target_pairs={{0,1},{1,0},{2,3},{3,2},{4,5},{5,4},{6,7},{7,6},{8,9},{9,8},{10,11... | collective-permute-start | bytes 156680 | tf_op jit(solution)/shard_map/ppermute | solution.py:24
  3.8 8.8 %collective-permute-start.4 = (bf16[24,2176]{1,0:T(8,128)(2,1)S(1)}, bf16[24,2176]{1,0:T(8,128)(2,1)S(1)}, u32[]{:S(2)}, u32[]{:S(2)}) collective-permute-start(bf16[24,2176]{1,0:T(8,128)(2,1)S(1)} %get-tuple-element.39), channel_id=1, source_target_pairs={{0,8},{8,0},{16,24},{24,16},{1,9},{9,1},{17,25},{25,17},{2,10},{10... | collective-permute-start | bytes 313352 | tf_op jit(solution)/shard_map/ppermute | solution.py:24
  6.7 10.8 %collective-permute-start.3 = (bf16[24,2176]{1,0:T(8,128)(2,1)S(1)}, bf16[24,2176]{1,0:T(8,128)(2,1)S(1)}, u32[]{:S(2)}, u32[]{:S(2)}) collective-permute-start(bf16[24,2176]{1,0:T(8,128)(2,1)S(1)} %get-tuple-element.39), channel_id=1, source_target_pairs={{0,6},{2,4},{4,2},{6,0},{1,7},{3,5},{5,3},{7,1},{8,14},{10,12},{12... | collective-permute-start | bytes 313352 | tf_op jit(solution)/shard_map/ppermute | solution.py:24
  10.3 8.8 %collective-permute-start.2 = (bf16[24,2176]{1,0:T(8,128)(2,1)S(1)}, bf16[24,2176]{1,0:T(8,128)(2,1)S(1)}, u32[]{:S(2)}, u32[]{:S(2)}) collective-permute-start(bf16[24,2176]{1,0:T(8,128)(2,1)S(1)} %get-tuple-element.39), channel_id=1, source_target_pairs={{0,4},{2,6},{4,0},{6,2},{1,5},{3,7},{5,1},{7,3},{8,12},{10,14},{12... | collective-permute-start | bytes 313352 | tf_op jit(solution)/shard_map/ppermute | solution.py:24
  10.3 8.8 %collective-permute-start.1 = (bf16[24,2176]{1,0:T(8,128)(2,1)S(1)}, bf16[24,2176]{1,0:T(8,128)(2,1)S(1)}, u32[]{:S(2)}, u32[]{:S(2)}) collective-permute-start(bf16[24,2176]{1,0:T(8,128)(2,1)S(1)} %get-tuple-element.39), channel_id=1, source_target_pairs={{0,2},{2,0},{4,6},{6,4},{1,3},{3,1},{5,7},{7,5},{8,10},{10,8},{12,... | collective-permute-start | bytes 313352 | tf_op jit(solution)/shard_map/ppermute | solution.py:24
  11.1 8.2 %collective-permute-start.6 = (bf16[24,2176]{1,0:T(8,128)(2,1)S(1)}, bf16[24,2176]{1,0:T(8,128)(2,1)S(1)}, u32[]{:S(2)}, u32[]{:S(2)}) collective-permute-start(bf16[24,2176]{1,0:T(8,128)(2,1)S(1)} %get-tuple-element.39), channel_id=1, source_target_pairs={{0,24},{8,16},{16,8},{24,0},{1,25},{9,17},{17,9},{25,1},{2,26},{10... | collective-permute-start | bytes 313352 | tf_op jit(solution)/shard_map/ppermute | solution.py:24
  12.6 6.7 %collective-permute-start.5 = (bf16[24,2176]{1,0:T(8,128)(2,1)S(1)}, bf16[24,2176]{1,0:T(8,128)(2,1)S(1)}, u32[]{:S(2)}, u32[]{:S(2)}) collective-permute-start(bf16[24,2176]{1,0:T(8,128)(2,1)S(1)} %get-tuple-element.39), channel_id=1, source_target_pairs={{0,16},{8,24},{16,0},{24,8},{1,17},{9,25},{17,1},{25,9},{2,18},{10... | collective-permute-start | bytes 313352 | tf_op jit(solution)/shard_map/ppermute | solution.py:24
  19.3 5.9 %collective-permute-start.7 = (bf16[168,2048]{1,0:T(8,128)(2,1)S(1)}, bf16[168,2048]{1,0:T(8,128)(2,1)S(1)}, u32[]{:S(2)}, u32[]{:S(2)}) collective-permute-start(bf16[168,2048]{1,0:T(8,128)(2,1)S(1)} %slice.74), channel_id=1, source_target_pairs={{0,1},{1,0},{2,3},{3,2},{4,5},{5,4},{6,7},{7,6},{8,9},{9,8},{10,11... | collective-permute-start | bytes 2064392 | tf_op jit(solution)/shard_map/ppermute | solution.py:24
  19.4 13.0 %collective-permute-start.9 = (bf16[72,2176]{1,0:T(8,128)(2,1)S(1)}, bf16[72,2176]{1,0:T(8,128)(2,1)S(1)}, u32[]{:S(2)}, u32[]{:S(2)}) collective-permute-start(bf16[72,2176]{1,0:T(8,128)(2,1)S(1)} %get-tuple-element.56), channel_id=1, source_target_pairs={{0,8},{8,0},{16,24},{24,16},{1,9},{9,1},{17,25},{25,17},{2,10},{10... | collective-permute-start | bytes 940040 | tf_op jit(solution)/shard_map/ppermute | solution.py:24
  20.0 12.4 %collective-permute-start.10 = (bf16[72,2176]{1,0:T(8,128)(2,1)S(1)}, bf16[72,2176]{1,0:T(8,128)(2,1)S(1)}, u32[]{:S(2)}, u32[]{:S(2)}) collective-permute-start(bf16[72,2176]{1,0:T(8,128)(2,1)S(1)} %get-tuple-element.56), channel_id=1, source_target_pairs={{0,16},{8,24},{16,0},{24,8},{1,17},{9,25},{17,1},{25,9},{2,18},{10... | collective-permute-start | bytes 940040 | tf_op jit(solution)/shard_map/ppermute | solution.py:24
  21.5 11.0 %collective-permute-start.12 = (bf16[24,2176]{1,0:T(8,128)(2,1)S(1)}, bf16[24,2176]{1,0:T(8,128)(2,1)S(1)}, u32[]{:S(2)}, u32[]{:S(2)}) collective-permute-start(bf16[24,2176]{1,0:T(8,128)(2,1)S(1)} %collective-permute-done.6), channel_id=1, source_target_pairs={{0,4},{2,6},{4,0},{6,2},{1,5},{3,7},{5,1},{7,3},{8,12},{10,14},{12... | collective-permute-start | bytes 313352 | tf_op jit(solution)/shard_map/ppermute | solution.py:24
  23.2 9.3 %collective-permute-start.11 = (bf16[24,2176]{1,0:T(8,128)(2,1)S(1)}, bf16[24,2176]{1,0:T(8,128)(2,1)S(1)}, u32[]{:S(2)}, u32[]{:S(2)}) collective-permute-start(bf16[24,2176]{1,0:T(8,128)(2,1)S(1)} %collective-permute-done.6), channel_id=1, source_target_pairs={{0,2},{2,0},{4,6},{6,4},{1,3},{3,1},{5,7},{7,5},{8,10},{10,8},{12,... | collective-permute-start | bytes 313352 | tf_op jit(solution)/shard_map/ppermute | solution.py:24
  25.2 7.3 %collective-permute-start.13 = (bf16[24,2176]{1,0:T(8,128)(2,1)S(1)}, bf16[24,2176]{1,0:T(8,128)(2,1)S(1)}, u32[]{:S(2)}, u32[]{:S(2)}) collective-permute-start(bf16[24,2176]{1,0:T(8,128)(2,1)S(1)} %collective-permute-done.6), channel_id=1, source_target_pairs={{0,6},{2,4},{4,2},{6,0},{1,7},{3,5},{5,3},{7,1},{8,14},{10,12},{12... | collective-permute-start | bytes 313352 | tf_op jit(solution)/shard_map/ppermute | solution.py:24
  32.7 2.7 %collective-permute-start.14 = (bf16[216,2048]{1,0:T(8,128)(2,1)S(1)}, bf16[216,2048]{1,0:T(8,128)(2,1)S(1)}, u32[]{:S(2)}, u32[]{:S(2)}) collective-permute-start(bf16[216,2048]{1,0:T(8,128)(2,1)S(1)} %slice.76), channel_id=1, source_target_pairs={{0,1},{1,0},{2,3},{3,2},{4,5},{5,4},{6,7},{7,6},{8,9},{9,8},{10,11... | collective-permute-start | bytes 2654216 | tf_op jit(solution)/shard_map/ppermute | solution.py:24
  32.8 5.8 %collective-permute-start.8 = (bf16[168,2048]{1,0:T(8,128)(2,1)S(1)}, bf16[168,2048]{1,0:T(8,128)(2,1)S(1)}, u32[]{:S(2)}, u32[]{:S(2)}) collective-permute-start(bf16[168,2048]{1,0:T(8,128)(2,1)S(1)} %get-tuple-element.29), channel_id=1, source_target_pairs={{0,1},{1,0},{2,3},{3,2},{4,5},{5,4},{6,7},{7,6},{8,9},{9,8},{10,11... | collective-permute-start | bytes 2064392 | tf_op jit(solution)/shard_map/ppermute | solution.py:24
  38.4 2.5 %collective-permute-start.15 = (bf16[216,2048]{1,0:T(8,128)(2,1)S(1)}, bf16[216,2048]{1,0:T(8,128)(2,1)S(1)}, u32[]{:S(2)}, u32[]{:S(2)}) collective-permute-start(bf16[216,2048]{1,0:T(8,128)(2,1)S(1)} %get-tuple-element.34), channel_id=1, source_target_pairs={{0,1},{1,0},{2,3},{3,2},{4,5},{5,4},{6,7},{7,6},{8,9},{9,8},{10,11... | collective-permute-start | bytes 2654216 | tf_op jit(solution)/shard_map/ppermute | solution.py:24
  40.3 21.2 %copy-start = (s32[8]{0:T(128)S(1)}, s32[8]{0:T(128)}, u32[]{:S(2)}) copy-start(s32[8]{0:T(128)} %refs_0_.3) | copy-start | bytes 100
  41.2 11.2 %collective-permute-start.17 = (bf16[96,2048]{1,0:T(8,128)(2,1)S(1)}, bf16[96,2048]{1,0:T(8,128)(2,1)S(1)}, u32[]{:S(2)}, u32[]{:S(2)}) collective-permute-start(bf16[96,2048]{1,0:T(8,128)(2,1)S(1)} %pad_maximum_fusion.1), channel_id=1, source_target_pairs={{0,16},{8,24},{16,0},{24,8},{1,17},{9,25},{17,1},{25,9},{2,18},{10... | collective-permute-start | bytes 1179656 | tf_op jit(solution)/shard_map/ppermute | solution.py:24
  41.8 10.9 %collective-permute-start.16 = (bf16[96,2048]{1,0:T(8,128)(2,1)S(1)}, bf16[96,2048]{1,0:T(8,128)(2,1)S(1)}, u32[]{:S(2)}, u32[]{:S(2)}) collective-permute-start(bf16[96,2048]{1,0:T(8,128)(2,1)S(1)} %pad_maximum_fusion), channel_id=1, source_target_pairs={{0,8},{8,0},{16,24},{24,16},{1,9},{9,1},{17,25},{25,17},{2,10},{10... | collective-permute-start | bytes 1179656 | tf_op jit(solution)/shard_map/ppermute | solution.py:24
  43.4 9.6 %collective-permute-start.23 = (bf16[24,2048]{1,0:T(8,128)(2,1)S(1)}, bf16[24,2048]{1,0:T(8,128)(2,1)S(1)}, u32[]{:S(2)}, u32[]{:S(2)}) collective-permute-start(bf16[24,2048]{1,0:T(8,128)(2,1)S(1)} %get-tuple-element.42), channel_id=1, source_target_pairs={{0,2},{2,0},{4,6},{6,4},{1,3},{3,1},{5,7},{7,5},{8,10},{10,8},{12,... | collective-permute-start | bytes 294920 | tf_op jit(solution)/shard_map/ppermute | solution.py:24
  45.2 10.2 %collective-permute-start.22 = (bf16[24,2048]{1,0:T(8,128)(2,1)S(1)}, bf16[24,2048]{1,0:T(8,128)(2,1)S(1)}, u32[]{:S(2)}, u32[]{:S(2)}) collective-permute-start(bf16[24,2048]{1,0:T(8,128)(2,1)S(1)} %get-tuple-element.43), channel_id=1, source_target_pairs={{0,4},{2,6},{4,0},{6,2},{1,5},{3,7},{5,1},{7,3},{8,12},{10,14},{12... | collective-permute-start | bytes 294920 | tf_op jit(solution)/shard_map/ppermute | solution.py:24
  46.5 8.8 %collective-permute-start.21 = (bf16[24,2048]{1,0:T(8,128)(2,1)S(1)}, bf16[24,2048]{1,0:T(8,128)(2,1)S(1)}, u32[]{:S(2)}, u32[]{:S(2)}) collective-permute-start(bf16[24,2048]{1,0:T(8,128)(2,1)S(1)} %get-tuple-element.44), channel_id=1, source_target_pairs={{0,6},{2,4},{4,2},{6,0},{1,7},{3,5},{5,3},{7,1},{8,14},{10,12},{12... | collective-permute-start | bytes 294920 | tf_op jit(solution)/shard_map/ppermute | solution.py:24
  55.4 7.5 %collective-permute-start.24 = (bf16[24,2048]{1,0:T(8,128)(2,1)S(1)}, bf16[24,2048]{1,0:T(8,128)(2,1)S(1)}, u32[]{:S(2)}, u32[]{:S(2)}) collective-permute-start(bf16[24,2048]{1,0:T(8,128)(2,1)S(1)} %add_convert_fusion.3), channel_id=1, source_target_pairs={{0,24},{8,16},{16,8},{24,0},{1,25},{9,17},{17,9},{25,1},{2,26},{10... | collective-permute-start | bytes 294920 | tf_op jit(solution)/shard_map/ppermute | solution.py:24
  57.1 5.9 %collective-permute-start.20 = (bf16[24,2048]{1,0:T(8,128)(2,1)S(1)}, bf16[24,2048]{1,0:T(8,128)(2,1)S(1)}, u32[]{:S(2)}, u32[]{:S(2)}) collective-permute-start(bf16[24,2048]{1,0:T(8,128)(2,1)S(1)} %get-tuple-element.48), channel_id=1, source_target_pairs={{0,2},{2,0},{4,6},{6,4},{1,3},{3,1},{5,7},{7,5},{8,10},{10,8},{12,... | collective-permute-start | bytes 294920 | tf_op jit(solution)/shard_map/ppermute | solution.py:24
  58.7 9.4 %collective-permute-start.19 = (bf16[24,2048]{1,0:T(8,128)(2,1)S(1)}, bf16[24,2048]{1,0:T(8,128)(2,1)S(1)}, u32[]{:S(2)}, u32[]{:S(2)}) collective-permute-start(bf16[24,2048]{1,0:T(8,128)(2,1)S(1)} %get-tuple-element.49), channel_id=1, source_target_pairs={{0,4},{2,6},{4,0},{6,2},{1,5},{3,7},{5,1},{7,3},{8,12},{10,14},{12... | collective-permute-start | bytes 294920 | tf_op jit(solution)/shard_map/ppermute | solution.py:24
  60.2 7.9 %collective-permute-start.18 = (bf16[24,2048]{1,0:T(8,128)(2,1)S(1)}, bf16[24,2048]{1,0:T(8,128)(2,1)S(1)}, u32[]{:S(2)}, u32[]{:S(2)}) collective-permute-start(bf16[24,2048]{1,0:T(8,128)(2,1)S(1)} %get-tuple-element.50), channel_id=1, source_target_pairs={{0,6},{2,4},{4,2},{6,0},{1,7},{3,5},{5,3},{7,1},{8,14},{10,12},{12... | collective-permute-start | bytes 294920 | tf_op jit(solution)/shard_map/ppermute | solution.py:24
  68.2 1.3 %collective-permute-start.25 = (bf16[12,2048]{1,0:T(8,128)(2,1)S(1)}, bf16[12,2048]{1,0:T(8,128)(2,1)S(1)}, u32[]{:S(2)}, u32[]{:S(2)}) collective-permute-start(bf16[12,2048]{1,0:T(8,128)(2,1)S(1)} %broadcast_select_fusion.4), channel_id=1, source_target_pairs={{0,1},{1,0},{2,3},{3,2},{4,5},{5,4},{6,7},{7,6},{8,9},{9,8},{10,11... | collective-permute-start | bytes 147464 | tf_op jit(solution)/shard_map/ppermute | solution.py:24

commit v20 on v19

--- a/solution.py
+++ b/solution.py
@@ -402,14 +402,13 @@
         fourth = []
         metas = [held, *near]
     metas = [block[:, block.shape[1] - LANES :] for block in metas]
-    total = collected(whole[0], received(whole))
-    came = []
+    total = parts(collected(whole[0], received(whole)))
+    came = along_chips(total[1:])
     if fourth:
-        fourth = collected(near_sums[3], behind(fourth, total))
-        came = [swap(fourth, "dp", 3)]
-    total = parts(total)
+        fourth = collected(near_sums[3], behind(fourth, came[-1]))
+        came.append(swap(fourth, "dp", 3))
     load = planned_load(metas, swap_slot, owners, per_device, top_count, total[0])
-    total = collected(total[0], along_chips(total[1:]) + came)
+    total = collected(total[0], came)
     upper, lower = total[:rows], total[rows:]
     arrived = swap(jnp.where(first, lower, upper), "core", 1)
     kept = jnp.where(first, upper, lower)

time: 70.4 us -> 66.8 us (0.949)
  waiting for transfers between devices: 16.4 us -> 12.5 us
    ppermute x26, waiting for transfers between devices: 16.4 us -> 12.5 us  [swap(): return row_major(lax.ppermute(row_major(value), axis, pairs))]
  transfers between devices with their start and end apart: 26 -> 26, of which waited for: 8 -> 8; matrix products, arithmetic and copies ran while one was open for 2% -> 2% of each run, Pallas kernels for 27% -> 29%
where the time goes in v20:
time: 66.8 us; the launch traced here: 66.6 us
  starting transfers between devices  29.9 us (45%)
  Pallas kernels  20.8 us (31%)
  waiting for transfers between devices  12.5 us (19%)
  other arithmetic  1.39 us (2%)
  local copies, waits for them, and re-layouts  1.02 us (2%)
  between operations  0.96 us (1%)
    ppermute x26, starting transfers between devices, swap(): return row_major(lax.ppermute(row_major(value), axis, pairs))  29.9 us
    pallas_call x4, Pallas kernels, call(): pl.pallas_call(kernel, in_specs=[pl.BlockSpec(memory_space=pltpu.SMEM)] +...  13 us
    ppermute x26, waiting for transfers between devices, swap(): return row_major(lax.ppermute(row_major(value), axis, pairs))  12.5 us
    pallas_call x1, Pallas kernels, loaded(): pl.pallas_call(load_weight_kernel, in_specs=[pl.BlockSpec(memory_space=pl...  4.58 us
    pallas_call x1, Pallas kernels, first_halves(): pl.pallas_call(first_kernel, in_specs=[pl.BlockSpec(memory_space=pltpu.SM...  1.56 us
    pallas_call x1, Pallas kernels, planned_load(): pl.pallas_call(lambda *refs: load_kernel(layout, *refs), in_specs=[pl.Blo...  1.44 us
  transfers between devices with their start and end apart: 26, of which 8 were waited for; matrix products, arithmetic and copies ran while one was open for 2% of the time, Pallas kernels for 29%

profile of v20, /device:TPU:0, one launch (start us, length us, event | category | flops | bytes accessed | tf_op | source)
XLA Modules:
  0.0 66.6 jit_solution(14214013506674883654)
XLA Ops:
  0.6 0.1 pad_add_fusion.place.refs_0_
  0.7 1.6 %shard_map.77 = (bf16[12,2176]{1,0:T(8,128)(2,1)S(1)}, bf16[12,2176]{1,0:T(8,128)(2,1)S(1)}) custom-call(s32[2]{0:T(128)S(1)} %pad_add_fusion.place.refs_0_, bf16[12,4096]{1,0:T(8,128)(2,1)} %refs_0_.2, s32[8,12]{1,0:T(8,128)} %bitcast.8, f32[8,12]{1,0:T(8,128)} %bitcast.9), custom_call_target="tpu_custom_call" | custom-call | tf_op jit(solution)/shard_map/pallas_call | solution.py:246
  2.3 0.5 collective-permute-start
  2.8 0.9 %collective-permute-done = bf16[12,2176]{1,0:T(8,128)(2,1)S(1)} collective-permute-done((bf16[12,2176]{1,0:T(8,128)(2,1)S(1)}, bf16[12,2176]{1,0:T(8,128)(2,1)S(1)}, u32[]{:S(2)}, u32[]{:S(2)}) %collective-permute-start) | collective-permute-done | bytes 52256 | tf_op jit(solution)/shard_map/ppermute | solution.py:24
  3.8 2.9 %collective-permute-start.4 = (bf16[24,2176]{1,0:T(8,128)(2,1)S(1)}, bf16[24,2176]{1,0:T(8,128)(2,1)S(1)}, u32[]{:S(2)}, u32[]{:S(2)}) collective-permute-start(bf16[24,2176]{1,0:T(8,128)(2,1)S(1)} %get-tuple-element.39), channel_id=1, source_target_pairs={{0,8},{8,0},{16,24},{24,16},{1,9},{9,1},{17,25},{25,17},{2,10},{10... | collective-permute-start | bytes 313352 | tf_op jit(solution)/shard_map/ppermute | solution.py:24
  6.7 3.6 %collective-permute-start.3 = (bf16[24,2176]{1,0:T(8,128)(2,1)S(1)}, bf16[24,2176]{1,0:T(8,128)(2,1)S(1)}, u32[]{:S(2)}, u32[]{:S(2)}) collective-permute-start(bf16[24,2176]{1,0:T(8,128)(2,1)S(1)} %get-tuple-element.39), channel_id=1, source_target_pairs={{0,6},{2,4},{4,2},{6,0},{1,7},{3,5},{5,3},{7,1},{8,14},{10,12},{12... | collective-permute-start | bytes 313352 | tf_op jit(solution)/shard_map/ppermute | solution.py:24
  10.3 0.8 %collective-permute-start.1 = (bf16[24,2176]{1,0:T(8,128)(2,1)S(1)}, bf16[24,2176]{1,0:T(8,128)(2,1)S(1)}, u32[]{:S(2)}, u32[]{:S(2)}) collective-permute-start(bf16[24,2176]{1,0:T(8,128)(2,1)S(1)} %get-tuple-element.39), channel_id=1, source_target_pairs={{0,2},{2,0},{4,6},{6,4},{1,3},{3,1},{5,7},{7,5},{8,10},{10,8},{12,... | collective-permute-start | bytes 313352 | tf_op jit(solution)/shard_map/ppermute | solution.py:24
  11.1 1.5 %collective-permute-start.6 = (bf16[24,2176]{1,0:T(8,128)(2,1)S(1)}, bf16[24,2176]{1,0:T(8,128)(2,1)S(1)}, u32[]{:S(2)}, u32[]{:S(2)}) collective-permute-start(bf16[24,2176]{1,0:T(8,128)(2,1)S(1)} %get-tuple-element.39), channel_id=1, source_target_pairs={{0,24},{8,16},{16,8},{24,0},{1,25},{9,17},{17,9},{25,1},{2,26},{10... | collective-permute-start | bytes 313352 | tf_op jit(solution)/shard_map/ppermute | solution.py:24
  12.6 0.3 collective-permute-start.5
  12.8 4.6 %shard_map.78 = (bf16[2,4096,768]{2,1,0:T(8,128)(2,1)S(1)}, f32[8,128]{1,0:T(8,128)S(1)}) custom-call(bf16[2,4096,768]{2,1,0:T(8,128)(2,1)} %weight_ref.1, bf16[24,2176]{1,0:T(8,128)(2,1)S(1)} %collective-permute-done.4._), custom_call_target="tpu_custom_call" | custom-call | bytes 12582912 | tf_op jit(solution)/shard_map/pallas_call | solution.py:56
  17.4 1.7 %collective-permute-done.2 = bf16[24,2176]{1,0:T(8,128)(2,1)S(1)} collective-permute-done((bf16[24,2176]{1,0:T(8,128)(2,1)S(1)}, bf16[24,2176]{1,0:T(8,128)(2,1)S(1)}, u32[]{:S(2)}, u32[]{:S(2)}) %collective-permute-start.2) | collective-permute-done | bytes 104480 | tf_op jit(solution)/shard_map/ppermute | solution.py:24
  19.3 0.1 slice.74
  19.3 0.1 collective-permute-start.7
  19.4 0.6 collective-permute-start.9
  20.0 1.5 %collective-permute-start.10 = (bf16[72,2176]{1,0:T(8,128)(2,1)S(1)}, bf16[72,2176]{1,0:T(8,128)(2,1)S(1)}, u32[]{:S(2)}, u32[]{:S(2)}) collective-permute-start(bf16[72,2176]{1,0:T(8,128)(2,1)S(1)} %get-tuple-element.56), channel_id=1, source_target_pairs={{0,16},{8,24},{16,0},{24,8},{1,17},{9,25},{17,1},{25,9},{2,18},{10... | collective-permute-start | bytes 940040 | tf_op jit(solution)/shard_map/ppermute | solution.py:24
  21.5 1.7 %collective-permute-start.12 = (bf16[24,2176]{1,0:T(8,128)(2,1)S(1)}, bf16[24,2176]{1,0:T(8,128)(2,1)S(1)}, u32[]{:S(2)}, u32[]{:S(2)}) collective-permute-start(bf16[24,2176]{1,0:T(8,128)(2,1)S(1)} %collective-permute-done.6), channel_id=1, source_target_pairs={{0,4},{2,6},{4,0},{6,2},{1,5},{3,7},{5,1},{7,3},{8,12},{10,14},{12... | collective-permute-start | bytes 313352 | tf_op jit(solution)/shard_map/ppermute | solution.py:24
  23.2 2.0 %collective-permute-start.11 = (bf16[24,2176]{1,0:T(8,128)(2,1)S(1)}, bf16[24,2176]{1,0:T(8,128)(2,1)S(1)}, u32[]{:S(2)}, u32[]{:S(2)}) collective-permute-start(bf16[24,2176]{1,0:T(8,128)(2,1)S(1)} %collective-permute-done.6), channel_id=1, source_target_pairs={{0,2},{2,0},{4,6},{6,4},{1,3},{3,1},{5,7},{7,5},{8,10},{10,8},{12,... | collective-permute-start | bytes 313352 | tf_op jit(solution)/shard_map/ppermute | solution.py:24
  25.2 0.7 %collective-permute-start.13 = (bf16[24,2176]{1,0:T(8,128)(2,1)S(1)}, bf16[24,2176]{1,0:T(8,128)(2,1)S(1)}, u32[]{:S(2)}, u32[]{:S(2)}) collective-permute-start(bf16[24,2176]{1,0:T(8,128)(2,1)S(1)} %collective-permute-done.6), channel_id=1, source_target_pairs={{0,6},{2,4},{4,2},{6,0},{1,7},{3,5},{5,3},{7,1},{8,14},{10,12},{12... | collective-permute-start | bytes 313352 | tf_op jit(solution)/shard_map/ppermute | solution.py:24
  25.9 6.5 %shard_map.79 = (bf16[168,2048]{1,0:T(8,128)(2,1)S(1)}, bf16[168,2048]{1,0:T(8,128)(2,1)S(1)}, bf16[768,4096]{1,0:T(8,128)(2,1)S(1)}) custom-call(s32[2]{0:T(128)S(1)} %pad_add_fusion.place.refs_0_, bf16[168,2176]{1,0:T(8,128)(2,1)S(1)} %constant_dynamic-update-slice_fusion.refs_1_, bf16[168,2048]{1,0:T(8,128)(2,1)S(1)} %collective-permute-done.7.refs_2_, ...), custom_call_target="tpu_custom_call" | custom-call | flops 3170893824 | tf_op jit(solution)/shard_map/pallas_call | solution.py:147
  32.6 0.1 slice.76
  32.7 0.1 collective-permute-start.14
  32.8 0.5 collective-permute-start.8
  33.3 2.1 %shard_map.80.refs_3_ = f32[2,216,768]{2,1,0:T(8,128)S(1)} custom-call(s32[2]{0:T(128)S(1)} %pad_add_fusion.place.refs_0_, bf16[216,2176]{1,0:T(8,128)(2,1)S(1)} %constant_dynamic-update-slice_fusion.10.own.refs_1_, bf16[2,4096,768]{2,1,0:T(8,128)(2,1)S(1)} %get-tuple-element.26.refs_3_.up.refs_4_), custom_call_target="tpu_custom_call" | custom-call | flops 1358954496 | tf_op jit(solution)/shard_map/pallas_call | solution.py:147
  35.4 3.0 %shard_map.81 = (bf16[216,2048]{1,0:T(8,128)(2,1)S(1)}, bf16[216,768]{1,0:T(8,128)(2,1)S(1)}) custom-call(s32[2]{0:T(128)S(1)} %pad_add_fusion.place.refs_0_, bf16[216,2176]{1,0:T(8,128)(2,1)S(1)} %constant_dynamic-update-slice_fusion.10.own.refs_1_, bf16[216,2048]{1,0:T(8,128)(2,1)S(1)} %collective-permute-done.14.refs_2_, ...), custom_call_target="tpu_custom_call" | custom-call | flops 2038431744 | tf_op jit(solution)/shard_map/pallas_call | solution.py:147
  38.4 0.1 collective-permute-start.15
  38.6 0.2 add_convert_fusion
  38.8 1.4 %shard_map.82.kept_ref = bf16[216,2048]{1,0:T(8,128)(2,1)S(1)} custom-call(s32[2]{0:T(128)S(1)} %pad_add_fusion.place.refs_0_, bf16[216,768]{1,0:T(8,128)(2,1)S(1)} %get-tuple-element.33.hidden, bf16[768,4096]{1,0:T(8,128)(2,1)S(1)} %get-tuple-element.32.refs_5_.down), custom_call_target="tpu_custom_call" | custom-call | flops 679477248 | tf_op jit(solution)/shard_map/pallas_call | solution.py:147
  40.3 0.6 collective-permute-done.15.taken_ref
  40.9 0.2 shard_map.83
  41.2 0.6 collective-permute-start.17
  41.8 1.6 %collective-permute-start.16 = (bf16[96,2048]{1,0:T(8,128)(2,1)S(1)}, bf16[96,2048]{1,0:T(8,128)(2,1)S(1)}, u32[]{:S(2)}, u32[]{:S(2)}) collective-permute-start(bf16[96,2048]{1,0:T(8,128)(2,1)S(1)} %pad_maximum_fusion), channel_id=1, source_target_pairs={{0,8},{8,0},{16,24},{24,16},{1,9},{9,1},{17,25},{25,17},{2,10},{10... | collective-permute-start | bytes 1179656 | tf_op jit(solution)/shard_map/ppermute | solution.py:24
  43.4 1.8 %collective-permute-start.23 = (bf16[24,2048]{1,0:T(8,128)(2,1)S(1)}, bf16[24,2048]{1,0:T(8,128)(2,1)S(1)}, u32[]{:S(2)}, u32[]{:S(2)}) collective-permute-start(bf16[24,2048]{1,0:T(8,128)(2,1)S(1)} %get-tuple-element.42), channel_id=1, source_target_pairs={{0,2},{2,0},{4,6},{6,4},{1,3},{3,1},{5,7},{7,5},{8,10},{10,8},{12,... | collective-permute-start | bytes 294920 | tf_op jit(solution)/shard_map/ppermute | solution.py:24
  45.2 1.3 %collective-permute-start.22 = (bf16[24,2048]{1,0:T(8,128)(2,1)S(1)}, bf16[24,2048]{1,0:T(8,128)(2,1)S(1)}, u32[]{:S(2)}, u32[]{:S(2)}) collective-permute-start(bf16[24,2048]{1,0:T(8,128)(2,1)S(1)} %get-tuple-element.43), channel_id=1, source_target_pairs={{0,4},{2,6},{4,0},{6,2},{1,5},{3,7},{5,1},{7,3},{8,12},{10,14},{12... | collective-permute-start | bytes 294920 | tf_op jit(solution)/shard_map/ppermute | solution.py:24
  46.5 1.3 %collective-permute-start.21 = (bf16[24,2048]{1,0:T(8,128)(2,1)S(1)}, bf16[24,2048]{1,0:T(8,128)(2,1)S(1)}, u32[]{:S(2)}, u32[]{:S(2)}) collective-permute-start(bf16[24,2048]{1,0:T(8,128)(2,1)S(1)} %get-tuple-element.44), channel_id=1, source_target_pairs={{0,6},{2,4},{4,2},{6,0},{1,7},{3,5},{5,3},{7,1},{8,14},{10,12},{12... | collective-permute-start | bytes 294920 | tf_op jit(solution)/shard_map/ppermute | solution.py:24
  47.8 4.6 %collective-permute-done.17 = bf16[96,2048]{1,0:T(8,128)(2,1)S(1)} collective-permute-done((bf16[96,2048]{1,0:T(8,128)(2,1)S(1)}, bf16[96,2048]{1,0:T(8,128)(2,1)S(1)}, u32[]{:S(2)}, u32[]{:S(2)}) %collective-permute-start.17) | collective-permute-done | bytes 393248 | tf_op jit(solution)/shard_map/ppermute | solution.py:24
  52.4 0.3 collective-permute-done.16
  52.7 0.1 add_convert_fusion.1
  52.9 1.9 %collective-permute-start.20 = (bf16[24,2048]{1,0:T(8,128)(2,1)S(1)}, bf16[24,2048]{1,0:T(8,128)(2,1)S(1)}, u32[]{:S(2)}, u32[]{:S(2)}) collective-permute-start(bf16[24,2048]{1,0:T(8,128)(2,1)S(1)} %get-tuple-element.48), channel_id=1, source_target_pairs={{0,2},{2,0},{4,6},{6,4},{1,3},{3,1},{5,7},{7,5},{8,10},{10,8},{12,... | collective-permute-start | bytes 294920 | tf_op jit(solution)/shard_map/ppermute | solution.py:24
  54.9 1.9 %collective-permute-start.19 = (bf16[24,2048]{1,0:T(8,128)(2,1)S(1)}, bf16[24,2048]{1,0:T(8,128)(2,1)S(1)}, u32[]{:S(2)}, u32[]{:S(2)}) collective-permute-start(bf16[24,2048]{1,0:T(8,128)(2,1)S(1)} %get-tuple-element.49), channel_id=1, source_target_pairs={{0,4},{2,6},{4,0},{6,2},{1,5},{3,7},{5,1},{7,3},{8,12},{10,14},{12... | collective-permute-start | bytes 294920 | tf_op jit(solution)/shard_map/ppermute | solution.py:24
  56.7 0.7 %collective-permute-start.18 = (bf16[24,2048]{1,0:T(8,128)(2,1)S(1)}, bf16[24,2048]{1,0:T(8,128)(2,1)S(1)}, u32[]{:S(2)}, u32[]{:S(2)}) collective-permute-start(bf16[24,2048]{1,0:T(8,128)(2,1)S(1)} %get-tuple-element.50), channel_id=1, source_target_pairs={{0,6},{2,4},{4,2},{6,0},{1,7},{3,5},{5,3},{7,1},{8,14},{10,12},{12... | collective-permute-start | bytes 294920 | tf_op jit(solution)/shard_map/ppermute | solution.py:24
  57.4 1.2 %collective-permute-done.20 = bf16[24,2048]{1,0:T(8,128)(2,1)S(1)} collective-permute-done((bf16[24,2048]{1,0:T(8,128)(2,1)S(1)}, bf16[24,2048]{1,0:T(8,128)(2,1)S(1)}, u32[]{:S(2)}, u32[]{:S(2)}) %collective-permute-start.20) | collective-permute-done | bytes 98336 | tf_op jit(solution)/shard_map/ppermute | solution.py:24
  58.7 1.9 %collective-permute-start.24 = (bf16[24,2048]{1,0:T(8,128)(2,1)S(1)}, bf16[24,2048]{1,0:T(8,128)(2,1)S(1)}, u32[]{:S(2)}, u32[]{:S(2)}) collective-permute-start(bf16[24,2048]{1,0:T(8,128)(2,1)S(1)} %add_convert_fusion.3), channel_id=1, source_target_pairs={{0,24},{8,16},{16,8},{24,0},{1,25},{9,17},{17,9},{25,1},{2,26},{10... | collective-permute-start | bytes 294920 | tf_op jit(solution)/shard_map/ppermute | solution.py:24
  60.6 1.4 %shard_map.84 = f32[1,128]{1,0:T(1,128)S(1)} custom-call(s32[8]{0:T(128)S(1)} %copy-done, bf16[168,128]{1,0:T(8,128)(2,1)S(1)} %slice.88.refs_1_, bf16[216,128]{1,0:T(8,128)(2,1)S(1)} %slice.89.refs_2_, bf16[24,2048]{1,0:T(8,128)(2,1)S(1)} %get-tuple-element.47.refs_3_), custom_call_target="tpu_custom_call" | custom-call | bytes 98304 | tf_op jit(solution)/shard_map/pallas_call | solution.py:314
  62.1 2.4 %collective-permute-done.19 = bf16[24,2048]{1,0:T(8,128)(2,1)S(1)} collective-permute-done((bf16[24,2048]{1,0:T(8,128)(2,1)S(1)}, bf16[24,2048]{1,0:T(8,128)(2,1)S(1)}, u32[]{:S(2)}, u32[]{:S(2)}) %collective-permute-start.19) | collective-permute-done | bytes 98336 | tf_op jit(solution)/shard_map/ppermute | solution.py:24
  64.6 0.1 collective-permute-start.25
  64.6 0.5 slice_bitcast_fusion
  65.1 0.7 %collective-permute-done.25 = bf16[12,2048]{1,0:T(8,128)(2,1)S(1)} collective-permute-done((bf16[12,2048]{1,0:T(8,128)(2,1)S(1)}, bf16[12,2048]{1,0:T(8,128)(2,1)S(1)}, u32[]{:S(2)}, u32[]{:S(2)}) %collective-permute-start.25) | collective-permute-done | bytes 49184 | tf_op jit(solution)/shard_map/ppermute | solution.py:24
  65.9 0.7 %pad_maximum_fusion.2 = bf16[12,4096]{1,0:T(8,128)(2,1)} fusion(bf16[12,2048]{1,0:T(8,128)(2,1)S(1)} %get-tuple-element.52, bf16[12,2048]{1,0:T(8,128)(2,1)S(1)} %get-tuple-element.51), kind=kLoop, calls=%fused_computation.6 | loop fusion | flops 196608 | bytes 196608 | tf_op jit(solution)/shard_map/concatenate | solution.py:416
  (46 shorter events, 0.7 us)
Async XLA Ops:
  2.3 1.4 %collective-permute-start = (bf16[12,2176]{1,0:T(8,128)(2,1)S(1)}, bf16[12,2176]{1,0:T(8,128)(2,1)S(1)}, u32[]{:S(2)}, u32[]{:S(2)}) collective-permute-start(bf16[12,2176]{1,0:T(8,128)(2,1)S(1)} %get-tuple-element.21), channel_id=1, source_target_pairs={{0,1},{1,0},{2,3},{3,2},{4,5},{5,4},{6,7},{7,6},{8,9},{9,8},{10,11... | collective-permute-start | bytes 156680 | tf_op jit(solution)/shard_map/ppermute | solution.py:24
  3.8 8.8 %collective-permute-start.4 = (bf16[24,2176]{1,0:T(8,128)(2,1)S(1)}, bf16[24,2176]{1,0:T(8,128)(2,1)S(1)}, u32[]{:S(2)}, u32[]{:S(2)}) collective-permute-start(bf16[24,2176]{1,0:T(8,128)(2,1)S(1)} %get-tuple-element.39), channel_id=1, source_target_pairs={{0,8},{8,0},{16,24},{24,16},{1,9},{9,1},{17,25},{25,17},{2,10},{10... | collective-permute-start | bytes 313352 | tf_op jit(solution)/shard_map/ppermute | solution.py:24
  6.7 10.8 %collective-permute-start.3 = (bf16[24,2176]{1,0:T(8,128)(2,1)S(1)}, bf16[24,2176]{1,0:T(8,128)(2,1)S(1)}, u32[]{:S(2)}, u32[]{:S(2)}) collective-permute-start(bf16[24,2176]{1,0:T(8,128)(2,1)S(1)} %get-tuple-element.39), channel_id=1, source_target_pairs={{0,6},{2,4},{4,2},{6,0},{1,7},{3,5},{5,3},{7,1},{8,14},{10,12},{12... | collective-permute-start | bytes 313352 | tf_op jit(solution)/shard_map/ppermute | solution.py:24
  10.3 8.8 %collective-permute-start.2 = (bf16[24,2176]{1,0:T(8,128)(2,1)S(1)}, bf16[24,2176]{1,0:T(8,128)(2,1)S(1)}, u32[]{:S(2)}, u32[]{:S(2)}) collective-permute-start(bf16[24,2176]{1,0:T(8,128)(2,1)S(1)} %get-tuple-element.39), channel_id=1, source_target_pairs={{0,4},{2,6},{4,0},{6,2},{1,5},{3,7},{5,1},{7,3},{8,12},{10,14},{12... | collective-permute-start | bytes 313352 | tf_op jit(solution)/shard_map/ppermute | solution.py:24
  10.3 8.8 %collective-permute-start.1 = (bf16[24,2176]{1,0:T(8,128)(2,1)S(1)}, bf16[24,2176]{1,0:T(8,128)(2,1)S(1)}, u32[]{:S(2)}, u32[]{:S(2)}) collective-permute-start(bf16[24,2176]{1,0:T(8,128)(2,1)S(1)} %get-tuple-element.39), channel_id=1, source_target_pairs={{0,2},{2,0},{4,6},{6,4},{1,3},{3,1},{5,7},{7,5},{8,10},{10,8},{12,... | collective-permute-start | bytes 313352 | tf_op jit(solution)/shard_map/ppermute | solution.py:24
  11.1 8.2 %collective-permute-start.6 = (bf16[24,2176]{1,0:T(8,128)(2,1)S(1)}, bf16[24,2176]{1,0:T(8,128)(2,1)S(1)}, u32[]{:S(2)}, u32[]{:S(2)}) collective-permute-start(bf16[24,2176]{1,0:T(8,128)(2,1)S(1)} %get-tuple-element.39), channel_id=1, source_target_pairs={{0,24},{8,16},{16,8},{24,0},{1,25},{9,17},{17,9},{25,1},{2,26},{10... | collective-permute-start | bytes 313352 | tf_op jit(solution)/shard_map/ppermute | solution.py:24
  12.6 6.7 %collective-permute-start.5 = (bf16[24,2176]{1,0:T(8,128)(2,1)S(1)}, bf16[24,2176]{1,0:T(8,128)(2,1)S(1)}, u32[]{:S(2)}, u32[]{:S(2)}) collective-permute-start(bf16[24,2176]{1,0:T(8,128)(2,1)S(1)} %get-tuple-element.39), channel_id=1, source_target_pairs={{0,16},{8,24},{16,0},{24,8},{1,17},{9,25},{17,1},{25,9},{2,18},{10... | collective-permute-start | bytes 313352 | tf_op jit(solution)/shard_map/ppermute | solution.py:24
  19.3 5.9 %collective-permute-start.7 = (bf16[168,2048]{1,0:T(8,128)(2,1)S(1)}, bf16[168,2048]{1,0:T(8,128)(2,1)S(1)}, u32[]{:S(2)}, u32[]{:S(2)}) collective-permute-start(bf16[168,2048]{1,0:T(8,128)(2,1)S(1)} %slice.74), channel_id=1, source_target_pairs={{0,1},{1,0},{2,3},{3,2},{4,5},{5,4},{6,7},{7,6},{8,9},{9,8},{10,11... | collective-permute-start | bytes 2064392 | tf_op jit(solution)/shard_map/ppermute | solution.py:24
  19.4 13.0 %collective-permute-start.9 = (bf16[72,2176]{1,0:T(8,128)(2,1)S(1)}, bf16[72,2176]{1,0:T(8,128)(2,1)S(1)}, u32[]{:S(2)}, u32[]{:S(2)}) collective-permute-start(bf16[72,2176]{1,0:T(8,128)(2,1)S(1)} %get-tuple-element.56), channel_id=1, source_target_pairs={{0,8},{8,0},{16,24},{24,16},{1,9},{9,1},{17,25},{25,17},{2,10},{10... | collective-permute-start | bytes 940040 | tf_op jit(solution)/shard_map/ppermute | solution.py:24
  20.0 12.4 %collective-permute-start.10 = (bf16[72,2176]{1,0:T(8,128)(2,1)S(1)}, bf16[72,2176]{1,0:T(8,128)(2,1)S(1)}, u32[]{:S(2)}, u32[]{:S(2)}) collective-permute-start(bf16[72,2176]{1,0:T(8,128)(2,1)S(1)} %get-tuple-element.56), channel_id=1, source_target_pairs={{0,16},{8,24},{16,0},{24,8},{1,17},{9,25},{17,1},{25,9},{2,18},{10... | collective-permute-start | bytes 940040 | tf_op jit(solution)/shard_map/ppermute | solution.py:24
  21.5 11.0 %collective-permute-start.12 = (bf16[24,2176]{1,0:T(8,128)(2,1)S(1)}, bf16[24,2176]{1,0:T(8,128)(2,1)S(1)}, u32[]{:S(2)}, u32[]{:S(2)}) collective-permute-start(bf16[24,2176]{1,0:T(8,128)(2,1)S(1)} %collective-permute-done.6), channel_id=1, source_target_pairs={{0,4},{2,6},{4,0},{6,2},{1,5},{3,7},{5,1},{7,3},{8,12},{10,14},{12... | collective-permute-start | bytes 313352 | tf_op jit(solution)/shard_map/ppermute | solution.py:24
  23.2 9.3 %collective-permute-start.11 = (bf16[24,2176]{1,0:T(8,128)(2,1)S(1)}, bf16[24,2176]{1,0:T(8,128)(2,1)S(1)}, u32[]{:S(2)}, u32[]{:S(2)}) collective-permute-start(bf16[24,2176]{1,0:T(8,128)(2,1)S(1)} %collective-permute-done.6), channel_id=1, source_target_pairs={{0,2},{2,0},{4,6},{6,4},{1,3},{3,1},{5,7},{7,5},{8,10},{10,8},{12,... | collective-permute-start | bytes 313352 | tf_op jit(solution)/shard_map/ppermute | solution.py:24
  25.2 7.3 %collective-permute-start.13 = (bf16[24,2176]{1,0:T(8,128)(2,1)S(1)}, bf16[24,2176]{1,0:T(8,128)(2,1)S(1)}, u32[]{:S(2)}, u32[]{:S(2)}) collective-permute-start(bf16[24,2176]{1,0:T(8,128)(2,1)S(1)} %collective-permute-done.6), channel_id=1, source_target_pairs={{0,6},{2,4},{4,2},{6,0},{1,7},{3,5},{5,3},{7,1},{8,14},{10,12},{12... | collective-permute-start | bytes 313352 | tf_op jit(solution)/shard_map/ppermute | solution.py:24
  32.7 2.7 %collective-permute-start.14 = (bf16[216,2048]{1,0:T(8,128)(2,1)S(1)}, bf16[216,2048]{1,0:T(8,128)(2,1)S(1)}, u32[]{:S(2)}, u32[]{:S(2)}) collective-permute-start(bf16[216,2048]{1,0:T(8,128)(2,1)S(1)} %slice.76), channel_id=1, source_target_pairs={{0,1},{1,0},{2,3},{3,2},{4,5},{5,4},{6,7},{7,6},{8,9},{9,8},{10,11... | collective-permute-start | bytes 2654216 | tf_op jit(solution)/shard_map/ppermute | solution.py:24
  32.8 5.8 %collective-permute-start.8 = (bf16[168,2048]{1,0:T(8,128)(2,1)S(1)}, bf16[168,2048]{1,0:T(8,128)(2,1)S(1)}, u32[]{:S(2)}, u32[]{:S(2)}) collective-permute-start(bf16[168,2048]{1,0:T(8,128)(2,1)S(1)} %get-tuple-element.29), channel_id=1, source_target_pairs={{0,1},{1,0},{2,3},{3,2},{4,5},{5,4},{6,7},{7,6},{8,9},{9,8},{10,11... | collective-permute-start | bytes 2064392 | tf_op jit(solution)/shard_map/ppermute | solution.py:24
  38.4 2.5 %collective-permute-start.15 = (bf16[216,2048]{1,0:T(8,128)(2,1)S(1)}, bf16[216,2048]{1,0:T(8,128)(2,1)S(1)}, u32[]{:S(2)}, u32[]{:S(2)}) collective-permute-start(bf16[216,2048]{1,0:T(8,128)(2,1)S(1)} %get-tuple-element.34), channel_id=1, source_target_pairs={{0,1},{1,0},{2,3},{3,2},{4,5},{5,4},{6,7},{7,6},{8,9},{9,8},{10,11... | collective-permute-start | bytes 2654216 | tf_op jit(solution)/shard_map/ppermute | solution.py:24
  40.3 20.3 %copy-start = (s32[8]{0:T(128)S(1)}, s32[8]{0:T(128)}, u32[]{:S(2)}) copy-start(s32[8]{0:T(128)} %refs_0_.3) | copy-start | bytes 100
  41.2 11.2 %collective-permute-start.17 = (bf16[96,2048]{1,0:T(8,128)(2,1)S(1)}, bf16[96,2048]{1,0:T(8,128)(2,1)S(1)}, u32[]{:S(2)}, u32[]{:S(2)}) collective-permute-start(bf16[96,2048]{1,0:T(8,128)(2,1)S(1)} %pad_maximum_fusion.1), channel_id=1, source_target_pairs={{0,16},{8,24},{16,0},{24,8},{1,17},{9,25},{17,1},{25,9},{2,18},{10... | collective-permute-start | bytes 1179656 | tf_op jit(solution)/shard_map/ppermute | solution.py:24
  41.8 10.9 %collective-permute-start.16 = (bf16[96,2048]{1,0:T(8,128)(2,1)S(1)}, bf16[96,2048]{1,0:T(8,128)(2,1)S(1)}, u32[]{:S(2)}, u32[]{:S(2)}) collective-permute-start(bf16[96,2048]{1,0:T(8,128)(2,1)S(1)} %pad_maximum_fusion), channel_id=1, source_target_pairs={{0,8},{8,0},{16,24},{24,16},{1,9},{9,1},{17,25},{25,17},{2,10},{10... | collective-permute-start | bytes 1179656 | tf_op jit(solution)/shard_map/ppermute | solution.py:24
  43.4 13.3 %collective-permute-start.23 = (bf16[24,2048]{1,0:T(8,128)(2,1)S(1)}, bf16[24,2048]{1,0:T(8,128)(2,1)S(1)}, u32[]{:S(2)}, u32[]{:S(2)}) collective-permute-start(bf16[24,2048]{1,0:T(8,128)(2,1)S(1)} %get-tuple-element.42), channel_id=1, source_target_pairs={{0,2},{2,0},{4,6},{6,4},{1,3},{3,1},{5,7},{7,5},{8,10},{10,8},{12,... | collective-permute-start | bytes 294920 | tf_op jit(solution)/shard_map/ppermute | solution.py:24
  45.2 12.3 %collective-permute-start.22 = (bf16[24,2048]{1,0:T(8,128)(2,1)S(1)}, bf16[24,2048]{1,0:T(8,128)(2,1)S(1)}, u32[]{:S(2)}, u32[]{:S(2)}) collective-permute-start(bf16[24,2048]{1,0:T(8,128)(2,1)S(1)} %get-tuple-element.43), channel_id=1, source_target_pairs={{0,4},{2,6},{4,0},{6,2},{1,5},{3,7},{5,1},{7,3},{8,12},{10,14},{12... | collective-permute-start | bytes 294920 | tf_op jit(solution)/shard_map/ppermute | solution.py:24
  46.5 10.9 %collective-permute-start.21 = (bf16[24,2048]{1,0:T(8,128)(2,1)S(1)}, bf16[24,2048]{1,0:T(8,128)(2,1)S(1)}, u32[]{:S(2)}, u32[]{:S(2)}) collective-permute-start(bf16[24,2048]{1,0:T(8,128)(2,1)S(1)} %get-tuple-element.44), channel_id=1, source_target_pairs={{0,6},{2,4},{4,2},{6,0},{1,7},{3,5},{5,3},{7,1},{8,14},{10,12},{12... | collective-permute-start | bytes 294920 | tf_op jit(solution)/shard_map/ppermute | solution.py:24
  52.9 5.7 %collective-permute-start.20 = (bf16[24,2048]{1,0:T(8,128)(2,1)S(1)}, bf16[24,2048]{1,0:T(8,128)(2,1)S(1)}, u32[]{:S(2)}, u32[]{:S(2)}) collective-permute-start(bf16[24,2048]{1,0:T(8,128)(2,1)S(1)} %get-tuple-element.48), channel_id=1, source_target_pairs={{0,2},{2,0},{4,6},{6,4},{1,3},{3,1},{5,7},{7,5},{8,10},{10,8},{12,... | collective-permute-start | bytes 294920 | tf_op jit(solution)/shard_map/ppermute | solution.py:24
  54.9 9.6 %collective-permute-start.19 = (bf16[24,2048]{1,0:T(8,128)(2,1)S(1)}, bf16[24,2048]{1,0:T(8,128)(2,1)S(1)}, u32[]{:S(2)}, u32[]{:S(2)}) collective-permute-start(bf16[24,2048]{1,0:T(8,128)(2,1)S(1)} %get-tuple-element.49), channel_id=1, source_target_pairs={{0,4},{2,6},{4,0},{6,2},{1,5},{3,7},{5,1},{7,3},{8,12},{10,14},{12... | collective-permute-start | bytes 294920 | tf_op jit(solution)/shard_map/ppermute | solution.py:24
  56.7 7.7 %collective-permute-start.18 = (bf16[24,2048]{1,0:T(8,128)(2,1)S(1)}, bf16[24,2048]{1,0:T(8,128)(2,1)S(1)}, u32[]{:S(2)}, u32[]{:S(2)}) collective-permute-start(bf16[24,2048]{1,0:T(8,128)(2,1)S(1)} %get-tuple-element.50), channel_id=1, source_target_pairs={{0,6},{2,4},{4,2},{6,0},{1,7},{3,5},{5,3},{7,1},{8,14},{10,12},{12... | collective-permute-start | bytes 294920 | tf_op jit(solution)/shard_map/ppermute | solution.py:24
  58.7 5.7 %collective-permute-start.24 = (bf16[24,2048]{1,0:T(8,128)(2,1)S(1)}, bf16[24,2048]{1,0:T(8,128)(2,1)S(1)}, u32[]{:S(2)}, u32[]{:S(2)}) collective-permute-start(bf16[24,2048]{1,0:T(8,128)(2,1)S(1)} %add_convert_fusion.3), channel_id=1, source_target_pairs={{0,24},{8,16},{16,8},{24,0},{1,25},{9,17},{17,9},{25,1},{2,26},{10... | collective-permute-start | bytes 294920 | tf_op jit(solution)/shard_map/ppermute | solution.py:24
  64.6 1.3 %collective-permute-start.25 = (bf16[12,2048]{1,0:T(8,128)(2,1)S(1)}, bf16[12,2048]{1,0:T(8,128)(2,1)S(1)}, u32[]{:S(2)}, u32[]{:S(2)}) collective-permute-start(bf16[12,2048]{1,0:T(8,128)(2,1)S(1)} %broadcast_select_fusion.4), channel_id=1, source_target_pairs={{0,1},{1,0},{2,3},{3,2},{4,5},{5,4},{6,7},{7,6},{8,9},{9,8},{10,11... | collective-permute-start | bytes 147464 | tf_op jit(solution)/shard_map/ppermute | solution.py:24

commit v21 on v20

--- a/solution.py
+++ b/solution.py
@@ -45,26 +45,34 @@
     return sum([wide(block) for block in others], wide(own)).astype(jnp.bfloat16)
 
 
-def load_weight_kernel(weight_ref, _, weight_out, mark_ref, sem):
-    copy = pltpu.make_async_copy(weight_ref, weight_out, sem)
-    copy.start()
+def load_weights_kernel(up_ref, down_ref, _, up_out, down_out, mark_ref, sems):
+    copies = [
+        pltpu.make_async_copy(up_ref, up_out, sems.at[0]),
+        pltpu.make_async_copy(down_ref, down_out, sems.at[1]),
+    ]
+    for copy in copies:
+        copy.start()
     mark_ref[...] = jnp.zeros_like(mark_ref)
-    copy.wait()
-
-
-def loaded(weight, after):
+    for copy in copies:
+        copy.wait()
+
+
+def loaded(up, down, after):
     return pl.pallas_call(
-        load_weight_kernel,
-        in_specs=[pl.BlockSpec(memory_space=pl.ANY)] * 2,
-        out_specs=[pl.BlockSpec(memory_space=pltpu.VMEM)] * 2,
+        load_weights_kernel,
+        in_specs=[pl.BlockSpec(memory_space=pl.ANY)] * 3,
+        out_specs=[pl.BlockSpec(memory_space=pltpu.VMEM)] * 3,
         out_shape=[
-            pltpu.VMEM(weight.shape, weight.dtype),
+            pltpu.VMEM(up.shape, up.dtype),
+            pltpu.VMEM(down.shape, down.dtype),
             pltpu.VMEM((8, LANES), jnp.float32),
         ],
-        scratch_shapes=[pltpu.SemaphoreType.DMA],
+        scratch_shapes=[pltpu.SemaphoreType.DMA((2,))],
         compiler_params=pltpu.CompilerParams(vmem_limit_bytes=VMEM_LIMIT),
-        cost_estimate=pl.CostEstimate(flops=0, bytes_accessed=weight.nbytes, transcendentals=0),
-    )(pltpu.with_memory_space_constraint(weight, pltpu.HBM), after)
+        cost_estimate=pl.CostEstimate(
+            flops=0, bytes_accessed=up.nbytes + down.nbytes, transcendentals=0
+        ),
+    )(*(pltpu.with_memory_space_constraint(x, pltpu.HBM) for x in (up, down)), after)
 
 
 def joined(blocks):
@@ -102,21 +110,14 @@
         ).astype(jnp.bfloat16)
 
 
-def sums_kernel(top_count, filling, place, own, other, up, *refs):
-    if filling:
-        down_ref, _, keep_ref, give_ref, down, acc, hidden, sem = refs
-        copy = pltpu.make_async_copy(down_ref, down, sem)
-        copy.start()
-    else:
-        down, keep_ref, give_ref, acc, hidden = refs
+def sums_kernel(top_count, place, own, other, up, down, *refs):
+    keep_ref, give_ref, acc, hidden = refs[-4:]
     part = other.shape[1]
     bases = [place[0] * part, (1 - place[0]) * part]
     acc[...] = jnp.zeros_like(acc)
     add_up(acc, [[own]], [part], up, bases[0])
     add_up(acc, [[other]], [part], up, bases[1])
     make_hidden(hidden, acc, [own], part, place[1], top_count)
-    if filling:
-        copy.wait()
     multiply_down(give_ref, hidden, down, bases[1])
     multiply_down(keep_ref, hidden, down, bases[0])
 
@@ -161,27 +162,19 @@
     )
 
 
-def gated_sums(place, top_count, own, other, up, down, mark=None):
+def gated_sums(place, top_count, own, other, up, down, *mark):
     count, part = other.shape
-    filling = mark is not None
     out = pltpu.VMEM((count, part), jnp.bfloat16)
-    out_shape = [out, out]
-    scratch = [
-        pltpu.VMEM((up.shape[0], count, up.shape[2]), jnp.float32),
-        pltpu.VMEM((count, down.shape[0]), jnp.bfloat16),
-    ]
-    operands = [place, own, other, up, down]
-    if filling:
-        operands[-1:] = [pltpu.with_memory_space_constraint(down, pltpu.HBM), mark]
-        out_shape.append(pltpu.VMEM(down.shape, down.dtype))
-        scratch.append(pltpu.SemaphoreType.DMA)
     return call(
-        lambda *refs: sums_kernel(top_count, filling, *refs),
-        operands,
-        out_shape,
-        scratch,
+        lambda *refs: sums_kernel(top_count, *refs),
+        [place, own, other, up, down, *mark],
+        [out, out],
+        [
+            pltpu.VMEM((up.shape[0], count, up.shape[2]), jnp.float32),
+            pltpu.VMEM((count, down.shape[0]), jnp.bfloat16),
+        ],
         flops=2 * count * (up.size + down.size),
-        unplaced=2 if filling else 0,
+        unplaced=len(mark),
     )
 
 
@@ -355,7 +348,9 @@
     chip_blocks = [swap(chip_rows, "chip", j) for j in range(chips - 1, 0, -1)]
     chip_blocks = [chip_rows, *chip_blocks[::-1]]
     direct = [swap(chip_rows, "dp", k) for k in range(1, groups)]
-    up, mark = loaded(in_weight, direct[0])
+    *weights, mark = loaded(
+        in_weight, out_weight.reshape(per_device * half_width, width), direct[0]
+    )
     chip_blocks[1:], mark = lax.optimization_barrier((chip_blocks[1:], mark))
     far = row_major(jnp.concatenate(chip_blocks[1:], 0))
     held = row_major(jnp.concatenate([*chip_blocks, *direct], 0))
@@ -363,11 +358,10 @@
     if groups == 4:
         fourth_rows = [swap(direct[2], "chip", j) for j in range(chips - 1, 0, -1)]
         fourth_rows = jnp.concatenate(fourth_rows[::-1], 0)
-    weights = [up, out_weight.reshape(per_device * half_width, width)]
     pieces = [held]
     if held.shape[0] > MOST_ROWS:
         pieces = [row_major(jnp.concatenate(chip_blocks, 0)), *direct]
-    keep, give, weights[1] = sums_of(pieces[0], weights, mark)
+    keep, give = sums_of(pieces[0], weights, mark)
     later = [sums_of(piece, weights) for piece in pieces[1:]]
     if later:
         keep, give = (jnp.concatenate(x, 0) for x in zip((keep, give), *later))

time: 66.8 us -> 68.4 us (1.024)
  waiting for transfers between devices: 12.5 us -> 14.1 us
    pallas_call x4, Pallas kernels: 13 us -> 10.8 us  [call(): pl.pallas_call(kernel, in_specs=[pl.BlockSpec(memory_space=pltpu.SMEM)] +...]
    pallas_call x1, Pallas kernels: 4.58 us -> 6.38 us  [loaded(): pl.pallas_call(load_weights_kernel, in_specs=[pl.BlockSpec(memory_space=p...]
    ppermute x26, waiting for transfers between devices: 12.5 us -> 14.1 us  [swap(): return row_major(lax.ppermute(row_major(value), axis, pairs))]
  transfers between devices with their start and end apart: 26 -> 26, of which waited for: 8 -> 9; matrix products, arithmetic and copies ran while one was open for 2% -> 2% of each run, Pallas kernels for 29% -> 27%
where the time goes in v21:
time: 68.4 us; the launch traced here: 68.3 us
  starting transfers between devices  30.5 us (45%)
  Pallas kernels  20.3 us (30%)
  waiting for transfers between devices  14.1 us (21%)
  other arithmetic  1.4 us (2%)
  local copies, waits for them, and re-layouts  1.02 us (1%)
  between operations  0.96 us (1%)
    ppermute x26, starting transfers between devices, swap(): return row_major(lax.ppermute(row_major(value), axis, pairs))  30.5 us
    ppermute x26, waiting for transfers between devices, swap(): return row_major(lax.ppermute(row_major(value), axis, pairs))  14.1 us
    pallas_call x4, Pallas kernels, call(): pl.pallas_call(kernel, in_specs=[pl.BlockSpec(memory_space=pltpu.SMEM)] +...  10.8 us
    pallas_call x1, Pallas kernels, loaded(): pl.pallas_call(load_weights_kernel, in_specs=[pl.BlockSpec(memory_space=p...  6.38 us
    pallas_call x1, Pallas kernels, first_halves(): pl.pallas_call(first_kernel, in_specs=[pl.BlockSpec(memory_space=pltpu.SM...  1.56 us
    pallas_call x1, Pallas kernels, planned_load(): pl.pallas_call(lambda *refs: load_kernel(layout, *refs), in_specs=[pl.Blo...  1.44 us
  transfers between devices with their start and end apart: 26, of which 9 were waited for; matrix products, arithmetic and copies ran while one was open for 2% of the time, Pallas kernels for 27%

profile of v21, /device:TPU:0, one launch (start us, length us, event | category | flops | bytes accessed | tf_op | source)
XLA Modules:
  0.0 68.3 jit_solution(13437927462409633987)
XLA Ops:
  0.6 0.1 pad_add_fusion.place.refs_0_
  0.7 1.6 %shard_map.77 = (bf16[12,2176]{1,0:T(8,128)(2,1)S(1)}, bf16[12,2176]{1,0:T(8,128)(2,1)S(1)}) custom-call(s32[2]{0:T(128)S(1)} %pad_add_fusion.place.refs_0_, bf16[12,4096]{1,0:T(8,128)(2,1)} %refs_0_.2, s32[8,12]{1,0:T(8,128)} %bitcast.8, f32[8,12]{1,0:T(8,128)} %bitcast.9), custom_call_target="tpu_custom_call" | custom-call | tf_op jit(solution)/shard_map/pallas_call | solution.py:239
  2.3 0.5 collective-permute-start
  2.8 0.9 %collective-permute-done = bf16[12,2176]{1,0:T(8,128)(2,1)S(1)} collective-permute-done((bf16[12,2176]{1,0:T(8,128)(2,1)S(1)}, bf16[12,2176]{1,0:T(8,128)(2,1)S(1)}, u32[]{:S(2)}, u32[]{:S(2)}) %collective-permute-start) | collective-permute-done | bytes 52256 | tf_op jit(solution)/shard_map/ppermute | solution.py:24
  3.8 2.9 %collective-permute-start.4 = (bf16[24,2176]{1,0:T(8,128)(2,1)S(1)}, bf16[24,2176]{1,0:T(8,128)(2,1)S(1)}, u32[]{:S(2)}, u32[]{:S(2)}) collective-permute-start(bf16[24,2176]{1,0:T(8,128)(2,1)S(1)} %get-tuple-element.39), channel_id=1, source_target_pairs={{0,8},{8,0},{16,24},{24,16},{1,9},{9,1},{17,25},{25,17},{2,10},{10... | collective-permute-start | bytes 313352 | tf_op jit(solution)/shard_map/ppermute | solution.py:24
  6.7 3.6 %collective-permute-start.3 = (bf16[24,2176]{1,0:T(8,128)(2,1)S(1)}, bf16[24,2176]{1,0:T(8,128)(2,1)S(1)}, u32[]{:S(2)}, u32[]{:S(2)}) collective-permute-start(bf16[24,2176]{1,0:T(8,128)(2,1)S(1)} %get-tuple-element.39), channel_id=1, source_target_pairs={{0,6},{2,4},{4,2},{6,0},{1,7},{3,5},{5,3},{7,1},{8,14},{10,12},{12... | collective-permute-start | bytes 313352 | tf_op jit(solution)/shard_map/ppermute | solution.py:24
  10.3 0.8 %collective-permute-start.1 = (bf16[24,2176]{1,0:T(8,128)(2,1)S(1)}, bf16[24,2176]{1,0:T(8,128)(2,1)S(1)}, u32[]{:S(2)}, u32[]{:S(2)}) collective-permute-start(bf16[24,2176]{1,0:T(8,128)(2,1)S(1)} %get-tuple-element.39), channel_id=1, source_target_pairs={{0,2},{2,0},{4,6},{6,4},{1,3},{3,1},{5,7},{7,5},{8,10},{10,8},{12,... | collective-permute-start | bytes 313352 | tf_op jit(solution)/shard_map/ppermute | solution.py:24
  11.1 1.5 %collective-permute-start.6 = (bf16[24,2176]{1,0:T(8,128)(2,1)S(1)}, bf16[24,2176]{1,0:T(8,128)(2,1)S(1)}, u32[]{:S(2)}, u32[]{:S(2)}) collective-permute-start(bf16[24,2176]{1,0:T(8,128)(2,1)S(1)} %get-tuple-element.39), channel_id=1, source_target_pairs={{0,24},{8,16},{16,8},{24,0},{1,25},{9,17},{17,9},{25,1},{2,26},{10... | collective-permute-start | bytes 313352 | tf_op jit(solution)/shard_map/ppermute | solution.py:24
  12.6 0.3 collective-permute-start.5
  12.8 6.4 %shard_map.78 = (bf16[2,4096,768]{2,1,0:T(8,128)(2,1)S(1)}, bf16[768,4096]{1,0:T(8,128)(2,1)S(1)}, f32[8,128]{1,0:T(8,128)S(1)}) custom-call(bf16[2,4096,768]{2,1,0:T(8,128)(2,1)} %up_ref.1, bf16[768,4096]{1,0:T(8,128)(2,1)} %bitcast.7, bf16[24,2176]{1,0:T(8,128)(2,1)S(1)} %collective-permute-done.4._), custom_call_target="tpu_custom_call" | custom-call | bytes 18874368 | tf_op jit(solution)/shard_map/pallas_call | solution.py:61
  19.5 0.1 collective-permute-start.7
  19.6 1.8 %collective-permute-start.9 = (bf16[72,2176]{1,0:T(8,128)(2,1)S(1)}, bf16[72,2176]{1,0:T(8,128)(2,1)S(1)}, u32[]{:S(2)}, u32[]{:S(2)}) collective-permute-start(bf16[72,2176]{1,0:T(8,128)(2,1)S(1)} %get-tuple-element.56), channel_id=1, source_target_pairs={{0,8},{8,0},{16,24},{24,16},{1,9},{9,1},{17,25},{25,17},{2,10},{10... | collective-permute-start | bytes 940040 | tf_op jit(solution)/shard_map/ppermute | solution.py:24
  21.4 1.5 %collective-permute-start.10 = (bf16[72,2176]{1,0:T(8,128)(2,1)S(1)}, bf16[72,2176]{1,0:T(8,128)(2,1)S(1)}, u32[]{:S(2)}, u32[]{:S(2)}) collective-permute-start(bf16[72,2176]{1,0:T(8,128)(2,1)S(1)} %get-tuple-element.56), channel_id=1, source_target_pairs={{0,16},{8,24},{16,0},{24,8},{1,17},{9,25},{17,1},{25,9},{2,18},{10... | collective-permute-start | bytes 940040 | tf_op jit(solution)/shard_map/ppermute | solution.py:24
  22.9 2.1 %collective-permute-start.12 = (bf16[24,2176]{1,0:T(8,128)(2,1)S(1)}, bf16[24,2176]{1,0:T(8,128)(2,1)S(1)}, u32[]{:S(2)}, u32[]{:S(2)}) collective-permute-start(bf16[24,2176]{1,0:T(8,128)(2,1)S(1)} %collective-permute-done.6), channel_id=1, source_target_pairs={{0,4},{2,6},{4,0},{6,2},{1,5},{3,7},{5,1},{7,3},{8,12},{10,14},{12... | collective-permute-start | bytes 313352 | tf_op jit(solution)/shard_map/ppermute | solution.py:24
  25.0 2.0 %collective-permute-start.11 = (bf16[24,2176]{1,0:T(8,128)(2,1)S(1)}, bf16[24,2176]{1,0:T(8,128)(2,1)S(1)}, u32[]{:S(2)}, u32[]{:S(2)}) collective-permute-start(bf16[24,2176]{1,0:T(8,128)(2,1)S(1)} %collective-permute-done.6), channel_id=1, source_target_pairs={{0,2},{2,0},{4,6},{6,4},{1,3},{3,1},{5,7},{7,5},{8,10},{10,8},{12,... | collective-permute-start | bytes 313352 | tf_op jit(solution)/shard_map/ppermute | solution.py:24
  27.0 0.2 collective-permute-start.13
  27.3 4.2 %shard_map.79 = (bf16[168,2048]{1,0:T(8,128)(2,1)S(1)}, bf16[168,2048]{1,0:T(8,128)(2,1)S(1)}) custom-call(s32[2]{0:T(128)S(1)} %pad_add_fusion.place.refs_0_, bf16[168,2176]{1,0:T(8,128)(2,1)S(1)} %constant_dynamic-update-slice_fusion.refs_1_, bf16[168,2048]{1,0:T(8,128)(2,1)S(1)} %collective-permute-done.7.refs_2_, ...), custom_call_target="tpu_custom_call" | custom-call | flops 3170893824 | tf_op jit(solution)/shard_map/pallas_call | solution.py:148
  31.6 1.0 %collective-permute-done.12 = bf16[24,2176]{1,0:T(8,128)(2,1)S(1)} collective-permute-done((bf16[24,2176]{1,0:T(8,128)(2,1)S(1)}, bf16[24,2176]{1,0:T(8,128)(2,1)S(1)}, u32[]{:S(2)}, u32[]{:S(2)}) %collective-permute-start.12) | collective-permute-done | bytes 104480 | tf_op jit(solution)/shard_map/ppermute | solution.py:24
  32.6 1.5 %collective-permute-done.13 = bf16[24,2176]{1,0:T(8,128)(2,1)S(1)} collective-permute-done((bf16[24,2176]{1,0:T(8,128)(2,1)S(1)}, bf16[24,2176]{1,0:T(8,128)(2,1)S(1)}, u32[]{:S(2)}, u32[]{:S(2)}) %collective-permute-start.13) | collective-permute-done | bytes 104480 | tf_op jit(solution)/shard_map/ppermute | solution.py:24
  34.1 0.1 slice.76
  34.2 0.1 collective-permute-start.14
  34.3 0.5 collective-permute-start.8
  34.8 2.1 %shard_map.80.refs_3_ = f32[2,216,768]{2,1,0:T(8,128)S(1)} custom-call(s32[2]{0:T(128)S(1)} %pad_add_fusion.place.refs_0_, bf16[216,2176]{1,0:T(8,128)(2,1)S(1)} %constant_dynamic-update-slice_fusion.10.own.refs_1_, bf16[2,4096,768]{2,1,0:T(8,128)(2,1)S(1)} %get-tuple-element.26.refs_3_.up.refs_4_), custom_call_target="tpu_custom_call" | custom-call | flops 1358954496 | tf_op jit(solution)/shard_map/pallas_call | solution.py:148
  36.9 3.0 %shard_map.81 = (bf16[216,2048]{1,0:T(8,128)(2,1)S(1)}, bf16[216,768]{1,0:T(8,128)(2,1)S(1)}) custom-call(s32[2]{0:T(128)S(1)} %pad_add_fusion.place.refs_0_, bf16[216,2176]{1,0:T(8,128)(2,1)S(1)} %constant_dynamic-update-slice_fusion.10.own.refs_1_, bf16[216,2048]{1,0:T(8,128)(2,1)S(1)} %collective-permute-done.14.refs_2_, ...), custom_call_target="tpu_custom_call" | custom-call | flops 2038431744 | tf_op jit(solution)/shard_map/pallas_call | solution.py:148
  39.9 0.1 collective-permute-start.15
  40.1 0.2 add_convert_fusion
  40.3 1.4 %shard_map.82.kept_ref = bf16[216,2048]{1,0:T(8,128)(2,1)S(1)} custom-call(s32[2]{0:T(128)S(1)} %pad_add_fusion.place.refs_0_, bf16[216,768]{1,0:T(8,128)(2,1)S(1)} %get-tuple-element.33.hidden, bf16[768,4096]{1,0:T(8,128)(2,1)S(1)} %get-tuple-element.27.refs_4_.refs_5_.down), custom_call_target="tpu_custom_call" | custom-call | flops 679477248 | tf_op jit(solution)/shard_map/pallas_call | solution.py:148
  41.8 0.6 collective-permute-done.15.taken_ref
  42.4 0.2 shard_map.83
  42.7 0.6 collective-permute-start.17
  43.3 0.6 collective-permute-start.16
  43.9 1.5 %collective-permute-start.23 = (bf16[24,2048]{1,0:T(8,128)(2,1)S(1)}, bf16[24,2048]{1,0:T(8,128)(2,1)S(1)}, u32[]{:S(2)}, u32[]{:S(2)}) collective-permute-start(bf16[24,2048]{1,0:T(8,128)(2,1)S(1)} %get-tuple-element.42), channel_id=1, source_target_pairs={{0,2},{2,0},{4,6},{6,4},{1,3},{3,1},{5,7},{7,5},{8,10},{10,8},{12,... | collective-permute-start | bytes 294920 | tf_op jit(solution)/shard_map/ppermute | solution.py:24
  45.5 1.9 %collective-permute-start.22 = (bf16[24,2048]{1,0:T(8,128)(2,1)S(1)}, bf16[24,2048]{1,0:T(8,128)(2,1)S(1)}, u32[]{:S(2)}, u32[]{:S(2)}) collective-permute-start(bf16[24,2048]{1,0:T(8,128)(2,1)S(1)} %get-tuple-element.43), channel_id=1, source_target_pairs={{0,4},{2,6},{4,0},{6,2},{1,5},{3,7},{5,1},{7,3},{8,12},{10,14},{12... | collective-permute-start | bytes 294920 | tf_op jit(solution)/shard_map/ppermute | solution.py:24
  47.3 1.4 %collective-permute-start.21 = (bf16[24,2048]{1,0:T(8,128)(2,1)S(1)}, bf16[24,2048]{1,0:T(8,128)(2,1)S(1)}, u32[]{:S(2)}, u32[]{:S(2)}) collective-permute-start(bf16[24,2048]{1,0:T(8,128)(2,1)S(1)} %get-tuple-element.44), channel_id=1, source_target_pairs={{0,6},{2,4},{4,2},{6,0},{1,7},{3,5},{5,3},{7,1},{8,14},{10,12},{12... | collective-permute-start | bytes 294920 | tf_op jit(solution)/shard_map/ppermute | solution.py:24
  48.7 5.2 %collective-permute-done.17 = bf16[96,2048]{1,0:T(8,128)(2,1)S(1)} collective-permute-done((bf16[96,2048]{1,0:T(8,128)(2,1)S(1)}, bf16[96,2048]{1,0:T(8,128)(2,1)S(1)}, u32[]{:S(2)}, u32[]{:S(2)}) %collective-permute-start.17) | collective-permute-done | bytes 393248 | tf_op jit(solution)/shard_map/ppermute | solution.py:24
  53.9 0.3 collective-permute-done.16
  54.2 0.1 add_convert_fusion.1
  54.4 1.8 %collective-permute-start.20 = (bf16[24,2048]{1,0:T(8,128)(2,1)S(1)}, bf16[24,2048]{1,0:T(8,128)(2,1)S(1)}, u32[]{:S(2)}, u32[]{:S(2)}) collective-permute-start(bf16[24,2048]{1,0:T(8,128)(2,1)S(1)} %get-tuple-element.48), channel_id=1, source_target_pairs={{0,2},{2,0},{4,6},{6,4},{1,3},{3,1},{5,7},{7,5},{8,10},{10,8},{12,... | collective-permute-start | bytes 294920 | tf_op jit(solution)/shard_map/ppermute | solution.py:24
  56.2 1.7 %collective-permute-start.19 = (bf16[24,2048]{1,0:T(8,128)(2,1)S(1)}, bf16[24,2048]{1,0:T(8,128)(2,1)S(1)}, u32[]{:S(2)}, u32[]{:S(2)}) collective-permute-start(bf16[24,2048]{1,0:T(8,128)(2,1)S(1)} %get-tuple-element.49), channel_id=1, source_target_pairs={{0,4},{2,6},{4,0},{6,2},{1,5},{3,7},{5,1},{7,3},{8,12},{10,14},{12... | collective-permute-start | bytes 294920 | tf_op jit(solution)/shard_map/ppermute | solution.py:24
  57.8 1.4 %collective-permute-start.18 = (bf16[24,2048]{1,0:T(8,128)(2,1)S(1)}, bf16[24,2048]{1,0:T(8,128)(2,1)S(1)}, u32[]{:S(2)}, u32[]{:S(2)}) collective-permute-start(bf16[24,2048]{1,0:T(8,128)(2,1)S(1)} %get-tuple-element.50), channel_id=1, source_target_pairs={{0,6},{2,4},{4,2},{6,0},{1,7},{3,5},{5,3},{7,1},{8,14},{10,12},{12... | collective-permute-start | bytes 294920 | tf_op jit(solution)/shard_map/ppermute | solution.py:24
  59.2 0.9 %collective-permute-done.20 = bf16[24,2048]{1,0:T(8,128)(2,1)S(1)} collective-permute-done((bf16[24,2048]{1,0:T(8,128)(2,1)S(1)}, bf16[24,2048]{1,0:T(8,128)(2,1)S(1)}, u32[]{:S(2)}, u32[]{:S(2)}) %collective-permute-start.20) | collective-permute-done | bytes 98336 | tf_op jit(solution)/shard_map/ppermute | solution.py:24
  60.2 1.6 %collective-permute-start.24 = (bf16[24,2048]{1,0:T(8,128)(2,1)S(1)}, bf16[24,2048]{1,0:T(8,128)(2,1)S(1)}, u32[]{:S(2)}, u32[]{:S(2)}) collective-permute-start(bf16[24,2048]{1,0:T(8,128)(2,1)S(1)} %add_convert_fusion.3), channel_id=1, source_target_pairs={{0,24},{8,16},{16,8},{24,0},{1,25},{9,17},{17,9},{25,1},{2,26},{10... | collective-permute-start | bytes 294920 | tf_op jit(solution)/shard_map/ppermute | solution.py:24
  61.8 1.4 %shard_map.84 = f32[1,128]{1,0:T(1,128)S(1)} custom-call(s32[8]{0:T(128)S(1)} %copy-done, bf16[168,128]{1,0:T(8,128)(2,1)S(1)} %slice.88.refs_1_, bf16[216,128]{1,0:T(8,128)(2,1)S(1)} %slice.89.refs_2_, bf16[24,2048]{1,0:T(8,128)(2,1)S(1)} %get-tuple-element.47.refs_3_), custom_call_target="tpu_custom_call" | custom-call | bytes 98304 | tf_op jit(solution)/shard_map/pallas_call | solution.py:307
  63.2 2.9 %collective-permute-done.19 = bf16[24,2048]{1,0:T(8,128)(2,1)S(1)} collective-permute-done((bf16[24,2048]{1,0:T(8,128)(2,1)S(1)}, bf16[24,2048]{1,0:T(8,128)(2,1)S(1)}, u32[]{:S(2)}, u32[]{:S(2)}) %collective-permute-start.19) | collective-permute-done | bytes 98336 | tf_op jit(solution)/shard_map/ppermute | solution.py:24
  66.3 0.1 collective-permute-start.25
  66.3 0.5 slice_bitcast_fusion
  66.9 0.7 %collective-permute-done.25 = bf16[12,2048]{1,0:T(8,128)(2,1)S(1)} collective-permute-done((bf16[12,2048]{1,0:T(8,128)(2,1)S(1)}, bf16[12,2048]{1,0:T(8,128)(2,1)S(1)}, u32[]{:S(2)}, u32[]{:S(2)}) %collective-permute-start.25) | collective-permute-done | bytes 49184 | tf_op jit(solution)/shard_map/ppermute | solution.py:24
  67.6 0.7 pad_maximum_fusion.2
  (46 shorter events, 0.7 us)
Async XLA Ops:
  2.3 1.4 %collective-permute-start = (bf16[12,2176]{1,0:T(8,128)(2,1)S(1)}, bf16[12,2176]{1,0:T(8,128)(2,1)S(1)}, u32[]{:S(2)}, u32[]{:S(2)}) collective-permute-start(bf16[12,2176]{1,0:T(8,128)(2,1)S(1)} %get-tuple-element.21), channel_id=1, source_target_pairs={{0,1},{1,0},{2,3},{3,2},{4,5},{5,4},{6,7},{7,6},{8,9},{9,8},{10,11... | collective-permute-start | bytes 156680 | tf_op jit(solution)/shard_map/ppermute | solution.py:24
  3.8 8.8 %collective-permute-start.4 = (bf16[24,2176]{1,0:T(8,128)(2,1)S(1)}, bf16[24,2176]{1,0:T(8,128)(2,1)S(1)}, u32[]{:S(2)}, u32[]{:S(2)}) collective-permute-start(bf16[24,2176]{1,0:T(8,128)(2,1)S(1)} %get-tuple-element.39), channel_id=1, source_target_pairs={{0,8},{8,0},{16,24},{24,16},{1,9},{9,1},{17,25},{25,17},{2,10},{10... | collective-permute-start | bytes 313352 | tf_op jit(solution)/shard_map/ppermute | solution.py:24
  6.7 12.6 %collective-permute-start.3 = (bf16[24,2176]{1,0:T(8,128)(2,1)S(1)}, bf16[24,2176]{1,0:T(8,128)(2,1)S(1)}, u32[]{:S(2)}, u32[]{:S(2)}) collective-permute-start(bf16[24,2176]{1,0:T(8,128)(2,1)S(1)} %get-tuple-element.39), channel_id=1, source_target_pairs={{0,6},{2,4},{4,2},{6,0},{1,7},{3,5},{5,3},{7,1},{8,14},{10,12},{12... | collective-permute-start | bytes 313352 | tf_op jit(solution)/shard_map/ppermute | solution.py:24
  10.3 9.0 %collective-permute-start.2 = (bf16[24,2176]{1,0:T(8,128)(2,1)S(1)}, bf16[24,2176]{1,0:T(8,128)(2,1)S(1)}, u32[]{:S(2)}, u32[]{:S(2)}) collective-permute-start(bf16[24,2176]{1,0:T(8,128)(2,1)S(1)} %get-tuple-element.39), channel_id=1, source_target_pairs={{0,4},{2,6},{4,0},{6,2},{1,5},{3,7},{5,1},{7,3},{8,12},{10,14},{12... | collective-permute-start | bytes 313352 | tf_op jit(solution)/shard_map/ppermute | solution.py:24
  10.3 9.0 %collective-permute-start.1 = (bf16[24,2176]{1,0:T(8,128)(2,1)S(1)}, bf16[24,2176]{1,0:T(8,128)(2,1)S(1)}, u32[]{:S(2)}, u32[]{:S(2)}) collective-permute-start(bf16[24,2176]{1,0:T(8,128)(2,1)S(1)} %get-tuple-element.39), channel_id=1, source_target_pairs={{0,2},{2,0},{4,6},{6,4},{1,3},{3,1},{5,7},{7,5},{8,10},{10,8},{12,... | collective-permute-start | bytes 313352 | tf_op jit(solution)/shard_map/ppermute | solution.py:24
  11.1 8.3 %collective-permute-start.6 = (bf16[24,2176]{1,0:T(8,128)(2,1)S(1)}, bf16[24,2176]{1,0:T(8,128)(2,1)S(1)}, u32[]{:S(2)}, u32[]{:S(2)}) collective-permute-start(bf16[24,2176]{1,0:T(8,128)(2,1)S(1)} %get-tuple-element.39), channel_id=1, source_target_pairs={{0,24},{8,16},{16,8},{24,0},{1,25},{9,17},{17,9},{25,1},{2,26},{10... | collective-permute-start | bytes 313352 | tf_op jit(solution)/shard_map/ppermute | solution.py:24
  12.6 6.8 %collective-permute-start.5 = (bf16[24,2176]{1,0:T(8,128)(2,1)S(1)}, bf16[24,2176]{1,0:T(8,128)(2,1)S(1)}, u32[]{:S(2)}, u32[]{:S(2)}) collective-permute-start(bf16[24,2176]{1,0:T(8,128)(2,1)S(1)} %get-tuple-element.39), channel_id=1, source_target_pairs={{0,16},{8,24},{16,0},{24,8},{1,17},{9,25},{17,1},{25,9},{2,18},{10... | collective-permute-start | bytes 313352 | tf_op jit(solution)/shard_map/ppermute | solution.py:24
  19.5 7.5 %collective-permute-start.7 = (bf16[168,2048]{1,0:T(8,128)(2,1)S(1)}, bf16[168,2048]{1,0:T(8,128)(2,1)S(1)}, u32[]{:S(2)}, u32[]{:S(2)}) collective-permute-start(bf16[168,2048]{1,0:T(8,128)(2,1)S(1)} %slice.74), channel_id=1, source_target_pairs={{0,1},{1,0},{2,3},{3,2},{4,5},{5,4},{6,7},{7,6},{8,9},{9,8},{10,11... | collective-permute-start | bytes 2064392 | tf_op jit(solution)/shard_map/ppermute | solution.py:24
  19.6 11.9 %collective-permute-start.9 = (bf16[72,2176]{1,0:T(8,128)(2,1)S(1)}, bf16[72,2176]{1,0:T(8,128)(2,1)S(1)}, u32[]{:S(2)}, u32[]{:S(2)}) collective-permute-start(bf16[72,2176]{1,0:T(8,128)(2,1)S(1)} %get-tuple-element.56), channel_id=1, source_target_pairs={{0,8},{8,0},{16,24},{24,16},{1,9},{9,1},{17,25},{25,17},{2,10},{10... | collective-permute-start | bytes 940040 | tf_op jit(solution)/shard_map/ppermute | solution.py:24
  21.4 10.1 %collective-permute-start.10 = (bf16[72,2176]{1,0:T(8,128)(2,1)S(1)}, bf16[72,2176]{1,0:T(8,128)(2,1)S(1)}, u32[]{:S(2)}, u32[]{:S(2)}) collective-permute-start(bf16[72,2176]{1,0:T(8,128)(2,1)S(1)} %get-tuple-element.56), channel_id=1, source_target_pairs={{0,16},{8,24},{16,0},{24,8},{1,17},{9,25},{17,1},{25,9},{2,18},{10... | collective-permute-start | bytes 940040 | tf_op jit(solution)/shard_map/ppermute | solution.py:24
  22.9 9.7 %collective-permute-start.12 = (bf16[24,2176]{1,0:T(8,128)(2,1)S(1)}, bf16[24,2176]{1,0:T(8,128)(2,1)S(1)}, u32[]{:S(2)}, u32[]{:S(2)}) collective-permute-start(bf16[24,2176]{1,0:T(8,128)(2,1)S(1)} %collective-permute-done.6), channel_id=1, source_target_pairs={{0,4},{2,6},{4,0},{6,2},{1,5},{3,7},{5,1},{7,3},{8,12},{10,14},{12... | collective-permute-start | bytes 313352 | tf_op jit(solution)/shard_map/ppermute | solution.py:24
  25.0 6.6 %collective-permute-start.11 = (bf16[24,2176]{1,0:T(8,128)(2,1)S(1)}, bf16[24,2176]{1,0:T(8,128)(2,1)S(1)}, u32[]{:S(2)}, u32[]{:S(2)}) collective-permute-start(bf16[24,2176]{1,0:T(8,128)(2,1)S(1)} %collective-permute-done.6), channel_id=1, source_target_pairs={{0,2},{2,0},{4,6},{6,4},{1,3},{3,1},{5,7},{7,5},{8,10},{10,8},{12,... | collective-permute-start | bytes 313352 | tf_op jit(solution)/shard_map/ppermute | solution.py:24
  27.0 7.0 %collective-permute-start.13 = (bf16[24,2176]{1,0:T(8,128)(2,1)S(1)}, bf16[24,2176]{1,0:T(8,128)(2,1)S(1)}, u32[]{:S(2)}, u32[]{:S(2)}) collective-permute-start(bf16[24,2176]{1,0:T(8,128)(2,1)S(1)} %collective-permute-done.6), channel_id=1, source_target_pairs={{0,6},{2,4},{4,2},{6,0},{1,7},{3,5},{5,3},{7,1},{8,14},{10,12},{12... | collective-permute-start | bytes 313352 | tf_op jit(solution)/shard_map/ppermute | solution.py:24
  34.2 2.7 %collective-permute-start.14 = (bf16[216,2048]{1,0:T(8,128)(2,1)S(1)}, bf16[216,2048]{1,0:T(8,128)(2,1)S(1)}, u32[]{:S(2)}, u32[]{:S(2)}) collective-permute-start(bf16[216,2048]{1,0:T(8,128)(2,1)S(1)} %slice.76), channel_id=1, source_target_pairs={{0,1},{1,0},{2,3},{3,2},{4,5},{5,4},{6,7},{7,6},{8,9},{9,8},{10,11... | collective-permute-start | bytes 2654216 | tf_op jit(solution)/shard_map/ppermute | solution.py:24
  34.3 5.8 %collective-permute-start.8 = (bf16[168,2048]{1,0:T(8,128)(2,1)S(1)}, bf16[168,2048]{1,0:T(8,128)(2,1)S(1)}, u32[]{:S(2)}, u32[]{:S(2)}) collective-permute-start(bf16[168,2048]{1,0:T(8,128)(2,1)S(1)} %get-tuple-element.30), channel_id=1, source_target_pairs={{0,1},{1,0},{2,3},{3,2},{4,5},{5,4},{6,7},{7,6},{8,9},{9,8},{10,11... | collective-permute-start | bytes 2064392 | tf_op jit(solution)/shard_map/ppermute | solution.py:24
  39.9 2.5 %collective-permute-start.15 = (bf16[216,2048]{1,0:T(8,128)(2,1)S(1)}, bf16[216,2048]{1,0:T(8,128)(2,1)S(1)}, u32[]{:S(2)}, u32[]{:S(2)}) collective-permute-start(bf16[216,2048]{1,0:T(8,128)(2,1)S(1)} %get-tuple-element.34), channel_id=1, source_target_pairs={{0,1},{1,0},{2,3},{3,2},{4,5},{5,4},{6,7},{7,6},{8,9},{9,8},{10,11... | collective-permute-start | bytes 2654216 | tf_op jit(solution)/shard_map/ppermute | solution.py:24
  41.8 20.0 %copy-start = (s32[8]{0:T(128)S(1)}, s32[8]{0:T(128)}, u32[]{:S(2)}) copy-start(s32[8]{0:T(128)} %refs_0_.3) | copy-start | bytes 100
  42.7 11.2 %collective-permute-start.17 = (bf16[96,2048]{1,0:T(8,128)(2,1)S(1)}, bf16[96,2048]{1,0:T(8,128)(2,1)S(1)}, u32[]{:S(2)}, u32[]{:S(2)}) collective-permute-start(bf16[96,2048]{1,0:T(8,128)(2,1)S(1)} %pad_maximum_fusion.1), channel_id=1, source_target_pairs={{0,16},{8,24},{16,0},{24,8},{1,17},{9,25},{17,1},{25,9},{2,18},{10... | collective-permute-start | bytes 1179656 | tf_op jit(solution)/shard_map/ppermute | solution.py:24
  43.3 10.9 %collective-permute-start.16 = (bf16[96,2048]{1,0:T(8,128)(2,1)S(1)}, bf16[96,2048]{1,0:T(8,128)(2,1)S(1)}, u32[]{:S(2)}, u32[]{:S(2)}) collective-permute-start(bf16[96,2048]{1,0:T(8,128)(2,1)S(1)} %pad_maximum_fusion), channel_id=1, source_target_pairs={{0,8},{8,0},{16,24},{24,16},{1,9},{9,1},{17,25},{25,17},{2,10},{10... | collective-permute-start | bytes 1179656 | tf_op jit(solution)/shard_map/ppermute | solution.py:24
  43.9 13.9 %collective-permute-start.23 = (bf16[24,2048]{1,0:T(8,128)(2,1)S(1)}, bf16[24,2048]{1,0:T(8,128)(2,1)S(1)}, u32[]{:S(2)}, u32[]{:S(2)}) collective-permute-start(bf16[24,2048]{1,0:T(8,128)(2,1)S(1)} %get-tuple-element.42), channel_id=1, source_target_pairs={{0,2},{2,0},{4,6},{6,4},{1,3},{3,1},{5,7},{7,5},{8,10},{10,8},{12,... | collective-permute-start | bytes 294920 | tf_op jit(solution)/shard_map/ppermute | solution.py:24
  45.5 13.8 %collective-permute-start.22 = (bf16[24,2048]{1,0:T(8,128)(2,1)S(1)}, bf16[24,2048]{1,0:T(8,128)(2,1)S(1)}, u32[]{:S(2)}, u32[]{:S(2)}) collective-permute-start(bf16[24,2048]{1,0:T(8,128)(2,1)S(1)} %get-tuple-element.43), channel_id=1, source_target_pairs={{0,4},{2,6},{4,0},{6,2},{1,5},{3,7},{5,1},{7,3},{8,12},{10,14},{12... | collective-permute-start | bytes 294920 | tf_op jit(solution)/shard_map/ppermute | solution.py:24
  47.3 11.9 %collective-permute-start.21 = (bf16[24,2048]{1,0:T(8,128)(2,1)S(1)}, bf16[24,2048]{1,0:T(8,128)(2,1)S(1)}, u32[]{:S(2)}, u32[]{:S(2)}) collective-permute-start(bf16[24,2048]{1,0:T(8,128)(2,1)S(1)} %get-tuple-element.44), channel_id=1, source_target_pairs={{0,6},{2,4},{4,2},{6,0},{1,7},{3,5},{5,3},{7,1},{8,14},{10,12},{12... | collective-permute-start | bytes 294920 | tf_op jit(solution)/shard_map/ppermute | solution.py:24
  54.4 5.7 %collective-permute-start.20 = (bf16[24,2048]{1,0:T(8,128)(2,1)S(1)}, bf16[24,2048]{1,0:T(8,128)(2,1)S(1)}, u32[]{:S(2)}, u32[]{:S(2)}) collective-permute-start(bf16[24,2048]{1,0:T(8,128)(2,1)S(1)} %get-tuple-element.48), channel_id=1, source_target_pairs={{0,2},{2,0},{4,6},{6,4},{1,3},{3,1},{5,7},{7,5},{8,10},{10,8},{12,... | collective-permute-start | bytes 294920 | tf_op jit(solution)/shard_map/ppermute | solution.py:24
  56.2 10.0 %collective-permute-start.19 = (bf16[24,2048]{1,0:T(8,128)(2,1)S(1)}, bf16[24,2048]{1,0:T(8,128)(2,1)S(1)}, u32[]{:S(2)}, u32[]{:S(2)}) collective-permute-start(bf16[24,2048]{1,0:T(8,128)(2,1)S(1)} %get-tuple-element.49), channel_id=1, source_target_pairs={{0,4},{2,6},{4,0},{6,2},{1,5},{3,7},{5,1},{7,3},{8,12},{10,14},{12... | collective-permute-start | bytes 294920 | tf_op jit(solution)/shard_map/ppermute | solution.py:24
  57.8 8.3 %collective-permute-start.18 = (bf16[24,2048]{1,0:T(8,128)(2,1)S(1)}, bf16[24,2048]{1,0:T(8,128)(2,1)S(1)}, u32[]{:S(2)}, u32[]{:S(2)}) collective-permute-start(bf16[24,2048]{1,0:T(8,128)(2,1)S(1)} %get-tuple-element.50), channel_id=1, source_target_pairs={{0,6},{2,4},{4,2},{6,0},{1,7},{3,5},{5,3},{7,1},{8,14},{10,12},{12... | collective-permute-start | bytes 294920 | tf_op jit(solution)/shard_map/ppermute | solution.py:24
  60.2 5.9 %collective-permute-start.24 = (bf16[24,2048]{1,0:T(8,128)(2,1)S(1)}, bf16[24,2048]{1,0:T(8,128)(2,1)S(1)}, u32[]{:S(2)}, u32[]{:S(2)}) collective-permute-start(bf16[24,2048]{1,0:T(8,128)(2,1)S(1)} %add_convert_fusion.3), channel_id=1, source_target_pairs={{0,24},{8,16},{16,8},{24,0},{1,25},{9,17},{17,9},{25,1},{2,26},{10... | collective-permute-start | bytes 294920 | tf_op jit(solution)/shard_map/ppermute | solution.py:24
  66.3 1.3 %collective-permute-start.25 = (bf16[12,2048]{1,0:T(8,128)(2,1)S(1)}, bf16[12,2048]{1,0:T(8,128)(2,1)S(1)}, u32[]{:S(2)}, u32[]{:S(2)}) collective-permute-start(bf16[12,2048]{1,0:T(8,128)(2,1)S(1)} %broadcast_select_fusion.4), channel_id=1, source_target_pairs={{0,1},{1,0},{2,3},{3,2},{4,5},{5,4},{6,7},{7,6},{8,9},{9,8},{10,11... | collective-permute-start | bytes 147464 | tf_op jit(solution)/shard_map/ppermute | solution.py:24

commit v22 on v20

--- a/solution.py
+++ b/solution.py
@@ -7,6 +7,7 @@
 from jax.sharding import Mesh, PartitionSpec as P
 
 LANES = 128
+DOWN_PARTS = 4
 PART = 1024.0
 CHUNK = 1024
 MOST_ROWS = 512
@@ -46,10 +47,20 @@
 
 
 def load_weight_kernel(weight_ref, _, weight_out, mark_ref, sem):
-    copy = pltpu.make_async_copy(weight_ref, weight_out, sem)
-    copy.start()
+    copies = piecewise(weight_ref.at, weight_out.at, sem, [(e, k) for e in range(weight_ref.shape[0]) for k in range(0, weight_ref.shape[1], CHUNK)])
     mark_ref[...] = jnp.zeros_like(mark_ref)
-    copy.wait()
+    for copy in copies:
+        copy.wait()
+
+
+def piecewise(source, target, sems, places):
+    copies = [
+        pltpu.make_async_copy(source[e, pl.ds(k, CHUNK)], target[e, pl.ds(k, CHUNK)], sems.at[n])
+        for n, (e, k) in enumerate(places)
+    ]
+    for copy in copies:
+        copy.start()
+    return copies
 
 
 def loaded(weight, after):
@@ -61,7 +72,9 @@
             pltpu.VMEM(weight.shape, weight.dtype),
             pltpu.VMEM((8, LANES), jnp.float32),
         ],
-        scratch_shapes=[pltpu.SemaphoreType.DMA],
+        scratch_shapes=[
+            pltpu.SemaphoreType.DMA((weight.shape[0] * weight.shape[1] // CHUNK,))
+        ],
         compiler_params=pltpu.CompilerParams(vmem_limit_bytes=VMEM_LIMIT),
         cost_estimate=pl.CostEstimate(flops=0, bytes_accessed=weight.nbytes, transcendentals=0),
     )(pltpu.with_memory_space_constraint(weight, pltpu.HBM), after)
@@ -105,8 +118,15 @@
 def sums_kernel(top_count, filling, place, own, other, up, *refs):
     if filling:
         down_ref, _, keep_ref, give_ref, down, acc, hidden, sem = refs
-        copy = pltpu.make_async_copy(down_ref, down, sem)
-        copy.start()
+        step = down.shape[0] // DOWN_PARTS
+        copies = [
+            pltpu.make_async_copy(
+                down_ref.at[pl.ds(n * step, step)], down.at[pl.ds(n * step, step)], sem.at[n]
+            )
+            for n in range(DOWN_PARTS)
+        ]
+        for copy in copies:
+            copy.start()
     else:
         down, keep_ref, give_ref, acc, hidden = refs
     part = other.shape[1]
@@ -116,7 +136,8 @@
     add_up(acc, [[other]], [part], up, bases[1])
     make_hidden(hidden, acc, [own], part, place[1], top_count)
     if filling:
-        copy.wait()
+        for copy in copies:
+            copy.wait()
     multiply_down(give_ref, hidden, down, bases[1])
     multiply_down(keep_ref, hidden, down, bases[0])
 
@@ -174,7 +195,7 @@
     if filling:
         operands[-1:] = [pltpu.with_memory_space_constraint(down, pltpu.HBM), mark]
         out_shape.append(pltpu.VMEM(down.shape, down.dtype))
-        scratch.append(pltpu.SemaphoreType.DMA)
+        scratch.append(pltpu.SemaphoreType.DMA((DOWN_PARTS,)))
     return call(
         lambda *refs: sums_kernel(top_count, filling, *refs),
         operands,

time: 66.8 us -> 66.8 us (level)
  no operation moved by 1% of the time
where the time goes in v22:
time: 66.8 us; the launch traced here: 66.6 us
  starting transfers between devices  29.9 us (45%)
  Pallas kernels  21.1 us (32%)
  waiting for transfers between devices  12.3 us (18%)
  other arithmetic  1.39 us (2%)
  local copies, waits for them, and re-layouts  1.02 us (2%)
  between operations  0.96 us (1%)
    ppermute x26, starting transfers between devices, swap(): return row_major(lax.ppermute(row_major(value), axis, pairs))  29.9 us
    pallas_call x4, Pallas kernels, call(): pl.pallas_call(kernel, in_specs=[pl.BlockSpec(memory_space=pltpu.SMEM)] +...  13.1 us
    ppermute x26, waiting for transfers between devices, swap(): return row_major(lax.ppermute(row_major(value), axis, pairs))  12.3 us
    pallas_call x1, Pallas kernels, loaded(): pl.pallas_call(load_weight_kernel, in_specs=[pl.BlockSpec(memory_space=pl...  4.7 us
    pallas_call x1, Pallas kernels, first_halves(): pl.pallas_call(first_kernel, in_specs=[pl.BlockSpec(memory_space=pltpu.SM...  1.56 us
    pallas_call x1, Pallas kernels, planned_load(): pl.pallas_call(lambda *refs: load_kernel(layout, *refs), in_specs=[pl.Blo...  1.44 us
  transfers between devices with their start and end apart: 26, of which 8 were waited for; matrix products, arithmetic and copies ran while one was open for 2% of the time, Pallas kernels for 29%

profile of v22, /device:TPU:0, one launch (start us, length us, event | category | flops | bytes accessed | tf_op | source)
XLA Modules:
  0.0 66.6 jit_solution(11181095248282817611)
XLA Ops:
  0.6 0.1 pad_add_fusion.place.refs_0_
  0.7 1.6 %shard_map.77 = (bf16[12,2176]{1,0:T(8,128)(2,1)S(1)}, bf16[12,2176]{1,0:T(8,128)(2,1)S(1)}) custom-call(s32[2]{0:T(128)S(1)} %pad_add_fusion.place.refs_0_, bf16[12,4096]{1,0:T(8,128)(2,1)} %refs_0_.2, s32[8,12]{1,0:T(8,128)} %bitcast.8, f32[8,12]{1,0:T(8,128)} %bitcast.9), custom_call_target="tpu_custom_call" | custom-call | tf_op jit(solution)/shard_map/pallas_call | solution.py:267
  2.3 0.5 collective-permute-start
  2.8 0.9 %collective-permute-done = bf16[12,2176]{1,0:T(8,128)(2,1)S(1)} collective-permute-done((bf16[12,2176]{1,0:T(8,128)(2,1)S(1)}, bf16[12,2176]{1,0:T(8,128)(2,1)S(1)}, u32[]{:S(2)}, u32[]{:S(2)}) %collective-permute-start) | collective-permute-done | bytes 52256 | tf_op jit(solution)/shard_map/ppermute | solution.py:25
  3.8 2.9 %collective-permute-start.4 = (bf16[24,2176]{1,0:T(8,128)(2,1)S(1)}, bf16[24,2176]{1,0:T(8,128)(2,1)S(1)}, u32[]{:S(2)}, u32[]{:S(2)}) collective-permute-start(bf16[24,2176]{1,0:T(8,128)(2,1)S(1)} %get-tuple-element.39), channel_id=1, source_target_pairs={{0,8},{8,0},{16,24},{24,16},{1,9},{9,1},{17,25},{25,17},{2,10},{10... | collective-permute-start | bytes 313352 | tf_op jit(solution)/shard_map/ppermute | solution.py:25
  6.7 3.6 %collective-permute-start.3 = (bf16[24,2176]{1,0:T(8,128)(2,1)S(1)}, bf16[24,2176]{1,0:T(8,128)(2,1)S(1)}, u32[]{:S(2)}, u32[]{:S(2)}) collective-permute-start(bf16[24,2176]{1,0:T(8,128)(2,1)S(1)} %get-tuple-element.39), channel_id=1, source_target_pairs={{0,6},{2,4},{4,2},{6,0},{1,7},{3,5},{5,3},{7,1},{8,14},{10,12},{12... | collective-permute-start | bytes 313352 | tf_op jit(solution)/shard_map/ppermute | solution.py:25
  10.3 0.8 %collective-permute-start.1 = (bf16[24,2176]{1,0:T(8,128)(2,1)S(1)}, bf16[24,2176]{1,0:T(8,128)(2,1)S(1)}, u32[]{:S(2)}, u32[]{:S(2)}) collective-permute-start(bf16[24,2176]{1,0:T(8,128)(2,1)S(1)} %get-tuple-element.39), channel_id=1, source_target_pairs={{0,2},{2,0},{4,6},{6,4},{1,3},{3,1},{5,7},{7,5},{8,10},{10,8},{12,... | collective-permute-start | bytes 313352 | tf_op jit(solution)/shard_map/ppermute | solution.py:25
  11.1 1.5 %collective-permute-start.6 = (bf16[24,2176]{1,0:T(8,128)(2,1)S(1)}, bf16[24,2176]{1,0:T(8,128)(2,1)S(1)}, u32[]{:S(2)}, u32[]{:S(2)}) collective-permute-start(bf16[24,2176]{1,0:T(8,128)(2,1)S(1)} %get-tuple-element.39), channel_id=1, source_target_pairs={{0,24},{8,16},{16,8},{24,0},{1,25},{9,17},{17,9},{25,1},{2,26},{10... | collective-permute-start | bytes 313352 | tf_op jit(solution)/shard_map/ppermute | solution.py:25
  12.6 0.3 collective-permute-start.5
  12.8 4.7 %shard_map.78 = (bf16[2,4096,768]{2,1,0:T(8,128)(2,1)S(1)}, f32[8,128]{1,0:T(8,128)S(1)}) custom-call(bf16[2,4096,768]{2,1,0:T(8,128)(2,1)} %weight_ref.1, bf16[24,2176]{1,0:T(8,128)(2,1)S(1)} %collective-permute-done.4._), custom_call_target="tpu_custom_call" | custom-call | bytes 12582912 | tf_op jit(solution)/shard_map/pallas_call | solution.py:67
  17.6 1.5 %collective-permute-done.2 = bf16[24,2176]{1,0:T(8,128)(2,1)S(1)} collective-permute-done((bf16[24,2176]{1,0:T(8,128)(2,1)S(1)}, bf16[24,2176]{1,0:T(8,128)(2,1)S(1)}, u32[]{:S(2)}, u32[]{:S(2)}) %collective-permute-start.2) | collective-permute-done | bytes 104480 | tf_op jit(solution)/shard_map/ppermute | solution.py:25
  19.3 0.1 slice.74
  19.3 0.1 collective-permute-start.7
  19.4 0.6 collective-permute-start.9
  20.0 1.5 %collective-permute-start.10 = (bf16[72,2176]{1,0:T(8,128)(2,1)S(1)}, bf16[72,2176]{1,0:T(8,128)(2,1)S(1)}, u32[]{:S(2)}, u32[]{:S(2)}) collective-permute-start(bf16[72,2176]{1,0:T(8,128)(2,1)S(1)} %get-tuple-element.56), channel_id=1, source_target_pairs={{0,16},{8,24},{16,0},{24,8},{1,17},{9,25},{17,1},{25,9},{2,18},{10... | collective-permute-start | bytes 940040 | tf_op jit(solution)/shard_map/ppermute | solution.py:25
  21.5 1.8 %collective-permute-start.12 = (bf16[24,2176]{1,0:T(8,128)(2,1)S(1)}, bf16[24,2176]{1,0:T(8,128)(2,1)S(1)}, u32[]{:S(2)}, u32[]{:S(2)}) collective-permute-start(bf16[24,2176]{1,0:T(8,128)(2,1)S(1)} %collective-permute-done.6), channel_id=1, source_target_pairs={{0,4},{2,6},{4,0},{6,2},{1,5},{3,7},{5,1},{7,3},{8,12},{10,14},{12... | collective-permute-start | bytes 313352 | tf_op jit(solution)/shard_map/ppermute | solution.py:25
  23.3 2.0 %collective-permute-start.11 = (bf16[24,2176]{1,0:T(8,128)(2,1)S(1)}, bf16[24,2176]{1,0:T(8,128)(2,1)S(1)}, u32[]{:S(2)}, u32[]{:S(2)}) collective-permute-start(bf16[24,2176]{1,0:T(8,128)(2,1)S(1)} %collective-permute-done.6), channel_id=1, source_target_pairs={{0,2},{2,0},{4,6},{6,4},{1,3},{3,1},{5,7},{7,5},{8,10},{10,8},{12,... | collective-permute-start | bytes 313352 | tf_op jit(solution)/shard_map/ppermute | solution.py:25
  25.4 0.6 collective-permute-start.13
  25.9 6.6 %shard_map.79 = (bf16[168,2048]{1,0:T(8,128)(2,1)S(1)}, bf16[168,2048]{1,0:T(8,128)(2,1)S(1)}, bf16[768,4096]{1,0:T(8,128)(2,1)S(1)}) custom-call(s32[2]{0:T(128)S(1)} %pad_add_fusion.place.refs_0_, bf16[168,2176]{1,0:T(8,128)(2,1)S(1)} %constant_dynamic-update-slice_fusion.refs_1_, bf16[168,2048]{1,0:T(8,128)(2,1)S(1)} %collective-permute-done.7.refs_2_, ...), custom_call_target="tpu_custom_call" | custom-call | flops 3170893824 | tf_op jit(solution)/shard_map/pallas_call | solution.py:168
  32.7 0.1 slice.76
  32.8 0.1 collective-permute-start.14
  32.9 0.5 collective-permute-start.8
  33.4 2.1 %shard_map.80.refs_3_ = f32[2,216,768]{2,1,0:T(8,128)S(1)} custom-call(s32[2]{0:T(128)S(1)} %pad_add_fusion.place.refs_0_, bf16[216,2176]{1,0:T(8,128)(2,1)S(1)} %constant_dynamic-update-slice_fusion.10.own.refs_1_, bf16[2,4096,768]{2,1,0:T(8,128)(2,1)S(1)} %get-tuple-element.26.refs_3_.up.refs_4_), custom_call_target="tpu_custom_call" | custom-call | flops 1358954496 | tf_op jit(solution)/shard_map/pallas_call | solution.py:168
  35.5 3.0 %shard_map.81 = (bf16[216,2048]{1,0:T(8,128)(2,1)S(1)}, bf16[216,768]{1,0:T(8,128)(2,1)S(1)}) custom-call(s32[2]{0:T(128)S(1)} %pad_add_fusion.place.refs_0_, bf16[216,2176]{1,0:T(8,128)(2,1)S(1)} %constant_dynamic-update-slice_fusion.10.own.refs_1_, bf16[216,2048]{1,0:T(8,128)(2,1)S(1)} %collective-permute-done.14.refs_2_, ...), custom_call_target="tpu_custom_call" | custom-call | flops 2038431744 | tf_op jit(solution)/shard_map/pallas_call | solution.py:168
  38.5 0.1 collective-permute-start.15
  38.7 0.2 add_convert_fusion
  38.9 1.4 %shard_map.82.kept_ref = bf16[216,2048]{1,0:T(8,128)(2,1)S(1)} custom-call(s32[2]{0:T(128)S(1)} %pad_add_fusion.place.refs_0_, bf16[216,768]{1,0:T(8,128)(2,1)S(1)} %get-tuple-element.33.hidden, bf16[768,4096]{1,0:T(8,128)(2,1)S(1)} %get-tuple-element.32.refs_5_.down), custom_call_target="tpu_custom_call" | custom-call | flops 679477248 | tf_op jit(solution)/shard_map/pallas_call | solution.py:168
  40.4 0.6 collective-permute-done.15.taken_ref
  41.0 0.2 shard_map.83
  41.3 0.6 collective-permute-start.17
  41.9 1.6 %collective-permute-start.16 = (bf16[96,2048]{1,0:T(8,128)(2,1)S(1)}, bf16[96,2048]{1,0:T(8,128)(2,1)S(1)}, u32[]{:S(2)}, u32[]{:S(2)}) collective-permute-start(bf16[96,2048]{1,0:T(8,128)(2,1)S(1)} %pad_maximum_fusion), channel_id=1, source_target_pairs={{0,8},{8,0},{16,24},{24,16},{1,9},{9,1},{17,25},{25,17},{2,10},{10... | collective-permute-start | bytes 1179656 | tf_op jit(solution)/shard_map/ppermute | solution.py:25
  43.5 1.7 %collective-permute-start.23 = (bf16[24,2048]{1,0:T(8,128)(2,1)S(1)}, bf16[24,2048]{1,0:T(8,128)(2,1)S(1)}, u32[]{:S(2)}, u32[]{:S(2)}) collective-permute-start(bf16[24,2048]{1,0:T(8,128)(2,1)S(1)} %get-tuple-element.42), channel_id=1, source_target_pairs={{0,2},{2,0},{4,6},{6,4},{1,3},{3,1},{5,7},{7,5},{8,10},{10,8},{12,... | collective-permute-start | bytes 294920 | tf_op jit(solution)/shard_map/ppermute | solution.py:25
  45.2 1.4 %collective-permute-start.22 = (bf16[24,2048]{1,0:T(8,128)(2,1)S(1)}, bf16[24,2048]{1,0:T(8,128)(2,1)S(1)}, u32[]{:S(2)}, u32[]{:S(2)}) collective-permute-start(bf16[24,2048]{1,0:T(8,128)(2,1)S(1)} %get-tuple-element.43), channel_id=1, source_target_pairs={{0,4},{2,6},{4,0},{6,2},{1,5},{3,7},{5,1},{7,3},{8,12},{10,14},{12... | collective-permute-start | bytes 294920 | tf_op jit(solution)/shard_map/ppermute | solution.py:25
  46.6 1.4 %collective-permute-start.21 = (bf16[24,2048]{1,0:T(8,128)(2,1)S(1)}, bf16[24,2048]{1,0:T(8,128)(2,1)S(1)}, u32[]{:S(2)}, u32[]{:S(2)}) collective-permute-start(bf16[24,2048]{1,0:T(8,128)(2,1)S(1)} %get-tuple-element.44), channel_id=1, source_target_pairs={{0,6},{2,4},{4,2},{6,0},{1,7},{3,5},{5,3},{7,1},{8,14},{10,12},{12... | collective-permute-start | bytes 294920 | tf_op jit(solution)/shard_map/ppermute | solution.py:25
  48.0 4.6 %collective-permute-done.17 = bf16[96,2048]{1,0:T(8,128)(2,1)S(1)} collective-permute-done((bf16[96,2048]{1,0:T(8,128)(2,1)S(1)}, bf16[96,2048]{1,0:T(8,128)(2,1)S(1)}, u32[]{:S(2)}, u32[]{:S(2)}) %collective-permute-start.17) | collective-permute-done | bytes 393248 | tf_op jit(solution)/shard_map/ppermute | solution.py:25
  52.5 0.3 collective-permute-done.16
  52.9 0.1 add_convert_fusion.1
  53.0 1.8 %collective-permute-start.20 = (bf16[24,2048]{1,0:T(8,128)(2,1)S(1)}, bf16[24,2048]{1,0:T(8,128)(2,1)S(1)}, u32[]{:S(2)}, u32[]{:S(2)}) collective-permute-start(bf16[24,2048]{1,0:T(8,128)(2,1)S(1)} %get-tuple-element.48), channel_id=1, source_target_pairs={{0,2},{2,0},{4,6},{6,4},{1,3},{3,1},{5,7},{7,5},{8,10},{10,8},{12,... | collective-permute-start | bytes 294920 | tf_op jit(solution)/shard_map/ppermute | solution.py:25
  54.9 2.1 %collective-permute-start.19 = (bf16[24,2048]{1,0:T(8,128)(2,1)S(1)}, bf16[24,2048]{1,0:T(8,128)(2,1)S(1)}, u32[]{:S(2)}, u32[]{:S(2)}) collective-permute-start(bf16[24,2048]{1,0:T(8,128)(2,1)S(1)} %get-tuple-element.49), channel_id=1, source_target_pairs={{0,4},{2,6},{4,0},{6,2},{1,5},{3,7},{5,1},{7,3},{8,12},{10,14},{12... | collective-permute-start | bytes 294920 | tf_op jit(solution)/shard_map/ppermute | solution.py:25
  56.9 0.6 collective-permute-start.18
  57.6 1.2 %collective-permute-done.20 = bf16[24,2048]{1,0:T(8,128)(2,1)S(1)} collective-permute-done((bf16[24,2048]{1,0:T(8,128)(2,1)S(1)}, bf16[24,2048]{1,0:T(8,128)(2,1)S(1)}, u32[]{:S(2)}, u32[]{:S(2)}) %collective-permute-start.20) | collective-permute-done | bytes 98336 | tf_op jit(solution)/shard_map/ppermute | solution.py:25
  58.8 1.8 %collective-permute-start.24 = (bf16[24,2048]{1,0:T(8,128)(2,1)S(1)}, bf16[24,2048]{1,0:T(8,128)(2,1)S(1)}, u32[]{:S(2)}, u32[]{:S(2)}) collective-permute-start(bf16[24,2048]{1,0:T(8,128)(2,1)S(1)} %add_convert_fusion.3), channel_id=1, source_target_pairs={{0,24},{8,16},{16,8},{24,0},{1,25},{9,17},{17,9},{25,1},{2,26},{10... | collective-permute-start | bytes 294920 | tf_op jit(solution)/shard_map/ppermute | solution.py:25
  60.7 1.4 %shard_map.84 = f32[1,128]{1,0:T(1,128)S(1)} custom-call(s32[8]{0:T(128)S(1)} %copy-done, bf16[168,128]{1,0:T(8,128)(2,1)S(1)} %slice.88.refs_1_, bf16[216,128]{1,0:T(8,128)(2,1)S(1)} %slice.89.refs_2_, bf16[24,2048]{1,0:T(8,128)(2,1)S(1)} %get-tuple-element.47.refs_3_), custom_call_target="tpu_custom_call" | custom-call | bytes 98304 | tf_op jit(solution)/shard_map/pallas_call | solution.py:335
  62.1 2.3 %collective-permute-done.19 = bf16[24,2048]{1,0:T(8,128)(2,1)S(1)} collective-permute-done((bf16[24,2048]{1,0:T(8,128)(2,1)S(1)}, bf16[24,2048]{1,0:T(8,128)(2,1)S(1)}, u32[]{:S(2)}, u32[]{:S(2)}) %collective-permute-start.19) | collective-permute-done | bytes 98336 | tf_op jit(solution)/shard_map/ppermute | solution.py:25
  64.6 0.1 collective-permute-start.25
  64.7 0.5 slice_bitcast_fusion
  65.2 0.7 %collective-permute-done.25 = bf16[12,2048]{1,0:T(8,128)(2,1)S(1)} collective-permute-done((bf16[12,2048]{1,0:T(8,128)(2,1)S(1)}, bf16[12,2048]{1,0:T(8,128)(2,1)S(1)}, u32[]{:S(2)}, u32[]{:S(2)}) %collective-permute-start.25) | collective-permute-done | bytes 49184 | tf_op jit(solution)/shard_map/ppermute | solution.py:25
  65.9 0.7 %pad_maximum_fusion.2 = bf16[12,4096]{1,0:T(8,128)(2,1)} fusion(bf16[12,2048]{1,0:T(8,128)(2,1)S(1)} %get-tuple-element.52, bf16[12,2048]{1,0:T(8,128)(2,1)S(1)} %get-tuple-element.51), kind=kLoop, calls=%fused_computation.6 | loop fusion | flops 196608 | bytes 196608 | tf_op jit(solution)/shard_map/concatenate | solution.py:437
  (46 shorter events, 0.7 us)
Async XLA Ops:
  2.3 1.4 %collective-permute-start = (bf16[12,2176]{1,0:T(8,128)(2,1)S(1)}, bf16[12,2176]{1,0:T(8,128)(2,1)S(1)}, u32[]{:S(2)}, u32[]{:S(2)}) collective-permute-start(bf16[12,2176]{1,0:T(8,128)(2,1)S(1)} %get-tuple-element.21), channel_id=1, source_target_pairs={{0,1},{1,0},{2,3},{3,2},{4,5},{5,4},{6,7},{7,6},{8,9},{9,8},{10,11... | collective-permute-start | bytes 156680 | tf_op jit(solution)/shard_map/ppermute | solution.py:25
  3.8 8.8 %collective-permute-start.4 = (bf16[24,2176]{1,0:T(8,128)(2,1)S(1)}, bf16[24,2176]{1,0:T(8,128)(2,1)S(1)}, u32[]{:S(2)}, u32[]{:S(2)}) collective-permute-start(bf16[24,2176]{1,0:T(8,128)(2,1)S(1)} %get-tuple-element.39), channel_id=1, source_target_pairs={{0,8},{8,0},{16,24},{24,16},{1,9},{9,1},{17,25},{25,17},{2,10},{10... | collective-permute-start | bytes 313352 | tf_op jit(solution)/shard_map/ppermute | solution.py:25
  6.7 10.9 %collective-permute-start.3 = (bf16[24,2176]{1,0:T(8,128)(2,1)S(1)}, bf16[24,2176]{1,0:T(8,128)(2,1)S(1)}, u32[]{:S(2)}, u32[]{:S(2)}) collective-permute-start(bf16[24,2176]{1,0:T(8,128)(2,1)S(1)} %get-tuple-element.39), channel_id=1, source_target_pairs={{0,6},{2,4},{4,2},{6,0},{1,7},{3,5},{5,3},{7,1},{8,14},{10,12},{12... | collective-permute-start | bytes 313352 | tf_op jit(solution)/shard_map/ppermute | solution.py:25
  10.3 8.8 %collective-permute-start.2 = (bf16[24,2176]{1,0:T(8,128)(2,1)S(1)}, bf16[24,2176]{1,0:T(8,128)(2,1)S(1)}, u32[]{:S(2)}, u32[]{:S(2)}) collective-permute-start(bf16[24,2176]{1,0:T(8,128)(2,1)S(1)} %get-tuple-element.39), channel_id=1, source_target_pairs={{0,4},{2,6},{4,0},{6,2},{1,5},{3,7},{5,1},{7,3},{8,12},{10,14},{12... | collective-permute-start | bytes 313352 | tf_op jit(solution)/shard_map/ppermute | solution.py:25
  10.3 8.8 %collective-permute-start.1 = (bf16[24,2176]{1,0:T(8,128)(2,1)S(1)}, bf16[24,2176]{1,0:T(8,128)(2,1)S(1)}, u32[]{:S(2)}, u32[]{:S(2)}) collective-permute-start(bf16[24,2176]{1,0:T(8,128)(2,1)S(1)} %get-tuple-element.39), channel_id=1, source_target_pairs={{0,2},{2,0},{4,6},{6,4},{1,3},{3,1},{5,7},{7,5},{8,10},{10,8},{12,... | collective-permute-start | bytes 313352 | tf_op jit(solution)/shard_map/ppermute | solution.py:25
  11.1 8.2 %collective-permute-start.6 = (bf16[24,2176]{1,0:T(8,128)(2,1)S(1)}, bf16[24,2176]{1,0:T(8,128)(2,1)S(1)}, u32[]{:S(2)}, u32[]{:S(2)}) collective-permute-start(bf16[24,2176]{1,0:T(8,128)(2,1)S(1)} %get-tuple-element.39), channel_id=1, source_target_pairs={{0,24},{8,16},{16,8},{24,0},{1,25},{9,17},{17,9},{25,1},{2,26},{10... | collective-permute-start | bytes 313352 | tf_op jit(solution)/shard_map/ppermute | solution.py:25
  12.6 6.7 %collective-permute-start.5 = (bf16[24,2176]{1,0:T(8,128)(2,1)S(1)}, bf16[24,2176]{1,0:T(8,128)(2,1)S(1)}, u32[]{:S(2)}, u32[]{:S(2)}) collective-permute-start(bf16[24,2176]{1,0:T(8,128)(2,1)S(1)} %get-tuple-element.39), channel_id=1, source_target_pairs={{0,16},{8,24},{16,0},{24,8},{1,17},{9,25},{17,1},{25,9},{2,18},{10... | collective-permute-start | bytes 313352 | tf_op jit(solution)/shard_map/ppermute | solution.py:25
  19.3 6.0 %collective-permute-start.7 = (bf16[168,2048]{1,0:T(8,128)(2,1)S(1)}, bf16[168,2048]{1,0:T(8,128)(2,1)S(1)}, u32[]{:S(2)}, u32[]{:S(2)}) collective-permute-start(bf16[168,2048]{1,0:T(8,128)(2,1)S(1)} %slice.74), channel_id=1, source_target_pairs={{0,1},{1,0},{2,3},{3,2},{4,5},{5,4},{6,7},{7,6},{8,9},{9,8},{10,11... | collective-permute-start | bytes 2064392 | tf_op jit(solution)/shard_map/ppermute | solution.py:25
  19.4 13.1 %collective-permute-start.9 = (bf16[72,2176]{1,0:T(8,128)(2,1)S(1)}, bf16[72,2176]{1,0:T(8,128)(2,1)S(1)}, u32[]{:S(2)}, u32[]{:S(2)}) collective-permute-start(bf16[72,2176]{1,0:T(8,128)(2,1)S(1)} %get-tuple-element.56), channel_id=1, source_target_pairs={{0,8},{8,0},{16,24},{24,16},{1,9},{9,1},{17,25},{25,17},{2,10},{10... | collective-permute-start | bytes 940040 | tf_op jit(solution)/shard_map/ppermute | solution.py:25
  20.0 12.5 %collective-permute-start.10 = (bf16[72,2176]{1,0:T(8,128)(2,1)S(1)}, bf16[72,2176]{1,0:T(8,128)(2,1)S(1)}, u32[]{:S(2)}, u32[]{:S(2)}) collective-permute-start(bf16[72,2176]{1,0:T(8,128)(2,1)S(1)} %get-tuple-element.56), channel_id=1, source_target_pairs={{0,16},{8,24},{16,0},{24,8},{1,17},{9,25},{17,1},{25,9},{2,18},{10... | collective-permute-start | bytes 940040 | tf_op jit(solution)/shard_map/ppermute | solution.py:25
  21.5 11.1 %collective-permute-start.12 = (bf16[24,2176]{1,0:T(8,128)(2,1)S(1)}, bf16[24,2176]{1,0:T(8,128)(2,1)S(1)}, u32[]{:S(2)}, u32[]{:S(2)}) collective-permute-start(bf16[24,2176]{1,0:T(8,128)(2,1)S(1)} %collective-permute-done.6), channel_id=1, source_target_pairs={{0,4},{2,6},{4,0},{6,2},{1,5},{3,7},{5,1},{7,3},{8,12},{10,14},{12... | collective-permute-start | bytes 313352 | tf_op jit(solution)/shard_map/ppermute | solution.py:25
  23.3 9.3 %collective-permute-start.11 = (bf16[24,2176]{1,0:T(8,128)(2,1)S(1)}, bf16[24,2176]{1,0:T(8,128)(2,1)S(1)}, u32[]{:S(2)}, u32[]{:S(2)}) collective-permute-start(bf16[24,2176]{1,0:T(8,128)(2,1)S(1)} %collective-permute-done.6), channel_id=1, source_target_pairs={{0,2},{2,0},{4,6},{6,4},{1,3},{3,1},{5,7},{7,5},{8,10},{10,8},{12,... | collective-permute-start | bytes 313352 | tf_op jit(solution)/shard_map/ppermute | solution.py:25
  25.4 7.3 %collective-permute-start.13 = (bf16[24,2176]{1,0:T(8,128)(2,1)S(1)}, bf16[24,2176]{1,0:T(8,128)(2,1)S(1)}, u32[]{:S(2)}, u32[]{:S(2)}) collective-permute-start(bf16[24,2176]{1,0:T(8,128)(2,1)S(1)} %collective-permute-done.6), channel_id=1, source_target_pairs={{0,6},{2,4},{4,2},{6,0},{1,7},{3,5},{5,3},{7,1},{8,14},{10,12},{12... | collective-permute-start | bytes 313352 | tf_op jit(solution)/shard_map/ppermute | solution.py:25
  32.8 2.7 %collective-permute-start.14 = (bf16[216,2048]{1,0:T(8,128)(2,1)S(1)}, bf16[216,2048]{1,0:T(8,128)(2,1)S(1)}, u32[]{:S(2)}, u32[]{:S(2)}) collective-permute-start(bf16[216,2048]{1,0:T(8,128)(2,1)S(1)} %slice.76), channel_id=1, source_target_pairs={{0,1},{1,0},{2,3},{3,2},{4,5},{5,4},{6,7},{7,6},{8,9},{9,8},{10,11... | collective-permute-start | bytes 2654216 | tf_op jit(solution)/shard_map/ppermute | solution.py:25
  32.9 5.8 %collective-permute-start.8 = (bf16[168,2048]{1,0:T(8,128)(2,1)S(1)}, bf16[168,2048]{1,0:T(8,128)(2,1)S(1)}, u32[]{:S(2)}, u32[]{:S(2)}) collective-permute-start(bf16[168,2048]{1,0:T(8,128)(2,1)S(1)} %get-tuple-element.29), channel_id=1, source_target_pairs={{0,1},{1,0},{2,3},{3,2},{4,5},{5,4},{6,7},{7,6},{8,9},{9,8},{10,11... | collective-permute-start | bytes 2064392 | tf_op jit(solution)/shard_map/ppermute | solution.py:25
  38.5 2.5 %collective-permute-start.15 = (bf16[216,2048]{1,0:T(8,128)(2,1)S(1)}, bf16[216,2048]{1,0:T(8,128)(2,1)S(1)}, u32[]{:S(2)}, u32[]{:S(2)}) collective-permute-start(bf16[216,2048]{1,0:T(8,128)(2,1)S(1)} %get-tuple-element.34), channel_id=1, source_target_pairs={{0,1},{1,0},{2,3},{3,2},{4,5},{5,4},{6,7},{7,6},{8,9},{9,8},{10,11... | collective-permute-start | bytes 2654216 | tf_op jit(solution)/shard_map/ppermute | solution.py:25
  40.4 20.3 %copy-start = (s32[8]{0:T(128)S(1)}, s32[8]{0:T(128)}, u32[]{:S(2)}) copy-start(s32[8]{0:T(128)} %refs_0_.3) | copy-start | bytes 100
  41.3 11.2 %collective-permute-start.17 = (bf16[96,2048]{1,0:T(8,128)(2,1)S(1)}, bf16[96,2048]{1,0:T(8,128)(2,1)S(1)}, u32[]{:S(2)}, u32[]{:S(2)}) collective-permute-start(bf16[96,2048]{1,0:T(8,128)(2,1)S(1)} %pad_maximum_fusion.1), channel_id=1, source_target_pairs={{0,16},{8,24},{16,0},{24,8},{1,17},{9,25},{17,1},{25,9},{2,18},{10... | collective-permute-start | bytes 1179656 | tf_op jit(solution)/shard_map/ppermute | solution.py:25
  41.9 10.9 %collective-permute-start.16 = (bf16[96,2048]{1,0:T(8,128)(2,1)S(1)}, bf16[96,2048]{1,0:T(8,128)(2,1)S(1)}, u32[]{:S(2)}, u32[]{:S(2)}) collective-permute-start(bf16[96,2048]{1,0:T(8,128)(2,1)S(1)} %pad_maximum_fusion), channel_id=1, source_target_pairs={{0,8},{8,0},{16,24},{24,16},{1,9},{9,1},{17,25},{25,17},{2,10},{10... | collective-permute-start | bytes 1179656 | tf_op jit(solution)/shard_map/ppermute | solution.py:25
  43.5 13.4 %collective-permute-start.23 = (bf16[24,2048]{1,0:T(8,128)(2,1)S(1)}, bf16[24,2048]{1,0:T(8,128)(2,1)S(1)}, u32[]{:S(2)}, u32[]{:S(2)}) collective-permute-start(bf16[24,2048]{1,0:T(8,128)(2,1)S(1)} %get-tuple-element.42), channel_id=1, source_target_pairs={{0,2},{2,0},{4,6},{6,4},{1,3},{3,1},{5,7},{7,5},{8,10},{10,8},{12,... | collective-permute-start | bytes 294920 | tf_op jit(solution)/shard_map/ppermute | solution.py:25
  45.2 12.4 %collective-permute-start.22 = (bf16[24,2048]{1,0:T(8,128)(2,1)S(1)}, bf16[24,2048]{1,0:T(8,128)(2,1)S(1)}, u32[]{:S(2)}, u32[]{:S(2)}) collective-permute-start(bf16[24,2048]{1,0:T(8,128)(2,1)S(1)} %get-tuple-element.43), channel_id=1, source_target_pairs={{0,4},{2,6},{4,0},{6,2},{1,5},{3,7},{5,1},{7,3},{8,12},{10,14},{12... | collective-permute-start | bytes 294920 | tf_op jit(solution)/shard_map/ppermute | solution.py:25
  46.6 11.0 %collective-permute-start.21 = (bf16[24,2048]{1,0:T(8,128)(2,1)S(1)}, bf16[24,2048]{1,0:T(8,128)(2,1)S(1)}, u32[]{:S(2)}, u32[]{:S(2)}) collective-permute-start(bf16[24,2048]{1,0:T(8,128)(2,1)S(1)} %get-tuple-element.44), channel_id=1, source_target_pairs={{0,6},{2,4},{4,2},{6,0},{1,7},{3,5},{5,3},{7,1},{8,14},{10,12},{12... | collective-permute-start | bytes 294920 | tf_op jit(solution)/shard_map/ppermute | solution.py:25
  53.0 5.7 %collective-permute-start.20 = (bf16[24,2048]{1,0:T(8,128)(2,1)S(1)}, bf16[24,2048]{1,0:T(8,128)(2,1)S(1)}, u32[]{:S(2)}, u32[]{:S(2)}) collective-permute-start(bf16[24,2048]{1,0:T(8,128)(2,1)S(1)} %get-tuple-element.48), channel_id=1, source_target_pairs={{0,2},{2,0},{4,6},{6,4},{1,3},{3,1},{5,7},{7,5},{8,10},{10,8},{12,... | collective-permute-start | bytes 294920 | tf_op jit(solution)/shard_map/ppermute | solution.py:25
  54.9 9.6 %collective-permute-start.19 = (bf16[24,2048]{1,0:T(8,128)(2,1)S(1)}, bf16[24,2048]{1,0:T(8,128)(2,1)S(1)}, u32[]{:S(2)}, u32[]{:S(2)}) collective-permute-start(bf16[24,2048]{1,0:T(8,128)(2,1)S(1)} %get-tuple-element.49), channel_id=1, source_target_pairs={{0,4},{2,6},{4,0},{6,2},{1,5},{3,7},{5,1},{7,3},{8,12},{10,14},{12... | collective-permute-start | bytes 294920 | tf_op jit(solution)/shard_map/ppermute | solution.py:25
  56.9 7.6 %collective-permute-start.18 = (bf16[24,2048]{1,0:T(8,128)(2,1)S(1)}, bf16[24,2048]{1,0:T(8,128)(2,1)S(1)}, u32[]{:S(2)}, u32[]{:S(2)}) collective-permute-start(bf16[24,2048]{1,0:T(8,128)(2,1)S(1)} %get-tuple-element.50), channel_id=1, source_target_pairs={{0,6},{2,4},{4,2},{6,0},{1,7},{3,5},{5,3},{7,1},{8,14},{10,12},{12... | collective-permute-start | bytes 294920 | tf_op jit(solution)/shard_map/ppermute | solution.py:25
  58.8 5.6 %collective-permute-start.24 = (bf16[24,2048]{1,0:T(8,128)(2,1)S(1)}, bf16[24,2048]{1,0:T(8,128)(2,1)S(1)}, u32[]{:S(2)}, u32[]{:S(2)}) collective-permute-start(bf16[24,2048]{1,0:T(8,128)(2,1)S(1)} %add_convert_fusion.3), channel_id=1, source_target_pairs={{0,24},{8,16},{16,8},{24,0},{1,25},{9,17},{17,9},{25,1},{2,26},{10... | collective-permute-start | bytes 294920 | tf_op jit(solution)/shard_map/ppermute | solution.py:25
  64.6 1.3 %collective-permute-start.25 = (bf16[12,2048]{1,0:T(8,128)(2,1)S(1)}, bf16[12,2048]{1,0:T(8,128)(2,1)S(1)}, u32[]{:S(2)}, u32[]{:S(2)}) collective-permute-start(bf16[12,2048]{1,0:T(8,128)(2,1)S(1)} %broadcast_select_fusion.4), channel_id=1, source_target_pairs={{0,1},{1,0},{2,3},{3,2},{4,5},{5,4},{6,7},{7,6},{8,9},{9,8},{10,11... | collective-permute-start | bytes 147464 | tf_op jit(solution)/shard_map/ppermute | solution.py:25
